TPU v7x, 32 devices: a whole 2x2x4 slice. The times are simulated.
32 devices in a mesh: groups: 2 (over x), row: 16 (over z, y, core).
Axes of the slice: x: 2, y: 2, z: 4, core: 2. Of those that a mesh axis runs over, the one named last changes fastest.
Arguments:
- pair_state: bfloat16 [256, 128, 128], P(('groups', 'row')), parts along dimension 0, may hold values from -24 to 24
- pair_mask: int32 [256, 128], P(('groups', 'row')), parts along dimension 0, may hold values from 0 to 1, as said below
- norm_gains: float32 [2, 2, 128], replicated, may hold values from 0.1 to 1.9
- norm_biases: float32 [2, 2, 128], replicated, may hold values from -3 to 3
- proj_weights: bfloat16 [2, 128, 512], replicated, may hold values from -0.5 to 0.5
- gate_weights: bfloat16 [2, 128, 128], replicated, may hold values from -0.5 to 0.5
- out_weights: bfloat16 [2, 128, 128], replicated, may hold values from -0.5 to 0.5
Outputs:
- pair_result: bfloat16 [256, 128, 128], P(('groups', 'row')), parts along dimension 0
There are 2 independent parts, one for each index of `groups`. A program takes and returns all parts, laid end to end along the dimension named above; an argument that names none is the same for every part. Nothing has to cross between parts.
Inputs may be any that keep to these rules, and one draw needn't show every extreme that they name: `pair_mask`: 1 where both tokens are real (not padding) and their chains may interact, 0 elsewhere.
All inputs are finite; a program needn't handle non-finite values.
Results may differ from a plain program's by a relative error of at most 0.0065.
Values may be sent and summed in bfloat16 or wider, within the bound.
No kernel may reach another device: no remote copies, remote signals or barrier semaphores. Data moves between devices by JAX's collectives and lax.ppermute only.
A program may use at most 64 MiB of HBM per device.

v0:
```python
import jax
import jax.numpy as jnp
from jax import lax
from jax.sharding import PartitionSpec as P

OUTWARD = "zcik,zcjk->zcij"


def layer_norm(values, norm_gain, norm_bias, reduce_dim):
    average = jnp.mean(values, axis=reduce_dim, keepdims=True)
    centred = values - average
    spread = jnp.mean(centred * centred, axis=reduce_dim, keepdims=True)
    return centred * lax.rsqrt(spread + 1e-05) * norm_gain + norm_bias


def triangle(
    pair_rows,
    mask_rows,
    which_layer,
    einsum_form,
    swapped,
    norm_gains,
    norm_biases,
    proj_weights,
    gate_weights,
    out_weights,
):
    groups = lax.axis_size("row")
    per_dev = pair_rows.shape[0]
    tokens = pair_rows.shape[1]
    channels = pair_rows.shape[2]
    per_group = channels // groups
    normed = layer_norm(
        pair_rows.astype(jnp.float32), norm_gains[which_layer, 0], norm_biases[which_layer, 0], 2
    ).astype(jnp.bfloat16)
    weights = proj_weights[which_layer]

    def gated(offset):
        gate_part = jnp.einsum(
            "rnd,de->ern",
            normed,
            weights[:, offset : offset + channels],
            preferred_element_type=jnp.float32,
        )
        value_part = jnp.einsum(
            "rnd,de->ern",
            normed,
            weights[:, offset + channels : offset + 2 * channels],
            preferred_element_type=jnp.float32,
        )
        masked = jax.nn.sigmoid(gate_part) * value_part * mask_rows[None]
        return masked.astype(jnp.bfloat16).reshape(groups, per_group, per_dev, tokens)

    if swapped:
        left_panel = gated(2 * channels)
        right_panel = gated(0)
    else:
        left_panel = gated(0)
        right_panel = gated(2 * channels)
    out_gate = jax.nn.sigmoid(
        jnp.einsum(
            "rnd,de->rne", normed, gate_weights[which_layer], preferred_element_type=jnp.float32
        )
    ).astype(jnp.bfloat16)
    product = jnp.einsum(
        einsum_form,
        lax.all_to_all(left_panel, "row", split_axis=0, concat_axis=2, tiled=True),
        lax.all_to_all(right_panel, "row", split_axis=0, concat_axis=2, tiled=True),
        preferred_element_type=jnp.float32,
    )
    merged = lax.all_to_all(
        product.astype(jnp.bfloat16), "row", split_axis=2, concat_axis=0, tiled=True
    )
    merged = merged.reshape(channels, per_dev, tokens)
    normed_out = layer_norm(
        merged.astype(jnp.float32),
        norm_gains[which_layer, 1][:, None, None],
        norm_biases[which_layer, 1][:, None, None],
        0,
    ).astype(jnp.bfloat16)
    projected = jnp.einsum(
        "crn,cd->rnd", normed_out, out_weights[which_layer], preferred_element_type=jnp.float32
    )
    return (pair_rows.astype(jnp.float32) + out_gate.astype(jnp.float32) * projected).astype(
        jnp.bfloat16
    )


def on_device(
    pair_state, pair_mask, norm_gains, norm_biases, proj_weights, gate_weights, out_weights
):
    mask_rows = pair_mask.astype(jnp.float32)
    middle = triangle(
        pair_state,
        mask_rows,
        0,
        OUTWARD,
        False,
        norm_gains,
        norm_biases,
        proj_weights,
        gate_weights,
        out_weights,
    )
    flipped, mask_flip = (
        lax.all_to_all(middle, "row", split_axis=1, concat_axis=0, tiled=True),
        lax.all_to_all(
            pair_mask.astype(jnp.bfloat16), "row", split_axis=1, concat_axis=0, tiled=True
        ),
    )
    second_flip = triangle(
        jnp.swapaxes(flipped, 0, 1),
        mask_flip.T.astype(jnp.float32),
        1,
        OUTWARD,
        True,
        norm_gains,
        norm_biases,
        proj_weights,
        gate_weights,
        out_weights,
    )
    restored = lax.all_to_all(second_flip, "row", split_axis=1, concat_axis=0, tiled=True)
    return jnp.swapaxes(restored, 0, 1)


def solution(mesh):
    return jax.shard_map(
        on_device,
        mesh=mesh,
        in_specs=(
            P(("groups", "row"), None, None),
            P(("groups", "row"), None),
            P(),
            P(),
            P(),
            P(),
            P(),
        ),
        out_specs=P(("groups", "row"), None, None),
        check_vma=False,
    )
```

profile of v0, /device:TPU:0, one launch (start us, length us, event | category | flops | bytes accessed | tf_op | source)
XLA Modules:
  0.0 131.8 jit_solution(1941318705768366268)
XLA Ops:
  0.0 1.2 convert_reduce_fusion
  1.2 0.4 fusion.42
  1.6 0.1 copy.129
  1.7 0.6 copy-done.3
  2.3 0.7 copy-done.4
  3.0 0.5 fusion.14
  3.5 0.5 fusion.36
  4.0 0.9 copy.87
  4.9 7.4 %all-to-all-start = ((bf16[16,8,8,128]{3,2,1,0:T(8,128)(2,1)}), bf16[16,8,8,128]{3,2,1,0:T(8,128)(2,1)S(1)}, u32[]{:S(2)}, u32[]{:S(2)}) async-start(bf16[16,8,8,128]{3,2,1,0:T(8,128)(2,1)} %bitcast.8), calls=%async_computation | async-start | bytes 524288 | tf_op jit(solution)/shard_map/all_to_all | solution.py:67
  12.3 0.5 fusion.11
  12.7 0.5 fusion.37
  13.2 0.2 copy.91
  13.4 8.9 %all-to-all-done = bf16[16,8,8,128]{3,2,1,0:T(8,128)(2,1)S(1)} async-done(((bf16[16,8,8,128]{3,2,1,0:T(8,128)(2,1)}), bf16[16,8,8,128]{3,2,1,0:T(8,128)(2,1)S(1)}, u32[]{:S(2)}, u32[]{:S(2)}) %all-to-all-start) | async-done | bytes 262176 | tf_op jit(solution)/shard_map/all_to_all | solution.py:67
  22.3 12.8 %all_to_all.118 = bf16[16,8,8,128]{3,2,1,0:T(8,128)(2,1)S(1)} all-to-all(bf16[16,8,8,128]{3,2,1,0:T(8,128)(2,1)S(1)} %bitcast.215), channel_id=1, replica_groups=mesh['groups'=2,'row'=16] {'row'}, dimensions={0} | all-to-all | bytes 524288 | tf_op jit(solution)/shard_map/all_to_all | solution.py:68
  35.1 0.3 fusion.34
  35.4 0.9 copy.93
  36.3 3.5 %all-to-all-start.2 = ((bf16[1,8,128,128]{3,1,0,2:T(8,128)(2,1)}), bf16[1,8,128,128]{3,1,0,2:T(8,128)(2,1)S(1)}, u32[]{:S(2)}, u32[]{:S(2)}) async-start(bf16[1,8,128,128]{3,1,0,2:T(8,128)(2,1)} %copy.93), calls=%async_computation.2 | async-start | bytes 524288 | tf_op jit(solution)/shard_map/all_to_all | solution.py:71
  39.8 0.1 mul.150
  39.9 0.1 copy.95
  40.0 0.1 add.110
  40.1 0.1 copy.96
  40.1 0.1 all_to_all.96
  40.3 0.6 copy.104
  40.9 0.5 fusion.31
  41.3 8.5 %all-to-all-done.2 = bf16[1,8,128,128]{3,1,0,2:T(8,128)(2,1)S(1)} async-done(((bf16[1,8,128,128]{3,1,0,2:T(8,128)(2,1)}), bf16[1,8,128,128]{3,1,0,2:T(8,128)(2,1)S(1)}, u32[]{:S(2)}, u32[]{:S(2)}) %all-to-all-start.2) | async-done | bytes 262176 | tf_op jit(solution)/shard_map/all_to_all | solution.py:71
  49.8 3.5 %all-to-all-start.4 = ((bf16[8,16,8]{2,0,1:T(8,128)(2,1)}), bf16[8,16,8]{2,0,1:T(8,128)(2,1)S(1)}, u32[]{:S(2)}, u32[]{:S(2)}) async-start(bf16[8,16,8]{2,0,1:T(8,128)(2,1)} %copy.104), calls=%async_computation.4 | async-start | bytes 65536 | tf_op jit(solution)/shard_map/all_to_all | solution.py:107
  53.3 0.1 fusion.55
  53.5 0.1 fusion.58
  53.6 0.3 fusion.61
  54.0 0.1 copy.97
  54.1 0.8 copy-done.2
  54.8 0.3 fusion.27
  55.1 0.9 copy.99
  56.0 4.0 %all-to-all-done.4 = bf16[8,16,8]{2,0,1:T(8,128)(2,1)S(1)} async-done(((bf16[8,16,8]{2,0,1:T(8,128)(2,1)}), bf16[8,16,8]{2,0,1:T(8,128)(2,1)S(1)}, u32[]{:S(2)}, u32[]{:S(2)}) %all-to-all-start.4) | async-done | bytes 2080 | tf_op jit(solution)/shard_map/all_to_all | solution.py:107
  59.9 3.5 %all-to-all-start.3 = ((bf16[8,128,128]{2,0,1:T(8,128)(2,1)}), bf16[8,128,128]{2,0,1:T(8,128)(2,1)S(1)}, u32[]{:S(2)}, u32[]{:S(2)}) async-start(bf16[8,128,128]{2,0,1:T(8,128)(2,1)} %copy.99), calls=%async_computation.3 | async-start | bytes 524288 | tf_op jit(solution)/shard_map/all_to_all | solution.py:106
  63.5 0.1 copy.130
  63.7 9.8 %all-to-all-done.3 = bf16[8,128,128]{2,0,1:T(8,128)(2,1)S(1)} async-done(((bf16[8,128,128]{2,0,1:T(8,128)(2,1)}), bf16[8,128,128]{2,0,1:T(8,128)(2,1)S(1)}, u32[]{:S(2)}, u32[]{:S(2)}) %all-to-all-start.3) | async-done | bytes 262176 | tf_op jit(solution)/shard_map/all_to_all | solution.py:106
  73.5 0.2 bitcast_reduce_fusion
  73.8 0.4 multiply_reduce_fusion
  74.1 0.5 fusion.5
  74.6 0.5 fusion.38
  75.1 0.9 copy.106
  76.0 3.5 %all-to-all-start.5 = ((bf16[16,8,8,128]{3,2,1,0:T(8,128)(2,1)}), bf16[16,8,8,128]{3,2,1,0:T(8,128)(2,1)S(1)}, u32[]{:S(2)}, u32[]{:S(2)}) async-start(bf16[16,8,8,128]{3,2,1,0:T(8,128)(2,1)} %bitcast.43), calls=%async_computation.5 | async-start | bytes 524288 | tf_op jit(solution)/shard_map/all_to_all | solution.py:67
  79.5 0.5 fusion.2
  80.0 0.5 fusion.39
  80.5 0.2 copy.110
  80.7 8.9 %all-to-all-done.5 = bf16[16,8,8,128]{3,2,1,0:T(8,128)(2,1)S(1)} async-done(((bf16[16,8,8,128]{3,2,1,0:T(8,128)(2,1)}), bf16[16,8,8,128]{3,2,1,0:T(8,128)(2,1)S(1)}, u32[]{:S(2)}, u32[]{:S(2)}) %all-to-all-start.5) | async-done | bytes 262176 | tf_op jit(solution)/shard_map/all_to_all | solution.py:67
  89.5 12.8 %all_to_all.119 = bf16[16,8,8,128]{3,2,1,0:T(8,128)(2,1)S(1)} all-to-all(bf16[16,8,8,128]{3,2,1,0:T(8,128)(2,1)S(1)} %bitcast.216), channel_id=1, replica_groups=mesh['groups'=2,'row'=16] {'row'}, dimensions={0} | all-to-all | bytes 524288 | tf_op jit(solution)/shard_map/all_to_all | solution.py:68
  102.3 0.3 fusion.35
  102.7 0.9 copy.112
  103.5 3.5 %all-to-all-start.7 = ((bf16[1,8,128,128]{3,1,0,2:T(8,128)(2,1)}), bf16[1,8,128,128]{3,1,0,2:T(8,128)(2,1)S(1)}, u32[]{:S(2)}, u32[]{:S(2)}) async-start(bf16[1,8,128,128]{3,1,0,2:T(8,128)(2,1)} %copy.112), calls=%async_computation.7 | async-start | bytes 524288 | tf_op jit(solution)/shard_map/all_to_all | solution.py:71
  107.1 0.1 mul.168
  107.1 0.1 copy.114
  107.2 0.1 add.122
  107.3 0.1 copy.115
  107.4 0.5 fusion.33
  107.9 9.2 %all-to-all-done.7 = bf16[1,8,128,128]{3,1,0,2:T(8,128)(2,1)S(1)} async-done(((bf16[1,8,128,128]{3,1,0,2:T(8,128)(2,1)}), bf16[1,8,128,128]{3,1,0,2:T(8,128)(2,1)S(1)}, u32[]{:S(2)}, u32[]{:S(2)}) %all-to-all-start.7) | async-done | bytes 262176 | tf_op jit(solution)/shard_map/all_to_all | solution.py:71
  117.1 0.1 fusion.47
  117.2 0.1 fusion.50
  117.4 0.3 fusion.53
  117.8 0.3 fusion.24
  118.0 0.2 copy.118
  118.2 12.8 %all_to_all.120 = bf16[8,128,128]{2,0,1:T(8,128)(2,1)S(1)} all-to-all(bf16[8,128,128]{2,0,1:T(8,128)(2,1)S(1)} %copy.118), channel_id=1, replica_groups=mesh['groups'=2,'row'=16] {'row'}, dimensions={1} | all-to-all | bytes 524288 | tf_op jit(solution)/shard_map/all_to_all | solution.py:123
  131.1 0.8 copy.177
  (26 shorter events, 0.3 us)
Async XLA Ops:
  0.0 1.2 copy-start
  0.0 1.6 %copy-start.1 = (bf16[2,128,512]{2,1,0:T(8,128)(2,1)S(1)}, bf16[2,128,512]{2,1,0:T(8,128)(2,1)}, u32[]{:S(2)}) copy-start(bf16[2,128,512]{2,1,0:T(8,128)(2,1)} %param.11) | copy-start | bytes 786436
  1.6 0.7 copy-start.3
  2.3 0.7 copy-start.4
  2.3 0.7 copy-start.5
  4.9 17.4 %all-to-all-start = ((bf16[16,8,8,128]{3,2,1,0:T(8,128)(2,1)}), bf16[16,8,8,128]{3,2,1,0:T(8,128)(2,1)S(1)}, u32[]{:S(2)}, u32[]{:S(2)}) async-start(bf16[16,8,8,128]{3,2,1,0:T(8,128)(2,1)} %bitcast.8), calls=%async_computation | async-start | bytes 524288 | tf_op jit(solution)/shard_map/all_to_all | solution.py:67
  36.3 13.5 %all-to-all-start.2 = ((bf16[1,8,128,128]{3,1,0,2:T(8,128)(2,1)}), bf16[1,8,128,128]{3,1,0,2:T(8,128)(2,1)S(1)}, u32[]{:S(2)}, u32[]{:S(2)}) async-start(bf16[1,8,128,128]{3,1,0,2:T(8,128)(2,1)} %copy.93), calls=%async_computation.2 | async-start | bytes 524288 | tf_op jit(solution)/shard_map/all_to_all | solution.py:71
  40.0 0.9 copy-start.6
  49.8 10.1 %all-to-all-start.4 = ((bf16[8,16,8]{2,0,1:T(8,128)(2,1)}), bf16[8,16,8]{2,0,1:T(8,128)(2,1)S(1)}, u32[]{:S(2)}, u32[]{:S(2)}) async-start(bf16[8,16,8]{2,0,1:T(8,128)(2,1)} %copy.104), calls=%async_computation.4 | async-start | bytes 65536 | tf_op jit(solution)/shard_map/all_to_all | solution.py:107
  54.0 0.8 copy-start.2
  59.9 13.5 %all-to-all-start.3 = ((bf16[8,128,128]{2,0,1:T(8,128)(2,1)}), bf16[8,128,128]{2,0,1:T(8,128)(2,1)S(1)}, u32[]{:S(2)}, u32[]{:S(2)}) async-start(bf16[8,128,128]{2,0,1:T(8,128)(2,1)} %copy.99), calls=%async_computation.3 | async-start | bytes 524288 | tf_op jit(solution)/shard_map/all_to_all | solution.py:106
  76.0 13.5 %all-to-all-start.5 = ((bf16[16,8,8,128]{3,2,1,0:T(8,128)(2,1)}), bf16[16,8,8,128]{3,2,1,0:T(8,128)(2,1)S(1)}, u32[]{:S(2)}, u32[]{:S(2)}) async-start(bf16[16,8,8,128]{3,2,1,0:T(8,128)(2,1)} %bitcast.43), calls=%async_computation.5 | async-start | bytes 524288 | tf_op jit(solution)/shard_map/all_to_all | solution.py:67
  103.5 13.5 %all-to-all-start.7 = ((bf16[1,8,128,128]{3,1,0,2:T(8,128)(2,1)}), bf16[1,8,128,128]{3,1,0,2:T(8,128)(2,1)S(1)}, u32[]{:S(2)}, u32[]{:S(2)}) async-start(bf16[1,8,128,128]{3,1,0,2:T(8,128)(2,1)} %copy.112), calls=%async_computation.7 | async-start | bytes 524288 | tf_op jit(solution)/shard_map/all_to_all | solution.py:71
where the time goes:
time: 133 us; the launch traced here: 132 us
  waiting for transfers between devices  49.2 us (37%)
  blocking collectives  38.4 us (29%)
  starting transfers between devices  25 us (19%)
  local copies, waits for them, and re-layouts  9.51 us (7%)
  matrix products  5.85 us (4%)
  other arithmetic  3.43 us (3%)
    all_to_all x2, blocking collectives, triangle(): lax.all_to_all(right_panel, 'row', split_axis=0, concat_axis=2, tiled=True)  25.6 us
    all_to_all x2, waiting for transfers between devices, triangle(): lax.all_to_all(left_panel, 'row', split_axis=0, concat_axis=2, tiled=True)  17.7 us
    all_to_all x2, waiting for transfers between devices, triangle(): lax.all_to_all(product.astype(jnp.bfloat16), 'row', split_axis=2, concat_...  17.7 us
    all_to_all x1, blocking collectives, on_device(): lax.all_to_all(second_flip, 'row', split_axis=1, concat_axis=0, tiled=True)  12.8 us
    all_to_all x2, starting transfers between devices, triangle(): lax.all_to_all(left_panel, 'row', split_axis=0, concat_axis=2, tiled=True)  10.9 us
    all_to_all x1, waiting for transfers between devices, on_device(): lax.all_to_all(middle, 'row', split_axis=1, concat_axis=0, tiled=True)  9.82 us
    all_to_all x2, starting transfers between devices, triangle(): lax.all_to_all(product.astype(jnp.bfloat16), 'row', split_axis=2, concat_...  7.07 us
    all_to_all x1, waiting for transfers between devices, on_device(): lax.all_to_all(pair_mask.astype(jnp.bfloat16), 'row', split_axis=1, conca...  3.97 us
  transfers between devices with their start and end apart: 6, of which 6 were waited for; matrix products, arithmetic and copies ran while one was open for 5% of the time, Pallas kernels for 0%

commit v1 on v0

v1 whole, which is shorter than its diff:
```python
import jax
import jax.numpy as jnp
from jax import lax
from jax.sharding import PartitionSpec as P


def layer_norm(values, norm_gain, norm_bias, reduce_dim):
    average = jnp.mean(values, axis=reduce_dim, keepdims=True)
    centred = values - average
    spread = jnp.mean(centred * centred, axis=reduce_dim, keepdims=True)
    return centred * lax.rsqrt(spread + 1e-05) * norm_gain + norm_bias


def triangle(pair_rows, mask_rows, which, form, norm_gains, norm_biases, proj_weights, gate_weights, out_weights):
    groups = lax.axis_size("row")
    per_dev, tokens, channels = pair_rows.shape
    per_group = channels // groups
    normed = layer_norm(
        pair_rows.astype(jnp.float32), norm_gains[which, 0], norm_biases[which, 0], 2
    ).astype(jnp.bfloat16)
    weights = proj_weights[which]

    def gated(offset):
        gate_part = jnp.einsum(
            "rnd,de->ern", normed, weights[:, offset : offset + channels], preferred_element_type=jnp.float32
        )
        value_part = jnp.einsum(
            "rnd,de->ern",
            normed,
            weights[:, offset + channels : offset + 2 * channels],
            preferred_element_type=jnp.float32,
        )
        masked = jax.nn.sigmoid(gate_part) * value_part * mask_rows[None]
        return masked.astype(jnp.bfloat16).reshape(groups, 1, per_group, per_dev, tokens)

    both = jnp.concatenate([gated(0), gated(2 * channels)], axis=1)
    out_gate = jax.nn.sigmoid(
        jnp.einsum("rnd,de->rne", normed, gate_weights[which], preferred_element_type=jnp.float32)
    ).astype(jnp.bfloat16)
    both = lax.all_to_all(both, "row", split_axis=0, concat_axis=0, tiled=True)
    left = jnp.moveaxis(both[:, 0], 0, 1).reshape(per_group, tokens, tokens)
    right = jnp.moveaxis(both[:, 1], 0, 1).reshape(per_group, tokens, tokens)
    product = jnp.einsum(form, left, right, preferred_element_type=jnp.float32).astype(jnp.bfloat16)
    product = product.reshape(per_group, groups, per_dev, tokens)
    merged = lax.all_to_all(product, "row", split_axis=1, concat_axis=0, tiled=True)
    merged = merged.reshape(channels, per_dev, tokens)
    normed_out = layer_norm(
        merged.astype(jnp.float32),
        norm_gains[which, 1][:, None, None],
        norm_biases[which, 1][:, None, None],
        0,
    ).astype(jnp.bfloat16)
    projected = jnp.einsum("crn,cd->rnd", normed_out, out_weights[which], preferred_element_type=jnp.float32)
    return (pair_rows.astype(jnp.float32) + out_gate.astype(jnp.float32) * projected).astype(jnp.bfloat16)


def on_device(pair_state, pair_mask, *params):
    mask_rows = pair_mask.astype(jnp.float32)
    middle = triangle(pair_state, mask_rows, 0, "cik,cjk->cij", *params)
    return triangle(middle, mask_rows, 1, "cki,ckj->cij", *params)


def solution(mesh):
    rows = ("groups", "row")
    return jax.shard_map(
        on_device,
        mesh=mesh,
        in_specs=(P(rows, None, None), P(rows, None), P(), P(), P(), P(), P()),
        out_specs=P(rows, None, None),
        check_vma=False,
    )
```

time: 133 us -> 79.7 us (0.60)
  waiting for transfers between devices: 49.2 us -> 18.2 us
  starting transfers between devices: 25 us -> 8.2 us
  local copies, waits for them, and re-layouts: 9.51 us -> 7.52 us
  other arithmetic: 3.43 us -> 1.8 us
  matrix products: 5.85 us -> 4.22 us
    all_to_all x6 -> x2, waiting for transfers between devices: 49.2 us -> 18.2 us  [triangle(): lax.all_to_all(product, 'row', split_axis=1, concat_axis=0, tiled=True)]
    all_to_all x6 -> x2, starting transfers between devices: 25 us -> 8.2 us  [triangle(): lax.all_to_all(product, 'row', split_axis=1, concat_axis=0, tiled=True)]
    convert_element_type x9 -> x0, local copies, waits for them, and re-layouts: 4.06 us -> none  [the longest x4 2.14 us: gated(): masked.astype(jnp.bfloat16).reshape(groups, per_group, per_dev, tokens)]
    unnamed x16 -> x15, local copies, waits for them, and re-layouts: 2.26 us -> 4.22 us
    reshape x0 -> x4, local copies, waits for them, and re-layouts: none -> 1.89 us  [the longest x2 1.54 us: triangle(): product = product.reshape(per_group, groups, per_dev, tokens)]
    all_to_all x3 -> x0, local copies, waits for them, and re-layouts: 1.47 us -> none  [the longest x1 0.75 us: on_device(): lax.all_to_all(second_flip, 'row', split_axis=1, concat_axis=0, tiled=True)]
    all_to_all x3 -> x2, blocking collectives: 38.4 us -> 38.9 us  [triangle(): both = lax.all_to_all(both, 'row', split_axis=0, concat_axis=0, tiled=True)]
  transfers between devices with their start and end apart: 6 -> 2, of which waited for: 6 -> 2; matrix products, arithmetic and copies ran while one was open for 5% -> 1% of each run, Pallas kernels for 0% -> 0%
where the time goes in v1:
time: 79.7 us; the launch traced here: 79.1 us
  blocking collectives  38.9 us (49%)
  waiting for transfers between devices  18.2 us (23%)
  starting transfers between devices  8.2 us (10%)
  local copies, waits for them, and re-layouts  7.52 us (9%)
  matrix products  4.22 us (5%)
  other arithmetic  1.8 us (2%)
    all_to_all x2, blocking collectives, triangle(): both = lax.all_to_all(both, 'row', split_axis=0, concat_axis=0, tiled=True)  38.9 us
    all_to_all x2, waiting for transfers between devices, triangle(): lax.all_to_all(product, 'row', split_axis=1, concat_axis=0, tiled=True)  18.2 us
    all_to_all x2, starting transfers between devices, triangle(): lax.all_to_all(product, 'row', split_axis=1, concat_axis=0, tiled=True)  8.2 us
    unnamed x15, local copies, waits for them, and re-layouts  4.22 us
  transfers between devices with their start and end apart: 2, of which 2 were waited for; matrix products, arithmetic and copies ran while one was open for 1% of the time, Pallas kernels for 0%

profile of v1, /device:TPU:0, one launch (start us, length us, event | category | flops | bytes accessed | tf_op | source)
XLA Modules:
  0.0 79.1 jit_solution(18356812239679539094)
XLA Ops:
  0.0 1.1 %copy.64 = bf16[8,128,128]{1,2,0:T(8,128)(2,1)S(1)} copy(bf16[8,128,128]{2,1,0:T(8,128)(2,1)} %param.7) | data formatting | bytes 524288 | tf_op args[0]
  1.1 0.0 copy-start
  1.2 0.1 fusion.43
  1.3 0.8 copy-done
  2.1 0.0 copy-start.3
  2.1 0.0 copy-start.4
  2.1 0.1 copy.111
  2.2 0.5 copy-done.3
  2.8 0.0 copy-done.4
  2.8 0.4 fusion.11
  3.2 0.0 copy-start.2
  3.2 0.4 fusion.8
  3.6 0.3 copy-done.2
  3.9 0.3 fusion.37
  4.2 0.3 fusion.38
  4.5 0.1 pad_maximum_fusion
  4.6 0.1 copy.108
  4.7 21.7 %all_to_all.28 = bf16[16,2,8,8,128]{4,2,3,1,0:T(8,128)(2,1)S(1)} all-to-all(bf16[16,2,8,8,128]{4,2,3,1,0:T(8,128)(2,1)S(1)} %copy.108), channel_id=1, replica_groups=mesh['groups'=2,'row'=16] {'row'}, dimensions={0} | all-to-all | bytes 1048576 | tf_op jit(solution)/shard_map/all_to_all | solution.py:40
  26.4 0.3 fusion.35
  26.7 0.8 copy.76
  27.5 4.1 %all-to-all-start.1 = ((bf16[8,16,8,128]{3,2,0,1:T(8,128)(2,1)}), bf16[8,16,8,128]{3,2,0,1:T(8,128)(2,1)S(1)}, u32[]{:S(2)}, u32[]{:S(2)}) async-start(bf16[8,16,8,128]{3,2,0,1:T(8,128)(2,1)} %copy.76), calls=%async_computation.1 | async-start | bytes 524288 | tf_op jit(solution)/shard_map/all_to_all | solution.py:45
  31.6 0.1 add.110
  31.7 0.1 mul.148
  31.8 0.0 copy-start.5
  31.8 0.1 copy.112
  31.9 0.7 copy-done.5
  32.6 0.4 fusion.34
  33.0 8.6 %all-to-all-done.1 = bf16[8,16,8,128]{3,2,0,1:T(8,128)(2,1)S(1)} async-done(((bf16[8,16,8,128]{3,2,0,1:T(8,128)(2,1)}), bf16[8,16,8,128]{3,2,0,1:T(8,128)(2,1)S(1)}, u32[]{:S(2)}, u32[]{:S(2)}) %all-to-all-start.1) | async-done | bytes 262176 | tf_op jit(solution)/shard_map/all_to_all | solution.py:45
  41.7 0.1 fusion.56
  41.8 0.1 fusion.59
  41.9 0.0 copy-start.1
  42.0 0.3 fusion.62
  42.3 0.5 copy-done.1
  42.8 0.3 fusion.85
  43.1 0.1 multiply_reduce_fusion
  43.2 0.2 add_convert_fusion
  43.4 0.3 fusion.5
  43.7 0.3 fusion.2
  44.0 0.2 fusion.39
  44.2 0.2 copy.86
  44.4 0.2 fusion.40
  44.6 0.2 copy.87
  44.8 0.1 pad_maximum_fusion.1
  44.8 17.2 %all_to_all.29 = bf16[16,2,8,8,128]{4,3,2,1,0:T(8,128)(2,1)S(1)} all-to-all(bf16[16,2,8,8,128]{4,3,2,1,0:T(8,128)(2,1)S(1)} %pad_maximum_fusion.1), channel_id=1, replica_groups=mesh['groups'=2,'row'=16] {'row'}, dimensions={0} | all-to-all | bytes 1048576 | tf_op jit(solution)/shard_map/all_to_all | solution.py:40
  62.1 0.3 fusion.36
  62.4 0.8 copy.91
  63.2 4.1 %all-to-all-start.3 = ((bf16[8,16,8,128]{3,2,0,1:T(8,128)(2,1)}), bf16[8,16,8,128]{3,2,0,1:T(8,128)(2,1)S(1)}, u32[]{:S(2)}, u32[]{:S(2)}) async-start(bf16[8,16,8,128]{3,2,0,1:T(8,128)(2,1)} %copy.91), calls=%async_computation.3 | async-start | bytes 524288 | tf_op jit(solution)/shard_map/all_to_all | solution.py:45
  67.3 0.1 add.122
  67.4 0.1 mul.165
  67.5 0.4 fusion.32
  67.8 9.5 %all-to-all-done.3 = bf16[8,16,8,128]{3,2,0,1:T(8,128)(2,1)S(1)} async-done(((bf16[8,16,8,128]{3,2,0,1:T(8,128)(2,1)}), bf16[8,16,8,128]{3,2,0,1:T(8,128)(2,1)S(1)}, u32[]{:S(2)}, u32[]{:S(2)}) %all-to-all-start.3) | async-done | bytes 262176 | tf_op jit(solution)/shard_map/all_to_all | solution.py:45
  77.3 0.1 fusion.48
  77.5 0.1 fusion.51
  77.6 0.3 fusion.54
  78.0 0.3 fusion.30
  78.3 0.9 %copy.94 = bf16[8,128,128]{2,1,0:T(8,128)(2,1)} copy(bf16[8,128,128]{1,2,0:T(8,128)(2,1)S(1)} %fusion.30) | data formatting | bytes 524288 | tf_op jit(solution)/shard_map/convert_element_type | solution.py:54
  (14 shorter events, 0.2 us)
Async XLA Ops:
  1.1 1.0 %copy-start = (bf16[2,128,512]{2,1,0:T(8,128)(2,1)S(1)}, bf16[2,128,512]{2,1,0:T(8,128)(2,1)}, u32[]{:S(2)}) copy-start(bf16[2,128,512]{2,1,0:T(8,128)(2,1)} %param.11) | copy-start | bytes 786436
  2.1 0.7 copy-start.3
  2.1 0.7 copy-start.4
  3.2 0.7 copy-start.2
  27.5 14.2 %all-to-all-start.1 = ((bf16[8,16,8,128]{3,2,0,1:T(8,128)(2,1)}), bf16[8,16,8,128]{3,2,0,1:T(8,128)(2,1)S(1)}, u32[]{:S(2)}, u32[]{:S(2)}) async-start(bf16[8,16,8,128]{3,2,0,1:T(8,128)(2,1)} %copy.76), calls=%async_computation.1 | async-start | bytes 524288 | tf_op jit(solution)/shard_map/all_to_all | solution.py:45
  31.8 0.9 %copy-start.5 = (bf16[2,128,128]{2,1,0:T(8,128)(2,1)S(1)}, bf16[2,128,128]{2,1,0:T(8,128)(2,1)}, u32[]{:S(2)}) copy-start(bf16[2,128,128]{2,1,0:T(8,128)(2,1)} %param.12) | copy-start | bytes 196612
  41.9 0.8 %copy-start.1 = (bf16[2,128,128]{2,1,0:T(8,128)(2,1)S(1)}, bf16[2,128,128]{2,1,0:T(8,128)(2,1)}, u32[]{:S(2)}) copy-start(bf16[2,128,128]{2,1,0:T(8,128)(2,1)} %param.13) | copy-start | bytes 196612
  63.2 14.2 %all-to-all-start.3 = ((bf16[8,16,8,128]{3,2,0,1:T(8,128)(2,1)}), bf16[8,16,8,128]{3,2,0,1:T(8,128)(2,1)S(1)}, u32[]{:S(2)}, u32[]{:S(2)}) async-start(bf16[8,16,8,128]{3,2,0,1:T(8,128)(2,1)} %copy.91), calls=%async_computation.3 | async-start | bytes 524288 | tf_op jit(solution)/shard_map/all_to_all | solution.py:45

commit v2 on v1

--- a/solution.py
+++ b/solution.py
@@ -9,6 +9,28 @@
     centred = values - average
     spread = jnp.mean(centred * centred, axis=reduce_dim, keepdims=True)
     return centred * lax.rsqrt(spread + 1e-05) * norm_gain + norm_bias
+
+
+def by_partner(blocks):
+    me = lax.axis_index("row")
+    count = blocks.shape[0]
+    bit = 1
+    while bit < count:
+        split = blocks.reshape((count // (2 * bit), 2, bit) + blocks.shape[1:])
+        blocks = jnp.where((me & bit) != 0, split[:, ::-1], split).reshape(blocks.shape)
+        bit *= 2
+    return blocks
+
+
+def exchange(blocks):
+    count = blocks.shape[0]
+    if count & (count - 1):
+        return lax.all_to_all(blocks, "row", split_axis=0, concat_axis=0, tiled=True)
+    out = by_partner(blocks)
+    got = [out[0]]
+    for k in range(1, count):
+        got.append(lax.ppermute(out[k], "row", [(d, d ^ k) for d in range(count)]))
+    return by_partner(jnp.stack(got))
 
 
 def triangle(pair_rows, mask_rows, which, form, norm_gains, norm_biases, proj_weights, gate_weights, out_weights):
@@ -37,12 +59,12 @@
     out_gate = jax.nn.sigmoid(
         jnp.einsum("rnd,de->rne", normed, gate_weights[which], preferred_element_type=jnp.float32)
     ).astype(jnp.bfloat16)
-    both = lax.all_to_all(both, "row", split_axis=0, concat_axis=0, tiled=True)
+    both = exchange(both)
     left = jnp.moveaxis(both[:, 0], 0, 1).reshape(per_group, tokens, tokens)
     right = jnp.moveaxis(both[:, 1], 0, 1).reshape(per_group, tokens, tokens)
     product = jnp.einsum(form, left, right, preferred_element_type=jnp.float32).astype(jnp.bfloat16)
-    product = product.reshape(per_group, groups, per_dev, tokens)
-    merged = lax.all_to_all(product, "row", split_axis=1, concat_axis=0, tiled=True)
+    product = jnp.moveaxis(product.reshape(per_group, groups, per_dev, tokens), 1, 0)
+    merged = exchange(product)
     merged = merged.reshape(channels, per_dev, tokens)
     normed_out = layer_norm(
         merged.astype(jnp.float32),

time: 79.7 us -> 120 us (1.51)
  starting transfers between devices: 8.2 us -> 84.7 us
  blocking collectives: 38.9 us -> 0 us
  other arithmetic: 1.8 us -> 5.22 us
  waiting for transfers between devices: 18.2 us -> 16.4 us
    ppermute x0 -> x60, starting transfers between devices: none -> 84.7 us  [exchange(): got.append(lax.ppermute(out[k], 'row', [(d, d ^ k) for d in range(count)]))]
    all_to_all x2 -> x0, blocking collectives: 38.9 us -> none  [triangle(): both = lax.all_to_all(both, 'row', split_axis=0, concat_axis=0, tiled=True)]
    all_to_all x2 -> x0, waiting for transfers between devices: 18.2 us -> none  [triangle(): lax.all_to_all(product, 'row', split_axis=1, concat_axis=0, tiled=True)]
    ppermute x0 -> x60, waiting for transfers between devices: none -> 16.4 us  [exchange(): got.append(lax.ppermute(out[k], 'row', [(d, d ^ k) for d in range(count)]))]
    all_to_all x2 -> x0, starting transfers between devices: 8.2 us -> none  [triangle(): lax.all_to_all(product, 'row', split_axis=1, concat_axis=0, tiled=True)]
    select_n x0 -> x30, other arithmetic: none -> 3.42 us  [by_partner(): jnp.where(me & bit != 0, split[:, ::-1], split).reshape(blocks.shape)]
    reshape x4 -> x2, local copies, waits for them, and re-layouts: 1.89 us -> 0.12 us  [by_partner(): split = blocks.reshape((count // (2 * bit), 2, bit) + blocks.shape[1:])]
    another operation x0 -> x8, local copies, waits for them, and re-layouts: none -> 1.41 us  [the longest x4 1.37 us: by_partner(): split = blocks.reshape((count // (2 * bit), 2, bit) + blocks.shape[1:])]
  transfers between devices with their start and end apart: 2 -> 60, of which waited for: 2 -> 12; matrix products, arithmetic and copies ran while one was open for 1% -> 2% of each run, Pallas kernels for 0% -> 0%
where the time goes in v2:
time: 120 us
  starting transfers between devices  84.7 us (71%)
  waiting for transfers between devices  16.4 us (14%)
  local copies, waits for them, and re-layouts  7.95 us (7%)
  other arithmetic  5.22 us (4%)
  matrix products  4.21 us (4%)
    ppermute x60, starting transfers between devices, exchange(): got.append(lax.ppermute(out[k], 'row', [(d, d ^ k) for d in range(count)]))  84.7 us
    ppermute x60, waiting for transfers between devices, exchange(): got.append(lax.ppermute(out[k], 'row', [(d, d ^ k) for d in range(count)]))  16.4 us
    unnamed x103, local copies, waits for them, and re-layouts  4.88 us
    select_n x30, other arithmetic, by_partner(): jnp.where(me & bit != 0, split[:, ::-1], split).reshape(blocks.shape)  3.42 us
  transfers between devices with their start and end apart: 60, of which 12 were waited for; matrix products, arithmetic and copies ran while one was open for 2% of the time, Pallas kernels for 0%

profile of v2, /device:TPU:0, one launch (start us, length us, event | category | flops | bytes accessed | tf_op | source)
XLA Modules:
  0.0 119.7 jit_solution(10676278812748310392)
XLA Ops:
  0.0 1.1 copy.100
  1.3 0.8 copy-done
  2.2 0.5 copy-done.3
  2.8 0.4 fusion.11
  3.2 0.4 fusion.8
  4.9 0.3 copy.108
  5.7 0.5 collective-permute-start
  6.3 2.6 %collective-permute-start.1 = (bf16[2,8,8,128]{3,1,2,0:T(8,128)(2,1)S(1)}, bf16[2,8,8,128]{3,1,2,0:T(8,128)(2,1)S(1)}, u32[]{:S(2)}, u32[]{:S(2)}) collective-permute-start(bf16[2,8,8,128]{3,1,2,0:T(8,128)(2,1)S(1)} %bitcast.495), channel_id=1, source_target_pairs={{0,2},{1,3},{2,0},{3,1},{4,6},{5,7},{6,4},{7,5},{8,10},{9,11},{10,... | collective-permute-start | bytes 98312 | tf_op jit(solution)/shard_map/ppermute | solution.py:32
  9.0 1.7 %collective-permute-start.3 = (bf16[2,8,8,128]{3,1,2,0:T(8,128)(2,1)S(1)}, bf16[2,8,8,128]{3,1,2,0:T(8,128)(2,1)S(1)}, u32[]{:S(2)}, u32[]{:S(2)}) collective-permute-start(bf16[2,8,8,128]{3,1,2,0:T(8,128)(2,1)S(1)} %bitcast.491), channel_id=1, source_target_pairs={{0,4},{1,5},{2,6},{3,7},{4,0},{5,1},{6,2},{7,3},{8,12},{9,13},{10,... | collective-permute-start | bytes 98312 | tf_op jit(solution)/shard_map/ppermute | solution.py:32
  10.9 2.7 %collective-permute-start.5 = (bf16[2,8,8,128]{3,1,2,0:T(8,128)(2,1)S(1)}, bf16[2,8,8,128]{3,1,2,0:T(8,128)(2,1)S(1)}, u32[]{:S(2)}, u32[]{:S(2)}) collective-permute-start(bf16[2,8,8,128]{3,1,2,0:T(8,128)(2,1)S(1)} %bitcast.487), channel_id=1, source_target_pairs={{0,6},{1,7},{2,4},{3,5},{4,2},{5,3},{6,0},{7,1},{8,14},{9,15},{10,... | collective-permute-start | bytes 98312 | tf_op jit(solution)/shard_map/ppermute | solution.py:32
  13.8 2.8 %collective-permute-start.7 = (bf16[2,8,8,128]{3,1,2,0:T(8,128)(2,1)S(1)}, bf16[2,8,8,128]{3,1,2,0:T(8,128)(2,1)S(1)}, u32[]{:S(2)}, u32[]{:S(2)}) collective-permute-start(bf16[2,8,8,128]{3,1,2,0:T(8,128)(2,1)S(1)} %bitcast.483), channel_id=1, source_target_pairs={{0,8},{1,9},{2,10},{3,11},{4,12},{5,13},{6,14},{7,15},{8,0},{9,1},... | collective-permute-start | bytes 98312 | tf_op jit(solution)/shard_map/ppermute | solution.py:32
  16.7 3.6 %collective-permute-start.9 = (bf16[2,8,8,128]{3,1,2,0:T(8,128)(2,1)S(1)}, bf16[2,8,8,128]{3,1,2,0:T(8,128)(2,1)S(1)}, u32[]{:S(2)}, u32[]{:S(2)}) collective-permute-start(bf16[2,8,8,128]{3,1,2,0:T(8,128)(2,1)S(1)} %bitcast.479), channel_id=1, source_target_pairs={{0,10},{1,11},{2,8},{3,9},{4,14},{5,15},{6,12},{7,13},{8,2},{9,3},... | collective-permute-start | bytes 98312 | tf_op jit(solution)/shard_map/ppermute | solution.py:32
  20.5 3.6 %collective-permute-start.11 = (bf16[2,8,8,128]{3,1,2,0:T(8,128)(2,1)S(1)}, bf16[2,8,8,128]{3,1,2,0:T(8,128)(2,1)S(1)}, u32[]{:S(2)}, u32[]{:S(2)}) collective-permute-start(bf16[2,8,8,128]{3,1,2,0:T(8,128)(2,1)S(1)} %bitcast.475), channel_id=1, source_target_pairs={{0,12},{1,13},{2,14},{3,15},{4,8},{5,9},{6,10},{7,11},{8,4},{9,5},... | collective-permute-start | bytes 98312 | tf_op jit(solution)/shard_map/ppermute | solution.py:32
  24.2 4.5 %collective-permute-start.13 = (bf16[2,8,8,128]{3,1,2,0:T(8,128)(2,1)S(1)}, bf16[2,8,8,128]{3,1,2,0:T(8,128)(2,1)S(1)}, u32[]{:S(2)}, u32[]{:S(2)}) collective-permute-start(bf16[2,8,8,128]{3,1,2,0:T(8,128)(2,1)S(1)} %bitcast.471), channel_id=1, source_target_pairs={{0,14},{1,15},{2,12},{3,13},{4,10},{5,11},{6,8},{7,9},{8,6},{9,7},... | collective-permute-start | bytes 98312 | tf_op jit(solution)/shard_map/ppermute | solution.py:32
  29.0 0.6 collective-permute-done.12
  29.5 1.9 %collective-permute-done.13 = bf16[2,8,8,128]{3,1,2,0:T(8,128)(2,1)S(1)} collective-permute-done((bf16[2,8,8,128]{3,1,2,0:T(8,128)(2,1)S(1)}, bf16[2,8,8,128]{3,1,2,0:T(8,128)(2,1)S(1)}, u32[]{:S(2)}, u32[]{:S(2)}) %collective-permute-start.13) | collective-permute-done | bytes 32800 | tf_op jit(solution)/shard_map/ppermute | solution.py:32
  31.4 3.4 %collective-permute-done.14 = bf16[2,8,8,128]{3,1,2,0:T(8,128)(2,1)S(1)} collective-permute-done((bf16[2,8,8,128]{3,1,2,0:T(8,128)(2,1)S(1)}, bf16[2,8,8,128]{3,1,2,0:T(8,128)(2,1)S(1)}, u32[]{:S(2)}, u32[]{:S(2)}) %collective-permute-start.14) | collective-permute-done | bytes 32800 | tf_op jit(solution)/shard_map/ppermute | solution.py:32
  35.2 0.3 copy.126
  36.8 0.6 copy-done.5
  37.3 0.4 fusion.34
  38.2 0.6 collective-permute-start.16
  38.8 1.0 collective-permute-start.17
  39.8 2.0 %collective-permute-start.19 = (bf16[8,8,128]{2,1,0:T(8,128)(2,1)S(1)}, bf16[8,8,128]{2,1,0:T(8,128)(2,1)S(1)}, u32[]{:S(2)}, u32[]{:S(2)}) collective-permute-start(bf16[8,8,128]{2,1,0:T(8,128)(2,1)S(1)} %get-tuple-element.69), channel_id=1, source_target_pairs={{0,5},{1,4},{2,7},{3,6},{4,1},{5,0},{6,3},{7,2},{8,13},{9,12},{10,... | collective-permute-start | bytes 49160 | tf_op jit(solution)/shard_map/ppermute | solution.py:32
  42.1 2.1 %collective-permute-start.21 = (bf16[8,8,128]{2,1,0:T(8,128)(2,1)S(1)}, bf16[8,8,128]{2,1,0:T(8,128)(2,1)S(1)}, u32[]{:S(2)}, u32[]{:S(2)}) collective-permute-start(bf16[8,8,128]{2,1,0:T(8,128)(2,1)S(1)} %get-tuple-element.67), channel_id=1, source_target_pairs={{0,7},{1,6},{2,5},{3,4},{4,3},{5,2},{6,1},{7,0},{8,15},{9,14},{10,... | collective-permute-start | bytes 49160 | tf_op jit(solution)/shard_map/ppermute | solution.py:32
  44.2 2.9 %collective-permute-start.23 = (bf16[8,8,128]{2,1,0:T(8,128)(2,1)S(1)}, bf16[8,8,128]{2,1,0:T(8,128)(2,1)S(1)}, u32[]{:S(2)}, u32[]{:S(2)}) collective-permute-start(bf16[8,8,128]{2,1,0:T(8,128)(2,1)S(1)} %get-tuple-element.65), channel_id=1, source_target_pairs={{0,9},{1,8},{2,11},{3,10},{4,13},{5,12},{6,15},{7,14},{8,1},{9,0},... | collective-permute-start | bytes 49160 | tf_op jit(solution)/shard_map/ppermute | solution.py:32
  47.4 3.0 %collective-permute-start.25 = (bf16[8,8,128]{2,1,0:T(8,128)(2,1)S(1)}, bf16[8,8,128]{2,1,0:T(8,128)(2,1)S(1)}, u32[]{:S(2)}, u32[]{:S(2)}) collective-permute-start(bf16[8,8,128]{2,1,0:T(8,128)(2,1)S(1)} %get-tuple-element.63), channel_id=1, source_target_pairs={{0,11},{1,10},{2,9},{3,8},{4,15},{5,14},{6,13},{7,12},{8,3},{9,2},... | collective-permute-start | bytes 49160 | tf_op jit(solution)/shard_map/ppermute | solution.py:32
  50.4 0.4 collective-permute-start.26
  50.8 3.4 %collective-permute-start.27 = (bf16[8,8,128]{2,1,0:T(8,128)(2,1)S(1)}, bf16[8,8,128]{2,1,0:T(8,128)(2,1)S(1)}, u32[]{:S(2)}, u32[]{:S(2)}) collective-permute-start(bf16[8,8,128]{2,1,0:T(8,128)(2,1)S(1)} %get-tuple-element.61), channel_id=1, source_target_pairs={{0,13},{1,12},{2,15},{3,14},{4,9},{5,8},{6,11},{7,10},{8,5},{9,4},... | collective-permute-start | bytes 49160 | tf_op jit(solution)/shard_map/ppermute | solution.py:32
  54.2 0.7 collective-permute-start.28
  54.9 3.5 %collective-permute-start.29 = (bf16[8,8,128]{2,1,0:T(8,128)(2,1)S(1)}, bf16[8,8,128]{2,1,0:T(8,128)(2,1)S(1)}, u32[]{:S(2)}, u32[]{:S(2)}) collective-permute-start(bf16[8,8,128]{2,1,0:T(8,128)(2,1)S(1)} %get-tuple-element.59), channel_id=1, source_target_pairs={{0,15},{1,14},{2,13},{3,12},{4,11},{5,10},{6,9},{7,8},{8,7},{9,6},... | collective-permute-start | bytes 49160 | tf_op jit(solution)/shard_map/ppermute | solution.py:32
  58.5 2.2 %collective-permute-done.28 = bf16[8,8,128]{2,1,0:T(8,128)(2,1)S(1)} collective-permute-done((bf16[8,8,128]{2,1,0:T(8,128)(2,1)S(1)}, bf16[8,8,128]{2,1,0:T(8,128)(2,1)S(1)}, u32[]{:S(2)}, u32[]{:S(2)}) %collective-permute-start.28) | collective-permute-done | bytes 16416 | tf_op jit(solution)/shard_map/ppermute | solution.py:32
  61.5 0.3 fusion.52
  61.8 0.5 copy-done.1
  64.3 0.3 copy.139
  65.3 1.3 %collective-permute-start.31 = (bf16[2,8,8,128]{3,1,2,0:T(8,128)(2,1)S(1)}, bf16[2,8,8,128]{3,1,2,0:T(8,128)(2,1)S(1)}, u32[]{:S(2)}, u32[]{:S(2)}) collective-permute-start(bf16[2,8,8,128]{3,1,2,0:T(8,128)(2,1)S(1)} %bitcast.496), channel_id=1, source_target_pairs={{0,2},{1,3},{2,0},{3,1},{4,6},{5,7},{6,4},{7,5},{8,10},{9,11},{10,... | collective-permute-start | bytes 98312 | tf_op jit(solution)/shard_map/ppermute | solution.py:32
  66.7 0.5 collective-permute-start.32
  67.2 1.7 %collective-permute-start.34 = (bf16[2,8,8,128]{3,1,2,0:T(8,128)(2,1)S(1)}, bf16[2,8,8,128]{3,1,2,0:T(8,128)(2,1)S(1)}, u32[]{:S(2)}, u32[]{:S(2)}) collective-permute-start(bf16[2,8,8,128]{3,1,2,0:T(8,128)(2,1)S(1)} %bitcast.490), channel_id=1, source_target_pairs={{0,5},{1,4},{2,7},{3,6},{4,1},{5,0},{6,3},{7,2},{8,13},{9,12},{10,... | collective-permute-start | bytes 98312 | tf_op jit(solution)/shard_map/ppermute | solution.py:32
  69.1 1.1 collective-permute-start.35
  70.2 1.7 %collective-permute-start.36 = (bf16[2,8,8,128]{3,1,2,0:T(8,128)(2,1)S(1)}, bf16[2,8,8,128]{3,1,2,0:T(8,128)(2,1)S(1)}, u32[]{:S(2)}, u32[]{:S(2)}) collective-permute-start(bf16[2,8,8,128]{3,1,2,0:T(8,128)(2,1)S(1)} %bitcast.486), channel_id=1, source_target_pairs={{0,7},{1,6},{2,5},{3,4},{4,3},{5,2},{6,1},{7,0},{8,15},{9,14},{10,... | collective-permute-start | bytes 98312 | tf_op jit(solution)/shard_map/ppermute | solution.py:32
  71.9 2.0 %collective-permute-start.37 = (bf16[2,8,8,128]{3,1,2,0:T(8,128)(2,1)S(1)}, bf16[2,8,8,128]{3,1,2,0:T(8,128)(2,1)S(1)}, u32[]{:S(2)}, u32[]{:S(2)}) collective-permute-start(bf16[2,8,8,128]{3,1,2,0:T(8,128)(2,1)S(1)} %bitcast.484), channel_id=1, source_target_pairs={{0,8},{1,9},{2,10},{3,11},{4,12},{5,13},{6,14},{7,15},{8,0},{9,1},... | collective-permute-start | bytes 98312 | tf_op jit(solution)/shard_map/ppermute | solution.py:32
  73.9 0.8 collective-permute-start.38
  74.7 3.0 %collective-permute-start.39 = (bf16[2,8,8,128]{3,1,2,0:T(8,128)(2,1)S(1)}, bf16[2,8,8,128]{3,1,2,0:T(8,128)(2,1)S(1)}, u32[]{:S(2)}, u32[]{:S(2)}) collective-permute-start(bf16[2,8,8,128]{3,1,2,0:T(8,128)(2,1)S(1)} %bitcast.480), channel_id=1, source_target_pairs={{0,10},{1,11},{2,8},{3,9},{4,14},{5,15},{6,12},{7,13},{8,2},{9,3},... | collective-permute-start | bytes 98312 | tf_op jit(solution)/shard_map/ppermute | solution.py:32
  77.7 0.7 collective-permute-start.40
  78.5 3.1 %collective-permute-start.41 = (bf16[2,8,8,128]{3,1,2,0:T(8,128)(2,1)S(1)}, bf16[2,8,8,128]{3,1,2,0:T(8,128)(2,1)S(1)}, u32[]{:S(2)}, u32[]{:S(2)}) collective-permute-start(bf16[2,8,8,128]{3,1,2,0:T(8,128)(2,1)S(1)} %bitcast.476), channel_id=1, source_target_pairs={{0,12},{1,13},{2,14},{3,15},{4,8},{5,9},{6,10},{7,11},{8,4},{9,5},... | collective-permute-start | bytes 98312 | tf_op jit(solution)/shard_map/ppermute | solution.py:32
  81.6 0.6 collective-permute-start.42
  82.2 4.1 %collective-permute-start.43 = (bf16[2,8,8,128]{3,1,2,0:T(8,128)(2,1)S(1)}, bf16[2,8,8,128]{3,1,2,0:T(8,128)(2,1)S(1)}, u32[]{:S(2)}, u32[]{:S(2)}) collective-permute-start(bf16[2,8,8,128]{3,1,2,0:T(8,128)(2,1)S(1)} %bitcast.472), channel_id=1, source_target_pairs={{0,14},{1,15},{2,12},{3,13},{4,10},{5,11},{6,8},{7,9},{8,6},{9,7},... | collective-permute-start | bytes 98312 | tf_op jit(solution)/shard_map/ppermute | solution.py:32
  86.3 0.5 collective-permute-start.44
  87.0 1.9 %collective-permute-done.43 = bf16[2,8,8,128]{3,1,2,0:T(8,128)(2,1)S(1)} collective-permute-done((bf16[2,8,8,128]{3,1,2,0:T(8,128)(2,1)S(1)}, bf16[2,8,8,128]{3,1,2,0:T(8,128)(2,1)S(1)}, u32[]{:S(2)}, u32[]{:S(2)}) %collective-permute-start.43) | collective-permute-done | bytes 32800 | tf_op jit(solution)/shard_map/ppermute | solution.py:32
  88.9 3.6 %collective-permute-done.44 = bf16[2,8,8,128]{3,1,2,0:T(8,128)(2,1)S(1)} collective-permute-done((bf16[2,8,8,128]{3,1,2,0:T(8,128)(2,1)S(1)}, bf16[2,8,8,128]{3,1,2,0:T(8,128)(2,1)S(1)}, u32[]{:S(2)}, u32[]{:S(2)}) %collective-permute-start.44) | collective-permute-done | bytes 32800 | tf_op jit(solution)/shard_map/ppermute | solution.py:32
  93.0 0.3 copy.157
  94.5 0.3 fusion.32
  94.8 0.4 collective-permute-start.46
  95.3 1.4 %collective-permute-start.47 = (bf16[8,8,128]{2,1,0:T(8,128)(2,1)S(1)}, bf16[8,8,128]{2,1,0:T(8,128)(2,1)S(1)}, u32[]{:S(2)}, u32[]{:S(2)}) collective-permute-start(bf16[8,8,128]{2,1,0:T(8,128)(2,1)S(1)} %get-tuple-element.53), channel_id=1, source_target_pairs={{0,3},{1,2},{2,1},{3,0},{4,7},{5,6},{6,5},{7,4},{8,11},{9,10},{10,... | collective-permute-start | bytes 49160 | tf_op jit(solution)/shard_map/ppermute | solution.py:32
  96.7 1.7 %collective-permute-start.49 = (bf16[8,8,128]{2,1,0:T(8,128)(2,1)S(1)}, bf16[8,8,128]{2,1,0:T(8,128)(2,1)S(1)}, u32[]{:S(2)}, u32[]{:S(2)}) collective-permute-start(bf16[8,8,128]{2,1,0:T(8,128)(2,1)S(1)} %get-tuple-element.51), channel_id=1, source_target_pairs={{0,5},{1,4},{2,7},{3,6},{4,1},{5,0},{6,3},{7,2},{8,13},{9,12},{10,... | collective-permute-start | bytes 49160 | tf_op jit(solution)/shard_map/ppermute | solution.py:32
  98.6 2.5 %collective-permute-start.51 = (bf16[8,8,128]{2,1,0:T(8,128)(2,1)S(1)}, bf16[8,8,128]{2,1,0:T(8,128)(2,1)S(1)}, u32[]{:S(2)}, u32[]{:S(2)}) collective-permute-start(bf16[8,8,128]{2,1,0:T(8,128)(2,1)S(1)} %get-tuple-element.49), channel_id=1, source_target_pairs={{0,7},{1,6},{2,5},{3,4},{4,3},{5,2},{6,1},{7,0},{8,15},{9,14},{10,... | collective-permute-start | bytes 49160 | tf_op jit(solution)/shard_map/ppermute | solution.py:32
  101.1 2.6 %collective-permute-start.53 = (bf16[8,8,128]{2,1,0:T(8,128)(2,1)S(1)}, bf16[8,8,128]{2,1,0:T(8,128)(2,1)S(1)}, u32[]{:S(2)}, u32[]{:S(2)}) collective-permute-start(bf16[8,8,128]{2,1,0:T(8,128)(2,1)S(1)} %get-tuple-element.47), channel_id=1, source_target_pairs={{0,9},{1,8},{2,11},{3,10},{4,13},{5,12},{6,15},{7,14},{8,1},{9,0},... | collective-permute-start | bytes 49160 | tf_op jit(solution)/shard_map/ppermute | solution.py:32
  104.0 3.4 %collective-permute-start.55 = (bf16[8,8,128]{2,1,0:T(8,128)(2,1)S(1)}, bf16[8,8,128]{2,1,0:T(8,128)(2,1)S(1)}, u32[]{:S(2)}, u32[]{:S(2)}) collective-permute-start(bf16[8,8,128]{2,1,0:T(8,128)(2,1)S(1)} %get-tuple-element.45), channel_id=1, source_target_pairs={{0,11},{1,10},{2,9},{3,8},{4,15},{5,14},{6,13},{7,12},{8,3},{9,2},... | collective-permute-start | bytes 49160 | tf_op jit(solution)/shard_map/ppermute | solution.py:32
  107.7 3.2 %collective-permute-start.57 = (bf16[8,8,128]{2,1,0:T(8,128)(2,1)S(1)}, bf16[8,8,128]{2,1,0:T(8,128)(2,1)S(1)}, u32[]{:S(2)}, u32[]{:S(2)}) collective-permute-start(bf16[8,8,128]{2,1,0:T(8,128)(2,1)S(1)} %get-tuple-element.43), channel_id=1, source_target_pairs={{0,13},{1,12},{2,15},{3,14},{4,9},{5,8},{6,11},{7,10},{8,5},{9,4},... | collective-permute-start | bytes 49160 | tf_op jit(solution)/shard_map/ppermute | solution.py:32
  110.9 0.9 collective-permute-start.58
  111.8 3.6 %collective-permute-start.59 = (bf16[8,8,128]{2,1,0:T(8,128)(2,1)S(1)}, bf16[8,8,128]{2,1,0:T(8,128)(2,1)S(1)}, u32[]{:S(2)}, u32[]{:S(2)}) collective-permute-start(bf16[8,8,128]{2,1,0:T(8,128)(2,1)S(1)} %get-tuple-element.41), channel_id=1, source_target_pairs={{0,15},{1,14},{2,13},{3,12},{4,11},{5,10},{6,9},{7,8},{8,7},{9,6},... | collective-permute-start | bytes 49160 | tf_op jit(solution)/shard_map/ppermute | solution.py:32
  115.4 1.9 %collective-permute-done.58 = bf16[8,8,128]{2,1,0:T(8,128)(2,1)S(1)} collective-permute-done((bf16[8,8,128]{2,1,0:T(8,128)(2,1)S(1)}, bf16[8,8,128]{2,1,0:T(8,128)(2,1)S(1)}, u32[]{:S(2)}, u32[]{:S(2)}) %collective-permute-start.58) | collective-permute-done | bytes 16416 | tf_op jit(solution)/shard_map/ppermute | solution.py:32
  117.3 0.4 collective-permute-done.59
  118.2 0.3 fusion.48
  118.8 0.9 copy.164
  (245 shorter events, 12.7 us)
Async XLA Ops:
  1.1 1.0 copy-start
  3.2 0.7 copy-start.2
  5.7 5.2 %collective-permute-start = (bf16[2,8,8,128]{3,1,2,0:T(8,128)(2,1)S(1)}, bf16[2,8,8,128]{3,1,2,0:T(8,128)(2,1)S(1)}, u32[]{:S(2)}, u32[]{:S(2)}) collective-permute-start(bf16[2,8,8,128]{3,1,2,0:T(8,128)(2,1)S(1)} %bitcast.497), channel_id=1, source_target_pairs={{0,1},{1,0},{2,3},{3,2},{4,5},{5,4},{6,7},{7,6},{8,9},{9,8},{10,11... | collective-permute-start | bytes 98312 | tf_op jit(solution)/shard_map/ppermute | solution.py:32
  6.3 7.4 %collective-permute-start.1 = (bf16[2,8,8,128]{3,1,2,0:T(8,128)(2,1)S(1)}, bf16[2,8,8,128]{3,1,2,0:T(8,128)(2,1)S(1)}, u32[]{:S(2)}, u32[]{:S(2)}) collective-permute-start(bf16[2,8,8,128]{3,1,2,0:T(8,128)(2,1)S(1)} %bitcast.495), channel_id=1, source_target_pairs={{0,2},{1,3},{2,0},{3,1},{4,6},{5,7},{6,4},{7,5},{8,10},{9,11},{10,... | collective-permute-start | bytes 98312 | tf_op jit(solution)/shard_map/ppermute | solution.py:32
  8.9 4.9 %collective-permute-start.2 = (bf16[2,8,8,128]{3,1,2,0:T(8,128)(2,1)S(1)}, bf16[2,8,8,128]{3,1,2,0:T(8,128)(2,1)S(1)}, u32[]{:S(2)}, u32[]{:S(2)}) collective-permute-start(bf16[2,8,8,128]{3,1,2,0:T(8,128)(2,1)S(1)} %bitcast.493), channel_id=1, source_target_pairs={{0,3},{1,2},{2,1},{3,0},{4,7},{5,6},{6,5},{7,4},{8,11},{9,10},{10,... | collective-permute-start | bytes 98312 | tf_op jit(solution)/shard_map/ppermute | solution.py:32
  9.0 7.6 %collective-permute-start.3 = (bf16[2,8,8,128]{3,1,2,0:T(8,128)(2,1)S(1)}, bf16[2,8,8,128]{3,1,2,0:T(8,128)(2,1)S(1)}, u32[]{:S(2)}, u32[]{:S(2)}) collective-permute-start(bf16[2,8,8,128]{3,1,2,0:T(8,128)(2,1)S(1)} %bitcast.491), channel_id=1, source_target_pairs={{0,4},{1,5},{2,6},{3,7},{4,0},{5,1},{6,2},{7,3},{8,12},{9,13},{10,... | collective-permute-start | bytes 98312 | tf_op jit(solution)/shard_map/ppermute | solution.py:32
  10.7 6.0 %collective-permute-start.4 = (bf16[2,8,8,128]{3,1,2,0:T(8,128)(2,1)S(1)}, bf16[2,8,8,128]{3,1,2,0:T(8,128)(2,1)S(1)}, u32[]{:S(2)}, u32[]{:S(2)}) collective-permute-start(bf16[2,8,8,128]{3,1,2,0:T(8,128)(2,1)S(1)} %bitcast.489), channel_id=1, source_target_pairs={{0,5},{1,4},{2,7},{3,6},{4,1},{5,0},{6,3},{7,2},{8,13},{9,12},{10,... | collective-permute-start | bytes 98312 | tf_op jit(solution)/shard_map/ppermute | solution.py:32
  10.9 9.4 %collective-permute-start.5 = (bf16[2,8,8,128]{3,1,2,0:T(8,128)(2,1)S(1)}, bf16[2,8,8,128]{3,1,2,0:T(8,128)(2,1)S(1)}, u32[]{:S(2)}, u32[]{:S(2)}) collective-permute-start(bf16[2,8,8,128]{3,1,2,0:T(8,128)(2,1)S(1)} %bitcast.487), channel_id=1, source_target_pairs={{0,6},{1,7},{2,4},{3,5},{4,2},{5,3},{6,0},{7,1},{8,14},{9,15},{10,... | collective-permute-start | bytes 98312 | tf_op jit(solution)/shard_map/ppermute | solution.py:32
  13.6 6.8 %collective-permute-start.6 = (bf16[2,8,8,128]{3,1,2,0:T(8,128)(2,1)S(1)}, bf16[2,8,8,128]{3,1,2,0:T(8,128)(2,1)S(1)}, u32[]{:S(2)}, u32[]{:S(2)}) collective-permute-start(bf16[2,8,8,128]{3,1,2,0:T(8,128)(2,1)S(1)} %bitcast.485), channel_id=1, source_target_pairs={{0,7},{1,6},{2,5},{3,4},{4,3},{5,2},{6,1},{7,0},{8,15},{9,14},{10,... | collective-permute-start | bytes 98312 | tf_op jit(solution)/shard_map/ppermute | solution.py:32
  13.8 10.3 %collective-permute-start.7 = (bf16[2,8,8,128]{3,1,2,0:T(8,128)(2,1)S(1)}, bf16[2,8,8,128]{3,1,2,0:T(8,128)(2,1)S(1)}, u32[]{:S(2)}, u32[]{:S(2)}) collective-permute-start(bf16[2,8,8,128]{3,1,2,0:T(8,128)(2,1)S(1)} %bitcast.483), channel_id=1, source_target_pairs={{0,8},{1,9},{2,10},{3,11},{4,12},{5,13},{6,14},{7,15},{8,0},{9,1},... | collective-permute-start | bytes 98312 | tf_op jit(solution)/shard_map/ppermute | solution.py:32
  16.6 7.6 %collective-permute-start.8 = (bf16[2,8,8,128]{3,1,2,0:T(8,128)(2,1)S(1)}, bf16[2,8,8,128]{3,1,2,0:T(8,128)(2,1)S(1)}, u32[]{:S(2)}, u32[]{:S(2)}) collective-permute-start(bf16[2,8,8,128]{3,1,2,0:T(8,128)(2,1)S(1)} %bitcast.481), channel_id=1, source_target_pairs={{0,9},{1,8},{2,11},{3,10},{4,13},{5,12},{6,15},{7,14},{8,1},{9,0},... | collective-permute-start | bytes 98312 | tf_op jit(solution)/shard_map/ppermute | solution.py:32
  16.7 12.0 %collective-permute-start.9 = (bf16[2,8,8,128]{3,1,2,0:T(8,128)(2,1)S(1)}, bf16[2,8,8,128]{3,1,2,0:T(8,128)(2,1)S(1)}, u32[]{:S(2)}, u32[]{:S(2)}) collective-permute-start(bf16[2,8,8,128]{3,1,2,0:T(8,128)(2,1)S(1)} %bitcast.479), channel_id=1, source_target_pairs={{0,10},{1,11},{2,8},{3,9},{4,14},{5,15},{6,12},{7,13},{8,2},{9,3},... | collective-permute-start | bytes 98312 | tf_op jit(solution)/shard_map/ppermute | solution.py:32
  20.3 8.6 %collective-permute-start.10 = (bf16[2,8,8,128]{3,1,2,0:T(8,128)(2,1)S(1)}, bf16[2,8,8,128]{3,1,2,0:T(8,128)(2,1)S(1)}, u32[]{:S(2)}, u32[]{:S(2)}) collective-permute-start(bf16[2,8,8,128]{3,1,2,0:T(8,128)(2,1)S(1)} %bitcast.477), channel_id=1, source_target_pairs={{0,11},{1,10},{2,9},{3,8},{4,15},{5,14},{6,13},{7,12},{8,3},{9,2},... | collective-permute-start | bytes 98312 | tf_op jit(solution)/shard_map/ppermute | solution.py:32
  20.5 8.4 %collective-permute-start.11 = (bf16[2,8,8,128]{3,1,2,0:T(8,128)(2,1)S(1)}, bf16[2,8,8,128]{3,1,2,0:T(8,128)(2,1)S(1)}, u32[]{:S(2)}, u32[]{:S(2)}) collective-permute-start(bf16[2,8,8,128]{3,1,2,0:T(8,128)(2,1)S(1)} %bitcast.475), channel_id=1, source_target_pairs={{0,12},{1,13},{2,14},{3,15},{4,8},{5,9},{6,10},{7,11},{8,4},{9,5},... | collective-permute-start | bytes 98312 | tf_op jit(solution)/shard_map/ppermute | solution.py:32
  24.1 5.4 %collective-permute-start.12 = (bf16[2,8,8,128]{3,1,2,0:T(8,128)(2,1)S(1)}, bf16[2,8,8,128]{3,1,2,0:T(8,128)(2,1)S(1)}, u32[]{:S(2)}, u32[]{:S(2)}) collective-permute-start(bf16[2,8,8,128]{3,1,2,0:T(8,128)(2,1)S(1)} %bitcast.473), channel_id=1, source_target_pairs={{0,13},{1,12},{2,15},{3,14},{4,9},{5,8},{6,11},{7,10},{8,5},{9,4},... | collective-permute-start | bytes 98312 | tf_op jit(solution)/shard_map/ppermute | solution.py:32
  24.2 7.2 %collective-permute-start.13 = (bf16[2,8,8,128]{3,1,2,0:T(8,128)(2,1)S(1)}, bf16[2,8,8,128]{3,1,2,0:T(8,128)(2,1)S(1)}, u32[]{:S(2)}, u32[]{:S(2)}) collective-permute-start(bf16[2,8,8,128]{3,1,2,0:T(8,128)(2,1)S(1)} %bitcast.471), channel_id=1, source_target_pairs={{0,14},{1,15},{2,12},{3,13},{4,10},{5,11},{6,8},{7,9},{8,6},{9,7},... | collective-permute-start | bytes 98312 | tf_op jit(solution)/shard_map/ppermute | solution.py:32
  28.8 6.1 %collective-permute-start.14 = (bf16[2,8,8,128]{3,1,2,0:T(8,128)(2,1)S(1)}, bf16[2,8,8,128]{3,1,2,0:T(8,128)(2,1)S(1)}, u32[]{:S(2)}, u32[]{:S(2)}) collective-permute-start(bf16[2,8,8,128]{3,1,2,0:T(8,128)(2,1)S(1)} %bitcast.469), channel_id=1, source_target_pairs={{0,15},{1,14},{2,13},{3,12},{4,11},{5,10},{6,9},{7,8},{8,7},{9,6},... | collective-permute-start | bytes 98312 | tf_op jit(solution)/shard_map/ppermute | solution.py:32
  36.5 0.8 copy-start.5
  36.5 5.2 %collective-permute-start.15 = (bf16[8,8,128]{2,1,0:T(8,128)(2,1)S(1)}, bf16[8,8,128]{2,1,0:T(8,128)(2,1)S(1)}, u32[]{:S(2)}, u32[]{:S(2)}) collective-permute-start(bf16[8,8,128]{2,1,0:T(8,128)(2,1)S(1)} %get-tuple-element.73), channel_id=1, source_target_pairs={{0,1},{1,0},{2,3},{3,2},{4,5},{5,4},{6,7},{7,6},{8,9},{9,8},{10,11... | collective-permute-start | bytes 49160 | tf_op jit(solution)/shard_map/ppermute | solution.py:32
  38.2 3.9 %collective-permute-start.16 = (bf16[8,8,128]{2,1,0:T(8,128)(2,1)S(1)}, bf16[8,8,128]{2,1,0:T(8,128)(2,1)S(1)}, u32[]{:S(2)}, u32[]{:S(2)}) collective-permute-start(bf16[8,8,128]{2,1,0:T(8,128)(2,1)S(1)} %get-tuple-element.72), channel_id=1, source_target_pairs={{0,2},{1,3},{2,0},{3,1},{4,6},{5,7},{6,4},{7,5},{8,10},{9,11},{10,... | collective-permute-start | bytes 49160 | tf_op jit(solution)/shard_map/ppermute | solution.py:32
  38.8 5.4 %collective-permute-start.17 = (bf16[8,8,128]{2,1,0:T(8,128)(2,1)S(1)}, bf16[8,8,128]{2,1,0:T(8,128)(2,1)S(1)}, u32[]{:S(2)}, u32[]{:S(2)}) collective-permute-start(bf16[8,8,128]{2,1,0:T(8,128)(2,1)S(1)} %get-tuple-element.71), channel_id=1, source_target_pairs={{0,3},{1,2},{2,1},{3,0},{4,7},{5,6},{6,5},{7,4},{8,11},{9,10},{10,... | collective-permute-start | bytes 49160 | tf_op jit(solution)/shard_map/ppermute | solution.py:32
  39.8 4.4 %collective-permute-start.18 = (bf16[8,8,128]{2,1,0:T(8,128)(2,1)S(1)}, bf16[8,8,128]{2,1,0:T(8,128)(2,1)S(1)}, u32[]{:S(2)}, u32[]{:S(2)}) collective-permute-start(bf16[8,8,128]{2,1,0:T(8,128)(2,1)S(1)} %get-tuple-element.70), channel_id=1, source_target_pairs={{0,4},{1,5},{2,6},{3,7},{4,0},{5,1},{6,2},{7,3},{8,12},{9,13},{10,... | collective-permute-start | bytes 49160 | tf_op jit(solution)/shard_map/ppermute | solution.py:32
  39.8 7.3 %collective-permute-start.19 = (bf16[8,8,128]{2,1,0:T(8,128)(2,1)S(1)}, bf16[8,8,128]{2,1,0:T(8,128)(2,1)S(1)}, u32[]{:S(2)}, u32[]{:S(2)}) collective-permute-start(bf16[8,8,128]{2,1,0:T(8,128)(2,1)S(1)} %get-tuple-element.69), channel_id=1, source_target_pairs={{0,5},{1,4},{2,7},{3,6},{4,1},{5,0},{6,3},{7,2},{8,13},{9,12},{10,... | collective-permute-start | bytes 49160 | tf_op jit(solution)/shard_map/ppermute | solution.py:32
  41.7 5.7 %collective-permute-start.20 = (bf16[8,8,128]{2,1,0:T(8,128)(2,1)S(1)}, bf16[8,8,128]{2,1,0:T(8,128)(2,1)S(1)}, u32[]{:S(2)}, u32[]{:S(2)}) collective-permute-start(bf16[8,8,128]{2,1,0:T(8,128)(2,1)S(1)} %get-tuple-element.68), channel_id=1, source_target_pairs={{0,6},{1,7},{2,4},{3,5},{4,2},{5,3},{6,0},{7,1},{8,14},{9,15},{10,... | collective-permute-start | bytes 49160 | tf_op jit(solution)/shard_map/ppermute | solution.py:32
  42.1 8.3 %collective-permute-start.21 = (bf16[8,8,128]{2,1,0:T(8,128)(2,1)S(1)}, bf16[8,8,128]{2,1,0:T(8,128)(2,1)S(1)}, u32[]{:S(2)}, u32[]{:S(2)}) collective-permute-start(bf16[8,8,128]{2,1,0:T(8,128)(2,1)S(1)} %get-tuple-element.67), channel_id=1, source_target_pairs={{0,7},{1,6},{2,5},{3,4},{4,3},{5,2},{6,1},{7,0},{8,15},{9,14},{10,... | collective-permute-start | bytes 49160 | tf_op jit(solution)/shard_map/ppermute | solution.py:32
  44.2 6.6 %collective-permute-start.22 = (bf16[8,8,128]{2,1,0:T(8,128)(2,1)S(1)}, bf16[8,8,128]{2,1,0:T(8,128)(2,1)S(1)}, u32[]{:S(2)}, u32[]{:S(2)}) collective-permute-start(bf16[8,8,128]{2,1,0:T(8,128)(2,1)S(1)} %get-tuple-element.66), channel_id=1, source_target_pairs={{0,8},{1,9},{2,10},{3,11},{4,12},{5,13},{6,14},{7,15},{8,0},{9,1},... | collective-permute-start | bytes 49160 | tf_op jit(solution)/shard_map/ppermute | solution.py:32
  44.2 10.0 %collective-permute-start.23 = (bf16[8,8,128]{2,1,0:T(8,128)(2,1)S(1)}, bf16[8,8,128]{2,1,0:T(8,128)(2,1)S(1)}, u32[]{:S(2)}, u32[]{:S(2)}) collective-permute-start(bf16[8,8,128]{2,1,0:T(8,128)(2,1)S(1)} %get-tuple-element.65), channel_id=1, source_target_pairs={{0,9},{1,8},{2,11},{3,10},{4,13},{5,12},{6,15},{7,14},{8,1},{9,0},... | collective-permute-start | bytes 49160 | tf_op jit(solution)/shard_map/ppermute | solution.py:32
  47.1 7.8 %collective-permute-start.24 = (bf16[8,8,128]{2,1,0:T(8,128)(2,1)S(1)}, bf16[8,8,128]{2,1,0:T(8,128)(2,1)S(1)}, u32[]{:S(2)}, u32[]{:S(2)}) collective-permute-start(bf16[8,8,128]{2,1,0:T(8,128)(2,1)S(1)} %get-tuple-element.64), channel_id=1, source_target_pairs={{0,10},{1,11},{2,8},{3,9},{4,14},{5,15},{6,12},{7,13},{8,2},{9,3},... | collective-permute-start | bytes 49160 | tf_op jit(solution)/shard_map/ppermute | solution.py:32
  47.4 11.1 %collective-permute-start.25 = (bf16[8,8,128]{2,1,0:T(8,128)(2,1)S(1)}, bf16[8,8,128]{2,1,0:T(8,128)(2,1)S(1)}, u32[]{:S(2)}, u32[]{:S(2)}) collective-permute-start(bf16[8,8,128]{2,1,0:T(8,128)(2,1)S(1)} %get-tuple-element.63), channel_id=1, source_target_pairs={{0,11},{1,10},{2,9},{3,8},{4,15},{5,14},{6,13},{7,12},{8,3},{9,2},... | collective-permute-start | bytes 49160 | tf_op jit(solution)/shard_map/ppermute | solution.py:32
  50.4 8.0 %collective-permute-start.26 = (bf16[8,8,128]{2,1,0:T(8,128)(2,1)S(1)}, bf16[8,8,128]{2,1,0:T(8,128)(2,1)S(1)}, u32[]{:S(2)}, u32[]{:S(2)}) collective-permute-start(bf16[8,8,128]{2,1,0:T(8,128)(2,1)S(1)} %get-tuple-element.62), channel_id=1, source_target_pairs={{0,12},{1,13},{2,14},{3,15},{4,8},{5,9},{6,10},{7,11},{8,4},{9,5},... | collective-permute-start | bytes 49160 | tf_op jit(solution)/shard_map/ppermute | solution.py:32
  50.8 7.7 %collective-permute-start.27 = (bf16[8,8,128]{2,1,0:T(8,128)(2,1)S(1)}, bf16[8,8,128]{2,1,0:T(8,128)(2,1)S(1)}, u32[]{:S(2)}, u32[]{:S(2)}) collective-permute-start(bf16[8,8,128]{2,1,0:T(8,128)(2,1)S(1)} %get-tuple-element.61), channel_id=1, source_target_pairs={{0,13},{1,12},{2,15},{3,14},{4,9},{5,8},{6,11},{7,10},{8,5},{9,4},... | collective-permute-start | bytes 49160 | tf_op jit(solution)/shard_map/ppermute | solution.py:32
  54.2 6.5 %collective-permute-start.28 = (bf16[8,8,128]{2,1,0:T(8,128)(2,1)S(1)}, bf16[8,8,128]{2,1,0:T(8,128)(2,1)S(1)}, u32[]{:S(2)}, u32[]{:S(2)}) collective-permute-start(bf16[8,8,128]{2,1,0:T(8,128)(2,1)S(1)} %get-tuple-element.60), channel_id=1, source_target_pairs={{0,14},{1,15},{2,12},{3,13},{4,10},{5,11},{6,8},{7,9},{8,6},{9,7},... | collective-permute-start | bytes 49160 | tf_op jit(solution)/shard_map/ppermute | solution.py:32
  54.9 6.0 %collective-permute-start.29 = (bf16[8,8,128]{2,1,0:T(8,128)(2,1)S(1)}, bf16[8,8,128]{2,1,0:T(8,128)(2,1)S(1)}, u32[]{:S(2)}, u32[]{:S(2)}) collective-permute-start(bf16[8,8,128]{2,1,0:T(8,128)(2,1)S(1)} %get-tuple-element.59), channel_id=1, source_target_pairs={{0,15},{1,14},{2,13},{3,12},{4,11},{5,10},{6,9},{7,8},{8,7},{9,6},... | collective-permute-start | bytes 49160 | tf_op jit(solution)/shard_map/ppermute | solution.py:32
  61.5 0.8 copy-start.1
  65.1 3.9 %collective-permute-start.30 = (bf16[2,8,8,128]{3,1,2,0:T(8,128)(2,1)S(1)}, bf16[2,8,8,128]{3,1,2,0:T(8,128)(2,1)S(1)}, u32[]{:S(2)}, u32[]{:S(2)}) collective-permute-start(bf16[2,8,8,128]{3,1,2,0:T(8,128)(2,1)S(1)} %bitcast.498), channel_id=1, source_target_pairs={{0,1},{1,0},{2,3},{3,2},{4,5},{5,4},{6,7},{7,6},{8,9},{9,8},{10,11... | collective-permute-start | bytes 98312 | tf_op jit(solution)/shard_map/ppermute | solution.py:32
  65.3 4.9 %collective-permute-start.31 = (bf16[2,8,8,128]{3,1,2,0:T(8,128)(2,1)S(1)}, bf16[2,8,8,128]{3,1,2,0:T(8,128)(2,1)S(1)}, u32[]{:S(2)}, u32[]{:S(2)}) collective-permute-start(bf16[2,8,8,128]{3,1,2,0:T(8,128)(2,1)S(1)} %bitcast.496), channel_id=1, source_target_pairs={{0,2},{1,3},{2,0},{3,1},{4,6},{5,7},{6,4},{7,5},{8,10},{9,11},{10,... | collective-permute-start | bytes 98312 | tf_op jit(solution)/shard_map/ppermute | solution.py:32
  66.7 5.3 %collective-permute-start.32 = (bf16[2,8,8,128]{3,1,2,0:T(8,128)(2,1)S(1)}, bf16[2,8,8,128]{3,1,2,0:T(8,128)(2,1)S(1)}, u32[]{:S(2)}, u32[]{:S(2)}) collective-permute-start(bf16[2,8,8,128]{3,1,2,0:T(8,128)(2,1)S(1)} %bitcast.494), channel_id=1, source_target_pairs={{0,3},{1,2},{2,1},{3,0},{4,7},{5,6},{6,5},{7,4},{8,11},{9,10},{10,... | collective-permute-start | bytes 98312 | tf_op jit(solution)/shard_map/ppermute | solution.py:32
  67.2 6.7 %collective-permute-start.33 = (bf16[2,8,8,128]{3,1,2,0:T(8,128)(2,1)S(1)}, bf16[2,8,8,128]{3,1,2,0:T(8,128)(2,1)S(1)}, u32[]{:S(2)}, u32[]{:S(2)}) collective-permute-start(bf16[2,8,8,128]{3,1,2,0:T(8,128)(2,1)S(1)} %bitcast.492), channel_id=1, source_target_pairs={{0,4},{1,5},{2,6},{3,7},{4,0},{5,1},{6,2},{7,3},{8,12},{9,13},{10,... | collective-permute-start | bytes 98312 | tf_op jit(solution)/shard_map/ppermute | solution.py:32
  67.2 7.5 %collective-permute-start.34 = (bf16[2,8,8,128]{3,1,2,0:T(8,128)(2,1)S(1)}, bf16[2,8,8,128]{3,1,2,0:T(8,128)(2,1)S(1)}, u32[]{:S(2)}, u32[]{:S(2)}) collective-permute-start(bf16[2,8,8,128]{3,1,2,0:T(8,128)(2,1)S(1)} %bitcast.490), channel_id=1, source_target_pairs={{0,5},{1,4},{2,7},{3,6},{4,1},{5,0},{6,3},{7,2},{8,13},{9,12},{10,... | collective-permute-start | bytes 98312 | tf_op jit(solution)/shard_map/ppermute | solution.py:32
  69.1 8.6 %collective-permute-start.35 = (bf16[2,8,8,128]{3,1,2,0:T(8,128)(2,1)S(1)}, bf16[2,8,8,128]{3,1,2,0:T(8,128)(2,1)S(1)}, u32[]{:S(2)}, u32[]{:S(2)}) collective-permute-start(bf16[2,8,8,128]{3,1,2,0:T(8,128)(2,1)S(1)} %bitcast.488), channel_id=1, source_target_pairs={{0,6},{1,7},{2,4},{3,5},{4,2},{5,3},{6,0},{7,1},{8,14},{9,15},{10,... | collective-permute-start | bytes 98312 | tf_op jit(solution)/shard_map/ppermute | solution.py:32
  70.2 8.3 %collective-permute-start.36 = (bf16[2,8,8,128]{3,1,2,0:T(8,128)(2,1)S(1)}, bf16[2,8,8,128]{3,1,2,0:T(8,128)(2,1)S(1)}, u32[]{:S(2)}, u32[]{:S(2)}) collective-permute-start(bf16[2,8,8,128]{3,1,2,0:T(8,128)(2,1)S(1)} %bitcast.486), channel_id=1, source_target_pairs={{0,7},{1,6},{2,5},{3,4},{4,3},{5,2},{6,1},{7,0},{8,15},{9,14},{10,... | collective-permute-start | bytes 98312 | tf_op jit(solution)/shard_map/ppermute | solution.py:32
  71.9 9.6 %collective-permute-start.37 = (bf16[2,8,8,128]{3,1,2,0:T(8,128)(2,1)S(1)}, bf16[2,8,8,128]{3,1,2,0:T(8,128)(2,1)S(1)}, u32[]{:S(2)}, u32[]{:S(2)}) collective-permute-start(bf16[2,8,8,128]{3,1,2,0:T(8,128)(2,1)S(1)} %bitcast.484), channel_id=1, source_target_pairs={{0,8},{1,9},{2,10},{3,11},{4,12},{5,13},{6,14},{7,15},{8,0},{9,1},... | collective-permute-start | bytes 98312 | tf_op jit(solution)/shard_map/ppermute | solution.py:32
  73.9 8.2 %collective-permute-start.38 = (bf16[2,8,8,128]{3,1,2,0:T(8,128)(2,1)S(1)}, bf16[2,8,8,128]{3,1,2,0:T(8,128)(2,1)S(1)}, u32[]{:S(2)}, u32[]{:S(2)}) collective-permute-start(bf16[2,8,8,128]{3,1,2,0:T(8,128)(2,1)S(1)} %bitcast.482), channel_id=1, source_target_pairs={{0,9},{1,8},{2,11},{3,10},{4,13},{5,12},{6,15},{7,14},{8,1},{9,0},... | collective-permute-start | bytes 98312 | tf_op jit(solution)/shard_map/ppermute | solution.py:32
  74.7 11.5 %collective-permute-start.39 = (bf16[2,8,8,128]{3,1,2,0:T(8,128)(2,1)S(1)}, bf16[2,8,8,128]{3,1,2,0:T(8,128)(2,1)S(1)}, u32[]{:S(2)}, u32[]{:S(2)}) collective-permute-start(bf16[2,8,8,128]{3,1,2,0:T(8,128)(2,1)S(1)} %bitcast.480), channel_id=1, source_target_pairs={{0,10},{1,11},{2,8},{3,9},{4,14},{5,15},{6,12},{7,13},{8,2},{9,3},... | collective-permute-start | bytes 98312 | tf_op jit(solution)/shard_map/ppermute | solution.py:32
  77.7 9.1 %collective-permute-start.40 = (bf16[2,8,8,128]{3,1,2,0:T(8,128)(2,1)S(1)}, bf16[2,8,8,128]{3,1,2,0:T(8,128)(2,1)S(1)}, u32[]{:S(2)}, u32[]{:S(2)}) collective-permute-start(bf16[2,8,8,128]{3,1,2,0:T(8,128)(2,1)S(1)} %bitcast.478), channel_id=1, source_target_pairs={{0,11},{1,10},{2,9},{3,8},{4,15},{5,14},{6,13},{7,12},{8,3},{9,2},... | collective-permute-start | bytes 98312 | tf_op jit(solution)/shard_map/ppermute | solution.py:32
  78.5 8.4 %collective-permute-start.41 = (bf16[2,8,8,128]{3,1,2,0:T(8,128)(2,1)S(1)}, bf16[2,8,8,128]{3,1,2,0:T(8,128)(2,1)S(1)}, u32[]{:S(2)}, u32[]{:S(2)}) collective-permute-start(bf16[2,8,8,128]{3,1,2,0:T(8,128)(2,1)S(1)} %bitcast.476), channel_id=1, source_target_pairs={{0,12},{1,13},{2,14},{3,15},{4,8},{5,9},{6,10},{7,11},{8,4},{9,5},... | collective-permute-start | bytes 98312 | tf_op jit(solution)/shard_map/ppermute | solution.py:32
  81.6 5.4 %collective-permute-start.42 = (bf16[2,8,8,128]{3,1,2,0:T(8,128)(2,1)S(1)}, bf16[2,8,8,128]{3,1,2,0:T(8,128)(2,1)S(1)}, u32[]{:S(2)}, u32[]{:S(2)}) collective-permute-start(bf16[2,8,8,128]{3,1,2,0:T(8,128)(2,1)S(1)} %bitcast.474), channel_id=1, source_target_pairs={{0,13},{1,12},{2,15},{3,14},{4,9},{5,8},{6,11},{7,10},{8,5},{9,4},... | collective-permute-start | bytes 98312 | tf_op jit(solution)/shard_map/ppermute | solution.py:32
  82.2 6.7 %collective-permute-start.43 = (bf16[2,8,8,128]{3,1,2,0:T(8,128)(2,1)S(1)}, bf16[2,8,8,128]{3,1,2,0:T(8,128)(2,1)S(1)}, u32[]{:S(2)}, u32[]{:S(2)}) collective-permute-start(bf16[2,8,8,128]{3,1,2,0:T(8,128)(2,1)S(1)} %bitcast.472), channel_id=1, source_target_pairs={{0,14},{1,15},{2,12},{3,13},{4,10},{5,11},{6,8},{7,9},{8,6},{9,7},... | collective-permute-start | bytes 98312 | tf_op jit(solution)/shard_map/ppermute | solution.py:32
  86.3 6.2 %collective-permute-start.44 = (bf16[2,8,8,128]{3,1,2,0:T(8,128)(2,1)S(1)}, bf16[2,8,8,128]{3,1,2,0:T(8,128)(2,1)S(1)}, u32[]{:S(2)}, u32[]{:S(2)}) collective-permute-start(bf16[2,8,8,128]{3,1,2,0:T(8,128)(2,1)S(1)} %bitcast.470), channel_id=1, source_target_pairs={{0,15},{1,14},{2,13},{3,12},{4,11},{5,10},{6,9},{7,8},{8,7},{9,6},... | collective-permute-start | bytes 98312 | tf_op jit(solution)/shard_map/ppermute | solution.py:32
  94.3 4.1 %collective-permute-start.45 = (bf16[8,8,128]{2,1,0:T(8,128)(2,1)S(1)}, bf16[8,8,128]{2,1,0:T(8,128)(2,1)S(1)}, u32[]{:S(2)}, u32[]{:S(2)}) collective-permute-start(bf16[8,8,128]{2,1,0:T(8,128)(2,1)S(1)} %get-tuple-element.55), channel_id=1, source_target_pairs={{0,1},{1,0},{2,3},{3,2},{4,5},{5,4},{6,7},{7,6},{8,9},{9,8},{10,11... | collective-permute-start | bytes 49160 | tf_op jit(solution)/shard_map/ppermute | solution.py:32
  94.8 3.8 %collective-permute-start.46 = (bf16[8,8,128]{2,1,0:T(8,128)(2,1)S(1)}, bf16[8,8,128]{2,1,0:T(8,128)(2,1)S(1)}, u32[]{:S(2)}, u32[]{:S(2)}) collective-permute-start(bf16[8,8,128]{2,1,0:T(8,128)(2,1)S(1)} %get-tuple-element.54), channel_id=1, source_target_pairs={{0,2},{1,3},{2,0},{3,1},{4,6},{5,7},{6,4},{7,5},{8,10},{9,11},{10,... | collective-permute-start | bytes 49160 | tf_op jit(solution)/shard_map/ppermute | solution.py:32
  95.3 5.8 %collective-permute-start.47 = (bf16[8,8,128]{2,1,0:T(8,128)(2,1)S(1)}, bf16[8,8,128]{2,1,0:T(8,128)(2,1)S(1)}, u32[]{:S(2)}, u32[]{:S(2)}) collective-permute-start(bf16[8,8,128]{2,1,0:T(8,128)(2,1)S(1)} %get-tuple-element.53), channel_id=1, source_target_pairs={{0,3},{1,2},{2,1},{3,0},{4,7},{5,6},{6,5},{7,4},{8,11},{9,10},{10,... | collective-permute-start | bytes 49160 | tf_op jit(solution)/shard_map/ppermute | solution.py:32
  96.7 4.5 %collective-permute-start.48 = (bf16[8,8,128]{2,1,0:T(8,128)(2,1)S(1)}, bf16[8,8,128]{2,1,0:T(8,128)(2,1)S(1)}, u32[]{:S(2)}, u32[]{:S(2)}) collective-permute-start(bf16[8,8,128]{2,1,0:T(8,128)(2,1)S(1)} %get-tuple-element.52), channel_id=1, source_target_pairs={{0,4},{1,5},{2,6},{3,7},{4,0},{5,1},{6,2},{7,3},{8,12},{9,13},{10,... | collective-permute-start | bytes 49160 | tf_op jit(solution)/shard_map/ppermute | solution.py:32
  96.7 7.1 %collective-permute-start.49 = (bf16[8,8,128]{2,1,0:T(8,128)(2,1)S(1)}, bf16[8,8,128]{2,1,0:T(8,128)(2,1)S(1)}, u32[]{:S(2)}, u32[]{:S(2)}) collective-permute-start(bf16[8,8,128]{2,1,0:T(8,128)(2,1)S(1)} %get-tuple-element.51), channel_id=1, source_target_pairs={{0,5},{1,4},{2,7},{3,6},{4,1},{5,0},{6,3},{7,2},{8,13},{9,12},{10,... | collective-permute-start | bytes 49160 | tf_op jit(solution)/shard_map/ppermute | solution.py:32
  98.4 5.6 %collective-permute-start.50 = (bf16[8,8,128]{2,1,0:T(8,128)(2,1)S(1)}, bf16[8,8,128]{2,1,0:T(8,128)(2,1)S(1)}, u32[]{:S(2)}, u32[]{:S(2)}) collective-permute-start(bf16[8,8,128]{2,1,0:T(8,128)(2,1)S(1)} %get-tuple-element.50), channel_id=1, source_target_pairs={{0,6},{1,7},{2,4},{3,5},{4,2},{5,3},{6,0},{7,1},{8,14},{9,15},{10,... | collective-permute-start | bytes 49160 | tf_op jit(solution)/shard_map/ppermute | solution.py:32
  98.6 8.7 %collective-permute-start.51 = (bf16[8,8,128]{2,1,0:T(8,128)(2,1)S(1)}, bf16[8,8,128]{2,1,0:T(8,128)(2,1)S(1)}, u32[]{:S(2)}, u32[]{:S(2)}) collective-permute-start(bf16[8,8,128]{2,1,0:T(8,128)(2,1)S(1)} %get-tuple-element.49), channel_id=1, source_target_pairs={{0,7},{1,6},{2,5},{3,4},{4,3},{5,2},{6,1},{7,0},{8,15},{9,14},{10,... | collective-permute-start | bytes 49160 | tf_op jit(solution)/shard_map/ppermute | solution.py:32
  101.1 6.6 %collective-permute-start.52 = (bf16[8,8,128]{2,1,0:T(8,128)(2,1)S(1)}, bf16[8,8,128]{2,1,0:T(8,128)(2,1)S(1)}, u32[]{:S(2)}, u32[]{:S(2)}) collective-permute-start(bf16[8,8,128]{2,1,0:T(8,128)(2,1)S(1)} %get-tuple-element.48), channel_id=1, source_target_pairs={{0,8},{1,9},{2,10},{3,11},{4,12},{5,13},{6,14},{7,15},{8,0},{9,1},... | collective-permute-start | bytes 49160 | tf_op jit(solution)/shard_map/ppermute | solution.py:32
  101.1 9.7 %collective-permute-start.53 = (bf16[8,8,128]{2,1,0:T(8,128)(2,1)S(1)}, bf16[8,8,128]{2,1,0:T(8,128)(2,1)S(1)}, u32[]{:S(2)}, u32[]{:S(2)}) collective-permute-start(bf16[8,8,128]{2,1,0:T(8,128)(2,1)S(1)} %get-tuple-element.47), channel_id=1, source_target_pairs={{0,9},{1,8},{2,11},{3,10},{4,13},{5,12},{6,15},{7,14},{8,1},{9,0},... | collective-permute-start | bytes 49160 | tf_op jit(solution)/shard_map/ppermute | solution.py:32
  103.7 8.1 %collective-permute-start.54 = (bf16[8,8,128]{2,1,0:T(8,128)(2,1)S(1)}, bf16[8,8,128]{2,1,0:T(8,128)(2,1)S(1)}, u32[]{:S(2)}, u32[]{:S(2)}) collective-permute-start(bf16[8,8,128]{2,1,0:T(8,128)(2,1)S(1)} %get-tuple-element.46), channel_id=1, source_target_pairs={{0,10},{1,11},{2,8},{3,9},{4,14},{5,15},{6,12},{7,13},{8,2},{9,3},... | collective-permute-start | bytes 49160 | tf_op jit(solution)/shard_map/ppermute | solution.py:32
  104.0 11.4 %collective-permute-start.55 = (bf16[8,8,128]{2,1,0:T(8,128)(2,1)S(1)}, bf16[8,8,128]{2,1,0:T(8,128)(2,1)S(1)}, u32[]{:S(2)}, u32[]{:S(2)}) collective-permute-start(bf16[8,8,128]{2,1,0:T(8,128)(2,1)S(1)} %get-tuple-element.45), channel_id=1, source_target_pairs={{0,11},{1,10},{2,9},{3,8},{4,15},{5,14},{6,13},{7,12},{8,3},{9,2},... | collective-permute-start | bytes 49160 | tf_op jit(solution)/shard_map/ppermute | solution.py:32
  107.4 8.0 %collective-permute-start.56 = (bf16[8,8,128]{2,1,0:T(8,128)(2,1)S(1)}, bf16[8,8,128]{2,1,0:T(8,128)(2,1)S(1)}, u32[]{:S(2)}, u32[]{:S(2)}) collective-permute-start(bf16[8,8,128]{2,1,0:T(8,128)(2,1)S(1)} %get-tuple-element.44), channel_id=1, source_target_pairs={{0,12},{1,13},{2,14},{3,15},{4,8},{5,9},{6,10},{7,11},{8,4},{9,5},... | collective-permute-start | bytes 49160 | tf_op jit(solution)/shard_map/ppermute | solution.py:32
  107.7 7.7 %collective-permute-start.57 = (bf16[8,8,128]{2,1,0:T(8,128)(2,1)S(1)}, bf16[8,8,128]{2,1,0:T(8,128)(2,1)S(1)}, u32[]{:S(2)}, u32[]{:S(2)}) collective-permute-start(bf16[8,8,128]{2,1,0:T(8,128)(2,1)S(1)} %get-tuple-element.43), channel_id=1, source_target_pairs={{0,13},{1,12},{2,15},{3,14},{4,9},{5,8},{6,11},{7,10},{8,5},{9,4},... | collective-permute-start | bytes 49160 | tf_op jit(solution)/shard_map/ppermute | solution.py:32
  110.9 6.4 %collective-permute-start.58 = (bf16[8,8,128]{2,1,0:T(8,128)(2,1)S(1)}, bf16[8,8,128]{2,1,0:T(8,128)(2,1)S(1)}, u32[]{:S(2)}, u32[]{:S(2)}) collective-permute-start(bf16[8,8,128]{2,1,0:T(8,128)(2,1)S(1)} %get-tuple-element.42), channel_id=1, source_target_pairs={{0,14},{1,15},{2,12},{3,13},{4,10},{5,11},{6,8},{7,9},{8,6},{9,7},... | collective-permute-start | bytes 49160 | tf_op jit(solution)/shard_map/ppermute | solution.py:32
  111.8 5.9 %collective-permute-start.59 = (bf16[8,8,128]{2,1,0:T(8,128)(2,1)S(1)}, bf16[8,8,128]{2,1,0:T(8,128)(2,1)S(1)}, u32[]{:S(2)}, u32[]{:S(2)}) collective-permute-start(bf16[8,8,128]{2,1,0:T(8,128)(2,1)S(1)} %get-tuple-element.41), channel_id=1, source_target_pairs={{0,15},{1,14},{2,13},{3,12},{4,11},{5,10},{6,9},{7,8},{8,7},{9,6},... | collective-permute-start | bytes 49160 | tf_op jit(solution)/shard_map/ppermute | solution.py:32
  (2 other events, 1.4 us)

commit v3 on v1

--- a/solution.py
+++ b/solution.py
@@ -9,6 +9,19 @@
     centred = values - average
     spread = jnp.mean(centred * centred, axis=reduce_dim, keepdims=True)
     return centred * lax.rsqrt(spread + 1e-05) * norm_gain + norm_bias
+
+
+def exchange(blocks):
+    count = blocks.shape[0]
+    core = lax.axis_index("row") % 2
+    split = blocks.reshape((count // 2, 2) + blocks.shape[1:])
+    keep = jnp.where(core == 0, split[:, 0], split[:, 1])
+    send = jnp.where(core == 0, split[:, 1], split[:, 0])
+    got = lax.ppermute(send, "row", [(d, d ^ 1) for d in range(count)])
+    split = jnp.where(core == 0, jnp.stack([keep, got], 1), jnp.stack([got, keep], 1))
+    same_core = [list(range(c, count, 2)) for c in range(2)]
+    split = lax.all_to_all(split, "row", split_axis=0, concat_axis=0, tiled=True, axis_index_groups=same_core)
+    return split.reshape(blocks.shape)
 
 
 def triangle(pair_rows, mask_rows, which, form, norm_gains, norm_biases, proj_weights, gate_weights, out_weights):
@@ -37,12 +50,12 @@
     out_gate = jax.nn.sigmoid(
         jnp.einsum("rnd,de->rne", normed, gate_weights[which], preferred_element_type=jnp.float32)
     ).astype(jnp.bfloat16)
-    both = lax.all_to_all(both, "row", split_axis=0, concat_axis=0, tiled=True)
+    both = exchange(both)
     left = jnp.moveaxis(both[:, 0], 0, 1).reshape(per_group, tokens, tokens)
     right = jnp.moveaxis(both[:, 1], 0, 1).reshape(per_group, tokens, tokens)
     product = jnp.einsum(form, left, right, preferred_element_type=jnp.float32).astype(jnp.bfloat16)
-    product = product.reshape(per_group, groups, per_dev, tokens)
-    merged = lax.all_to_all(product, "row", split_axis=1, concat_axis=0, tiled=True)
+    product = jnp.moveaxis(product.reshape(per_group, groups, per_dev, tokens), 1, 0)
+    merged = exchange(product)
     merged = merged.reshape(channels, per_dev, tokens)
     normed_out = layer_norm(
         merged.astype(jnp.float32),

time: 79.7 us -> 85.3 us (1.070)
  waiting for transfers between devices: 18.2 us -> 21.8 us
  blocking collectives: 38.9 us -> 40 us
    ppermute x0 -> x4, waiting for transfers between devices: none -> 5.28 us  [exchange(): got = lax.ppermute(send, 'row', [(d, d ^ 1) for d in range(count)])]
    reshape x4 -> x1, local copies, waits for them, and re-layouts: 1.89 us -> 0.06 us  [triangle(): product.reshape(per_group, groups, per_dev, tokens)]
    all_to_all x2, waiting for transfers between devices: 18.2 us -> 16.5 us  [exchange(): lax.all_to_all(split, 'row', split_axis=0, concat_axis=0, tiled=True, axi...]
    select_n x0 -> x3, local copies, waits for them, and re-layouts: none -> 1.48 us  [exchange(): jnp.where(core == 0, jnp.stack([keep, got], 1), jnp.stack([got, keep], 1))]
    all_to_all x2, blocking collectives: 38.9 us -> 40 us  [exchange(): lax.all_to_all(split, 'row', split_axis=0, concat_axis=0, tiled=True, axi...]
    all_to_all x2, starting transfers between devices: 8.2 us -> 7.27 us  [exchange(): lax.all_to_all(split, 'row', split_axis=0, concat_axis=0, tiled=True, axi...]
    unnamed x15 -> x17, local copies, waits for them, and re-layouts: 4.22 us -> 4.94 us
  transfers between devices with their start and end apart: 2 -> 6, of which waited for: 2 -> 6; matrix products, arithmetic and copies ran while one was open for 1% -> 2% of each run, Pallas kernels for 0% -> 0%
where the time goes in v3:
time: 85.3 us; the launch traced here: 84.7 us
  blocking collectives  40 us (47%)
  waiting for transfers between devices  21.8 us (26%)
  local copies, waits for them, and re-layouts  8.23 us (10%)
  starting transfers between devices  8.01 us (9%)
  matrix products  4.2 us (5%)
  other arithmetic  2.08 us (2%)
    all_to_all x2, blocking collectives, exchange(): lax.all_to_all(split, 'row', split_axis=0, concat_axis=0, tiled=True, axi...  40 us
    all_to_all x2, waiting for transfers between devices, exchange(): lax.all_to_all(split, 'row', split_axis=0, concat_axis=0, tiled=True, axi...  16.5 us
    all_to_all x2, starting transfers between devices, exchange(): lax.all_to_all(split, 'row', split_axis=0, concat_axis=0, tiled=True, axi...  7.27 us
    ppermute x4, waiting for transfers between devices, exchange(): got = lax.ppermute(send, 'row', [(d, d ^ 1) for d in range(count)])  5.28 us
    unnamed x17, local copies, waits for them, and re-layouts  4.94 us
  transfers between devices with their start and end apart: 6, of which 6 were waited for; matrix products, arithmetic and copies ran while one was open for 2% of the time, Pallas kernels for 0%

profile of v3, /device:TPU:0, one launch (start us, length us, event | category | flops | bytes accessed | tf_op | source)
XLA Modules:
  0.0 84.7 jit_solution(13908849597493303282)
XLA Ops:
  0.0 1.1 %copy.130 = bf16[8,128,128]{1,2,0:T(8,128)(2,1)S(1)} copy(bf16[8,128,128]{2,1,0:T(8,128)(2,1)} %param.7) | data formatting | bytes 524288 | tf_op args[0]
  1.1 0.0 copy-start
  1.2 0.1 fusion.41
  1.3 0.8 copy-done
  2.1 0.0 copy-start.3
  2.1 0.0 copy-start.4
  2.1 0.1 copy.192
  2.2 0.5 copy-done.3
  2.8 0.0 copy-done.4
  2.8 0.4 fusion.8
  3.2 0.4 fusion.11
  3.6 0.0 copy-start.2
  3.6 0.7 copy-done.2
  4.3 0.3 fusion.28
  4.6 0.3 fusion.29
  4.9 0.2 copy_dynamic-update-slice_fusion.3
  5.1 0.2 copy_dynamic-update-slice_fusion.2
  5.3 0.5 collective-permute-start
  5.9 1.1 %collective-permute-done = bf16[8,2,8,8,128]{4,3,2,1,0:T(8,128)(2,1)S(1)} collective-permute-done((bf16[8,2,8,8,128]{4,3,2,1,0:T(8,128)(2,1)S(1)}, bf16[8,2,8,8,128]{4,3,2,1,0:T(8,128)(2,1)S(1)}, u32[]{:S(2)}, u32[]{:S(2)}) %collective-permute-start) | collective-permute-done | bytes 262176 | tf_op jit(solution)/shard_map/ppermute | solution.py:20
  7.1 21.8 %all_to_all.20 = bf16[8,2,2,8,8,128]{5,4,3,2,1,0:T(8,128)(2,1)S(1)} all-to-all(bf16[8,2,2,8,8,128]{5,4,3,2,1,0:T(8,128)(2,1)S(1)} %maximum_select_fusion), channel_id=1, replica_groups={{0,2,4,6,8,10,12,14},{1,3,5,7,9,11,13,15},{16,18,20,22,24,26,28,30},{17..., dimensions={0} | all-to-all | bytes 1048576 | tf_op jit(solution)/shard_map/all_to_all | solution.py:23
  28.9 0.3 convolution_convert_fusion.1
  29.2 0.1 copy.146
  29.3 0.1 collective-permute-start.1
  29.4 1.3 %collective-permute-done.1 = bf16[8,8,8,128]{3,2,1,0:T(8,128)(2,1)S(1)} collective-permute-done((bf16[8,8,8,128]{3,2,1,0:T(8,128)(2,1)S(1)}, bf16[8,8,8,128]{3,2,1,0:T(8,128)(2,1)S(1)}, u32[]{:S(2)}, u32[]{:S(2)}) %collective-permute-start.1) | collective-permute-done | bytes 131104 | tf_op jit(solution)/shard_map/ppermute | solution.py:20
  30.8 0.7 copy.151
  31.5 3.6 %all-to-all-start.1 = ((bf16[8,2,8,8,128]{4,3,2,1,0:T(8,128)(2,1)}), bf16[8,2,8,8,128]{4,3,2,1,0:T(8,128)(2,1)S(1)}, u32[]{:S(2)}, u32[]{:S(2)}) async-start(bf16[8,2,8,8,128]{4,3,2,1,0:T(8,128)(2,1)} %copy.151), calls=%async_computation.1 | async-start | bytes 524288 | tf_op jit(solution)/shard_map/all_to_all | solution.py:23
  35.1 0.1 add.118
  35.2 0.1 mul.148
  35.3 0.1 copy.194
  35.5 0.7 copy-done.5
  36.2 0.4 fusion.34
  36.6 7.8 %all-to-all-done.1 = bf16[8,2,8,8,128]{4,3,2,1,0:T(8,128)(2,1)S(1)} async-done(((bf16[8,2,8,8,128]{4,3,2,1,0:T(8,128)(2,1)}), bf16[8,2,8,8,128]{4,3,2,1,0:T(8,128)(2,1)S(1)}, u32[]{:S(2)}, u32[]{:S(2)}) %all-to-all-start.1) | async-done | bytes 262176 | tf_op jit(solution)/shard_map/all_to_all | solution.py:23
  44.4 0.1 convert_reduce_fusion.2
  44.5 0.1 fusion.49
  44.7 0.3 fusion.52
  45.0 0.5 copy-done.1
  45.5 0.3 fusion.79
  45.8 0.1 multiply_reduce_fusion
  45.9 0.2 add_convert_fusion
  46.1 0.3 fusion.2
  46.4 0.3 fusion.5
  46.7 0.2 fusion.24
  46.9 0.2 fusion.25
  47.1 0.2 copy_dynamic-update-slice_fusion.1
  47.3 0.2 copy_dynamic-update-slice_fusion
  47.6 0.1 collective-permute-start.2
  47.6 1.5 %collective-permute-done.2 = bf16[8,2,8,8,128]{4,3,2,1,0:T(8,128)(2,1)S(1)} collective-permute-done((bf16[8,2,8,8,128]{4,3,2,1,0:T(8,128)(2,1)S(1)}, bf16[8,2,8,8,128]{4,3,2,1,0:T(8,128)(2,1)S(1)}, u32[]{:S(2)}, u32[]{:S(2)}) %collective-permute-start.2) | collective-permute-done | bytes 262176 | tf_op jit(solution)/shard_map/ppermute | solution.py:20
  49.2 0.1 maximum_select_fusion.1
  49.3 18.2 %all_to_all.21 = bf16[8,2,2,8,8,128]{5,4,3,2,1,0:T(8,128)(2,1)S(1)} all-to-all(bf16[8,2,2,8,8,128]{5,4,3,2,1,0:T(8,128)(2,1)S(1)} %copy.163), channel_id=1, replica_groups={{0,2,4,6,8,10,12,14},{1,3,5,7,9,11,13,15},{16,18,20,22,24,26,28,30},{17..., dimensions={0} | all-to-all | bytes 1048576 | tf_op jit(solution)/shard_map/all_to_all | solution.py:23
  67.5 0.3 convolution_convert_fusion
  67.8 0.1 fusion.77
  67.9 0.1 collective-permute-start.3
  68.0 1.3 %collective-permute-done.3 = bf16[8,8,8,128]{3,2,1,0:T(8,128)(2,1)S(1)} collective-permute-done((bf16[8,8,8,128]{3,2,1,0:T(8,128)(2,1)S(1)}, bf16[8,8,8,128]{3,2,1,0:T(8,128)(2,1)S(1)}, u32[]{:S(2)}, u32[]{:S(2)}) %collective-permute-start.3) | collective-permute-done | bytes 131104 | tf_op jit(solution)/shard_map/ppermute | solution.py:20
  69.3 0.7 copy.170
  70.0 3.6 %all-to-all-start.3 = ((bf16[8,2,8,8,128]{4,3,2,1,0:T(8,128)(2,1)}), bf16[8,2,8,8,128]{4,3,2,1,0:T(8,128)(2,1)S(1)}, u32[]{:S(2)}, u32[]{:S(2)}) async-start(bf16[8,2,8,8,128]{4,3,2,1,0:T(8,128)(2,1)} %copy.170), calls=%async_computation.3 | async-start | bytes 524288 | tf_op jit(solution)/shard_map/all_to_all | solution.py:23
  73.7 0.1 add.130
  73.8 0.1 mul.165
  73.9 0.3 fusion.32
  74.2 8.7 %all-to-all-done.3 = bf16[8,2,8,8,128]{4,3,2,1,0:T(8,128)(2,1)S(1)} async-done(((bf16[8,2,8,8,128]{4,3,2,1,0:T(8,128)(2,1)}), bf16[8,2,8,8,128]{4,3,2,1,0:T(8,128)(2,1)S(1)}, u32[]{:S(2)}, u32[]{:S(2)}) %all-to-all-start.3) | async-done | bytes 262176 | tf_op jit(solution)/shard_map/all_to_all | solution.py:23
  82.9 0.1 convert_reduce_fusion.1
  83.1 0.1 fusion.45
  83.2 0.3 fusion.48
  83.6 0.3 fusion.30
  83.8 0.9 %copy.173 = bf16[8,128,128]{2,1,0:T(8,128)(2,1)} copy(bf16[8,128,128]{1,2,0:T(8,128)(2,1)S(1)} %fusion.30) | data formatting | bytes 524288 | tf_op jit(solution)/shard_map/convert_element_type | solution.py:67
  (26 shorter events, 0.6 us)
Async XLA Ops:
  1.1 1.0 %copy-start = (bf16[2,128,512]{2,1,0:T(8,128)(2,1)S(1)}, bf16[2,128,512]{2,1,0:T(8,128)(2,1)}, u32[]{:S(2)}) copy-start(bf16[2,128,512]{2,1,0:T(8,128)(2,1)} %param.11) | copy-start | bytes 786436
  2.1 0.7 copy-start.3
  2.1 0.7 copy-start.4
  3.6 0.7 copy-start.2
  5.3 1.7 %collective-permute-start = (bf16[8,2,8,8,128]{4,3,2,1,0:T(8,128)(2,1)S(1)}, bf16[8,2,8,8,128]{4,3,2,1,0:T(8,128)(2,1)S(1)}, u32[]{:S(2)}, u32[]{:S(2)}) collective-permute-start(bf16[8,2,8,8,128]{4,3,2,1,0:T(8,128)(2,1)S(1)} %select_bitcast_fusion.1), channel_id=1, source_target_pairs={{0,1},{1,0},{2,3},{3,2},{4,5},{5,4},{6,7},{7,6},{8,9},{9,8},{10,11... | collective-permute-start | bytes 786440 | tf_op jit(solution)/shard_map/ppermute | solution.py:20
  29.3 1.4 %collective-permute-start.1 = (bf16[8,8,8,128]{3,2,1,0:T(8,128)(2,1)S(1)}, bf16[8,8,8,128]{3,2,1,0:T(8,128)(2,1)S(1)}, u32[]{:S(2)}, u32[]{:S(2)}) collective-permute-start(bf16[8,8,8,128]{3,2,1,0:T(8,128)(2,1)S(1)} %fusion.63), channel_id=1, source_target_pairs={{0,1},{1,0},{2,3},{3,2},{4,5},{5,4},{6,7},{7,6},{8,9},{9,8},{10,11... | collective-permute-start | bytes 393224 | tf_op jit(solution)/shard_map/ppermute | solution.py:20
  31.5 12.9 %all-to-all-start.1 = ((bf16[8,2,8,8,128]{4,3,2,1,0:T(8,128)(2,1)}), bf16[8,2,8,8,128]{4,3,2,1,0:T(8,128)(2,1)S(1)}, u32[]{:S(2)}, u32[]{:S(2)}) async-start(bf16[8,2,8,8,128]{4,3,2,1,0:T(8,128)(2,1)} %copy.151), calls=%async_computation.1 | async-start | bytes 524288 | tf_op jit(solution)/shard_map/all_to_all | solution.py:23
  35.3 0.8 copy-start.5
  44.7 0.8 copy-start.1
  47.6 1.6 %collective-permute-start.2 = (bf16[8,2,8,8,128]{4,3,2,1,0:T(8,128)(2,1)S(1)}, bf16[8,2,8,8,128]{4,3,2,1,0:T(8,128)(2,1)S(1)}, u32[]{:S(2)}, u32[]{:S(2)}) collective-permute-start(bf16[8,2,8,8,128]{4,3,2,1,0:T(8,128)(2,1)S(1)} %get-tuple-element.12), channel_id=1, source_target_pairs={{0,1},{1,0},{2,3},{3,2},{4,5},{5,4},{6,7},{7,6},{8,9},{9,8},{10,11... | collective-permute-start | bytes 786440 | tf_op jit(solution)/shard_map/ppermute | solution.py:20
  67.9 1.4 %collective-permute-start.3 = (bf16[8,8,8,128]{3,2,1,0:T(8,128)(2,1)S(1)}, bf16[8,8,8,128]{3,2,1,0:T(8,128)(2,1)S(1)}, u32[]{:S(2)}, u32[]{:S(2)}) collective-permute-start(bf16[8,8,8,128]{3,2,1,0:T(8,128)(2,1)S(1)} %get-tuple-element.16), channel_id=1, source_target_pairs={{0,1},{1,0},{2,3},{3,2},{4,5},{5,4},{6,7},{7,6},{8,9},{9,8},{10,11... | collective-permute-start | bytes 393224 | tf_op jit(solution)/shard_map/ppermute | solution.py:20
  70.0 12.9 %all-to-all-start.3 = ((bf16[8,2,8,8,128]{4,3,2,1,0:T(8,128)(2,1)}), bf16[8,2,8,8,128]{4,3,2,1,0:T(8,128)(2,1)S(1)}, u32[]{:S(2)}, u32[]{:S(2)}) async-start(bf16[8,2,8,8,128]{4,3,2,1,0:T(8,128)(2,1)} %copy.170), calls=%async_computation.3 | async-start | bytes 524288 | tf_op jit(solution)/shard_map/all_to_all | solution.py:23

commit v4 on v1

v4 whole, which is shorter than its diff:
```python
import functools

import jax
import jax.numpy as jnp
from jax import lax
from jax.experimental import pallas as pl
from jax.experimental.pallas import tpu as pltpu
from jax.sharding import PartitionSpec as P

F32 = jnp.float32
BF16 = jnp.bfloat16
NT = (((1,), (1,)), ((), ()))
NN = (((1,), (0,)), ((), ()))
TN = (((0,), (0,)), ((), ()))


def dot(a, b, dims):
    return lax.dot_general(a, b, dims, preferred_element_type=F32)


def sigmoid(values):
    return 0.5 * jnp.tanh(0.5 * values) + 0.5


def unit(values, axis):
    scale = 1.0 / values.shape[axis]
    centred = values - jnp.sum(values, axis=axis, keepdims=True) * scale
    spread = jnp.sum(centred * centred, axis=axis, keepdims=True) * scale
    return centred * lax.rsqrt(spread + 1e-05)


def project_kernel(per_group, pair_ref, mask_ref, gain_ref, bias_ref, proj_ref, gatew_ref, both_ref, gate_ref, panels):
    project_rows(per_group, 0, lambda r: pair_ref[r], mask_ref, gain_ref, bias_ref, proj_ref, gatew_ref, both_ref, gate_ref, panels)


def project_rows(per_group, which, pair_row, mask_ref, gain_ref, bias_ref, proj_ref, gatew_ref, both_ref, gate_ref, panels):
    rows = mask_ref.shape[0]
    channels = gatew_ref.shape[2]
    groups = channels // per_group
    weights_t = proj_ref[which].T
    gain = gain_ref[which, 0:1]
    bias = bias_ref[which, 0:1]
    for r in range(rows):
        normed = (unit(pair_row(r).astype(F32), 1) * gain + bias).astype(BF16)
        products = dot(weights_t, normed, NT)
        mask = mask_ref[r : r + 1].astype(F32)
        for side in range(2):
            base = 2 * side * channels
            gated = sigmoid(products[base : base + channels]) * products[base + channels : base + 2 * channels] * mask
            for g in range(groups):
                start = (2 * g + side) * per_group
                panels[start : start + per_group, r, :] = gated[g * per_group : (g + 1) * per_group]
        gate_ref[r] = sigmoid(dot(normed, gatew_ref[which], NN)).astype(BF16)
    both_ref[...] = panels[...].astype(BF16).reshape(both_ref.shape)


def finish_rows(which, store, merged_ref, pair_ref, gate_ref, gain_ref, bias_ref, outw_ref, unit_scratch):
    channels, rows, tokens = unit_scratch.shape
    unit_scratch[...] = unit(merged_ref[...].astype(F32).reshape(channels, rows, tokens), 0)
    gain = jnp.broadcast_to(gain_ref[which, 1:2], (tokens, channels)).T
    bias = jnp.broadcast_to(bias_ref[which, 1:2], (tokens, channels)).T
    for r in range(rows):
        normed = (unit_scratch[:, r, :] * gain + bias).astype(BF16)
        projected = dot(normed, outw_ref[which], TN)
        store(r, (pair_ref[r].astype(F32) + gate_ref[r].astype(F32) * projected).astype(BF16))


def mix_kernel(per_group, rows, incoming, both_ref, product_ref):
    groups, _, tokens = both_ref.shape
    step = 2 * rows

    def matrices(side, pair):
        start = (side * per_group + 2 * pair) * rows
        block = both_ref[:, start : start + step, :].astype(F32)
        return [block[:, h * rows : (h + 1) * rows].reshape(groups * rows, tokens).astype(BF16) for h in range(2)]

    for pair in range(per_group // 2):
        lefts, rights = matrices(0, pair), matrices(1, pair)
        sums = [
            dot(left, right, TN if incoming else NT).reshape(groups, rows, tokens)
            for left, right in zip(lefts, rights)
        ]
        product_ref[:, pair * step : (pair + 1) * step, :] = jnp.concatenate(sums, axis=1).astype(BF16)


def step_kernel(
    per_group, merged_ref, pair_ref, gate_ref, mask_ref, gain_ref, bias_ref, outw_ref, proj_ref,
    gatew_ref, middle_ref, both_ref, gate1_ref, unit_scratch, panels,
):
    def store(r, values):
        middle_ref[r] = values

    finish_rows(0, store, merged_ref, pair_ref, gate_ref, gain_ref, bias_ref, outw_ref, unit_scratch)
    project_rows(
        per_group, 1, lambda r: middle_ref[r], mask_ref, gain_ref, bias_ref, proj_ref, gatew_ref, both_ref, gate1_ref, panels
    )


def finish_kernel(merged_ref, pair_ref, gate_ref, gain_ref, bias_ref, outw_ref, result_ref, unit_scratch):
    def store(r, values):
        result_ref[r] = values

    finish_rows(1, store, merged_ref, pair_ref, gate_ref, gain_ref, bias_ref, outw_ref, unit_scratch)


def on_device(pair, mask, gains, biases, proj, gatew, outw):
    groups = lax.axis_size("row")
    rows, tokens, channels = pair.shape
    per_group = channels // groups
    whole = pl.BlockSpec(memory_space=pltpu.VMEM)
    params = pltpu.CompilerParams(vmem_limit_bytes=48 * 1024 * 1024)
    both_shape = jax.ShapeDtypeStruct((2 * channels * rows, tokens), BF16)
    pair_shape = jax.ShapeDtypeStruct(pair.shape, BF16)
    panels = pltpu.VMEM((2 * channels, rows, tokens), F32)
    unit_scratch = pltpu.VMEM((channels, rows, tokens), F32)

    def exchange(array):
        return lax.all_to_all(array, "row", split_axis=0, concat_axis=0, tiled=True)

    def mix(both, incoming):
        product = pl.pallas_call(
            functools.partial(mix_kernel, per_group, rows, incoming),
            out_shape=jax.ShapeDtypeStruct((groups, per_group * rows, tokens), BF16),
            in_specs=[whole],
            out_specs=whole,
            compiler_params=params,
            name="mix",
        )(both.reshape(groups, 2 * per_group * rows, tokens))
        return product.reshape(channels * rows, tokens)

    both, gate = pl.pallas_call(
        functools.partial(project_kernel, per_group),
        out_shape=(both_shape, pair_shape),
        in_specs=[whole] * 6,
        out_specs=(whole, whole),
        scratch_shapes=[panels],
        compiler_params=params,
        name="project",
    )(pair, mask, gains, biases, proj, gatew)
    merged = exchange(mix(exchange(both), False))
    middle, both, gate = pl.pallas_call(
        functools.partial(step_kernel, per_group),
        out_shape=(pair_shape, both_shape, pair_shape),
        in_specs=[whole] * 9,
        out_specs=(whole, whole, whole),
        scratch_shapes=[unit_scratch, panels],
        compiler_params=params,
        name="finish_project",
    )(merged, pair, gate, mask, gains, biases, outw, proj, gatew)
    merged = exchange(mix(exchange(both), True))
    return pl.pallas_call(
        finish_kernel,
        out_shape=pair_shape,
        in_specs=[whole] * 6,
        out_specs=whole,
        scratch_shapes=[unit_scratch],
        compiler_params=params,
        name="finish",
    )(merged, middle, gate, gains, biases, outw)


def solution(mesh):
    rows = ("groups", "row")
    return jax.shard_map(
        on_device,
        mesh=mesh,
        in_specs=(P(rows, None, None), P(rows, None), P(), P(), P(), P(), P()),
        out_specs=P(rows, None, None),
        check_vma=False,
    )
```

time: 79.7 us -> 78.5 us (0.985)
  blocking collectives: 38.9 us -> 66.9 us
  waiting for transfers between devices: 18.2 us -> 0 us
  starting transfers between devices: 8.2 us -> 0 us
  Pallas kernels: 0 us -> 5.61 us
  matrix products: 4.22 us -> 0 us
  local copies, waits for them, and re-layouts: 7.52 us -> 5.45 us
  other arithmetic: 1.8 us -> 0 us
    all_to_all x2 -> x4, blocking collectives: 38.9 us -> 66.9 us  [exchange(): return lax.all_to_all(array, 'row', split_axis=0, concat_axis=0, tiled=True)]
    all_to_all x2 -> x0, waiting for transfers between devices: 18.2 us -> none  [triangle(): lax.all_to_all(product, 'row', split_axis=1, concat_axis=0, tiled=True)]
    all_to_all x2 -> x0, starting transfers between devices: 8.2 us -> none  [triangle(): lax.all_to_all(product, 'row', split_axis=1, concat_axis=0, tiled=True)]
    pallas_call x0 -> x5, Pallas kernels: none -> 5.61 us  [the longest x1 2.1 us: on_device(): pl.pallas_call(functools.partial(step_kernel, per_group), out_shape=(pair...]
    dot_general x14 -> x0, matrix products: 4.22 us -> none  [the longest x4 1.33 us: gated(): jnp.einsum('rnd,de->ern', normed, weights[:, offset:offset + channels], p...]
    reshape x4 -> x0, local copies, waits for them, and re-layouts: 1.89 us -> none  [the longest x2 1.54 us: triangle(): product = product.reshape(per_group, groups, per_dev, tokens)]
    unnamed x15 -> x26, local copies, waits for them, and re-layouts: 4.22 us -> 5.45 us
    convert_element_type x4 -> x0, other arithmetic: 0.9 us -> none  [the longest x2 0.68 us: triangle(): normed_out = layer_norm(merged.astype(jnp.float32), norm_gains[which, 1][...]
  transfers between devices with their start and end apart: 2 -> 0, of which waited for: 2 -> 0; matrix products, arithmetic and copies ran while one was open for 1% -> 0% of each run, Pallas kernels for 0% -> 0%
where the time goes in v4:
time: 78.5 us; the launch traced here: 78.1 us
  blocking collectives  66.9 us (85%)
  Pallas kernels  5.61 us (7%)
  local copies, waits for them, and re-layouts  5.45 us (7%)
    all_to_all x4, blocking collectives, exchange(): return lax.all_to_all(array, 'row', split_axis=0, concat_axis=0, tiled=True)  66.9 us
    unnamed x26, local copies, waits for them, and re-layouts  5.45 us
    pallas_call x1, Pallas kernels, on_device(): pl.pallas_call(functools.partial(step_kernel, per_group), out_shape=(pair...  2.1 us

profile of v4, /device:TPU:0, one launch (start us, length us, event | category | flops | bytes accessed | tf_op | source)
XLA Modules:
  0.0 78.1 jit_solution(9867832928510064926)
XLA Ops:
  0.0 0.0 copy-start
  0.0 0.9 %copy-done = bf16[8,128,128]{2,1,0:T(8,128)(2,1)S(1)} copy-done((bf16[8,128,128]{2,1,0:T(8,128)(2,1)S(1)}, bf16[8,128,128]{2,1,0:T(8,128)(2,1)}, u32[]{:S(2)}) %copy-start) | copy-done | bytes 262168
  1.0 0.0 copy-start.2
  1.0 0.9 %copy-done.2 = bf16[2,128,512]{2,1,0:T(8,128)(2,1)S(1)} copy-done((bf16[2,128,512]{2,1,0:T(8,128)(2,1)S(1)}, bf16[2,128,512]{2,1,0:T(8,128)(2,1)}, u32[]{:S(2)}) %copy-start.2) | copy-done | bytes 262168
  1.9 0.0 copy-start.4
  1.9 0.8 %copy-done.4 = bf16[2,128,128]{2,1,0:T(8,128)(2,1)S(1)} copy-done((bf16[2,128,128]{2,1,0:T(8,128)(2,1)S(1)}, bf16[2,128,128]{2,1,0:T(8,128)(2,1)}, u32[]{:S(2)}) %copy-start.4) | copy-done | bytes 65560
  2.7 0.0 copy-start.7
  2.7 0.7 copy-done.7
  3.4 0.0 copy-start.9
  3.4 0.7 copy-done.9
  4.1 0.0 copy-start.11
  4.1 0.7 copy-done.11
  4.8 1.4 %project.1 = (bf16[2048,128]{1,0:T(8,128)(2,1)S(1)}, bf16[8,128,128]{2,1,0:T(8,128)(2,1)S(1)}) custom-call(bf16[8,128,128]{2,1,0:T(8,128)(2,1)S(1)} %copy-done, s32[8,128]{1,0:T(8,128)S(1)} %copy-done.11, f32[2,2,128]{2,1,0:T(2,128)S(1)} %copy-done.7, f32[2,2,128]{2,1,0:T(2,128)S(1)} %copy-done.9, bf16[2,128,512]{2,1,0:T(8,128)(2,1)S(1)} %copy-done.2, ...), custom_call_target="tpu_custom_call" | custom-call | tf_op jit(solution)/shard_map/project/pallas_call | solution.py:131
  6.2 21.7 %all_to_all.34.both_ref = bf16[16,128,128]{2,1,0:T(8,128)(2,1)S(1)} all-to-all(bf16[16,128,128]{2,1,0:T(8,128)(2,1)S(1)} %bitcast.7), channel_id=1, replica_groups=mesh['groups'=2,'row'=16] {'row'}, dimensions={0} | all-to-all | bytes 1048576 | tf_op jit(solution)/shard_map/all_to_all | solution.py:118
  27.9 0.0 copy-start.5
  27.9 0.0 copy-start.6
  27.9 0.0 copy-start.10
  27.9 0.0 copy-start.12
  27.9 0.3 mix.2
  28.2 0.0 copy-start.1
  28.2 0.0 copy-start.3
  28.2 14.1 %all_to_all.35 = bf16[16,64,128]{2,1,0:T(8,128)(2,1)S(1)} all-to-all(bf16[16,64,128]{2,1,0:T(8,128)(2,1)S(1)} %mix.2), channel_id=1, replica_groups=mesh['groups'=2,'row'=16] {'row'}, dimensions={0} | all-to-all | bytes 524288 | tf_op jit(solution)/shard_map/all_to_all | solution.py:118
  42.3 0.0 copy-start.8
  42.3 0.0 copy-done.5
  42.3 0.0 copy-done.6
  42.3 0.0 copy-done.10
  42.3 0.0 copy-done.12
  42.3 0.0 copy-done.1
  42.3 0.0 copy-done.3
  42.3 0.6 copy-done.8
  43.0 2.1 %finish_project.1 = (bf16[8,128,128]{2,1,0:T(8,128)(2,1)S(1)}, bf16[2048,128]{1,0:T(8,128)(2,1)S(1)}, bf16[8,128,128]{2,1,0:T(8,128)(2,1)S(1)}) custom-call(bf16[1024,128]{1,0:T(8,128)(2,1)S(1)} %bitcast.5, bf16[8,128,128]{2,1,0:T(8,128)(2,1)S(1)} %copy-done.1, bf16[8,128,128]{2,1,0:T(8,128)(2,1)S(1)} %get-tuple-element.11.gate_ref, ...), custom_call_target="tpu_custom_call" | custom-call | tf_op jit(solution)/shard_map/finish_project/pallas_call | solution.py:141
  45.1 17.2 %all_to_all.36.both_ref = bf16[16,128,128]{2,1,0:T(8,128)(2,1)S(1)} all-to-all(bf16[16,128,128]{2,1,0:T(8,128)(2,1)S(1)} %bitcast.6), channel_id=1, replica_groups=mesh['groups'=2,'row'=16] {'row'}, dimensions={0} | all-to-all | bytes 1048576 | tf_op jit(solution)/shard_map/all_to_all | solution.py:118
  62.3 0.3 mix.3
  62.6 13.9 %all_to_all.37 = bf16[16,64,128]{2,1,0:T(8,128)(2,1)S(1)} all-to-all(bf16[16,64,128]{2,1,0:T(8,128)(2,1)S(1)} %mix.3), channel_id=1, replica_groups=mesh['groups'=2,'row'=16] {'row'}, dimensions={0} | all-to-all | bytes 524288 | tf_op jit(solution)/shard_map/all_to_all | solution.py:118
  76.5 1.5 %finish.1 = bf16[8,128,128]{2,1,0:T(8,128)(2,1)} custom-call(bf16[1024,128]{1,0:T(8,128)(2,1)S(1)} %bitcast.4, bf16[8,128,128]{2,1,0:T(8,128)(2,1)S(1)} %get-tuple-element.13.pair_ref, bf16[8,128,128]{2,1,0:T(8,128)(2,1)S(1)} %get-tuple-element.14.gate_ref, f32[2,2,128]{2,1,0:T(2,128)S(1)} %copy-done.8, f32[2,2,128]{2,1,0:T(2,128)S(1)} %copy-done.10, ...), custom_call_target="tpu_custom_call" | custom-call | tf_op jit(solution)/shard_map/finish/pallas_call | solution.py:151
Async XLA Ops:
  0.0 0.9 %copy-start = (bf16[8,128,128]{2,1,0:T(8,128)(2,1)S(1)}, bf16[8,128,128]{2,1,0:T(8,128)(2,1)}, u32[]{:S(2)}) copy-start(bf16[8,128,128]{2,1,0:T(8,128)(2,1)} %pair_ref.3) | copy-start | bytes 786436
  1.0 0.9 %copy-start.2 = (bf16[2,128,512]{2,1,0:T(8,128)(2,1)S(1)}, bf16[2,128,512]{2,1,0:T(8,128)(2,1)}, u32[]{:S(2)}) copy-start(bf16[2,128,512]{2,1,0:T(8,128)(2,1)} %proj_ref.3) | copy-start | bytes 786436
  1.9 0.8 %copy-start.4 = (bf16[2,128,128]{2,1,0:T(8,128)(2,1)S(1)}, bf16[2,128,128]{2,1,0:T(8,128)(2,1)}, u32[]{:S(2)}) copy-start(bf16[2,128,128]{2,1,0:T(8,128)(2,1)} %gatew_ref.3) | copy-start | bytes 196612
  2.7 0.7 copy-start.7
  3.4 0.7 copy-start.9
  4.1 0.7 copy-start.11
  27.9 14.4 %copy-start.5 = (bf16[2,128,128]{2,1,0:T(8,128)(2,1)S(1)}, bf16[2,128,128]{2,1,0:T(8,128)(2,1)}, u32[]{:S(2)}) copy-start(bf16[2,128,128]{2,1,0:T(8,128)(2,1)} %gatew_ref.3) | copy-start | bytes 196612
  27.9 14.4 %copy-start.6 = (bf16[2,128,128]{2,1,0:T(8,128)(2,1)S(1)}, bf16[2,128,128]{2,1,0:T(8,128)(2,1)}, u32[]{:S(2)}) copy-start(bf16[2,128,128]{2,1,0:T(8,128)(2,1)} %outw_ref.3) | copy-start | bytes 196612
  27.9 14.4 %copy-start.10 = (f32[2,2,128]{2,1,0:T(2,128)S(1)}, f32[2,2,128]{2,1,0:T(2,128)}, u32[]{:S(2)}) copy-start(f32[2,2,128]{2,1,0:T(2,128)} %bias_ref.5) | copy-start | bytes 6148
  27.9 14.4 %copy-start.12 = (s32[8,128]{1,0:T(8,128)S(1)}, s32[8,128]{1,0:T(8,128)}, u32[]{:S(2)}) copy-start(s32[8,128]{1,0:T(8,128)} %mask_ref.3) | copy-start | bytes 12292
  28.2 14.1 %copy-start.1 = (bf16[8,128,128]{2,1,0:T(8,128)(2,1)S(1)}, bf16[8,128,128]{2,1,0:T(8,128)(2,1)}, u32[]{:S(2)}) copy-start(bf16[8,128,128]{2,1,0:T(8,128)(2,1)} %pair_ref.3) | copy-start | bytes 786436
  28.2 14.1 %copy-start.3 = (bf16[2,128,512]{2,1,0:T(8,128)(2,1)S(1)}, bf16[2,128,512]{2,1,0:T(8,128)(2,1)}, u32[]{:S(2)}) copy-start(bf16[2,128,512]{2,1,0:T(8,128)(2,1)} %proj_ref.3) | copy-start | bytes 786436
  42.3 0.7 copy-start.8

commit v5 on v4

--- a/solution.py
+++ b/solution.py
@@ -29,7 +29,14 @@
     return centred * lax.rsqrt(spread + 1e-05)
 
 
-def project_kernel(per_group, pair_ref, mask_ref, gain_ref, bias_ref, proj_ref, gatew_ref, both_ref, gate_ref, panels):
+def project_kernel(per_group, *refs):
+    inputs, (both_ref, gate_ref), held, (panels, sems) = refs[:7], refs[7:9], refs[9:16], refs[16:]
+    copies = [pltpu.make_async_copy(src, dst, sems.at[n]) for n, (src, dst) in enumerate(zip(inputs, held))]
+    for copy in copies:
+        copy.start()
+    for copy in copies:
+        copy.wait()
+    pair_ref, mask_ref, gain_ref, bias_ref, proj_ref, gatew_ref, _ = held
     project_rows(per_group, 0, lambda r: pair_ref[r], mask_ref, gain_ref, bias_ref, proj_ref, gatew_ref, both_ref, gate_ref, panels)
 
 
@@ -96,11 +103,17 @@
     )
 
 
-def finish_kernel(merged_ref, pair_ref, gate_ref, gain_ref, bias_ref, outw_ref, result_ref, unit_scratch):
+def finish_kernel(merged_ref, pair_ref, gate_ref, gain_ref, bias_ref, outw_ref, result_ref, unit_scratch, done, sems):
+    copies = []
+
     def store(r, values):
-        result_ref[r] = values
+        done[r] = values
+        copies.append(pltpu.make_async_copy(done.at[r], result_ref.at[r], sems.at[r]))
+        copies[-1].start()
 
     finish_rows(1, store, merged_ref, pair_ref, gate_ref, gain_ref, bias_ref, outw_ref, unit_scratch)
+    for copy in copies:
+        copy.wait()
 
 
 def on_device(pair, mask, gains, biases, proj, gatew, outw):
@@ -108,6 +121,7 @@
     rows, tokens, channels = pair.shape
     per_group = channels // groups
     whole = pl.BlockSpec(memory_space=pltpu.VMEM)
+    hbm = pl.BlockSpec(memory_space=pltpu.HBM)
     params = pltpu.CompilerParams(vmem_limit_bytes=48 * 1024 * 1024)
     both_shape = jax.ShapeDtypeStruct((2 * channels * rows, tokens), BF16)
     pair_shape = jax.ShapeDtypeStruct(pair.shape, BF16)
@@ -128,15 +142,16 @@
         )(both.reshape(groups, 2 * per_group * rows, tokens))
         return product.reshape(channels * rows, tokens)
 
-    both, gate = pl.pallas_call(
+    inputs = (pair, mask, gains, biases, proj, gatew, outw)
+    both, gate, pair, mask, gains, biases, proj, gatew, outw = pl.pallas_call(
         functools.partial(project_kernel, per_group),
-        out_shape=(both_shape, pair_shape),
-        in_specs=[whole] * 6,
-        out_specs=(whole, whole),
-        scratch_shapes=[panels],
+        out_shape=(both_shape, pair_shape) + tuple(jax.ShapeDtypeStruct(a.shape, a.dtype) for a in inputs),
+        in_specs=[hbm] * 7,
+        out_specs=(whole,) * 9,
+        scratch_shapes=[panels, pltpu.SemaphoreType.DMA((7,))],
         compiler_params=params,
         name="project",
-    )(pair, mask, gains, biases, proj, gatew)
+    )(*(pltpu.with_memory_space_constraint(a, pltpu.HBM) for a in inputs))
     merged = exchange(mix(exchange(both), False))
     middle, both, gate = pl.pallas_call(
         functools.partial(step_kernel, per_group),
@@ -152,8 +167,8 @@
         finish_kernel,
         out_shape=pair_shape,
         in_specs=[whole] * 6,
-        out_specs=whole,
-        scratch_shapes=[unit_scratch],
+        out_specs=hbm,
+        scratch_shapes=[unit_scratch, pltpu.VMEM(pair.shape, BF16), pltpu.SemaphoreType.DMA((rows,))],
         compiler_params=params,
         name="finish",
     )(merged, middle, gate, gains, biases, outw)

time: 78.5 us -> 73.8 us (0.940)
  local copies, waits for them, and re-layouts: 5.45 us -> 0 us
  Pallas kernels: 5.61 us -> 6.74 us
    unnamed x26 -> x0, local copies, waits for them, and re-layouts: 5.45 us -> none
    pallas_call x1, Pallas kernels: 1.43 us -> 2.58 us  [on_device(): pl.pallas_call(functools.partial(project_kernel, per_group), out_shape=(b...]
where the time goes in v5:
time: 73.8 us; the launch traced here: 73.6 us
  blocking collectives  66.8 us (91%)
  Pallas kernels  6.74 us (9%)
    all_to_all x4, blocking collectives, exchange(): return lax.all_to_all(array, 'row', split_axis=0, concat_axis=0, tiled=True)  66.8 us
    pallas_call x1, Pallas kernels, on_device(): pl.pallas_call(functools.partial(project_kernel, per_group), out_shape=(b...  2.58 us
    pallas_call x1, Pallas kernels, on_device(): pl.pallas_call(functools.partial(step_kernel, per_group), out_shape=(pair...  2.1 us
    pallas_call x1, Pallas kernels, on_device(): pl.pallas_call(finish_kernel, out_shape=pair_shape, in_specs=[whole] * 6,...  1.51 us

profile of v5, /device:TPU:0, one launch (start us, length us, event | category | flops | bytes accessed | tf_op | source)
XLA Modules:
  0.0 73.6 jit_solution(3342925005171369275)
XLA Ops:
  0.0 2.6 %project.1 = (bf16[2048,128]{1,0:T(8,128)(2,1)S(1)}, bf16[8,128,128]{2,1,0:T(8,128)(2,1)S(1)}, bf16[8,128,128]{2,1,0:T(8,128)(2,1)S(1)}, s32[8,128]{1,0:T(8,128)...) custom-call(bf16[8,128,128]{2,1,0:T(8,128)(2,1)} %refs_0_.1, ...), custom_call_target="tpu_custom_call" | custom-call | tf_op jit(solution)/shard_map/project/pallas_call | solution.py:146
  2.6 21.7 %all_to_all.34.both_ref = bf16[16,128,128]{2,1,0:T(8,128)(2,1)S(1)} all-to-all(bf16[16,128,128]{2,1,0:T(8,128)(2,1)S(1)} %bitcast.6), channel_id=1, replica_groups=mesh['groups'=2,'row'=16] {'row'}, dimensions={0} | all-to-all | bytes 1048576 | tf_op jit(solution)/shard_map/all_to_all | solution.py:132
  24.2 0.3 mix.2
  24.5 13.9 %all_to_all.35 = bf16[16,64,128]{2,1,0:T(8,128)(2,1)S(1)} all-to-all(bf16[16,64,128]{2,1,0:T(8,128)(2,1)S(1)} %mix.2), channel_id=1, replica_groups=mesh['groups'=2,'row'=16] {'row'}, dimensions={0} | all-to-all | bytes 524288 | tf_op jit(solution)/shard_map/all_to_all | solution.py:132
  38.5 2.1 %finish_project.1 = (bf16[8,128,128]{2,1,0:T(8,128)(2,1)S(1)}, bf16[2048,128]{1,0:T(8,128)(2,1)S(1)}, bf16[8,128,128]{2,1,0:T(8,128)(2,1)S(1)}) custom-call(bf16[1024,128]{1,0:T(8,128)(2,1)S(1)} %bitcast.5, bf16[8,128,128]{2,1,0:T(8,128)(2,1)S(1)} %get-tuple-element.18.pair_ref, bf16[8,128,128]{2,1,0:T(8,128)(2,1)S(1)} %get-tuple-element.19.gate_ref, ...), custom_call_target="tpu_custom_call" | custom-call | tf_op jit(solution)/shard_map/finish_project/pallas_call | solution.py:156
  40.6 17.2 %all_to_all.36.both_ref = bf16[16,128,128]{2,1,0:T(8,128)(2,1)S(1)} all-to-all(bf16[16,128,128]{2,1,0:T(8,128)(2,1)S(1)} %bitcast.7), channel_id=1, replica_groups=mesh['groups'=2,'row'=16] {'row'}, dimensions={0} | all-to-all | bytes 1048576 | tf_op jit(solution)/shard_map/all_to_all | solution.py:132
  57.8 0.3 mix.3
  58.1 13.9 %all_to_all.37 = bf16[16,64,128]{2,1,0:T(8,128)(2,1)S(1)} all-to-all(bf16[16,64,128]{2,1,0:T(8,128)(2,1)S(1)} %mix.3), channel_id=1, replica_groups=mesh['groups'=2,'row'=16] {'row'}, dimensions={0} | all-to-all | bytes 524288 | tf_op jit(solution)/shard_map/all_to_all | solution.py:132
  72.0 1.5 %finish.1 = bf16[8,128,128]{2,1,0:T(8,128)(2,1)} custom-call(bf16[1024,128]{1,0:T(8,128)(2,1)S(1)} %bitcast.4, bf16[8,128,128]{2,1,0:T(8,128)(2,1)S(1)} %get-tuple-element.27.pair_ref, bf16[8,128,128]{2,1,0:T(8,128)(2,1)S(1)} %get-tuple-element.28.gate_ref, f32[2,2,128]{2,1,0:T(2,128)S(1)} %get-tuple-element.21.gain_ref, ...), custom_call_target="tpu_custom_call" | custom-call | tf_op jit(solution)/shard_map/finish/pallas_call | solution.py:166

commit v6 on v5

v6 whole, which is shorter than its diff:
```python
import functools

import jax
import jax.numpy as jnp
from jax import lax
from jax.experimental import pallas as pl
from jax.experimental.pallas import tpu as pltpu
from jax.sharding import PartitionSpec as P

F32 = jnp.float32
BF16 = jnp.bfloat16
NT = (((1,), (1,)), ((), ()))
NN = (((1,), (0,)), ((), ()))
TN = (((0,), (0,)), ((), ()))


def dot(a, b, dims):
    return lax.dot_general(a, b, dims, preferred_element_type=F32)


def sigmoid(values):
    return 0.5 * jnp.tanh(0.5 * values) + 0.5


def unit(values, axis):
    scale = 1.0 / values.shape[axis]
    centred = values - jnp.sum(values, axis=axis, keepdims=True) * scale
    spread = jnp.sum(centred * centred, axis=axis, keepdims=True) * scale
    return centred * lax.rsqrt(spread + 1e-05)


def chunks(rows, tokens):
    wide = max(1, min(rows, 256 // tokens))
    return [list(range(start, min(start + wide, rows))) for start in range(0, rows, wide)]


def span(chunk, tokens):
    return slice(chunk[0] * tokens, (chunk[-1] + 1) * tokens)


def lanes(parts):
    return parts[0] if len(parts) == 1 else jnp.concatenate(parts, axis=1)


def affine(values, gain, bias, tokens):
    parts = [values[:, n : n + tokens] * gain + bias for n in range(0, values.shape[1], tokens)]
    return lanes(parts).astype(BF16)


def store_panels(panels, per_group, chunk, tokens, products, mask):
    channels = products.shape[0] // 4
    for side in range(2):
        base = 2 * side * channels
        gated = sigmoid(products[base : base + channels]) * products[base + channels : base + 2 * channels] * mask
        for h, r in enumerate(chunk):
            for g in range(channels // per_group):
                start = (2 * g + side) * per_group
                panels[start : start + per_group, r, :] = gated[
                    g * per_group : (g + 1) * per_group, h * tokens : (h + 1) * tokens
                ]


def mask_lanes(mask_ref, chunk):
    return lanes([mask_ref[r : r + 1].astype(F32) for r in chunk])


def project_kernel(per_group, *refs):
    inputs, both_ref, held, (panels, sems) = refs[:7], refs[7], refs[8:15], refs[15:]
    copies = [pltpu.make_async_copy(src, dst, sems.at[n]) for n, (src, dst) in enumerate(zip(inputs, held))]
    for copy in copies:
        copy.start()
    for copy in copies[:5]:
        copy.wait()
    pair_ref, mask_ref, gain_ref, bias_ref, proj_ref, _, _ = held
    rows, tokens, channels = pair_ref.shape
    weights_t = proj_ref[0].T
    for chunk in chunks(rows, tokens):
        pair = pair_ref[chunk[0] : chunk[-1] + 1].reshape(len(chunk) * tokens, channels)
        normed = (unit(pair.astype(F32), 1) * gain_ref[0, 0:1] + bias_ref[0, 0:1]).astype(BF16)
        products = dot(weights_t, normed, NT)
        store_panels(panels, per_group, chunk, tokens, products, mask_lanes(mask_ref, chunk))
    both_ref[...] = panels[...].astype(BF16).reshape(both_ref.shape)
    for copy in copies[5:]:
        copy.wait()


def prepare_kernel(
    pair_ref, gain_ref, bias_ref, proj_ref, gatew_ref, outw_ref,
    pair_t_ref, gate_t_ref, columns_ref, proj_t_ref, gatew_t_ref, outw_t_ref,
):
    rows, tokens, channels = pair_ref.shape

    def column(ref, which, norm):
        return jnp.broadcast_to(ref[which, norm : norm + 1], (tokens, channels)).T

    for n, (which, norm) in enumerate(((0, 1), (1, 0), (1, 1))):
        columns_ref[2 * n] = column(gain_ref, which, norm)
        columns_ref[2 * n + 1] = column(bias_ref, which, norm)
    proj_t_ref[...] = proj_ref[1].T
    gatew_t_ref[...] = gatew_ref[1].T
    outw_t_ref[0] = outw_ref[0].T
    outw_t_ref[1] = outw_ref[1].T
    first_t = gatew_ref[0].T
    gain, bias = column(gain_ref, 0, 0), column(bias_ref, 0, 0)
    for chunk in chunks(rows, tokens):
        pair_t = lanes([pair_ref[r].T for r in chunk])
        pair_t_ref[:, span(chunk, tokens)] = pair_t
        normed = affine(unit(pair_t.astype(F32), 0), gain, bias, tokens)
        gate_t_ref[:, span(chunk, tokens)] = sigmoid(dot(first_t, normed, NN)).astype(BF16)


def gate_kernel(normed_t_ref, gatew_t_ref, gate_t_ref):
    step = min(256, normed_t_ref.shape[1])
    for start in range(0, normed_t_ref.shape[1], step):
        gate = sigmoid(dot(gatew_t_ref[...], normed_t_ref[:, start : start + step], NN))
        gate_t_ref[:, start : start + step] = gate.astype(BF16)


def mix_kernel(per_group, rows, incoming, both_ref, product_ref):
    groups, _, tokens = both_ref.shape
    step = 2 * rows

    def matrices(side, pair):
        start = (side * per_group + 2 * pair) * rows
        block = both_ref[:, start : start + step, :].astype(F32)
        return [block[:, h * rows : (h + 1) * rows].reshape(groups * rows, tokens).astype(BF16) for h in range(2)]

    for pair in range(per_group // 2):
        lefts, rights = matrices(0, pair), matrices(1, pair)
        sums = [
            dot(left, right, TN if incoming else NT).reshape(groups, rows, tokens)
            for left, right in zip(lefts, rights)
        ]
        product_ref[:, pair * step : (pair + 1) * step, :] = jnp.concatenate(sums, axis=1).astype(BF16)


def finish_rows(emit, merged_ref, pair_t_ref, gate_t_ref, gain, bias, outw_t, unit_scratch):
    channels, rows, tokens = unit_scratch.shape
    unit_scratch[...] = unit(merged_ref[...].astype(F32).reshape(channels, rows, tokens), 0)
    for chunk in chunks(rows, tokens):
        normed = lanes([(unit_scratch[:, r, :] * gain + bias).astype(BF16) for r in chunk])
        part = span(chunk, tokens)
        change = gate_t_ref[:, part].astype(F32) * dot(outw_t, normed, NN)
        emit(chunk, part, (pair_t_ref[:, part].astype(F32) + change).astype(BF16))


def step_kernel(
    per_group, merged_ref, pair_t_ref, gate_t_ref, mask_ref, columns_ref, outw_t_ref, proj_t_ref,
    both_ref, middle_t_ref, normed_t_ref, unit_scratch, panels,
):
    tokens = mask_ref.shape[1]

    def emit(chunk, part, middle):
        middle_t_ref[:, part] = middle
        normed = affine(unit(middle.astype(F32), 0), columns_ref[2], columns_ref[3], tokens)
        normed_t_ref[:, part] = normed
        products = dot(proj_t_ref[...], normed, NN)
        store_panels(panels, per_group, chunk, tokens, products, mask_lanes(mask_ref, chunk))

    finish_rows(
        emit, merged_ref, pair_t_ref, gate_t_ref, columns_ref[0], columns_ref[1], outw_t_ref[0], unit_scratch
    )
    both_ref[...] = panels[...].astype(BF16).reshape(both_ref.shape)


def finish_kernel(
    merged_ref, middle_t_ref, gate_t_ref, columns_ref, outw_t_ref, result_ref, unit_scratch, done, sems
):
    tokens = unit_scratch.shape[2]
    copies = []

    def emit(chunk, part, result):
        for h, r in enumerate(chunk):
            done[r] = result[:, h * tokens : (h + 1) * tokens].T
            copies.append(pltpu.make_async_copy(done.at[r], result_ref.at[r], sems.at[r]))
            copies[-1].start()

    finish_rows(
        emit, merged_ref, middle_t_ref, gate_t_ref, columns_ref[4], columns_ref[5], outw_t_ref[1], unit_scratch
    )
    for copy in copies:
        copy.wait()


def on_device(*inputs):
    groups = lax.axis_size("row")
    rows, tokens, channels = inputs[0].shape
    per_group = channels // groups
    whole = pl.BlockSpec(memory_space=pltpu.VMEM)
    hbm = pl.BlockSpec(memory_space=pltpu.HBM)
    params = pltpu.CompilerParams(vmem_limit_bytes=48 * 1024 * 1024)
    shape = jax.ShapeDtypeStruct
    both_shape = shape((2 * channels * rows, tokens), BF16)
    flat_shape = shape((channels, rows * tokens), BF16)
    panels = pltpu.VMEM((2 * channels, rows, tokens), F32)
    unit_scratch = pltpu.VMEM((channels, rows, tokens), F32)
    beside = pl.CostEstimate(flops=10**9, bytes_accessed=4 * 2**20, transcendentals=0)

    def exchange(array):
        return lax.all_to_all(array, "row", split_axis=0, concat_axis=0, tiled=True)

    def mix(both, incoming):
        product = pl.pallas_call(
            functools.partial(mix_kernel, per_group, rows, incoming),
            out_shape=shape((groups, per_group * rows, tokens), BF16),
            in_specs=[whole],
            out_specs=whole,
            compiler_params=params,
            name="mix",
        )(both.reshape(groups, 2 * per_group * rows, tokens))
        return product.reshape(channels * rows, tokens)

    both, pair, mask, gains, biases, proj, gatew, outw = pl.pallas_call(
        functools.partial(project_kernel, per_group),
        out_shape=(both_shape,) + tuple(shape(a.shape, a.dtype) for a in inputs),
        in_specs=[hbm] * 7,
        out_specs=(whole,) * 8,
        scratch_shapes=[panels, pltpu.SemaphoreType.DMA((7,))],
        compiler_params=params,
        name="project",
    )(*(pltpu.with_memory_space_constraint(a, pltpu.HBM) for a in inputs))
    both = exchange(both)
    pair_t, gate_t, columns, proj_t, gatew_t, outw_t = pl.pallas_call(
        prepare_kernel,
        out_shape=(
            flat_shape,
            flat_shape,
            shape((6, channels, tokens), F32),
            shape((4 * channels, channels), BF16),
            shape((channels, channels), BF16),
            shape((2, channels, channels), BF16),
        ),
        in_specs=[whole] * 6,
        out_specs=(whole,) * 6,
        compiler_params=params,
        cost_estimate=beside,
        name="prepare",
    )(pair, gains, biases, proj, gatew, outw)
    merged = exchange(mix(both, False))
    both, middle_t, normed_t = pl.pallas_call(
        functools.partial(step_kernel, per_group),
        out_shape=(both_shape, flat_shape, flat_shape),
        in_specs=[whole] * 7,
        out_specs=(whole,) * 3,
        scratch_shapes=[unit_scratch, panels],
        compiler_params=params,
        name="finish_project",
    )(merged, pair_t, gate_t, mask, columns, outw_t, proj_t)
    both = exchange(both)
    gate_t = pl.pallas_call(
        gate_kernel,
        out_shape=flat_shape,
        in_specs=[whole] * 2,
        out_specs=whole,
        compiler_params=params,
        cost_estimate=beside,
        name="gate",
    )(normed_t, gatew_t)
    merged = exchange(mix(both, True))
    return pl.pallas_call(
        finish_kernel,
        out_shape=shape((rows, tokens, channels), BF16),
        in_specs=[whole] * 5,
        out_specs=hbm,
        scratch_shapes=[unit_scratch, pltpu.VMEM((rows, tokens, channels), BF16), pltpu.SemaphoreType.DMA((rows,))],
        compiler_params=params,
        name="finish",
    )(merged, middle_t, gate_t, columns, outw_t)


def solution(mesh):
    rows = ("groups", "row")
    return jax.shard_map(
        on_device,
        mesh=mesh,
        in_specs=(P(rows, None, None), P(rows, None), P(), P(), P(), P(), P()),
        out_specs=P(rows, None, None),
        check_vma=False,
    )
```

time: 73.8 us -> 75.7 us (1.026)
  blocking collectives: 66.8 us -> 38.9 us
  waiting for transfers between devices: 0 us -> 19.4 us
  starting transfers between devices: 0 us -> 8.2 us
  Pallas kernels: 6.74 us -> 8.77 us
    all_to_all x4 -> x2, blocking collectives: 66.8 us -> 38.9 us  [exchange(): return lax.all_to_all(array, 'row', split_axis=0, concat_axis=0, tiled=True)]
    all_to_all x0 -> x2, waiting for transfers between devices: none -> 19.4 us  [exchange(): return lax.all_to_all(array, 'row', split_axis=0, concat_axis=0, tiled=True)]
    all_to_all x0 -> x2, starting transfers between devices: none -> 8.2 us  [exchange(): return lax.all_to_all(array, 'row', split_axis=0, concat_axis=0, tiled=True)]
    pallas_call x2, Pallas kernels: 0.55 us -> 1.97 us  [mix(): pl.pallas_call(functools.partial(mix_kernel, per_group, rows, incoming),...]
    pallas_call x2 -> x4, Pallas kernels: 3.61 us -> 4.29 us  [the longest x1 2.06 us: on_device(): pl.pallas_call(functools.partial(step_kernel, per_group), out_shape=(both...]
  transfers between devices with their start and end apart: 0 -> 2, of which waited for: 0 -> 2; matrix products, arithmetic and copies ran while one was open for 0% -> 0% of each run, Pallas kernels for 0% -> 1%
where the time goes in v6:
time: 75.7 us; the launch traced here: 75.3 us
  blocking collectives  38.9 us (51%)
  waiting for transfers between devices  19.4 us (26%)
  Pallas kernels  8.77 us (12%)
  starting transfers between devices  8.2 us (11%)
    all_to_all x2, blocking collectives, exchange(): return lax.all_to_all(array, 'row', split_axis=0, concat_axis=0, tiled=True)  38.9 us
    all_to_all x2, waiting for transfers between devices, exchange(): return lax.all_to_all(array, 'row', split_axis=0, concat_axis=0, tiled=True)  19.4 us
    all_to_all x2, starting transfers between devices, exchange(): return lax.all_to_all(array, 'row', split_axis=0, concat_axis=0, tiled=True)  8.2 us
    pallas_call x1, Pallas kernels, on_device(): pl.pallas_call(functools.partial(project_kernel, per_group), out_shape=(b...  2.51 us
    pallas_call x1, Pallas kernels, on_device(): pl.pallas_call(functools.partial(step_kernel, per_group), out_shape=(both...  2.06 us
    pallas_call x2, Pallas kernels, mix(): pl.pallas_call(functools.partial(mix_kernel, per_group, rows, incoming),...  1.97 us
  transfers between devices with their start and end apart: 2, of which 2 were waited for; matrix products, arithmetic and copies ran while one was open for 0% of the time, Pallas kernels for 1%

profile of v6, /device:TPU:0, one launch (start us, length us, event | category | flops | bytes accessed | tf_op | source)
XLA Modules:
  0.0 75.3 jit_solution(13178688514870220013)
XLA Ops:
  0.0 2.5 %project.1 = (bf16[2048,128]{1,0:T(8,128)(2,1)S(1)}, bf16[8,128,128]{2,1,0:T(8,128)(2,1)S(1)}, s32[8,128]{1,0:T(8,128)S(1)}, f32[2,2,128]{2,1,0:T(2,128)S(1)}, f...) custom-call(bf16[8,128,128]{2,1,0:T(8,128)(2,1)} %refs_0_.1, ...), custom_call_target="tpu_custom_call" | custom-call | tf_op jit(solution)/shard_map/project/pallas_call | solution.py:213
  2.5 21.7 %all_to_all.34.both_ref = bf16[16,128,128]{2,1,0:T(8,128)(2,1)S(1)} all-to-all(bf16[16,128,128]{2,1,0:T(8,128)(2,1)S(1)} %bitcast.6), channel_id=1, replica_groups=mesh['groups'=2,'row'=16] {'row'}, dimensions={0} | all-to-all | bytes 1048576 | tf_op jit(solution)/shard_map/all_to_all | solution.py:200
  24.2 1.0 %mix.2 = bf16[16,64,128]{2,1,0:T(8,128)(2,1)} custom-call(bf16[16,128,128]{2,1,0:T(8,128)(2,1)S(1)} %all_to_all.34.both_ref), custom_call_target="tpu_custom_call" | custom-call | tf_op jit(solution)/shard_map/mix/pallas_call | solution.py:203
  25.2 4.1 %all-to-all-start.1 = ((bf16[16,64,128]{2,1,0:T(8,128)(2,1)}), bf16[16,64,128]{2,1,0:T(8,128)(2,1)S(1)}, u32[]{:S(2)}, u32[]{:S(2)}) async-start(bf16[16,64,128]{2,1,0:T(8,128)(2,1)} %mix.2), calls=%async_computation.1 | async-start | bytes 524288 | tf_op jit(solution)/shard_map/all_to_all | solution.py:200
  29.3 0.5 prepare.1
  29.8 9.6 %all-to-all-done.1 = bf16[16,64,128]{2,1,0:T(8,128)(2,1)S(1)} async-done(((bf16[16,64,128]{2,1,0:T(8,128)(2,1)}), bf16[16,64,128]{2,1,0:T(8,128)(2,1)S(1)}, u32[]{:S(2)}, u32[]{:S(2)}) %all-to-all-start.1) | async-done | bytes 262176 | tf_op jit(solution)/shard_map/all_to_all | solution.py:200
  39.3 2.1 %finish_project.1 = (bf16[2048,128]{1,0:T(8,128)(2,1)S(1)}, bf16[128,1024]{1,0:T(8,128)(2,1)S(1)}, bf16[128,1024]{1,0:T(8,128)(2,1)S(1)}) custom-call(bf16[1024,128]{1,0:T(8,128)(2,1)S(1)} %bitcast.4, bf16[128,1024]{1,0:T(8,128)(2,1)S(1)} %get-tuple-element.29.pair_t_ref, bf16[128,1024]{1,0:T(8,128)(2,1)S(1)} %get-tuple-element.30.gate_t_ref, ...), custom_call_target="tpu_custom_call" | custom-call | tf_op jit(solution)/shard_map/finish_project/pallas_call | solution.py:240
  41.4 17.2 %all_to_all.35.both_ref = bf16[16,128,128]{2,1,0:T(8,128)(2,1)S(1)} all-to-all(bf16[16,128,128]{2,1,0:T(8,128)(2,1)S(1)} %bitcast.7), channel_id=1, replica_groups=mesh['groups'=2,'row'=16] {'row'}, dimensions={0} | all-to-all | bytes 1048576 | tf_op jit(solution)/shard_map/all_to_all | solution.py:200
  58.6 1.0 %mix.3 = bf16[16,64,128]{2,1,0:T(8,128)(2,1)} custom-call(bf16[16,128,128]{2,1,0:T(8,128)(2,1)S(1)} %all_to_all.35.both_ref), custom_call_target="tpu_custom_call" | custom-call | tf_op jit(solution)/shard_map/mix/pallas_call | solution.py:203
  59.6 4.1 %all-to-all-start.3 = ((bf16[16,64,128]{2,1,0:T(8,128)(2,1)}), bf16[16,64,128]{2,1,0:T(8,128)(2,1)S(1)}, u32[]{:S(2)}, u32[]{:S(2)}) async-start(bf16[16,64,128]{2,1,0:T(8,128)(2,1)} %mix.3), calls=%async_computation.3 | async-start | bytes 524288 | tf_op jit(solution)/shard_map/all_to_all | solution.py:200
  63.7 0.2 gate.1.gate_t_ref
  64.0 9.8 %all-to-all-done.3 = bf16[16,64,128]{2,1,0:T(8,128)(2,1)S(1)} async-done(((bf16[16,64,128]{2,1,0:T(8,128)(2,1)}), bf16[16,64,128]{2,1,0:T(8,128)(2,1)S(1)}, u32[]{:S(2)}, u32[]{:S(2)}) %all-to-all-start.3) | async-done | bytes 262176 | tf_op jit(solution)/shard_map/all_to_all | solution.py:200
  73.8 1.5 %finish.1 = bf16[8,128,128]{2,1,0:T(8,128)(2,1)} custom-call(bf16[1024,128]{1,0:T(8,128)(2,1)S(1)} %bitcast.5, bf16[128,1024]{1,0:T(8,128)(2,1)S(1)} %get-tuple-element.36.middle_t_ref, bf16[128,1024]{1,0:T(8,128)(2,1)S(1)} %gate.1.gate_t_ref, f32[6,128,128]{2,1,0:T(8,128)S(1)} %get-tuple-element.32.columns_ref, ...), custom_call_target="tpu_custom_call" | custom-call | tf_op jit(solution)/shard_map/finish/pallas_call | solution.py:260
Async XLA Ops:
  25.2 14.2 %all-to-all-start.1 = ((bf16[16,64,128]{2,1,0:T(8,128)(2,1)}), bf16[16,64,128]{2,1,0:T(8,128)(2,1)S(1)}, u32[]{:S(2)}, u32[]{:S(2)}) async-start(bf16[16,64,128]{2,1,0:T(8,128)(2,1)} %mix.2), calls=%async_computation.1 | async-start | bytes 524288 | tf_op jit(solution)/shard_map/all_to_all | solution.py:200
  59.6 14.2 %all-to-all-start.3 = ((bf16[16,64,128]{2,1,0:T(8,128)(2,1)}), bf16[16,64,128]{2,1,0:T(8,128)(2,1)S(1)}, u32[]{:S(2)}, u32[]{:S(2)}) async-start(bf16[16,64,128]{2,1,0:T(8,128)(2,1)} %mix.3), calls=%async_computation.3 | async-start | bytes 524288 | tf_op jit(solution)/shard_map/all_to_all | solution.py:200

commit v7 on v6

v7 whole, which is shorter than its diff:
```python
import functools

import jax
import jax.numpy as jnp
from jax import lax
from jax.experimental import pallas as pl
from jax.experimental.pallas import tpu as pltpu
from jax.sharding import PartitionSpec as P

F32 = jnp.float32
BF16 = jnp.bfloat16
LANES = 128
NT = (((1,), (1,)), ((), ()))
NN = (((1,), (0,)), ((), ()))
TN = (((0,), (0,)), ((), ()))


def dot(a, b, dims):
    return lax.dot_general(a, b, dims, preferred_element_type=F32)


def sigmoid(values):
    return 0.5 * jnp.tanh(0.5 * values) + 0.5


def unit(values, axis):
    scale = 1.0 / values.shape[axis]
    centred = values - jnp.sum(values, axis=axis, keepdims=True) * scale
    spread = jnp.sum(centred * centred, axis=axis, keepdims=True) * scale
    return centred * lax.rsqrt(spread + 1e-05)


def chunks(rows, tokens):
    wide = max(1, min(rows, 256 // tokens))
    return [list(range(start, min(start + wide, rows))) for start in range(0, rows, wide)]


def span(chunk, tokens):
    return slice(chunk[0] * tokens, (chunk[-1] + 1) * tokens)


def lanes(parts):
    return parts[0] if len(parts) == 1 else jnp.concatenate(parts, axis=1)


def affine(values, gain, bias, tokens):
    parts = [values[:, n : n + tokens] * gain + bias for n in range(0, values.shape[1], tokens)]
    return lanes(parts).astype(BF16)


def store_panels(panels, per_group, rows, chunk, tokens, products, mask):
    channels = products.shape[0] // 5
    for side in range(2):
        base = 2 * side * channels
        gated = sigmoid(products[base : base + channels]) * products[base + channels : base + 2 * channels] * mask
        for h, r in enumerate(chunk):
            for g in range(channels // per_group):
                where = pl.ds((2 * g + side) * per_group * rows + r, per_group, stride=rows)
                for t in range(tokens // LANES):
                    first = h * tokens + t * LANES
                    panels[t, where, :] = gated[g * per_group : (g + 1) * per_group, first : first + LANES]
    return sigmoid(products[4 * channels :]).astype(BF16)


def mask_lanes(mask_ref, chunk):
    return lanes([mask_ref[r : r + 1].astype(F32) for r in chunk])


def column(ref, which, norm, tokens):
    row = ref[which, norm : norm + 1]
    return jnp.broadcast_to(row, (tokens, row.shape[1])).T


def project_kernel(per_group, *refs):
    inputs, refs = refs[:7], refs[7:]
    both_ref, pair_t_ref, gate_t_ref, mask_ref, columns_ref, proj_t_ref, outw_t_ref = refs[:7]
    pair_ref, gain_ref, bias_ref, proj_ref, gatew_ref, outw_ref, panels, sems = refs[7:]
    held = (pair_ref, mask_ref, gain_ref, bias_ref, proj_ref, gatew_ref, outw_ref)
    copies = [pltpu.make_async_copy(src, dst, sems.at[n]) for n, (src, dst) in enumerate(zip(inputs, held))]
    for copy in copies:
        copy.start()
    for copy in copies:
        copy.wait()
    rows, tokens, channels = pair_ref.shape
    for which in range(2):
        proj_t_ref[which, : 4 * channels] = proj_ref[which].T
        proj_t_ref[which, 4 * channels :] = gatew_ref[which].T
        outw_t_ref[which] = outw_ref[which].T
    for n, (which, norm) in enumerate(((0, 1), (1, 0), (1, 1))):
        columns_ref[2 * n] = column(gain_ref, which, norm, tokens)
        columns_ref[2 * n + 1] = column(bias_ref, which, norm, tokens)
    gain, bias = column(gain_ref, 0, 0, tokens), column(bias_ref, 0, 0, tokens)
    for chunk in chunks(rows, tokens):
        part = span(chunk, tokens)
        pair_t = lanes([pair_ref[r].T for r in chunk])
        pair_t_ref[:, part] = pair_t
        normed = affine(unit(pair_t.astype(F32), 0), gain, bias, tokens)
        products = dot(proj_t_ref[0], normed, NN)
        gate_t_ref[:, part] = store_panels(
            panels, per_group, rows, chunk, tokens, products, mask_lanes(mask_ref, chunk)
        )
    for t in range(tokens // LANES):
        both_ref[:, t * LANES : (t + 1) * LANES] = panels[t].astype(BF16)


def mix_kernel(per_group, rows, incoming, both_ref, product_ref):
    groups, _, tokens = both_ref.shape
    step = 2 * rows

    def matrices(side, pair):
        start = (side * per_group + 2 * pair) * rows
        block = both_ref[:, start : start + step, :].astype(F32)
        return [block[:, h * rows : (h + 1) * rows].reshape(groups * rows, tokens).astype(BF16) for h in range(2)]

    for pair in range(per_group // 2):
        lefts, rights = matrices(0, pair), matrices(1, pair)
        sums = [
            dot(left, right, TN if incoming else NT).reshape(groups, rows, tokens)
            for left, right in zip(lefts, rights)
        ]
        product_ref[:, pair * step : (pair + 1) * step, :] = jnp.concatenate(sums, axis=1).astype(BF16)


def finish_rows(emit, rows, merged_ref, pair_t_ref, gate_t_ref, gain, bias, outw_t, unit_scratch):
    tokens = merged_ref.shape[1]
    channels = merged_ref.shape[0] // rows
    sums = merged_ref[...].astype(F32).reshape(channels, rows, tokens)
    units = unit(sums, 0).reshape(channels * rows, tokens)
    tiles = range(tokens // LANES)
    for t in tiles:
        unit_scratch[t] = units[:, t * LANES : (t + 1) * LANES]
    for chunk in chunks(rows, tokens):
        part = span(chunk, tokens)
        units = lanes([unit_scratch[t, pl.ds(r, channels, stride=rows), :] for r in chunk for t in tiles])
        normed = affine(units, gain, bias, tokens)
        change = gate_t_ref[:, part].astype(F32) * dot(outw_t, normed, NN)
        emit(chunk, part, (pair_t_ref[:, part].astype(F32) + change).astype(BF16))


def step_kernel(
    per_group, merged_ref, pair_t_ref, gate_t_ref, mask_ref, columns_ref, outw_t_ref, proj_t_ref,
    both_ref, middle_t_ref, gate1_t_ref, unit_scratch, panels,
):
    rows, tokens = mask_ref.shape

    def emit(chunk, part, middle):
        middle_t_ref[:, part] = middle
        normed = affine(unit(middle.astype(F32), 0), columns_ref[2], columns_ref[3], tokens)
        products = dot(proj_t_ref[1], normed, NN)
        gate1_t_ref[:, part] = store_panels(
            panels, per_group, rows, chunk, tokens, products, mask_lanes(mask_ref, chunk)
        )

    finish_rows(
        emit, rows, merged_ref, pair_t_ref, gate_t_ref, columns_ref[0], columns_ref[1], outw_t_ref[0], unit_scratch
    )
    for t in range(tokens // LANES):
        both_ref[:, t * LANES : (t + 1) * LANES] = panels[t].astype(BF16)


def finish_kernel(
    merged_ref, middle_t_ref, gate_t_ref, columns_ref, outw_t_ref, result_ref, unit_scratch, done, sems
):
    rows, tokens, _ = result_ref.shape
    copies = []

    def emit(chunk, part, result):
        for h, r in enumerate(chunk):
            done[r] = result[:, h * tokens : (h + 1) * tokens].T
            copies.append(pltpu.make_async_copy(done.at[r], result_ref.at[r], sems.at[r]))
            copies[-1].start()

    finish_rows(
        emit, rows, merged_ref, middle_t_ref, gate_t_ref, columns_ref[4], columns_ref[5], outw_t_ref[1], unit_scratch
    )
    for copy in copies:
        copy.wait()


def on_device(*inputs):
    groups = lax.axis_size("row")
    rows, tokens, channels = inputs[0].shape
    per_group = channels // groups
    whole = pl.BlockSpec(memory_space=pltpu.VMEM)
    hbm = pl.BlockSpec(memory_space=pltpu.HBM)
    params = pltpu.CompilerParams(vmem_limit_bytes=48 * 1024 * 1024)
    shape = jax.ShapeDtypeStruct
    both_shape = shape((2 * channels * rows, tokens), BF16)
    flat_shape = shape((channels, rows * tokens), BF16)
    panels = pltpu.VMEM((tokens // LANES, 2 * channels * rows, LANES), F32)
    unit_scratch = pltpu.VMEM((tokens // LANES, channels * rows, LANES), F32)

    def exchange(array):
        return lax.all_to_all(array, "row", split_axis=0, concat_axis=0, tiled=True)

    def mix(both, incoming):
        product = pl.pallas_call(
            functools.partial(mix_kernel, per_group, rows, incoming),
            out_shape=shape((groups, per_group * rows, tokens), BF16),
            in_specs=[whole],
            out_specs=whole,
            compiler_params=params,
            name="mix",
        )(both.reshape(groups, 2 * per_group * rows, tokens))
        return product.reshape(channels * rows, tokens)

    both, pair_t, gate_t, mask, columns, proj_t, outw_t = pl.pallas_call(
        functools.partial(project_kernel, per_group),
        out_shape=(
            both_shape,
            flat_shape,
            flat_shape,
            shape((rows, tokens), inputs[1].dtype),
            shape((6, channels, tokens), F32),
            shape((2, 5 * channels, channels), BF16),
            shape((2, channels, channels), BF16),
        ),
        in_specs=[hbm] * 7,
        out_specs=(whole,) * 7,
        scratch_shapes=[pltpu.VMEM(inputs[n].shape, inputs[n].dtype) for n in (0, 2, 3, 4, 5, 6)]
        + [panels, pltpu.SemaphoreType.DMA((7,))],
        compiler_params=params,
        name="project",
    )(*(pltpu.with_memory_space_constraint(a, pltpu.HBM) for a in inputs))
    merged = exchange(mix(exchange(both), False))
    both, middle_t, gate_t = pl.pallas_call(
        functools.partial(step_kernel, per_group),
        out_shape=(both_shape, flat_shape, flat_shape),
        in_specs=[whole] * 7,
        out_specs=(whole,) * 3,
        scratch_shapes=[unit_scratch, panels],
        compiler_params=params,
        name="finish_project",
    )(merged, pair_t, gate_t, mask, columns, outw_t, proj_t)
    merged = exchange(mix(exchange(both), True))
    return pl.pallas_call(
        finish_kernel,
        out_shape=shape((rows, tokens, channels), BF16),
        in_specs=[whole] * 5,
        out_specs=hbm,
        scratch_shapes=[unit_scratch, pltpu.VMEM((rows, tokens, channels), BF16), pltpu.SemaphoreType.DMA((rows,))],
        compiler_params=params,
        name="finish",
    )(merged, middle_t, gate_t, columns, outw_t)


def solution(mesh):
    rows = ("groups", "row")
    return jax.shard_map(
        on_device,
        mesh=mesh,
        in_specs=(P(rows, None, None), P(rows, None), P(), P(), P(), P(), P()),
        out_specs=P(rows, None, None),
        check_vma=False,
    )
```

time: 75.7 us -> 72.5 us (0.958)
  blocking collectives: 38.9 us -> 66.8 us
  waiting for transfers between devices: 19.4 us -> 0 us
  starting transfers between devices: 8.2 us -> 0 us
  Pallas kernels: 8.77 us -> 5.37 us
    all_to_all x2 -> x4, blocking collectives: 38.9 us -> 66.8 us  [exchange(): return lax.all_to_all(array, 'row', split_axis=0, concat_axis=0, tiled=True)]
    all_to_all x2 -> x0, waiting for transfers between devices: 19.4 us -> none  [exchange(): return lax.all_to_all(array, 'row', split_axis=0, concat_axis=0, tiled=True)]
    all_to_all x2 -> x0, starting transfers between devices: 8.2 us -> none  [exchange(): return lax.all_to_all(array, 'row', split_axis=0, concat_axis=0, tiled=True)]
    pallas_call x2, Pallas kernels: 1.97 us -> 0.55 us  [mix(): pl.pallas_call(functools.partial(mix_kernel, per_group, rows, incoming),...]
  transfers between devices with their start and end apart: 2 -> 0, of which waited for: 2 -> 0; matrix products, arithmetic and copies ran while one was open for 0% -> 0% of each run, Pallas kernels for 1% -> 0%
where the time goes in v7:
time: 72.5 us; the launch traced here: 72.2 us
  blocking collectives  66.8 us (92%)
  Pallas kernels  5.37 us (7%)
    all_to_all x4, blocking collectives, exchange(): return lax.all_to_all(array, 'row', split_axis=0, concat_axis=0, tiled=True)  66.8 us
    pallas_call x1, Pallas kernels, on_device(): pl.pallas_call(functools.partial(project_kernel, per_group), out_shape=(b...  1.98 us
    pallas_call x1, Pallas kernels, on_device(): pl.pallas_call(functools.partial(step_kernel, per_group), out_shape=(both...  1.5 us

profile of v7, /device:TPU:0, one launch (start us, length us, event | category | flops | bytes accessed | tf_op | source)
XLA Modules:
  0.0 72.2 jit_solution(1557936990387152331)
XLA Ops:
  0.0 2.0 %project.1 = (bf16[2048,128]{1,0:T(8,128)(2,1)S(1)}, bf16[128,1024]{1,0:T(8,128)(2,1)S(1)}, bf16[128,1024]{1,0:T(8,128)(2,1)S(1)}, s32[8,128]{1,0:T(8,128)S(1)},...) custom-call(bf16[8,128,128]{2,1,0:T(8,128)(2,1)} %refs_0_.1, ...), custom_call_target="tpu_custom_call" | custom-call | tf_op jit(solution)/shard_map/project/pallas_call | solution.py:207
  2.0 21.7 %all_to_all.34.both_ref = bf16[16,128,128]{2,1,0:T(8,128)(2,1)S(1)} all-to-all(bf16[16,128,128]{2,1,0:T(8,128)(2,1)S(1)} %bitcast.7), channel_id=1, replica_groups=mesh['groups'=2,'row'=16] {'row'}, dimensions={0} | all-to-all | bytes 1048576 | tf_op jit(solution)/shard_map/all_to_all | solution.py:194
  23.6 0.3 mix.2
  23.9 13.9 %all_to_all.35 = bf16[16,64,128]{2,1,0:T(8,128)(2,1)S(1)} all-to-all(bf16[16,64,128]{2,1,0:T(8,128)(2,1)S(1)} %mix.2), channel_id=1, replica_groups=mesh['groups'=2,'row'=16] {'row'}, dimensions={0} | all-to-all | bytes 524288 | tf_op jit(solution)/shard_map/all_to_all | solution.py:194
  37.9 1.5 %finish_project.1 = (bf16[2048,128]{1,0:T(8,128)(2,1)S(1)}, bf16[128,1024]{1,0:T(8,128)(2,1)S(1)}, bf16[128,1024]{1,0:T(8,128)(2,1)S(1)}) custom-call(bf16[1024,128]{1,0:T(8,128)(2,1)S(1)} %bitcast.4, bf16[128,1024]{1,0:T(8,128)(2,1)S(1)} %get-tuple-element.16.pair_t_ref, bf16[128,1024]{1,0:T(8,128)(2,1)S(1)} %get-tuple-element.17.gate_t_ref, ...), custom_call_target="tpu_custom_call" | custom-call | tf_op jit(solution)/shard_map/finish_project/pallas_call | solution.py:226
  39.4 17.2 %all_to_all.36.both_ref = bf16[16,128,128]{2,1,0:T(8,128)(2,1)S(1)} all-to-all(bf16[16,128,128]{2,1,0:T(8,128)(2,1)S(1)} %bitcast.6), channel_id=1, replica_groups=mesh['groups'=2,'row'=16] {'row'}, dimensions={0} | all-to-all | bytes 1048576 | tf_op jit(solution)/shard_map/all_to_all | solution.py:194
  56.6 0.3 mix.3
  56.9 13.9 %all_to_all.37 = bf16[16,64,128]{2,1,0:T(8,128)(2,1)S(1)} all-to-all(bf16[16,64,128]{2,1,0:T(8,128)(2,1)S(1)} %mix.3), channel_id=1, replica_groups=mesh['groups'=2,'row'=16] {'row'}, dimensions={0} | all-to-all | bytes 524288 | tf_op jit(solution)/shard_map/all_to_all | solution.py:194
  70.8 1.3 %finish.1 = bf16[8,128,128]{2,1,0:T(8,128)(2,1)} custom-call(bf16[1024,128]{1,0:T(8,128)(2,1)S(1)} %bitcast.5, bf16[128,1024]{1,0:T(8,128)(2,1)S(1)} %get-tuple-element.23.middle_t_ref, bf16[128,1024]{1,0:T(8,128)(2,1)S(1)} %get-tuple-element.24.gate_t_ref, f32[6,128,128]{2,1,0:T(8,128)S(1)} %get-tuple-element.19.columns_ref, ...), custom_call_target="tpu_custom_call" | custom-call | tf_op jit(solution)/shard_map/finish/pallas_call | solution.py:236

commit v8 on v7

v8 whole, which is shorter than its diff:
```python
import functools

import jax
import jax.numpy as jnp
from jax import lax
from jax.experimental import pallas as pl
from jax.experimental.pallas import tpu as pltpu
from jax.sharding import PartitionSpec as P

F32 = jnp.float32
BF16 = jnp.bfloat16
LANES = 128
NT = (((1,), (1,)), ((), ()))
NN = (((1,), (0,)), ((), ()))
TN = (((0,), (0,)), ((), ()))


def dot(a, b, dims):
    return lax.dot_general(a, b, dims, preferred_element_type=F32)


def sigmoid(values):
    return 0.5 * jnp.tanh(0.5 * values) + 0.5


def unit(values, axis):
    scale = 1.0 / values.shape[axis]
    centred = values - jnp.sum(values, axis=axis, keepdims=True) * scale
    spread = jnp.sum(centred * centred, axis=axis, keepdims=True) * scale
    return centred * lax.rsqrt(spread + 1e-05)


def chunks(rows, tokens):
    wide = max(1, min(rows, 256 // tokens))
    return [list(range(start, min(start + wide, rows))) for start in range(0, rows, wide)]


def span(chunk, tokens):
    return slice(chunk[0] * tokens, (chunk[-1] + 1) * tokens)


def lanes(parts):
    return parts[0] if len(parts) == 1 else jnp.concatenate(parts, axis=1)


def affine(values, gain, bias, tokens):
    parts = [values[:, n : n + tokens] * gain + bias for n in range(0, values.shape[1], tokens)]
    return lanes(parts).astype(BF16)


def store_panels(panels, per_group, rows, chunk, tokens, products, mask):
    channels = products.shape[0] // 5
    for side in range(2):
        base = 2 * side * channels
        gated = sigmoid(products[base : base + channels]) * products[base + channels : base + 2 * channels] * mask
        for h, r in enumerate(chunk):
            for g in range(channels // per_group):
                where = pl.ds((2 * g + side) * per_group * rows + r, per_group, stride=rows)
                for t in range(tokens // LANES):
                    first = h * tokens + t * LANES
                    panels[t, where, :] = gated[g * per_group : (g + 1) * per_group, first : first + LANES]
    return sigmoid(products[4 * channels :]).astype(BF16)


def mask_lanes(mask_ref, chunk):
    return lanes([mask_ref[r : r + 1].astype(F32) for r in chunk])


def column(ref, which, norm, tokens):
    row = ref[which, norm : norm + 1]
    return jnp.broadcast_to(row, (tokens, row.shape[1])).T


def fetch(copies):
    for copy in copies:
        copy.start()
    for copy in copies:
        copy.wait()


def weights_kernel(
    gain_hbm, bias_hbm, proj_hbm, gatew_hbm, outw_hbm, columns_ref, proj_t_ref, outw_t_ref,
    gain_ref, bias_ref, proj_ref, gatew_ref, outw_ref, sems,
):
    pairs = (
        (gain_hbm, gain_ref), (bias_hbm, bias_ref), (proj_hbm, proj_ref), (gatew_hbm, gatew_ref), (outw_hbm, outw_ref)
    )
    fetch([pltpu.make_async_copy(src, dst, sems.at[n]) for n, (src, dst) in enumerate(pairs)])
    tokens = columns_ref.shape[2]
    channels = outw_ref.shape[1]
    for which in range(2):
        proj_t_ref[which, : 4 * channels] = proj_ref[which].T
        proj_t_ref[which, 4 * channels :] = gatew_ref[which].T
        outw_t_ref[which] = outw_ref[which].T
        for norm in range(2):
            columns_ref[4 * which + 2 * norm] = column(gain_ref, which, norm, tokens)
            columns_ref[4 * which + 2 * norm + 1] = column(bias_ref, which, norm, tokens)


def project_kernel(per_group, rows, pair_rows, mask_rows, refs):
    columns_ref, proj_t_ref, both_ref, pair_t_ref, gate_t_ref, mask_ref, panels = refs
    tokens = mask_ref.shape[1]
    for r in range(rows):
        mask_ref[r : r + 1] = mask_rows(r)
    for chunk in chunks(rows, tokens):
        part = span(chunk, tokens)
        pair_t = lanes([pair_rows(r).T for r in chunk])
        pair_t_ref[:, part] = pair_t
        normed = affine(unit(pair_t.astype(F32), 0), columns_ref[0], columns_ref[1], tokens)
        products = dot(proj_t_ref[0], normed, NN)
        gate_t_ref[:, part] = store_panels(
            panels, per_group, rows, chunk, tokens, products, mask_lanes(mask_ref, chunk)
        )
    for t in range(tokens // LANES):
        both_ref[:, t * LANES : (t + 1) * LANES] = panels[t].astype(BF16)


def project_own(per_group, pair_hbm, mask_hbm, *refs):
    refs, (pair_ref, mask_ref, sems) = refs[:-3], refs[-3:]
    pairs = ((pair_hbm, pair_ref), (mask_hbm, mask_ref))
    fetch([pltpu.make_async_copy(src, dst, sems.at[n]) for n, (src, dst) in enumerate(pairs)])
    project_kernel(
        per_group, pair_ref.shape[0], lambda r: pair_ref[r], lambda r: mask_ref[r : r + 1].astype(F32), refs
    )


def project_moved(per_group, stay_ref, kept_ref, first_ref, second_ref, *refs):
    half, tokens = kept_ref.shape[0], kept_ref.shape[1] - 1
    stay = jnp.full((tokens, kept_ref.shape[2]), stay_ref[0]) != 0

    def pair_rows(r):
        if r >= half:
            return second_ref[r - half, :tokens]
        return jnp.where(stay, kept_ref[r, :tokens].astype(F32), first_ref[r, :tokens].astype(F32)).astype(BF16)

    def mask_rows(r):
        if r >= half:
            return second_ref[r - half, tokens:].astype(F32)
        return jnp.where(stay[:1], kept_ref[r, tokens:].astype(F32), first_ref[r, tokens:].astype(F32))

    project_kernel(per_group, 2 * half, pair_rows, mask_rows, refs)


def regroup(blocks):
    count, rows, _ = blocks.shape
    swapped = jnp.concatenate([blocks[count // 2 :], blocks[: count // 2]], axis=0)
    return jnp.where(lax.broadcasted_iota(jnp.int32, blocks.shape, 1) < rows // 2, blocks, swapped)


def mix_kernel(per_group, rows, incoming, moved, both_ref, product_ref):
    groups, _, tokens = both_ref.shape
    step = 2 * rows

    def matrices(side, pair):
        start = (side * per_group + 2 * pair) * rows
        block = both_ref[:, start : start + step, :].astype(F32)
        blocks = [block[:, h * rows : (h + 1) * rows] for h in range(2)]
        if moved and side == 1 and not incoming:
            blocks = [regroup(b) for b in blocks]
        return [b.reshape(groups * rows, tokens).astype(BF16) for b in blocks]

    for pair in range(per_group // 2):
        lefts, rights = matrices(0, pair), matrices(1, pair)
        sums = [
            dot(left, right, TN if incoming else NT).reshape(groups, rows, tokens)
            for left, right in zip(lefts, rights)
        ]
        if moved and incoming:
            sums = [regroup(b) for b in sums]
        product_ref[:, pair * step : (pair + 1) * step, :] = jnp.concatenate(sums, axis=1).astype(BF16)


def finish_rows(emit, rows, merged_ref, pair_t_ref, gate_t_ref, gain, bias, outw_t, unit_scratch):
    tokens = merged_ref.shape[1]
    channels = merged_ref.shape[0] // rows
    sums = merged_ref[...].astype(F32).reshape(channels, rows, tokens)
    units = unit(sums, 0).reshape(channels * rows, tokens)
    tiles = range(tokens // LANES)
    for t in tiles:
        unit_scratch[t] = units[:, t * LANES : (t + 1) * LANES]
    for chunk in chunks(rows, tokens):
        part = span(chunk, tokens)
        units = lanes([unit_scratch[t, pl.ds(r, channels, stride=rows), :] for r in chunk for t in tiles])
        normed = affine(units, gain, bias, tokens)
        change = gate_t_ref[:, part].astype(F32) * dot(outw_t, normed, NN)
        emit(chunk, part, (pair_t_ref[:, part].astype(F32) + change).astype(BF16))


def step_kernel(
    per_group, merged_ref, pair_t_ref, gate_t_ref, mask_ref, columns_ref, outw_t_ref, proj_t_ref,
    both_ref, middle_t_ref, gate1_t_ref, unit_scratch, panels,
):
    rows, tokens = mask_ref.shape

    def emit(chunk, part, middle):
        middle_t_ref[:, part] = middle
        normed = affine(unit(middle.astype(F32), 0), columns_ref[4], columns_ref[5], tokens)
        products = dot(proj_t_ref[1], normed, NN)
        gate1_t_ref[:, part] = store_panels(
            panels, per_group, rows, chunk, tokens, products, mask_lanes(mask_ref, chunk)
        )

    finish_rows(
        emit, rows, merged_ref, pair_t_ref, gate_t_ref, columns_ref[2], columns_ref[3], outw_t_ref[0], unit_scratch
    )
    for t in range(tokens // LANES):
        both_ref[:, t * LANES : (t + 1) * LANES] = panels[t].astype(BF16)


def finish_kernel(
    rows, merged_ref, middle_t_ref, gate_t_ref, columns_ref, outw_t_ref, result_ref, unit_scratch, done, sems
):
    tokens = merged_ref.shape[1]
    copies = []

    def emit(chunk, part, result):
        for h, r in enumerate(chunk):
            done[r] = result[:, h * tokens : (h + 1) * tokens].T
            copies.append(pltpu.make_async_copy(done.at[r], result_ref.at[r], sems.at[r]))
            copies[-1].start()

    finish_rows(
        emit, rows, merged_ref, middle_t_ref, gate_t_ref, columns_ref[6], columns_ref[7], outw_t_ref[1], unit_scratch
    )
    for copy in copies:
        copy.wait()


def finish_moved(
    rows, merged_ref, middle_t_ref, gate_t_ref, columns_ref, outw_t_ref, first_ref, second_ref, unit_scratch
):
    tokens = merged_ref.shape[1]

    def emit(chunk, part, result):
        for h, r in enumerate(chunk):
            half, place = ((first_ref, r), (second_ref, r - rows // 2))[r >= rows // 2]
            half[place] = result[:, h * tokens : (h + 1) * tokens].T

    finish_rows(
        emit, rows, merged_ref, middle_t_ref, gate_t_ref, columns_ref[6], columns_ref[7], outw_t_ref[1], unit_scratch
    )


def cube_moves(count):
    half = count // 2
    seconds, firsts = [], []
    for group in range(2):
        for d in range(count):
            here = group * count + d
            stays = (d >= half) == (group == 1)
            near = (1 - group) * count + d
            along = group * count + (d + half) % count
            seconds.append((here, near if stays else along))
            if not stays:
                firsts.append((here, (1 - group) * count + (d + half) % count))
    cubes = [list(range(c * half, (c + 1) * half)) + list(range(count + c * half, count + (c + 1) * half)) for c in range(2)]
    return firsts, seconds, cubes


def on_device(pair, mask, gains, biases, proj, gatew, outw):
    axes = ("groups", "row")
    groups = lax.axis_size("row")
    rows, tokens, channels = pair.shape
    per_group = channels // groups
    whole = pl.BlockSpec(memory_space=pltpu.VMEM)
    hbm = pl.BlockSpec(memory_space=pltpu.HBM)
    params = pltpu.CompilerParams(vmem_limit_bytes=48 * 1024 * 1024)
    shape = jax.ShapeDtypeStruct
    both_shape = shape((2 * channels * rows, tokens), BF16)
    flat_shape = shape((channels, rows * tokens), BF16)
    panels = pltpu.VMEM((tokens // LANES, 2 * channels * rows, LANES), F32)
    unit_scratch = pltpu.VMEM((tokens // LANES, channels * rows, LANES), F32)
    moved = lax.axis_size("groups") == 2 and groups == 16 and rows == 8
    firsts, seconds, cubes = cube_moves(groups)

    def kernel(body, out_shape, operands, name, in_specs=None, out_specs=whole, scratch=(), cost=None):
        return pl.pallas_call(
            body,
            out_shape=out_shape,
            in_specs=in_specs or [whole] * len(operands),
            out_specs=jax.tree.map(lambda _: out_specs, out_shape),
            scratch_shapes=scratch,
            compiler_params=params,
            cost_estimate=cost,
            name=name,
        )(*operands)

    def from_hbm(arrays):
        return [pltpu.with_memory_space_constraint(a, pltpu.HBM) for a in arrays]

    def held(arrays):
        return [pltpu.VMEM(a.shape, a.dtype) for a in arrays] + [pltpu.SemaphoreType.DMA((len(arrays),))]

    def exchange(array):
        if moved:
            return lax.all_to_all(array, axes, split_axis=0, concat_axis=0, tiled=True, axis_index_groups=cubes)
        return lax.all_to_all(array, "row", split_axis=0, concat_axis=0, tiled=True)

    def mix(both, incoming):
        product = kernel(
            functools.partial(mix_kernel, per_group, rows, incoming, moved),
            shape((groups, per_group * rows, tokens), BF16),
            [both.reshape(groups, 2 * per_group * rows, tokens)],
            "mix",
        )
        return product.reshape(channels * rows, tokens)

    params_in = (gains, biases, proj, gatew, outw)
    columns, proj_t, outw_t = kernel(
        weights_kernel,
        (shape((8, channels, tokens), F32), shape((2, 5 * channels, channels), BF16), shape((2, channels, channels), BF16)),
        from_hbm(params_in),
        "weights",
        in_specs=[hbm] * 5,
        scratch=held(params_in),
        cost=pl.CostEstimate(flops=10**9, bytes_accessed=4 * 2**20, transcendentals=0),
    )
    project_out = (both_shape, flat_shape, flat_shape, shape((rows, tokens), F32))
    if moved:
        half = rows // 2
        with_mask = jnp.concatenate([pair, mask.astype(BF16)[:, :, None].swapaxes(1, 2)], axis=1)
        kept = with_mask[:half]
        second = lax.ppermute(with_mask[half:], axes, seconds)
        first = lax.ppermute(kept, axes, firsts)
        stays = (lax.axis_index("row") >= groups // 2) == (lax.axis_index("groups") == 1)
        both, pair_t, gate_t, mask_rows = kernel(
            functools.partial(project_moved, per_group),
            project_out,
            [stays.astype(jnp.int32).reshape(1), kept, first, second, columns, proj_t],
            "project",
            in_specs=[pl.BlockSpec(memory_space=pltpu.SMEM)] + [whole] * 5,
            scratch=[panels],
        )
    else:
        both, pair_t, gate_t, mask_rows = kernel(
            functools.partial(project_own, per_group),
            project_out,
            from_hbm((pair, mask)) + [columns, proj_t],
            "project",
            in_specs=[hbm] * 2 + [whole] * 2,
            scratch=[panels] + held((pair, mask)),
        )
    merged = exchange(mix(exchange(both), False))
    both, middle_t, gate_t = kernel(
        functools.partial(step_kernel, per_group),
        (both_shape, flat_shape, flat_shape),
        [merged, pair_t, gate_t, mask_rows, columns, outw_t, proj_t],
        "finish_project",
        scratch=[unit_scratch, panels],
    )
    merged = exchange(mix(exchange(both), True))
    operands = [merged, middle_t, gate_t, columns, outw_t]
    if not moved:
        return kernel(
            functools.partial(finish_kernel, rows),
            shape(pair.shape, BF16),
            operands,
            "finish",
            out_specs=hbm,
            scratch=[unit_scratch, pltpu.VMEM(pair.shape, BF16), pltpu.SemaphoreType.DMA((rows,))],
        )
    half_shape = shape((half, tokens, channels), BF16)
    first, second = kernel(
        functools.partial(finish_moved, rows), (half_shape, half_shape), operands, "finish", scratch=[unit_scratch]
    )
    second = lax.ppermute(second, axes, [(b, a) for a, b in seconds])
    back = lax.ppermute(first, axes, [(b, a) for a, b in firsts])
    return jnp.concatenate([jnp.where(stays, first, back), second], axis=0)


def solution(mesh):
    rows = ("groups", "row")
    return jax.shard_map(
        on_device,
        mesh=mesh,
        in_specs=(P(rows, None, None), P(rows, None), P(), P(), P(), P(), P()),
        out_specs=P(rows, None, None),
        check_vma=False,
    )
```

time: 72.5 us -> 83.2 us (1.15)
  the two profiles are of different devices: /device:TPU:0 before, /device:TPU:2 now
where the time goes in v8:
time: 83.2 us; the launch traced here: 82.9 us
  blocking collectives  47.2 us (57%)
  waiting for transfers between devices  17.4 us (21%)
  starting transfers between devices  10.9 us (13%)
  Pallas kernels  4.83 us (6%)
  other arithmetic  1.43 us (2%)
  local copies, waits for them, and re-layouts  1 us (1%)
    all_to_all x4, blocking collectives, exchange(): lax.all_to_all(array, axes, split_axis=0, concat_axis=0, tiled=True, axis...  47.2 us
    ppermute x1, waiting for transfers between devices, on_device(): first = lax.ppermute(kept, axes, firsts)  8.46 us
    ppermute x1, starting transfers between devices, on_device(): back = lax.ppermute(first, axes, [(b, a) for a, b in firsts])  6.25 us
    ppermute x1, waiting for transfers between devices, on_device(): back = lax.ppermute(first, axes, [(b, a) for a, b in firsts])  5.73 us
    pallas_call x6, Pallas kernels, kernel(): pl.pallas_call(body, out_shape=out_shape, in_specs=in_specs or [whole] *...  4.83 us
    ppermute x1, starting transfers between devices, on_device(): second = lax.ppermute(with_mask[half:], axes, seconds)  2.64 us
    ppermute x1, waiting for transfers between devices, on_device(): second = lax.ppermute(second, axes, [(b, a) for a, b in seconds])  2.41 us
    ppermute x1, starting transfers between devices, on_device(): first = lax.ppermute(kept, axes, firsts)  1.91 us
  transfers between devices with their start and end apart: 4, of which 4 were waited for; matrix products, arithmetic and copies ran while one was open for 0% of the time, Pallas kernels for 2%

profile of v8, /device:TPU:2, one launch (start us, length us, event | category | flops | bytes accessed | tf_op | source)
XLA Modules:
  0.0 82.9 jit_solution(835826987510420291)
XLA Ops:
  0.0 0.7 convert_bitcast_fusion
  0.7 1.0 %constant_dynamic-update-slice_fusion.1 = bf16[8,129,128]{2,1,0:T(8,128)(2,1)S(1)} fusion(bf16[8,128,128]{2,1,0:T(8,128)(2,1)} %param.7), kind=kLoop, calls=%fused_computation.3 | loop fusion | bytes 524288
  1.7 2.6 %collective-permute-start.1 = (bf16[4,129,128]{2,1,0:T(8,128)(2,1)S(1)}, bf16[4,129,128]{2,1,0:T(8,128)(2,1)S(1)}, u32[]{:S(2)}, u32[]{:S(2)}) collective-permute-start(bf16[4,129,128]{2,1,0:T(8,128)(2,1)S(1)} %get-tuple-element.29), channel_id=1, source_target_pairs={{0,16},{1,17},{2,18},{3,19},{4,20},{5,21},{6,22},{7,23},{8,0},{9,1... | collective-permute-start | bytes 396296 | tf_op jit(solution)/shard_map/ppermute | solution.py:323
  4.3 1.9 %collective-permute-start = (bf16[4,129,128]{2,1,0:T(8,128)(2,1)S(1)}, bf16[4,129,128]{2,1,0:T(8,128)(2,1)S(1)}, u32[]{:S(2)}, u32[]{:S(2)}) collective-permute-start(bf16[4,129,128]{2,1,0:T(8,128)(2,1)S(1)} %get-tuple-element.30.kept_ref), channel_id=1, source_target_pairs={{8,16},{9,17},{10,18},{11,19},{12,20},{13,21},{14,22},{15,23},{16,... | collective-permute-start | bytes 396296 | tf_op jit(solution)/shard_map/ppermute | solution.py:324
  6.3 1.4 %weights.1 = (f32[8,128,128]{2,1,0:T(8,128)S(1)}, bf16[2,640,128]{2,1,0:T(8,128)(2,1)S(1)}, bf16[2,128,128]{2,1,0:T(8,128)(2,1)S(1)}) custom-call(f32[2,2,128]{2,1,0:T(2,128)} %gain_hbm.1, f32[2,2,128]{2,1,0:T(2,128)} %bias_hbm.1, bf16[2,128,512]{2,1,0:T(8,128)(2,1)} %proj_hbm.1, bf16[2,128,128]{2,1,0:T(8,128)(2,1)} %gatew_hbm.1, bf16[2,128,128]{2,1,0:T(8,128)(2,1)} %outw_hbm.1), custom_call_target="tpu_custom_call" | custom-call | flops 1000000000 | bytes 4194304 | tf_op jit(solution)/shard_map/weights/pallas_call | solution.py:277
  7.6 0.8 %collective-permute-done.1.second_ref = bf16[4,129,128]{2,1,0:T(8,128)(2,1)S(1)} collective-permute-done((bf16[4,129,128]{2,1,0:T(8,128)(2,1)S(1)}, bf16[4,129,128]{2,1,0:T(8,128)(2,1)S(1)}, u32[]{:S(2)}, u32[]{:S(2)}) %collective-permute-start.1) | collective-permute-done | bytes 132128 | tf_op jit(solution)/shard_map/ppermute | solution.py:323
  8.5 8.5 %collective-permute-done.first_ref = bf16[4,129,128]{2,1,0:T(8,128)(2,1)S(1)} collective-permute-done((bf16[4,129,128]{2,1,0:T(8,128)(2,1)S(1)}, bf16[4,129,128]{2,1,0:T(8,128)(2,1)S(1)}, u32[]{:S(2)}, u32[]{:S(2)}) %collective-permute-start) | collective-permute-done | bytes 132128 | tf_op jit(solution)/shard_map/ppermute | solution.py:324
  16.9 0.8 project.1
  17.8 13.4 %all_to_all.34.both_ref = bf16[16,128,128]{2,1,0:T(8,128)(2,1)S(1)} all-to-all(bf16[16,128,128]{2,1,0:T(8,128)(2,1)S(1)} %bitcast.9), channel_id=1, replica_groups={{0,1,2,3,4,5,6,7,16,17,18,19,20,21,22,23},{8,9,10,11,12,13,14,15,24,25,..., dimensions={0} | all-to-all | bytes 1048576 | tf_op jit(solution)/shard_map/all_to_all | solution.py:296
  31.2 0.3 mix.2
  31.5 10.3 %all_to_all.35 = bf16[16,64,128]{2,1,0:T(8,128)(2,1)S(1)} all-to-all(bf16[16,64,128]{2,1,0:T(8,128)(2,1)S(1)} %mix.2), channel_id=1, replica_groups={{0,1,2,3,4,5,6,7,16,17,18,19,20,21,22,23},{8,9,10,11,12,13,14,15,24,25,..., dimensions={0} | all-to-all | bytes 524288 | tf_op jit(solution)/shard_map/all_to_all | solution.py:296
  41.8 1.5 %finish_project.1 = (bf16[2048,128]{1,0:T(8,128)(2,1)S(1)}, bf16[128,1024]{1,0:T(8,128)(2,1)S(1)}, bf16[128,1024]{1,0:T(8,128)(2,1)S(1)}) custom-call(bf16[1024,128]{1,0:T(8,128)(2,1)S(1)} %bitcast.7, bf16[128,1024]{1,0:T(8,128)(2,1)S(1)} %get-tuple-element.20.pair_t_ref, bf16[128,1024]{1,0:T(8,128)(2,1)S(1)} %get-tuple-element.21.gate_t_ref, ...), custom_call_target="tpu_custom_call" | custom-call | tf_op jit(solution)/shard_map/finish_project/pallas_call | solution.py:277
  43.3 13.2 %all_to_all.36.both_ref = bf16[16,128,128]{2,1,0:T(8,128)(2,1)S(1)} all-to-all(bf16[16,128,128]{2,1,0:T(8,128)(2,1)S(1)} %bitcast.10), channel_id=1, replica_groups={{0,1,2,3,4,5,6,7,16,17,18,19,20,21,22,23},{8,9,10,11,12,13,14,15,24,25,..., dimensions={0} | all-to-all | bytes 1048576 | tf_op jit(solution)/shard_map/all_to_all | solution.py:296
  56.4 0.3 mix.3
  56.7 10.3 %all_to_all.37 = bf16[16,64,128]{2,1,0:T(8,128)(2,1)S(1)} all-to-all(bf16[16,64,128]{2,1,0:T(8,128)(2,1)S(1)} %mix.3), channel_id=1, replica_groups={{0,1,2,3,4,5,6,7,16,17,18,19,20,21,22,23},{8,9,10,11,12,13,14,15,24,25,..., dimensions={0} | all-to-all | bytes 524288 | tf_op jit(solution)/shard_map/all_to_all | solution.py:296
  67.0 0.6 finish.1
  67.7 6.2 %collective-permute-start.2 = (bf16[4,128,128]{2,1,0:T(8,128)(2,1)S(1)}, bf16[4,128,128]{2,1,0:T(8,128)(2,1)S(1)}, u32[]{:S(2)}, u32[]{:S(2)}) collective-permute-start(bf16[4,128,128]{2,1,0:T(8,128)(2,1)S(1)} %get-tuple-element.27), channel_id=1, source_target_pairs={{16,8},{17,9},{18,10},{19,11},{20,12},{21,13},{22,14},{23,15},{8,1... | collective-permute-start | bytes 393224 | tf_op jit(solution)/shard_map/ppermute | solution.py:367
  73.9 0.1 collective-permute-start.3
  74.0 5.7 %collective-permute-done.2 = bf16[4,128,128]{2,1,0:T(8,128)(2,1)S(1)} collective-permute-done((bf16[4,128,128]{2,1,0:T(8,128)(2,1)S(1)}, bf16[4,128,128]{2,1,0:T(8,128)(2,1)S(1)}, u32[]{:S(2)}, u32[]{:S(2)}) %collective-permute-start.2) | collective-permute-done | bytes 131104 | tf_op jit(solution)/shard_map/ppermute | solution.py:367
  79.7 2.4 %collective-permute-done.3 = bf16[4,128,128]{2,1,0:T(8,128)(2,1)S(1)} collective-permute-done((bf16[4,128,128]{2,1,0:T(8,128)(2,1)S(1)}, bf16[4,128,128]{2,1,0:T(8,128)(2,1)S(1)}, u32[]{:S(2)}, u32[]{:S(2)}) %collective-permute-start.3) | collective-permute-done | bytes 131104 | tf_op jit(solution)/shard_map/ppermute | solution.py:366
  82.2 0.7 pad_maximum_fusion
  (3 shorter events, 0.0 us)
Async XLA Ops:
  1.7 6.8 %collective-permute-start.1 = (bf16[4,129,128]{2,1,0:T(8,128)(2,1)S(1)}, bf16[4,129,128]{2,1,0:T(8,128)(2,1)S(1)}, u32[]{:S(2)}, u32[]{:S(2)}) collective-permute-start(bf16[4,129,128]{2,1,0:T(8,128)(2,1)S(1)} %get-tuple-element.29), channel_id=1, source_target_pairs={{0,16},{1,17},{2,18},{3,19},{4,20},{5,21},{6,22},{7,23},{8,0},{9,1... | collective-permute-start | bytes 396296 | tf_op jit(solution)/shard_map/ppermute | solution.py:323
  4.3 12.6 %collective-permute-start = (bf16[4,129,128]{2,1,0:T(8,128)(2,1)S(1)}, bf16[4,129,128]{2,1,0:T(8,128)(2,1)S(1)}, u32[]{:S(2)}, u32[]{:S(2)}) collective-permute-start(bf16[4,129,128]{2,1,0:T(8,128)(2,1)S(1)} %get-tuple-element.30.kept_ref), channel_id=1, source_target_pairs={{8,16},{9,17},{10,18},{11,19},{12,20},{13,21},{14,22},{15,23},{16,... | collective-permute-start | bytes 396296 | tf_op jit(solution)/shard_map/ppermute | solution.py:324
  67.7 12.1 %collective-permute-start.2 = (bf16[4,128,128]{2,1,0:T(8,128)(2,1)S(1)}, bf16[4,128,128]{2,1,0:T(8,128)(2,1)S(1)}, u32[]{:S(2)}, u32[]{:S(2)}) collective-permute-start(bf16[4,128,128]{2,1,0:T(8,128)(2,1)S(1)} %get-tuple-element.27), channel_id=1, source_target_pairs={{16,8},{17,9},{18,10},{19,11},{20,12},{21,13},{22,14},{23,15},{8,1... | collective-permute-start | bytes 393224 | tf_op jit(solution)/shard_map/ppermute | solution.py:367
  73.9 8.2 %collective-permute-start.3 = (bf16[4,128,128]{2,1,0:T(8,128)(2,1)S(1)}, bf16[4,128,128]{2,1,0:T(8,128)(2,1)S(1)}, u32[]{:S(2)}, u32[]{:S(2)}) collective-permute-start(bf16[4,128,128]{2,1,0:T(8,128)(2,1)S(1)} %get-tuple-element.28), channel_id=1, source_target_pairs={{16,0},{17,1},{18,2},{19,3},{20,4},{21,5},{22,6},{23,7},{0,8},{1,9... | collective-permute-start | bytes 393224 | tf_op jit(solution)/shard_map/ppermute | solution.py:366

commit v9 on v7

--- a/solution.py
+++ b/solution.py
@@ -103,13 +103,26 @@
         both_ref[:, t * LANES : (t + 1) * LANES] = panels[t].astype(BF16)
 
 
+def rank_order(count):
+    parts = 4 if count % 4 == 0 else 1
+    return [(rank % parts) * (count // parts) + rank // parts for rank in range(count)]
+
+
+def take(blocks, places):
+    return jnp.concatenate([blocks[n : n + 1] for n in places], axis=0)
+
+
 def mix_kernel(per_group, rows, incoming, both_ref, product_ref):
     groups, _, tokens = both_ref.shape
     step = 2 * rows
+    order = rank_order(groups)
+    ranks = [order.index(device) for device in range(groups)]
 
     def matrices(side, pair):
         start = (side * per_group + 2 * pair) * rows
         block = both_ref[:, start : start + step, :].astype(F32)
+        if side == 1 and not incoming:
+            block = take(block, ranks)
         return [block[:, h * rows : (h + 1) * rows].reshape(groups * rows, tokens).astype(BF16) for h in range(2)]
 
     for pair in range(per_group // 2):
@@ -118,7 +131,10 @@
             dot(left, right, TN if incoming else NT).reshape(groups, rows, tokens)
             for left, right in zip(lefts, rights)
         ]
-        product_ref[:, pair * step : (pair + 1) * step, :] = jnp.concatenate(sums, axis=1).astype(BF16)
+        sums = jnp.concatenate(sums, axis=1)
+        if incoming:
+            sums = take(sums, order)
+        product_ref[:, pair * step : (pair + 1) * step, :] = sums.astype(BF16)
 
 
 def finish_rows(emit, rows, merged_ref, pair_t_ref, gate_t_ref, gain, bias, outw_t, unit_scratch):
@@ -191,7 +207,9 @@
     unit_scratch = pltpu.VMEM((tokens // LANES, channels * rows, LANES), F32)
 
     def exchange(array):
-        return lax.all_to_all(array, "row", split_axis=0, concat_axis=0, tiled=True)
+        return lax.all_to_all(
+            array, "row", split_axis=0, concat_axis=0, tiled=True, axis_index_groups=[rank_order(groups)]
+        )
 
     def mix(both, incoming):
         product = pl.pallas_call(

time: 72.5 us -> 73.9 us (1.019)
  blocking collectives: 66.8 us -> 68.2 us
    all_to_all x4, blocking collectives: 66.8 us -> 68.2 us  [exchange(): lax.all_to_all(array, 'row', split_axis=0, concat_axis=0, tiled=True, axi...]
where the time goes in v9:
time: 73.9 us; the launch traced here: 73.6 us
  blocking collectives  68.2 us (92%)
  Pallas kernels  5.37 us (7%)
    all_to_all x4, blocking collectives, exchange(): lax.all_to_all(array, 'row', split_axis=0, concat_axis=0, tiled=True, axi...  68.2 us
    pallas_call x1, Pallas kernels, on_device(): pl.pallas_call(functools.partial(project_kernel, per_group), out_shape=(b...  1.98 us
    pallas_call x1, Pallas kernels, on_device(): pl.pallas_call(functools.partial(step_kernel, per_group), out_shape=(both...  1.49 us

profile of v9, /device:TPU:0, one launch (start us, length us, event | category | flops | bytes accessed | tf_op | source)
XLA Modules:
  0.0 73.6 jit_solution(14718780258843540763)
XLA Ops:
  0.0 2.0 %project.1 = (bf16[2048,128]{1,0:T(8,128)(2,1)S(1)}, bf16[128,1024]{1,0:T(8,128)(2,1)S(1)}, bf16[128,1024]{1,0:T(8,128)(2,1)S(1)}, s32[8,128]{1,0:T(8,128)S(1)},...) custom-call(bf16[8,128,128]{2,1,0:T(8,128)(2,1)} %refs_0_.1, ...), custom_call_target="tpu_custom_call" | custom-call | tf_op jit(solution)/shard_map/project/pallas_call | solution.py:225
  2.0 22.9 %all_to_all.34.both_ref = bf16[16,128,128]{2,1,0:T(8,128)(2,1)S(1)} all-to-all(bf16[16,128,128]{2,1,0:T(8,128)(2,1)S(1)} %bitcast.7), channel_id=1, replica_groups={{0,4,8,12,1,5,9,13,2,6,10,14,3,7,11,15},{16,20,24,28,17,21,25,29,18,22,..., dimensions={0} | all-to-all | bytes 1048576 | tf_op jit(solution)/shard_map/all_to_all | solution.py:210
  24.9 0.3 mix.2
  25.2 13.2 %all_to_all.35 = bf16[16,64,128]{2,1,0:T(8,128)(2,1)S(1)} all-to-all(bf16[16,64,128]{2,1,0:T(8,128)(2,1)S(1)} %mix.2), channel_id=1, replica_groups={{0,4,8,12,1,5,9,13,2,6,10,14,3,7,11,15},{16,20,24,28,17,21,25,29,18,22,..., dimensions={0} | all-to-all | bytes 524288 | tf_op jit(solution)/shard_map/all_to_all | solution.py:210
  38.4 1.5 %finish_project.1 = (bf16[2048,128]{1,0:T(8,128)(2,1)S(1)}, bf16[128,1024]{1,0:T(8,128)(2,1)S(1)}, bf16[128,1024]{1,0:T(8,128)(2,1)S(1)}) custom-call(bf16[1024,128]{1,0:T(8,128)(2,1)S(1)} %bitcast.4, bf16[128,1024]{1,0:T(8,128)(2,1)S(1)} %get-tuple-element.16.pair_t_ref, bf16[128,1024]{1,0:T(8,128)(2,1)S(1)} %get-tuple-element.17.gate_t_ref, ...), custom_call_target="tpu_custom_call" | custom-call | tf_op jit(solution)/shard_map/finish_project/pallas_call | solution.py:244
  39.9 18.8 %all_to_all.36.both_ref = bf16[16,128,128]{2,1,0:T(8,128)(2,1)S(1)} all-to-all(bf16[16,128,128]{2,1,0:T(8,128)(2,1)S(1)} %bitcast.6), channel_id=1, replica_groups={{0,4,8,12,1,5,9,13,2,6,10,14,3,7,11,15},{16,20,24,28,17,21,25,29,18,22,..., dimensions={0} | all-to-all | bytes 1048576 | tf_op jit(solution)/shard_map/all_to_all | solution.py:210
  58.8 0.3 mix.3
  59.0 13.2 %all_to_all.37 = bf16[16,64,128]{2,1,0:T(8,128)(2,1)S(1)} all-to-all(bf16[16,64,128]{2,1,0:T(8,128)(2,1)S(1)} %mix.3), channel_id=1, replica_groups={{0,4,8,12,1,5,9,13,2,6,10,14,3,7,11,15},{16,20,24,28,17,21,25,29,18,22,..., dimensions={0} | all-to-all | bytes 524288 | tf_op jit(solution)/shard_map/all_to_all | solution.py:210
  72.3 1.3 %finish.1 = bf16[8,128,128]{2,1,0:T(8,128)(2,1)} custom-call(bf16[1024,128]{1,0:T(8,128)(2,1)S(1)} %bitcast.5, bf16[128,1024]{1,0:T(8,128)(2,1)S(1)} %get-tuple-element.23.middle_t_ref, bf16[128,1024]{1,0:T(8,128)(2,1)S(1)} %get-tuple-element.24.gate_t_ref, f32[6,128,128]{2,1,0:T(8,128)S(1)} %get-tuple-element.19.columns_ref, ...), custom_call_target="tpu_custom_call" | custom-call | tf_op jit(solution)/shard_map/finish/pallas_call | solution.py:254

commit v10 on v9

--- a/solution.py
+++ b/solution.py
@@ -104,8 +104,10 @@
 
 
 def rank_order(count):
-    parts = 4 if count % 4 == 0 else 1
-    return [(rank % parts) * (count // parts) + rank // parts for rank in range(count)]
+    if count % 4:
+        return list(range(count))
+    quarter = count // 4
+    return [part * quarter + n for part in (0, 1, 3, 2) for n in range(quarter)]
 
 
 def take(blocks, places):

time: 73.9 us -> 74.2 us (level)
  no operation moved by 1% of the time
where the time goes in v10:
time: 74.2 us; the launch traced here: 73.9 us
  blocking collectives  68.5 us (92%)
  Pallas kernels  5.36 us (7%)
    all_to_all x4, blocking collectives, exchange(): lax.all_to_all(array, 'row', split_axis=0, concat_axis=0, tiled=True, axi...  68.5 us
    pallas_call x1, Pallas kernels, on_device(): pl.pallas_call(functools.partial(project_kernel, per_group), out_shape=(b...  1.98 us
    pallas_call x1, Pallas kernels, on_device(): pl.pallas_call(functools.partial(step_kernel, per_group), out_shape=(both...  1.49 us

profile of v10, /device:TPU:0, one launch (start us, length us, event | category | flops | bytes accessed | tf_op | source)
XLA Modules:
  0.0 73.9 jit_solution(7647707319814297738)
XLA Ops:
  0.0 2.0 %project.1 = (bf16[2048,128]{1,0:T(8,128)(2,1)S(1)}, bf16[128,1024]{1,0:T(8,128)(2,1)S(1)}, bf16[128,1024]{1,0:T(8,128)(2,1)S(1)}, s32[8,128]{1,0:T(8,128)S(1)},...) custom-call(bf16[8,128,128]{2,1,0:T(8,128)(2,1)} %refs_0_.1, ...), custom_call_target="tpu_custom_call" | custom-call | tf_op jit(solution)/shard_map/project/pallas_call | solution.py:227
  2.0 23.4 %all_to_all.34.both_ref = bf16[16,128,128]{2,1,0:T(8,128)(2,1)S(1)} all-to-all(bf16[16,128,128]{2,1,0:T(8,128)(2,1)S(1)} %bitcast.7), channel_id=1, replica_groups={{0,1,2,3,4,5,6,7,12,13,14,15,8,9,10,11},{16,17,18,19,20,21,22,23,28,29,..., dimensions={0} | all-to-all | bytes 1048576 | tf_op jit(solution)/shard_map/all_to_all | solution.py:212
  25.3 0.3 mix.2
  25.6 13.2 %all_to_all.35 = bf16[16,64,128]{2,1,0:T(8,128)(2,1)S(1)} all-to-all(bf16[16,64,128]{2,1,0:T(8,128)(2,1)S(1)} %mix.2), channel_id=1, replica_groups={{0,1,2,3,4,5,6,7,12,13,14,15,8,9,10,11},{16,17,18,19,20,21,22,23,28,29,..., dimensions={0} | all-to-all | bytes 524288 | tf_op jit(solution)/shard_map/all_to_all | solution.py:212
  38.8 1.5 %finish_project.1 = (bf16[2048,128]{1,0:T(8,128)(2,1)S(1)}, bf16[128,1024]{1,0:T(8,128)(2,1)S(1)}, bf16[128,1024]{1,0:T(8,128)(2,1)S(1)}) custom-call(bf16[1024,128]{1,0:T(8,128)(2,1)S(1)} %bitcast.4, bf16[128,1024]{1,0:T(8,128)(2,1)S(1)} %get-tuple-element.16.pair_t_ref, bf16[128,1024]{1,0:T(8,128)(2,1)S(1)} %get-tuple-element.17.gate_t_ref, ...), custom_call_target="tpu_custom_call" | custom-call | tf_op jit(solution)/shard_map/finish_project/pallas_call | solution.py:246
  40.3 18.8 %all_to_all.36.both_ref = bf16[16,128,128]{2,1,0:T(8,128)(2,1)S(1)} all-to-all(bf16[16,128,128]{2,1,0:T(8,128)(2,1)S(1)} %bitcast.6), channel_id=1, replica_groups={{0,1,2,3,4,5,6,7,12,13,14,15,8,9,10,11},{16,17,18,19,20,21,22,23,28,29,..., dimensions={0} | all-to-all | bytes 1048576 | tf_op jit(solution)/shard_map/all_to_all | solution.py:212
  59.1 0.3 mix.3
  59.4 13.2 %all_to_all.37 = bf16[16,64,128]{2,1,0:T(8,128)(2,1)S(1)} all-to-all(bf16[16,64,128]{2,1,0:T(8,128)(2,1)S(1)} %mix.3), channel_id=1, replica_groups={{0,1,2,3,4,5,6,7,12,13,14,15,8,9,10,11},{16,17,18,19,20,21,22,23,28,29,..., dimensions={0} | all-to-all | bytes 524288 | tf_op jit(solution)/shard_map/all_to_all | solution.py:212
  72.6 1.3 %finish.1 = bf16[8,128,128]{2,1,0:T(8,128)(2,1)} custom-call(bf16[1024,128]{1,0:T(8,128)(2,1)S(1)} %bitcast.5, bf16[128,1024]{1,0:T(8,128)(2,1)S(1)} %get-tuple-element.23.middle_t_ref, bf16[128,1024]{1,0:T(8,128)(2,1)S(1)} %get-tuple-element.24.gate_t_ref, f32[6,128,128]{2,1,0:T(8,128)S(1)} %get-tuple-element.19.columns_ref, ...), custom_call_target="tpu_custom_call" | custom-call | tf_op jit(solution)/shard_map/finish/pallas_call | solution.py:256

commit v11 on v10

--- a/solution.py
+++ b/solution.py
@@ -107,7 +107,7 @@
     if count % 4:
         return list(range(count))
     quarter = count // 4
-    return [part * quarter + n for part in (0, 1, 3, 2) for n in range(quarter)]
+    return [part * quarter + n for part in (0, 2, 1, 3) for n in range(quarter)]
 
 
 def take(blocks, places):

time: 74.2 us -> 73.7 us (level)
  no operation moved by 1% of the time
where the time goes in v11:
time: 73.7 us; the launch traced here: 73.4 us
  blocking collectives  68 us (92%)
  Pallas kernels  5.36 us (7%)
    all_to_all x4, blocking collectives, exchange(): lax.all_to_all(array, 'row', split_axis=0, concat_axis=0, tiled=True, axi...  68 us
    pallas_call x1, Pallas kernels, on_device(): pl.pallas_call(functools.partial(project_kernel, per_group), out_shape=(b...  1.98 us
    pallas_call x1, Pallas kernels, on_device(): pl.pallas_call(functools.partial(step_kernel, per_group), out_shape=(both...  1.49 us

profile of v11, /device:TPU:0, one launch (start us, length us, event | category | flops | bytes accessed | tf_op | source)
XLA Modules:
  0.0 73.4 jit_solution(7756395240852439666)
XLA Ops:
  0.0 2.0 %project.1 = (bf16[2048,128]{1,0:T(8,128)(2,1)S(1)}, bf16[128,1024]{1,0:T(8,128)(2,1)S(1)}, bf16[128,1024]{1,0:T(8,128)(2,1)S(1)}, s32[8,128]{1,0:T(8,128)S(1)},...) custom-call(bf16[8,128,128]{2,1,0:T(8,128)(2,1)} %refs_0_.1, ...), custom_call_target="tpu_custom_call" | custom-call | tf_op jit(solution)/shard_map/project/pallas_call | solution.py:227
  2.0 21.6 %all_to_all.34.both_ref = bf16[16,128,128]{2,1,0:T(8,128)(2,1)S(1)} all-to-all(bf16[16,128,128]{2,1,0:T(8,128)(2,1)S(1)} %bitcast.7), channel_id=1, replica_groups={{0,1,2,3,8,9,10,11,4,5,6,7,12,13,14,15},{16,17,18,19,24,25,26,27,20,21,..., dimensions={0} | all-to-all | bytes 1048576 | tf_op jit(solution)/shard_map/all_to_all | solution.py:212
  23.6 0.3 mix.2
  23.9 14.4 %all_to_all.35 = bf16[16,64,128]{2,1,0:T(8,128)(2,1)S(1)} all-to-all(bf16[16,64,128]{2,1,0:T(8,128)(2,1)S(1)} %mix.2), channel_id=1, replica_groups={{0,1,2,3,8,9,10,11,4,5,6,7,12,13,14,15},{16,17,18,19,24,25,26,27,20,21,..., dimensions={0} | all-to-all | bytes 524288 | tf_op jit(solution)/shard_map/all_to_all | solution.py:212
  38.3 1.5 %finish_project.1 = (bf16[2048,128]{1,0:T(8,128)(2,1)S(1)}, bf16[128,1024]{1,0:T(8,128)(2,1)S(1)}, bf16[128,1024]{1,0:T(8,128)(2,1)S(1)}) custom-call(bf16[1024,128]{1,0:T(8,128)(2,1)S(1)} %bitcast.4, bf16[128,1024]{1,0:T(8,128)(2,1)S(1)} %get-tuple-element.16.pair_t_ref, bf16[128,1024]{1,0:T(8,128)(2,1)S(1)} %get-tuple-element.17.gate_t_ref, ...), custom_call_target="tpu_custom_call" | custom-call | tf_op jit(solution)/shard_map/finish_project/pallas_call | solution.py:246
  39.8 17.5 %all_to_all.36.both_ref = bf16[16,128,128]{2,1,0:T(8,128)(2,1)S(1)} all-to-all(bf16[16,128,128]{2,1,0:T(8,128)(2,1)S(1)} %bitcast.6), channel_id=1, replica_groups={{0,1,2,3,8,9,10,11,4,5,6,7,12,13,14,15},{16,17,18,19,24,25,26,27,20,21,..., dimensions={0} | all-to-all | bytes 1048576 | tf_op jit(solution)/shard_map/all_to_all | solution.py:212
  57.4 0.3 mix.3
  57.6 14.4 %all_to_all.37 = bf16[16,64,128]{2,1,0:T(8,128)(2,1)S(1)} all-to-all(bf16[16,64,128]{2,1,0:T(8,128)(2,1)S(1)} %mix.3), channel_id=1, replica_groups={{0,1,2,3,8,9,10,11,4,5,6,7,12,13,14,15},{16,17,18,19,24,25,26,27,20,21,..., dimensions={0} | all-to-all | bytes 524288 | tf_op jit(solution)/shard_map/all_to_all | solution.py:212
  72.1 1.3 %finish.1 = bf16[8,128,128]{2,1,0:T(8,128)(2,1)} custom-call(bf16[1024,128]{1,0:T(8,128)(2,1)S(1)} %bitcast.5, bf16[128,1024]{1,0:T(8,128)(2,1)S(1)} %get-tuple-element.23.middle_t_ref, bf16[128,1024]{1,0:T(8,128)(2,1)S(1)} %get-tuple-element.24.gate_t_ref, f32[6,128,128]{2,1,0:T(8,128)S(1)} %get-tuple-element.19.columns_ref, ...), custom_call_target="tpu_custom_call" | custom-call | tf_op jit(solution)/shard_map/finish/pallas_call | solution.py:256

commit v12 on v7

--- a/solution.py
+++ b/solution.py
@@ -19,10 +19,6 @@
     return lax.dot_general(a, b, dims, preferred_element_type=F32)
 
 
-def sigmoid(values):
-    return 0.5 * jnp.tanh(0.5 * values) + 0.5
-
-
 def unit(values, axis):
     scale = 1.0 / values.shape[axis]
     centred = values - jnp.sum(values, axis=axis, keepdims=True) * scale
@@ -30,8 +26,8 @@
     return centred * lax.rsqrt(spread + 1e-05)
 
 
-def chunks(rows, tokens):
-    wide = max(1, min(rows, 256 // tokens))
+def chunks(rows, tokens, limit):
+    wide = max(1, min(rows, limit // tokens))
     return [list(range(start, min(start + wide, rows))) for start in range(0, rows, wide)]
 
 
@@ -48,27 +44,23 @@
     return lanes(parts).astype(BF16)
 
 
-def store_panels(panels, per_group, rows, chunk, tokens, products, mask):
+def store_panels(panels, per_group, rows, chunk, tokens, products, half_mask):
     channels = products.shape[0] // 5
     for side in range(2):
         base = 2 * side * channels
-        gated = sigmoid(products[base : base + channels]) * products[base + channels : base + 2 * channels] * mask
+        gate, value = products[base : base + channels], products[base + channels : base + 2 * channels]
+        gated = (jnp.tanh(gate) + 1.0) * (value * half_mask)
         for h, r in enumerate(chunk):
             for g in range(channels // per_group):
                 where = pl.ds((2 * g + side) * per_group * rows + r, per_group, stride=rows)
                 for t in range(tokens // LANES):
                     first = h * tokens + t * LANES
                     panels[t, where, :] = gated[g * per_group : (g + 1) * per_group, first : first + LANES]
-    return sigmoid(products[4 * channels :]).astype(BF16)
-
-
-def mask_lanes(mask_ref, chunk):
-    return lanes([mask_ref[r : r + 1].astype(F32) for r in chunk])
-
-
-def column(ref, which, norm, tokens):
-    row = ref[which, norm : norm + 1]
-    return jnp.broadcast_to(row, (tokens, row.shape[1])).T
+    return (0.5 * jnp.tanh(products[4 * channels :]) + 0.5).astype(BF16)
+
+
+def half_lanes(mask_ref, chunk):
+    return lanes([mask_ref[r : r + 1].astype(F32) * 0.5 for r in chunk])
 
 
 def project_kernel(per_group, *refs):
@@ -82,22 +74,25 @@
     for copy in copies:
         copy.wait()
     rows, tokens, channels = pair_ref.shape
+    small = jnp.concatenate([ref[which] for ref in (gain_ref, bias_ref) for which in range(2)], axis=0).T
+    for n in range(4):
+        for side in range(2):
+            place = 4 * side + n
+            columns_ref[2 * n + side] = jnp.broadcast_to(small[:, place : place + 1], (channels, tokens))
     for which in range(2):
-        proj_t_ref[which, : 4 * channels] = proj_ref[which].T
-        proj_t_ref[which, 4 * channels :] = gatew_ref[which].T
+        for part in range(4):
+            block = proj_ref[which, :, part * channels : (part + 1) * channels].T
+            proj_t_ref[which, part * channels : (part + 1) * channels] = block if part % 2 else block * 0.5
+        proj_t_ref[which, 4 * channels :] = gatew_ref[which].T * 0.5
         outw_t_ref[which] = outw_ref[which].T
-    for n, (which, norm) in enumerate(((0, 1), (1, 0), (1, 1))):
-        columns_ref[2 * n] = column(gain_ref, which, norm, tokens)
-        columns_ref[2 * n + 1] = column(bias_ref, which, norm, tokens)
-    gain, bias = column(gain_ref, 0, 0, tokens), column(bias_ref, 0, 0, tokens)
-    for chunk in chunks(rows, tokens):
+    for chunk in chunks(rows, tokens, 1024):
         part = span(chunk, tokens)
         pair_t = lanes([pair_ref[r].T for r in chunk])
         pair_t_ref[:, part] = pair_t
-        normed = affine(unit(pair_t.astype(F32), 0), gain, bias, tokens)
+        normed = affine(unit(pair_t.astype(F32), 0), columns_ref[0], columns_ref[1], tokens)
         products = dot(proj_t_ref[0], normed, NN)
         gate_t_ref[:, part] = store_panels(
-            panels, per_group, rows, chunk, tokens, products, mask_lanes(mask_ref, chunk)
+            panels, per_group, rows, chunk, tokens, products, half_lanes(mask_ref, chunk)
         )
     for t in range(tokens // LANES):
         both_ref[:, t * LANES : (t + 1) * LANES] = panels[t].astype(BF16)
@@ -129,7 +124,7 @@
     tiles = range(tokens // LANES)
     for t in tiles:
         unit_scratch[t] = units[:, t * LANES : (t + 1) * LANES]
-    for chunk in chunks(rows, tokens):
+    for chunk in chunks(rows, tokens, 512):
         part = span(chunk, tokens)
         units = lanes([unit_scratch[t, pl.ds(r, channels, stride=rows), :] for r in chunk for t in tiles])
         normed = affine(units, gain, bias, tokens)
@@ -145,14 +140,14 @@
 
     def emit(chunk, part, middle):
         middle_t_ref[:, part] = middle
-        normed = affine(unit(middle.astype(F32), 0), columns_ref[2], columns_ref[3], tokens)
+        normed = affine(unit(middle.astype(F32), 0), columns_ref[4], columns_ref[5], tokens)
         products = dot(proj_t_ref[1], normed, NN)
         gate1_t_ref[:, part] = store_panels(
-            panels, per_group, rows, chunk, tokens, products, mask_lanes(mask_ref, chunk)
+            panels, per_group, rows, chunk, tokens, products, half_lanes(mask_ref, chunk)
         )
 
     finish_rows(
-        emit, rows, merged_ref, pair_t_ref, gate_t_ref, columns_ref[0], columns_ref[1], outw_t_ref[0], unit_scratch
+        emit, rows, merged_ref, pair_t_ref, gate_t_ref, columns_ref[2], columns_ref[3], outw_t_ref[0], unit_scratch
     )
     for t in range(tokens // LANES):
         both_ref[:, t * LANES : (t + 1) * LANES] = panels[t].astype(BF16)
@@ -171,7 +166,7 @@
             copies[-1].start()
 
     finish_rows(
-        emit, rows, merged_ref, middle_t_ref, gate_t_ref, columns_ref[4], columns_ref[5], outw_t_ref[1], unit_scratch
+        emit, rows, merged_ref, middle_t_ref, gate_t_ref, columns_ref[6], columns_ref[7], outw_t_ref[1], unit_scratch
     )
     for copy in copies:
         copy.wait()
@@ -211,7 +206,7 @@
             flat_shape,
             flat_shape,
             shape((rows, tokens), inputs[1].dtype),
-            shape((6, channels, tokens), F32),
+            shape((8, channels, tokens), F32),
             shape((2, 5 * channels, channels), BF16),
             shape((2, channels, channels), BF16),
         ),

time: 72.5 us -> 72.5 us (level)
  no operation moved by 1% of the time
where the time goes in v12:
time: 72.5 us; the launch traced here: 72.2 us
  blocking collectives  66.8 us (92%)
  Pallas kernels  5.39 us (7%)
    all_to_all x4, blocking collectives, exchange(): return lax.all_to_all(array, 'row', split_axis=0, concat_axis=0, tiled=True)  66.8 us
    pallas_call x1, Pallas kernels, on_device(): pl.pallas_call(functools.partial(project_kernel, per_group), out_shape=(b...  2.02 us
    pallas_call x1, Pallas kernels, on_device(): pl.pallas_call(functools.partial(step_kernel, per_group), out_shape=(both...  1.47 us

profile of v12, /device:TPU:0, one launch (start us, length us, event | category | flops | bytes accessed | tf_op | source)
XLA Modules:
  0.0 72.2 jit_solution(15996884345136785922)
XLA Ops:
  0.0 2.0 %project.1 = (bf16[2048,128]{1,0:T(8,128)(2,1)S(1)}, bf16[128,1024]{1,0:T(8,128)(2,1)S(1)}, bf16[128,1024]{1,0:T(8,128)(2,1)S(1)}, s32[8,128]{1,0:T(8,128)S(1)},...) custom-call(bf16[8,128,128]{2,1,0:T(8,128)(2,1)} %refs_0_.1, ...), custom_call_target="tpu_custom_call" | custom-call | tf_op jit(solution)/shard_map/project/pallas_call | solution.py:202
  2.0 21.7 %all_to_all.34.both_ref = bf16[16,128,128]{2,1,0:T(8,128)(2,1)S(1)} all-to-all(bf16[16,128,128]{2,1,0:T(8,128)(2,1)S(1)} %bitcast.7), channel_id=1, replica_groups=mesh['groups'=2,'row'=16] {'row'}, dimensions={0} | all-to-all | bytes 1048576 | tf_op jit(solution)/shard_map/all_to_all | solution.py:189
  23.7 0.3 mix.2
  24.0 13.9 %all_to_all.35 = bf16[16,64,128]{2,1,0:T(8,128)(2,1)S(1)} all-to-all(bf16[16,64,128]{2,1,0:T(8,128)(2,1)S(1)} %mix.2), channel_id=1, replica_groups=mesh['groups'=2,'row'=16] {'row'}, dimensions={0} | all-to-all | bytes 524288 | tf_op jit(solution)/shard_map/all_to_all | solution.py:189
  37.9 1.5 %finish_project.1 = (bf16[2048,128]{1,0:T(8,128)(2,1)S(1)}, bf16[128,1024]{1,0:T(8,128)(2,1)S(1)}, bf16[128,1024]{1,0:T(8,128)(2,1)S(1)}) custom-call(bf16[1024,128]{1,0:T(8,128)(2,1)S(1)} %bitcast.5, bf16[128,1024]{1,0:T(8,128)(2,1)S(1)} %get-tuple-element.16.pair_t_ref, bf16[128,1024]{1,0:T(8,128)(2,1)S(1)} %get-tuple-element.17.gate_t_ref, ...), custom_call_target="tpu_custom_call" | custom-call | tf_op jit(solution)/shard_map/finish_project/pallas_call | solution.py:221
  39.4 17.2 %all_to_all.36.both_ref = bf16[16,128,128]{2,1,0:T(8,128)(2,1)S(1)} all-to-all(bf16[16,128,128]{2,1,0:T(8,128)(2,1)S(1)} %bitcast.6), channel_id=1, replica_groups=mesh['groups'=2,'row'=16] {'row'}, dimensions={0} | all-to-all | bytes 1048576 | tf_op jit(solution)/shard_map/all_to_all | solution.py:189
  56.7 0.3 mix.3
  56.9 13.9 %all_to_all.37 = bf16[16,64,128]{2,1,0:T(8,128)(2,1)S(1)} all-to-all(bf16[16,64,128]{2,1,0:T(8,128)(2,1)S(1)} %mix.3), channel_id=1, replica_groups=mesh['groups'=2,'row'=16] {'row'}, dimensions={0} | all-to-all | bytes 524288 | tf_op jit(solution)/shard_map/all_to_all | solution.py:189
  70.9 1.3 %finish.1 = bf16[8,128,128]{2,1,0:T(8,128)(2,1)} custom-call(bf16[1024,128]{1,0:T(8,128)(2,1)S(1)} %bitcast.4, bf16[128,1024]{1,0:T(8,128)(2,1)S(1)} %get-tuple-element.23.middle_t_ref, bf16[128,1024]{1,0:T(8,128)(2,1)S(1)} %get-tuple-element.24.gate_t_ref, f32[8,128,128]{2,1,0:T(8,128)S(1)} %get-tuple-element.19.columns_ref, ...), custom_call_target="tpu_custom_call" | custom-call | tf_op jit(solution)/shard_map/finish/pallas_call | solution.py:231

commit v13 on v12

--- a/solution.py
+++ b/solution.py
@@ -44,19 +44,20 @@
     return lanes(parts).astype(BF16)
 
 
-def store_panels(panels, per_group, rows, chunk, tokens, products, half_mask):
-    channels = products.shape[0] // 5
-    for side in range(2):
-        base = 2 * side * channels
-        gate, value = products[base : base + channels], products[base + channels : base + 2 * channels]
-        gated = (jnp.tanh(gate) + 1.0) * (value * half_mask)
+def project_chunk(panels, per_group, rows, chunk, tokens, weights_t, normed, half_mask):
+    channels = normed.shape[0]
+    size = channels // 2
+    for block in range(4):
+        side, first = block // 2, block % 2 * size
+        products = dot(weights_t[2 * size * block : 2 * size * (block + 1)], normed, NN)
+        gated = (jnp.tanh(products[:size]) + 1.0) * (products[size:] * half_mask)
         for h, r in enumerate(chunk):
-            for g in range(channels // per_group):
-                where = pl.ds((2 * g + side) * per_group * rows + r, per_group, stride=rows)
+            for c in range(0, size, per_group):
+                where = pl.ds((2 * (first + c) + side * per_group) * rows + r, per_group, stride=rows)
                 for t in range(tokens // LANES):
-                    first = h * tokens + t * LANES
-                    panels[t, where, :] = gated[g * per_group : (g + 1) * per_group, first : first + LANES]
-    return (0.5 * jnp.tanh(products[4 * channels :]) + 0.5).astype(BF16)
+                    lane = h * tokens + t * LANES
+                    panels[t, where, :] = gated[c : c + per_group, lane : lane + LANES]
+    return (0.5 * jnp.tanh(dot(weights_t[4 * channels :], normed, NN)) + 0.5).astype(BF16)
 
 
 def half_lanes(mask_ref, chunk):
@@ -80,19 +81,22 @@
             place = 4 * side + n
             columns_ref[2 * n + side] = jnp.broadcast_to(small[:, place : place + 1], (channels, tokens))
     for which in range(2):
+        size = channels // 2
         for part in range(4):
             block = proj_ref[which, :, part * channels : (part + 1) * channels].T
-            proj_t_ref[which, part * channels : (part + 1) * channels] = block if part % 2 else block * 0.5
+            block = block if part % 2 else block * 0.5
+            for h in range(2):
+                start = (part // 2 * 4 + h * 2 + part % 2) * size
+                proj_t_ref[which, start : start + size] = block[h * size : (h + 1) * size]
         proj_t_ref[which, 4 * channels :] = gatew_ref[which].T * 0.5
         outw_t_ref[which] = outw_ref[which].T
-    for chunk in chunks(rows, tokens, 1024):
+    for chunk in chunks(rows, tokens, 256):
         part = span(chunk, tokens)
         pair_t = lanes([pair_ref[r].T for r in chunk])
         pair_t_ref[:, part] = pair_t
         normed = affine(unit(pair_t.astype(F32), 0), columns_ref[0], columns_ref[1], tokens)
-        products = dot(proj_t_ref[0], normed, NN)
-        gate_t_ref[:, part] = store_panels(
-            panels, per_group, rows, chunk, tokens, products, half_lanes(mask_ref, chunk)
+        gate_t_ref[:, part] = project_chunk(
+            panels, per_group, rows, chunk, tokens, proj_t_ref.at[0], normed, half_lanes(mask_ref, chunk)
         )
     for t in range(tokens // LANES):
         both_ref[:, t * LANES : (t + 1) * LANES] = panels[t].astype(BF16)
@@ -119,12 +123,20 @@
 def finish_rows(emit, rows, merged_ref, pair_t_ref, gate_t_ref, gain, bias, outw_t, unit_scratch):
     tokens = merged_ref.shape[1]
     channels = merged_ref.shape[0] // rows
-    sums = merged_ref[...].astype(F32).reshape(channels, rows, tokens)
-    units = unit(sums, 0).reshape(channels * rows, tokens)
     tiles = range(tokens // LANES)
-    for t in tiles:
-        unit_scratch[t] = units[:, t * LANES : (t + 1) * LANES]
-    for chunk in chunks(rows, tokens, 512):
+    parts = [slice(first * rows, (first + 16) * rows) for first in range(0, channels, 16)]
+
+    def sums(part):
+        return merged_ref[part].astype(F32).reshape(16, rows, tokens)
+
+    average = sum(jnp.sum(sums(part), axis=0) for part in parts) * (1.0 / channels)
+    spread = sum(jnp.sum(jnp.square(sums(part) - average), axis=0) for part in parts) * (1.0 / channels)
+    inverse = lax.rsqrt(spread + 1e-05)
+    for part in parts:
+        units = ((sums(part) - average) * inverse).reshape(16 * rows, tokens)
+        for t in tiles:
+            unit_scratch[t, part, :] = units[:, t * LANES : (t + 1) * LANES]
+    for chunk in chunks(rows, tokens, 256):
         part = span(chunk, tokens)
         units = lanes([unit_scratch[t, pl.ds(r, channels, stride=rows), :] for r in chunk for t in tiles])
         normed = affine(units, gain, bias, tokens)
@@ -141,9 +153,8 @@
     def emit(chunk, part, middle):
         middle_t_ref[:, part] = middle
         normed = affine(unit(middle.astype(F32), 0), columns_ref[4], columns_ref[5], tokens)
-        products = dot(proj_t_ref[1], normed, NN)
-        gate1_t_ref[:, part] = store_panels(
-            panels, per_group, rows, chunk, tokens, products, half_lanes(mask_ref, chunk)
+        gate1_t_ref[:, part] = project_chunk(
+            panels, per_group, rows, chunk, tokens, proj_t_ref.at[1], normed, half_lanes(mask_ref, chunk)
         )
 
     finish_rows(

time: 72.5 us -> 72.5 us (level)
  no operation moved by 1% of the time
where the time goes in v13:
time: 72.5 us; the launch traced here: 72.2 us
  blocking collectives  66.8 us (92%)
  Pallas kernels  5.37 us (7%)
    all_to_all x4, blocking collectives, exchange(): return lax.all_to_all(array, 'row', split_axis=0, concat_axis=0, tiled=True)  66.8 us
    pallas_call x1, Pallas kernels, on_device(): pl.pallas_call(functools.partial(project_kernel, per_group), out_shape=(b...  1.98 us
    pallas_call x1, Pallas kernels, on_device(): pl.pallas_call(functools.partial(step_kernel, per_group), out_shape=(both...  1.62 us

profile of v13, /device:TPU:0, one launch (start us, length us, event | category | flops | bytes accessed | tf_op | source)
XLA Modules:
  0.0 72.2 jit_solution(13366595210906534913)
XLA Ops:
  0.0 2.0 %project.1 = (bf16[2048,128]{1,0:T(8,128)(2,1)S(1)}, bf16[128,1024]{1,0:T(8,128)(2,1)S(1)}, bf16[128,1024]{1,0:T(8,128)(2,1)S(1)}, s32[8,128]{1,0:T(8,128)S(1)},...) custom-call(bf16[8,128,128]{2,1,0:T(8,128)(2,1)} %refs_0_.1, ...), custom_call_target="tpu_custom_call" | custom-call | tf_op jit(solution)/shard_map/project/pallas_call | solution.py:213
  2.0 21.7 %all_to_all.34.both_ref = bf16[16,128,128]{2,1,0:T(8,128)(2,1)S(1)} all-to-all(bf16[16,128,128]{2,1,0:T(8,128)(2,1)S(1)} %bitcast.7), channel_id=1, replica_groups=mesh['groups'=2,'row'=16] {'row'}, dimensions={0} | all-to-all | bytes 1048576 | tf_op jit(solution)/shard_map/all_to_all | solution.py:200
  23.6 0.3 mix.2
  23.9 13.9 %all_to_all.35 = bf16[16,64,128]{2,1,0:T(8,128)(2,1)S(1)} all-to-all(bf16[16,64,128]{2,1,0:T(8,128)(2,1)S(1)} %mix.2), channel_id=1, replica_groups=mesh['groups'=2,'row'=16] {'row'}, dimensions={0} | all-to-all | bytes 524288 | tf_op jit(solution)/shard_map/all_to_all | solution.py:200
  37.9 1.6 %finish_project.1 = (bf16[2048,128]{1,0:T(8,128)(2,1)S(1)}, bf16[128,1024]{1,0:T(8,128)(2,1)S(1)}, bf16[128,1024]{1,0:T(8,128)(2,1)S(1)}) custom-call(bf16[1024,128]{1,0:T(8,128)(2,1)S(1)} %bitcast.5, bf16[128,1024]{1,0:T(8,128)(2,1)S(1)} %get-tuple-element.16.pair_t_ref, bf16[128,1024]{1,0:T(8,128)(2,1)S(1)} %get-tuple-element.17.gate_t_ref, ...), custom_call_target="tpu_custom_call" | custom-call | tf_op jit(solution)/shard_map/finish_project/pallas_call | solution.py:232
  39.5 17.2 %all_to_all.36.both_ref = bf16[16,128,128]{2,1,0:T(8,128)(2,1)S(1)} all-to-all(bf16[16,128,128]{2,1,0:T(8,128)(2,1)S(1)} %bitcast.6), channel_id=1, replica_groups=mesh['groups'=2,'row'=16] {'row'}, dimensions={0} | all-to-all | bytes 1048576 | tf_op jit(solution)/shard_map/all_to_all | solution.py:200
  56.8 0.3 mix.3
  57.0 13.9 %all_to_all.37 = bf16[16,64,128]{2,1,0:T(8,128)(2,1)S(1)} all-to-all(bf16[16,64,128]{2,1,0:T(8,128)(2,1)S(1)} %mix.3), channel_id=1, replica_groups=mesh['groups'=2,'row'=16] {'row'}, dimensions={0} | all-to-all | bytes 524288 | tf_op jit(solution)/shard_map/all_to_all | solution.py:200
  71.0 1.2 %finish.1 = bf16[8,128,128]{2,1,0:T(8,128)(2,1)} custom-call(bf16[1024,128]{1,0:T(8,128)(2,1)S(1)} %bitcast.4, bf16[128,1024]{1,0:T(8,128)(2,1)S(1)} %get-tuple-element.23.middle_t_ref, bf16[128,1024]{1,0:T(8,128)(2,1)S(1)} %get-tuple-element.24.gate_t_ref, f32[8,128,128]{2,1,0:T(8,128)S(1)} %get-tuple-element.19.columns_ref, ...), custom_call_target="tpu_custom_call" | custom-call | tf_op jit(solution)/shard_map/finish/pallas_call | solution.py:242

commit v14 on v12

--- a/solution.py
+++ b/solution.py
@@ -52,11 +52,19 @@
         gated = (jnp.tanh(gate) + 1.0) * (value * half_mask)
         for h, r in enumerate(chunk):
             for g in range(channels // per_group):
-                where = pl.ds((2 * g + side) * per_group * rows + r, per_group, stride=rows)
+                where = pl.ds((2 * g + side) * per_group * (rows + 1) + r, per_group, stride=rows + 1)
                 for t in range(tokens // LANES):
                     first = h * tokens + t * LANES
                     panels[t, where, :] = gated[g * per_group : (g + 1) * per_group, first : first + LANES]
     return (0.5 * jnp.tanh(products[4 * channels :]) + 0.5).astype(BF16)
+
+
+def pack_panels(panels, both_ref, rows):
+    for t in range(both_ref.shape[1] // LANES):
+        for first in range(0, both_ref.shape[0] // rows, 16):
+            parts = [panels[t, pl.ds(c * (rows + 1), rows), :] for c in range(first, first + 16)]
+            packed = jnp.concatenate(parts, axis=0).astype(BF16)
+            both_ref[first * rows : (first + 16) * rows, t * LANES : (t + 1) * LANES] = packed
 
 
 def half_lanes(mask_ref, chunk):
@@ -85,7 +93,7 @@
             proj_t_ref[which, part * channels : (part + 1) * channels] = block if part % 2 else block * 0.5
         proj_t_ref[which, 4 * channels :] = gatew_ref[which].T * 0.5
         outw_t_ref[which] = outw_ref[which].T
-    for chunk in chunks(rows, tokens, 1024):
+    for chunk in chunks(rows, tokens, 256):
         part = span(chunk, tokens)
         pair_t = lanes([pair_ref[r].T for r in chunk])
         pair_t_ref[:, part] = pair_t
@@ -94,8 +102,7 @@
         gate_t_ref[:, part] = store_panels(
             panels, per_group, rows, chunk, tokens, products, half_lanes(mask_ref, chunk)
         )
-    for t in range(tokens // LANES):
-        both_ref[:, t * LANES : (t + 1) * LANES] = panels[t].astype(BF16)
+    pack_panels(panels, both_ref, rows)
 
 
 def mix_kernel(per_group, rows, incoming, both_ref, product_ref):
@@ -119,14 +126,24 @@
 def finish_rows(emit, rows, merged_ref, pair_t_ref, gate_t_ref, gain, bias, outw_t, unit_scratch):
     tokens = merged_ref.shape[1]
     channels = merged_ref.shape[0] // rows
-    sums = merged_ref[...].astype(F32).reshape(channels, rows, tokens)
-    units = unit(sums, 0).reshape(channels * rows, tokens)
     tiles = range(tokens // LANES)
-    for t in tiles:
-        unit_scratch[t] = units[:, t * LANES : (t + 1) * LANES]
-    for chunk in chunks(rows, tokens, 512):
+    parts = [slice(first * rows, (first + 16) * rows) for first in range(0, channels, 16)]
+
+    def sums(part):
+        return merged_ref[part].astype(F32).reshape(16, rows, tokens)
+
+    average = sum(jnp.sum(sums(part), axis=0) for part in parts) * (1.0 / channels)
+    spread = sum(jnp.sum(jnp.square(sums(part) - average), axis=0) for part in parts) * (1.0 / channels)
+    inverse = lax.rsqrt(spread + 1e-05)
+    for part in parts:
+        units = (sums(part) - average) * inverse
+        for t in tiles:
+            for n in range(16):
+                where = pl.ds((part.start // rows + n) * (rows + 1), rows)
+                unit_scratch[t, where, :] = units[n, :, t * LANES : (t + 1) * LANES]
+    for chunk in chunks(rows, tokens, 256):
         part = span(chunk, tokens)
-        units = lanes([unit_scratch[t, pl.ds(r, channels, stride=rows), :] for r in chunk for t in tiles])
+        units = lanes([unit_scratch[t, pl.ds(r, channels, stride=rows + 1), :] for r in chunk for t in tiles])
         normed = affine(units, gain, bias, tokens)
         change = gate_t_ref[:, part].astype(F32) * dot(outw_t, normed, NN)
         emit(chunk, part, (pair_t_ref[:, part].astype(F32) + change).astype(BF16))
@@ -149,8 +166,7 @@
     finish_rows(
         emit, rows, merged_ref, pair_t_ref, gate_t_ref, columns_ref[2], columns_ref[3], outw_t_ref[0], unit_scratch
     )
-    for t in range(tokens // LANES):
-        both_ref[:, t * LANES : (t + 1) * LANES] = panels[t].astype(BF16)
+    pack_panels(panels, both_ref, rows)
 
 
 def finish_kernel(
@@ -182,8 +198,8 @@
     shape = jax.ShapeDtypeStruct
     both_shape = shape((2 * channels * rows, tokens), BF16)
     flat_shape = shape((channels, rows * tokens), BF16)
-    panels = pltpu.VMEM((tokens // LANES, 2 * channels * rows, LANES), F32)
-    unit_scratch = pltpu.VMEM((tokens // LANES, channels * rows, LANES), F32)
+    panels = pltpu.VMEM((tokens // LANES, 2 * channels * (rows + 1), LANES), F32)
+    unit_scratch = pltpu.VMEM((tokens // LANES, channels * (rows + 1), LANES), F32)
 
     def exchange(array):
         return lax.all_to_all(array, "row", split_axis=0, concat_axis=0, tiled=True)

time: 72.5 us -> 72.2 us (level)
  no operation moved by 1% of the time
where the time goes in v14:
time: 72.2 us; the launch traced here: 71.9 us
  blocking collectives  66.8 us (93%)
  Pallas kernels  5.07 us (7%)
    all_to_all x4, blocking collectives, exchange(): return lax.all_to_all(array, 'row', split_axis=0, concat_axis=0, tiled=True)  66.8 us
    pallas_call x1, Pallas kernels, on_device(): pl.pallas_call(functools.partial(project_kernel, per_group), out_shape=(b...  2 us

profile of v14, /device:TPU:0, one launch (start us, length us, event | category | flops | bytes accessed | tf_op | source)
XLA Modules:
  0.0 71.9 jit_solution(8369177317023234749)
XLA Ops:
  0.0 2.0 %project.1 = (bf16[2048,128]{1,0:T(8,128)(2,1)S(1)}, bf16[128,1024]{1,0:T(8,128)(2,1)S(1)}, bf16[128,1024]{1,0:T(8,128)(2,1)S(1)}, s32[8,128]{1,0:T(8,128)S(1)},...) custom-call(bf16[8,128,128]{2,1,0:T(8,128)(2,1)} %refs_0_.1, ...), custom_call_target="tpu_custom_call" | custom-call | tf_op jit(solution)/shard_map/project/pallas_call | solution.py:218
  2.0 21.7 %all_to_all.34.both_ref = bf16[16,128,128]{2,1,0:T(8,128)(2,1)S(1)} all-to-all(bf16[16,128,128]{2,1,0:T(8,128)(2,1)S(1)} %bitcast.7), channel_id=1, replica_groups=mesh['groups'=2,'row'=16] {'row'}, dimensions={0} | all-to-all | bytes 1048576 | tf_op jit(solution)/shard_map/all_to_all | solution.py:205
  23.7 0.3 mix.2
  24.0 13.9 %all_to_all.35 = bf16[16,64,128]{2,1,0:T(8,128)(2,1)S(1)} all-to-all(bf16[16,64,128]{2,1,0:T(8,128)(2,1)S(1)} %mix.2), channel_id=1, replica_groups=mesh['groups'=2,'row'=16] {'row'}, dimensions={0} | all-to-all | bytes 524288 | tf_op jit(solution)/shard_map/all_to_all | solution.py:205
  37.9 1.3 %finish_project.1 = (bf16[2048,128]{1,0:T(8,128)(2,1)S(1)}, bf16[128,1024]{1,0:T(8,128)(2,1)S(1)}, bf16[128,1024]{1,0:T(8,128)(2,1)S(1)}) custom-call(bf16[1024,128]{1,0:T(8,128)(2,1)S(1)} %bitcast.5, bf16[128,1024]{1,0:T(8,128)(2,1)S(1)} %get-tuple-element.16.pair_t_ref, bf16[128,1024]{1,0:T(8,128)(2,1)S(1)} %get-tuple-element.17.gate_t_ref, ...), custom_call_target="tpu_custom_call" | custom-call | tf_op jit(solution)/shard_map/finish_project/pallas_call | solution.py:237
  39.2 17.2 %all_to_all.36.both_ref = bf16[16,128,128]{2,1,0:T(8,128)(2,1)S(1)} all-to-all(bf16[16,128,128]{2,1,0:T(8,128)(2,1)S(1)} %bitcast.6), channel_id=1, replica_groups=mesh['groups'=2,'row'=16] {'row'}, dimensions={0} | all-to-all | bytes 1048576 | tf_op jit(solution)/shard_map/all_to_all | solution.py:205
  56.5 0.3 mix.3
  56.7 13.9 %all_to_all.37 = bf16[16,64,128]{2,1,0:T(8,128)(2,1)S(1)} all-to-all(bf16[16,64,128]{2,1,0:T(8,128)(2,1)S(1)} %mix.3), channel_id=1, replica_groups=mesh['groups'=2,'row'=16] {'row'}, dimensions={0} | all-to-all | bytes 524288 | tf_op jit(solution)/shard_map/all_to_all | solution.py:205
  70.7 1.2 %finish.1 = bf16[8,128,128]{2,1,0:T(8,128)(2,1)} custom-call(bf16[1024,128]{1,0:T(8,128)(2,1)S(1)} %bitcast.4, bf16[128,1024]{1,0:T(8,128)(2,1)S(1)} %get-tuple-element.23.middle_t_ref, bf16[128,1024]{1,0:T(8,128)(2,1)S(1)} %get-tuple-element.24.gate_t_ref, f32[8,128,128]{2,1,0:T(8,128)S(1)} %get-tuple-element.19.columns_ref, ...), custom_call_target="tpu_custom_call" | custom-call | tf_op jit(solution)/shard_map/finish/pallas_call | solution.py:247

commit v15 on v14

--- a/solution.py
+++ b/solution.py
@@ -67,14 +67,43 @@
             both_ref[first * rows : (first + 16) * rows, t * LANES : (t + 1) * LANES] = packed
 
 
+def split_panels(panels, core_ref, left_ref, right_ref, other_ref, rows):
+    size = left_ref.shape[0]
+    for t in range(left_ref.shape[1] // LANES):
+        for first in range(0, size // rows, 16):
+            first_core = jnp.full((16 * rows, LANES), core_ref[0]) == 0
+            for side, own_ref in enumerate((left_ref, right_ref)):
+                mine, others = [
+                    jnp.concatenate(
+                        [
+                            panels[t, pl.ds(((2 * g + side) * (size // rows) + c) * (rows + 1), rows), :]
+                            for c in range(first, first + 16)
+                        ],
+                        axis=0,
+                    )
+                    for g in range(2)
+                ]
+                lane = slice(t * LANES, (t + 1) * LANES)
+                part = slice(first * rows, (first + 16) * rows)
+                own_ref[part, lane] = jnp.where(first_core, mine, others).astype(BF16)
+                part = slice(side * size + first * rows, side * size + (first + 16) * rows)
+                other_ref[part, lane] = jnp.where(first_core, others, mine).astype(BF16)
+
+
 def half_lanes(mask_ref, chunk):
     return lanes([mask_ref[r : r + 1].astype(F32) * 0.5 for r in chunk])
 
 
-def project_kernel(per_group, *refs):
+def project_kernel(per_group, by_core, *refs):
+    core_ref, refs = (refs[0], refs[1:]) if by_core else (None, refs)
     inputs, refs = refs[:7], refs[7:]
-    both_ref, pair_t_ref, gate_t_ref, mask_ref, columns_ref, proj_t_ref, outw_t_ref = refs[:7]
-    pair_ref, gain_ref, bias_ref, proj_ref, gatew_ref, outw_ref, panels, sems = refs[7:]
+    if by_core:
+        outs, refs = refs[:3], refs[3:]
+        both_ref = None
+    else:
+        both_ref, refs = refs[0], refs[1:]
+    pair_t_ref, gate_t_ref, mask_ref, columns_ref, proj_t_ref, outw_t_ref = refs[:6]
+    pair_ref, gain_ref, bias_ref, proj_ref, gatew_ref, outw_ref, panels, sems = refs[6:]
     held = (pair_ref, mask_ref, gain_ref, bias_ref, proj_ref, gatew_ref, outw_ref)
     copies = [pltpu.make_async_copy(src, dst, sems.at[n]) for n, (src, dst) in enumerate(zip(inputs, held))]
     for copy in copies:
@@ -102,7 +131,10 @@
         gate_t_ref[:, part] = store_panels(
             panels, per_group, rows, chunk, tokens, products, half_lanes(mask_ref, chunk)
         )
-    pack_panels(panels, both_ref, rows)
+    if by_core:
+        split_panels(panels, core_ref, *outs, rows)
+    else:
+        pack_panels(panels, both_ref, rows)
 
 
 def mix_kernel(per_group, rows, incoming, both_ref, product_ref):
@@ -123,14 +155,25 @@
         product_ref[:, pair * step : (pair + 1) * step, :] = jnp.concatenate(sums, axis=1).astype(BF16)
 
 
-def finish_rows(emit, rows, merged_ref, pair_t_ref, gate_t_ref, gain, bias, outw_t, unit_scratch):
-    tokens = merged_ref.shape[1]
-    channels = merged_ref.shape[0] // rows
+def mix_gathered(rows, core_ref, own_ref, got_ref, right_ref, keep_ref, send_ref):
+    chips, _, count, _, tokens = right_ref.shape
+    first_core = jnp.full((chips, rows, tokens), core_ref[0]) == 0
+    for c in range(count):
+        mine, others = right_ref[:, 0, c].astype(F32), right_ref[:, 1, c].astype(F32)
+        halves = [jnp.where(first_core, mine, others), jnp.where(first_core, others, mine)]
+        right = jnp.concatenate(halves, axis=1).reshape(2 * chips * rows, tokens).astype(BF16)
+        left = jnp.concatenate([own_ref[c].astype(F32), got_ref[c].astype(F32)], axis=0).astype(BF16)
+        sums = dot(left, right, NT)
+        keep_ref[c] = sums[:rows].astype(BF16)
+        send_ref[c] = sums[rows:].astype(BF16)
+
+
+def finish_rows(emit, rows, channels, tokens, load, pair_t_ref, gate_t_ref, gain, bias, outw_t, unit_scratch):
     tiles = range(tokens // LANES)
     parts = [slice(first * rows, (first + 16) * rows) for first in range(0, channels, 16)]
 
     def sums(part):
-        return merged_ref[part].astype(F32).reshape(16, rows, tokens)
+        return load(part).reshape(16, rows, tokens)
 
     average = sum(jnp.sum(sums(part), axis=0) for part in parts) * (1.0 / channels)
     spread = sum(jnp.sum(jnp.square(sums(part) - average), axis=0) for part in parts) * (1.0 / channels)
@@ -149,8 +192,24 @@
         emit(chunk, part, (pair_t_ref[:, part].astype(F32) + change).astype(BF16))
 
 
-def step_kernel(
-    per_group, merged_ref, pair_t_ref, gate_t_ref, mask_ref, columns_ref, outw_t_ref, proj_t_ref,
+def step_kernel(per_group, by_core, *refs):
+    if not by_core:
+        merged_ref, refs = refs[0], refs[1:]
+        return step_rows(per_group, lambda part: merged_ref[part].astype(F32), *refs)
+    core_ref, keep_ref, got_ref, refs = refs[0], refs[1], refs[2], refs[3:]
+    size = keep_ref.shape[0]
+
+    def load(part):
+        late = part.start >= size
+        part = slice(part.start - size, part.stop - size) if late else part
+        keep, got = keep_ref[part].astype(F32), got_ref[part].astype(F32)
+        return jnp.where(jnp.full(keep.shape, core_ref[0]) == int(late), keep, got)
+
+    step_rows(per_group, load, *refs)
+
+
+def step_rows(
+    per_group, load, pair_t_ref, gate_t_ref, mask_ref, columns_ref, outw_t_ref, proj_t_ref,
     both_ref, middle_t_ref, gate1_t_ref, unit_scratch, panels,
 ):
     rows, tokens = mask_ref.shape
@@ -164,7 +223,8 @@
         )
 
     finish_rows(
-        emit, rows, merged_ref, pair_t_ref, gate_t_ref, columns_ref[2], columns_ref[3], outw_t_ref[0], unit_scratch
+        emit, rows, pair_t_ref.shape[0], tokens, load, pair_t_ref, gate_t_ref, columns_ref[2], columns_ref[3],
+        outw_t_ref[0], unit_scratch,
     )
     pack_panels(panels, both_ref, rows)
 
@@ -182,7 +242,8 @@
             copies[-1].start()
 
     finish_rows(
-        emit, rows, merged_ref, middle_t_ref, gate_t_ref, columns_ref[6], columns_ref[7], outw_t_ref[1], unit_scratch
+        emit, rows, middle_t_ref.shape[0], tokens, lambda part: merged_ref[part].astype(F32), middle_t_ref, gate_t_ref,
+        columns_ref[6], columns_ref[7], outw_t_ref[1], unit_scratch,
     )
     for copy in copies:
         copy.wait()
@@ -215,10 +276,16 @@
         )(both.reshape(groups, 2 * per_group * rows, tokens))
         return product.reshape(channels * rows, tokens)
 
-    both, pair_t, gate_t, mask, columns, proj_t, outw_t = pl.pallas_call(
-        functools.partial(project_kernel, per_group),
-        out_shape=(
-            both_shape,
+    half = channels // 2
+    by_core = groups % 2 == 0 and groups * rows * tokens * half * 2 <= 4 * 2**20
+    smem = pl.BlockSpec(memory_space=pltpu.SMEM)
+    core = (lax.axis_index("row") % 2).astype(jnp.int32).reshape(1)
+    half_shape = shape((half * rows, tokens), BF16)
+    projected = (half_shape, half_shape, shape((2 * half * rows, tokens), BF16)) if by_core else (both_shape,)
+    results = pl.pallas_call(
+        functools.partial(project_kernel, half if by_core else per_group, by_core),
+        out_shape=projected
+        + (
             flat_shape,
             flat_shape,
             shape((rows, tokens), inputs[1].dtype),
@@ -226,23 +293,52 @@
             shape((2, 5 * channels, channels), BF16),
             shape((2, channels, channels), BF16),
         ),
-        in_specs=[hbm] * 7,
-        out_specs=(whole,) * 7,
+        in_specs=[smem] * by_core + [hbm] * 7,
+        out_specs=(whole,) * (len(projected) + 6),
         scratch_shapes=[pltpu.VMEM(inputs[n].shape, inputs[n].dtype) for n in (0, 2, 3, 4, 5, 6)]
         + [panels, pltpu.SemaphoreType.DMA((7,))],
         compiler_params=params,
         name="project",
-    )(*(pltpu.with_memory_space_constraint(a, pltpu.HBM) for a in inputs))
-    merged = exchange(mix(exchange(both), False))
+    )(*[core] * by_core, *(pltpu.with_memory_space_constraint(a, pltpu.HBM) for a in inputs))
+    pair_t, gate_t, mask, columns, proj_t, outw_t = results[-6:]
+    if by_core:
+        left, right, other = results[:3]
+        swap = [(d, d ^ 1) for d in range(groups)]
+        got = lax.ppermute(other, "row", swap)
+        gathered = lax.all_gather(
+            jnp.concatenate([right, got[half * rows :]], axis=0),
+            "row",
+            axis_index_groups=[list(range(c, groups, 2)) for c in range(2)],
+        )
+        block = half // 4
+        keep, send = pl.pallas_call(
+            functools.partial(mix_gathered, rows),
+            grid=(4,),
+            out_shape=(shape((half, rows, tokens), BF16),) * 2,
+            in_specs=[smem]
+            + [pl.BlockSpec((block, rows, tokens), lambda n: (n, 0, 0))] * 2
+            + [pl.BlockSpec((groups // 2, 2, block, rows, tokens), lambda n: (0, 0, n, 0, 0))],
+            out_specs=(pl.BlockSpec((block, rows, tokens), lambda n: (n, 0, 0)),) * 2,
+            compiler_params=params,
+            name="mix_gathered",
+        )(
+            core,
+            left.reshape(half, rows, tokens),
+            got.reshape(2 * half, rows, tokens),
+            gathered.reshape(groups // 2, 2, half, rows, tokens),
+        )
+        merged = (core, keep.reshape(half * rows, tokens), lax.ppermute(send, "row", swap).reshape(half * rows, tokens))
+    else:
+        merged = (exchange(mix(exchange(results[0]), False)),)
     both, middle_t, gate_t = pl.pallas_call(
-        functools.partial(step_kernel, per_group),
+        functools.partial(step_kernel, per_group, by_core),
         out_shape=(both_shape, flat_shape, flat_shape),
-        in_specs=[whole] * 7,
+        in_specs=[smem] * by_core + [whole] * (len(merged) - by_core + 6),
         out_specs=(whole,) * 3,
         scratch_shapes=[unit_scratch, panels],
         compiler_params=params,
         name="finish_project",
-    )(merged, pair_t, gate_t, mask, columns, outw_t, proj_t)
+    )(*merged, pair_t, gate_t, mask, columns, outw_t, proj_t)
     merged = exchange(mix(exchange(both), True))
     return pl.pallas_call(
         finish_kernel,

time: 72.2 us -> 109 us (1.51)
  waiting for transfers between devices: 0 us -> 54.6 us
  blocking collectives: 66.8 us -> 31.4 us
  between operations: 0.03 us -> 13.4 us
  local copies, waits for them, and re-layouts: 0 us -> 1.6 us
  Pallas kernels: 5.07 us -> 6.5 us
    all_gather x0 -> x1, waiting for transfers between devices: none -> 52.1 us  [on_device(): lax.all_gather(jnp.concatenate([right, got[half * rows:]], axis=0), 'row'...]
    all_to_all x4 -> x2, blocking collectives: 66.8 us -> 31.4 us  [exchange(): return lax.all_to_all(array, 'row', split_axis=0, concat_axis=0, tiled=True)]
    ppermute x0 -> x2, waiting for transfers between devices: none -> 2.5 us  [the longest x1 1.34 us: on_device(): lax.ppermute(send, 'row', swap).reshape(half * rows, tokens)]
    pallas_call x2 -> x3, Pallas kernels: 3.3 us -> 5.03 us  [the longest x1 1.99 us: on_device(): pl.pallas_call(functools.partial(project_kernel, half if by_core else per...]
    unnamed x0 -> x2, local copies, waits for them, and re-layouts: none -> 1.59 us
  transfers between devices with their start and end apart: 0 -> 3, of which waited for: 0 -> 3; matrix products, arithmetic and copies ran while one was open for 0% -> 0% of each run, Pallas kernels for 0% -> 0%
where the time goes in v15:
time: 109 us
  waiting for transfers between devices  54.6 us (50%)
  blocking collectives  31.4 us (29%)
  between operations  13.4 us (12%)
  Pallas kernels  6.5 us (6%)
  local copies, waits for them, and re-layouts  1.6 us (1%)
    all_gather x1, waiting for transfers between devices, on_device(): lax.all_gather(jnp.concatenate([right, got[half * rows:]], axis=0), 'row'...  52.1 us
    all_to_all x2, blocking collectives, exchange(): return lax.all_to_all(array, 'row', split_axis=0, concat_axis=0, tiled=True)  31.4 us
  transfers between devices with their start and end apart: 3, of which 3 were waited for; matrix products, arithmetic and copies ran while one was open for 0% of the time, Pallas kernels for 0%

profile of v15, /device:TPU:0, one launch (start us, length us, event | category | flops | bytes accessed | tf_op | source)
XLA Modules:
  0.0 108.8 jit_solution(11397073971831187980)
XLA Ops:
  6.5 0.0 all-gather.3.cloned.1.call-start
  6.5 2.0 %project.1 = (bf16[512,128]{1,0:T(8,128)(2,1)S(1)}, bf16[512,128]{1,0:T(8,128)(2,1)S(1)}, bf16[1024,128]{1,0:T(8,128)(2,1)S(1)}, bf16[128,1024]{1,0:T(8,128)(2,1...) custom-call(s32[1]{0:T(128)} %bitcast.refs_0_.core_ref, ...), custom_call_target="tpu_custom_call" | custom-call | tf_op jit(solution)/shard_map/project/pallas_call | solution.py:285
  8.5 0.5 collective-permute-start
  9.1 1.2 %collective-permute-done = bf16[1024,128]{1,0:T(8,128)(2,1)S(1)} collective-permute-done((bf16[1024,128]{1,0:T(8,128)(2,1)S(1)}, bf16[1024,128]{1,0:T(8,128)(2,1)S(1)}, u32[]{:S(2)}, u32[]{:S(2)}) %collective-permute-start) | collective-permute-done | bytes 262176 | tf_op jit(solution)/shard_map/ppermute | solution.py:307
  10.2 0.7 pad_maximum_fusion
  10.9 0.0 all-gather.3.cloned.1.call-update
  11.0 52.1 %all-gather.3.cloned.1.call-done = bf16[8192,128]{1,0:T(8,128)(2,1)} async-done(((bf16[1024,128]{1,0:T(8,128)(2,1)}), bf16[8192,128]{1,0:T(8,128)(2,1)}) %all-gather.3.cloned.1.call-update) | async-done | bytes 2097168 | tf_op jit(solution)/shard_map/all_gather | solution.py:308
  63.0 0.0 copy-start
  63.0 1.6 %copy-done = bf16[8192,128]{1,0:T(8,128)(2,1)S(1)} copy-done((bf16[8192,128]{1,0:T(8,128)(2,1)S(1)}, bf16[8192,128]{1,0:T(8,128)(2,1)}, u32[]{:S(2)}) %copy-start) | copy-done | bytes 2097176
  64.6 1.7 %mix_gathered.1 = (bf16[64,8,128]{2,1,0:T(8,128)(2,1)S(1)}, bf16[64,8,128]{2,1,0:T(8,128)(2,1)S(1)}) custom-call(s32[1]{0:T(128)} %bitcast.refs_0_.core_ref, bf16[64,8,128]{2,1,0:T(8,128)(2,1)S(1)} %bitcast.14, bf16[128,8,128]{2,1,0:T(8,128)(2,1)S(1)} %bitcast.10, bf16[8,2,64,8,128]{4,3,2,1,0:T(8,128)(2,1)S(1)} %bitcast.8), custom_call_target="tpu_custom_call" | custom-call | tf_op jit(solution)/shard_map/mix_gathered/pallas_call | solution.py:314
  66.3 0.0 collective-permute-start.1
  66.4 1.3 %collective-permute-done.1 = bf16[64,8,128]{2,1,0:T(8,128)(2,1)S(1)} collective-permute-done((bf16[64,8,128]{2,1,0:T(8,128)(2,1)S(1)}, bf16[64,8,128]{2,1,0:T(8,128)(2,1)S(1)}, u32[]{:S(2)}, u32[]{:S(2)}) %collective-permute-start.1) | collective-permute-done | bytes 131104 | tf_op jit(solution)/shard_map/ppermute | solution.py:330
  67.7 1.3 %finish_project.1 = (bf16[2048,128]{1,0:T(8,128)(2,1)S(1)}, bf16[128,1024]{1,0:T(8,128)(2,1)S(1)}, bf16[128,1024]{1,0:T(8,128)(2,1)S(1)}) custom-call(s32[1]{0:T(128)} %bitcast.refs_0_.core_ref, bf16[512,128]{1,0:T(8,128)(2,1)S(1)} %bitcast.12, bf16[512,128]{1,0:T(8,128)(2,1)S(1)} %bitcast.13, bf16[128,1024]{1,0:T(8,128)(2,1)S(1)} %get-tuple-element.24.refs_3_, ...), custom_call_target="tpu_custom_call" | custom-call | tf_op jit(solution)/shard_map/finish_project/pallas_call | solution.py:333
  69.1 17.5 %all_to_all.17.both_ref = bf16[16,128,128]{2,1,0:T(8,128)(2,1)S(1)} all-to-all(bf16[16,128,128]{2,1,0:T(8,128)(2,1)S(1)} %bitcast.11), channel_id=1, replica_groups=mesh['groups'=2,'row'=16] {'row'}, dimensions={0} | all-to-all | bytes 1048576 | tf_op jit(solution)/shard_map/all_to_all | solution.py:266
  86.5 0.3 mix.1
  86.8 13.9 %all_to_all.18 = bf16[16,64,128]{2,1,0:T(8,128)(2,1)S(1)} all-to-all(bf16[16,64,128]{2,1,0:T(8,128)(2,1)S(1)} %mix.1), channel_id=1, replica_groups=mesh['groups'=2,'row'=16] {'row'}, dimensions={0} | all-to-all | bytes 524288 | tf_op jit(solution)/shard_map/all_to_all | solution.py:266
  100.7 1.2 %finish.1 = bf16[8,128,128]{2,1,0:T(8,128)(2,1)} custom-call(bf16[1024,128]{1,0:T(8,128)(2,1)S(1)} %bitcast.9, bf16[128,1024]{1,0:T(8,128)(2,1)S(1)} %get-tuple-element.31.middle_t_ref, bf16[128,1024]{1,0:T(8,128)(2,1)S(1)} %get-tuple-element.32.gate_t_ref, f32[8,128,128]{2,1,0:T(8,128)S(1)} %get-tuple-element.27.refs_6_.columns_ref, ...), custom_call_target="tpu_custom_call" | custom-call | tf_op jit(solution)/shard_map/finish/pallas_call | solution.py:343
  (1 shorter events, 0.0 us)
Async XLA Ops:
  6.5 56.5 %all-gather.3.cloned.1.call-start = ((), (), s32[]{:S(2)}) async-start(), calls=%async_computation.2 | async-start | bytes 2359296 | tf_op jit(solution)/shard_map/all_gather | solution.py:308
  8.5 1.7 %collective-permute-start = (bf16[1024,128]{1,0:T(8,128)(2,1)S(1)}, bf16[1024,128]{1,0:T(8,128)(2,1)S(1)}, u32[]{:S(2)}, u32[]{:S(2)}) collective-permute-start(bf16[1024,128]{1,0:T(8,128)(2,1)S(1)} %get-tuple-element.20), channel_id=1, source_target_pairs={{0,1},{1,0},{2,3},{3,2},{4,5},{5,4},{6,7},{7,6},{8,9},{9,8},{10,11... | collective-permute-start | bytes 786440 | tf_op jit(solution)/shard_map/ppermute | solution.py:307
  63.0 1.6 %copy-start = (bf16[8192,128]{1,0:T(8,128)(2,1)S(1)}, bf16[8192,128]{1,0:T(8,128)(2,1)}, u32[]{:S(2)}) copy-start(bf16[8192,128]{1,0:T(8,128)(2,1)} %all-gather.3.cloned.1.call-done) | copy-start | bytes 6291460
  66.3 1.4 %collective-permute-start.1 = (bf16[64,8,128]{2,1,0:T(8,128)(2,1)S(1)}, bf16[64,8,128]{2,1,0:T(8,128)(2,1)S(1)}, u32[]{:S(2)}, u32[]{:S(2)}) collective-permute-start(bf16[64,8,128]{2,1,0:T(8,128)(2,1)S(1)} %get-tuple-element.23), channel_id=1, source_target_pairs={{0,1},{1,0},{2,3},{3,2},{4,5},{5,4},{6,7},{7,6},{8,9},{9,8},{10,11... | collective-permute-start | bytes 393224 | tf_op jit(solution)/shard_map/ppermute | solution.py:330
Sparse Core Ops, SparseCore 0:
  11.1 51.8 all-gather.2

commit v16 on v15

--- a/solution.py
+++ b/solution.py
@@ -67,12 +67,12 @@
             both_ref[first * rows : (first + 16) * rows, t * LANES : (t + 1) * LANES] = packed
 
 
-def split_panels(panels, core_ref, left_ref, right_ref, other_ref, rows):
+def split_panels(panels, core_ref, left_ref, right_ref, other_left_ref, other_right_ref, rows):
     size = left_ref.shape[0]
     for t in range(left_ref.shape[1] // LANES):
         for first in range(0, size // rows, 16):
             first_core = jnp.full((16 * rows, LANES), core_ref[0]) == 0
-            for side, own_ref in enumerate((left_ref, right_ref)):
+            for side, (own_ref, other_ref) in enumerate(((left_ref, other_left_ref), (right_ref, other_right_ref))):
                 mine, others = [
                     jnp.concatenate(
                         [
@@ -86,7 +86,6 @@
                 lane = slice(t * LANES, (t + 1) * LANES)
                 part = slice(first * rows, (first + 16) * rows)
                 own_ref[part, lane] = jnp.where(first_core, mine, others).astype(BF16)
-                part = slice(side * size + first * rows, side * size + (first + 16) * rows)
                 other_ref[part, lane] = jnp.where(first_core, others, mine).astype(BF16)
 
 
@@ -98,7 +97,7 @@
     core_ref, refs = (refs[0], refs[1:]) if by_core else (None, refs)
     inputs, refs = refs[:7], refs[7:]
     if by_core:
-        outs, refs = refs[:3], refs[3:]
+        outs, refs = refs[:4], refs[4:]
         both_ref = None
     else:
         both_ref, refs = refs[0], refs[1:]
@@ -155,17 +154,42 @@
         product_ref[:, pair * step : (pair + 1) * step, :] = jnp.concatenate(sums, axis=1).astype(BF16)
 
 
-def mix_gathered(rows, core_ref, own_ref, got_ref, right_ref, keep_ref, send_ref):
-    chips, _, count, _, tokens = right_ref.shape
-    first_core = jnp.full((chips, rows, tokens), core_ref[0]) == 0
-    for c in range(count):
-        mine, others = right_ref[:, 0, c].astype(F32), right_ref[:, 1, c].astype(F32)
-        halves = [jnp.where(first_core, mine, others), jnp.where(first_core, others, mine)]
-        right = jnp.concatenate(halves, axis=1).reshape(2 * chips * rows, tokens).astype(BF16)
-        left = jnp.concatenate([own_ref[c].astype(F32), got_ref[c].astype(F32)], axis=0).astype(BF16)
-        sums = dot(left, right, NT)
-        keep_ref[c] = sums[:rows].astype(BF16)
-        send_ref[c] = sums[rows:].astype(BF16)
+def ring_chips(count):
+    return list(range(0, count, 2)) + list(range(count - 1, 0, -2))
+
+
+def token_order(place_ref, chips, rows, tokens):
+    shape = (tokens, tokens)
+    lane, token = (lax.broadcasted_iota(jnp.int32, shape, axis) for axis in range(2))
+    core, place = jnp.full(shape, place_ref[0]), jnp.full(shape, place_ref[1])
+    device = token // rows
+    chip, source_core = device // 2, device % 2
+    source = jnp.where(chip % 2 == 0, chip // 2, chips - 1 - chip // 2)
+    distance = (place - source + chips) % chips
+    slot = 2 * distance + jnp.where(source_core == core, 0, 1)
+    return jnp.where(lane == slot * rows + token % rows, 1.0, 0.0).astype(BF16)
+
+
+def mix_gathered(place_ref, own_ref, got_ref, *refs):
+    rights, (keep_ref, send_ref) = refs[:-2], refs[-2:]
+    count, rows, tokens = own_ref.shape
+    order = token_order(place_ref, len(rights) // 2, rows, tokens)
+    group = 8
+
+    def body(n, carry):
+        part = pl.ds(n * group, group)
+        lefts = jnp.concatenate([own_ref[part].astype(F32), got_ref[part].astype(F32)], axis=1).astype(BF16)
+        blocks = [ref[part].astype(F32) for ref in rights]
+        sums = []
+        for c in range(group):
+            right = jnp.concatenate([block[c] for block in blocks], axis=0).astype(BF16)
+            sums.append(dot(lefts[c], right, NT).astype(BF16))
+        sums = dot(jnp.concatenate(sums, axis=0), order, NN).reshape(group, 2 * rows, tokens)
+        keep_ref[part] = sums[:, :rows].astype(BF16)
+        send_ref[part] = sums[:, rows:].astype(BF16)
+        return carry
+
+    lax.fori_loop(0, count // group, body, 0)
 
 
 def finish_rows(emit, rows, channels, tokens, load, pair_t_ref, gate_t_ref, gain, bias, outw_t, unit_scratch):
@@ -277,11 +301,11 @@
         return product.reshape(channels * rows, tokens)
 
     half = channels // 2
-    by_core = groups % 2 == 0 and groups * rows * tokens * half * 2 <= 4 * 2**20
+    by_core = groups % 4 == 0 and groups * rows * tokens * half * 2 <= 4 * 2**20
     smem = pl.BlockSpec(memory_space=pltpu.SMEM)
     core = (lax.axis_index("row") % 2).astype(jnp.int32).reshape(1)
     half_shape = shape((half * rows, tokens), BF16)
-    projected = (half_shape, half_shape, shape((2 * half * rows, tokens), BF16)) if by_core else (both_shape,)
+    projected = (half_shape,) * 4 if by_core else (both_shape,)
     results = pl.pallas_call(
         functools.partial(project_kernel, half if by_core else per_group, by_core),
         out_shape=projected
@@ -302,30 +326,43 @@
     )(*[core] * by_core, *(pltpu.with_memory_space_constraint(a, pltpu.HBM) for a in inputs))
     pair_t, gate_t, mask, columns, proj_t, outw_t = results[-6:]
     if by_core:
-        left, right, other = results[:3]
+        left, right, other_left, other_right = results[:4]
+        chips = groups // 2
+        ring = ring_chips(chips)
+
+        def along(array, step):
+            pairs = [(2 * q + c, 2 * ring[(p + step) % chips] + c) for p, q in enumerate(ring) for c in range(2)]
+            return lax.ppermute(array, "row", pairs)
+
+        def rounds(array, step, count):
+            arrays = [array]
+            for _ in range(count):
+                arrays.append(along(arrays[-1], step))
+            return arrays
+
         swap = [(d, d ^ 1) for d in range(groups)]
-        got = lax.ppermute(other, "row", swap)
-        gathered = lax.all_gather(
-            jnp.concatenate([right, got[half * rows :]], axis=0),
-            "row",
-            axis_index_groups=[list(range(c, groups, 2)) for c in range(2)],
-        )
-        block = half // 4
+        got_right = lax.ppermute(other_right, "row", swap)
+        got_left = lax.ppermute(other_left, "row", swap)
+        middle = chips // 2
+        ups = [rounds(right, 1, middle), rounds(got_right, 1, middle - 1)]
+        downs = [rounds(right, -1, middle - 1), rounds(got_right, -1, middle)]
+        rights = [
+            ups[piece][distance] if distance < len(ups[piece]) else downs[piece][chips - distance]
+            for distance in range(chips)
+            for piece in range(2)
+        ]
+        chip = lax.axis_index("row") // 2
+        place = jnp.where(chip % 2 == 0, chip // 2, chips - 1 - chip // 2).astype(jnp.int32)
         keep, send = pl.pallas_call(
-            functools.partial(mix_gathered, rows),
-            grid=(4,),
+            mix_gathered,
             out_shape=(shape((half, rows, tokens), BF16),) * 2,
-            in_specs=[smem]
-            + [pl.BlockSpec((block, rows, tokens), lambda n: (n, 0, 0))] * 2
-            + [pl.BlockSpec((groups // 2, 2, block, rows, tokens), lambda n: (0, 0, n, 0, 0))],
-            out_specs=(pl.BlockSpec((block, rows, tokens), lambda n: (n, 0, 0)),) * 2,
+            in_specs=[smem] + [whole] * (2 + len(rights)),
+            out_specs=(whole,) * 2,
             compiler_params=params,
             name="mix_gathered",
         )(
-            core,
-            left.reshape(half, rows, tokens),
-            got.reshape(2 * half, rows, tokens),
-            gathered.reshape(groups // 2, 2, half, rows, tokens),
+            jnp.concatenate([core, place.reshape(1)]),
+            *(array.reshape(half, rows, tokens) for array in (left, got_left, *rights)),
         )
         merged = (core, keep.reshape(half * rows, tokens), lax.ppermute(send, "row", swap).reshape(half * rows, tokens))
     else:

time: 109 us -> 71.5 us (0.66)
  waiting for transfers between devices: 54.6 us -> 9.69 us
  starting transfers between devices: 0.55 us -> 18.6 us
  between operations: 13.4 us -> 0.05 us
  Pallas kernels: 6.5 us -> 9.28 us
  blocking collectives: 31.4 us -> 33.5 us
  local copies, waits for them, and re-layouts: 1.6 us -> 0 us
    all_gather x1 -> x0, waiting for transfers between devices: 52.1 us -> none  [on_device(): lax.all_gather(jnp.concatenate([right, got[half * rows:]], axis=0), 'row'...]
    ppermute x1 -> x16, starting transfers between devices: 0.52 us -> 18.6 us  [the longest x14 18.1 us: along(): return lax.ppermute(array, 'row', pairs)]
    ppermute x1 -> x16, waiting for transfers between devices: 1.16 us -> 8.36 us  [the longest x14 8.35 us: along(): return lax.ppermute(array, 'row', pairs)]
    pallas_call x1, Pallas kernels: 1.69 us -> 3.95 us  [on_device(): pl.pallas_call(mix_gathered, out_shape=(shape((half, rows, tokens), BF16)...]
    all_to_all x2, blocking collectives: 31.4 us -> 33.5 us  [exchange(): return lax.all_to_all(array, 'row', split_axis=0, concat_axis=0, tiled=True)]
    unnamed x2 -> x0, local copies, waits for them, and re-layouts: 1.59 us -> none
  transfers between devices with their start and end apart: 3 -> 17, of which waited for: 3 -> 9; matrix products, arithmetic and copies ran while one was open for 0% -> 0% of each run, Pallas kernels for 0% -> 0%
where the time goes in v16:
time: 71.5 us; the launch traced here: 71.3 us
  blocking collectives  33.5 us (47%)
  starting transfers between devices  18.6 us (26%)
  waiting for transfers between devices  9.69 us (14%)
  Pallas kernels  9.28 us (13%)
    all_to_all x2, blocking collectives, exchange(): return lax.all_to_all(array, 'row', split_axis=0, concat_axis=0, tiled=True)  33.5 us
    ppermute x14, starting transfers between devices, along(): return lax.ppermute(array, 'row', pairs)  18.1 us
    ppermute x14, waiting for transfers between devices, along(): return lax.ppermute(array, 'row', pairs)  8.35 us
    pallas_call x1, Pallas kernels, on_device(): pl.pallas_call(mix_gathered, out_shape=(shape((half, rows, tokens), BF16)...  3.95 us
    pallas_call x1, Pallas kernels, on_device(): pl.pallas_call(functools.partial(project_kernel, half if by_core else per...  2.52 us
  transfers between devices with their start and end apart: 17, of which 9 were waited for; matrix products, arithmetic and copies ran while one was open for 0% of the time, Pallas kernels for 0%

profile of v16, /device:TPU:0, one launch (start us, length us, event | category | flops | bytes accessed | tf_op | source)
XLA Modules:
  0.0 71.3 jit_solution(14740273272532095679)
XLA Ops:
  0.0 2.5 %project.1 = (bf16[512,128]{1,0:T(8,128)(2,1)S(1)}, bf16[512,128]{1,0:T(8,128)(2,1)S(1)}, bf16[512,128]{1,0:T(8,128)(2,1)}, bf16[512,128]{1,0:T(8,128)(2,1)S(1)}...) custom-call(s32[1]{0:T(128)} %bitcast.refs_0_, ...), custom_call_target="tpu_custom_call" | custom-call | tf_op jit(solution)/shard_map/project/pallas_call | solution.py:309
  2.5 0.5 collective-permute-start.1
  3.0 2.6 %collective-permute-start.2 = (bf16[512,128]{1,0:T(8,128)(2,1)S(1)}, bf16[512,128]{1,0:T(8,128)(2,1)S(1)}, u32[]{:S(2)}, u32[]{:S(2)}) collective-permute-start(bf16[512,128]{1,0:T(8,128)(2,1)S(1)} %get-tuple-element.22), channel_id=1, source_target_pairs={{0,4},{1,5},{4,8},{5,9},{8,12},{9,13},{12,14},{13,15},{14,10},{15,... | collective-permute-start | bytes 393224 | tf_op jit(solution)/shard_map/ppermute | solution.py:335
  5.7 0.0 collective-permute-done.1
  5.7 1.2 %collective-permute-start.9 = (bf16[512,128]{1,0:T(8,128)(2,1)S(1)}, bf16[512,128]{1,0:T(8,128)(2,1)S(1)}, u32[]{:S(2)}, u32[]{:S(2)}) collective-permute-start(bf16[512,128]{1,0:T(8,128)(2,1)S(1)} %collective-permute-done.1), channel_id=1, source_target_pairs={{0,2},{1,3},{4,0},{5,1},{8,4},{9,5},{12,8},{13,9},{14,12},{15,13},... | collective-permute-start | bytes 393224 | tf_op jit(solution)/shard_map/ppermute | solution.py:335
  6.9 1.6 %collective-permute-start.13 = (bf16[512,128]{1,0:T(8,128)(2,1)S(1)}, bf16[512,128]{1,0:T(8,128)(2,1)S(1)}, u32[]{:S(2)}, u32[]{:S(2)}) collective-permute-start(bf16[512,128]{1,0:T(8,128)(2,1)S(1)} %get-tuple-element.22), channel_id=1, source_target_pairs={{0,2},{1,3},{4,0},{5,1},{8,4},{9,5},{12,8},{13,9},{14,12},{15,13},... | collective-permute-start | bytes 393224 | tf_op jit(solution)/shard_map/ppermute | solution.py:335
  8.5 0.4 collective-permute-start.3
  8.9 0.8 %collective-permute-done.2 = bf16[512,128]{1,0:T(8,128)(2,1)S(1)} collective-permute-done((bf16[512,128]{1,0:T(8,128)(2,1)S(1)}, bf16[512,128]{1,0:T(8,128)(2,1)S(1)}, u32[]{:S(2)}, u32[]{:S(2)}) %collective-permute-start.2) | collective-permute-done | bytes 131104 | tf_op jit(solution)/shard_map/ppermute | solution.py:335
  9.7 2.1 %collective-permute-start.4 = (bf16[512,128]{1,0:T(8,128)(2,1)S(1)}, bf16[512,128]{1,0:T(8,128)(2,1)S(1)}, u32[]{:S(2)}, u32[]{:S(2)}) collective-permute-start(bf16[512,128]{1,0:T(8,128)(2,1)S(1)} %collective-permute-done.2), channel_id=1, source_target_pairs={{0,4},{1,5},{4,8},{5,9},{8,12},{9,13},{12,14},{13,15},{14,10},{15,... | collective-permute-start | bytes 393224 | tf_op jit(solution)/shard_map/ppermute | solution.py:335
  11.9 0.2 collective-permute-done.9
  12.0 1.2 %collective-permute-start.10 = (bf16[512,128]{1,0:T(8,128)(2,1)S(1)}, bf16[512,128]{1,0:T(8,128)(2,1)S(1)}, u32[]{:S(2)}, u32[]{:S(2)}) collective-permute-start(bf16[512,128]{1,0:T(8,128)(2,1)S(1)} %collective-permute-done.9), channel_id=1, source_target_pairs={{0,2},{1,3},{4,0},{5,1},{8,4},{9,5},{12,8},{13,9},{14,12},{15,13},... | collective-permute-start | bytes 393224 | tf_op jit(solution)/shard_map/ppermute | solution.py:335
  13.2 1.3 %collective-permute-done.13 = bf16[512,128]{1,0:T(8,128)(2,1)S(1)} collective-permute-done((bf16[512,128]{1,0:T(8,128)(2,1)S(1)}, bf16[512,128]{1,0:T(8,128)(2,1)S(1)}, u32[]{:S(2)}, u32[]{:S(2)}) %collective-permute-start.13) | collective-permute-done | bytes 131104 | tf_op jit(solution)/shard_map/ppermute | solution.py:335
  14.5 1.5 %collective-permute-start.14 = (bf16[512,128]{1,0:T(8,128)(2,1)S(1)}, bf16[512,128]{1,0:T(8,128)(2,1)S(1)}, u32[]{:S(2)}, u32[]{:S(2)}) collective-permute-start(bf16[512,128]{1,0:T(8,128)(2,1)S(1)} %collective-permute-done.13), channel_id=1, source_target_pairs={{0,2},{1,3},{4,0},{5,1},{8,4},{9,5},{12,8},{13,9},{14,12},{15,13},... | collective-permute-start | bytes 393224 | tf_op jit(solution)/shard_map/ppermute | solution.py:335
  16.1 0.0 collective-permute-done.3
  16.1 0.5 collective-permute-start.5
  16.6 0.0 collective-permute-done.4
  16.6 1.6 %collective-permute-start.6 = (bf16[512,128]{1,0:T(8,128)(2,1)S(1)}, bf16[512,128]{1,0:T(8,128)(2,1)S(1)}, u32[]{:S(2)}, u32[]{:S(2)}) collective-permute-start(bf16[512,128]{1,0:T(8,128)(2,1)S(1)} %collective-permute-done.4), channel_id=1, source_target_pairs={{0,4},{1,5},{4,8},{5,9},{8,12},{9,13},{12,14},{13,15},{14,10},{15,... | collective-permute-start | bytes 393224 | tf_op jit(solution)/shard_map/ppermute | solution.py:335
  18.2 0.0 collective-permute-done.10
  18.2 1.2 %collective-permute-start.11 = (bf16[512,128]{1,0:T(8,128)(2,1)S(1)}, bf16[512,128]{1,0:T(8,128)(2,1)S(1)}, u32[]{:S(2)}, u32[]{:S(2)}) collective-permute-start(bf16[512,128]{1,0:T(8,128)(2,1)S(1)} %collective-permute-done.10), channel_id=1, source_target_pairs={{0,2},{1,3},{4,0},{5,1},{8,4},{9,5},{12,8},{13,9},{14,12},{15,13},... | collective-permute-start | bytes 393224 | tf_op jit(solution)/shard_map/ppermute | solution.py:335
  19.3 0.0 collective-permute-start
  19.3 1.5 %collective-permute-done.14 = bf16[512,128]{1,0:T(8,128)(2,1)S(1)} collective-permute-done((bf16[512,128]{1,0:T(8,128)(2,1)S(1)}, bf16[512,128]{1,0:T(8,128)(2,1)S(1)}, u32[]{:S(2)}, u32[]{:S(2)}) %collective-permute-start.14) | collective-permute-done | bytes 131104 | tf_op jit(solution)/shard_map/ppermute | solution.py:335
  20.9 1.5 %collective-permute-start.15 = (bf16[512,128]{1,0:T(8,128)(2,1)S(1)}, bf16[512,128]{1,0:T(8,128)(2,1)S(1)}, u32[]{:S(2)}, u32[]{:S(2)}) collective-permute-start(bf16[512,128]{1,0:T(8,128)(2,1)S(1)} %collective-permute-done.14), channel_id=1, source_target_pairs={{0,2},{1,3},{4,0},{5,1},{8,4},{9,5},{12,8},{13,9},{14,12},{15,13},... | collective-permute-start | bytes 393224 | tf_op jit(solution)/shard_map/ppermute | solution.py:335
  22.4 0.0 collective-permute-done.5
  22.4 0.5 collective-permute-start.7
  22.9 0.0 collective-permute-done.6
  22.9 1.6 %collective-permute-start.8 = (bf16[512,128]{1,0:T(8,128)(2,1)S(1)}, bf16[512,128]{1,0:T(8,128)(2,1)}, u32[]{:S(2)}, u32[]{:S(2)}) collective-permute-start(bf16[512,128]{1,0:T(8,128)(2,1)S(1)} %collective-permute-done.6), channel_id=1, source_target_pairs={{0,4},{1,5},{4,8},{5,9},{8,12},{9,13},{12,14},{13,15},{14,10},{15,... | collective-permute-start | bytes 393224 | tf_op jit(solution)/shard_map/ppermute | solution.py:335
  24.5 0.0 collective-permute-done.11
  24.5 0.5 collective-permute-start.12
  25.0 0.1 pad_add_fusion.place_ref
  25.0 0.0 collective-permute-done
  25.0 2.3 %collective-permute-done.15 = bf16[512,128]{1,0:T(8,128)(2,1)S(1)} collective-permute-done((bf16[512,128]{1,0:T(8,128)(2,1)S(1)}, bf16[512,128]{1,0:T(8,128)(2,1)S(1)}, u32[]{:S(2)}, u32[]{:S(2)}) %collective-permute-start.15) | collective-permute-done | bytes 131104 | tf_op jit(solution)/shard_map/ppermute | solution.py:335
  27.3 0.6 collective-permute-done.7
  28.0 1.5 %collective-permute-done.8 = bf16[512,128]{1,0:T(8,128)(2,1)} collective-permute-done((bf16[512,128]{1,0:T(8,128)(2,1)S(1)}, bf16[512,128]{1,0:T(8,128)(2,1)}, u32[]{:S(2)}, u32[]{:S(2)}) %collective-permute-start.8) | collective-permute-done | bytes 131104 | tf_op jit(solution)/shard_map/ppermute | solution.py:335
  29.5 0.1 collective-permute-done.12
  29.6 4.0 %mix_gathered.1 = (bf16[64,8,128]{2,1,0:T(8,128)(2,1)S(1)}, bf16[64,8,128]{2,1,0:T(8,128)(2,1)S(1)}) custom-call(s32[2]{0:T(128)S(1)} %pad_add_fusion.place_ref, bf16[64,8,128]{2,1,0:T(8,128)(2,1)S(1)} %bitcast.26, bf16[64,8,128]{2,1,0:T(8,128)(2,1)S(1)} %bitcast.39, bf16[64,8,128]{2,1,0:T(8,128)(2,1)S(1)} %bitcast.27, bf16[64,8,128]{2,1,0:T(8,128)(2,1)S(1)} %bitcast.28, ...), custom_call_target="tpu_custom_call" | custom-call | tf_op jit(solution)/shard_map/mix_gathered/pallas_call | solution.py:356
  33.5 0.0 collective-permute-start.16
  33.6 1.3 %collective-permute-done.16 = bf16[64,8,128]{2,1,0:T(8,128)(2,1)S(1)} collective-permute-done((bf16[64,8,128]{2,1,0:T(8,128)(2,1)S(1)}, bf16[64,8,128]{2,1,0:T(8,128)(2,1)S(1)}, u32[]{:S(2)}, u32[]{:S(2)}) %collective-permute-start.16) | collective-permute-done | bytes 131104 | tf_op jit(solution)/shard_map/ppermute | solution.py:367
  34.9 1.4 %finish_project.1 = (bf16[2048,128]{1,0:T(8,128)(2,1)S(1)}, bf16[128,1024]{1,0:T(8,128)(2,1)S(1)}, bf16[128,1024]{1,0:T(8,128)(2,1)S(1)}) custom-call(s32[1]{0:T(128)} %bitcast.refs_0_, bf16[512,128]{1,0:T(8,128)(2,1)S(1)} %bitcast.42, bf16[512,128]{1,0:T(8,128)(2,1)S(1)} %bitcast.43, bf16[128,1024]{1,0:T(8,128)(2,1)S(1)} %get-tuple-element.26.refs_3_, ...), custom_call_target="tpu_custom_call" | custom-call | tf_op jit(solution)/shard_map/finish_project/pallas_call | solution.py:370
  36.3 19.6 %all_to_all.17.both_ref = bf16[16,128,128]{2,1,0:T(8,128)(2,1)S(1)} all-to-all(bf16[16,128,128]{2,1,0:T(8,128)(2,1)S(1)} %bitcast.25), channel_id=1, replica_groups=mesh['groups'=2,'row'=16] {'row'}, dimensions={0} | all-to-all | bytes 1048576 | tf_op jit(solution)/shard_map/all_to_all | solution.py:290
  55.8 0.3 mix.1
  56.1 13.9 %all_to_all.18 = bf16[16,64,128]{2,1,0:T(8,128)(2,1)S(1)} all-to-all(bf16[16,64,128]{2,1,0:T(8,128)(2,1)S(1)} %mix.1), channel_id=1, replica_groups=mesh['groups'=2,'row'=16] {'row'}, dimensions={0} | all-to-all | bytes 524288 | tf_op jit(solution)/shard_map/all_to_all | solution.py:290
  70.1 1.2 %finish.1 = bf16[8,128,128]{2,1,0:T(8,128)(2,1)} custom-call(bf16[1024,128]{1,0:T(8,128)(2,1)S(1)} %bitcast.24, bf16[128,1024]{1,0:T(8,128)(2,1)S(1)} %get-tuple-element.33.middle_t_ref, bf16[128,1024]{1,0:T(8,128)(2,1)S(1)} %get-tuple-element.34.gate_t_ref, f32[8,128,128]{2,1,0:T(8,128)S(1)} %get-tuple-element.29.refs_6_.columns_ref, ...), custom_call_target="tpu_custom_call" | custom-call | tf_op jit(solution)/shard_map/finish/pallas_call | solution.py:380
Async XLA Ops:
  2.5 3.2 %collective-permute-start.1 = (bf16[512,128]{1,0:T(8,128)(2,1)S(1)}, bf16[512,128]{1,0:T(8,128)(2,1)S(1)}, u32[]{:S(2)}, u32[]{:S(2)}) collective-permute-start(bf16[512,128]{1,0:T(8,128)(2,1)S(1)} %get-tuple-element.23), channel_id=1, source_target_pairs={{0,1},{1,0},{2,3},{3,2},{4,5},{5,4},{6,7},{7,6},{8,9},{9,8},{10,11... | collective-permute-start | bytes 393224 | tf_op jit(solution)/shard_map/ppermute | solution.py:344
  3.0 6.7 %collective-permute-start.2 = (bf16[512,128]{1,0:T(8,128)(2,1)S(1)}, bf16[512,128]{1,0:T(8,128)(2,1)S(1)}, u32[]{:S(2)}, u32[]{:S(2)}) collective-permute-start(bf16[512,128]{1,0:T(8,128)(2,1)S(1)} %get-tuple-element.22), channel_id=1, source_target_pairs={{0,4},{1,5},{4,8},{5,9},{8,12},{9,13},{12,14},{13,15},{14,10},{15,... | collective-permute-start | bytes 393224 | tf_op jit(solution)/shard_map/ppermute | solution.py:335
  5.7 6.3 %collective-permute-start.9 = (bf16[512,128]{1,0:T(8,128)(2,1)S(1)}, bf16[512,128]{1,0:T(8,128)(2,1)S(1)}, u32[]{:S(2)}, u32[]{:S(2)}) collective-permute-start(bf16[512,128]{1,0:T(8,128)(2,1)S(1)} %collective-permute-done.1), channel_id=1, source_target_pairs={{0,2},{1,3},{4,0},{5,1},{8,4},{9,5},{12,8},{13,9},{14,12},{15,13},... | collective-permute-start | bytes 393224 | tf_op jit(solution)/shard_map/ppermute | solution.py:335
  6.9 7.6 %collective-permute-start.13 = (bf16[512,128]{1,0:T(8,128)(2,1)S(1)}, bf16[512,128]{1,0:T(8,128)(2,1)S(1)}, u32[]{:S(2)}, u32[]{:S(2)}) collective-permute-start(bf16[512,128]{1,0:T(8,128)(2,1)S(1)} %get-tuple-element.22), channel_id=1, source_target_pairs={{0,2},{1,3},{4,0},{5,1},{8,4},{9,5},{12,8},{13,9},{14,12},{15,13},... | collective-permute-start | bytes 393224 | tf_op jit(solution)/shard_map/ppermute | solution.py:335
  8.5 7.6 %collective-permute-start.3 = (bf16[512,128]{1,0:T(8,128)(2,1)S(1)}, bf16[512,128]{1,0:T(8,128)(2,1)S(1)}, u32[]{:S(2)}, u32[]{:S(2)}) collective-permute-start(bf16[512,128]{1,0:T(8,128)(2,1)S(1)} %collective-permute-done.1), channel_id=1, source_target_pairs={{0,4},{1,5},{4,8},{5,9},{8,12},{9,13},{12,14},{13,15},{14,10},{15,... | collective-permute-start | bytes 393224 | tf_op jit(solution)/shard_map/ppermute | solution.py:335
  9.7 6.9 %collective-permute-start.4 = (bf16[512,128]{1,0:T(8,128)(2,1)S(1)}, bf16[512,128]{1,0:T(8,128)(2,1)S(1)}, u32[]{:S(2)}, u32[]{:S(2)}) collective-permute-start(bf16[512,128]{1,0:T(8,128)(2,1)S(1)} %collective-permute-done.2), channel_id=1, source_target_pairs={{0,4},{1,5},{4,8},{5,9},{8,12},{9,13},{12,14},{13,15},{14,10},{15,... | collective-permute-start | bytes 393224 | tf_op jit(solution)/shard_map/ppermute | solution.py:335
  12.0 6.1 %collective-permute-start.10 = (bf16[512,128]{1,0:T(8,128)(2,1)S(1)}, bf16[512,128]{1,0:T(8,128)(2,1)S(1)}, u32[]{:S(2)}, u32[]{:S(2)}) collective-permute-start(bf16[512,128]{1,0:T(8,128)(2,1)S(1)} %collective-permute-done.9), channel_id=1, source_target_pairs={{0,2},{1,3},{4,0},{5,1},{8,4},{9,5},{12,8},{13,9},{14,12},{15,13},... | collective-permute-start | bytes 393224 | tf_op jit(solution)/shard_map/ppermute | solution.py:335
  14.5 6.3 %collective-permute-start.14 = (bf16[512,128]{1,0:T(8,128)(2,1)S(1)}, bf16[512,128]{1,0:T(8,128)(2,1)S(1)}, u32[]{:S(2)}, u32[]{:S(2)}) collective-permute-start(bf16[512,128]{1,0:T(8,128)(2,1)S(1)} %collective-permute-done.13), channel_id=1, source_target_pairs={{0,2},{1,3},{4,0},{5,1},{8,4},{9,5},{12,8},{13,9},{14,12},{15,13},... | collective-permute-start | bytes 393224 | tf_op jit(solution)/shard_map/ppermute | solution.py:335
  16.1 6.4 %collective-permute-start.5 = (bf16[512,128]{1,0:T(8,128)(2,1)S(1)}, bf16[512,128]{1,0:T(8,128)(2,1)S(1)}, u32[]{:S(2)}, u32[]{:S(2)}) collective-permute-start(bf16[512,128]{1,0:T(8,128)(2,1)S(1)} %collective-permute-done.3), channel_id=1, source_target_pairs={{0,4},{1,5},{4,8},{5,9},{8,12},{9,13},{12,14},{13,15},{14,10},{15,... | collective-permute-start | bytes 393224 | tf_op jit(solution)/shard_map/ppermute | solution.py:335
  16.6 6.3 %collective-permute-start.6 = (bf16[512,128]{1,0:T(8,128)(2,1)S(1)}, bf16[512,128]{1,0:T(8,128)(2,1)S(1)}, u32[]{:S(2)}, u32[]{:S(2)}) collective-permute-start(bf16[512,128]{1,0:T(8,128)(2,1)S(1)} %collective-permute-done.4), channel_id=1, source_target_pairs={{0,4},{1,5},{4,8},{5,9},{8,12},{9,13},{12,14},{13,15},{14,10},{15,... | collective-permute-start | bytes 393224 | tf_op jit(solution)/shard_map/ppermute | solution.py:335
  18.2 6.3 %collective-permute-start.11 = (bf16[512,128]{1,0:T(8,128)(2,1)S(1)}, bf16[512,128]{1,0:T(8,128)(2,1)S(1)}, u32[]{:S(2)}, u32[]{:S(2)}) collective-permute-start(bf16[512,128]{1,0:T(8,128)(2,1)S(1)} %collective-permute-done.10), channel_id=1, source_target_pairs={{0,2},{1,3},{4,0},{5,1},{8,4},{9,5},{12,8},{13,9},{14,12},{15,13},... | collective-permute-start | bytes 393224 | tf_op jit(solution)/shard_map/ppermute | solution.py:335
  19.3 5.7 %collective-permute-start = (bf16[512,128]{1,0:T(8,128)(2,1)}, bf16[512,128]{1,0:T(8,128)(2,1)S(1)}, u32[]{:S(2)}, u32[]{:S(2)}) collective-permute-start(bf16[512,128]{1,0:T(8,128)(2,1)} %get-tuple-element.21), channel_id=1, source_target_pairs={{0,1},{1,0},{2,3},{3,2},{4,5},{5,4},{6,7},{7,6},{8,9},{9,8},{10,11... | collective-permute-start | bytes 393224 | tf_op jit(solution)/shard_map/ppermute | solution.py:345
  20.9 6.4 %collective-permute-start.15 = (bf16[512,128]{1,0:T(8,128)(2,1)S(1)}, bf16[512,128]{1,0:T(8,128)(2,1)S(1)}, u32[]{:S(2)}, u32[]{:S(2)}) collective-permute-start(bf16[512,128]{1,0:T(8,128)(2,1)S(1)} %collective-permute-done.14), channel_id=1, source_target_pairs={{0,2},{1,3},{4,0},{5,1},{8,4},{9,5},{12,8},{13,9},{14,12},{15,13},... | collective-permute-start | bytes 393224 | tf_op jit(solution)/shard_map/ppermute | solution.py:335
  22.4 5.5 %collective-permute-start.7 = (bf16[512,128]{1,0:T(8,128)(2,1)S(1)}, bf16[512,128]{1,0:T(8,128)(2,1)S(1)}, u32[]{:S(2)}, u32[]{:S(2)}) collective-permute-start(bf16[512,128]{1,0:T(8,128)(2,1)S(1)} %collective-permute-done.5), channel_id=1, source_target_pairs={{0,4},{1,5},{4,8},{5,9},{8,12},{9,13},{12,14},{13,15},{14,10},{15,... | collective-permute-start | bytes 393224 | tf_op jit(solution)/shard_map/ppermute | solution.py:335
  22.9 6.5 %collective-permute-start.8 = (bf16[512,128]{1,0:T(8,128)(2,1)S(1)}, bf16[512,128]{1,0:T(8,128)(2,1)}, u32[]{:S(2)}, u32[]{:S(2)}) collective-permute-start(bf16[512,128]{1,0:T(8,128)(2,1)S(1)} %collective-permute-done.6), channel_id=1, source_target_pairs={{0,4},{1,5},{4,8},{5,9},{8,12},{9,13},{12,14},{13,15},{14,10},{15,... | collective-permute-start | bytes 393224 | tf_op jit(solution)/shard_map/ppermute | solution.py:335
  24.5 5.1 %collective-permute-start.12 = (bf16[512,128]{1,0:T(8,128)(2,1)S(1)}, bf16[512,128]{1,0:T(8,128)(2,1)}, u32[]{:S(2)}, u32[]{:S(2)}) collective-permute-start(bf16[512,128]{1,0:T(8,128)(2,1)S(1)} %collective-permute-done.11), channel_id=1, source_target_pairs={{0,2},{1,3},{4,0},{5,1},{8,4},{9,5},{12,8},{13,9},{14,12},{15,13},... | collective-permute-start | bytes 393224 | tf_op jit(solution)/shard_map/ppermute | solution.py:335
  33.5 1.4 %collective-permute-start.16 = (bf16[64,8,128]{2,1,0:T(8,128)(2,1)S(1)}, bf16[64,8,128]{2,1,0:T(8,128)(2,1)S(1)}, u32[]{:S(2)}, u32[]{:S(2)}) collective-permute-start(bf16[64,8,128]{2,1,0:T(8,128)(2,1)S(1)} %get-tuple-element.25), channel_id=1, source_target_pairs={{0,1},{1,0},{2,3},{3,2},{4,5},{5,4},{6,7},{7,6},{8,9},{9,8},{10,11... | collective-permute-start | bytes 393224 | tf_op jit(solution)/shard_map/ppermute | solution.py:367

commit v17 on v16

--- a/solution.py
+++ b/solution.py
@@ -52,41 +52,26 @@
         gated = (jnp.tanh(gate) + 1.0) * (value * half_mask)
         for h, r in enumerate(chunk):
             for g in range(channels // per_group):
-                where = pl.ds((2 * g + side) * per_group * (rows + 1) + r, per_group, stride=rows + 1)
+                where = pl.ds((2 * g + side) * per_group * rows + r, per_group, stride=rows)
                 for t in range(tokens // LANES):
                     first = h * tokens + t * LANES
                     panels[t, where, :] = gated[g * per_group : (g + 1) * per_group, first : first + LANES]
     return (0.5 * jnp.tanh(products[4 * channels :]) + 0.5).astype(BF16)
 
 
-def pack_panels(panels, both_ref, rows):
+def pack_panels(panels, both_ref):
     for t in range(both_ref.shape[1] // LANES):
-        for first in range(0, both_ref.shape[0] // rows, 16):
-            parts = [panels[t, pl.ds(c * (rows + 1), rows), :] for c in range(first, first + 16)]
-            packed = jnp.concatenate(parts, axis=0).astype(BF16)
-            both_ref[first * rows : (first + 16) * rows, t * LANES : (t + 1) * LANES] = packed
-
-
-def split_panels(panels, core_ref, left_ref, right_ref, other_left_ref, other_right_ref, rows):
+        both_ref[:, t * LANES : (t + 1) * LANES] = panels[t].astype(BF16)
+
+
+def split_panels(panels, core_ref, left_ref, right_ref, other_left_ref, other_right_ref):
     size = left_ref.shape[0]
+    core = core_ref[0]
     for t in range(left_ref.shape[1] // LANES):
-        for first in range(0, size // rows, 16):
-            first_core = jnp.full((16 * rows, LANES), core_ref[0]) == 0
-            for side, (own_ref, other_ref) in enumerate(((left_ref, other_left_ref), (right_ref, other_right_ref))):
-                mine, others = [
-                    jnp.concatenate(
-                        [
-                            panels[t, pl.ds(((2 * g + side) * (size // rows) + c) * (rows + 1), rows), :]
-                            for c in range(first, first + 16)
-                        ],
-                        axis=0,
-                    )
-                    for g in range(2)
-                ]
-                lane = slice(t * LANES, (t + 1) * LANES)
-                part = slice(first * rows, (first + 16) * rows)
-                own_ref[part, lane] = jnp.where(first_core, mine, others).astype(BF16)
-                other_ref[part, lane] = jnp.where(first_core, others, mine).astype(BF16)
+        for side, (own_ref, other_ref) in enumerate(((left_ref, other_left_ref), (right_ref, other_right_ref))):
+            for group, ref in ((core, own_ref), (1 - core, other_ref)):
+                start = pl.multiple_of((2 * group + side) * size, size)
+                ref[:, t * LANES : (t + 1) * LANES] = panels[t, pl.ds(start, size), :].astype(BF16)
 
 
 def half_lanes(mask_ref, chunk):
@@ -131,9 +116,9 @@
             panels, per_group, rows, chunk, tokens, products, half_lanes(mask_ref, chunk)
         )
     if by_core:
-        split_panels(panels, core_ref, *outs, rows)
+        split_panels(panels, core_ref, *outs)
     else:
-        pack_panels(panels, both_ref, rows)
+        pack_panels(panels, both_ref)
 
 
 def mix_kernel(per_group, rows, incoming, both_ref, product_ref):
@@ -158,7 +143,8 @@
     return list(range(0, count, 2)) + list(range(count - 1, 0, -2))
 
 
-def token_order(place_ref, chips, rows, tokens):
+def token_order(place_ref, distances, rows, tokens):
+    chips = len(distances)
     shape = (tokens, tokens)
     lane, token = (lax.broadcasted_iota(jnp.int32, shape, axis) for axis in range(2))
     core, place = jnp.full(shape, place_ref[0]), jnp.full(shape, place_ref[1])
@@ -166,30 +152,40 @@
     chip, source_core = device // 2, device % 2
     source = jnp.where(chip % 2 == 0, chip // 2, chips - 1 - chip // 2)
     distance = (place - source + chips) % chips
-    slot = 2 * distance + jnp.where(source_core == core, 0, 1)
+    place_of = sum(jnp.where(distance == d, n, 0) for n, d in enumerate(distances))
+    slot = 2 * place_of + jnp.where(source_core == core, 0, 1)
     return jnp.where(lane == slot * rows + token % rows, 1.0, 0.0).astype(BF16)
 
 
-def mix_gathered(place_ref, own_ref, got_ref, *refs):
+def gathered_sums(own_ref, got_ref, rights, first_lane, c):
+    _, rows, tokens = own_ref.shape
+    left = jnp.concatenate([own_ref[c].astype(F32), got_ref[c].astype(F32)], axis=0).astype(BF16)
+    blocks = [ref[c].astype(F32) for ref in rights]
+    last = first_lane + len(blocks) * rows
+    empty = [jnp.zeros((n, tokens), F32) for n in (first_lane, tokens - last)]
+    blocks = [block for block in (empty[0], *blocks, empty[1]) if block.shape[0]]
+    return dot(left, jnp.concatenate(blocks, axis=0).astype(BF16), NT)
+
+
+def mix_early(own_ref, got_ref, *refs):
+    rights, early_ref = refs[:-1], refs[-1]
+    for c in range(own_ref.shape[0]):
+        early_ref[c] = gathered_sums(own_ref, got_ref, rights, 0, c).astype(BF16)
+
+
+def mix_late(distances, early, place_ref, own_ref, got_ref, early_ref, *refs):
     rights, (keep_ref, send_ref) = refs[:-2], refs[-2:]
     count, rows, tokens = own_ref.shape
-    order = token_order(place_ref, len(rights) // 2, rows, tokens)
+    order = token_order(place_ref, distances, rows, tokens)
     group = 8
-
-    def body(n, carry):
-        part = pl.ds(n * group, group)
-        lefts = jnp.concatenate([own_ref[part].astype(F32), got_ref[part].astype(F32)], axis=1).astype(BF16)
-        blocks = [ref[part].astype(F32) for ref in rights]
-        sums = []
-        for c in range(group):
-            right = jnp.concatenate([block[c] for block in blocks], axis=0).astype(BF16)
-            sums.append(dot(lefts[c], right, NT).astype(BF16))
+    for first in range(0, count, group):
+        sums = [
+            (gathered_sums(own_ref, got_ref, rights, early * rows, c) + early_ref[c].astype(F32)).astype(BF16)
+            for c in range(first, first + group)
+        ]
         sums = dot(jnp.concatenate(sums, axis=0), order, NN).reshape(group, 2 * rows, tokens)
-        keep_ref[part] = sums[:, :rows].astype(BF16)
-        send_ref[part] = sums[:, rows:].astype(BF16)
-        return carry
-
-    lax.fori_loop(0, count // group, body, 0)
+        keep_ref[first : first + group] = sums[:, :rows].astype(BF16)
+        send_ref[first : first + group] = sums[:, rows:].astype(BF16)
 
 
 def finish_rows(emit, rows, channels, tokens, load, pair_t_ref, gate_t_ref, gain, bias, outw_t, unit_scratch):
@@ -203,14 +199,12 @@
     spread = sum(jnp.sum(jnp.square(sums(part) - average), axis=0) for part in parts) * (1.0 / channels)
     inverse = lax.rsqrt(spread + 1e-05)
     for part in parts:
-        units = (sums(part) - average) * inverse
+        units = ((sums(part) - average) * inverse).reshape(16 * rows, tokens)
         for t in tiles:
-            for n in range(16):
-                where = pl.ds((part.start // rows + n) * (rows + 1), rows)
-                unit_scratch[t, where, :] = units[n, :, t * LANES : (t + 1) * LANES]
+            unit_scratch[t, part, :] = units[:, t * LANES : (t + 1) * LANES]
     for chunk in chunks(rows, tokens, 256):
         part = span(chunk, tokens)
-        units = lanes([unit_scratch[t, pl.ds(r, channels, stride=rows + 1), :] for r in chunk for t in tiles])
+        units = lanes([unit_scratch[t, pl.ds(r, channels, stride=rows), :] for r in chunk for t in tiles])
         normed = affine(units, gain, bias, tokens)
         change = gate_t_ref[:, part].astype(F32) * dot(outw_t, normed, NN)
         emit(chunk, part, (pair_t_ref[:, part].astype(F32) + change).astype(BF16))
@@ -250,7 +244,7 @@
         emit, rows, pair_t_ref.shape[0], tokens, load, pair_t_ref, gate_t_ref, columns_ref[2], columns_ref[3],
         outw_t_ref[0], unit_scratch,
     )
-    pack_panels(panels, both_ref, rows)
+    pack_panels(panels, both_ref)
 
 
 def finish_kernel(
@@ -283,8 +277,8 @@
     shape = jax.ShapeDtypeStruct
     both_shape = shape((2 * channels * rows, tokens), BF16)
     flat_shape = shape((channels, rows * tokens), BF16)
-    panels = pltpu.VMEM((tokens // LANES, 2 * channels * (rows + 1), LANES), F32)
-    unit_scratch = pltpu.VMEM((tokens // LANES, channels * (rows + 1), LANES), F32)
+    panels = pltpu.VMEM((tokens // LANES, 2 * channels * rows, LANES), F32)
+    unit_scratch = pltpu.VMEM((tokens // LANES, channels * rows, LANES), F32)
 
     def exchange(array):
         return lax.all_to_all(array, "row", split_axis=0, concat_axis=0, tiled=True)
@@ -346,24 +340,32 @@
         middle = chips // 2
         ups = [rounds(right, 1, middle), rounds(got_right, 1, middle - 1)]
         downs = [rounds(right, -1, middle - 1), rounds(got_right, -1, middle)]
+        distances = sorted(range(chips), key=lambda d: min(d, chips - d))
+        early = 2 * (chips // 2 + 1)
         rights = [
-            ups[piece][distance] if distance < len(ups[piece]) else downs[piece][chips - distance]
-            for distance in range(chips)
-            for piece in range(2)
+            ups[piece][d] if d < len(ups[piece]) else downs[piece][chips - d] for d in distances for piece in range(2)
         ]
+        rights = [array.reshape(half, rows, tokens) for array in rights]
+        lefts = [array.reshape(half, rows, tokens) for array in (left, got_left)]
         chip = lax.axis_index("row") // 2
         place = jnp.where(chip % 2 == 0, chip // 2, chips - 1 - chip // 2).astype(jnp.int32)
+        first_sums = pl.pallas_call(
+            mix_early,
+            out_shape=shape((half, 2 * rows, tokens), BF16),
+            in_specs=[whole] * (2 + early),
+            out_specs=whole,
+            compiler_params=params,
+            cost_estimate=pl.CostEstimate(flops=10**9, bytes_accessed=4 * 2**20, transcendentals=0),
+            name="mix_early",
+        )(*lefts, *rights[:early])
         keep, send = pl.pallas_call(
-            mix_gathered,
+            functools.partial(mix_late, distances, early),
             out_shape=(shape((half, rows, tokens), BF16),) * 2,
-            in_specs=[smem] + [whole] * (2 + len(rights)),
+            in_specs=[smem] + [whole] * (3 + len(rights) - early),
             out_specs=(whole,) * 2,
             compiler_params=params,
-            name="mix_gathered",
-        )(
-            jnp.concatenate([core, place.reshape(1)]),
-            *(array.reshape(half, rows, tokens) for array in (left, got_left, *rights)),
-        )
+            name="mix_late",
+        )(jnp.concatenate([core, place.reshape(1)]), *lefts, first_sums, *rights[early:])
         merged = (core, keep.reshape(half * rows, tokens), lax.ppermute(send, "row", swap).reshape(half * rows, tokens))
     else:
         merged = (exchange(mix(exchange(results[0]), False)),)

time: 71.5 us -> 69.4 us (0.971)
  Pallas kernels: 9.28 us -> 8.08 us
  waiting for transfers between devices: 9.69 us -> 8.81 us
    ppermute x14, waiting for transfers between devices: 8.35 us -> 7.47 us  [along(): return lax.ppermute(array, 'row', pairs)]
    pallas_call x1 -> x2, Pallas kernels: 3.95 us -> 3.22 us  [the longest x1 2.45 us: on_device(): pl.pallas_call(functools.partial(mix_late, distances, early), out_shape=(...]
  transfers between devices with their start and end apart: 17 -> 17, of which waited for: 9 -> 9; matrix products, arithmetic and copies ran while one was open for 0% -> 0% of each run, Pallas kernels for 0% -> 1%
where the time goes in v17:
time: 69.4 us; the launch traced here: 69.2 us
  blocking collectives  33.5 us (48%)
  starting transfers between devices  18.6 us (27%)
  waiting for transfers between devices  8.81 us (13%)
  Pallas kernels  8.08 us (12%)
    all_to_all x2, blocking collectives, exchange(): return lax.all_to_all(array, 'row', split_axis=0, concat_axis=0, tiled=True)  33.5 us
    ppermute x14, starting transfers between devices, along(): return lax.ppermute(array, 'row', pairs)  18.1 us
    ppermute x14, waiting for transfers between devices, along(): return lax.ppermute(array, 'row', pairs)  7.47 us
    pallas_call x1, Pallas kernels, on_device(): pl.pallas_call(functools.partial(mix_late, distances, early), out_shape=(...  2.45 us
    pallas_call x1, Pallas kernels, on_device(): pl.pallas_call(functools.partial(project_kernel, half if by_core else per...  2 us
  transfers between devices with their start and end apart: 17, of which 9 were waited for; matrix products, arithmetic and copies ran while one was open for 0% of the time, Pallas kernels for 1%

profile of v17, /device:TPU:0, one launch (start us, length us, event | category | flops | bytes accessed | tf_op | source)
XLA Modules:
  0.0 69.2 jit_solution(12935927438106871216)
XLA Ops:
  0.0 2.0 %project.1 = (bf16[512,128]{1,0:T(8,128)(2,1)S(1)}, bf16[512,128]{1,0:T(8,128)(2,1)S(1)}, bf16[512,128]{1,0:T(8,128)(2,1)S(1)}, bf16[512,128]{1,0:T(8,128)(2,1)S...) custom-call(s32[1]{0:T(128)} %bitcast.refs_0_, ...), custom_call_target="tpu_custom_call" | custom-call | tf_op jit(solution)/shard_map/project/pallas_call | solution.py:303
  2.0 0.5 collective-permute-start.1
  2.5 2.6 %collective-permute-start.2 = (bf16[512,128]{1,0:T(8,128)(2,1)S(1)}, bf16[512,128]{1,0:T(8,128)(2,1)S(1)}, u32[]{:S(2)}, u32[]{:S(2)}) collective-permute-start(bf16[512,128]{1,0:T(8,128)(2,1)S(1)} %get-tuple-element.22), channel_id=1, source_target_pairs={{0,4},{1,5},{4,8},{5,9},{8,12},{9,13},{12,14},{13,15},{14,10},{15,... | collective-permute-start | bytes 393224 | tf_op jit(solution)/shard_map/ppermute | solution.py:329
  5.2 0.0 collective-permute-done.1
  5.2 1.2 %collective-permute-start.5 = (bf16[512,128]{1,0:T(8,128)(2,1)S(1)}, bf16[512,128]{1,0:T(8,128)(2,1)S(1)}, u32[]{:S(2)}, u32[]{:S(2)}) collective-permute-start(bf16[512,128]{1,0:T(8,128)(2,1)S(1)} %collective-permute-done.1), channel_id=1, source_target_pairs={{0,2},{1,3},{4,0},{5,1},{8,4},{9,5},{12,8},{13,9},{14,12},{15,13},... | collective-permute-start | bytes 393224 | tf_op jit(solution)/shard_map/ppermute | solution.py:329
  6.4 1.6 %collective-permute-start.4 = (bf16[512,128]{1,0:T(8,128)(2,1)S(1)}, bf16[512,128]{1,0:T(8,128)(2,1)S(1)}, u32[]{:S(2)}, u32[]{:S(2)}) collective-permute-start(bf16[512,128]{1,0:T(8,128)(2,1)S(1)} %get-tuple-element.22), channel_id=1, source_target_pairs={{0,2},{1,3},{4,0},{5,1},{8,4},{9,5},{12,8},{13,9},{14,12},{15,13},... | collective-permute-start | bytes 393224 | tf_op jit(solution)/shard_map/ppermute | solution.py:329
  8.0 0.4 collective-permute-start.3
  8.4 0.8 %collective-permute-done.2 = bf16[512,128]{1,0:T(8,128)(2,1)S(1)} collective-permute-done((bf16[512,128]{1,0:T(8,128)(2,1)S(1)}, bf16[512,128]{1,0:T(8,128)(2,1)S(1)}, u32[]{:S(2)}, u32[]{:S(2)}) %collective-permute-start.2) | collective-permute-done | bytes 131104 | tf_op jit(solution)/shard_map/ppermute | solution.py:329
  9.2 2.1 %collective-permute-start.6 = (bf16[512,128]{1,0:T(8,128)(2,1)S(1)}, bf16[512,128]{1,0:T(8,128)(2,1)S(1)}, u32[]{:S(2)}, u32[]{:S(2)}) collective-permute-start(bf16[512,128]{1,0:T(8,128)(2,1)S(1)} %collective-permute-done.2), channel_id=1, source_target_pairs={{0,4},{1,5},{4,8},{5,9},{8,12},{9,13},{12,14},{13,15},{14,10},{15,... | collective-permute-start | bytes 393224 | tf_op jit(solution)/shard_map/ppermute | solution.py:329
  11.4 0.2 collective-permute-done.5
  11.5 1.2 %collective-permute-start.9 = (bf16[512,128]{1,0:T(8,128)(2,1)S(1)}, bf16[512,128]{1,0:T(8,128)(2,1)S(1)}, u32[]{:S(2)}, u32[]{:S(2)}) collective-permute-start(bf16[512,128]{1,0:T(8,128)(2,1)S(1)} %collective-permute-done.5), channel_id=1, source_target_pairs={{0,2},{1,3},{4,0},{5,1},{8,4},{9,5},{12,8},{13,9},{14,12},{15,13},... | collective-permute-start | bytes 393224 | tf_op jit(solution)/shard_map/ppermute | solution.py:329
  12.7 1.3 %collective-permute-done.4 = bf16[512,128]{1,0:T(8,128)(2,1)S(1)} collective-permute-done((bf16[512,128]{1,0:T(8,128)(2,1)S(1)}, bf16[512,128]{1,0:T(8,128)(2,1)S(1)}, u32[]{:S(2)}, u32[]{:S(2)}) %collective-permute-start.4) | collective-permute-done | bytes 131104 | tf_op jit(solution)/shard_map/ppermute | solution.py:329
  14.0 1.5 %collective-permute-start.8 = (bf16[512,128]{1,0:T(8,128)(2,1)S(1)}, bf16[512,128]{1,0:T(8,128)(2,1)S(1)}, u32[]{:S(2)}, u32[]{:S(2)}) collective-permute-start(bf16[512,128]{1,0:T(8,128)(2,1)S(1)} %collective-permute-done.4), channel_id=1, source_target_pairs={{0,2},{1,3},{4,0},{5,1},{8,4},{9,5},{12,8},{13,9},{14,12},{15,13},... | collective-permute-start | bytes 393224 | tf_op jit(solution)/shard_map/ppermute | solution.py:329
  15.5 0.0 collective-permute-done.3
  15.5 0.5 collective-permute-start.7
  16.1 0.0 collective-permute-done.6
  16.1 1.6 %collective-permute-start.10 = (bf16[512,128]{1,0:T(8,128)(2,1)S(1)}, bf16[512,128]{1,0:T(8,128)(2,1)S(1)}, u32[]{:S(2)}, u32[]{:S(2)}) collective-permute-start(bf16[512,128]{1,0:T(8,128)(2,1)S(1)} %collective-permute-done.6), channel_id=1, source_target_pairs={{0,4},{1,5},{4,8},{5,9},{8,12},{9,13},{12,14},{13,15},{14,10},{15,... | collective-permute-start | bytes 393224 | tf_op jit(solution)/shard_map/ppermute | solution.py:329
  17.6 0.0 collective-permute-done.9
  17.6 1.2 %collective-permute-start.13 = (bf16[512,128]{1,0:T(8,128)(2,1)S(1)}, bf16[512,128]{1,0:T(8,128)(2,1)S(1)}, u32[]{:S(2)}, u32[]{:S(2)}) collective-permute-start(bf16[512,128]{1,0:T(8,128)(2,1)S(1)} %collective-permute-done.9), channel_id=1, source_target_pairs={{0,2},{1,3},{4,0},{5,1},{8,4},{9,5},{12,8},{13,9},{14,12},{15,13},... | collective-permute-start | bytes 393224 | tf_op jit(solution)/shard_map/ppermute | solution.py:329
  18.8 0.0 collective-permute-start
  18.8 1.5 %collective-permute-done.8 = bf16[512,128]{1,0:T(8,128)(2,1)S(1)} collective-permute-done((bf16[512,128]{1,0:T(8,128)(2,1)S(1)}, bf16[512,128]{1,0:T(8,128)(2,1)S(1)}, u32[]{:S(2)}, u32[]{:S(2)}) %collective-permute-start.8) | collective-permute-done | bytes 131104 | tf_op jit(solution)/shard_map/ppermute | solution.py:329
  20.4 1.5 %collective-permute-start.12 = (bf16[512,128]{1,0:T(8,128)(2,1)S(1)}, bf16[512,128]{1,0:T(8,128)(2,1)S(1)}, u32[]{:S(2)}, u32[]{:S(2)}) collective-permute-start(bf16[512,128]{1,0:T(8,128)(2,1)S(1)} %collective-permute-done.8), channel_id=1, source_target_pairs={{0,2},{1,3},{4,0},{5,1},{8,4},{9,5},{12,8},{13,9},{14,12},{15,13},... | collective-permute-start | bytes 393224 | tf_op jit(solution)/shard_map/ppermute | solution.py:329
  21.9 0.0 collective-permute-done.7
  21.9 0.5 collective-permute-start.11
  22.4 0.0 collective-permute-done.10
  22.4 1.6 %collective-permute-start.14 = (bf16[512,128]{1,0:T(8,128)(2,1)S(1)}, bf16[512,128]{1,0:T(8,128)(2,1)S(1)}, u32[]{:S(2)}, u32[]{:S(2)}) collective-permute-start(bf16[512,128]{1,0:T(8,128)(2,1)S(1)} %collective-permute-done.10), channel_id=1, source_target_pairs={{0,4},{1,5},{4,8},{5,9},{8,12},{9,13},{12,14},{13,15},{14,10},{15,... | collective-permute-start | bytes 393224 | tf_op jit(solution)/shard_map/ppermute | solution.py:329
  24.0 0.0 collective-permute-done.13
  24.0 0.5 collective-permute-start.15
  24.4 0.1 pad_add_fusion.place_ref
  24.5 0.0 collective-permute-done
  24.5 0.8 %mix_early.1.early_ref = bf16[64,16,128]{2,1,0:T(8,128)(2,1)S(1)} custom-call(bf16[64,8,128]{2,1,0:T(8,128)(2,1)S(1)} %bitcast.26, bf16[64,8,128]{2,1,0:T(8,128)(2,1)S(1)} %bitcast.30, bf16[64,8,128]{2,1,0:T(8,128)(2,1)S(1)} %bitcast.38, bf16[64,8,128]{2,1,0:T(8,128)(2,1)S(1)} %bitcast.39, bf16[64,8,128]{2,1,0:T(8,128)(2,1)S(1)} %bitcast.40, ...), custom_call_target="tpu_custom_call" | custom-call | flops 1000000000 | bytes 4194304 | tf_op jit(solution)/shard_map/mix_early/pallas_call | solution.py:352
  25.3 1.5 %collective-permute-done.12 = bf16[512,128]{1,0:T(8,128)(2,1)S(1)} collective-permute-done((bf16[512,128]{1,0:T(8,128)(2,1)S(1)}, bf16[512,128]{1,0:T(8,128)(2,1)S(1)}, u32[]{:S(2)}, u32[]{:S(2)}) %collective-permute-start.12) | collective-permute-done | bytes 131104 | tf_op jit(solution)/shard_map/ppermute | solution.py:329
  26.8 0.6 collective-permute-done.11
  27.4 1.4 %collective-permute-done.14 = bf16[512,128]{1,0:T(8,128)(2,1)S(1)} collective-permute-done((bf16[512,128]{1,0:T(8,128)(2,1)S(1)}, bf16[512,128]{1,0:T(8,128)(2,1)S(1)}, u32[]{:S(2)}, u32[]{:S(2)}) %collective-permute-start.14) | collective-permute-done | bytes 131104 | tf_op jit(solution)/shard_map/ppermute | solution.py:329
  28.9 0.1 collective-permute-done.15
  29.0 2.4 %mix_late.1 = (bf16[64,8,128]{2,1,0:T(8,128)(2,1)S(1)}, bf16[64,8,128]{2,1,0:T(8,128)(2,1)S(1)}) custom-call(s32[2]{0:T(128)S(1)} %pad_add_fusion.place_ref, bf16[64,8,128]{2,1,0:T(8,128)(2,1)S(1)} %bitcast.27, bf16[64,8,128]{2,1,0:T(8,128)(2,1)S(1)} %bitcast.31, bf16[64,16,128]{2,1,0:T(8,128)(2,1)S(1)} %mix_early.1.early_ref, ...), custom_call_target="tpu_custom_call" | custom-call | tf_op jit(solution)/shard_map/mix_late/pallas_call | solution.py:361
  31.4 0.0 collective-permute-start.16
  31.4 1.3 %collective-permute-done.16 = bf16[64,8,128]{2,1,0:T(8,128)(2,1)S(1)} collective-permute-done((bf16[64,8,128]{2,1,0:T(8,128)(2,1)S(1)}, bf16[64,8,128]{2,1,0:T(8,128)(2,1)S(1)}, u32[]{:S(2)}, u32[]{:S(2)}) %collective-permute-start.16) | collective-permute-done | bytes 131104 | tf_op jit(solution)/shard_map/ppermute | solution.py:369
  32.8 1.4 %finish_project.1 = (bf16[2048,128]{1,0:T(8,128)(2,1)S(1)}, bf16[128,1024]{1,0:T(8,128)(2,1)S(1)}, bf16[128,1024]{1,0:T(8,128)(2,1)S(1)}) custom-call(s32[1]{0:T(128)} %bitcast.refs_0_, bf16[512,128]{1,0:T(8,128)(2,1)S(1)} %bitcast.36, bf16[512,128]{1,0:T(8,128)(2,1)S(1)} %bitcast.37, bf16[128,1024]{1,0:T(8,128)(2,1)S(1)} %get-tuple-element.26.refs_3_, ...), custom_call_target="tpu_custom_call" | custom-call | tf_op jit(solution)/shard_map/finish_project/pallas_call | solution.py:372
  34.2 19.6 %all_to_all.17.both_ref = bf16[16,128,128]{2,1,0:T(8,128)(2,1)S(1)} all-to-all(bf16[16,128,128]{2,1,0:T(8,128)(2,1)S(1)} %bitcast.25), channel_id=1, replica_groups=mesh['groups'=2,'row'=16] {'row'}, dimensions={0} | all-to-all | bytes 1048576 | tf_op jit(solution)/shard_map/all_to_all | solution.py:284
  53.7 0.3 mix.1
  54.0 13.9 %all_to_all.18 = bf16[16,64,128]{2,1,0:T(8,128)(2,1)S(1)} all-to-all(bf16[16,64,128]{2,1,0:T(8,128)(2,1)S(1)} %mix.1), channel_id=1, replica_groups=mesh['groups'=2,'row'=16] {'row'}, dimensions={0} | all-to-all | bytes 524288 | tf_op jit(solution)/shard_map/all_to_all | solution.py:284
  68.0 1.2 %finish.1 = bf16[8,128,128]{2,1,0:T(8,128)(2,1)} custom-call(bf16[1024,128]{1,0:T(8,128)(2,1)S(1)} %bitcast.24, bf16[128,1024]{1,0:T(8,128)(2,1)S(1)} %get-tuple-element.33.middle_t_ref, bf16[128,1024]{1,0:T(8,128)(2,1)S(1)} %get-tuple-element.34.gate_t_ref, f32[8,128,128]{2,1,0:T(8,128)S(1)} %get-tuple-element.29.refs_6_.columns_ref, ...), custom_call_target="tpu_custom_call" | custom-call | tf_op jit(solution)/shard_map/finish/pallas_call | solution.py:382
Async XLA Ops:
  2.0 3.2 %collective-permute-start.1 = (bf16[512,128]{1,0:T(8,128)(2,1)S(1)}, bf16[512,128]{1,0:T(8,128)(2,1)S(1)}, u32[]{:S(2)}, u32[]{:S(2)}) collective-permute-start(bf16[512,128]{1,0:T(8,128)(2,1)S(1)} %get-tuple-element.23), channel_id=1, source_target_pairs={{0,1},{1,0},{2,3},{3,2},{4,5},{5,4},{6,7},{7,6},{8,9},{9,8},{10,11... | collective-permute-start | bytes 393224 | tf_op jit(solution)/shard_map/ppermute | solution.py:338
  2.5 6.7 %collective-permute-start.2 = (bf16[512,128]{1,0:T(8,128)(2,1)S(1)}, bf16[512,128]{1,0:T(8,128)(2,1)S(1)}, u32[]{:S(2)}, u32[]{:S(2)}) collective-permute-start(bf16[512,128]{1,0:T(8,128)(2,1)S(1)} %get-tuple-element.22), channel_id=1, source_target_pairs={{0,4},{1,5},{4,8},{5,9},{8,12},{9,13},{12,14},{13,15},{14,10},{15,... | collective-permute-start | bytes 393224 | tf_op jit(solution)/shard_map/ppermute | solution.py:329
  5.2 6.3 %collective-permute-start.5 = (bf16[512,128]{1,0:T(8,128)(2,1)S(1)}, bf16[512,128]{1,0:T(8,128)(2,1)S(1)}, u32[]{:S(2)}, u32[]{:S(2)}) collective-permute-start(bf16[512,128]{1,0:T(8,128)(2,1)S(1)} %collective-permute-done.1), channel_id=1, source_target_pairs={{0,2},{1,3},{4,0},{5,1},{8,4},{9,5},{12,8},{13,9},{14,12},{15,13},... | collective-permute-start | bytes 393224 | tf_op jit(solution)/shard_map/ppermute | solution.py:329
  6.4 7.6 %collective-permute-start.4 = (bf16[512,128]{1,0:T(8,128)(2,1)S(1)}, bf16[512,128]{1,0:T(8,128)(2,1)S(1)}, u32[]{:S(2)}, u32[]{:S(2)}) collective-permute-start(bf16[512,128]{1,0:T(8,128)(2,1)S(1)} %get-tuple-element.22), channel_id=1, source_target_pairs={{0,2},{1,3},{4,0},{5,1},{8,4},{9,5},{12,8},{13,9},{14,12},{15,13},... | collective-permute-start | bytes 393224 | tf_op jit(solution)/shard_map/ppermute | solution.py:329
  8.0 7.6 %collective-permute-start.3 = (bf16[512,128]{1,0:T(8,128)(2,1)S(1)}, bf16[512,128]{1,0:T(8,128)(2,1)S(1)}, u32[]{:S(2)}, u32[]{:S(2)}) collective-permute-start(bf16[512,128]{1,0:T(8,128)(2,1)S(1)} %collective-permute-done.1), channel_id=1, source_target_pairs={{0,4},{1,5},{4,8},{5,9},{8,12},{9,13},{12,14},{13,15},{14,10},{15,... | collective-permute-start | bytes 393224 | tf_op jit(solution)/shard_map/ppermute | solution.py:329
  9.2 6.9 %collective-permute-start.6 = (bf16[512,128]{1,0:T(8,128)(2,1)S(1)}, bf16[512,128]{1,0:T(8,128)(2,1)S(1)}, u32[]{:S(2)}, u32[]{:S(2)}) collective-permute-start(bf16[512,128]{1,0:T(8,128)(2,1)S(1)} %collective-permute-done.2), channel_id=1, source_target_pairs={{0,4},{1,5},{4,8},{5,9},{8,12},{9,13},{12,14},{13,15},{14,10},{15,... | collective-permute-start | bytes 393224 | tf_op jit(solution)/shard_map/ppermute | solution.py:329
  11.5 6.1 %collective-permute-start.9 = (bf16[512,128]{1,0:T(8,128)(2,1)S(1)}, bf16[512,128]{1,0:T(8,128)(2,1)S(1)}, u32[]{:S(2)}, u32[]{:S(2)}) collective-permute-start(bf16[512,128]{1,0:T(8,128)(2,1)S(1)} %collective-permute-done.5), channel_id=1, source_target_pairs={{0,2},{1,3},{4,0},{5,1},{8,4},{9,5},{12,8},{13,9},{14,12},{15,13},... | collective-permute-start | bytes 393224 | tf_op jit(solution)/shard_map/ppermute | solution.py:329
  14.0 6.3 %collective-permute-start.8 = (bf16[512,128]{1,0:T(8,128)(2,1)S(1)}, bf16[512,128]{1,0:T(8,128)(2,1)S(1)}, u32[]{:S(2)}, u32[]{:S(2)}) collective-permute-start(bf16[512,128]{1,0:T(8,128)(2,1)S(1)} %collective-permute-done.4), channel_id=1, source_target_pairs={{0,2},{1,3},{4,0},{5,1},{8,4},{9,5},{12,8},{13,9},{14,12},{15,13},... | collective-permute-start | bytes 393224 | tf_op jit(solution)/shard_map/ppermute | solution.py:329
  15.5 6.4 %collective-permute-start.7 = (bf16[512,128]{1,0:T(8,128)(2,1)S(1)}, bf16[512,128]{1,0:T(8,128)(2,1)S(1)}, u32[]{:S(2)}, u32[]{:S(2)}) collective-permute-start(bf16[512,128]{1,0:T(8,128)(2,1)S(1)} %collective-permute-done.3), channel_id=1, source_target_pairs={{0,4},{1,5},{4,8},{5,9},{8,12},{9,13},{12,14},{13,15},{14,10},{15,... | collective-permute-start | bytes 393224 | tf_op jit(solution)/shard_map/ppermute | solution.py:329
  16.1 6.3 %collective-permute-start.10 = (bf16[512,128]{1,0:T(8,128)(2,1)S(1)}, bf16[512,128]{1,0:T(8,128)(2,1)S(1)}, u32[]{:S(2)}, u32[]{:S(2)}) collective-permute-start(bf16[512,128]{1,0:T(8,128)(2,1)S(1)} %collective-permute-done.6), channel_id=1, source_target_pairs={{0,4},{1,5},{4,8},{5,9},{8,12},{9,13},{12,14},{13,15},{14,10},{15,... | collective-permute-start | bytes 393224 | tf_op jit(solution)/shard_map/ppermute | solution.py:329
  17.6 6.3 %collective-permute-start.13 = (bf16[512,128]{1,0:T(8,128)(2,1)S(1)}, bf16[512,128]{1,0:T(8,128)(2,1)S(1)}, u32[]{:S(2)}, u32[]{:S(2)}) collective-permute-start(bf16[512,128]{1,0:T(8,128)(2,1)S(1)} %collective-permute-done.9), channel_id=1, source_target_pairs={{0,2},{1,3},{4,0},{5,1},{8,4},{9,5},{12,8},{13,9},{14,12},{15,13},... | collective-permute-start | bytes 393224 | tf_op jit(solution)/shard_map/ppermute | solution.py:329
  18.8 5.7 %collective-permute-start = (bf16[512,128]{1,0:T(8,128)(2,1)S(1)}, bf16[512,128]{1,0:T(8,128)(2,1)S(1)}, u32[]{:S(2)}, u32[]{:S(2)}) collective-permute-start(bf16[512,128]{1,0:T(8,128)(2,1)S(1)} %get-tuple-element.21), channel_id=1, source_target_pairs={{0,1},{1,0},{2,3},{3,2},{4,5},{5,4},{6,7},{7,6},{8,9},{9,8},{10,11... | collective-permute-start | bytes 393224 | tf_op jit(solution)/shard_map/ppermute | solution.py:339
  20.4 6.4 %collective-permute-start.12 = (bf16[512,128]{1,0:T(8,128)(2,1)S(1)}, bf16[512,128]{1,0:T(8,128)(2,1)S(1)}, u32[]{:S(2)}, u32[]{:S(2)}) collective-permute-start(bf16[512,128]{1,0:T(8,128)(2,1)S(1)} %collective-permute-done.8), channel_id=1, source_target_pairs={{0,2},{1,3},{4,0},{5,1},{8,4},{9,5},{12,8},{13,9},{14,12},{15,13},... | collective-permute-start | bytes 393224 | tf_op jit(solution)/shard_map/ppermute | solution.py:329
  21.9 5.5 %collective-permute-start.11 = (bf16[512,128]{1,0:T(8,128)(2,1)S(1)}, bf16[512,128]{1,0:T(8,128)(2,1)S(1)}, u32[]{:S(2)}, u32[]{:S(2)}) collective-permute-start(bf16[512,128]{1,0:T(8,128)(2,1)S(1)} %collective-permute-done.7), channel_id=1, source_target_pairs={{0,4},{1,5},{4,8},{5,9},{8,12},{9,13},{12,14},{13,15},{14,10},{15,... | collective-permute-start | bytes 393224 | tf_op jit(solution)/shard_map/ppermute | solution.py:329
  22.4 6.4 %collective-permute-start.14 = (bf16[512,128]{1,0:T(8,128)(2,1)S(1)}, bf16[512,128]{1,0:T(8,128)(2,1)S(1)}, u32[]{:S(2)}, u32[]{:S(2)}) collective-permute-start(bf16[512,128]{1,0:T(8,128)(2,1)S(1)} %collective-permute-done.10), channel_id=1, source_target_pairs={{0,4},{1,5},{4,8},{5,9},{8,12},{9,13},{12,14},{13,15},{14,10},{15,... | collective-permute-start | bytes 393224 | tf_op jit(solution)/shard_map/ppermute | solution.py:329
  24.0 5.0 %collective-permute-start.15 = (bf16[512,128]{1,0:T(8,128)(2,1)S(1)}, bf16[512,128]{1,0:T(8,128)(2,1)S(1)}, u32[]{:S(2)}, u32[]{:S(2)}) collective-permute-start(bf16[512,128]{1,0:T(8,128)(2,1)S(1)} %collective-permute-done.13), channel_id=1, source_target_pairs={{0,2},{1,3},{4,0},{5,1},{8,4},{9,5},{12,8},{13,9},{14,12},{15,13},... | collective-permute-start | bytes 393224 | tf_op jit(solution)/shard_map/ppermute | solution.py:329
  31.4 1.4 %collective-permute-start.16 = (bf16[64,8,128]{2,1,0:T(8,128)(2,1)S(1)}, bf16[64,8,128]{2,1,0:T(8,128)(2,1)S(1)}, u32[]{:S(2)}, u32[]{:S(2)}) collective-permute-start(bf16[64,8,128]{2,1,0:T(8,128)(2,1)S(1)} %get-tuple-element.25), channel_id=1, source_target_pairs={{0,1},{1,0},{2,3},{3,2},{4,5},{5,4},{6,7},{7,6},{8,9},{9,8},{10,11... | collective-permute-start | bytes 393224 | tf_op jit(solution)/shard_map/ppermute | solution.py:369

commit v18 on v17

--- a/solution.py
+++ b/solution.py
@@ -143,18 +143,21 @@
     return list(range(0, count, 2)) + list(range(count - 1, 0, -2))
 
 
-def token_order(place_ref, distances, rows, tokens):
-    chips = len(distances)
-    shape = (tokens, tokens)
-    lane, token = (lax.broadcasted_iota(jnp.int32, shape, axis) for axis in range(2))
-    core, place = jnp.full(shape, place_ref[0]), jnp.full(shape, place_ref[1])
-    device = token // rows
-    chip, source_core = device // 2, device % 2
-    source = jnp.where(chip % 2 == 0, chip // 2, chips - 1 - chip // 2)
-    distance = (place - source + chips) % chips
-    place_of = sum(jnp.where(distance == d, n, 0) for n, d in enumerate(distances))
-    slot = 2 * place_of + jnp.where(source_core == core, 0, 1)
-    return jnp.where(lane == slot * rows + token % rows, 1.0, 0.0).astype(BF16)
+def token_order(chips, distances, rows):
+    device = lax.axis_index("row")
+    chip, core = device // 2, device % 2
+    place = jnp.where(chip % 2 == 0, chip // 2, chips - 1 - chip // 2)
+    size = 2 * chips * rows
+    lane, token = (lax.broadcasted_iota(jnp.int32, (size, size), axis) for axis in range(2))
+    first = jnp.zeros((size, size), jnp.int32)
+    for n, d in enumerate(distances):
+        source = place - d + jnp.where(place < d, chips, 0)
+        source = jnp.where(2 * source < chips, 2 * source, 2 * (chips - 1 - source) + 1)
+        for piece in range(2):
+            start = (2 * n + piece) * rows
+            block = 2 * source + (1 - core if piece else core)
+            first = jnp.where((lane >= start) & (lane < start + rows), block * rows - start, first)
+    return (token == lane + first).astype(BF16)
 
 
 def gathered_sums(own_ref, got_ref, rights, first_lane, c):
@@ -173,10 +176,10 @@
         early_ref[c] = gathered_sums(own_ref, got_ref, rights, 0, c).astype(BF16)
 
 
-def mix_late(distances, early, place_ref, own_ref, got_ref, early_ref, *refs):
+def mix_late(early, order_ref, own_ref, got_ref, early_ref, *refs):
     rights, (keep_ref, send_ref) = refs[:-2], refs[-2:]
     count, rows, tokens = own_ref.shape
-    order = token_order(place_ref, distances, rows, tokens)
+    order = order_ref[...]
     group = 8
     for first in range(0, count, group):
         sums = [
@@ -337,6 +340,7 @@
         swap = [(d, d ^ 1) for d in range(groups)]
         got_right = lax.ppermute(other_right, "row", swap)
         got_left = lax.ppermute(other_left, "row", swap)
+        got_right, got_left = lax.optimization_barrier((got_right, got_left))
         middle = chips // 2
         ups = [rounds(right, 1, middle), rounds(got_right, 1, middle - 1)]
         downs = [rounds(right, -1, middle - 1), rounds(got_right, -1, middle)]
@@ -347,8 +351,6 @@
         ]
         rights = [array.reshape(half, rows, tokens) for array in rights]
         lefts = [array.reshape(half, rows, tokens) for array in (left, got_left)]
-        chip = lax.axis_index("row") // 2
-        place = jnp.where(chip % 2 == 0, chip // 2, chips - 1 - chip // 2).astype(jnp.int32)
         first_sums = pl.pallas_call(
             mix_early,
             out_shape=shape((half, 2 * rows, tokens), BF16),
@@ -359,13 +361,13 @@
             name="mix_early",
         )(*lefts, *rights[:early])
         keep, send = pl.pallas_call(
-            functools.partial(mix_late, distances, early),
+            functools.partial(mix_late, early),
             out_shape=(shape((half, rows, tokens), BF16),) * 2,
-            in_specs=[smem] + [whole] * (3 + len(rights) - early),
+            in_specs=[whole] * (4 + len(rights) - early),
             out_specs=(whole,) * 2,
             compiler_params=params,
             name="mix_late",
-        )(jnp.concatenate([core, place.reshape(1)]), *lefts, first_sums, *rights[early:])
+        )(token_order(chips, distances, rows), *lefts, first_sums, *rights[early:])
         merged = (core, keep.reshape(half * rows, tokens), lax.ppermute(send, "row", swap).reshape(half * rows, tokens))
     else:
         merged = (exchange(mix(exchange(results[0]), False)),)

time: 69.4 us -> 70.3 us (1.013)
  waiting for transfers between devices: 8.81 us -> 12 us
  starting transfers between devices: 18.6 us -> 16.7 us
    ppermute x14, waiting for transfers between devices: 7.47 us -> 9.69 us  [along(): return lax.ppermute(array, 'row', pairs)]
    ppermute x14, starting transfers between devices: 18.1 us -> 16.2 us  [along(): return lax.ppermute(array, 'row', pairs)]
    ppermute x1, waiting for transfers between devices: 0.01 us -> 0.81 us  [on_device(): got_right = lax.ppermute(other_right, 'row', swap)]
  transfers between devices with their start and end apart: 17 -> 17, of which waited for: 9 -> 12; matrix products, arithmetic and copies ran while one was open for 0% -> 1% of each run, Pallas kernels for 1% -> 1%
where the time goes in v18:
time: 70.3 us; the launch traced here: 70.1 us
  blocking collectives  33.3 us (47%)
  starting transfers between devices  16.7 us (24%)
  waiting for transfers between devices  12 us (17%)
  Pallas kernels  7.54 us (11%)
    all_to_all x2, blocking collectives, exchange(): return lax.all_to_all(array, 'row', split_axis=0, concat_axis=0, tiled=True)  33.3 us
    ppermute x14, starting transfers between devices, along(): return lax.ppermute(array, 'row', pairs)  16.2 us
    ppermute x14, waiting for transfers between devices, along(): return lax.ppermute(array, 'row', pairs)  9.69 us
    pallas_call x1, Pallas kernels, on_device(): pl.pallas_call(functools.partial(project_kernel, half if by_core else per...  2 us
    pallas_call x1, Pallas kernels, on_device(): pl.pallas_call(functools.partial(mix_late, early), out_shape=(shape((half...  1.91 us
  transfers between devices with their start and end apart: 17, of which 12 were waited for; matrix products, arithmetic and copies ran while one was open for 1% of the time, Pallas kernels for 1%

profile of v18, /device:TPU:0, one launch (start us, length us, event | category | flops | bytes accessed | tf_op | source)
XLA Modules:
  0.0 70.1 jit_solution(14307552059061054113)
XLA Ops:
  0.0 2.0 %project.1 = (bf16[512,128]{1,0:T(8,128)(2,1)S(1)}, bf16[512,128]{1,0:T(8,128)(2,1)S(1)}, bf16[512,128]{1,0:T(8,128)(2,1)S(1)}, bf16[512,128]{1,0:T(8,128)(2,1)S...) custom-call(s32[1]{0:T(128)} %bitcast.refs_0_, ...), custom_call_target="tpu_custom_call" | custom-call | tf_op jit(solution)/shard_map/project/pallas_call | solution.py:306
  2.0 3.0 %collective-permute-start.4 = (bf16[512,128]{1,0:T(8,128)(2,1)S(1)}, bf16[512,128]{1,0:T(8,128)(2,1)S(1)}, u32[]{:S(2)}, u32[]{:S(2)}) collective-permute-start(bf16[512,128]{1,0:T(8,128)(2,1)S(1)} %get-tuple-element.26), channel_id=1, source_target_pairs={{0,2},{1,3},{4,0},{5,1},{8,4},{9,5},{12,8},{13,9},{14,12},{15,13},... | collective-permute-start | bytes 393224 | tf_op jit(solution)/shard_map/ppermute | solution.py:332
  5.0 0.1 collective-permute-start.2
  5.2 0.0 collective-permute-start
  5.2 0.5 collective-permute-start.1
  5.7 0.8 %collective-permute-done = bf16[512,128]{1,0:T(8,128)(2,1)S(1)} collective-permute-done((bf16[512,128]{1,0:T(8,128)(2,1)S(1)}, bf16[512,128]{1,0:T(8,128)(2,1)S(1)}, u32[]{:S(2)}, u32[]{:S(2)}) %collective-permute-start) | collective-permute-done | bytes 131104 | tf_op jit(solution)/shard_map/ppermute | solution.py:341
  6.5 0.2 collective-permute-done.1
  6.7 1.9 %collective-permute-start.5 = (bf16[512,128]{1,0:T(8,128)(2,1)S(1)}, bf16[512,128]{1,0:T(8,128)(2,1)S(1)}, u32[]{:S(2)}, u32[]{:S(2)}) collective-permute-start(bf16[512,128]{1,0:T(8,128)(2,1)S(1)} %collective-permute-done), channel_id=1, source_target_pairs={{0,2},{1,3},{4,0},{5,1},{8,4},{9,5},{12,8},{13,9},{14,12},{15,13},... | collective-permute-start | bytes 393224 | tf_op jit(solution)/shard_map/ppermute | solution.py:332
  8.6 0.2 collective-permute-start.3
  8.8 1.2 %collective-permute-done.2 = bf16[512,128]{1,0:T(8,128)(2,1)S(1)} collective-permute-done((bf16[512,128]{1,0:T(8,128)(2,1)S(1)}, bf16[512,128]{1,0:T(8,128)(2,1)S(1)}, u32[]{:S(2)}, u32[]{:S(2)}) %collective-permute-start.2) | collective-permute-done | bytes 131104 | tf_op jit(solution)/shard_map/ppermute | solution.py:332
  10.0 0.7 %collective-permute-start.6 = (bf16[512,128]{1,0:T(8,128)(2,1)S(1)}, bf16[512,128]{1,0:T(8,128)(2,1)S(1)}, u32[]{:S(2)}, u32[]{:S(2)}) collective-permute-start(bf16[512,128]{1,0:T(8,128)(2,1)S(1)} %collective-permute-done.2), channel_id=1, source_target_pairs={{0,4},{1,5},{4,8},{5,9},{8,12},{9,13},{12,14},{13,15},{14,10},{15,... | collective-permute-start | bytes 393224 | tf_op jit(solution)/shard_map/ppermute | solution.py:332
  10.7 1.9 %collective-permute-done.5 = bf16[512,128]{1,0:T(8,128)(2,1)S(1)} collective-permute-done((bf16[512,128]{1,0:T(8,128)(2,1)S(1)}, bf16[512,128]{1,0:T(8,128)(2,1)S(1)}, u32[]{:S(2)}, u32[]{:S(2)}) %collective-permute-start.5) | collective-permute-done | bytes 131104 | tf_op jit(solution)/shard_map/ppermute | solution.py:332
  12.6 1.7 %collective-permute-start.9 = (bf16[512,128]{1,0:T(8,128)(2,1)S(1)}, bf16[512,128]{1,0:T(8,128)(2,1)S(1)}, u32[]{:S(2)}, u32[]{:S(2)}) collective-permute-start(bf16[512,128]{1,0:T(8,128)(2,1)S(1)} %collective-permute-done.5), channel_id=1, source_target_pairs={{0,2},{1,3},{4,0},{5,1},{8,4},{9,5},{12,8},{13,9},{14,12},{15,13},... | collective-permute-start | bytes 393224 | tf_op jit(solution)/shard_map/ppermute | solution.py:332
  14.3 0.0 collective-permute-done.4
  14.3 1.6 %collective-permute-start.8 = (bf16[512,128]{1,0:T(8,128)(2,1)S(1)}, bf16[512,128]{1,0:T(8,128)(2,1)S(1)}, u32[]{:S(2)}, u32[]{:S(2)}) collective-permute-start(bf16[512,128]{1,0:T(8,128)(2,1)S(1)} %collective-permute-done.4), channel_id=1, source_target_pairs={{0,2},{1,3},{4,0},{5,1},{8,4},{9,5},{12,8},{13,9},{14,12},{15,13},... | collective-permute-start | bytes 393224 | tf_op jit(solution)/shard_map/ppermute | solution.py:332
  16.0 0.0 collective-permute-done.3
  16.0 0.4 collective-permute-start.7
  16.4 0.5 collective-permute-done.6
  16.9 0.3 collective-permute-start.10
  17.3 1.8 %collective-permute-done.9 = bf16[512,128]{1,0:T(8,128)(2,1)S(1)} collective-permute-done((bf16[512,128]{1,0:T(8,128)(2,1)S(1)}, bf16[512,128]{1,0:T(8,128)(2,1)S(1)}, u32[]{:S(2)}, u32[]{:S(2)}) %collective-permute-start.9) | collective-permute-done | bytes 131104 | tf_op jit(solution)/shard_map/ppermute | solution.py:332
  19.0 1.6 %collective-permute-start.13 = (bf16[512,128]{1,0:T(8,128)(2,1)S(1)}, bf16[512,128]{1,0:T(8,128)(2,1)S(1)}, u32[]{:S(2)}, u32[]{:S(2)}) collective-permute-start(bf16[512,128]{1,0:T(8,128)(2,1)S(1)} %collective-permute-done.9), channel_id=1, source_target_pairs={{0,2},{1,3},{4,0},{5,1},{8,4},{9,5},{12,8},{13,9},{14,12},{15,13},... | collective-permute-start | bytes 393224 | tf_op jit(solution)/shard_map/ppermute | solution.py:332
  20.7 1.2 %collective-permute-done.8 = bf16[512,128]{1,0:T(8,128)(2,1)S(1)} collective-permute-done((bf16[512,128]{1,0:T(8,128)(2,1)S(1)}, bf16[512,128]{1,0:T(8,128)(2,1)S(1)}, u32[]{:S(2)}, u32[]{:S(2)}) %collective-permute-start.8) | collective-permute-done | bytes 131104 | tf_op jit(solution)/shard_map/ppermute | solution.py:332
  21.8 1.6 %collective-permute-start.12 = (bf16[512,128]{1,0:T(8,128)(2,1)S(1)}, bf16[512,128]{1,0:T(8,128)(2,1)S(1)}, u32[]{:S(2)}, u32[]{:S(2)}) collective-permute-start(bf16[512,128]{1,0:T(8,128)(2,1)S(1)} %collective-permute-done.8), channel_id=1, source_target_pairs={{0,2},{1,3},{4,0},{5,1},{8,4},{9,5},{12,8},{13,9},{14,12},{15,13},... | collective-permute-start | bytes 393224 | tf_op jit(solution)/shard_map/ppermute | solution.py:332
  23.5 0.0 collective-permute-done.7
  23.5 0.4 collective-permute-start.11
  23.9 0.0 collective-permute-done.10
  23.9 1.8 %collective-permute-start.14 = (bf16[512,128]{1,0:T(8,128)(2,1)S(1)}, bf16[512,128]{1,0:T(8,128)(2,1)S(1)}, u32[]{:S(2)}, u32[]{:S(2)}) collective-permute-start(bf16[512,128]{1,0:T(8,128)(2,1)S(1)} %collective-permute-done.10), channel_id=1, source_target_pairs={{0,4},{1,5},{4,8},{5,9},{8,12},{9,13},{12,14},{13,15},{14,10},{15,... | collective-permute-start | bytes 393224 | tf_op jit(solution)/shard_map/ppermute | solution.py:332
  25.6 0.0 collective-permute-done.13
  25.7 0.7 collective-permute-start.15
  26.3 0.3 fusion.order_ref
  26.7 0.8 %mix_early.1.early_ref = bf16[64,16,128]{2,1,0:T(8,128)(2,1)S(1)} custom-call(bf16[64,8,128]{2,1,0:T(8,128)(2,1)S(1)} %bitcast.27, bf16[64,8,128]{2,1,0:T(8,128)(2,1)S(1)} %bitcast.29, bf16[64,8,128]{2,1,0:T(8,128)(2,1)S(1)} %bitcast.37, bf16[64,8,128]{2,1,0:T(8,128)(2,1)S(1)} %bitcast.40, bf16[64,8,128]{2,1,0:T(8,128)(2,1)S(1)} %bitcast.39, ...), custom_call_target="tpu_custom_call" | custom-call | flops 1000000000 | bytes 4194304 | tf_op jit(solution)/shard_map/mix_early/pallas_call | solution.py:354
  27.5 0.3 collective-permute-done.12
  27.7 0.8 %collective-permute-done.11 = bf16[512,128]{1,0:T(8,128)(2,1)S(1)} collective-permute-done((bf16[512,128]{1,0:T(8,128)(2,1)S(1)}, bf16[512,128]{1,0:T(8,128)(2,1)S(1)}, u32[]{:S(2)}, u32[]{:S(2)}) %collective-permute-start.11) | collective-permute-done | bytes 131104 | tf_op jit(solution)/shard_map/ppermute | solution.py:332
  28.5 1.4 %collective-permute-done.14 = bf16[512,128]{1,0:T(8,128)(2,1)S(1)} collective-permute-done((bf16[512,128]{1,0:T(8,128)(2,1)S(1)}, bf16[512,128]{1,0:T(8,128)(2,1)S(1)}, u32[]{:S(2)}, u32[]{:S(2)}) %collective-permute-start.14) | collective-permute-done | bytes 131104 | tf_op jit(solution)/shard_map/ppermute | solution.py:332
  29.9 0.8 %collective-permute-done.15 = bf16[512,128]{1,0:T(8,128)(2,1)S(1)} collective-permute-done((bf16[512,128]{1,0:T(8,128)(2,1)S(1)}, bf16[512,128]{1,0:T(8,128)(2,1)S(1)}, u32[]{:S(2)}, u32[]{:S(2)}) %collective-permute-start.15) | collective-permute-done | bytes 131104 | tf_op jit(solution)/shard_map/ppermute | solution.py:332
  30.6 1.9 %mix_late.1 = (bf16[64,8,128]{2,1,0:T(8,128)(2,1)S(1)}, bf16[64,8,128]{2,1,0:T(8,128)(2,1)S(1)}) custom-call(bf16[128,128]{1,0:T(8,128)(2,1)S(1)} %fusion.order_ref, bf16[64,8,128]{2,1,0:T(8,128)(2,1)S(1)} %bitcast.28, bf16[64,8,128]{2,1,0:T(8,128)(2,1)S(1)} %bitcast.30, bf16[64,16,128]{2,1,0:T(8,128)(2,1)S(1)} %mix_early.1.early_ref, ...), custom_call_target="tpu_custom_call" | custom-call | tf_op jit(solution)/shard_map/mix_late/pallas_call | solution.py:363
  32.5 0.0 collective-permute-start.16
  32.6 1.3 %collective-permute-done.16 = bf16[64,8,128]{2,1,0:T(8,128)(2,1)S(1)} collective-permute-done((bf16[64,8,128]{2,1,0:T(8,128)(2,1)S(1)}, bf16[64,8,128]{2,1,0:T(8,128)(2,1)S(1)}, u32[]{:S(2)}, u32[]{:S(2)}) %collective-permute-start.16) | collective-permute-done | bytes 131104 | tf_op jit(solution)/shard_map/ppermute | solution.py:371
  33.9 1.4 %finish_project.1 = (bf16[2048,128]{1,0:T(8,128)(2,1)S(1)}, bf16[128,1024]{1,0:T(8,128)(2,1)S(1)}, bf16[128,1024]{1,0:T(8,128)(2,1)S(1)}) custom-call(s32[1]{0:T(128)} %bitcast.refs_0_, bf16[512,128]{1,0:T(8,128)(2,1)S(1)} %bitcast.25, bf16[512,128]{1,0:T(8,128)(2,1)S(1)} %bitcast.26, bf16[128,1024]{1,0:T(8,128)(2,1)S(1)} %get-tuple-element.30.refs_3_, ...), custom_call_target="tpu_custom_call" | custom-call | tf_op jit(solution)/shard_map/finish_project/pallas_call | solution.py:374
  35.3 19.4 %all_to_all.17.both_ref = bf16[16,128,128]{2,1,0:T(8,128)(2,1)S(1)} all-to-all(bf16[16,128,128]{2,1,0:T(8,128)(2,1)S(1)} %bitcast.24), channel_id=1, replica_groups=mesh['groups'=2,'row'=16] {'row'}, dimensions={0} | all-to-all | bytes 1048576 | tf_op jit(solution)/shard_map/all_to_all | solution.py:287
  54.7 0.3 mix.1
  54.9 13.9 %all_to_all.18 = bf16[16,64,128]{2,1,0:T(8,128)(2,1)S(1)} all-to-all(bf16[16,64,128]{2,1,0:T(8,128)(2,1)S(1)} %mix.1), channel_id=1, replica_groups=mesh['groups'=2,'row'=16] {'row'}, dimensions={0} | all-to-all | bytes 524288 | tf_op jit(solution)/shard_map/all_to_all | solution.py:287
  68.9 1.2 %finish.1 = bf16[8,128,128]{2,1,0:T(8,128)(2,1)} custom-call(bf16[1024,128]{1,0:T(8,128)(2,1)S(1)} %bitcast.23, bf16[128,1024]{1,0:T(8,128)(2,1)S(1)} %get-tuple-element.37.middle_t_ref, bf16[128,1024]{1,0:T(8,128)(2,1)S(1)} %get-tuple-element.38.gate_t_ref, f32[8,128,128]{2,1,0:T(8,128)S(1)} %get-tuple-element.33.refs_6_.columns_ref, ...), custom_call_target="tpu_custom_call" | custom-call | tf_op jit(solution)/shard_map/finish/pallas_call | solution.py:384
  (9 shorter events, 0.0 us)
Async XLA Ops:
  2.0 12.3 %collective-permute-start.4 = (bf16[512,128]{1,0:T(8,128)(2,1)S(1)}, bf16[512,128]{1,0:T(8,128)(2,1)S(1)}, u32[]{:S(2)}, u32[]{:S(2)}) collective-permute-start(bf16[512,128]{1,0:T(8,128)(2,1)S(1)} %get-tuple-element.26), channel_id=1, source_target_pairs={{0,2},{1,3},{4,0},{5,1},{8,4},{9,5},{12,8},{13,9},{14,12},{15,13},... | collective-permute-start | bytes 393224 | tf_op jit(solution)/shard_map/ppermute | solution.py:332
  5.0 5.0 %collective-permute-start.2 = (bf16[512,128]{1,0:T(8,128)(2,1)S(1)}, bf16[512,128]{1,0:T(8,128)(2,1)S(1)}, u32[]{:S(2)}, u32[]{:S(2)}) collective-permute-start(bf16[512,128]{1,0:T(8,128)(2,1)S(1)} %get-tuple-element.26), channel_id=1, source_target_pairs={{0,4},{1,5},{4,8},{5,9},{8,12},{9,13},{12,14},{13,15},{14,10},{15,... | collective-permute-start | bytes 393224 | tf_op jit(solution)/shard_map/ppermute | solution.py:332
  5.2 1.3 %collective-permute-start = (bf16[512,128]{1,0:T(8,128)(2,1)S(1)}, bf16[512,128]{1,0:T(8,128)(2,1)S(1)}, u32[]{:S(2)}, u32[]{:S(2)}) collective-permute-start(bf16[512,128]{1,0:T(8,128)(2,1)S(1)} %get-tuple-element.23), channel_id=1, source_target_pairs={{0,1},{1,0},{2,3},{3,2},{4,5},{5,4},{6,7},{7,6},{8,9},{9,8},{10,11... | collective-permute-start | bytes 393224 | tf_op jit(solution)/shard_map/ppermute | solution.py:341
  5.2 1.5 %collective-permute-start.1 = (bf16[512,128]{1,0:T(8,128)(2,1)S(1)}, bf16[512,128]{1,0:T(8,128)(2,1)S(1)}, u32[]{:S(2)}, u32[]{:S(2)}) collective-permute-start(bf16[512,128]{1,0:T(8,128)(2,1)S(1)} %get-tuple-element.24), channel_id=1, source_target_pairs={{0,1},{1,0},{2,3},{3,2},{4,5},{5,4},{6,7},{7,6},{8,9},{9,8},{10,11... | collective-permute-start | bytes 393224 | tf_op jit(solution)/shard_map/ppermute | solution.py:342
  6.7 5.9 %collective-permute-start.5 = (bf16[512,128]{1,0:T(8,128)(2,1)S(1)}, bf16[512,128]{1,0:T(8,128)(2,1)S(1)}, u32[]{:S(2)}, u32[]{:S(2)}) collective-permute-start(bf16[512,128]{1,0:T(8,128)(2,1)S(1)} %collective-permute-done), channel_id=1, source_target_pairs={{0,2},{1,3},{4,0},{5,1},{8,4},{9,5},{12,8},{13,9},{14,12},{15,13},... | collective-permute-start | bytes 393224 | tf_op jit(solution)/shard_map/ppermute | solution.py:332
  8.6 7.4 %collective-permute-start.3 = (bf16[512,128]{1,0:T(8,128)(2,1)S(1)}, bf16[512,128]{1,0:T(8,128)(2,1)S(1)}, u32[]{:S(2)}, u32[]{:S(2)}) collective-permute-start(bf16[512,128]{1,0:T(8,128)(2,1)S(1)} %collective-permute-done), channel_id=1, source_target_pairs={{0,4},{1,5},{4,8},{5,9},{8,12},{9,13},{12,14},{13,15},{14,10},{15,... | collective-permute-start | bytes 393224 | tf_op jit(solution)/shard_map/ppermute | solution.py:332
  10.0 6.9 %collective-permute-start.6 = (bf16[512,128]{1,0:T(8,128)(2,1)S(1)}, bf16[512,128]{1,0:T(8,128)(2,1)S(1)}, u32[]{:S(2)}, u32[]{:S(2)}) collective-permute-start(bf16[512,128]{1,0:T(8,128)(2,1)S(1)} %collective-permute-done.2), channel_id=1, source_target_pairs={{0,4},{1,5},{4,8},{5,9},{8,12},{9,13},{12,14},{13,15},{14,10},{15,... | collective-permute-start | bytes 393224 | tf_op jit(solution)/shard_map/ppermute | solution.py:332
  12.6 6.4 %collective-permute-start.9 = (bf16[512,128]{1,0:T(8,128)(2,1)S(1)}, bf16[512,128]{1,0:T(8,128)(2,1)S(1)}, u32[]{:S(2)}, u32[]{:S(2)}) collective-permute-start(bf16[512,128]{1,0:T(8,128)(2,1)S(1)} %collective-permute-done.5), channel_id=1, source_target_pairs={{0,2},{1,3},{4,0},{5,1},{8,4},{9,5},{12,8},{13,9},{14,12},{15,13},... | collective-permute-start | bytes 393224 | tf_op jit(solution)/shard_map/ppermute | solution.py:332
  14.3 7.5 %collective-permute-start.8 = (bf16[512,128]{1,0:T(8,128)(2,1)S(1)}, bf16[512,128]{1,0:T(8,128)(2,1)S(1)}, u32[]{:S(2)}, u32[]{:S(2)}) collective-permute-start(bf16[512,128]{1,0:T(8,128)(2,1)S(1)} %collective-permute-done.4), channel_id=1, source_target_pairs={{0,2},{1,3},{4,0},{5,1},{8,4},{9,5},{12,8},{13,9},{14,12},{15,13},... | collective-permute-start | bytes 393224 | tf_op jit(solution)/shard_map/ppermute | solution.py:332
  16.0 7.5 %collective-permute-start.7 = (bf16[512,128]{1,0:T(8,128)(2,1)S(1)}, bf16[512,128]{1,0:T(8,128)(2,1)S(1)}, u32[]{:S(2)}, u32[]{:S(2)}) collective-permute-start(bf16[512,128]{1,0:T(8,128)(2,1)S(1)} %collective-permute-done.3), channel_id=1, source_target_pairs={{0,4},{1,5},{4,8},{5,9},{8,12},{9,13},{12,14},{13,15},{14,10},{15,... | collective-permute-start | bytes 393224 | tf_op jit(solution)/shard_map/ppermute | solution.py:332
  16.9 7.0 %collective-permute-start.10 = (bf16[512,128]{1,0:T(8,128)(2,1)S(1)}, bf16[512,128]{1,0:T(8,128)(2,1)S(1)}, u32[]{:S(2)}, u32[]{:S(2)}) collective-permute-start(bf16[512,128]{1,0:T(8,128)(2,1)S(1)} %collective-permute-done.6), channel_id=1, source_target_pairs={{0,4},{1,5},{4,8},{5,9},{8,12},{9,13},{12,14},{13,15},{14,10},{15,... | collective-permute-start | bytes 393224 | tf_op jit(solution)/shard_map/ppermute | solution.py:332
  19.0 6.6 %collective-permute-start.13 = (bf16[512,128]{1,0:T(8,128)(2,1)S(1)}, bf16[512,128]{1,0:T(8,128)(2,1)S(1)}, u32[]{:S(2)}, u32[]{:S(2)}) collective-permute-start(bf16[512,128]{1,0:T(8,128)(2,1)S(1)} %collective-permute-done.9), channel_id=1, source_target_pairs={{0,2},{1,3},{4,0},{5,1},{8,4},{9,5},{12,8},{13,9},{14,12},{15,13},... | collective-permute-start | bytes 393224 | tf_op jit(solution)/shard_map/ppermute | solution.py:332
  21.8 5.9 %collective-permute-start.12 = (bf16[512,128]{1,0:T(8,128)(2,1)S(1)}, bf16[512,128]{1,0:T(8,128)(2,1)S(1)}, u32[]{:S(2)}, u32[]{:S(2)}) collective-permute-start(bf16[512,128]{1,0:T(8,128)(2,1)S(1)} %collective-permute-done.8), channel_id=1, source_target_pairs={{0,2},{1,3},{4,0},{5,1},{8,4},{9,5},{12,8},{13,9},{14,12},{15,13},... | collective-permute-start | bytes 393224 | tf_op jit(solution)/shard_map/ppermute | solution.py:332
  23.5 5.0 %collective-permute-start.11 = (bf16[512,128]{1,0:T(8,128)(2,1)S(1)}, bf16[512,128]{1,0:T(8,128)(2,1)S(1)}, u32[]{:S(2)}, u32[]{:S(2)}) collective-permute-start(bf16[512,128]{1,0:T(8,128)(2,1)S(1)} %collective-permute-done.7), channel_id=1, source_target_pairs={{0,4},{1,5},{4,8},{5,9},{8,12},{9,13},{12,14},{13,15},{14,10},{15,... | collective-permute-start | bytes 393224 | tf_op jit(solution)/shard_map/ppermute | solution.py:332
  23.9 6.0 %collective-permute-start.14 = (bf16[512,128]{1,0:T(8,128)(2,1)S(1)}, bf16[512,128]{1,0:T(8,128)(2,1)S(1)}, u32[]{:S(2)}, u32[]{:S(2)}) collective-permute-start(bf16[512,128]{1,0:T(8,128)(2,1)S(1)} %collective-permute-done.10), channel_id=1, source_target_pairs={{0,4},{1,5},{4,8},{5,9},{8,12},{9,13},{12,14},{13,15},{14,10},{15,... | collective-permute-start | bytes 393224 | tf_op jit(solution)/shard_map/ppermute | solution.py:332
  25.7 5.0 %collective-permute-start.15 = (bf16[512,128]{1,0:T(8,128)(2,1)S(1)}, bf16[512,128]{1,0:T(8,128)(2,1)S(1)}, u32[]{:S(2)}, u32[]{:S(2)}) collective-permute-start(bf16[512,128]{1,0:T(8,128)(2,1)S(1)} %collective-permute-done.13), channel_id=1, source_target_pairs={{0,2},{1,3},{4,0},{5,1},{8,4},{9,5},{12,8},{13,9},{14,12},{15,13},... | collective-permute-start | bytes 393224 | tf_op jit(solution)/shard_map/ppermute | solution.py:332
  32.5 1.4 %collective-permute-start.16 = (bf16[64,8,128]{2,1,0:T(8,128)(2,1)S(1)}, bf16[64,8,128]{2,1,0:T(8,128)(2,1)S(1)}, u32[]{:S(2)}, u32[]{:S(2)}) collective-permute-start(bf16[64,8,128]{2,1,0:T(8,128)(2,1)S(1)} %get-tuple-element.29), channel_id=1, source_target_pairs={{0,1},{1,0},{2,3},{3,2},{4,5},{5,4},{6,7},{7,6},{8,9},{9,8},{10,11... | collective-permute-start | bytes 393224 | tf_op jit(solution)/shard_map/ppermute | solution.py:371

commit v19 on v18

--- a/solution.py
+++ b/solution.py
@@ -177,16 +177,16 @@
 
 
 def mix_late(early, order_ref, own_ref, got_ref, early_ref, *refs):
-    rights, (keep_ref, send_ref) = refs[:-2], refs[-2:]
+    rights, (keep_ref, send_ref, sums_ref) = refs[:-3], refs[-3:]
     count, rows, tokens = own_ref.shape
+    for c in range(count):
+        sums = gathered_sums(own_ref, got_ref, rights, early * rows, c)
+        sums_ref[2 * rows * c : 2 * rows * (c + 1)] = (sums + early_ref[c].astype(F32)).astype(BF16)
     order = order_ref[...]
-    group = 8
+    group = 16
     for first in range(0, count, group):
-        sums = [
-            (gathered_sums(own_ref, got_ref, rights, early * rows, c) + early_ref[c].astype(F32)).astype(BF16)
-            for c in range(first, first + group)
-        ]
-        sums = dot(jnp.concatenate(sums, axis=0), order, NN).reshape(group, 2 * rows, tokens)
+        sums = dot(sums_ref[2 * rows * first : 2 * rows * (first + group)], order, NN)
+        sums = sums.reshape(group, 2 * rows, tokens)
         keep_ref[first : first + group] = sums[:, :rows].astype(BF16)
         send_ref[first : first + group] = sums[:, rows:].astype(BF16)
 
@@ -340,7 +340,6 @@
         swap = [(d, d ^ 1) for d in range(groups)]
         got_right = lax.ppermute(other_right, "row", swap)
         got_left = lax.ppermute(other_left, "row", swap)
-        got_right, got_left = lax.optimization_barrier((got_right, got_left))
         middle = chips // 2
         ups = [rounds(right, 1, middle), rounds(got_right, 1, middle - 1)]
         downs = [rounds(right, -1, middle - 1), rounds(got_right, -1, middle)]
@@ -365,6 +364,7 @@
             out_shape=(shape((half, rows, tokens), BF16),) * 2,
             in_specs=[whole] * (4 + len(rights) - early),
             out_specs=(whole,) * 2,
+            scratch_shapes=[pltpu.VMEM((2 * half * rows, tokens), BF16)],
             compiler_params=params,
             name="mix_late",
         )(token_order(chips, distances, rows), *lefts, first_sums, *rights[early:])

time: 70.3 us -> 69.2 us (0.984)
  transfers between devices with their start and end apart: 17 -> 17, of which waited for: 12 -> 11; matrix products, arithmetic and copies ran while one was open for 1% -> 1% of each run, Pallas kernels for 1% -> 1%
where the time goes in v19:
time: 69.2 us; the launch traced here: 69 us
  blocking collectives  33.3 us (48%)
  starting transfers between devices  16.2 us (23%)
  waiting for transfers between devices  12.1 us (17%)
  Pallas kernels  6.96 us (10%)
    all_to_all x2, blocking collectives, exchange(): return lax.all_to_all(array, 'row', split_axis=0, concat_axis=0, tiled=True)  33.3 us
    ppermute x14, starting transfers between devices, along(): return lax.ppermute(array, 'row', pairs)  15.6 us
    ppermute x14, waiting for transfers between devices, along(): return lax.ppermute(array, 'row', pairs)  9.92 us
    pallas_call x1, Pallas kernels, on_device(): pl.pallas_call(functools.partial(project_kernel, half if by_core else per...  2 us
    pallas_call x1, Pallas kernels, on_device(): pl.pallas_call(functools.partial(step_kernel, per_group, by_core), out_sh...  1.39 us
  transfers between devices with their start and end apart: 17, of which 11 were waited for; matrix products, arithmetic and copies ran while one was open for 1% of the time, Pallas kernels for 1%

profile of v19, /device:TPU:0, one launch (start us, length us, event | category | flops | bytes accessed | tf_op | source)
XLA Modules:
  0.0 69.0 jit_solution(11049263172245677960)
XLA Ops:
  0.0 2.0 %project.1 = (bf16[512,128]{1,0:T(8,128)(2,1)S(1)}, bf16[512,128]{1,0:T(8,128)(2,1)S(1)}, bf16[512,128]{1,0:T(8,128)(2,1)S(1)}, bf16[512,128]{1,0:T(8,128)(2,1)S...) custom-call(s32[1]{0:T(128)} %bitcast.refs_0_, ...), custom_call_target="tpu_custom_call" | custom-call | tf_op jit(solution)/shard_map/project/pallas_call | solution.py:306
  2.0 3.0 %collective-permute-start.4 = (bf16[512,128]{1,0:T(8,128)(2,1)S(1)}, bf16[512,128]{1,0:T(8,128)(2,1)S(1)}, u32[]{:S(2)}, u32[]{:S(2)}) collective-permute-start(bf16[512,128]{1,0:T(8,128)(2,1)S(1)} %get-tuple-element.22), channel_id=1, source_target_pairs={{0,2},{1,3},{4,0},{5,1},{8,4},{9,5},{12,8},{13,9},{14,12},{15,13},... | collective-permute-start | bytes 393224 | tf_op jit(solution)/shard_map/ppermute | solution.py:332
  5.0 0.1 collective-permute-start.2
  5.2 0.0 collective-permute-start.1
  5.2 0.5 collective-permute-start
  5.7 0.8 %collective-permute-done.1 = bf16[512,128]{1,0:T(8,128)(2,1)S(1)} collective-permute-done((bf16[512,128]{1,0:T(8,128)(2,1)S(1)}, bf16[512,128]{1,0:T(8,128)(2,1)S(1)}, u32[]{:S(2)}, u32[]{:S(2)}) %collective-permute-start.1) | collective-permute-done | bytes 131104 | tf_op jit(solution)/shard_map/ppermute | solution.py:341
  6.5 1.9 %collective-permute-start.5 = (bf16[512,128]{1,0:T(8,128)(2,1)S(1)}, bf16[512,128]{1,0:T(8,128)(2,1)S(1)}, u32[]{:S(2)}, u32[]{:S(2)}) collective-permute-start(bf16[512,128]{1,0:T(8,128)(2,1)S(1)} %collective-permute-done.1), channel_id=1, source_target_pairs={{0,2},{1,3},{4,0},{5,1},{8,4},{9,5},{12,8},{13,9},{14,12},{15,13},... | collective-permute-start | bytes 393224 | tf_op jit(solution)/shard_map/ppermute | solution.py:332
  8.4 0.2 collective-permute-start.3
  8.6 1.4 %collective-permute-done.2 = bf16[512,128]{1,0:T(8,128)(2,1)S(1)} collective-permute-done((bf16[512,128]{1,0:T(8,128)(2,1)S(1)}, bf16[512,128]{1,0:T(8,128)(2,1)S(1)}, u32[]{:S(2)}, u32[]{:S(2)}) %collective-permute-start.2) | collective-permute-done | bytes 131104 | tf_op jit(solution)/shard_map/ppermute | solution.py:332
  10.0 0.6 collective-permute-start.6
  10.6 1.7 %collective-permute-done.5 = bf16[512,128]{1,0:T(8,128)(2,1)S(1)} collective-permute-done((bf16[512,128]{1,0:T(8,128)(2,1)S(1)}, bf16[512,128]{1,0:T(8,128)(2,1)S(1)}, u32[]{:S(2)}, u32[]{:S(2)}) %collective-permute-start.5) | collective-permute-done | bytes 131104 | tf_op jit(solution)/shard_map/ppermute | solution.py:332
  12.3 1.7 %collective-permute-start.9 = (bf16[512,128]{1,0:T(8,128)(2,1)S(1)}, bf16[512,128]{1,0:T(8,128)(2,1)S(1)}, u32[]{:S(2)}, u32[]{:S(2)}) collective-permute-start(bf16[512,128]{1,0:T(8,128)(2,1)S(1)} %collective-permute-done.5), channel_id=1, source_target_pairs={{0,2},{1,3},{4,0},{5,1},{8,4},{9,5},{12,8},{13,9},{14,12},{15,13},... | collective-permute-start | bytes 393224 | tf_op jit(solution)/shard_map/ppermute | solution.py:332
  14.0 0.0 collective-permute-done.4
  14.0 1.6 %collective-permute-start.8 = (bf16[512,128]{1,0:T(8,128)(2,1)S(1)}, bf16[512,128]{1,0:T(8,128)(2,1)S(1)}, u32[]{:S(2)}, u32[]{:S(2)}) collective-permute-start(bf16[512,128]{1,0:T(8,128)(2,1)S(1)} %collective-permute-done.4), channel_id=1, source_target_pairs={{0,2},{1,3},{4,0},{5,1},{8,4},{9,5},{12,8},{13,9},{14,12},{15,13},... | collective-permute-start | bytes 393224 | tf_op jit(solution)/shard_map/ppermute | solution.py:332
  15.6 0.0 collective-permute-done.3
  15.6 0.4 collective-permute-start.7
  16.1 0.5 collective-permute-done.6
  16.6 0.4 collective-permute-start.10
  16.9 1.8 %collective-permute-done.9 = bf16[512,128]{1,0:T(8,128)(2,1)S(1)} collective-permute-done((bf16[512,128]{1,0:T(8,128)(2,1)S(1)}, bf16[512,128]{1,0:T(8,128)(2,1)S(1)}, u32[]{:S(2)}, u32[]{:S(2)}) %collective-permute-start.9) | collective-permute-done | bytes 131104 | tf_op jit(solution)/shard_map/ppermute | solution.py:332
  18.7 1.4 %collective-permute-start.13 = (bf16[512,128]{1,0:T(8,128)(2,1)S(1)}, bf16[512,128]{1,0:T(8,128)(2,1)S(1)}, u32[]{:S(2)}, u32[]{:S(2)}) collective-permute-start(bf16[512,128]{1,0:T(8,128)(2,1)S(1)} %collective-permute-done.9), channel_id=1, source_target_pairs={{0,2},{1,3},{4,0},{5,1},{8,4},{9,5},{12,8},{13,9},{14,12},{15,13},... | collective-permute-start | bytes 393224 | tf_op jit(solution)/shard_map/ppermute | solution.py:332
  20.1 1.4 %collective-permute-done.8 = bf16[512,128]{1,0:T(8,128)(2,1)S(1)} collective-permute-done((bf16[512,128]{1,0:T(8,128)(2,1)S(1)}, bf16[512,128]{1,0:T(8,128)(2,1)S(1)}, u32[]{:S(2)}, u32[]{:S(2)}) %collective-permute-start.8) | collective-permute-done | bytes 131104 | tf_op jit(solution)/shard_map/ppermute | solution.py:332
  21.5 1.4 %collective-permute-start.12 = (bf16[512,128]{1,0:T(8,128)(2,1)S(1)}, bf16[512,128]{1,0:T(8,128)(2,1)S(1)}, u32[]{:S(2)}, u32[]{:S(2)}) collective-permute-start(bf16[512,128]{1,0:T(8,128)(2,1)S(1)} %collective-permute-done.8), channel_id=1, source_target_pairs={{0,2},{1,3},{4,0},{5,1},{8,4},{9,5},{12,8},{13,9},{14,12},{15,13},... | collective-permute-start | bytes 393224 | tf_op jit(solution)/shard_map/ppermute | solution.py:332
  22.9 0.0 collective-permute-done.10
  22.9 0.6 collective-permute-start.14
  23.5 0.0 collective-permute-done.7
  23.5 1.6 %collective-permute-start.11 = (bf16[512,128]{1,0:T(8,128)(2,1)S(1)}, bf16[512,128]{1,0:T(8,128)(2,1)S(1)}, u32[]{:S(2)}, u32[]{:S(2)}) collective-permute-start(bf16[512,128]{1,0:T(8,128)(2,1)S(1)} %collective-permute-done.7), channel_id=1, source_target_pairs={{0,4},{1,5},{4,8},{5,9},{8,12},{9,13},{12,14},{13,15},{14,10},{15,... | collective-permute-start | bytes 393224 | tf_op jit(solution)/shard_map/ppermute | solution.py:332
  25.1 0.0 collective-permute-done.13
  25.1 0.7 collective-permute-start.15
  25.8 0.3 fusion.order_ref
  26.1 0.0 collective-permute-done
  26.1 0.8 %mix_early.1.early_ref = bf16[64,16,128]{2,1,0:T(8,128)(2,1)S(1)} custom-call(bf16[64,8,128]{2,1,0:T(8,128)(2,1)S(1)} %bitcast.27, bf16[64,8,128]{2,1,0:T(8,128)(2,1)S(1)} %bitcast.29, bf16[64,8,128]{2,1,0:T(8,128)(2,1)S(1)} %bitcast.37, bf16[64,8,128]{2,1,0:T(8,128)(2,1)S(1)} %bitcast.40, bf16[64,8,128]{2,1,0:T(8,128)(2,1)S(1)} %bitcast.39, ...), custom_call_target="tpu_custom_call" | custom-call | flops 1000000000 | bytes 4194304 | tf_op jit(solution)/shard_map/mix_early/pallas_call | solution.py:353
  26.9 0.8 %collective-permute-done.12 = bf16[512,128]{1,0:T(8,128)(2,1)S(1)} collective-permute-done((bf16[512,128]{1,0:T(8,128)(2,1)S(1)}, bf16[512,128]{1,0:T(8,128)(2,1)S(1)}, u32[]{:S(2)}, u32[]{:S(2)}) %collective-permute-start.12) | collective-permute-done | bytes 131104 | tf_op jit(solution)/shard_map/ppermute | solution.py:332
  27.7 0.2 collective-permute-done.14
  27.9 1.4 %collective-permute-done.11 = bf16[512,128]{1,0:T(8,128)(2,1)S(1)} collective-permute-done((bf16[512,128]{1,0:T(8,128)(2,1)S(1)}, bf16[512,128]{1,0:T(8,128)(2,1)S(1)}, u32[]{:S(2)}, u32[]{:S(2)}) %collective-permute-start.11) | collective-permute-done | bytes 131104 | tf_op jit(solution)/shard_map/ppermute | solution.py:332
  29.3 0.8 %collective-permute-done.15 = bf16[512,128]{1,0:T(8,128)(2,1)S(1)} collective-permute-done((bf16[512,128]{1,0:T(8,128)(2,1)S(1)}, bf16[512,128]{1,0:T(8,128)(2,1)S(1)}, u32[]{:S(2)}, u32[]{:S(2)}) %collective-permute-start.15) | collective-permute-done | bytes 131104 | tf_op jit(solution)/shard_map/ppermute | solution.py:332
  30.1 1.3 %mix_late.1 = (bf16[64,8,128]{2,1,0:T(8,128)(2,1)S(1)}, bf16[64,8,128]{2,1,0:T(8,128)(2,1)S(1)}) custom-call(bf16[128,128]{1,0:T(8,128)(2,1)S(1)} %fusion.order_ref, bf16[64,8,128]{2,1,0:T(8,128)(2,1)S(1)} %bitcast.28, bf16[64,8,128]{2,1,0:T(8,128)(2,1)S(1)} %bitcast.30, bf16[64,16,128]{2,1,0:T(8,128)(2,1)S(1)} %mix_early.1.early_ref, ...), custom_call_target="tpu_custom_call" | custom-call | tf_op jit(solution)/shard_map/mix_late/pallas_call | solution.py:362
  31.4 0.1 collective-permute-start.16
  31.5 1.3 %collective-permute-done.16 = bf16[64,8,128]{2,1,0:T(8,128)(2,1)S(1)} collective-permute-done((bf16[64,8,128]{2,1,0:T(8,128)(2,1)S(1)}, bf16[64,8,128]{2,1,0:T(8,128)(2,1)S(1)}, u32[]{:S(2)}, u32[]{:S(2)}) %collective-permute-start.16) | collective-permute-done | bytes 131104 | tf_op jit(solution)/shard_map/ppermute | solution.py:371
  32.8 1.4 %finish_project.1 = (bf16[2048,128]{1,0:T(8,128)(2,1)S(1)}, bf16[128,1024]{1,0:T(8,128)(2,1)S(1)}, bf16[128,1024]{1,0:T(8,128)(2,1)S(1)}) custom-call(s32[1]{0:T(128)} %bitcast.refs_0_, bf16[512,128]{1,0:T(8,128)(2,1)S(1)} %bitcast.25, bf16[512,128]{1,0:T(8,128)(2,1)S(1)} %bitcast.26, bf16[128,1024]{1,0:T(8,128)(2,1)S(1)} %get-tuple-element.26.refs_3_, ...), custom_call_target="tpu_custom_call" | custom-call | tf_op jit(solution)/shard_map/finish_project/pallas_call | solution.py:374
  34.2 19.3 %all_to_all.17.both_ref = bf16[16,128,128]{2,1,0:T(8,128)(2,1)S(1)} all-to-all(bf16[16,128,128]{2,1,0:T(8,128)(2,1)S(1)} %bitcast.24), channel_id=1, replica_groups=mesh['groups'=2,'row'=16] {'row'}, dimensions={0} | all-to-all | bytes 1048576 | tf_op jit(solution)/shard_map/all_to_all | solution.py:287
  53.6 0.3 mix.1
  53.8 13.9 %all_to_all.18 = bf16[16,64,128]{2,1,0:T(8,128)(2,1)S(1)} all-to-all(bf16[16,64,128]{2,1,0:T(8,128)(2,1)S(1)} %mix.1), channel_id=1, replica_groups=mesh['groups'=2,'row'=16] {'row'}, dimensions={0} | all-to-all | bytes 524288 | tf_op jit(solution)/shard_map/all_to_all | solution.py:287
  67.8 1.2 %finish.1 = bf16[8,128,128]{2,1,0:T(8,128)(2,1)} custom-call(bf16[1024,128]{1,0:T(8,128)(2,1)S(1)} %bitcast.23, bf16[128,1024]{1,0:T(8,128)(2,1)S(1)} %get-tuple-element.33.middle_t_ref, bf16[128,1024]{1,0:T(8,128)(2,1)S(1)} %get-tuple-element.34.gate_t_ref, f32[8,128,128]{2,1,0:T(8,128)S(1)} %get-tuple-element.29.refs_6_.columns_ref, ...), custom_call_target="tpu_custom_call" | custom-call | tf_op jit(solution)/shard_map/finish/pallas_call | solution.py:384
  (9 shorter events, 0.0 us)
Async XLA Ops:
  2.0 12.0 %collective-permute-start.4 = (bf16[512,128]{1,0:T(8,128)(2,1)S(1)}, bf16[512,128]{1,0:T(8,128)(2,1)S(1)}, u32[]{:S(2)}, u32[]{:S(2)}) collective-permute-start(bf16[512,128]{1,0:T(8,128)(2,1)S(1)} %get-tuple-element.22), channel_id=1, source_target_pairs={{0,2},{1,3},{4,0},{5,1},{8,4},{9,5},{12,8},{13,9},{14,12},{15,13},... | collective-permute-start | bytes 393224 | tf_op jit(solution)/shard_map/ppermute | solution.py:332
  5.0 5.0 %collective-permute-start.2 = (bf16[512,128]{1,0:T(8,128)(2,1)S(1)}, bf16[512,128]{1,0:T(8,128)(2,1)S(1)}, u32[]{:S(2)}, u32[]{:S(2)}) collective-permute-start(bf16[512,128]{1,0:T(8,128)(2,1)S(1)} %get-tuple-element.22), channel_id=1, source_target_pairs={{0,4},{1,5},{4,8},{5,9},{8,12},{9,13},{12,14},{13,15},{14,10},{15,... | collective-permute-start | bytes 393224 | tf_op jit(solution)/shard_map/ppermute | solution.py:332
  5.2 1.3 %collective-permute-start.1 = (bf16[512,128]{1,0:T(8,128)(2,1)S(1)}, bf16[512,128]{1,0:T(8,128)(2,1)S(1)}, u32[]{:S(2)}, u32[]{:S(2)}) collective-permute-start(bf16[512,128]{1,0:T(8,128)(2,1)S(1)} %get-tuple-element.23), channel_id=1, source_target_pairs={{0,1},{1,0},{2,3},{3,2},{4,5},{5,4},{6,7},{7,6},{8,9},{9,8},{10,11... | collective-permute-start | bytes 393224 | tf_op jit(solution)/shard_map/ppermute | solution.py:341
  5.2 21.0 %collective-permute-start = (bf16[512,128]{1,0:T(8,128)(2,1)S(1)}, bf16[512,128]{1,0:T(8,128)(2,1)S(1)}, u32[]{:S(2)}, u32[]{:S(2)}) collective-permute-start(bf16[512,128]{1,0:T(8,128)(2,1)S(1)} %get-tuple-element.21), channel_id=1, source_target_pairs={{0,1},{1,0},{2,3},{3,2},{4,5},{5,4},{6,7},{7,6},{8,9},{9,8},{10,11... | collective-permute-start | bytes 393224 | tf_op jit(solution)/shard_map/ppermute | solution.py:342
  6.5 5.8 %collective-permute-start.5 = (bf16[512,128]{1,0:T(8,128)(2,1)S(1)}, bf16[512,128]{1,0:T(8,128)(2,1)S(1)}, u32[]{:S(2)}, u32[]{:S(2)}) collective-permute-start(bf16[512,128]{1,0:T(8,128)(2,1)S(1)} %collective-permute-done.1), channel_id=1, source_target_pairs={{0,2},{1,3},{4,0},{5,1},{8,4},{9,5},{12,8},{13,9},{14,12},{15,13},... | collective-permute-start | bytes 393224 | tf_op jit(solution)/shard_map/ppermute | solution.py:332
  8.4 7.2 %collective-permute-start.3 = (bf16[512,128]{1,0:T(8,128)(2,1)S(1)}, bf16[512,128]{1,0:T(8,128)(2,1)S(1)}, u32[]{:S(2)}, u32[]{:S(2)}) collective-permute-start(bf16[512,128]{1,0:T(8,128)(2,1)S(1)} %collective-permute-done.1), channel_id=1, source_target_pairs={{0,4},{1,5},{4,8},{5,9},{8,12},{9,13},{12,14},{13,15},{14,10},{15,... | collective-permute-start | bytes 393224 | tf_op jit(solution)/shard_map/ppermute | solution.py:332
  10.0 6.6 %collective-permute-start.6 = (bf16[512,128]{1,0:T(8,128)(2,1)S(1)}, bf16[512,128]{1,0:T(8,128)(2,1)S(1)}, u32[]{:S(2)}, u32[]{:S(2)}) collective-permute-start(bf16[512,128]{1,0:T(8,128)(2,1)S(1)} %collective-permute-done.2), channel_id=1, source_target_pairs={{0,4},{1,5},{4,8},{5,9},{8,12},{9,13},{12,14},{13,15},{14,10},{15,... | collective-permute-start | bytes 393224 | tf_op jit(solution)/shard_map/ppermute | solution.py:332
  12.3 6.4 %collective-permute-start.9 = (bf16[512,128]{1,0:T(8,128)(2,1)S(1)}, bf16[512,128]{1,0:T(8,128)(2,1)S(1)}, u32[]{:S(2)}, u32[]{:S(2)}) collective-permute-start(bf16[512,128]{1,0:T(8,128)(2,1)S(1)} %collective-permute-done.5), channel_id=1, source_target_pairs={{0,2},{1,3},{4,0},{5,1},{8,4},{9,5},{12,8},{13,9},{14,12},{15,13},... | collective-permute-start | bytes 393224 | tf_op jit(solution)/shard_map/ppermute | solution.py:332
  14.0 7.5 %collective-permute-start.8 = (bf16[512,128]{1,0:T(8,128)(2,1)S(1)}, bf16[512,128]{1,0:T(8,128)(2,1)S(1)}, u32[]{:S(2)}, u32[]{:S(2)}) collective-permute-start(bf16[512,128]{1,0:T(8,128)(2,1)S(1)} %collective-permute-done.4), channel_id=1, source_target_pairs={{0,2},{1,3},{4,0},{5,1},{8,4},{9,5},{12,8},{13,9},{14,12},{15,13},... | collective-permute-start | bytes 393224 | tf_op jit(solution)/shard_map/ppermute | solution.py:332
  15.6 7.9 %collective-permute-start.7 = (bf16[512,128]{1,0:T(8,128)(2,1)S(1)}, bf16[512,128]{1,0:T(8,128)(2,1)S(1)}, u32[]{:S(2)}, u32[]{:S(2)}) collective-permute-start(bf16[512,128]{1,0:T(8,128)(2,1)S(1)} %collective-permute-done.3), channel_id=1, source_target_pairs={{0,4},{1,5},{4,8},{5,9},{8,12},{9,13},{12,14},{13,15},{14,10},{15,... | collective-permute-start | bytes 393224 | tf_op jit(solution)/shard_map/ppermute | solution.py:332
  16.6 6.4 %collective-permute-start.10 = (bf16[512,128]{1,0:T(8,128)(2,1)S(1)}, bf16[512,128]{1,0:T(8,128)(2,1)S(1)}, u32[]{:S(2)}, u32[]{:S(2)}) collective-permute-start(bf16[512,128]{1,0:T(8,128)(2,1)S(1)} %collective-permute-done.6), channel_id=1, source_target_pairs={{0,4},{1,5},{4,8},{5,9},{8,12},{9,13},{12,14},{13,15},{14,10},{15,... | collective-permute-start | bytes 393224 | tf_op jit(solution)/shard_map/ppermute | solution.py:332
  18.7 6.4 %collective-permute-start.13 = (bf16[512,128]{1,0:T(8,128)(2,1)S(1)}, bf16[512,128]{1,0:T(8,128)(2,1)S(1)}, u32[]{:S(2)}, u32[]{:S(2)}) collective-permute-start(bf16[512,128]{1,0:T(8,128)(2,1)S(1)} %collective-permute-done.9), channel_id=1, source_target_pairs={{0,2},{1,3},{4,0},{5,1},{8,4},{9,5},{12,8},{13,9},{14,12},{15,13},... | collective-permute-start | bytes 393224 | tf_op jit(solution)/shard_map/ppermute | solution.py:332
  21.5 6.2 %collective-permute-start.12 = (bf16[512,128]{1,0:T(8,128)(2,1)S(1)}, bf16[512,128]{1,0:T(8,128)(2,1)S(1)}, u32[]{:S(2)}, u32[]{:S(2)}) collective-permute-start(bf16[512,128]{1,0:T(8,128)(2,1)S(1)} %collective-permute-done.8), channel_id=1, source_target_pairs={{0,2},{1,3},{4,0},{5,1},{8,4},{9,5},{12,8},{13,9},{14,12},{15,13},... | collective-permute-start | bytes 393224 | tf_op jit(solution)/shard_map/ppermute | solution.py:332
  22.9 5.0 %collective-permute-start.14 = (bf16[512,128]{1,0:T(8,128)(2,1)S(1)}, bf16[512,128]{1,0:T(8,128)(2,1)S(1)}, u32[]{:S(2)}, u32[]{:S(2)}) collective-permute-start(bf16[512,128]{1,0:T(8,128)(2,1)S(1)} %collective-permute-done.10), channel_id=1, source_target_pairs={{0,4},{1,5},{4,8},{5,9},{8,12},{9,13},{12,14},{13,15},{14,10},{15,... | collective-permute-start | bytes 393224 | tf_op jit(solution)/shard_map/ppermute | solution.py:332
  23.5 5.8 %collective-permute-start.11 = (bf16[512,128]{1,0:T(8,128)(2,1)S(1)}, bf16[512,128]{1,0:T(8,128)(2,1)S(1)}, u32[]{:S(2)}, u32[]{:S(2)}) collective-permute-start(bf16[512,128]{1,0:T(8,128)(2,1)S(1)} %collective-permute-done.7), channel_id=1, source_target_pairs={{0,4},{1,5},{4,8},{5,9},{8,12},{9,13},{12,14},{13,15},{14,10},{15,... | collective-permute-start | bytes 393224 | tf_op jit(solution)/shard_map/ppermute | solution.py:332
  25.1 5.0 %collective-permute-start.15 = (bf16[512,128]{1,0:T(8,128)(2,1)S(1)}, bf16[512,128]{1,0:T(8,128)(2,1)S(1)}, u32[]{:S(2)}, u32[]{:S(2)}) collective-permute-start(bf16[512,128]{1,0:T(8,128)(2,1)S(1)} %collective-permute-done.13), channel_id=1, source_target_pairs={{0,2},{1,3},{4,0},{5,1},{8,4},{9,5},{12,8},{13,9},{14,12},{15,13},... | collective-permute-start | bytes 393224 | tf_op jit(solution)/shard_map/ppermute | solution.py:332
  31.4 1.4 %collective-permute-start.16 = (bf16[64,8,128]{2,1,0:T(8,128)(2,1)S(1)}, bf16[64,8,128]{2,1,0:T(8,128)(2,1)S(1)}, u32[]{:S(2)}, u32[]{:S(2)}) collective-permute-start(bf16[64,8,128]{2,1,0:T(8,128)(2,1)S(1)} %get-tuple-element.25), channel_id=1, source_target_pairs={{0,1},{1,0},{2,3},{3,2},{4,5},{5,4},{6,7},{7,6},{8,9},{9,8},{10,11... | collective-permute-start | bytes 393224 | tf_op jit(solution)/shard_map/ppermute | solution.py:371

commit v20 on v19

--- a/solution.py
+++ b/solution.py
@@ -217,7 +217,11 @@
     if not by_core:
         merged_ref, refs = refs[0], refs[1:]
         return step_rows(per_group, lambda part: merged_ref[part].astype(F32), *refs)
-    core_ref, keep_ref, got_ref, refs = refs[0], refs[1], refs[2], refs[3:]
+    core_ref, refs = refs[0], refs[1:]
+    step_rows(per_group, core_halves(core_ref, refs[0], refs[1]), *refs[2:], core_ref=core_ref)
+
+
+def core_halves(core_ref, keep_ref, got_ref):
     size = keep_ref.shape[0]
 
     def load(part):
@@ -226,13 +230,13 @@
         keep, got = keep_ref[part].astype(F32), got_ref[part].astype(F32)
         return jnp.where(jnp.full(keep.shape, core_ref[0]) == int(late), keep, got)
 
-    step_rows(per_group, load, *refs)
+    return load
 
 
 def step_rows(
-    per_group, load, pair_t_ref, gate_t_ref, mask_ref, columns_ref, outw_t_ref, proj_t_ref,
-    both_ref, middle_t_ref, gate1_t_ref, unit_scratch, panels,
+    per_group, load, pair_t_ref, gate_t_ref, mask_ref, columns_ref, outw_t_ref, proj_t_ref, *refs, core_ref=None
 ):
+    outs, (middle_t_ref, gate1_t_ref, unit_scratch, panels) = refs[:-4], refs[-4:]
     rows, tokens = mask_ref.shape
 
     def emit(chunk, part, middle):
@@ -247,12 +251,22 @@
         emit, rows, pair_t_ref.shape[0], tokens, load, pair_t_ref, gate_t_ref, columns_ref[2], columns_ref[3],
         outw_t_ref[0], unit_scratch,
     )
-    pack_panels(panels, both_ref)
-
-
-def finish_kernel(
-    merged_ref, middle_t_ref, gate_t_ref, columns_ref, outw_t_ref, result_ref, unit_scratch, done, sems
-):
+    if core_ref is None:
+        pack_panels(panels, *outs)
+    else:
+        split_panels(panels, core_ref, *outs)
+
+
+def finish_kernel(by_core, *refs):
+    if by_core:
+        load, refs = core_halves(*refs[:3]), refs[3:]
+    else:
+        merged_ref, refs = refs[0], refs[1:]
+
+        def load(part):
+            return merged_ref[part].astype(F32)
+
+    middle_t_ref, gate_t_ref, columns_ref, outw_t_ref, result_ref, unit_scratch, done, sems = refs
     rows, tokens, _ = result_ref.shape
     copies = []
 
@@ -263,11 +277,48 @@
             copies[-1].start()
 
     finish_rows(
-        emit, rows, middle_t_ref.shape[0], tokens, lambda part: merged_ref[part].astype(F32), middle_t_ref, gate_t_ref,
+        emit, rows, middle_t_ref.shape[0], tokens, load, middle_t_ref, gate_t_ref,
         columns_ref[6], columns_ref[7], outw_t_ref[1], unit_scratch,
     )
     for copy in copies:
         copy.wait()
+
+
+def chip_rows(chips_ref, distance, count):
+    return pl.ds(pl.multiple_of(chips_ref[distance] * count, count), count)
+
+
+def scatter_start(first, up, down, chips_ref, *refs):
+    own_left, got_left, own_right, got_right, sums_ref, up_ref, down_ref = refs
+    rows = own_left.shape[1]
+    for c in range(sums_ref.shape[0]):
+        left, right = [
+            jnp.concatenate([own[first + c].astype(F32), got[first + c].astype(F32)], axis=0).astype(BF16)
+            for own, got in ((own_left, got_left), (own_right, got_right))
+        ]
+        sums_ref[c] = dot(left, right, TN)
+    for distance, ref in ((up, up_ref), (down, down_ref)):
+        ref[...] = sums_ref[:, chip_rows(chips_ref, distance, 2 * rows), :].astype(BF16)
+
+
+def scatter_add(distance, chips_ref, got_ref, sums_ref, out_ref):
+    here = sums_ref[:, chip_rows(chips_ref, distance, got_ref.shape[1]), :]
+    out_ref[...] = (got_ref[...].astype(F32) + here).astype(BF16)
+
+
+def scatter_end(core_ref, chips_ref, *refs):
+    pieces, (keep_ref, send_ref) = refs[:-2], refs[-2:]
+    rows = keep_ref.shape[1]
+    first = 0
+    for n in range(0, len(pieces), 3):
+        sums_ref, up_ref, down_ref = pieces[n : n + 3]
+        count = sums_ref.shape[0]
+        sums = sums_ref[:, chip_rows(chips_ref, 0, 2 * rows), :] + up_ref[...].astype(F32) + down_ref[...].astype(F32)
+        halves = sums[:, :rows], sums[:, rows:]
+        first_core = jnp.full(halves[0].shape, core_ref[0]) == 0
+        keep_ref[first : first + count] = jnp.where(first_core, *halves).astype(BF16)
+        send_ref[first : first + count] = jnp.where(first_core, *halves[::-1]).astype(BF16)
+        first += count
 
 
 def on_device(*inputs):
@@ -276,7 +327,7 @@
     per_group = channels // groups
     whole = pl.BlockSpec(memory_space=pltpu.VMEM)
     hbm = pl.BlockSpec(memory_space=pltpu.HBM)
-    params = pltpu.CompilerParams(vmem_limit_bytes=48 * 1024 * 1024)
+    params = pltpu.CompilerParams(vmem_limit_bytes=32 * 1024 * 1024)
     shape = jax.ShapeDtypeStruct
     both_shape = shape((2 * channels * rows, tokens), BF16)
     flat_shape = shape((channels, rows * tokens), BF16)
@@ -371,25 +422,71 @@
         merged = (core, keep.reshape(half * rows, tokens), lax.ppermute(send, "row", swap).reshape(half * rows, tokens))
     else:
         merged = (exchange(mix(exchange(results[0]), False)),)
-    both, middle_t, gate_t = pl.pallas_call(
-        functools.partial(step_kernel, per_group, by_core),
-        out_shape=(both_shape, flat_shape, flat_shape),
+    results = pl.pallas_call(
+        functools.partial(step_kernel, half if by_core else per_group, by_core),
+        out_shape=projected + (flat_shape, flat_shape),
         in_specs=[smem] * by_core + [whole] * (len(merged) - by_core + 6),
-        out_specs=(whole,) * 3,
+        out_specs=(whole,) * (len(projected) + 2),
         scratch_shapes=[unit_scratch, panels],
         compiler_params=params,
         name="finish_project",
     )(*merged, pair_t, gate_t, mask, columns, outw_t, proj_t)
-    merged = exchange(mix(exchange(both), True))
+    middle_t, gate_t = results[-2:]
+    if by_core:
+        left, right, other_left, other_right = results[:4]
+        got_left = lax.ppermute(other_left, "row", swap)
+        got_right = lax.ppermute(other_right, "row", swap)
+        operands = [array.reshape(half, rows, tokens) for array in (left, got_left, right, got_right)]
+        chip = lax.axis_index("row") // 2
+        place = jnp.where(chip % 2 == 0, chip // 2, chips - 1 - chip // 2)
+        spots = [place + d - jnp.where(place + d >= chips, chips, 0) for d in range(chips)]
+        chips_at = jnp.stack([jnp.where(2 * p < chips, 2 * p, 2 * (chips - 1 - p) + 1) for p in spots]).astype(jnp.int32)
+        size = half // 2
+        part_shape = shape((size, 2 * rows, tokens), BF16)
+        pieces = []
+        for piece in range(2):
+            hops = (middle, middle - 1) if piece == 0 else (middle - 1, middle)
+            sums, *travelling = pl.pallas_call(
+                functools.partial(scatter_start, piece * size, hops[0], chips - hops[1]),
+                out_shape=(shape((size, tokens, tokens), F32), part_shape, part_shape),
+                in_specs=[smem] + [whole] * 4,
+                out_specs=(whole,) * 3,
+                compiler_params=params,
+                name="scatter_start",
+            )(chips_at, *operands)
+            for way, (step, count) in enumerate(zip((1, -1), hops)):
+                for left_over in reversed(range(count)):
+                    travelling[way] = along(travelling[way], step)
+                    if left_over:
+                        travelling[way] = pl.pallas_call(
+                            functools.partial(scatter_add, step * left_over % chips),
+                            out_shape=part_shape,
+                            in_specs=[smem] + [whole] * 2,
+                            out_specs=whole,
+                            compiler_params=params,
+                            name="scatter_add",
+                        )(chips_at, travelling[way], sums)
+            pieces += [sums, *travelling]
+        keep, send = pl.pallas_call(
+            scatter_end,
+            out_shape=(shape((half, rows, tokens), BF16),) * 2,
+            in_specs=[smem] * 2 + [whole] * len(pieces),
+            out_specs=(whole,) * 2,
+            compiler_params=params,
+            name="scatter_end",
+        )(core, chips_at, *pieces)
+        merged = (core, keep.reshape(half * rows, tokens), lax.ppermute(send, "row", swap).reshape(half * rows, tokens))
+    else:
+        merged = (exchange(mix(exchange(results[0]), True)),)
     return pl.pallas_call(
-        finish_kernel,
+        functools.partial(finish_kernel, by_core),
         out_shape=shape((rows, tokens, channels), BF16),
-        in_specs=[whole] * 5,
+        in_specs=[smem] * by_core + [whole] * (len(merged) - by_core + 4),
         out_specs=hbm,
         scratch_shapes=[unit_scratch, pltpu.VMEM((rows, tokens, channels), BF16), pltpu.SemaphoreType.DMA((rows,))],
         compiler_params=params,
         name="finish",
-    )(merged, middle_t, gate_t, columns, outw_t)
+    )(*merged, middle_t, gate_t, columns, outw_t)
 
 
 def solution(mesh):

time: 69.2 us -> 69.1 us (level)
  blocking collectives: 33.3 us -> 0 us
  starting transfers between devices: 16.2 us -> 32.2 us
  waiting for transfers between devices: 12.1 us -> 20.9 us
  Pallas kernels: 6.96 us -> 15.2 us
    all_to_all x2 -> x0, blocking collectives: 33.3 us -> none  [exchange(): return lax.all_to_all(array, 'row', split_axis=0, concat_axis=0, tiled=True)]
    ppermute x14 -> x28, starting transfers between devices: 15.6 us -> 31 us  [along(): return lax.ppermute(array, 'row', pairs)]
    pallas_call x3 -> x15, Pallas kernels: 2.86 us -> 11.1 us  [the longest x10 5.68 us: on_device(): pl.pallas_call(functools.partial(scatter_add, step * left_over % chips),...]
    ppermute x14 -> x28, waiting for transfers between devices: 9.92 us -> 16.3 us  [along(): return lax.ppermute(array, 'row', pairs)]
    ppermute x1 -> x2, waiting for transfers between devices: 1.33 us -> 2.67 us  [on_device(): lax.ppermute(send, 'row', swap).reshape(half * rows, tokens)]
    ppermute x1 -> x2, starting transfers between devices: 0.01 us -> 0.87 us  [on_device(): got_right = lax.ppermute(other_right, 'row', swap)]
    ppermute x1 -> x2, waiting for transfers between devices: 0.01 us -> 0.76 us  [on_device(): got_left = lax.ppermute(other_left, 'row', swap)]
  transfers between devices with their start and end apart: 17 -> 34, of which waited for: 11 -> 20; matrix products, arithmetic and copies ran while one was open for 1% -> 1% of each run, Pallas kernels for 1% -> 11%
where the time goes in v20:
time: 69.1 us; the launch traced here: 68.9 us
  starting transfers between devices  32.2 us (47%)
  waiting for transfers between devices  20.9 us (30%)
  Pallas kernels  15.2 us (22%)
    ppermute x28, starting transfers between devices, along(): return lax.ppermute(array, 'row', pairs)  31 us
    ppermute x28, waiting for transfers between devices, along(): return lax.ppermute(array, 'row', pairs)  16.3 us
    pallas_call x10, Pallas kernels, on_device(): pl.pallas_call(functools.partial(scatter_add, step * left_over % chips),...  5.68 us
    ppermute x2, waiting for transfers between devices, on_device(): lax.ppermute(send, 'row', swap).reshape(half * rows, tokens)  2.67 us
    pallas_call x2, Pallas kernels, on_device(): pl.pallas_call(functools.partial(scatter_start, piece * size, hops[0], ch...  2.1 us
    pallas_call x1, Pallas kernels, on_device(): pl.pallas_call(functools.partial(project_kernel, half if by_core else per...  2.01 us
  transfers between devices with their start and end apart: 34, of which 20 were waited for; matrix products, arithmetic and copies ran while one was open for 1% of the time, Pallas kernels for 11%

profile of v20, /device:TPU:0, one launch (start us, length us, event | category | flops | bytes accessed | tf_op | source)
XLA Modules:
  0.0 68.9 jit_solution(2394392860460682393)
XLA Ops:
  0.0 2.0 %project.1 = (bf16[512,128]{1,0:T(8,128)(2,1)S(1)}, bf16[512,128]{1,0:T(8,128)(2,1)S(1)}, bf16[512,128]{1,0:T(8,128)(2,1)S(1)}, bf16[512,128]{1,0:T(8,128)(2,1)S...) custom-call(s32[1]{0:T(128)} %bitcast.refs_0_.core_ref, ...), custom_call_target="tpu_custom_call" | custom-call | tf_op jit(solution)/shard_map/project/pallas_call | solution.py:357
  2.0 3.0 %collective-permute-start.4 = (bf16[512,128]{1,0:T(8,128)(2,1)S(1)}, bf16[512,128]{1,0:T(8,128)(2,1)S(1)}, u32[]{:S(2)}, u32[]{:S(2)}) collective-permute-start(bf16[512,128]{1,0:T(8,128)(2,1)S(1)} %get-tuple-element.33), channel_id=1, source_target_pairs={{0,2},{1,3},{4,0},{5,1},{8,4},{9,5},{12,8},{13,9},{14,12},{15,13},... | collective-permute-start | bytes 393224 | tf_op jit(solution)/shard_map/ppermute | solution.py:383
  5.2 0.5 collective-permute-start.1
  5.7 1.0 %collective-permute-done.1 = bf16[512,128]{1,0:T(8,128)(2,1)S(1)} collective-permute-done((bf16[512,128]{1,0:T(8,128)(2,1)S(1)}, bf16[512,128]{1,0:T(8,128)(2,1)S(1)}, u32[]{:S(2)}, u32[]{:S(2)}) %collective-permute-start.1) | collective-permute-done | bytes 131104 | tf_op jit(solution)/shard_map/ppermute | solution.py:392
  6.7 1.9 %collective-permute-start.5 = (bf16[512,128]{1,0:T(8,128)(2,1)S(1)}, bf16[512,128]{1,0:T(8,128)(2,1)S(1)}, u32[]{:S(2)}, u32[]{:S(2)}) collective-permute-start(bf16[512,128]{1,0:T(8,128)(2,1)S(1)} %collective-permute-done.1), channel_id=1, source_target_pairs={{0,2},{1,3},{4,0},{5,1},{8,4},{9,5},{12,8},{13,9},{14,12},{15,13},... | collective-permute-start | bytes 393224 | tf_op jit(solution)/shard_map/ppermute | solution.py:383
  8.8 1.2 %collective-permute-done.2 = bf16[512,128]{1,0:T(8,128)(2,1)S(1)} collective-permute-done((bf16[512,128]{1,0:T(8,128)(2,1)S(1)}, bf16[512,128]{1,0:T(8,128)(2,1)S(1)}, u32[]{:S(2)}, u32[]{:S(2)}) %collective-permute-start.2) | collective-permute-done | bytes 131104 | tf_op jit(solution)/shard_map/ppermute | solution.py:383
  10.0 0.7 %collective-permute-start.6 = (bf16[512,128]{1,0:T(8,128)(2,1)S(1)}, bf16[512,128]{1,0:T(8,128)(2,1)S(1)}, u32[]{:S(2)}, u32[]{:S(2)}) collective-permute-start(bf16[512,128]{1,0:T(8,128)(2,1)S(1)} %collective-permute-done.2), channel_id=1, source_target_pairs={{0,4},{1,5},{4,8},{5,9},{8,12},{9,13},{12,14},{13,15},{14,10},{15,... | collective-permute-start | bytes 393224 | tf_op jit(solution)/shard_map/ppermute | solution.py:383
  10.8 1.9 %collective-permute-done.5 = bf16[512,128]{1,0:T(8,128)(2,1)S(1)} collective-permute-done((bf16[512,128]{1,0:T(8,128)(2,1)S(1)}, bf16[512,128]{1,0:T(8,128)(2,1)S(1)}, u32[]{:S(2)}, u32[]{:S(2)}) %collective-permute-start.5) | collective-permute-done | bytes 131104 | tf_op jit(solution)/shard_map/ppermute | solution.py:383
  12.6 1.7 %collective-permute-start.9 = (bf16[512,128]{1,0:T(8,128)(2,1)S(1)}, bf16[512,128]{1,0:T(8,128)(2,1)S(1)}, u32[]{:S(2)}, u32[]{:S(2)}) collective-permute-start(bf16[512,128]{1,0:T(8,128)(2,1)S(1)} %collective-permute-done.5), channel_id=1, source_target_pairs={{0,2},{1,3},{4,0},{5,1},{8,4},{9,5},{12,8},{13,9},{14,12},{15,13},... | collective-permute-start | bytes 393224 | tf_op jit(solution)/shard_map/ppermute | solution.py:383
  14.3 1.6 %collective-permute-start.8 = (bf16[512,128]{1,0:T(8,128)(2,1)S(1)}, bf16[512,128]{1,0:T(8,128)(2,1)S(1)}, u32[]{:S(2)}, u32[]{:S(2)}) collective-permute-start(bf16[512,128]{1,0:T(8,128)(2,1)S(1)} %collective-permute-done.4), channel_id=1, source_target_pairs={{0,2},{1,3},{4,0},{5,1},{8,4},{9,5},{12,8},{13,9},{14,12},{15,13},... | collective-permute-start | bytes 393224 | tf_op jit(solution)/shard_map/ppermute | solution.py:383
  16.0 0.4 collective-permute-start.7
  16.4 0.5 collective-permute-done.6
  16.9 0.3 collective-permute-start.10
  17.3 1.8 %collective-permute-done.9 = bf16[512,128]{1,0:T(8,128)(2,1)S(1)} collective-permute-done((bf16[512,128]{1,0:T(8,128)(2,1)S(1)}, bf16[512,128]{1,0:T(8,128)(2,1)S(1)}, u32[]{:S(2)}, u32[]{:S(2)}) %collective-permute-start.9) | collective-permute-done | bytes 131104 | tf_op jit(solution)/shard_map/ppermute | solution.py:383
  19.0 1.6 %collective-permute-start.13 = (bf16[512,128]{1,0:T(8,128)(2,1)S(1)}, bf16[512,128]{1,0:T(8,128)(2,1)S(1)}, u32[]{:S(2)}, u32[]{:S(2)}) collective-permute-start(bf16[512,128]{1,0:T(8,128)(2,1)S(1)} %collective-permute-done.9), channel_id=1, source_target_pairs={{0,2},{1,3},{4,0},{5,1},{8,4},{9,5},{12,8},{13,9},{14,12},{15,13},... | collective-permute-start | bytes 393224 | tf_op jit(solution)/shard_map/ppermute | solution.py:383
  20.7 1.2 %collective-permute-done.8 = bf16[512,128]{1,0:T(8,128)(2,1)S(1)} collective-permute-done((bf16[512,128]{1,0:T(8,128)(2,1)S(1)}, bf16[512,128]{1,0:T(8,128)(2,1)S(1)}, u32[]{:S(2)}, u32[]{:S(2)}) %collective-permute-start.8) | collective-permute-done | bytes 131104 | tf_op jit(solution)/shard_map/ppermute | solution.py:383
  21.8 1.6 %collective-permute-start.12 = (bf16[512,128]{1,0:T(8,128)(2,1)S(1)}, bf16[512,128]{1,0:T(8,128)(2,1)S(1)}, u32[]{:S(2)}, u32[]{:S(2)}) collective-permute-start(bf16[512,128]{1,0:T(8,128)(2,1)S(1)} %collective-permute-done.8), channel_id=1, source_target_pairs={{0,2},{1,3},{4,0},{5,1},{8,4},{9,5},{12,8},{13,9},{14,12},{15,13},... | collective-permute-start | bytes 393224 | tf_op jit(solution)/shard_map/ppermute | solution.py:383
  23.5 0.4 collective-permute-start.11
  23.9 1.8 %collective-permute-start.14 = (bf16[512,128]{1,0:T(8,128)(2,1)S(1)}, bf16[512,128]{1,0:T(8,128)(2,1)S(1)}, u32[]{:S(2)}, u32[]{:S(2)}) collective-permute-start(bf16[512,128]{1,0:T(8,128)(2,1)S(1)} %collective-permute-done.10), channel_id=1, source_target_pairs={{0,4},{1,5},{4,8},{5,9},{8,12},{9,13},{12,14},{13,15},{14,10},{15,... | collective-permute-start | bytes 393224 | tf_op jit(solution)/shard_map/ppermute | solution.py:383
  25.7 0.7 collective-permute-start.15
  26.7 0.8 %mix_early.1.early_ref = bf16[64,16,128]{2,1,0:T(8,128)(2,1)S(1)} custom-call(bf16[64,8,128]{2,1,0:T(8,128)(2,1)S(1)} %bitcast.47, bf16[64,8,128]{2,1,0:T(8,128)(2,1)S(1)} %bitcast.49, bf16[64,8,128]{2,1,0:T(8,128)(2,1)S(1)} %bitcast.57, bf16[64,8,128]{2,1,0:T(8,128)(2,1)S(1)} %bitcast.60, bf16[64,8,128]{2,1,0:T(8,128)(2,1)S(1)} %bitcast.59, ...), custom_call_target="tpu_custom_call" | custom-call | flops 1000000000 | bytes 4194304 | tf_op jit(solution)/shard_map/mix_early/pallas_call | solution.py:404
  27.7 0.8 %collective-permute-done.11 = bf16[512,128]{1,0:T(8,128)(2,1)S(1)} collective-permute-done((bf16[512,128]{1,0:T(8,128)(2,1)S(1)}, bf16[512,128]{1,0:T(8,128)(2,1)S(1)}, u32[]{:S(2)}, u32[]{:S(2)}) %collective-permute-start.11) | collective-permute-done | bytes 131104 | tf_op jit(solution)/shard_map/ppermute | solution.py:383
  28.5 1.4 %collective-permute-done.14 = bf16[512,128]{1,0:T(8,128)(2,1)S(1)} collective-permute-done((bf16[512,128]{1,0:T(8,128)(2,1)S(1)}, bf16[512,128]{1,0:T(8,128)(2,1)S(1)}, u32[]{:S(2)}, u32[]{:S(2)}) %collective-permute-start.14) | collective-permute-done | bytes 131104 | tf_op jit(solution)/shard_map/ppermute | solution.py:383
  29.9 0.8 %collective-permute-done.15 = bf16[512,128]{1,0:T(8,128)(2,1)S(1)} collective-permute-done((bf16[512,128]{1,0:T(8,128)(2,1)S(1)}, bf16[512,128]{1,0:T(8,128)(2,1)S(1)}, u32[]{:S(2)}, u32[]{:S(2)}) %collective-permute-start.15) | collective-permute-done | bytes 131104 | tf_op jit(solution)/shard_map/ppermute | solution.py:383
  30.6 1.3 %mix_late.1 = (bf16[64,8,128]{2,1,0:T(8,128)(2,1)S(1)}, bf16[64,8,128]{2,1,0:T(8,128)(2,1)S(1)}) custom-call(bf16[128,128]{1,0:T(8,128)(2,1)S(1)} %fusion.order_ref, bf16[64,8,128]{2,1,0:T(8,128)(2,1)S(1)} %bitcast.48, bf16[64,8,128]{2,1,0:T(8,128)(2,1)S(1)} %bitcast.50, bf16[64,16,128]{2,1,0:T(8,128)(2,1)S(1)} %mix_early.1.early_ref, ...), custom_call_target="tpu_custom_call" | custom-call | tf_op jit(solution)/shard_map/mix_late/pallas_call | solution.py:413
  32.0 1.3 %collective-permute-done.16 = bf16[64,8,128]{2,1,0:T(8,128)(2,1)S(1)} collective-permute-done((bf16[64,8,128]{2,1,0:T(8,128)(2,1)S(1)}, bf16[64,8,128]{2,1,0:T(8,128)(2,1)S(1)}, u32[]{:S(2)}, u32[]{:S(2)}) %collective-permute-start.16) | collective-permute-done | bytes 131104 | tf_op jit(solution)/shard_map/ppermute | solution.py:422
  33.4 1.4 %finish_project.1 = (bf16[512,128]{1,0:T(8,128)(2,1)S(1)}, bf16[512,128]{1,0:T(8,128)(2,1)S(1)}, bf16[512,128]{1,0:T(8,128)(2,1)S(1)}, bf16[512,128]{1,0:T(8,128...) custom-call(s32[1]{0:T(128)} %bitcast.refs_0_.core_ref, bf16[512,128]{1,0:T(8,128)(2,1)S(1)} %bitcast.43, ...), custom_call_target="tpu_custom_call" | custom-call | tf_op jit(solution)/shard_map/finish_project/pallas_call | solution.py:425
  35.0 0.4 collective-permute-start.18
  35.4 0.8 %collective-permute-done.17 = bf16[512,128]{1,0:T(8,128)(2,1)S(1)} collective-permute-done((bf16[512,128]{1,0:T(8,128)(2,1)S(1)}, bf16[512,128]{1,0:T(8,128)(2,1)S(1)}, u32[]{:S(2)}, u32[]{:S(2)}) %collective-permute-start.17) | collective-permute-done | bytes 131104 | tf_op jit(solution)/shard_map/ppermute | solution.py:437
  36.3 1.0 %scatter_start.3 = (f32[32,128,128]{2,1,0:T(8,128)S(1)}, bf16[32,16,128]{2,1,0:T(8,128)(2,1)S(1)}, bf16[32,16,128]{2,1,0:T(8,128)(2,1)S(1)}) custom-call(s32[8]{0:T(128)S(1)} %stack.35.chips_ref, bf16[64,8,128]{2,1,0:T(8,128)(2,1)S(1)} %bitcast.35, bf16[64,8,128]{2,1,0:T(8,128)(2,1)S(1)} %bitcast.39, bf16[64,8,128]{2,1,0:T(8,128)(2,1)S(1)} %bitcast.37, ...), custom_call_target="tpu_custom_call" | custom-call | tf_op jit(solution)/shard_map/scatter_start/pallas_call | solution.py:449
  37.4 0.9 %collective-permute-start.29 = (bf16[32,16,128]{2,1,0:T(8,128)(2,1)S(1)}, bf16[32,16,128]{2,1,0:T(8,128)(2,1)S(1)}, u32[]{:S(2)}, u32[]{:S(2)}) collective-permute-start(bf16[32,16,128]{2,1,0:T(8,128)(2,1)S(1)} %get-tuple-element.52), channel_id=1, source_target_pairs={{0,2},{1,3},{4,0},{5,1},{8,4},{9,5},{12,8},{13,9},{14,12},{15,13},... | collective-permute-start | bytes 393224 | tf_op jit(solution)/shard_map/ppermute | solution.py:383
  38.3 1.0 %scatter_start.2 = (f32[32,128,128]{2,1,0:T(8,128)S(1)}, bf16[32,16,128]{2,1,0:T(8,128)(2,1)S(1)}, bf16[32,16,128]{2,1,0:T(8,128)(2,1)S(1)}) custom-call(s32[8]{0:T(128)S(1)} %stack.35.chips_ref, bf16[64,8,128]{2,1,0:T(8,128)(2,1)S(1)} %bitcast.36, bf16[64,8,128]{2,1,0:T(8,128)(2,1)S(1)} %bitcast.40, bf16[64,8,128]{2,1,0:T(8,128)(2,1)S(1)} %bitcast.38, ...), custom_call_target="tpu_custom_call" | custom-call | tf_op jit(solution)/shard_map/scatter_start/pallas_call | solution.py:449
  39.3 1.3 %collective-permute-start.19 = (bf16[32,16,128]{2,1,0:T(8,128)(2,1)S(1)}, bf16[32,16,128]{2,1,0:T(8,128)(2,1)S(1)}, u32[]{:S(2)}, u32[]{:S(2)}) collective-permute-start(bf16[32,16,128]{2,1,0:T(8,128)(2,1)S(1)} %get-tuple-element.48), channel_id=1, source_target_pairs={{0,4},{1,5},{4,8},{5,9},{8,12},{9,13},{12,14},{13,15},{14,10},{15,... | collective-permute-start | bytes 393224 | tf_op jit(solution)/shard_map/ppermute | solution.py:383
  40.6 1.6 %collective-permute-start.26 = (bf16[32,16,128]{2,1,0:T(8,128)(2,1)S(1)}, bf16[32,16,128]{2,1,0:T(8,128)(2,1)S(1)}, u32[]{:S(2)}, u32[]{:S(2)}) collective-permute-start(bf16[32,16,128]{2,1,0:T(8,128)(2,1)S(1)} %get-tuple-element.51), channel_id=1, source_target_pairs={{0,4},{1,5},{4,8},{5,9},{8,12},{9,13},{12,14},{13,15},{14,10},{15,... | collective-permute-start | bytes 393224 | tf_op jit(solution)/shard_map/ppermute | solution.py:383
  42.2 0.4 collective-permute-start.23
  42.6 0.6 collective-permute-done.29.got_ref
  43.2 0.6 scatter_add.17
  43.8 0.9 %collective-permute-start.30 = (bf16[32,16,128]{2,1,0:T(8,128)(2,1)S(1)}, bf16[32,16,128]{2,1,0:T(8,128)(2,1)S(1)}, u32[]{:S(2)}, u32[]{:S(2)}) collective-permute-start(bf16[32,16,128]{2,1,0:T(8,128)(2,1)S(1)} %scatter_add.17), channel_id=1, source_target_pairs={{0,2},{1,3},{4,0},{5,1},{8,4},{9,5},{12,8},{13,9},{14,12},{15,13},... | collective-permute-start | bytes 393224 | tf_op jit(solution)/shard_map/ppermute | solution.py:383
  44.6 1.1 %collective-permute-done.19.got_ref = bf16[32,16,128]{2,1,0:T(8,128)(2,1)S(1)} collective-permute-done((bf16[32,16,128]{2,1,0:T(8,128)(2,1)S(1)}, bf16[32,16,128]{2,1,0:T(8,128)(2,1)S(1)}, u32[]{:S(2)}, u32[]{:S(2)}) %collective-permute-start.19) | collective-permute-done | bytes 131104 | tf_op jit(solution)/shard_map/ppermute | solution.py:383
  45.7 0.6 scatter_add.10
  46.3 1.3 %collective-permute-start.20 = (bf16[32,16,128]{2,1,0:T(8,128)(2,1)S(1)}, bf16[32,16,128]{2,1,0:T(8,128)(2,1)S(1)}, u32[]{:S(2)}, u32[]{:S(2)}) collective-permute-start(bf16[32,16,128]{2,1,0:T(8,128)(2,1)S(1)} %scatter_add.10), channel_id=1, source_target_pairs={{0,4},{1,5},{4,8},{5,9},{8,12},{9,13},{12,14},{13,15},{14,10},{15,... | collective-permute-start | bytes 393224 | tf_op jit(solution)/shard_map/ppermute | solution.py:383
  47.6 0.4 collective-permute-done.26.got_ref
  48.0 0.6 scatter_add.15
  48.5 1.3 %collective-permute-start.27 = (bf16[32,16,128]{2,1,0:T(8,128)(2,1)S(1)}, bf16[32,16,128]{2,1,0:T(8,128)(2,1)S(1)}, u32[]{:S(2)}, u32[]{:S(2)}) collective-permute-start(bf16[32,16,128]{2,1,0:T(8,128)(2,1)S(1)} %scatter_add.15), channel_id=1, source_target_pairs={{0,4},{1,5},{4,8},{5,9},{8,12},{9,13},{12,14},{13,15},{14,10},{15,... | collective-permute-start | bytes 393224 | tf_op jit(solution)/shard_map/ppermute | solution.py:383
  49.8 0.6 scatter_add.13
  50.4 0.9 %collective-permute-start.24 = (bf16[32,16,128]{2,1,0:T(8,128)(2,1)S(1)}, bf16[32,16,128]{2,1,0:T(8,128)(2,1)S(1)}, u32[]{:S(2)}, u32[]{:S(2)}) collective-permute-start(bf16[32,16,128]{2,1,0:T(8,128)(2,1)S(1)} %scatter_add.13), channel_id=1, source_target_pairs={{0,2},{1,3},{4,0},{5,1},{8,4},{9,5},{12,8},{13,9},{14,12},{15,13},... | collective-permute-start | bytes 393224 | tf_op jit(solution)/shard_map/ppermute | solution.py:383
  51.2 0.6 scatter_add.18
  51.8 1.6 %collective-permute-start.31 = (bf16[32,16,128]{2,1,0:T(8,128)(2,1)S(1)}, bf16[32,16,128]{2,1,0:T(8,128)(2,1)S(1)}, u32[]{:S(2)}, u32[]{:S(2)}) collective-permute-start(bf16[32,16,128]{2,1,0:T(8,128)(2,1)S(1)} %scatter_add.18), channel_id=1, source_target_pairs={{0,2},{1,3},{4,0},{5,1},{8,4},{9,5},{12,8},{13,9},{14,12},{15,13},... | collective-permute-start | bytes 393224 | tf_op jit(solution)/shard_map/ppermute | solution.py:383
  53.5 0.6 scatter_add.11
  54.0 0.5 collective-permute-start.21
  54.5 0.6 scatter_add.16
  55.1 1.6 %collective-permute-start.28 = (bf16[32,16,128]{2,1,0:T(8,128)(2,1)S(1)}, bf16[32,16,128]{2,1,0:T(8,128)(2,1)S(1)}, u32[]{:S(2)}, u32[]{:S(2)}) collective-permute-start(bf16[32,16,128]{2,1,0:T(8,128)(2,1)S(1)} %scatter_add.16), channel_id=1, source_target_pairs={{0,4},{1,5},{4,8},{5,9},{8,12},{9,13},{12,14},{13,15},{14,10},{15,... | collective-permute-start | bytes 393224 | tf_op jit(solution)/shard_map/ppermute | solution.py:383
  56.7 0.6 scatter_add.14
  57.2 0.6 collective-permute-start.25
  57.8 0.6 scatter_add.19
  58.4 1.6 %collective-permute-start.32 = (bf16[32,16,128]{2,1,0:T(8,128)(2,1)S(1)}, bf16[32,16,128]{2,1,0:T(8,128)(2,1)S(1)}, u32[]{:S(2)}, u32[]{:S(2)}) collective-permute-start(bf16[32,16,128]{2,1,0:T(8,128)(2,1)S(1)} %scatter_add.19), channel_id=1, source_target_pairs={{0,2},{1,3},{4,0},{5,1},{8,4},{9,5},{12,8},{13,9},{14,12},{15,13},... | collective-permute-start | bytes 393224 | tf_op jit(solution)/shard_map/ppermute | solution.py:383
  60.0 0.6 scatter_add.12
  60.6 0.5 collective-permute-start.22
  61.1 1.2 %collective-permute-done.25.refs_2_ = bf16[32,16,128]{2,1,0:T(8,128)(2,1)S(1)} collective-permute-done((bf16[32,16,128]{2,1,0:T(8,128)(2,1)S(1)}, bf16[32,16,128]{2,1,0:T(8,128)(2,1)S(1)}, u32[]{:S(2)}, u32[]{:S(2)}) %collective-permute-start.25) | collective-permute-done | bytes 131104 | tf_op jit(solution)/shard_map/ppermute | solution.py:383
  62.3 1.4 %collective-permute-done.32.refs_5_ = bf16[32,16,128]{2,1,0:T(8,128)(2,1)S(1)} collective-permute-done((bf16[32,16,128]{2,1,0:T(8,128)(2,1)S(1)}, bf16[32,16,128]{2,1,0:T(8,128)(2,1)S(1)}, u32[]{:S(2)}, u32[]{:S(2)}) %collective-permute-start.32) | collective-permute-done | bytes 131104 | tf_op jit(solution)/shard_map/ppermute | solution.py:383
  63.7 2.0 %collective-permute-done.22.refs_1_ = bf16[32,16,128]{2,1,0:T(8,128)(2,1)S(1)} collective-permute-done((bf16[32,16,128]{2,1,0:T(8,128)(2,1)S(1)}, bf16[32,16,128]{2,1,0:T(8,128)(2,1)S(1)}, u32[]{:S(2)}, u32[]{:S(2)}) %collective-permute-start.22) | collective-permute-done | bytes 131104 | tf_op jit(solution)/shard_map/ppermute | solution.py:383
  65.6 0.6 scatter_end.1
  66.3 1.3 %collective-permute-done.33 = bf16[64,8,128]{2,1,0:T(8,128)(2,1)S(1)} collective-permute-done((bf16[64,8,128]{2,1,0:T(8,128)(2,1)S(1)}, bf16[64,8,128]{2,1,0:T(8,128)(2,1)S(1)}, u32[]{:S(2)}, u32[]{:S(2)}) %collective-permute-start.33) | collective-permute-done | bytes 131104 | tf_op jit(solution)/shard_map/ppermute | solution.py:478
  67.7 1.3 %finish.1 = bf16[8,128,128]{2,1,0:T(8,128)(2,1)} custom-call(s32[1]{0:T(128)} %bitcast.refs_0_.core_ref, bf16[512,128]{1,0:T(8,128)(2,1)S(1)} %bitcast.44, bf16[512,128]{1,0:T(8,128)(2,1)S(1)} %bitcast.46, bf16[128,1024]{1,0:T(8,128)(2,1)S(1)} %get-tuple-element.55.refs_3_, bf16[128,1024]{1,0:T(8,128)(2,1)S(1)} %get-tuple-element.56.refs_4_, ...), custom_call_target="tpu_custom_call" | custom-call | tf_op jit(solution)/shard_map/finish/pallas_call | solution.py:481
  (33 shorter events, 1.6 us)
Async XLA Ops:
  2.0 12.3 %collective-permute-start.4 = (bf16[512,128]{1,0:T(8,128)(2,1)S(1)}, bf16[512,128]{1,0:T(8,128)(2,1)S(1)}, u32[]{:S(2)}, u32[]{:S(2)}) collective-permute-start(bf16[512,128]{1,0:T(8,128)(2,1)S(1)} %get-tuple-element.33), channel_id=1, source_target_pairs={{0,2},{1,3},{4,0},{5,1},{8,4},{9,5},{12,8},{13,9},{14,12},{15,13},... | collective-permute-start | bytes 393224 | tf_op jit(solution)/shard_map/ppermute | solution.py:383
  5.0 5.0 %collective-permute-start.2 = (bf16[512,128]{1,0:T(8,128)(2,1)S(1)}, bf16[512,128]{1,0:T(8,128)(2,1)S(1)}, u32[]{:S(2)}, u32[]{:S(2)}) collective-permute-start(bf16[512,128]{1,0:T(8,128)(2,1)S(1)} %get-tuple-element.33), channel_id=1, source_target_pairs={{0,4},{1,5},{4,8},{5,9},{8,12},{9,13},{12,14},{13,15},{14,10},{15,... | collective-permute-start | bytes 393224 | tf_op jit(solution)/shard_map/ppermute | solution.py:383
  5.2 21.5 %collective-permute-start = (bf16[512,128]{1,0:T(8,128)(2,1)S(1)}, bf16[512,128]{1,0:T(8,128)(2,1)S(1)}, u32[]{:S(2)}, u32[]{:S(2)}) collective-permute-start(bf16[512,128]{1,0:T(8,128)(2,1)S(1)} %get-tuple-element.32), channel_id=1, source_target_pairs={{0,1},{1,0},{2,3},{3,2},{4,5},{5,4},{6,7},{7,6},{8,9},{9,8},{10,11... | collective-permute-start | bytes 393224 | tf_op jit(solution)/shard_map/ppermute | solution.py:393
  5.2 1.5 %collective-permute-start.1 = (bf16[512,128]{1,0:T(8,128)(2,1)S(1)}, bf16[512,128]{1,0:T(8,128)(2,1)S(1)}, u32[]{:S(2)}, u32[]{:S(2)}) collective-permute-start(bf16[512,128]{1,0:T(8,128)(2,1)S(1)} %get-tuple-element.34), channel_id=1, source_target_pairs={{0,1},{1,0},{2,3},{3,2},{4,5},{5,4},{6,7},{7,6},{8,9},{9,8},{10,11... | collective-permute-start | bytes 393224 | tf_op jit(solution)/shard_map/ppermute | solution.py:392
  6.7 5.9 %collective-permute-start.5 = (bf16[512,128]{1,0:T(8,128)(2,1)S(1)}, bf16[512,128]{1,0:T(8,128)(2,1)S(1)}, u32[]{:S(2)}, u32[]{:S(2)}) collective-permute-start(bf16[512,128]{1,0:T(8,128)(2,1)S(1)} %collective-permute-done.1), channel_id=1, source_target_pairs={{0,2},{1,3},{4,0},{5,1},{8,4},{9,5},{12,8},{13,9},{14,12},{15,13},... | collective-permute-start | bytes 393224 | tf_op jit(solution)/shard_map/ppermute | solution.py:383
  8.6 7.4 %collective-permute-start.3 = (bf16[512,128]{1,0:T(8,128)(2,1)S(1)}, bf16[512,128]{1,0:T(8,128)(2,1)S(1)}, u32[]{:S(2)}, u32[]{:S(2)}) collective-permute-start(bf16[512,128]{1,0:T(8,128)(2,1)S(1)} %collective-permute-done.1), channel_id=1, source_target_pairs={{0,4},{1,5},{4,8},{5,9},{8,12},{9,13},{12,14},{13,15},{14,10},{15,... | collective-permute-start | bytes 393224 | tf_op jit(solution)/shard_map/ppermute | solution.py:383
  10.0 6.9 %collective-permute-start.6 = (bf16[512,128]{1,0:T(8,128)(2,1)S(1)}, bf16[512,128]{1,0:T(8,128)(2,1)S(1)}, u32[]{:S(2)}, u32[]{:S(2)}) collective-permute-start(bf16[512,128]{1,0:T(8,128)(2,1)S(1)} %collective-permute-done.2), channel_id=1, source_target_pairs={{0,4},{1,5},{4,8},{5,9},{8,12},{9,13},{12,14},{13,15},{14,10},{15,... | collective-permute-start | bytes 393224 | tf_op jit(solution)/shard_map/ppermute | solution.py:383
  12.6 6.4 %collective-permute-start.9 = (bf16[512,128]{1,0:T(8,128)(2,1)S(1)}, bf16[512,128]{1,0:T(8,128)(2,1)S(1)}, u32[]{:S(2)}, u32[]{:S(2)}) collective-permute-start(bf16[512,128]{1,0:T(8,128)(2,1)S(1)} %collective-permute-done.5), channel_id=1, source_target_pairs={{0,2},{1,3},{4,0},{5,1},{8,4},{9,5},{12,8},{13,9},{14,12},{15,13},... | collective-permute-start | bytes 393224 | tf_op jit(solution)/shard_map/ppermute | solution.py:383
  14.3 7.5 %collective-permute-start.8 = (bf16[512,128]{1,0:T(8,128)(2,1)S(1)}, bf16[512,128]{1,0:T(8,128)(2,1)S(1)}, u32[]{:S(2)}, u32[]{:S(2)}) collective-permute-start(bf16[512,128]{1,0:T(8,128)(2,1)S(1)} %collective-permute-done.4), channel_id=1, source_target_pairs={{0,2},{1,3},{4,0},{5,1},{8,4},{9,5},{12,8},{13,9},{14,12},{15,13},... | collective-permute-start | bytes 393224 | tf_op jit(solution)/shard_map/ppermute | solution.py:383
  16.0 7.5 %collective-permute-start.7 = (bf16[512,128]{1,0:T(8,128)(2,1)S(1)}, bf16[512,128]{1,0:T(8,128)(2,1)S(1)}, u32[]{:S(2)}, u32[]{:S(2)}) collective-permute-start(bf16[512,128]{1,0:T(8,128)(2,1)S(1)} %collective-permute-done.3), channel_id=1, source_target_pairs={{0,4},{1,5},{4,8},{5,9},{8,12},{9,13},{12,14},{13,15},{14,10},{15,... | collective-permute-start | bytes 393224 | tf_op jit(solution)/shard_map/ppermute | solution.py:383
  16.9 7.0 %collective-permute-start.10 = (bf16[512,128]{1,0:T(8,128)(2,1)S(1)}, bf16[512,128]{1,0:T(8,128)(2,1)S(1)}, u32[]{:S(2)}, u32[]{:S(2)}) collective-permute-start(bf16[512,128]{1,0:T(8,128)(2,1)S(1)} %collective-permute-done.6), channel_id=1, source_target_pairs={{0,4},{1,5},{4,8},{5,9},{8,12},{9,13},{12,14},{13,15},{14,10},{15,... | collective-permute-start | bytes 393224 | tf_op jit(solution)/shard_map/ppermute | solution.py:383
  19.0 6.6 %collective-permute-start.13 = (bf16[512,128]{1,0:T(8,128)(2,1)S(1)}, bf16[512,128]{1,0:T(8,128)(2,1)S(1)}, u32[]{:S(2)}, u32[]{:S(2)}) collective-permute-start(bf16[512,128]{1,0:T(8,128)(2,1)S(1)} %collective-permute-done.9), channel_id=1, source_target_pairs={{0,2},{1,3},{4,0},{5,1},{8,4},{9,5},{12,8},{13,9},{14,12},{15,13},... | collective-permute-start | bytes 393224 | tf_op jit(solution)/shard_map/ppermute | solution.py:383
  21.8 5.9 %collective-permute-start.12 = (bf16[512,128]{1,0:T(8,128)(2,1)S(1)}, bf16[512,128]{1,0:T(8,128)(2,1)S(1)}, u32[]{:S(2)}, u32[]{:S(2)}) collective-permute-start(bf16[512,128]{1,0:T(8,128)(2,1)S(1)} %collective-permute-done.8), channel_id=1, source_target_pairs={{0,2},{1,3},{4,0},{5,1},{8,4},{9,5},{12,8},{13,9},{14,12},{15,13},... | collective-permute-start | bytes 393224 | tf_op jit(solution)/shard_map/ppermute | solution.py:383
  23.5 5.0 %collective-permute-start.11 = (bf16[512,128]{1,0:T(8,128)(2,1)S(1)}, bf16[512,128]{1,0:T(8,128)(2,1)S(1)}, u32[]{:S(2)}, u32[]{:S(2)}) collective-permute-start(bf16[512,128]{1,0:T(8,128)(2,1)S(1)} %collective-permute-done.7), channel_id=1, source_target_pairs={{0,4},{1,5},{4,8},{5,9},{8,12},{9,13},{12,14},{13,15},{14,10},{15,... | collective-permute-start | bytes 393224 | tf_op jit(solution)/shard_map/ppermute | solution.py:383
  23.9 6.0 %collective-permute-start.14 = (bf16[512,128]{1,0:T(8,128)(2,1)S(1)}, bf16[512,128]{1,0:T(8,128)(2,1)S(1)}, u32[]{:S(2)}, u32[]{:S(2)}) collective-permute-start(bf16[512,128]{1,0:T(8,128)(2,1)S(1)} %collective-permute-done.10), channel_id=1, source_target_pairs={{0,4},{1,5},{4,8},{5,9},{8,12},{9,13},{12,14},{13,15},{14,10},{15,... | collective-permute-start | bytes 393224 | tf_op jit(solution)/shard_map/ppermute | solution.py:383
  25.7 5.0 %collective-permute-start.15 = (bf16[512,128]{1,0:T(8,128)(2,1)S(1)}, bf16[512,128]{1,0:T(8,128)(2,1)S(1)}, u32[]{:S(2)}, u32[]{:S(2)}) collective-permute-start(bf16[512,128]{1,0:T(8,128)(2,1)S(1)} %collective-permute-done.13), channel_id=1, source_target_pairs={{0,2},{1,3},{4,0},{5,1},{8,4},{9,5},{12,8},{13,9},{14,12},{15,13},... | collective-permute-start | bytes 393224 | tf_op jit(solution)/shard_map/ppermute | solution.py:383
  32.0 1.4 %collective-permute-start.16 = (bf16[64,8,128]{2,1,0:T(8,128)(2,1)S(1)}, bf16[64,8,128]{2,1,0:T(8,128)(2,1)S(1)}, u32[]{:S(2)}, u32[]{:S(2)}) collective-permute-start(bf16[64,8,128]{2,1,0:T(8,128)(2,1)S(1)} %get-tuple-element.36), channel_id=1, source_target_pairs={{0,1},{1,0},{2,3},{3,2},{4,5},{5,4},{6,7},{7,6},{8,9},{9,8},{10,11... | collective-permute-start | bytes 393224 | tf_op jit(solution)/shard_map/ppermute | solution.py:422
  34.7 1.4 %collective-permute-start.17 = (bf16[512,128]{1,0:T(8,128)(2,1)S(1)}, bf16[512,128]{1,0:T(8,128)(2,1)S(1)}, u32[]{:S(2)}, u32[]{:S(2)}) collective-permute-start(bf16[512,128]{1,0:T(8,128)(2,1)S(1)} %get-tuple-element.44), channel_id=1, source_target_pairs={{0,1},{1,0},{2,3},{3,2},{4,5},{5,4},{6,7},{7,6},{8,9},{9,8},{10,11... | collective-permute-start | bytes 393224 | tf_op jit(solution)/shard_map/ppermute | solution.py:437
  35.0 1.4 %collective-permute-start.18 = (bf16[512,128]{1,0:T(8,128)(2,1)S(1)}, bf16[512,128]{1,0:T(8,128)(2,1)S(1)}, u32[]{:S(2)}, u32[]{:S(2)}) collective-permute-start(bf16[512,128]{1,0:T(8,128)(2,1)S(1)} %get-tuple-element.46), channel_id=1, source_target_pairs={{0,1},{1,0},{2,3},{3,2},{4,5},{5,4},{6,7},{7,6},{8,9},{9,8},{10,11... | collective-permute-start | bytes 393224 | tf_op jit(solution)/shard_map/ppermute | solution.py:438
  37.4 5.8 %collective-permute-start.29 = (bf16[32,16,128]{2,1,0:T(8,128)(2,1)S(1)}, bf16[32,16,128]{2,1,0:T(8,128)(2,1)S(1)}, u32[]{:S(2)}, u32[]{:S(2)}) collective-permute-start(bf16[32,16,128]{2,1,0:T(8,128)(2,1)S(1)} %get-tuple-element.52), channel_id=1, source_target_pairs={{0,2},{1,3},{4,0},{5,1},{8,4},{9,5},{12,8},{13,9},{14,12},{15,13},... | collective-permute-start | bytes 393224 | tf_op jit(solution)/shard_map/ppermute | solution.py:383
  39.3 6.4 %collective-permute-start.19 = (bf16[32,16,128]{2,1,0:T(8,128)(2,1)S(1)}, bf16[32,16,128]{2,1,0:T(8,128)(2,1)S(1)}, u32[]{:S(2)}, u32[]{:S(2)}) collective-permute-start(bf16[32,16,128]{2,1,0:T(8,128)(2,1)S(1)} %get-tuple-element.48), channel_id=1, source_target_pairs={{0,4},{1,5},{4,8},{5,9},{8,12},{9,13},{12,14},{13,15},{14,10},{15,... | collective-permute-start | bytes 393224 | tf_op jit(solution)/shard_map/ppermute | solution.py:383
  40.6 7.4 %collective-permute-start.26 = (bf16[32,16,128]{2,1,0:T(8,128)(2,1)S(1)}, bf16[32,16,128]{2,1,0:T(8,128)(2,1)S(1)}, u32[]{:S(2)}, u32[]{:S(2)}) collective-permute-start(bf16[32,16,128]{2,1,0:T(8,128)(2,1)S(1)} %get-tuple-element.51), channel_id=1, source_target_pairs={{0,4},{1,5},{4,8},{5,9},{8,12},{9,13},{12,14},{13,15},{14,10},{15,... | collective-permute-start | bytes 393224 | tf_op jit(solution)/shard_map/ppermute | solution.py:383
  42.2 7.6 %collective-permute-start.23 = (bf16[32,16,128]{2,1,0:T(8,128)(2,1)S(1)}, bf16[32,16,128]{2,1,0:T(8,128)(2,1)S(1)}, u32[]{:S(2)}, u32[]{:S(2)}) collective-permute-start(bf16[32,16,128]{2,1,0:T(8,128)(2,1)S(1)} %get-tuple-element.49), channel_id=1, source_target_pairs={{0,2},{1,3},{4,0},{5,1},{8,4},{9,5},{12,8},{13,9},{14,12},{15,13},... | collective-permute-start | bytes 393224 | tf_op jit(solution)/shard_map/ppermute | solution.py:383
  43.8 7.5 %collective-permute-start.30 = (bf16[32,16,128]{2,1,0:T(8,128)(2,1)S(1)}, bf16[32,16,128]{2,1,0:T(8,128)(2,1)S(1)}, u32[]{:S(2)}, u32[]{:S(2)}) collective-permute-start(bf16[32,16,128]{2,1,0:T(8,128)(2,1)S(1)} %scatter_add.17), channel_id=1, source_target_pairs={{0,2},{1,3},{4,0},{5,1},{8,4},{9,5},{12,8},{13,9},{14,12},{15,13},... | collective-permute-start | bytes 393224 | tf_op jit(solution)/shard_map/ppermute | solution.py:383
  46.3 7.1 %collective-permute-start.20 = (bf16[32,16,128]{2,1,0:T(8,128)(2,1)S(1)}, bf16[32,16,128]{2,1,0:T(8,128)(2,1)S(1)}, u32[]{:S(2)}, u32[]{:S(2)}) collective-permute-start(bf16[32,16,128]{2,1,0:T(8,128)(2,1)S(1)} %scatter_add.10), channel_id=1, source_target_pairs={{0,4},{1,5},{4,8},{5,9},{8,12},{9,13},{12,14},{13,15},{14,10},{15,... | collective-permute-start | bytes 393224 | tf_op jit(solution)/shard_map/ppermute | solution.py:383
  48.5 6.0 %collective-permute-start.27 = (bf16[32,16,128]{2,1,0:T(8,128)(2,1)S(1)}, bf16[32,16,128]{2,1,0:T(8,128)(2,1)S(1)}, u32[]{:S(2)}, u32[]{:S(2)}) collective-permute-start(bf16[32,16,128]{2,1,0:T(8,128)(2,1)S(1)} %scatter_add.15), channel_id=1, source_target_pairs={{0,4},{1,5},{4,8},{5,9},{8,12},{9,13},{12,14},{13,15},{14,10},{15,... | collective-permute-start | bytes 393224 | tf_op jit(solution)/shard_map/ppermute | solution.py:383
  50.4 6.3 %collective-permute-start.24 = (bf16[32,16,128]{2,1,0:T(8,128)(2,1)S(1)}, bf16[32,16,128]{2,1,0:T(8,128)(2,1)S(1)}, u32[]{:S(2)}, u32[]{:S(2)}) collective-permute-start(bf16[32,16,128]{2,1,0:T(8,128)(2,1)S(1)} %scatter_add.13), channel_id=1, source_target_pairs={{0,2},{1,3},{4,0},{5,1},{8,4},{9,5},{12,8},{13,9},{14,12},{15,13},... | collective-permute-start | bytes 393224 | tf_op jit(solution)/shard_map/ppermute | solution.py:383
  51.8 6.0 %collective-permute-start.31 = (bf16[32,16,128]{2,1,0:T(8,128)(2,1)S(1)}, bf16[32,16,128]{2,1,0:T(8,128)(2,1)S(1)}, u32[]{:S(2)}, u32[]{:S(2)}) collective-permute-start(bf16[32,16,128]{2,1,0:T(8,128)(2,1)S(1)} %scatter_add.18), channel_id=1, source_target_pairs={{0,2},{1,3},{4,0},{5,1},{8,4},{9,5},{12,8},{13,9},{14,12},{15,13},... | collective-permute-start | bytes 393224 | tf_op jit(solution)/shard_map/ppermute | solution.py:383
  54.0 6.0 %collective-permute-start.21 = (bf16[32,16,128]{2,1,0:T(8,128)(2,1)S(1)}, bf16[32,16,128]{2,1,0:T(8,128)(2,1)S(1)}, u32[]{:S(2)}, u32[]{:S(2)}) collective-permute-start(bf16[32,16,128]{2,1,0:T(8,128)(2,1)S(1)} %scatter_add.11), channel_id=1, source_target_pairs={{0,4},{1,5},{4,8},{5,9},{8,12},{9,13},{12,14},{13,15},{14,10},{15,... | collective-permute-start | bytes 393224 | tf_op jit(solution)/shard_map/ppermute | solution.py:383
  55.1 6.0 %collective-permute-start.28 = (bf16[32,16,128]{2,1,0:T(8,128)(2,1)S(1)}, bf16[32,16,128]{2,1,0:T(8,128)(2,1)S(1)}, u32[]{:S(2)}, u32[]{:S(2)}) collective-permute-start(bf16[32,16,128]{2,1,0:T(8,128)(2,1)S(1)} %scatter_add.16), channel_id=1, source_target_pairs={{0,4},{1,5},{4,8},{5,9},{8,12},{9,13},{12,14},{13,15},{14,10},{15,... | collective-permute-start | bytes 393224 | tf_op jit(solution)/shard_map/ppermute | solution.py:383
  57.2 5.0 %collective-permute-start.25 = (bf16[32,16,128]{2,1,0:T(8,128)(2,1)S(1)}, bf16[32,16,128]{2,1,0:T(8,128)(2,1)S(1)}, u32[]{:S(2)}, u32[]{:S(2)}) collective-permute-start(bf16[32,16,128]{2,1,0:T(8,128)(2,1)S(1)} %scatter_add.14), channel_id=1, source_target_pairs={{0,2},{1,3},{4,0},{5,1},{8,4},{9,5},{12,8},{13,9},{14,12},{15,13},... | collective-permute-start | bytes 393224 | tf_op jit(solution)/shard_map/ppermute | solution.py:383
  58.4 5.3 %collective-permute-start.32 = (bf16[32,16,128]{2,1,0:T(8,128)(2,1)S(1)}, bf16[32,16,128]{2,1,0:T(8,128)(2,1)S(1)}, u32[]{:S(2)}, u32[]{:S(2)}) collective-permute-start(bf16[32,16,128]{2,1,0:T(8,128)(2,1)S(1)} %scatter_add.19), channel_id=1, source_target_pairs={{0,2},{1,3},{4,0},{5,1},{8,4},{9,5},{12,8},{13,9},{14,12},{15,13},... | collective-permute-start | bytes 393224 | tf_op jit(solution)/shard_map/ppermute | solution.py:383
  60.6 5.0 %collective-permute-start.22 = (bf16[32,16,128]{2,1,0:T(8,128)(2,1)S(1)}, bf16[32,16,128]{2,1,0:T(8,128)(2,1)S(1)}, u32[]{:S(2)}, u32[]{:S(2)}) collective-permute-start(bf16[32,16,128]{2,1,0:T(8,128)(2,1)S(1)} %scatter_add.12), channel_id=1, source_target_pairs={{0,4},{1,5},{4,8},{5,9},{8,12},{9,13},{12,14},{13,15},{14,10},{15,... | collective-permute-start | bytes 393224 | tf_op jit(solution)/shard_map/ppermute | solution.py:383
  66.3 1.4 %collective-permute-start.33 = (bf16[64,8,128]{2,1,0:T(8,128)(2,1)S(1)}, bf16[64,8,128]{2,1,0:T(8,128)(2,1)S(1)}, u32[]{:S(2)}, u32[]{:S(2)}) collective-permute-start(bf16[64,8,128]{2,1,0:T(8,128)(2,1)S(1)} %get-tuple-element.54), channel_id=1, source_target_pairs={{0,1},{1,0},{2,3},{3,2},{4,5},{5,4},{6,7},{7,6},{8,9},{9,8},{10,11... | collective-permute-start | bytes 393224 | tf_op jit(solution)/shard_map/ppermute | solution.py:478

commit v21 on v20

--- a/solution.py
+++ b/solution.py
@@ -284,40 +284,39 @@
         copy.wait()
 
 
-def chip_rows(chips_ref, distance, count):
-    return pl.ds(pl.multiple_of(chips_ref[distance] * count, count), count)
-
-
-def scatter_start(first, up, down, chips_ref, *refs):
-    own_left, got_left, own_right, got_right, sums_ref, up_ref, down_ref = refs
-    rows = own_left.shape[1]
-    for c in range(sums_ref.shape[0]):
-        left, right = [
-            jnp.concatenate([own[first + c].astype(F32), got[first + c].astype(F32)], axis=0).astype(BF16)
-            for own, got in ((own_left, got_left), (own_right, got_right))
-        ]
-        sums_ref[c] = dot(left, right, TN)
+def scatter_start(first, up, down, order_ref, own_left, got_left, own_right, got_right, sums_ref, up_ref, down_ref):
+    rows, tokens = own_left.shape[1:]
+    count = sums_ref.shape[0]
+
+    def both(own, got, c):
+        return jnp.concatenate([own[first + c].astype(F32), got[first + c].astype(F32)], axis=0).astype(BF16)
+
+    lefts = jnp.concatenate([both(own_left, got_left, c) for c in range(count)], axis=0)
+    lefts = dot(lefts, order_ref[...], NT).astype(BF16).reshape(count, 2 * rows, tokens)
+    for c in range(count):
+        sums_ref[c] = dot(lefts[c], both(own_right, got_right, c), TN)
     for distance, ref in ((up, up_ref), (down, down_ref)):
-        ref[...] = sums_ref[:, chip_rows(chips_ref, distance, 2 * rows), :].astype(BF16)
-
-
-def scatter_add(distance, chips_ref, got_ref, sums_ref, out_ref):
-    here = sums_ref[:, chip_rows(chips_ref, distance, got_ref.shape[1]), :]
-    out_ref[...] = (got_ref[...].astype(F32) + here).astype(BF16)
-
-
-def scatter_end(core_ref, chips_ref, *refs):
+        ref[...] = at_distance(sums_ref, distance, 2 * rows).astype(BF16)
+
+
+def at_distance(sums_ref, distance, count):
+    return sums_ref[:, distance * count : (distance + 1) * count, :]
+
+
+def scatter_add(distance, got_ref, sums_ref, out_ref):
+    out_ref[...] = (got_ref[...].astype(F32) + at_distance(sums_ref, distance, got_ref.shape[1])).astype(BF16)
+
+
+def scatter_end(*refs):
     pieces, (keep_ref, send_ref) = refs[:-2], refs[-2:]
     rows = keep_ref.shape[1]
     first = 0
     for n in range(0, len(pieces), 3):
         sums_ref, up_ref, down_ref = pieces[n : n + 3]
         count = sums_ref.shape[0]
-        sums = sums_ref[:, chip_rows(chips_ref, 0, 2 * rows), :] + up_ref[...].astype(F32) + down_ref[...].astype(F32)
-        halves = sums[:, :rows], sums[:, rows:]
-        first_core = jnp.full(halves[0].shape, core_ref[0]) == 0
-        keep_ref[first : first + count] = jnp.where(first_core, *halves).astype(BF16)
-        send_ref[first : first + count] = jnp.where(first_core, *halves[::-1]).astype(BF16)
+        sums = at_distance(sums_ref, 0, 2 * rows) + up_ref[...].astype(F32) + down_ref[...].astype(F32)
+        keep_ref[first : first + count] = sums[:, :rows].astype(BF16)
+        send_ref[first : first + count] = sums[:, rows:].astype(BF16)
         first += count
 
 
@@ -437,10 +436,7 @@
         got_left = lax.ppermute(other_left, "row", swap)
         got_right = lax.ppermute(other_right, "row", swap)
         operands = [array.reshape(half, rows, tokens) for array in (left, got_left, right, got_right)]
-        chip = lax.axis_index("row") // 2
-        place = jnp.where(chip % 2 == 0, chip // 2, chips - 1 - chip // 2)
-        spots = [place + d - jnp.where(place + d >= chips, chips, 0) for d in range(chips)]
-        chips_at = jnp.stack([jnp.where(2 * p < chips, 2 * p, 2 * (chips - 1 - p) + 1) for p in spots]).astype(jnp.int32)
+        order = token_order(chips, [-d % chips for d in range(chips)], rows)
         size = half // 2
         part_shape = shape((size, 2 * rows, tokens), BF16)
         pieces = []
@@ -449,11 +445,11 @@
             sums, *travelling = pl.pallas_call(
                 functools.partial(scatter_start, piece * size, hops[0], chips - hops[1]),
                 out_shape=(shape((size, tokens, tokens), F32), part_shape, part_shape),
-                in_specs=[smem] + [whole] * 4,
+                in_specs=[whole] * 5,
                 out_specs=(whole,) * 3,
                 compiler_params=params,
                 name="scatter_start",
-            )(chips_at, *operands)
+            )(order, *operands)
             for way, (step, count) in enumerate(zip((1, -1), hops)):
                 for left_over in reversed(range(count)):
                     travelling[way] = along(travelling[way], step)
@@ -461,20 +457,20 @@
                         travelling[way] = pl.pallas_call(
                             functools.partial(scatter_add, step * left_over % chips),
                             out_shape=part_shape,
-                            in_specs=[smem] + [whole] * 2,
+                            in_specs=[whole] * 2,
                             out_specs=whole,
                             compiler_params=params,
                             name="scatter_add",
-                        )(chips_at, travelling[way], sums)
+                        )(travelling[way], sums)
             pieces += [sums, *travelling]
         keep, send = pl.pallas_call(
             scatter_end,
             out_shape=(shape((half, rows, tokens), BF16),) * 2,
-            in_specs=[smem] * 2 + [whole] * len(pieces),
+            in_specs=[whole] * len(pieces),
             out_specs=(whole,) * 2,
             compiler_params=params,
             name="scatter_end",
-        )(core, chips_at, *pieces)
+        )(*pieces)
         merged = (core, keep.reshape(half * rows, tokens), lax.ppermute(send, "row", swap).reshape(half * rows, tokens))
     else:
         merged = (exchange(mix(exchange(results[0]), True)),)

time: 69.1 us -> 65.7 us (0.951)
  Pallas kernels: 15.2 us -> 8.4 us
  waiting for transfers between devices: 20.9 us -> 23.5 us
    pallas_call x10, Pallas kernels: 5.68 us -> 0.25 us  [on_device(): pl.pallas_call(functools.partial(scatter_add, step * left_over % chips),...]
    ppermute x28, waiting for transfers between devices: 16.3 us -> 19.2 us  [along(): return lax.ppermute(array, 'row', pairs)]
    pallas_call x2, Pallas kernels: 2.1 us -> 1.33 us  [on_device(): pl.pallas_call(functools.partial(scatter_start, piece * size, hops[0], ch...]
  transfers between devices with their start and end apart: 34 -> 34, of which waited for: 20 -> 22; matrix products, arithmetic and copies ran while one was open for 1% -> 1% of each run, Pallas kernels for 11% -> 3%
where the time goes in v21:
time: 65.7 us; the launch traced here: 65.5 us
  starting transfers between devices  32.7 us (50%)
  waiting for transfers between devices  23.5 us (36%)
  Pallas kernels  8.4 us (13%)
  other arithmetic  0.72 us (1%)
    ppermute x28, starting transfers between devices, along(): return lax.ppermute(array, 'row', pairs)  31.5 us
    ppermute x28, waiting for transfers between devices, along(): return lax.ppermute(array, 'row', pairs)  19.2 us
    ppermute x2, waiting for transfers between devices, on_device(): lax.ppermute(send, 'row', swap).reshape(half * rows, tokens)  2.61 us
    pallas_call x1, Pallas kernels, on_device(): pl.pallas_call(functools.partial(project_kernel, half if by_core else per...  2 us
    pallas_call x1, Pallas kernels, on_device(): pl.pallas_call(functools.partial(step_kernel, half if by_core else per_gr...  1.38 us
    pallas_call x2, Pallas kernels, on_device(): pl.pallas_call(functools.partial(scatter_start, piece * size, hops[0], ch...  1.33 us
    pallas_call x1, Pallas kernels, on_device(): pl.pallas_call(functools.partial(mix_late, early), out_shape=(shape((half...  1.32 us
  transfers between devices with their start and end apart: 34, of which 22 were waited for; matrix products, arithmetic and copies ran while one was open for 1% of the time, Pallas kernels for 3%

profile of v21, /device:TPU:0, one launch (start us, length us, event | category | flops | bytes accessed | tf_op | source)
XLA Modules:
  0.0 65.5 jit_solution(15657292871457244435)
XLA Ops:
  0.0 2.0 %project.1 = (bf16[512,128]{1,0:T(8,128)(2,1)S(1)}, bf16[512,128]{1,0:T(8,128)(2,1)S(1)}, bf16[512,128]{1,0:T(8,128)(2,1)S(1)}, bf16[512,128]{1,0:T(8,128)(2,1)S...) custom-call(s32[1]{0:T(128)} %bitcast.refs_0_, ...), custom_call_target="tpu_custom_call" | custom-call | tf_op jit(solution)/shard_map/project/pallas_call | solution.py:356
  2.0 3.0 %collective-permute-start.4 = (bf16[512,128]{1,0:T(8,128)(2,1)S(1)}, bf16[512,128]{1,0:T(8,128)(2,1)S(1)}, u32[]{:S(2)}, u32[]{:S(2)}) collective-permute-start(bf16[512,128]{1,0:T(8,128)(2,1)S(1)} %get-tuple-element.33), channel_id=1, source_target_pairs={{0,2},{1,3},{4,0},{5,1},{8,4},{9,5},{12,8},{13,9},{14,12},{15,13},... | collective-permute-start | bytes 393224 | tf_op jit(solution)/shard_map/ppermute | solution.py:382
  5.0 0.1 collective-permute-start.2
  5.2 0.5 collective-permute-start.1
  5.7 1.0 %collective-permute-done.1 = bf16[512,128]{1,0:T(8,128)(2,1)S(1)} collective-permute-done((bf16[512,128]{1,0:T(8,128)(2,1)S(1)}, bf16[512,128]{1,0:T(8,128)(2,1)S(1)}, u32[]{:S(2)}, u32[]{:S(2)}) %collective-permute-start.1) | collective-permute-done | bytes 131104 | tf_op jit(solution)/shard_map/ppermute | solution.py:391
  6.7 1.9 %collective-permute-start.5 = (bf16[512,128]{1,0:T(8,128)(2,1)S(1)}, bf16[512,128]{1,0:T(8,128)(2,1)S(1)}, u32[]{:S(2)}, u32[]{:S(2)}) collective-permute-start(bf16[512,128]{1,0:T(8,128)(2,1)S(1)} %collective-permute-done.1), channel_id=1, source_target_pairs={{0,2},{1,3},{4,0},{5,1},{8,4},{9,5},{12,8},{13,9},{14,12},{15,13},... | collective-permute-start | bytes 393224 | tf_op jit(solution)/shard_map/ppermute | solution.py:382
  8.6 0.2 collective-permute-start.3
  8.8 1.2 %collective-permute-done.2 = bf16[512,128]{1,0:T(8,128)(2,1)S(1)} collective-permute-done((bf16[512,128]{1,0:T(8,128)(2,1)S(1)}, bf16[512,128]{1,0:T(8,128)(2,1)S(1)}, u32[]{:S(2)}, u32[]{:S(2)}) %collective-permute-start.2) | collective-permute-done | bytes 131104 | tf_op jit(solution)/shard_map/ppermute | solution.py:382
  10.0 0.7 %collective-permute-start.6 = (bf16[512,128]{1,0:T(8,128)(2,1)S(1)}, bf16[512,128]{1,0:T(8,128)(2,1)S(1)}, u32[]{:S(2)}, u32[]{:S(2)}) collective-permute-start(bf16[512,128]{1,0:T(8,128)(2,1)S(1)} %collective-permute-done.2), channel_id=1, source_target_pairs={{0,4},{1,5},{4,8},{5,9},{8,12},{9,13},{12,14},{13,15},{14,10},{15,... | collective-permute-start | bytes 393224 | tf_op jit(solution)/shard_map/ppermute | solution.py:382
  10.7 1.9 %collective-permute-done.5 = bf16[512,128]{1,0:T(8,128)(2,1)S(1)} collective-permute-done((bf16[512,128]{1,0:T(8,128)(2,1)S(1)}, bf16[512,128]{1,0:T(8,128)(2,1)S(1)}, u32[]{:S(2)}, u32[]{:S(2)}) %collective-permute-start.5) | collective-permute-done | bytes 131104 | tf_op jit(solution)/shard_map/ppermute | solution.py:382
  12.6 1.7 %collective-permute-start.9 = (bf16[512,128]{1,0:T(8,128)(2,1)S(1)}, bf16[512,128]{1,0:T(8,128)(2,1)S(1)}, u32[]{:S(2)}, u32[]{:S(2)}) collective-permute-start(bf16[512,128]{1,0:T(8,128)(2,1)S(1)} %collective-permute-done.5), channel_id=1, source_target_pairs={{0,2},{1,3},{4,0},{5,1},{8,4},{9,5},{12,8},{13,9},{14,12},{15,13},... | collective-permute-start | bytes 393224 | tf_op jit(solution)/shard_map/ppermute | solution.py:382
  14.3 1.6 %collective-permute-start.8 = (bf16[512,128]{1,0:T(8,128)(2,1)S(1)}, bf16[512,128]{1,0:T(8,128)(2,1)S(1)}, u32[]{:S(2)}, u32[]{:S(2)}) collective-permute-start(bf16[512,128]{1,0:T(8,128)(2,1)S(1)} %collective-permute-done.4), channel_id=1, source_target_pairs={{0,2},{1,3},{4,0},{5,1},{8,4},{9,5},{12,8},{13,9},{14,12},{15,13},... | collective-permute-start | bytes 393224 | tf_op jit(solution)/shard_map/ppermute | solution.py:382
  16.0 0.4 collective-permute-start.7
  16.4 0.5 collective-permute-done.6
  16.9 0.3 collective-permute-start.10
  17.3 1.8 %collective-permute-done.9 = bf16[512,128]{1,0:T(8,128)(2,1)S(1)} collective-permute-done((bf16[512,128]{1,0:T(8,128)(2,1)S(1)}, bf16[512,128]{1,0:T(8,128)(2,1)S(1)}, u32[]{:S(2)}, u32[]{:S(2)}) %collective-permute-start.9) | collective-permute-done | bytes 131104 | tf_op jit(solution)/shard_map/ppermute | solution.py:382
  19.0 1.6 %collective-permute-start.13 = (bf16[512,128]{1,0:T(8,128)(2,1)S(1)}, bf16[512,128]{1,0:T(8,128)(2,1)S(1)}, u32[]{:S(2)}, u32[]{:S(2)}) collective-permute-start(bf16[512,128]{1,0:T(8,128)(2,1)S(1)} %collective-permute-done.9), channel_id=1, source_target_pairs={{0,2},{1,3},{4,0},{5,1},{8,4},{9,5},{12,8},{13,9},{14,12},{15,13},... | collective-permute-start | bytes 393224 | tf_op jit(solution)/shard_map/ppermute | solution.py:382
  20.7 1.2 %collective-permute-done.8 = bf16[512,128]{1,0:T(8,128)(2,1)S(1)} collective-permute-done((bf16[512,128]{1,0:T(8,128)(2,1)S(1)}, bf16[512,128]{1,0:T(8,128)(2,1)S(1)}, u32[]{:S(2)}, u32[]{:S(2)}) %collective-permute-start.8) | collective-permute-done | bytes 131104 | tf_op jit(solution)/shard_map/ppermute | solution.py:382
  21.8 1.6 %collective-permute-start.12 = (bf16[512,128]{1,0:T(8,128)(2,1)S(1)}, bf16[512,128]{1,0:T(8,128)(2,1)S(1)}, u32[]{:S(2)}, u32[]{:S(2)}) collective-permute-start(bf16[512,128]{1,0:T(8,128)(2,1)S(1)} %collective-permute-done.8), channel_id=1, source_target_pairs={{0,2},{1,3},{4,0},{5,1},{8,4},{9,5},{12,8},{13,9},{14,12},{15,13},... | collective-permute-start | bytes 393224 | tf_op jit(solution)/shard_map/ppermute | solution.py:382
  23.5 0.4 collective-permute-start.11
  23.9 1.8 %collective-permute-start.14 = (bf16[512,128]{1,0:T(8,128)(2,1)S(1)}, bf16[512,128]{1,0:T(8,128)(2,1)S(1)}, u32[]{:S(2)}, u32[]{:S(2)}) collective-permute-start(bf16[512,128]{1,0:T(8,128)(2,1)S(1)} %collective-permute-done.10), channel_id=1, source_target_pairs={{0,4},{1,5},{4,8},{5,9},{8,12},{9,13},{12,14},{13,15},{14,10},{15,... | collective-permute-start | bytes 393224 | tf_op jit(solution)/shard_map/ppermute | solution.py:382
  25.7 0.7 %collective-permute-start.15 = (bf16[512,128]{1,0:T(8,128)(2,1)S(1)}, bf16[512,128]{1,0:T(8,128)(2,1)S(1)}, u32[]{:S(2)}, u32[]{:S(2)}) collective-permute-start(bf16[512,128]{1,0:T(8,128)(2,1)S(1)} %collective-permute-done.13), channel_id=1, source_target_pairs={{0,2},{1,3},{4,0},{5,1},{8,4},{9,5},{12,8},{13,9},{14,12},{15,13},... | collective-permute-start | bytes 393224 | tf_op jit(solution)/shard_map/ppermute | solution.py:382
  26.3 0.3 fusion.30.order_ref
  26.7 0.8 %mix_early.1.early_ref = bf16[64,16,128]{2,1,0:T(8,128)(2,1)S(1)} custom-call(bf16[64,8,128]{2,1,0:T(8,128)(2,1)S(1)} %bitcast.39, bf16[64,8,128]{2,1,0:T(8,128)(2,1)S(1)} %bitcast.41, bf16[64,8,128]{2,1,0:T(8,128)(2,1)S(1)} %bitcast.49, bf16[64,8,128]{2,1,0:T(8,128)(2,1)S(1)} %bitcast.52, bf16[64,8,128]{2,1,0:T(8,128)(2,1)S(1)} %bitcast.51, ...), custom_call_target="tpu_custom_call" | custom-call | flops 1000000000 | bytes 4194304 | tf_op jit(solution)/shard_map/mix_early/pallas_call | solution.py:403
  27.5 0.2 collective-permute-done.12
  27.7 0.8 %collective-permute-done.11 = bf16[512,128]{1,0:T(8,128)(2,1)S(1)} collective-permute-done((bf16[512,128]{1,0:T(8,128)(2,1)S(1)}, bf16[512,128]{1,0:T(8,128)(2,1)S(1)}, u32[]{:S(2)}, u32[]{:S(2)}) %collective-permute-start.11) | collective-permute-done | bytes 131104 | tf_op jit(solution)/shard_map/ppermute | solution.py:382
  28.5 1.4 %collective-permute-done.14 = bf16[512,128]{1,0:T(8,128)(2,1)S(1)} collective-permute-done((bf16[512,128]{1,0:T(8,128)(2,1)S(1)}, bf16[512,128]{1,0:T(8,128)(2,1)S(1)}, u32[]{:S(2)}, u32[]{:S(2)}) %collective-permute-start.14) | collective-permute-done | bytes 131104 | tf_op jit(solution)/shard_map/ppermute | solution.py:382
  29.9 0.8 %collective-permute-done.15 = bf16[512,128]{1,0:T(8,128)(2,1)S(1)} collective-permute-done((bf16[512,128]{1,0:T(8,128)(2,1)S(1)}, bf16[512,128]{1,0:T(8,128)(2,1)S(1)}, u32[]{:S(2)}, u32[]{:S(2)}) %collective-permute-start.15) | collective-permute-done | bytes 131104 | tf_op jit(solution)/shard_map/ppermute | solution.py:382
  30.6 1.3 %mix_late.1 = (bf16[64,8,128]{2,1,0:T(8,128)(2,1)S(1)}, bf16[64,8,128]{2,1,0:T(8,128)(2,1)S(1)}) custom-call(bf16[128,128]{1,0:T(8,128)(2,1)S(1)} %fusion.30.order_ref, bf16[64,8,128]{2,1,0:T(8,128)(2,1)S(1)} %bitcast.40, bf16[64,8,128]{2,1,0:T(8,128)(2,1)S(1)} %bitcast.42, bf16[64,16,128]{2,1,0:T(8,128)(2,1)S(1)} %mix_early.1.early_ref, ...), custom_call_target="tpu_custom_call" | custom-call | tf_op jit(solution)/shard_map/mix_late/pallas_call | solution.py:412
  32.1 1.3 %collective-permute-done.16 = bf16[64,8,128]{2,1,0:T(8,128)(2,1)S(1)} collective-permute-done((bf16[64,8,128]{2,1,0:T(8,128)(2,1)S(1)}, bf16[64,8,128]{2,1,0:T(8,128)(2,1)S(1)}, u32[]{:S(2)}, u32[]{:S(2)}) %collective-permute-start.16) | collective-permute-done | bytes 131104 | tf_op jit(solution)/shard_map/ppermute | solution.py:421
  33.3 1.4 %finish_project.1 = (bf16[512,128]{1,0:T(8,128)(2,1)S(1)}, bf16[512,128]{1,0:T(8,128)(2,1)S(1)}, bf16[512,128]{1,0:T(8,128)(2,1)S(1)}, bf16[512,128]{1,0:T(8,128...) custom-call(s32[1]{0:T(128)} %bitcast.refs_0_, bf16[512,128]{1,0:T(8,128)(2,1)S(1)} %bitcast.35, ...), custom_call_target="tpu_custom_call" | custom-call | tf_op jit(solution)/shard_map/finish_project/pallas_call | solution.py:424
  34.7 0.2 collective-permute-start.17
  34.9 0.4 collective-permute-start.18
  35.3 0.3 fusion.31.order_ref
  35.7 0.5 collective-permute-done.17
  36.1 0.2 collective-permute-done.18
  36.3 0.7 %scatter_start.3 = (f32[32,128,128]{2,1,0:T(8,128)S(1)}, bf16[32,16,128]{2,1,0:T(8,128)(2,1)S(1)}, bf16[32,16,128]{2,1,0:T(8,128)(2,1)S(1)}) custom-call(bf16[128,128]{1,0:T(8,128)(2,1)S(1)} %fusion.31.order_ref, bf16[64,8,128]{2,1,0:T(8,128)(2,1)S(1)} %bitcast.27, bf16[64,8,128]{2,1,0:T(8,128)(2,1)S(1)} %bitcast.31, bf16[64,8,128]{2,1,0:T(8,128)(2,1)S(1)} %bitcast.29, ...), custom_call_target="tpu_custom_call" | custom-call | tf_op jit(solution)/shard_map/scatter_start/pallas_call | solution.py:445
  37.0 0.9 %collective-permute-start.29 = (bf16[32,16,128]{2,1,0:T(8,128)(2,1)S(1)}, bf16[32,16,128]{2,1,0:T(8,128)(2,1)S(1)}, u32[]{:S(2)}, u32[]{:S(2)}) collective-permute-start(bf16[32,16,128]{2,1,0:T(8,128)(2,1)S(1)} %get-tuple-element.52), channel_id=1, source_target_pairs={{0,2},{1,3},{4,0},{5,1},{8,4},{9,5},{12,8},{13,9},{14,12},{15,13},... | collective-permute-start | bytes 393224 | tf_op jit(solution)/shard_map/ppermute | solution.py:382
  37.9 0.7 %scatter_start.2 = (f32[32,128,128]{2,1,0:T(8,128)S(1)}, bf16[32,16,128]{2,1,0:T(8,128)(2,1)S(1)}, bf16[32,16,128]{2,1,0:T(8,128)(2,1)S(1)}) custom-call(bf16[128,128]{1,0:T(8,128)(2,1)S(1)} %fusion.31.order_ref, bf16[64,8,128]{2,1,0:T(8,128)(2,1)S(1)} %bitcast.28, bf16[64,8,128]{2,1,0:T(8,128)(2,1)S(1)} %bitcast.32, bf16[64,8,128]{2,1,0:T(8,128)(2,1)S(1)} %bitcast.30, ...), custom_call_target="tpu_custom_call" | custom-call | tf_op jit(solution)/shard_map/scatter_start/pallas_call | solution.py:445
  38.5 1.3 %collective-permute-start.19 = (bf16[32,16,128]{2,1,0:T(8,128)(2,1)S(1)}, bf16[32,16,128]{2,1,0:T(8,128)(2,1)S(1)}, u32[]{:S(2)}, u32[]{:S(2)}) collective-permute-start(bf16[32,16,128]{2,1,0:T(8,128)(2,1)S(1)} %get-tuple-element.48), channel_id=1, source_target_pairs={{0,4},{1,5},{4,8},{5,9},{8,12},{9,13},{12,14},{13,15},{14,10},{15,... | collective-permute-start | bytes 393224 | tf_op jit(solution)/shard_map/ppermute | solution.py:382
  39.8 1.6 %collective-permute-start.26 = (bf16[32,16,128]{2,1,0:T(8,128)(2,1)S(1)}, bf16[32,16,128]{2,1,0:T(8,128)(2,1)S(1)}, u32[]{:S(2)}, u32[]{:S(2)}) collective-permute-start(bf16[32,16,128]{2,1,0:T(8,128)(2,1)S(1)} %get-tuple-element.51), channel_id=1, source_target_pairs={{0,4},{1,5},{4,8},{5,9},{8,12},{9,13},{12,14},{13,15},{14,10},{15,... | collective-permute-start | bytes 393224 | tf_op jit(solution)/shard_map/ppermute | solution.py:382
  41.4 0.5 collective-permute-start.23
  41.8 1.0 %collective-permute-done.29.got_ref = bf16[32,16,128]{2,1,0:T(8,128)(2,1)S(1)} collective-permute-done((bf16[32,16,128]{2,1,0:T(8,128)(2,1)S(1)}, bf16[32,16,128]{2,1,0:T(8,128)(2,1)S(1)}, u32[]{:S(2)}, u32[]{:S(2)}) %collective-permute-start.29) | collective-permute-done | bytes 131104 | tf_op jit(solution)/shard_map/ppermute | solution.py:382
  42.8 0.9 %collective-permute-start.30 = (bf16[32,16,128]{2,1,0:T(8,128)(2,1)S(1)}, bf16[32,16,128]{2,1,0:T(8,128)(2,1)S(1)}, u32[]{:S(2)}, u32[]{:S(2)}) collective-permute-start(bf16[32,16,128]{2,1,0:T(8,128)(2,1)S(1)} %scatter_add.17), channel_id=1, source_target_pairs={{0,2},{1,3},{4,0},{5,1},{8,4},{9,5},{12,8},{13,9},{14,12},{15,13},... | collective-permute-start | bytes 393224 | tf_op jit(solution)/shard_map/ppermute | solution.py:382
  43.7 1.3 %collective-permute-done.19.got_ref = bf16[32,16,128]{2,1,0:T(8,128)(2,1)S(1)} collective-permute-done((bf16[32,16,128]{2,1,0:T(8,128)(2,1)S(1)}, bf16[32,16,128]{2,1,0:T(8,128)(2,1)S(1)}, u32[]{:S(2)}, u32[]{:S(2)}) %collective-permute-start.19) | collective-permute-done | bytes 131104 | tf_op jit(solution)/shard_map/ppermute | solution.py:382
  45.0 1.3 %collective-permute-start.20 = (bf16[32,16,128]{2,1,0:T(8,128)(2,1)S(1)}, bf16[32,16,128]{2,1,0:T(8,128)(2,1)S(1)}, u32[]{:S(2)}, u32[]{:S(2)}) collective-permute-start(bf16[32,16,128]{2,1,0:T(8,128)(2,1)S(1)} %scatter_add.10), channel_id=1, source_target_pairs={{0,4},{1,5},{4,8},{5,9},{8,12},{9,13},{12,14},{13,15},{14,10},{15,... | collective-permute-start | bytes 393224 | tf_op jit(solution)/shard_map/ppermute | solution.py:382
  46.2 1.5 %collective-permute-done.26.got_ref = bf16[32,16,128]{2,1,0:T(8,128)(2,1)S(1)} collective-permute-done((bf16[32,16,128]{2,1,0:T(8,128)(2,1)S(1)}, bf16[32,16,128]{2,1,0:T(8,128)(2,1)S(1)}, u32[]{:S(2)}, u32[]{:S(2)}) %collective-permute-start.26) | collective-permute-done | bytes 131104 | tf_op jit(solution)/shard_map/ppermute | solution.py:382
  47.8 1.3 %collective-permute-start.27 = (bf16[32,16,128]{2,1,0:T(8,128)(2,1)S(1)}, bf16[32,16,128]{2,1,0:T(8,128)(2,1)S(1)}, u32[]{:S(2)}, u32[]{:S(2)}) collective-permute-start(bf16[32,16,128]{2,1,0:T(8,128)(2,1)S(1)} %scatter_add.15), channel_id=1, source_target_pairs={{0,4},{1,5},{4,8},{5,9},{8,12},{9,13},{12,14},{13,15},{14,10},{15,... | collective-permute-start | bytes 393224 | tf_op jit(solution)/shard_map/ppermute | solution.py:382
  49.1 0.9 %collective-permute-start.24 = (bf16[32,16,128]{2,1,0:T(8,128)(2,1)S(1)}, bf16[32,16,128]{2,1,0:T(8,128)(2,1)S(1)}, u32[]{:S(2)}, u32[]{:S(2)}) collective-permute-start(bf16[32,16,128]{2,1,0:T(8,128)(2,1)S(1)} %scatter_add.13), channel_id=1, source_target_pairs={{0,2},{1,3},{4,0},{5,1},{8,4},{9,5},{12,8},{13,9},{14,12},{15,13},... | collective-permute-start | bytes 393224 | tf_op jit(solution)/shard_map/ppermute | solution.py:382
  50.0 1.6 %collective-permute-start.31 = (bf16[32,16,128]{2,1,0:T(8,128)(2,1)S(1)}, bf16[32,16,128]{2,1,0:T(8,128)(2,1)S(1)}, u32[]{:S(2)}, u32[]{:S(2)}) collective-permute-start(bf16[32,16,128]{2,1,0:T(8,128)(2,1)S(1)} %scatter_add.18), channel_id=1, source_target_pairs={{0,2},{1,3},{4,0},{5,1},{8,4},{9,5},{12,8},{13,9},{14,12},{15,13},... | collective-permute-start | bytes 393224 | tf_op jit(solution)/shard_map/ppermute | solution.py:382
  51.6 0.9 %collective-permute-start.21 = (bf16[32,16,128]{2,1,0:T(8,128)(2,1)S(1)}, bf16[32,16,128]{2,1,0:T(8,128)(2,1)S(1)}, u32[]{:S(2)}, u32[]{:S(2)}) collective-permute-start(bf16[32,16,128]{2,1,0:T(8,128)(2,1)S(1)} %scatter_add.11), channel_id=1, source_target_pairs={{0,4},{1,5},{4,8},{5,9},{8,12},{9,13},{12,14},{13,15},{14,10},{15,... | collective-permute-start | bytes 393224 | tf_op jit(solution)/shard_map/ppermute | solution.py:382
  52.6 1.3 %collective-permute-done.27.got_ref = bf16[32,16,128]{2,1,0:T(8,128)(2,1)S(1)} collective-permute-done((bf16[32,16,128]{2,1,0:T(8,128)(2,1)S(1)}, bf16[32,16,128]{2,1,0:T(8,128)(2,1)S(1)}, u32[]{:S(2)}, u32[]{:S(2)}) %collective-permute-start.27) | collective-permute-done | bytes 131104 | tf_op jit(solution)/shard_map/ppermute | solution.py:382
  53.9 1.7 %collective-permute-start.28 = (bf16[32,16,128]{2,1,0:T(8,128)(2,1)S(1)}, bf16[32,16,128]{2,1,0:T(8,128)(2,1)S(1)}, u32[]{:S(2)}, u32[]{:S(2)}) collective-permute-start(bf16[32,16,128]{2,1,0:T(8,128)(2,1)S(1)} %scatter_add.16), channel_id=1, source_target_pairs={{0,4},{1,5},{4,8},{5,9},{8,12},{9,13},{12,14},{13,15},{14,10},{15,... | collective-permute-start | bytes 393224 | tf_op jit(solution)/shard_map/ppermute | solution.py:382
  55.6 0.5 collective-permute-start.25
  56.1 1.6 %collective-permute-start.32 = (bf16[32,16,128]{2,1,0:T(8,128)(2,1)S(1)}, bf16[32,16,128]{2,1,0:T(8,128)(2,1)S(1)}, u32[]{:S(2)}, u32[]{:S(2)}) collective-permute-start(bf16[32,16,128]{2,1,0:T(8,128)(2,1)S(1)} %scatter_add.19), channel_id=1, source_target_pairs={{0,2},{1,3},{4,0},{5,1},{8,4},{9,5},{12,8},{13,9},{14,12},{15,13},... | collective-permute-start | bytes 393224 | tf_op jit(solution)/shard_map/ppermute | solution.py:382
  57.8 0.6 collective-permute-start.22
  58.3 1.6 %collective-permute-done.28.refs_4_ = bf16[32,16,128]{2,1,0:T(8,128)(2,1)S(1)} collective-permute-done((bf16[32,16,128]{2,1,0:T(8,128)(2,1)S(1)}, bf16[32,16,128]{2,1,0:T(8,128)(2,1)S(1)}, u32[]{:S(2)}, u32[]{:S(2)}) %collective-permute-start.28) | collective-permute-done | bytes 131104 | tf_op jit(solution)/shard_map/ppermute | solution.py:382
  59.9 0.7 %collective-permute-done.25.refs_2_ = bf16[32,16,128]{2,1,0:T(8,128)(2,1)S(1)} collective-permute-done((bf16[32,16,128]{2,1,0:T(8,128)(2,1)S(1)}, bf16[32,16,128]{2,1,0:T(8,128)(2,1)S(1)}, u32[]{:S(2)}, u32[]{:S(2)}) %collective-permute-start.25) | collective-permute-done | bytes 131104 | tf_op jit(solution)/shard_map/ppermute | solution.py:382
  60.6 1.4 %collective-permute-done.32.refs_5_ = bf16[32,16,128]{2,1,0:T(8,128)(2,1)S(1)} collective-permute-done((bf16[32,16,128]{2,1,0:T(8,128)(2,1)S(1)}, bf16[32,16,128]{2,1,0:T(8,128)(2,1)S(1)}, u32[]{:S(2)}, u32[]{:S(2)}) %collective-permute-start.32) | collective-permute-done | bytes 131104 | tf_op jit(solution)/shard_map/ppermute | solution.py:382
  62.0 0.8 %collective-permute-done.22.refs_1_ = bf16[32,16,128]{2,1,0:T(8,128)(2,1)S(1)} collective-permute-done((bf16[32,16,128]{2,1,0:T(8,128)(2,1)S(1)}, bf16[32,16,128]{2,1,0:T(8,128)(2,1)S(1)}, u32[]{:S(2)}, u32[]{:S(2)}) %collective-permute-start.22) | collective-permute-done | bytes 131104 | tf_op jit(solution)/shard_map/ppermute | solution.py:382
  62.8 0.1 scatter_end.1
  62.9 0.1 collective-permute-start.33
  63.0 1.3 %collective-permute-done.33 = bf16[64,8,128]{2,1,0:T(8,128)(2,1)S(1)} collective-permute-done((bf16[64,8,128]{2,1,0:T(8,128)(2,1)S(1)}, bf16[64,8,128]{2,1,0:T(8,128)(2,1)S(1)}, u32[]{:S(2)}, u32[]{:S(2)}) %collective-permute-start.33) | collective-permute-done | bytes 131104 | tf_op jit(solution)/shard_map/ppermute | solution.py:474
  64.3 1.3 %finish.1 = bf16[8,128,128]{2,1,0:T(8,128)(2,1)} custom-call(s32[1]{0:T(128)} %bitcast.refs_0_, bf16[512,128]{1,0:T(8,128)(2,1)S(1)} %bitcast.37, bf16[512,128]{1,0:T(8,128)(2,1)S(1)} %bitcast.38, bf16[128,1024]{1,0:T(8,128)(2,1)S(1)} %get-tuple-element.55.refs_3_, bf16[128,1024]{1,0:T(8,128)(2,1)S(1)} %get-tuple-element.56.refs_4_, ...), custom_call_target="tpu_custom_call" | custom-call | tf_op jit(solution)/shard_map/finish/pallas_call | solution.py:477
  (33 shorter events, 0.4 us)
Async XLA Ops:
  2.0 12.3 %collective-permute-start.4 = (bf16[512,128]{1,0:T(8,128)(2,1)S(1)}, bf16[512,128]{1,0:T(8,128)(2,1)S(1)}, u32[]{:S(2)}, u32[]{:S(2)}) collective-permute-start(bf16[512,128]{1,0:T(8,128)(2,1)S(1)} %get-tuple-element.33), channel_id=1, source_target_pairs={{0,2},{1,3},{4,0},{5,1},{8,4},{9,5},{12,8},{13,9},{14,12},{15,13},... | collective-permute-start | bytes 393224 | tf_op jit(solution)/shard_map/ppermute | solution.py:382
  5.0 5.0 %collective-permute-start.2 = (bf16[512,128]{1,0:T(8,128)(2,1)S(1)}, bf16[512,128]{1,0:T(8,128)(2,1)S(1)}, u32[]{:S(2)}, u32[]{:S(2)}) collective-permute-start(bf16[512,128]{1,0:T(8,128)(2,1)S(1)} %get-tuple-element.33), channel_id=1, source_target_pairs={{0,4},{1,5},{4,8},{5,9},{8,12},{9,13},{12,14},{13,15},{14,10},{15,... | collective-permute-start | bytes 393224 | tf_op jit(solution)/shard_map/ppermute | solution.py:382
  5.2 21.5 %collective-permute-start = (bf16[512,128]{1,0:T(8,128)(2,1)S(1)}, bf16[512,128]{1,0:T(8,128)(2,1)S(1)}, u32[]{:S(2)}, u32[]{:S(2)}) collective-permute-start(bf16[512,128]{1,0:T(8,128)(2,1)S(1)} %get-tuple-element.32), channel_id=1, source_target_pairs={{0,1},{1,0},{2,3},{3,2},{4,5},{5,4},{6,7},{7,6},{8,9},{9,8},{10,11... | collective-permute-start | bytes 393224 | tf_op jit(solution)/shard_map/ppermute | solution.py:392
  5.2 1.5 %collective-permute-start.1 = (bf16[512,128]{1,0:T(8,128)(2,1)S(1)}, bf16[512,128]{1,0:T(8,128)(2,1)S(1)}, u32[]{:S(2)}, u32[]{:S(2)}) collective-permute-start(bf16[512,128]{1,0:T(8,128)(2,1)S(1)} %get-tuple-element.34), channel_id=1, source_target_pairs={{0,1},{1,0},{2,3},{3,2},{4,5},{5,4},{6,7},{7,6},{8,9},{9,8},{10,11... | collective-permute-start | bytes 393224 | tf_op jit(solution)/shard_map/ppermute | solution.py:391
  6.7 5.9 %collective-permute-start.5 = (bf16[512,128]{1,0:T(8,128)(2,1)S(1)}, bf16[512,128]{1,0:T(8,128)(2,1)S(1)}, u32[]{:S(2)}, u32[]{:S(2)}) collective-permute-start(bf16[512,128]{1,0:T(8,128)(2,1)S(1)} %collective-permute-done.1), channel_id=1, source_target_pairs={{0,2},{1,3},{4,0},{5,1},{8,4},{9,5},{12,8},{13,9},{14,12},{15,13},... | collective-permute-start | bytes 393224 | tf_op jit(solution)/shard_map/ppermute | solution.py:382
  8.6 7.4 %collective-permute-start.3 = (bf16[512,128]{1,0:T(8,128)(2,1)S(1)}, bf16[512,128]{1,0:T(8,128)(2,1)S(1)}, u32[]{:S(2)}, u32[]{:S(2)}) collective-permute-start(bf16[512,128]{1,0:T(8,128)(2,1)S(1)} %collective-permute-done.1), channel_id=1, source_target_pairs={{0,4},{1,5},{4,8},{5,9},{8,12},{9,13},{12,14},{13,15},{14,10},{15,... | collective-permute-start | bytes 393224 | tf_op jit(solution)/shard_map/ppermute | solution.py:382
  10.0 6.9 %collective-permute-start.6 = (bf16[512,128]{1,0:T(8,128)(2,1)S(1)}, bf16[512,128]{1,0:T(8,128)(2,1)S(1)}, u32[]{:S(2)}, u32[]{:S(2)}) collective-permute-start(bf16[512,128]{1,0:T(8,128)(2,1)S(1)} %collective-permute-done.2), channel_id=1, source_target_pairs={{0,4},{1,5},{4,8},{5,9},{8,12},{9,13},{12,14},{13,15},{14,10},{15,... | collective-permute-start | bytes 393224 | tf_op jit(solution)/shard_map/ppermute | solution.py:382
  12.6 6.4 %collective-permute-start.9 = (bf16[512,128]{1,0:T(8,128)(2,1)S(1)}, bf16[512,128]{1,0:T(8,128)(2,1)S(1)}, u32[]{:S(2)}, u32[]{:S(2)}) collective-permute-start(bf16[512,128]{1,0:T(8,128)(2,1)S(1)} %collective-permute-done.5), channel_id=1, source_target_pairs={{0,2},{1,3},{4,0},{5,1},{8,4},{9,5},{12,8},{13,9},{14,12},{15,13},... | collective-permute-start | bytes 393224 | tf_op jit(solution)/shard_map/ppermute | solution.py:382
  14.3 7.5 %collective-permute-start.8 = (bf16[512,128]{1,0:T(8,128)(2,1)S(1)}, bf16[512,128]{1,0:T(8,128)(2,1)S(1)}, u32[]{:S(2)}, u32[]{:S(2)}) collective-permute-start(bf16[512,128]{1,0:T(8,128)(2,1)S(1)} %collective-permute-done.4), channel_id=1, source_target_pairs={{0,2},{1,3},{4,0},{5,1},{8,4},{9,5},{12,8},{13,9},{14,12},{15,13},... | collective-permute-start | bytes 393224 | tf_op jit(solution)/shard_map/ppermute | solution.py:382
  16.0 7.5 %collective-permute-start.7 = (bf16[512,128]{1,0:T(8,128)(2,1)S(1)}, bf16[512,128]{1,0:T(8,128)(2,1)S(1)}, u32[]{:S(2)}, u32[]{:S(2)}) collective-permute-start(bf16[512,128]{1,0:T(8,128)(2,1)S(1)} %collective-permute-done.3), channel_id=1, source_target_pairs={{0,4},{1,5},{4,8},{5,9},{8,12},{9,13},{12,14},{13,15},{14,10},{15,... | collective-permute-start | bytes 393224 | tf_op jit(solution)/shard_map/ppermute | solution.py:382
  16.9 7.0 %collective-permute-start.10 = (bf16[512,128]{1,0:T(8,128)(2,1)S(1)}, bf16[512,128]{1,0:T(8,128)(2,1)S(1)}, u32[]{:S(2)}, u32[]{:S(2)}) collective-permute-start(bf16[512,128]{1,0:T(8,128)(2,1)S(1)} %collective-permute-done.6), channel_id=1, source_target_pairs={{0,4},{1,5},{4,8},{5,9},{8,12},{9,13},{12,14},{13,15},{14,10},{15,... | collective-permute-start | bytes 393224 | tf_op jit(solution)/shard_map/ppermute | solution.py:382
  19.0 6.6 %collective-permute-start.13 = (bf16[512,128]{1,0:T(8,128)(2,1)S(1)}, bf16[512,128]{1,0:T(8,128)(2,1)S(1)}, u32[]{:S(2)}, u32[]{:S(2)}) collective-permute-start(bf16[512,128]{1,0:T(8,128)(2,1)S(1)} %collective-permute-done.9), channel_id=1, source_target_pairs={{0,2},{1,3},{4,0},{5,1},{8,4},{9,5},{12,8},{13,9},{14,12},{15,13},... | collective-permute-start | bytes 393224 | tf_op jit(solution)/shard_map/ppermute | solution.py:382
  21.8 5.9 %collective-permute-start.12 = (bf16[512,128]{1,0:T(8,128)(2,1)S(1)}, bf16[512,128]{1,0:T(8,128)(2,1)S(1)}, u32[]{:S(2)}, u32[]{:S(2)}) collective-permute-start(bf16[512,128]{1,0:T(8,128)(2,1)S(1)} %collective-permute-done.8), channel_id=1, source_target_pairs={{0,2},{1,3},{4,0},{5,1},{8,4},{9,5},{12,8},{13,9},{14,12},{15,13},... | collective-permute-start | bytes 393224 | tf_op jit(solution)/shard_map/ppermute | solution.py:382
  23.5 5.0 %collective-permute-start.11 = (bf16[512,128]{1,0:T(8,128)(2,1)S(1)}, bf16[512,128]{1,0:T(8,128)(2,1)S(1)}, u32[]{:S(2)}, u32[]{:S(2)}) collective-permute-start(bf16[512,128]{1,0:T(8,128)(2,1)S(1)} %collective-permute-done.7), channel_id=1, source_target_pairs={{0,4},{1,5},{4,8},{5,9},{8,12},{9,13},{12,14},{13,15},{14,10},{15,... | collective-permute-start | bytes 393224 | tf_op jit(solution)/shard_map/ppermute | solution.py:382
  23.9 6.0 %collective-permute-start.14 = (bf16[512,128]{1,0:T(8,128)(2,1)S(1)}, bf16[512,128]{1,0:T(8,128)(2,1)S(1)}, u32[]{:S(2)}, u32[]{:S(2)}) collective-permute-start(bf16[512,128]{1,0:T(8,128)(2,1)S(1)} %collective-permute-done.10), channel_id=1, source_target_pairs={{0,4},{1,5},{4,8},{5,9},{8,12},{9,13},{12,14},{13,15},{14,10},{15,... | collective-permute-start | bytes 393224 | tf_op jit(solution)/shard_map/ppermute | solution.py:382
  25.7 5.0 %collective-permute-start.15 = (bf16[512,128]{1,0:T(8,128)(2,1)S(1)}, bf16[512,128]{1,0:T(8,128)(2,1)S(1)}, u32[]{:S(2)}, u32[]{:S(2)}) collective-permute-start(bf16[512,128]{1,0:T(8,128)(2,1)S(1)} %collective-permute-done.13), channel_id=1, source_target_pairs={{0,2},{1,3},{4,0},{5,1},{8,4},{9,5},{12,8},{13,9},{14,12},{15,13},... | collective-permute-start | bytes 393224 | tf_op jit(solution)/shard_map/ppermute | solution.py:382
  31.9 1.4 %collective-permute-start.16 = (bf16[64,8,128]{2,1,0:T(8,128)(2,1)S(1)}, bf16[64,8,128]{2,1,0:T(8,128)(2,1)S(1)}, u32[]{:S(2)}, u32[]{:S(2)}) collective-permute-start(bf16[64,8,128]{2,1,0:T(8,128)(2,1)S(1)} %get-tuple-element.36), channel_id=1, source_target_pairs={{0,1},{1,0},{2,3},{3,2},{4,5},{5,4},{6,7},{7,6},{8,9},{9,8},{10,11... | collective-permute-start | bytes 393224 | tf_op jit(solution)/shard_map/ppermute | solution.py:421
  34.7 1.4 %collective-permute-start.17 = (bf16[512,128]{1,0:T(8,128)(2,1)S(1)}, bf16[512,128]{1,0:T(8,128)(2,1)S(1)}, u32[]{:S(2)}, u32[]{:S(2)}) collective-permute-start(bf16[512,128]{1,0:T(8,128)(2,1)S(1)} %get-tuple-element.44), channel_id=1, source_target_pairs={{0,1},{1,0},{2,3},{3,2},{4,5},{5,4},{6,7},{7,6},{8,9},{9,8},{10,11... | collective-permute-start | bytes 393224 | tf_op jit(solution)/shard_map/ppermute | solution.py:436
  34.9 1.4 %collective-permute-start.18 = (bf16[512,128]{1,0:T(8,128)(2,1)S(1)}, bf16[512,128]{1,0:T(8,128)(2,1)S(1)}, u32[]{:S(2)}, u32[]{:S(2)}) collective-permute-start(bf16[512,128]{1,0:T(8,128)(2,1)S(1)} %get-tuple-element.46), channel_id=1, source_target_pairs={{0,1},{1,0},{2,3},{3,2},{4,5},{5,4},{6,7},{7,6},{8,9},{9,8},{10,11... | collective-permute-start | bytes 393224 | tf_op jit(solution)/shard_map/ppermute | solution.py:437
  37.0 5.8 %collective-permute-start.29 = (bf16[32,16,128]{2,1,0:T(8,128)(2,1)S(1)}, bf16[32,16,128]{2,1,0:T(8,128)(2,1)S(1)}, u32[]{:S(2)}, u32[]{:S(2)}) collective-permute-start(bf16[32,16,128]{2,1,0:T(8,128)(2,1)S(1)} %get-tuple-element.52), channel_id=1, source_target_pairs={{0,2},{1,3},{4,0},{5,1},{8,4},{9,5},{12,8},{13,9},{14,12},{15,13},... | collective-permute-start | bytes 393224 | tf_op jit(solution)/shard_map/ppermute | solution.py:382
  38.5 6.4 %collective-permute-start.19 = (bf16[32,16,128]{2,1,0:T(8,128)(2,1)S(1)}, bf16[32,16,128]{2,1,0:T(8,128)(2,1)S(1)}, u32[]{:S(2)}, u32[]{:S(2)}) collective-permute-start(bf16[32,16,128]{2,1,0:T(8,128)(2,1)S(1)} %get-tuple-element.48), channel_id=1, source_target_pairs={{0,4},{1,5},{4,8},{5,9},{8,12},{9,13},{12,14},{13,15},{14,10},{15,... | collective-permute-start | bytes 393224 | tf_op jit(solution)/shard_map/ppermute | solution.py:382
  39.8 8.0 %collective-permute-start.26 = (bf16[32,16,128]{2,1,0:T(8,128)(2,1)S(1)}, bf16[32,16,128]{2,1,0:T(8,128)(2,1)S(1)}, u32[]{:S(2)}, u32[]{:S(2)}) collective-permute-start(bf16[32,16,128]{2,1,0:T(8,128)(2,1)S(1)} %get-tuple-element.51), channel_id=1, source_target_pairs={{0,4},{1,5},{4,8},{5,9},{8,12},{9,13},{12,14},{13,15},{14,10},{15,... | collective-permute-start | bytes 393224 | tf_op jit(solution)/shard_map/ppermute | solution.py:382
  41.4 7.7 %collective-permute-start.23 = (bf16[32,16,128]{2,1,0:T(8,128)(2,1)S(1)}, bf16[32,16,128]{2,1,0:T(8,128)(2,1)S(1)}, u32[]{:S(2)}, u32[]{:S(2)}) collective-permute-start(bf16[32,16,128]{2,1,0:T(8,128)(2,1)S(1)} %get-tuple-element.49), channel_id=1, source_target_pairs={{0,2},{1,3},{4,0},{5,1},{8,4},{9,5},{12,8},{13,9},{14,12},{15,13},... | collective-permute-start | bytes 393224 | tf_op jit(solution)/shard_map/ppermute | solution.py:382
  42.8 7.1 %collective-permute-start.30 = (bf16[32,16,128]{2,1,0:T(8,128)(2,1)S(1)}, bf16[32,16,128]{2,1,0:T(8,128)(2,1)S(1)}, u32[]{:S(2)}, u32[]{:S(2)}) collective-permute-start(bf16[32,16,128]{2,1,0:T(8,128)(2,1)S(1)} %scatter_add.17), channel_id=1, source_target_pairs={{0,2},{1,3},{4,0},{5,1},{8,4},{9,5},{12,8},{13,9},{14,12},{15,13},... | collective-permute-start | bytes 393224 | tf_op jit(solution)/shard_map/ppermute | solution.py:382
  45.0 6.6 %collective-permute-start.20 = (bf16[32,16,128]{2,1,0:T(8,128)(2,1)S(1)}, bf16[32,16,128]{2,1,0:T(8,128)(2,1)S(1)}, u32[]{:S(2)}, u32[]{:S(2)}) collective-permute-start(bf16[32,16,128]{2,1,0:T(8,128)(2,1)S(1)} %scatter_add.10), channel_id=1, source_target_pairs={{0,4},{1,5},{4,8},{5,9},{8,12},{9,13},{12,14},{13,15},{14,10},{15,... | collective-permute-start | bytes 393224 | tf_op jit(solution)/shard_map/ppermute | solution.py:382
  47.8 6.1 %collective-permute-start.27 = (bf16[32,16,128]{2,1,0:T(8,128)(2,1)S(1)}, bf16[32,16,128]{2,1,0:T(8,128)(2,1)S(1)}, u32[]{:S(2)}, u32[]{:S(2)}) collective-permute-start(bf16[32,16,128]{2,1,0:T(8,128)(2,1)S(1)} %scatter_add.15), channel_id=1, source_target_pairs={{0,4},{1,5},{4,8},{5,9},{8,12},{9,13},{12,14},{13,15},{14,10},{15,... | collective-permute-start | bytes 393224 | tf_op jit(solution)/shard_map/ppermute | solution.py:382
  49.1 6.5 %collective-permute-start.24 = (bf16[32,16,128]{2,1,0:T(8,128)(2,1)S(1)}, bf16[32,16,128]{2,1,0:T(8,128)(2,1)S(1)}, u32[]{:S(2)}, u32[]{:S(2)}) collective-permute-start(bf16[32,16,128]{2,1,0:T(8,128)(2,1)S(1)} %scatter_add.13), channel_id=1, source_target_pairs={{0,2},{1,3},{4,0},{5,1},{8,4},{9,5},{12,8},{13,9},{14,12},{15,13},... | collective-permute-start | bytes 393224 | tf_op jit(solution)/shard_map/ppermute | solution.py:382
  50.0 6.1 %collective-permute-start.31 = (bf16[32,16,128]{2,1,0:T(8,128)(2,1)S(1)}, bf16[32,16,128]{2,1,0:T(8,128)(2,1)S(1)}, u32[]{:S(2)}, u32[]{:S(2)}) collective-permute-start(bf16[32,16,128]{2,1,0:T(8,128)(2,1)S(1)} %scatter_add.18), channel_id=1, source_target_pairs={{0,2},{1,3},{4,0},{5,1},{8,4},{9,5},{12,8},{13,9},{14,12},{15,13},... | collective-permute-start | bytes 393224 | tf_op jit(solution)/shard_map/ppermute | solution.py:382
  51.6 6.1 %collective-permute-start.21 = (bf16[32,16,128]{2,1,0:T(8,128)(2,1)S(1)}, bf16[32,16,128]{2,1,0:T(8,128)(2,1)S(1)}, u32[]{:S(2)}, u32[]{:S(2)}) collective-permute-start(bf16[32,16,128]{2,1,0:T(8,128)(2,1)S(1)} %scatter_add.11), channel_id=1, source_target_pairs={{0,4},{1,5},{4,8},{5,9},{8,12},{9,13},{12,14},{13,15},{14,10},{15,... | collective-permute-start | bytes 393224 | tf_op jit(solution)/shard_map/ppermute | solution.py:382
  53.9 6.0 %collective-permute-start.28 = (bf16[32,16,128]{2,1,0:T(8,128)(2,1)S(1)}, bf16[32,16,128]{2,1,0:T(8,128)(2,1)S(1)}, u32[]{:S(2)}, u32[]{:S(2)}) collective-permute-start(bf16[32,16,128]{2,1,0:T(8,128)(2,1)S(1)} %scatter_add.16), channel_id=1, source_target_pairs={{0,4},{1,5},{4,8},{5,9},{8,12},{9,13},{12,14},{13,15},{14,10},{15,... | collective-permute-start | bytes 393224 | tf_op jit(solution)/shard_map/ppermute | solution.py:382
  55.6 5.0 %collective-permute-start.25 = (bf16[32,16,128]{2,1,0:T(8,128)(2,1)S(1)}, bf16[32,16,128]{2,1,0:T(8,128)(2,1)S(1)}, u32[]{:S(2)}, u32[]{:S(2)}) collective-permute-start(bf16[32,16,128]{2,1,0:T(8,128)(2,1)S(1)} %scatter_add.14), channel_id=1, source_target_pairs={{0,2},{1,3},{4,0},{5,1},{8,4},{9,5},{12,8},{13,9},{14,12},{15,13},... | collective-permute-start | bytes 393224 | tf_op jit(solution)/shard_map/ppermute | solution.py:382
  56.1 5.9 %collective-permute-start.32 = (bf16[32,16,128]{2,1,0:T(8,128)(2,1)S(1)}, bf16[32,16,128]{2,1,0:T(8,128)(2,1)S(1)}, u32[]{:S(2)}, u32[]{:S(2)}) collective-permute-start(bf16[32,16,128]{2,1,0:T(8,128)(2,1)S(1)} %scatter_add.19), channel_id=1, source_target_pairs={{0,2},{1,3},{4,0},{5,1},{8,4},{9,5},{12,8},{13,9},{14,12},{15,13},... | collective-permute-start | bytes 393224 | tf_op jit(solution)/shard_map/ppermute | solution.py:382
  57.8 5.0 %collective-permute-start.22 = (bf16[32,16,128]{2,1,0:T(8,128)(2,1)S(1)}, bf16[32,16,128]{2,1,0:T(8,128)(2,1)S(1)}, u32[]{:S(2)}, u32[]{:S(2)}) collective-permute-start(bf16[32,16,128]{2,1,0:T(8,128)(2,1)S(1)} %scatter_add.12), channel_id=1, source_target_pairs={{0,4},{1,5},{4,8},{5,9},{8,12},{9,13},{12,14},{13,15},{14,10},{15,... | collective-permute-start | bytes 393224 | tf_op jit(solution)/shard_map/ppermute | solution.py:382
  62.9 1.4 %collective-permute-start.33 = (bf16[64,8,128]{2,1,0:T(8,128)(2,1)S(1)}, bf16[64,8,128]{2,1,0:T(8,128)(2,1)S(1)}, u32[]{:S(2)}, u32[]{:S(2)}) collective-permute-start(bf16[64,8,128]{2,1,0:T(8,128)(2,1)S(1)} %get-tuple-element.54), channel_id=1, source_target_pairs={{0,1},{1,0},{2,3},{3,2},{4,5},{5,4},{6,7},{7,6},{8,9},{9,8},{10,11... | collective-permute-start | bytes 393224 | tf_op jit(solution)/shard_map/ppermute | solution.py:474

commit v22 on v21

--- a/solution.py
+++ b/solution.py
@@ -160,27 +160,36 @@
     return (token == lane + first).astype(BF16)
 
 
-def gathered_sums(own_ref, got_ref, rights, first_lane, c):
-    _, rows, tokens = own_ref.shape
-    left = jnp.concatenate([own_ref[c].astype(F32), got_ref[c].astype(F32)], axis=0).astype(BF16)
-    blocks = [ref[c].astype(F32) for ref in rights]
-    last = first_lane + len(blocks) * rows
-    empty = [jnp.zeros((n, tokens), F32) for n in (first_lane, tokens - last)]
+def joined(own_ref, got_ref, c):
+    return jnp.concatenate([own_ref[c].astype(F32), got_ref[c].astype(F32)], axis=0).astype(BF16)
+
+
+def join_kernel(own_ref, got_ref, block_ref):
+    for c in range(own_ref.shape[0]):
+        block_ref[c] = joined(own_ref, got_ref, c)
+
+
+def gathered_sums(left, blocks, first):
+    count, tokens = blocks[0].shape
+    empty = [jnp.zeros((n * count, tokens), BF16) for n in (first, tokens // count - first - len(blocks))]
     blocks = [block for block in (empty[0], *blocks, empty[1]) if block.shape[0]]
-    return dot(left, jnp.concatenate(blocks, axis=0).astype(BF16), NT)
+    return dot(left, jnp.concatenate(blocks, axis=0), NT)
 
 
 def mix_early(own_ref, got_ref, *refs):
     rights, early_ref = refs[:-1], refs[-1]
     for c in range(own_ref.shape[0]):
-        early_ref[c] = gathered_sums(own_ref, got_ref, rights, 0, c).astype(BF16)
+        sums = gathered_sums(joined(own_ref, got_ref, c), [ref[c] for ref in rights], 0)
+        early_ref[c] = sums.astype(BF16)
 
 
 def mix_late(early, order_ref, own_ref, got_ref, early_ref, *refs):
-    rights, (keep_ref, send_ref, sums_ref) = refs[:-3], refs[-3:]
+    rights, halves, (keep_ref, send_ref, sums_ref) = refs[:-5], refs[-5:-3], refs[-3:]
     count, rows, tokens = own_ref.shape
+    size = count // 2
     for c in range(count):
-        sums = gathered_sums(own_ref, got_ref, rights, early * rows, c)
+        blocks = [ref[c] for ref in rights] + [halves[c // size][c % size]]
+        sums = gathered_sums(joined(own_ref, got_ref, c), blocks, early)
         sums_ref[2 * rows * c : 2 * rows * (c + 1)] = (sums + early_ref[c].astype(F32)).astype(BF16)
     order = order_ref[...]
     group = 16
@@ -284,40 +293,41 @@
         copy.wait()
 
 
-def scatter_start(first, up, down, order_ref, own_left, got_left, own_right, got_right, sums_ref, up_ref, down_ref):
+def scatter_start(first, distance, order_ref, own_left, got_left, own_right, got_right, sums_ref, far_ref):
     rows, tokens = own_left.shape[1:]
     count = sums_ref.shape[0]
-
-    def both(own, got, c):
-        return jnp.concatenate([own[first + c].astype(F32), got[first + c].astype(F32)], axis=0).astype(BF16)
-
-    lefts = jnp.concatenate([both(own_left, got_left, c) for c in range(count)], axis=0)
+    lefts = jnp.concatenate([joined(own_left, got_left, first + c) for c in range(count)], axis=0)
     lefts = dot(lefts, order_ref[...], NT).astype(BF16).reshape(count, 2 * rows, tokens)
     for c in range(count):
-        sums_ref[c] = dot(lefts[c], both(own_right, got_right, c), TN)
-    for distance, ref in ((up, up_ref), (down, down_ref)):
-        ref[...] = at_distance(sums_ref, distance, 2 * rows).astype(BF16)
+        sums_ref[c] = dot(lefts[c], joined(own_right, got_right, first + c), TN)
+    far_ref[...] = at_distance(sums_ref, distance, 2 * rows).astype(BF16)
 
 
 def at_distance(sums_ref, distance, count):
     return sums_ref[:, distance * count : (distance + 1) * count, :]
 
 
-def scatter_add(distance, got_ref, sums_ref, out_ref):
-    out_ref[...] = (got_ref[...].astype(F32) + at_distance(sums_ref, distance, got_ref.shape[1])).astype(BF16)
-
-
-def scatter_end(*refs):
-    pieces, (keep_ref, send_ref) = refs[:-2], refs[-2:]
+def scatter_add(distance, half, got_ref, *refs):
+    sums_refs, out_ref = refs[:-1], refs[-1]
+    size = sums_refs[0].shape[0]
+    for n, sums_ref in enumerate(sums_refs):
+        sums = at_distance(sums_ref, distance, out_ref.shape[1])
+        if half is None:
+            sums = sums + got_ref[n * size : (n + 1) * size].astype(F32)
+        elif half == n:
+            sums = sums + got_ref[...].astype(F32)
+        out_ref[n * size : (n + 1) * size] = sums.astype(BF16)
+
+
+def scatter_end(up_ref, down_ref, *refs):
+    sums_refs, (keep_ref, send_ref) = refs[:-2], refs[-2:]
     rows = keep_ref.shape[1]
-    first = 0
-    for n in range(0, len(pieces), 3):
-        sums_ref, up_ref, down_ref = pieces[n : n + 3]
-        count = sums_ref.shape[0]
-        sums = at_distance(sums_ref, 0, 2 * rows) + up_ref[...].astype(F32) + down_ref[...].astype(F32)
-        keep_ref[first : first + count] = sums[:, :rows].astype(BF16)
-        send_ref[first : first + count] = sums[:, rows:].astype(BF16)
-        first += count
+    size = sums_refs[0].shape[0]
+    for n, sums_ref in enumerate(sums_refs):
+        part = slice(n * size, (n + 1) * size)
+        sums = at_distance(sums_ref, 0, 2 * rows) + up_ref[part].astype(F32) + down_ref[part].astype(F32)
+        keep_ref[part] = sums[:, :rows].astype(BF16)
+        send_ref[part] = sums[:, rows:].astype(BF16)
 
 
 def on_device(*inputs):
@@ -391,18 +401,25 @@
         got_right = lax.ppermute(other_right, "row", swap)
         got_left = lax.ppermute(other_left, "row", swap)
         middle = chips // 2
-        ups = [rounds(right, 1, middle), rounds(got_right, 1, middle - 1)]
-        downs = [rounds(right, -1, middle - 1), rounds(got_right, -1, middle)]
+        size = half // 2
+        block_shape = shape((half, 2 * rows, tokens), BF16)
+        lefts = [array.reshape(half, rows, tokens) for array in (left, got_left)]
+        block = pl.pallas_call(
+            join_kernel,
+            out_shape=block_shape,
+            in_specs=[whole] * 2,
+            out_specs=whole,
+            compiler_params=params,
+            name="join",
+        )(right.reshape(half, rows, tokens), got_right.reshape(half, rows, tokens))
+        ups, downs = rounds(block, 1, middle - 1), rounds(block, -1, middle - 1)
+        halves = [along(ups[-1][:size], 1), along(downs[-1][size:], -1)]
         distances = sorted(range(chips), key=lambda d: min(d, chips - d))
-        early = 2 * (chips // 2 + 1)
-        rights = [
-            ups[piece][d] if d < len(ups[piece]) else downs[piece][chips - d] for d in distances for piece in range(2)
-        ]
-        rights = [array.reshape(half, rows, tokens) for array in rights]
-        lefts = [array.reshape(half, rows, tokens) for array in (left, got_left)]
+        early = middle + 1
+        rights = [ups[d] if d < middle else downs[chips - d] for d in distances[:-1]]
         first_sums = pl.pallas_call(
             mix_early,
-            out_shape=shape((half, 2 * rows, tokens), BF16),
+            out_shape=block_shape,
             in_specs=[whole] * (2 + early),
             out_specs=whole,
             compiler_params=params,
@@ -412,12 +429,12 @@
         keep, send = pl.pallas_call(
             functools.partial(mix_late, early),
             out_shape=(shape((half, rows, tokens), BF16),) * 2,
-            in_specs=[whole] * (4 + len(rights) - early),
+            in_specs=[whole] * (6 + len(rights) - early),
             out_specs=(whole,) * 2,
             scratch_shapes=[pltpu.VMEM((2 * half * rows, tokens), BF16)],
             compiler_params=params,
             name="mix_late",
-        )(token_order(chips, distances, rows), *lefts, first_sums, *rights[early:])
+        )(token_order(chips, distances, rows), *lefts, first_sums, *rights[early:], *halves)
         merged = (core, keep.reshape(half * rows, tokens), lax.ppermute(send, "row", swap).reshape(half * rows, tokens))
     else:
         merged = (exchange(mix(exchange(results[0]), False)),)
@@ -437,32 +454,33 @@
         got_right = lax.ppermute(other_right, "row", swap)
         operands = [array.reshape(half, rows, tokens) for array in (left, got_left, right, got_right)]
         order = token_order(chips, [-d % chips for d in range(chips)], rows)
-        size = half // 2
-        part_shape = shape((size, 2 * rows, tokens), BF16)
-        pieces = []
+        sums, far = [], []
         for piece in range(2):
-            hops = (middle, middle - 1) if piece == 0 else (middle - 1, middle)
-            sums, *travelling = pl.pallas_call(
-                functools.partial(scatter_start, piece * size, hops[0], chips - hops[1]),
-                out_shape=(shape((size, tokens, tokens), F32), part_shape, part_shape),
+            part = pl.pallas_call(
+                functools.partial(scatter_start, piece * size, middle),
+                out_shape=(shape((size, tokens, tokens), F32), shape((size, 2 * rows, tokens), BF16)),
                 in_specs=[whole] * 5,
-                out_specs=(whole,) * 3,
+                out_specs=(whole,) * 2,
                 compiler_params=params,
                 name="scatter_start",
             )(order, *operands)
-            for way, (step, count) in enumerate(zip((1, -1), hops)):
-                for left_over in reversed(range(count)):
-                    travelling[way] = along(travelling[way], step)
-                    if left_over:
-                        travelling[way] = pl.pallas_call(
-                            functools.partial(scatter_add, step * left_over % chips),
-                            out_shape=part_shape,
-                            in_specs=[whole] * 2,
-                            out_specs=whole,
-                            compiler_params=params,
-                            name="scatter_add",
-                        )(travelling[way], sums)
-            pieces += [sums, *travelling]
+            sums.append(part[0])
+            far.append(part[1])
+        for piece, step in enumerate((1, -1)):
+            for left_over in reversed(range(middle)):
+                far[piece] = along(far[piece], step)
+                if left_over:
+                    far[piece] = pl.pallas_call(
+                        functools.partial(
+                            scatter_add, step * left_over % chips, piece if left_over == middle - 1 else None
+                        ),
+                        out_shape=block_shape,
+                        in_specs=[whole] * 3,
+                        out_specs=whole,
+                        compiler_params=params,
+                        name="scatter_add",
+                    )(far[piece], *sums)
+        pieces = (*far, *sums)
         keep, send = pl.pallas_call(
             scatter_end,
             out_shape=(shape((half, rows, tokens), BF16),) * 2,

time: 65.7 us -> 72.2 us (1.099)
  waiting for transfers between devices: 23.5 us -> 38.5 us
  starting transfers between devices: 32.7 us -> 19.1 us
  other arithmetic: 0.72 us -> 4.86 us
    ppermute x28 -> x16, waiting for transfers between devices: 19.2 us -> 34.4 us  [along(): return lax.ppermute(array, 'row', pairs)]
    ppermute x28 -> x16, starting transfers between devices: 31.5 us -> 17.8 us  [along(): return lax.ppermute(array, 'row', pairs)]
    and x8, other arithmetic: 0.05 us -> 2.88 us  [token_order(): (lane >= start) & (lane < start + rows)]
    convert_element_type x2, other arithmetic: 0.67 us -> 1.41 us  [token_order(): return (token == lane + first).astype(BF16)]
    pallas_call x13 -> x10, Pallas kernels: 2.35 us -> 2.43 us  [the longest x2 1.32 us: on_device(): pl.pallas_call(functools.partial(scatter_start, piece * size, middle), ou...]
  transfers between devices with their start and end apart: 34 -> 22, of which waited for: 22 -> 16; matrix products, arithmetic and copies ran while one was open for 1% -> 7% of each run, Pallas kernels for 3% -> 2%
where the time goes in v22:
time: 72.2 us; the launch traced here: 72 us
  waiting for transfers between devices  38.5 us (53%)
  starting transfers between devices  19.1 us (26%)
  Pallas kernels  9.12 us (13%)
  other arithmetic  4.86 us (7%)
    ppermute x16, waiting for transfers between devices, along(): return lax.ppermute(array, 'row', pairs)  34.4 us
    ppermute x16, starting transfers between devices, along(): return lax.ppermute(array, 'row', pairs)  17.8 us
    and x8, other arithmetic, token_order(): (lane >= start) & (lane < start + rows)  2.88 us
    pallas_call x1, Pallas kernels, on_device(): pl.pallas_call(functools.partial(project_kernel, half if by_core else per...  2.65 us
    ppermute x2, waiting for transfers between devices, on_device(): lax.ppermute(send, 'row', swap).reshape(half * rows, tokens)  2.61 us
  transfers between devices with their start and end apart: 22, of which 16 were waited for; matrix products, arithmetic and copies ran while one was open for 7% of the time, Pallas kernels for 2%

profile of v22, /device:TPU:0, one launch (start us, length us, event | category | flops | bytes accessed | tf_op | source)
XLA Modules:
  0.0 72.0 jit_solution(546012080360271166)
XLA Ops:
  0.0 2.7 %project.1 = (bf16[512,128]{1,0:T(8,128)(2,1)S(1)}, bf16[512,128]{1,0:T(8,128)(2,1)S(1)}, bf16[512,128]{1,0:T(8,128)(2,1)}, bf16[512,128]{1,0:T(8,128)(2,1)S(1)}...) custom-call(s32[1]{0:T(128)} %bitcast.refs_0_, ...), custom_call_target="tpu_custom_call" | custom-call | tf_op jit(solution)/shard_map/project/pallas_call | solution.py:366
  2.7 0.5 collective-permute-start.1
  3.2 0.1 collective-permute-start
  3.3 0.9 %collective-permute-done.1 = bf16[512,128]{1,0:T(8,128)(2,1)S(1)} collective-permute-done((bf16[512,128]{1,0:T(8,128)(2,1)S(1)}, bf16[512,128]{1,0:T(8,128)(2,1)S(1)}, u32[]{:S(2)}, u32[]{:S(2)}) %collective-permute-start.1) | collective-permute-done | bytes 131104 | tf_op jit(solution)/shard_map/ppermute | solution.py:401
  4.2 2.9 %collective-permute-start.3 = (bf16[64,16,128]{2,1,0:T(8,128)(2,1)S(1)}, bf16[64,16,128]{2,1,0:T(8,128)(2,1)S(1)}, u32[]{:S(2)}, u32[]{:S(2)}) collective-permute-start(bf16[64,16,128]{2,1,0:T(8,128)(2,1)S(1)} %join.1.refs_0_), channel_id=1, source_target_pairs={{0,2},{1,3},{4,0},{5,1},{8,4},{9,5},{12,8},{13,9},{14,12},{15,13},... | collective-permute-start | bytes 786440 | tf_op jit(solution)/shard_map/ppermute | solution.py:392
  7.1 0.1 collective-permute-start.2
  7.3 0.6 compare_and_fusion.10
  7.9 0.6 compare_and_fusion.8
  8.5 5.4 %collective-permute-done.3.refs_2_ = bf16[64,16,128]{2,1,0:T(8,128)(2,1)S(1)} collective-permute-done((bf16[64,16,128]{2,1,0:T(8,128)(2,1)S(1)}, bf16[64,16,128]{2,1,0:T(8,128)(2,1)S(1)}, u32[]{:S(2)}, u32[]{:S(2)}) %collective-permute-start.3) | collective-permute-done | bytes 262176 | tf_op jit(solution)/shard_map/ppermute | solution.py:392
  13.8 1.7 %collective-permute-start.5 = (bf16[64,16,128]{2,1,0:T(8,128)(2,1)S(1)}, bf16[64,16,128]{2,1,0:T(8,128)(2,1)S(1)}, u32[]{:S(2)}, u32[]{:S(2)}) collective-permute-start(bf16[64,16,128]{2,1,0:T(8,128)(2,1)S(1)} %collective-permute-done.3.refs_2_), channel_id=1, source_target_pairs={{0,2},{1,3},{4,0},{5,1},{8,4},{9,5},{12,8},{13,9},{14,12},{15,13},... | collective-permute-start | bytes 786440 | tf_op jit(solution)/shard_map/ppermute | solution.py:392
  15.5 0.0 collective-permute-done.2.refs_1_
  15.5 0.3 collective-permute-start.4
  15.9 0.5 compare_and_fusion.14
  16.4 0.6 compare_and_fusion.6
  16.9 0.6 compare_and_fusion.4
  17.5 4.1 %collective-permute-done.5.refs_4_ = bf16[64,16,128]{2,1,0:T(8,128)(2,1)S(1)} collective-permute-done((bf16[64,16,128]{2,1,0:T(8,128)(2,1)S(1)}, bf16[64,16,128]{2,1,0:T(8,128)(2,1)S(1)}, u32[]{:S(2)}, u32[]{:S(2)}) %collective-permute-start.5) | collective-permute-done | bytes 262176 | tf_op jit(solution)/shard_map/ppermute | solution.py:392
  21.7 1.4 %collective-permute-start.7 = (bf16[64,16,128]{2,1,0:T(8,128)(2,1)S(1)}, bf16[64,16,128]{2,1,0:T(8,128)(2,1)S(1)}, u32[]{:S(2)}, u32[]{:S(2)}) collective-permute-start(bf16[64,16,128]{2,1,0:T(8,128)(2,1)S(1)} %collective-permute-done.5.refs_4_), channel_id=1, source_target_pairs={{0,2},{1,3},{4,0},{5,1},{8,4},{9,5},{12,8},{13,9},{14,12},{15,13},... | collective-permute-start | bytes 786440 | tf_op jit(solution)/shard_map/ppermute | solution.py:392
  23.0 0.0 collective-permute-done.4.refs_3_
  23.0 0.7 collective-permute-start.6
  23.7 0.6 compare_select_fusion
  24.3 0.0 copy-start.13
  24.3 0.0 copy-start.15
  24.3 4.3 %collective-permute-done.7.refs_1_ = bf16[64,16,128]{2,1,0:T(8,128)(2,1)S(1)} collective-permute-done((bf16[64,16,128]{2,1,0:T(8,128)(2,1)S(1)}, bf16[64,16,128]{2,1,0:T(8,128)(2,1)S(1)}, u32[]{:S(2)}, u32[]{:S(2)}) %collective-permute-start.7) | collective-permute-done | bytes 262176 | tf_op jit(solution)/shard_map/ppermute | solution.py:392
  28.6 1.1 %collective-permute-start.9 = (bf16[32,16,128]{2,1,0:T(8,128)(2,1)S(1)}, bf16[32,16,128]{2,1,0:T(8,128)(2,1)S(1)}, u32[]{:S(2)}, u32[]{:S(2)}) collective-permute-start(bf16[32,16,128]{2,1,0:T(8,128)(2,1)S(1)} %slice.9), channel_id=1, source_target_pairs={{0,2},{1,3},{4,0},{5,1},{8,4},{9,5},{12,8},{13,9},{14,12},{15,13},... | collective-permute-start | bytes 393224 | tf_op jit(solution)/shard_map/ppermute | solution.py:392
  29.7 0.0 collective-permute-done.6.refs_0_
  29.7 1.1 %collective-permute-start.8 = (bf16[32,16,128]{2,1,0:T(8,128)(2,1)S(1)}, bf16[32,16,128]{2,1,0:T(8,128)(2,1)S(1)}, u32[]{:S(2)}, u32[]{:S(2)}) collective-permute-start(bf16[32,16,128]{2,1,0:T(8,128)(2,1)S(1)} %slice.8), channel_id=1, source_target_pairs={{0,4},{1,5},{4,8},{5,9},{8,12},{9,13},{12,14},{13,15},{14,10},{15,... | collective-permute-start | bytes 393224 | tf_op jit(solution)/shard_map/ppermute | solution.py:392
  30.8 1.1 %fusion.30.order_ref = bf16[128,128]{1,0:T(8,128)(2,1)S(1)} fusion(s32[]{:T(128)S(6)} %sub.222, s32[]{:T(128)S(6)} %sub.221, s32[]{:T(128)S(6)} %sub.220, s32[]{:T(128)S(6)} %sub.219, s32[]{:T(128)S(6)} %sub.218, s32[]{:T(128)S(6)} %sub.217, s32[]{:T(128)S(6)} %sub.216, s32[]{:T(128)S(6)} %sub.215, s32[]{:T(128)S(6)} %sub.214, s32[]{:T(128)S(6)} %sub.213, ...), kind=kLoop, calls=%fused_computation.32 | loop fusion | flops 294912 | bytes 35260 | tf_op jit(solution)/shard_map/convert_element_type | solution.py:160
  31.8 0.0 collective-permute-done
  31.9 0.8 %mix_early.1.early_ref = bf16[64,16,128]{2,1,0:T(8,128)(2,1)S(1)} custom-call(bf16[64,8,128]{2,1,0:T(8,128)(2,1)S(1)} %bitcast.27, bf16[64,8,128]{2,1,0:T(8,128)(2,1)S(1)} %bitcast.29, bf16[64,16,128]{2,1,0:T(8,128)(2,1)S(1)} %join.1.refs_0_, bf16[64,16,128]{2,1,0:T(8,128)(2,1)S(1)} %collective-permute-done.2.refs_1_, ...), custom_call_target="tpu_custom_call" | custom-call | flops 1000000000 | bytes 4194304 | tf_op jit(solution)/shard_map/mix_early/pallas_call | solution.py:420
  32.7 0.0 copy-start.1
  32.7 0.0 copy-start.2
  32.8 0.9 %collective-permute-done.9.refs_3_ = bf16[32,16,128]{2,1,0:T(8,128)(2,1)S(1)} collective-permute-done((bf16[32,16,128]{2,1,0:T(8,128)(2,1)S(1)}, bf16[32,16,128]{2,1,0:T(8,128)(2,1)S(1)}, u32[]{:S(2)}, u32[]{:S(2)}) %collective-permute-start.9) | collective-permute-done | bytes 131104 | tf_op jit(solution)/shard_map/ppermute | solution.py:392
  33.7 1.1 %collective-permute-done.8.refs_2_ = bf16[32,16,128]{2,1,0:T(8,128)(2,1)S(1)} collective-permute-done((bf16[32,16,128]{2,1,0:T(8,128)(2,1)S(1)}, bf16[32,16,128]{2,1,0:T(8,128)(2,1)S(1)}, u32[]{:S(2)}, u32[]{:S(2)}) %collective-permute-start.8) | collective-permute-done | bytes 131104 | tf_op jit(solution)/shard_map/ppermute | solution.py:392
  34.7 1.3 %mix_late.1 = (bf16[64,8,128]{2,1,0:T(8,128)(2,1)S(1)}, bf16[64,8,128]{2,1,0:T(8,128)(2,1)S(1)}) custom-call(bf16[128,128]{1,0:T(8,128)(2,1)S(1)} %fusion.30.order_ref, bf16[64,8,128]{2,1,0:T(8,128)(2,1)S(1)} %bitcast.28, bf16[64,8,128]{2,1,0:T(8,128)(2,1)S(1)} %bitcast.30, bf16[64,16,128]{2,1,0:T(8,128)(2,1)S(1)} %mix_early.1.early_ref, ...), custom_call_target="tpu_custom_call" | custom-call | tf_op jit(solution)/shard_map/mix_late/pallas_call | solution.py:429
  36.1 0.1 collective-permute-start.10
  36.2 1.3 %collective-permute-done.10 = bf16[64,8,128]{2,1,0:T(8,128)(2,1)S(1)} collective-permute-done((bf16[64,8,128]{2,1,0:T(8,128)(2,1)S(1)}, bf16[64,8,128]{2,1,0:T(8,128)(2,1)S(1)}, u32[]{:S(2)}, u32[]{:S(2)}) %collective-permute-start.10) | collective-permute-done | bytes 131104 | tf_op jit(solution)/shard_map/ppermute | solution.py:438
  37.5 1.4 %finish_project.1 = (bf16[512,128]{1,0:T(8,128)(2,1)S(1)}, bf16[512,128]{1,0:T(8,128)(2,1)S(1)}, bf16[512,128]{1,0:T(8,128)(2,1)S(1)}, bf16[512,128]{1,0:T(8,128...) custom-call(s32[1]{0:T(128)} %bitcast.refs_0_, bf16[512,128]{1,0:T(8,128)(2,1)S(1)} %bitcast.21, ...), custom_call_target="tpu_custom_call" | custom-call | tf_op jit(solution)/shard_map/finish_project/pallas_call | solution.py:441
  38.9 0.2 collective-permute-start.11
  39.1 0.4 collective-permute-start.12
  39.5 0.4 fusion.31.order_ref
  39.9 0.4 collective-permute-done.11
  40.3 0.2 collective-permute-done.12
  40.5 0.7 scatter_start.2
  41.1 1.1 %collective-permute-start.13 = (bf16[32,16,128]{2,1,0:T(8,128)(2,1)S(1)}, bf16[32,16,128]{2,1,0:T(8,128)(2,1)S(1)}, u32[]{:S(2)}, u32[]{:S(2)}) collective-permute-start(bf16[32,16,128]{2,1,0:T(8,128)(2,1)S(1)} %get-tuple-element.45), channel_id=1, source_target_pairs={{0,4},{1,5},{4,8},{5,9},{8,12},{9,13},{12,14},{13,15},{14,10},{15,... | collective-permute-start | bytes 393224 | tf_op jit(solution)/shard_map/ppermute | solution.py:392
  42.2 0.7 scatter_start.3
  42.8 1.1 %collective-permute-start.17 = (bf16[32,16,128]{2,1,0:T(8,128)(2,1)S(1)}, bf16[32,16,128]{2,1,0:T(8,128)(2,1)S(1)}, u32[]{:S(2)}, u32[]{:S(2)}) collective-permute-start(bf16[32,16,128]{2,1,0:T(8,128)(2,1)S(1)} %get-tuple-element.48), channel_id=1, source_target_pairs={{0,2},{1,3},{4,0},{5,1},{8,4},{9,5},{12,8},{13,9},{14,12},{15,13},... | collective-permute-start | bytes 393224 | tf_op jit(solution)/shard_map/ppermute | solution.py:392
  43.9 3.0 %collective-permute-done.13.got_ref = bf16[32,16,128]{2,1,0:T(8,128)(2,1)S(1)} collective-permute-done((bf16[32,16,128]{2,1,0:T(8,128)(2,1)S(1)}, bf16[32,16,128]{2,1,0:T(8,128)(2,1)S(1)}, u32[]{:S(2)}, u32[]{:S(2)}) %collective-permute-start.13) | collective-permute-done | bytes 131104 | tf_op jit(solution)/shard_map/ppermute | solution.py:392
  47.0 1.1 %collective-permute-start.14 = (bf16[64,16,128]{2,1,0:T(8,128)(2,1)S(1)}, bf16[64,16,128]{2,1,0:T(8,128)(2,1)S(1)}, u32[]{:S(2)}, u32[]{:S(2)}) collective-permute-start(bf16[64,16,128]{2,1,0:T(8,128)(2,1)S(1)} %scatter_add.6), channel_id=1, source_target_pairs={{0,4},{1,5},{4,8},{5,9},{8,12},{9,13},{12,14},{13,15},{14,10},{15,... | collective-permute-start | bytes 786440 | tf_op jit(solution)/shard_map/ppermute | solution.py:392
  48.0 0.3 collective-permute-done.17.got_ref
  48.4 1.1 %collective-permute-start.18 = (bf16[64,16,128]{2,1,0:T(8,128)(2,1)S(1)}, bf16[64,16,128]{2,1,0:T(8,128)(2,1)S(1)}, u32[]{:S(2)}, u32[]{:S(2)}) collective-permute-start(bf16[64,16,128]{2,1,0:T(8,128)(2,1)S(1)} %scatter_add.9), channel_id=1, source_target_pairs={{0,2},{1,3},{4,0},{5,1},{8,4},{9,5},{12,8},{13,9},{14,12},{15,13},... | collective-permute-start | bytes 786440 | tf_op jit(solution)/shard_map/ppermute | solution.py:392
  49.5 5.3 %collective-permute-done.14.got_ref = bf16[64,16,128]{2,1,0:T(8,128)(2,1)S(1)} collective-permute-done((bf16[64,16,128]{2,1,0:T(8,128)(2,1)S(1)}, bf16[64,16,128]{2,1,0:T(8,128)(2,1)S(1)}, u32[]{:S(2)}, u32[]{:S(2)}) %collective-permute-start.14) | collective-permute-done | bytes 262176 | tf_op jit(solution)/shard_map/ppermute | solution.py:392
  54.8 1.1 %collective-permute-start.15 = (bf16[64,16,128]{2,1,0:T(8,128)(2,1)S(1)}, bf16[64,16,128]{2,1,0:T(8,128)(2,1)S(1)}, u32[]{:S(2)}, u32[]{:S(2)}) collective-permute-start(bf16[64,16,128]{2,1,0:T(8,128)(2,1)S(1)} %scatter_add.7), channel_id=1, source_target_pairs={{0,4},{1,5},{4,8},{5,9},{8,12},{9,13},{12,14},{13,15},{14,10},{15,... | collective-permute-start | bytes 786440 | tf_op jit(solution)/shard_map/ppermute | solution.py:392
  55.8 0.0 collective-permute-done.18.got_ref
  55.9 1.1 %collective-permute-start.19 = (bf16[64,16,128]{2,1,0:T(8,128)(2,1)S(1)}, bf16[64,16,128]{2,1,0:T(8,128)(2,1)S(1)}, u32[]{:S(2)}, u32[]{:S(2)}) collective-permute-start(bf16[64,16,128]{2,1,0:T(8,128)(2,1)S(1)} %scatter_add.10), channel_id=1, source_target_pairs={{0,2},{1,3},{4,0},{5,1},{8,4},{9,5},{12,8},{13,9},{14,12},{15,13},... | collective-permute-start | bytes 786440 | tf_op jit(solution)/shard_map/ppermute | solution.py:392
  57.0 4.7 %collective-permute-done.15.got_ref = bf16[64,16,128]{2,1,0:T(8,128)(2,1)S(1)} collective-permute-done((bf16[64,16,128]{2,1,0:T(8,128)(2,1)S(1)}, bf16[64,16,128]{2,1,0:T(8,128)(2,1)S(1)}, u32[]{:S(2)}, u32[]{:S(2)}) %collective-permute-start.15) | collective-permute-done | bytes 262176 | tf_op jit(solution)/shard_map/ppermute | solution.py:392
  61.7 1.1 %collective-permute-start.16 = (bf16[64,16,128]{2,1,0:T(8,128)(2,1)S(1)}, bf16[64,16,128]{2,1,0:T(8,128)(2,1)S(1)}, u32[]{:S(2)}, u32[]{:S(2)}) collective-permute-start(bf16[64,16,128]{2,1,0:T(8,128)(2,1)S(1)} %scatter_add.8), channel_id=1, source_target_pairs={{0,4},{1,5},{4,8},{5,9},{8,12},{9,13},{12,14},{13,15},{14,10},{15,... | collective-permute-start | bytes 786440 | tf_op jit(solution)/shard_map/ppermute | solution.py:392
  62.8 0.0 collective-permute-done.19.got_ref
  62.8 1.1 %collective-permute-start.20 = (bf16[64,16,128]{2,1,0:T(8,128)(2,1)S(1)}, bf16[64,16,128]{2,1,0:T(8,128)(2,1)S(1)}, u32[]{:S(2)}, u32[]{:S(2)}) collective-permute-start(bf16[64,16,128]{2,1,0:T(8,128)(2,1)S(1)} %scatter_add.11), channel_id=1, source_target_pairs={{0,2},{1,3},{4,0},{5,1},{8,4},{9,5},{12,8},{13,9},{14,12},{15,13},... | collective-permute-start | bytes 786440 | tf_op jit(solution)/shard_map/ppermute | solution.py:392
  63.9 4.2 %collective-permute-done.16.up_ref = bf16[64,16,128]{2,1,0:T(8,128)(2,1)S(1)} collective-permute-done((bf16[64,16,128]{2,1,0:T(8,128)(2,1)S(1)}, bf16[64,16,128]{2,1,0:T(8,128)(2,1)S(1)}, u32[]{:S(2)}, u32[]{:S(2)}) %collective-permute-start.16) | collective-permute-done | bytes 262176 | tf_op jit(solution)/shard_map/ppermute | solution.py:392
  68.1 1.1 %collective-permute-done.20.down_ref = bf16[64,16,128]{2,1,0:T(8,128)(2,1)S(1)} collective-permute-done((bf16[64,16,128]{2,1,0:T(8,128)(2,1)S(1)}, bf16[64,16,128]{2,1,0:T(8,128)(2,1)S(1)}, u32[]{:S(2)}, u32[]{:S(2)}) %collective-permute-start.20) | collective-permute-done | bytes 262176 | tf_op jit(solution)/shard_map/ppermute | solution.py:392
  69.2 0.1 scatter_end.1
  69.3 0.1 collective-permute-start.21
  69.4 1.3 %collective-permute-done.21 = bf16[64,8,128]{2,1,0:T(8,128)(2,1)S(1)} collective-permute-done((bf16[64,8,128]{2,1,0:T(8,128)(2,1)S(1)}, bf16[64,8,128]{2,1,0:T(8,128)(2,1)S(1)}, u32[]{:S(2)}, u32[]{:S(2)}) %collective-permute-start.21) | collective-permute-done | bytes 131104 | tf_op jit(solution)/shard_map/ppermute | solution.py:492
  70.7 1.3 %finish.1 = bf16[8,128,128]{2,1,0:T(8,128)(2,1)} custom-call(s32[1]{0:T(128)} %bitcast.refs_0_, bf16[512,128]{1,0:T(8,128)(2,1)S(1)} %bitcast.23, bf16[512,128]{1,0:T(8,128)(2,1)S(1)} %bitcast.24, bf16[128,1024]{1,0:T(8,128)(2,1)S(1)} %get-tuple-element.51.refs_3_, bf16[128,1024]{1,0:T(8,128)(2,1)S(1)} %get-tuple-element.52.refs_4_, ...), custom_call_target="tpu_custom_call" | custom-call | tf_op jit(solution)/shard_map/finish/pallas_call | solution.py:495
  (42 shorter events, 0.4 us)
Async XLA Ops:
  2.7 1.5 %collective-permute-start.1 = (bf16[512,128]{1,0:T(8,128)(2,1)S(1)}, bf16[512,128]{1,0:T(8,128)(2,1)S(1)}, u32[]{:S(2)}, u32[]{:S(2)}) collective-permute-start(bf16[512,128]{1,0:T(8,128)(2,1)S(1)} %get-tuple-element.32), channel_id=1, source_target_pairs={{0,1},{1,0},{2,3},{3,2},{4,5},{5,4},{6,7},{7,6},{8,9},{9,8},{10,11... | collective-permute-start | bytes 393224 | tf_op jit(solution)/shard_map/ppermute | solution.py:401
  3.2 28.7 %collective-permute-start = (bf16[512,128]{1,0:T(8,128)(2,1)}, bf16[512,128]{1,0:T(8,128)(2,1)S(1)}, u32[]{:S(2)}, u32[]{:S(2)}) collective-permute-start(bf16[512,128]{1,0:T(8,128)(2,1)} %get-tuple-element.30), channel_id=1, source_target_pairs={{0,1},{1,0},{2,3},{3,2},{4,5},{5,4},{6,7},{7,6},{8,9},{9,8},{10,11... | collective-permute-start | bytes 393224 | tf_op jit(solution)/shard_map/ppermute | solution.py:402
  4.2 9.6 %collective-permute-start.3 = (bf16[64,16,128]{2,1,0:T(8,128)(2,1)S(1)}, bf16[64,16,128]{2,1,0:T(8,128)(2,1)S(1)}, u32[]{:S(2)}, u32[]{:S(2)}) collective-permute-start(bf16[64,16,128]{2,1,0:T(8,128)(2,1)S(1)} %join.1.refs_0_), channel_id=1, source_target_pairs={{0,2},{1,3},{4,0},{5,1},{8,4},{9,5},{12,8},{13,9},{14,12},{15,13},... | collective-permute-start | bytes 786440 | tf_op jit(solution)/shard_map/ppermute | solution.py:392
  7.1 8.4 %collective-permute-start.2 = (bf16[64,16,128]{2,1,0:T(8,128)(2,1)S(1)}, bf16[64,16,128]{2,1,0:T(8,128)(2,1)S(1)}, u32[]{:S(2)}, u32[]{:S(2)}) collective-permute-start(bf16[64,16,128]{2,1,0:T(8,128)(2,1)S(1)} %join.1.refs_0_), channel_id=1, source_target_pairs={{0,4},{1,5},{4,8},{5,9},{8,12},{9,13},{12,14},{13,15},{14,10},{15,... | collective-permute-start | bytes 786440 | tf_op jit(solution)/shard_map/ppermute | solution.py:392
  13.8 7.8 %collective-permute-start.5 = (bf16[64,16,128]{2,1,0:T(8,128)(2,1)S(1)}, bf16[64,16,128]{2,1,0:T(8,128)(2,1)S(1)}, u32[]{:S(2)}, u32[]{:S(2)}) collective-permute-start(bf16[64,16,128]{2,1,0:T(8,128)(2,1)S(1)} %collective-permute-done.3.refs_2_), channel_id=1, source_target_pairs={{0,2},{1,3},{4,0},{5,1},{8,4},{9,5},{12,8},{13,9},{14,12},{15,13},... | collective-permute-start | bytes 786440 | tf_op jit(solution)/shard_map/ppermute | solution.py:392
  15.5 7.5 %collective-permute-start.4 = (bf16[64,16,128]{2,1,0:T(8,128)(2,1)S(1)}, bf16[64,16,128]{2,1,0:T(8,128)(2,1)S(1)}, u32[]{:S(2)}, u32[]{:S(2)}) collective-permute-start(bf16[64,16,128]{2,1,0:T(8,128)(2,1)S(1)} %collective-permute-done.2.refs_1_), channel_id=1, source_target_pairs={{0,4},{1,5},{4,8},{5,9},{8,12},{9,13},{12,14},{13,15},{14,10},{15,... | collective-permute-start | bytes 786440 | tf_op jit(solution)/shard_map/ppermute | solution.py:392
  21.7 6.9 %collective-permute-start.7 = (bf16[64,16,128]{2,1,0:T(8,128)(2,1)S(1)}, bf16[64,16,128]{2,1,0:T(8,128)(2,1)S(1)}, u32[]{:S(2)}, u32[]{:S(2)}) collective-permute-start(bf16[64,16,128]{2,1,0:T(8,128)(2,1)S(1)} %collective-permute-done.5.refs_4_), channel_id=1, source_target_pairs={{0,2},{1,3},{4,0},{5,1},{8,4},{9,5},{12,8},{13,9},{14,12},{15,13},... | collective-permute-start | bytes 786440 | tf_op jit(solution)/shard_map/ppermute | solution.py:392
  23.0 6.7 %collective-permute-start.6 = (bf16[64,16,128]{2,1,0:T(8,128)(2,1)S(1)}, bf16[64,16,128]{2,1,0:T(8,128)(2,1)S(1)}, u32[]{:S(2)}, u32[]{:S(2)}) collective-permute-start(bf16[64,16,128]{2,1,0:T(8,128)(2,1)S(1)} %collective-permute-done.4.refs_3_), channel_id=1, source_target_pairs={{0,4},{1,5},{4,8},{5,9},{8,12},{9,13},{12,14},{13,15},{14,10},{15,... | collective-permute-start | bytes 786440 | tf_op jit(solution)/shard_map/ppermute | solution.py:392
  24.3 7.6 %copy-start.9 = (pred[128]{0:T(512)(128)(4,1)}, pred[128]{0:T(512)(128)(4,1)S(1)}, u32[]{:S(2)}) copy-start(pred[128]{0:T(512)(128)(4,1)S(1)} %get-tuple-element.55) | copy-start | bytes 388
  24.3 7.6 %copy-start.11 = (pred[128]{0:T(512)(128)(4,1)}, pred[128]{0:T(512)(128)(4,1)S(1)}, u32[]{:S(2)}) copy-start(pred[128]{0:T(512)(128)(4,1)S(1)} %get-tuple-element.56) | copy-start | bytes 388
  24.3 7.6 %copy-start.13 = (pred[128]{0:T(512)(128)(4,1)}, pred[128]{0:T(512)(128)(4,1)S(1)}, u32[]{:S(2)}) copy-start(pred[128]{0:T(512)(128)(4,1)S(1)} %get-tuple-element.53) | copy-start | bytes 388
  24.3 7.6 %copy-start.15 = (pred[128]{0:T(512)(128)(4,1)}, pred[128]{0:T(512)(128)(4,1)S(1)}, u32[]{:S(2)}) copy-start(pred[128]{0:T(512)(128)(4,1)S(1)} %get-tuple-element.54) | copy-start | bytes 388
  28.6 5.0 %collective-permute-start.9 = (bf16[32,16,128]{2,1,0:T(8,128)(2,1)S(1)}, bf16[32,16,128]{2,1,0:T(8,128)(2,1)S(1)}, u32[]{:S(2)}, u32[]{:S(2)}) collective-permute-start(bf16[32,16,128]{2,1,0:T(8,128)(2,1)S(1)} %slice.9), channel_id=1, source_target_pairs={{0,2},{1,3},{4,0},{5,1},{8,4},{9,5},{12,8},{13,9},{14,12},{15,13},... | collective-permute-start | bytes 393224 | tf_op jit(solution)/shard_map/ppermute | solution.py:392
  29.7 5.0 %collective-permute-start.8 = (bf16[32,16,128]{2,1,0:T(8,128)(2,1)S(1)}, bf16[32,16,128]{2,1,0:T(8,128)(2,1)S(1)}, u32[]{:S(2)}, u32[]{:S(2)}) collective-permute-start(bf16[32,16,128]{2,1,0:T(8,128)(2,1)S(1)} %slice.8), channel_id=1, source_target_pairs={{0,4},{1,5},{4,8},{5,9},{8,12},{9,13},{12,14},{13,15},{14,10},{15,... | collective-permute-start | bytes 393224 | tf_op jit(solution)/shard_map/ppermute | solution.py:392
  32.7 6.8 %copy-start = (pred[128]{0:T(512)(128)(4,1)S(1)}, pred[128]{0:T(512)(128)(4,1)}, u32[]{:S(2)}) copy-start(pred[128]{0:T(512)(128)(4,1)} %get-tuple-element.64) | copy-start | bytes 388
  32.7 6.8 %copy-start.1 = (pred[128]{0:T(512)(128)(4,1)S(1)}, pred[128]{0:T(512)(128)(4,1)}, u32[]{:S(2)}) copy-start(pred[128]{0:T(512)(128)(4,1)} %get-tuple-element.61) | copy-start | bytes 388
  32.7 6.8 %copy-start.2 = (pred[128]{0:T(512)(128)(4,1)S(1)}, pred[128]{0:T(512)(128)(4,1)}, u32[]{:S(2)}) copy-start(pred[128]{0:T(512)(128)(4,1)} %get-tuple-element.62) | copy-start | bytes 388
  32.7 6.7 %copy-start.3 = (pred[128]{0:T(512)(128)(4,1)S(1)}, pred[128]{0:T(512)(128)(4,1)}, u32[]{:S(2)}) copy-start(pred[128]{0:T(512)(128)(4,1)} %compare_and_fusion.14) | copy-start | bytes 388
  32.7 6.7 %copy-start.4 = (pred[128]{0:T(512)(128)(4,1)S(1)}, pred[128]{0:T(512)(128)(4,1)}, u32[]{:S(2)}) copy-start(pred[128]{0:T(512)(128)(4,1)} %get-tuple-element.59) | copy-start | bytes 388
  32.7 6.7 %copy-start.5 = (pred[128]{0:T(512)(128)(4,1)S(1)}, pred[128]{0:T(512)(128)(4,1)}, u32[]{:S(2)}) copy-start(pred[128]{0:T(512)(128)(4,1)} %get-tuple-element.60) | copy-start | bytes 388
  32.7 6.7 %copy-start.6 = (pred[128]{0:T(512)(128)(4,1)S(1)}, pred[128]{0:T(512)(128)(4,1)}, u32[]{:S(2)}) copy-start(pred[128]{0:T(512)(128)(4,1)} %get-tuple-element.57) | copy-start | bytes 388
  32.7 6.7 %copy-start.7 = (pred[128]{0:T(512)(128)(4,1)S(1)}, pred[128]{0:T(512)(128)(4,1)}, u32[]{:S(2)}) copy-start(pred[128]{0:T(512)(128)(4,1)} %get-tuple-element.58) | copy-start | bytes 388
  32.8 6.7 %copy-start.8 = (s32[128]{0:T(128)S(1)}, s32[128]{0:T(128)}, u32[]{:S(2)}) copy-start(s32[128]{0:T(128)} %compare_select_fusion) | copy-start | bytes 1540
  32.8 6.7 %copy-start.10 = (pred[128]{0:T(512)(128)(4,1)S(1)}, pred[128]{0:T(512)(128)(4,1)}, u32[]{:S(2)}) copy-start(pred[128]{0:T(512)(128)(4,1)} %copy-done.9) | copy-start | bytes 388
  32.8 6.7 %copy-start.12 = (pred[128]{0:T(512)(128)(4,1)S(1)}, pred[128]{0:T(512)(128)(4,1)}, u32[]{:S(2)}) copy-start(pred[128]{0:T(512)(128)(4,1)} %copy-done.11) | copy-start | bytes 388
  32.8 6.7 %copy-start.14 = (pred[128]{0:T(512)(128)(4,1)S(1)}, pred[128]{0:T(512)(128)(4,1)}, u32[]{:S(2)}) copy-start(pred[128]{0:T(512)(128)(4,1)} %copy-done.13) | copy-start | bytes 388
  32.8 6.7 %copy-start.16 = (pred[128]{0:T(512)(128)(4,1)S(1)}, pred[128]{0:T(512)(128)(4,1)}, u32[]{:S(2)}) copy-start(pred[128]{0:T(512)(128)(4,1)} %copy-done.15) | copy-start | bytes 388
  36.1 1.4 %collective-permute-start.10 = (bf16[64,8,128]{2,1,0:T(8,128)(2,1)S(1)}, bf16[64,8,128]{2,1,0:T(8,128)(2,1)S(1)}, u32[]{:S(2)}, u32[]{:S(2)}) collective-permute-start(bf16[64,8,128]{2,1,0:T(8,128)(2,1)S(1)} %get-tuple-element.34), channel_id=1, source_target_pairs={{0,1},{1,0},{2,3},{3,2},{4,5},{5,4},{6,7},{7,6},{8,9},{9,8},{10,11... | collective-permute-start | bytes 393224 | tf_op jit(solution)/shard_map/ppermute | solution.py:438
  38.9 1.4 %collective-permute-start.11 = (bf16[512,128]{1,0:T(8,128)(2,1)S(1)}, bf16[512,128]{1,0:T(8,128)(2,1)S(1)}, u32[]{:S(2)}, u32[]{:S(2)}) collective-permute-start(bf16[512,128]{1,0:T(8,128)(2,1)S(1)} %get-tuple-element.42), channel_id=1, source_target_pairs={{0,1},{1,0},{2,3},{3,2},{4,5},{5,4},{6,7},{7,6},{8,9},{9,8},{10,11... | collective-permute-start | bytes 393224 | tf_op jit(solution)/shard_map/ppermute | solution.py:453
  39.1 1.4 %collective-permute-start.12 = (bf16[512,128]{1,0:T(8,128)(2,1)S(1)}, bf16[512,128]{1,0:T(8,128)(2,1)S(1)}, u32[]{:S(2)}, u32[]{:S(2)}) collective-permute-start(bf16[512,128]{1,0:T(8,128)(2,1)S(1)} %get-tuple-element.44), channel_id=1, source_target_pairs={{0,1},{1,0},{2,3},{3,2},{4,5},{5,4},{6,7},{7,6},{8,9},{9,8},{10,11... | collective-permute-start | bytes 393224 | tf_op jit(solution)/shard_map/ppermute | solution.py:454
  41.1 5.8 %collective-permute-start.13 = (bf16[32,16,128]{2,1,0:T(8,128)(2,1)S(1)}, bf16[32,16,128]{2,1,0:T(8,128)(2,1)S(1)}, u32[]{:S(2)}, u32[]{:S(2)}) collective-permute-start(bf16[32,16,128]{2,1,0:T(8,128)(2,1)S(1)} %get-tuple-element.45), channel_id=1, source_target_pairs={{0,4},{1,5},{4,8},{5,9},{8,12},{9,13},{12,14},{13,15},{14,10},{15,... | collective-permute-start | bytes 393224 | tf_op jit(solution)/shard_map/ppermute | solution.py:392
  42.8 5.5 %collective-permute-start.17 = (bf16[32,16,128]{2,1,0:T(8,128)(2,1)S(1)}, bf16[32,16,128]{2,1,0:T(8,128)(2,1)S(1)}, u32[]{:S(2)}, u32[]{:S(2)}) collective-permute-start(bf16[32,16,128]{2,1,0:T(8,128)(2,1)S(1)} %get-tuple-element.48), channel_id=1, source_target_pairs={{0,2},{1,3},{4,0},{5,1},{8,4},{9,5},{12,8},{13,9},{14,12},{15,13},... | collective-permute-start | bytes 393224 | tf_op jit(solution)/shard_map/ppermute | solution.py:392
  47.0 7.8 %collective-permute-start.14 = (bf16[64,16,128]{2,1,0:T(8,128)(2,1)S(1)}, bf16[64,16,128]{2,1,0:T(8,128)(2,1)S(1)}, u32[]{:S(2)}, u32[]{:S(2)}) collective-permute-start(bf16[64,16,128]{2,1,0:T(8,128)(2,1)S(1)} %scatter_add.6), channel_id=1, source_target_pairs={{0,4},{1,5},{4,8},{5,9},{8,12},{9,13},{12,14},{13,15},{14,10},{15,... | collective-permute-start | bytes 786440 | tf_op jit(solution)/shard_map/ppermute | solution.py:392
  48.4 7.5 %collective-permute-start.18 = (bf16[64,16,128]{2,1,0:T(8,128)(2,1)S(1)}, bf16[64,16,128]{2,1,0:T(8,128)(2,1)S(1)}, u32[]{:S(2)}, u32[]{:S(2)}) collective-permute-start(bf16[64,16,128]{2,1,0:T(8,128)(2,1)S(1)} %scatter_add.9), channel_id=1, source_target_pairs={{0,2},{1,3},{4,0},{5,1},{8,4},{9,5},{12,8},{13,9},{14,12},{15,13},... | collective-permute-start | bytes 786440 | tf_op jit(solution)/shard_map/ppermute | solution.py:392
  54.8 6.9 %collective-permute-start.15 = (bf16[64,16,128]{2,1,0:T(8,128)(2,1)S(1)}, bf16[64,16,128]{2,1,0:T(8,128)(2,1)S(1)}, u32[]{:S(2)}, u32[]{:S(2)}) collective-permute-start(bf16[64,16,128]{2,1,0:T(8,128)(2,1)S(1)} %scatter_add.7), channel_id=1, source_target_pairs={{0,4},{1,5},{4,8},{5,9},{8,12},{9,13},{12,14},{13,15},{14,10},{15,... | collective-permute-start | bytes 786440 | tf_op jit(solution)/shard_map/ppermute | solution.py:392
  55.9 6.8 %collective-permute-start.19 = (bf16[64,16,128]{2,1,0:T(8,128)(2,1)S(1)}, bf16[64,16,128]{2,1,0:T(8,128)(2,1)S(1)}, u32[]{:S(2)}, u32[]{:S(2)}) collective-permute-start(bf16[64,16,128]{2,1,0:T(8,128)(2,1)S(1)} %scatter_add.10), channel_id=1, source_target_pairs={{0,2},{1,3},{4,0},{5,1},{8,4},{9,5},{12,8},{13,9},{14,12},{15,13},... | collective-permute-start | bytes 786440 | tf_op jit(solution)/shard_map/ppermute | solution.py:392
  61.7 6.4 %collective-permute-start.16 = (bf16[64,16,128]{2,1,0:T(8,128)(2,1)S(1)}, bf16[64,16,128]{2,1,0:T(8,128)(2,1)S(1)}, u32[]{:S(2)}, u32[]{:S(2)}) collective-permute-start(bf16[64,16,128]{2,1,0:T(8,128)(2,1)S(1)} %scatter_add.8), channel_id=1, source_target_pairs={{0,4},{1,5},{4,8},{5,9},{8,12},{9,13},{12,14},{13,15},{14,10},{15,... | collective-permute-start | bytes 786440 | tf_op jit(solution)/shard_map/ppermute | solution.py:392
  62.8 6.4 %collective-permute-start.20 = (bf16[64,16,128]{2,1,0:T(8,128)(2,1)S(1)}, bf16[64,16,128]{2,1,0:T(8,128)(2,1)S(1)}, u32[]{:S(2)}, u32[]{:S(2)}) collective-permute-start(bf16[64,16,128]{2,1,0:T(8,128)(2,1)S(1)} %scatter_add.11), channel_id=1, source_target_pairs={{0,2},{1,3},{4,0},{5,1},{8,4},{9,5},{12,8},{13,9},{14,12},{15,13},... | collective-permute-start | bytes 786440 | tf_op jit(solution)/shard_map/ppermute | solution.py:392
  69.3 1.4 %collective-permute-start.21 = (bf16[64,8,128]{2,1,0:T(8,128)(2,1)S(1)}, bf16[64,8,128]{2,1,0:T(8,128)(2,1)S(1)}, u32[]{:S(2)}, u32[]{:S(2)}) collective-permute-start(bf16[64,8,128]{2,1,0:T(8,128)(2,1)S(1)} %get-tuple-element.50), channel_id=1, source_target_pairs={{0,1},{1,0},{2,3},{3,2},{4,5},{5,4},{6,7},{7,6},{8,9},{9,8},{10,11... | collective-permute-start | bytes 393224 | tf_op jit(solution)/shard_map/ppermute | solution.py:492

commit v23 on v21

--- a/solution.py
+++ b/solution.py
@@ -147,9 +147,9 @@
     device = lax.axis_index("row")
     chip, core = device // 2, device % 2
     place = jnp.where(chip % 2 == 0, chip // 2, chips - 1 - chip // 2)
-    size = 2 * chips * rows
-    lane, token = (lax.broadcasted_iota(jnp.int32, (size, size), axis) for axis in range(2))
-    first = jnp.zeros((size, size), jnp.int32)
+    extent = (2 * len(distances) * rows, 2 * chips * rows)
+    lane, token = (lax.broadcasted_iota(jnp.int32, extent, axis) for axis in range(2))
+    first = jnp.zeros(extent, jnp.int32)
     for n, d in enumerate(distances):
         source = place - d + jnp.where(place < d, chips, 0)
         source = jnp.where(2 * source < chips, 2 * source, 2 * (chips - 1 - source) + 1)
@@ -160,35 +160,32 @@
     return (token == lane + first).astype(BF16)
 
 
-def gathered_sums(own_ref, got_ref, rights, first_lane, c):
-    _, rows, tokens = own_ref.shape
-    left = jnp.concatenate([own_ref[c].astype(F32), got_ref[c].astype(F32)], axis=0).astype(BF16)
-    blocks = [ref[c].astype(F32) for ref in rights]
-    last = first_lane + len(blocks) * rows
-    empty = [jnp.zeros((n, tokens), F32) for n in (first_lane, tokens - last)]
-    blocks = [block for block in (empty[0], *blocks, empty[1]) if block.shape[0]]
-    return dot(left, jnp.concatenate(blocks, axis=0).astype(BF16), NT)
-
-
-def mix_early(own_ref, got_ref, *refs):
-    rights, early_ref = refs[:-1], refs[-1]
-    for c in range(own_ref.shape[0]):
-        early_ref[c] = gathered_sums(own_ref, got_ref, rights, 0, c).astype(BF16)
-
-
-def mix_late(early, order_ref, own_ref, got_ref, early_ref, *refs):
-    rights, (keep_ref, send_ref, sums_ref) = refs[:-3], refs[-3:]
+def gathered_sums(order_ref, own_ref, got_ref, rights, sums_ref):
     count, rows, tokens = own_ref.shape
     for c in range(count):
-        sums = gathered_sums(own_ref, got_ref, rights, early * rows, c)
-        sums_ref[2 * rows * c : 2 * rows * (c + 1)] = (sums + early_ref[c].astype(F32)).astype(BF16)
+        left = jnp.concatenate([own_ref[c].astype(F32), got_ref[c].astype(F32)], axis=0).astype(BF16)
+        right = jnp.concatenate([ref[c].astype(F32) for ref in rights], axis=0).astype(BF16)
+        sums_ref[2 * rows * c : 2 * rows * (c + 1)] = dot(left, right, NT).astype(BF16)
     order = order_ref[...]
     group = 16
     for first in range(0, count, group):
         sums = dot(sums_ref[2 * rows * first : 2 * rows * (first + group)], order, NN)
-        sums = sums.reshape(group, 2 * rows, tokens)
-        keep_ref[first : first + group] = sums[:, :rows].astype(BF16)
-        send_ref[first : first + group] = sums[:, rows:].astype(BF16)
+        yield slice(first, first + group), sums.reshape(group, 2 * rows, tokens)
+
+
+def mix_early(order_ref, own_ref, got_ref, *refs):
+    rights, (early_ref, sums_ref) = refs[:-2], refs[-2:]
+    for part, sums in gathered_sums(order_ref, own_ref, got_ref, rights, sums_ref):
+        early_ref[part] = sums.astype(BF16)
+
+
+def mix_late(order_ref, own_ref, got_ref, early_ref, *refs):
+    rights, (keep_ref, send_ref, sums_ref) = refs[:-3], refs[-3:]
+    rows = own_ref.shape[1]
+    for part, sums in gathered_sums(order_ref, own_ref, got_ref, rights, sums_ref):
+        sums = sums + early_ref[part].astype(F32)
+        keep_ref[part] = sums[:, :rows].astype(BF16)
+        send_ref[part] = sums[:, rows:].astype(BF16)
 
 
 def finish_rows(emit, rows, channels, tokens, load, pair_t_ref, gate_t_ref, gain, bias, outw_t, unit_scratch):
@@ -403,21 +400,22 @@
         first_sums = pl.pallas_call(
             mix_early,
             out_shape=shape((half, 2 * rows, tokens), BF16),
-            in_specs=[whole] * (2 + early),
+            in_specs=[whole] * (3 + early),
             out_specs=whole,
+            scratch_shapes=[pltpu.VMEM((2 * half * rows, early * rows), BF16)],
             compiler_params=params,
             cost_estimate=pl.CostEstimate(flops=10**9, bytes_accessed=4 * 2**20, transcendentals=0),
             name="mix_early",
-        )(*lefts, *rights[:early])
+        )(token_order(chips, distances[: early // 2], rows), *lefts, *rights[:early])
         keep, send = pl.pallas_call(
-            functools.partial(mix_late, early),
+            mix_late,
             out_shape=(shape((half, rows, tokens), BF16),) * 2,
             in_specs=[whole] * (4 + len(rights) - early),
             out_specs=(whole,) * 2,
-            scratch_shapes=[pltpu.VMEM((2 * half * rows, tokens), BF16)],
+            scratch_shapes=[pltpu.VMEM((2 * half * rows, (len(rights) - early) * rows), BF16)],
             compiler_params=params,
             name="mix_late",
-        )(token_order(chips, distances, rows), *lefts, first_sums, *rights[early:])
+        )(token_order(chips, distances[early // 2 :], rows), *lefts, first_sums, *rights[early:])
         merged = (core, keep.reshape(half * rows, tokens), lax.ppermute(send, "row", swap).reshape(half * rows, tokens))
     else:
         merged = (exchange(mix(exchange(results[0]), False)),)

time: 65.7 us -> 65 us (0.989)
    pallas_call x1, Pallas kernels: 1.32 us -> 0.65 us  [on_device(): pl.pallas_call(mix_late, out_shape=(shape((half, rows, tokens), BF16),) *...]
where the time goes in v23:
time: 65 us; the launch traced here: 64.9 us
  starting transfers between devices  32.7 us (50%)
  waiting for transfers between devices  23.2 us (36%)
  Pallas kernels  7.86 us (12%)
  other arithmetic  0.73 us (1%)
    ppermute x28, starting transfers between devices, along(): return lax.ppermute(array, 'row', pairs)  31.5 us
    ppermute x28, waiting for transfers between devices, along(): return lax.ppermute(array, 'row', pairs)  19.4 us
    ppermute x2, waiting for transfers between devices, on_device(): lax.ppermute(send, 'row', swap).reshape(half * rows, tokens)  2.58 us
    pallas_call x1, Pallas kernels, on_device(): pl.pallas_call(functools.partial(project_kernel, half if by_core else per...  2 us
    pallas_call x1, Pallas kernels, on_device(): pl.pallas_call(functools.partial(step_kernel, half if by_core else per_gr...  1.37 us
    pallas_call x2, Pallas kernels, on_device(): pl.pallas_call(functools.partial(scatter_start, piece * size, hops[0], ch...  1.33 us
  transfers between devices with their start and end apart: 34, of which 22 were waited for; matrix products, arithmetic and copies ran while one was open for 1% of the time, Pallas kernels for 3%

profile of v23, /device:TPU:0, one launch (start us, length us, event | category | flops | bytes accessed | tf_op | source)
XLA Modules:
  0.0 64.9 jit_solution(3306345655361338770)
XLA Ops:
  0.0 2.0 %project.1 = (bf16[512,128]{1,0:T(8,128)(2,1)S(1)}, bf16[512,128]{1,0:T(8,128)(2,1)S(1)}, bf16[512,128]{1,0:T(8,128)(2,1)S(1)}, bf16[512,128]{1,0:T(8,128)(2,1)S...) custom-call(s32[1]{0:T(128)} %bitcast.refs_0_, ...), custom_call_target="tpu_custom_call" | custom-call | tf_op jit(solution)/shard_map/project/pallas_call | solution.py:353
  2.0 3.0 %collective-permute-start.4 = (bf16[512,128]{1,0:T(8,128)(2,1)S(1)}, bf16[512,128]{1,0:T(8,128)(2,1)S(1)}, u32[]{:S(2)}, u32[]{:S(2)}) collective-permute-start(bf16[512,128]{1,0:T(8,128)(2,1)S(1)} %get-tuple-element.33), channel_id=1, source_target_pairs={{0,2},{1,3},{4,0},{5,1},{8,4},{9,5},{12,8},{13,9},{14,12},{15,13},... | collective-permute-start | bytes 393224 | tf_op jit(solution)/shard_map/ppermute | solution.py:379
  5.0 0.1 collective-permute-start.2
  5.2 0.5 collective-permute-start.1
  5.8 0.2 fusion.1.order_ref
  6.0 0.1 fusion.2.order_ref
  6.1 0.6 collective-permute-done.1
  6.7 1.9 %collective-permute-start.5 = (bf16[512,128]{1,0:T(8,128)(2,1)S(1)}, bf16[512,128]{1,0:T(8,128)(2,1)S(1)}, u32[]{:S(2)}, u32[]{:S(2)}) collective-permute-start(bf16[512,128]{1,0:T(8,128)(2,1)S(1)} %collective-permute-done.1), channel_id=1, source_target_pairs={{0,2},{1,3},{4,0},{5,1},{8,4},{9,5},{12,8},{13,9},{14,12},{15,13},... | collective-permute-start | bytes 393224 | tf_op jit(solution)/shard_map/ppermute | solution.py:379
  8.6 0.2 collective-permute-start.3
  8.8 1.2 %collective-permute-done.2 = bf16[512,128]{1,0:T(8,128)(2,1)S(1)} collective-permute-done((bf16[512,128]{1,0:T(8,128)(2,1)S(1)}, bf16[512,128]{1,0:T(8,128)(2,1)S(1)}, u32[]{:S(2)}, u32[]{:S(2)}) %collective-permute-start.2) | collective-permute-done | bytes 131104 | tf_op jit(solution)/shard_map/ppermute | solution.py:379
  10.0 0.7 %collective-permute-start.6 = (bf16[512,128]{1,0:T(8,128)(2,1)S(1)}, bf16[512,128]{1,0:T(8,128)(2,1)S(1)}, u32[]{:S(2)}, u32[]{:S(2)}) collective-permute-start(bf16[512,128]{1,0:T(8,128)(2,1)S(1)} %collective-permute-done.2), channel_id=1, source_target_pairs={{0,4},{1,5},{4,8},{5,9},{8,12},{9,13},{12,14},{13,15},{14,10},{15,... | collective-permute-start | bytes 393224 | tf_op jit(solution)/shard_map/ppermute | solution.py:379
  10.7 1.9 %collective-permute-done.5 = bf16[512,128]{1,0:T(8,128)(2,1)S(1)} collective-permute-done((bf16[512,128]{1,0:T(8,128)(2,1)S(1)}, bf16[512,128]{1,0:T(8,128)(2,1)S(1)}, u32[]{:S(2)}, u32[]{:S(2)}) %collective-permute-start.5) | collective-permute-done | bytes 131104 | tf_op jit(solution)/shard_map/ppermute | solution.py:379
  12.6 1.7 %collective-permute-start.9 = (bf16[512,128]{1,0:T(8,128)(2,1)S(1)}, bf16[512,128]{1,0:T(8,128)(2,1)S(1)}, u32[]{:S(2)}, u32[]{:S(2)}) collective-permute-start(bf16[512,128]{1,0:T(8,128)(2,1)S(1)} %collective-permute-done.5), channel_id=1, source_target_pairs={{0,2},{1,3},{4,0},{5,1},{8,4},{9,5},{12,8},{13,9},{14,12},{15,13},... | collective-permute-start | bytes 393224 | tf_op jit(solution)/shard_map/ppermute | solution.py:379
  14.3 1.6 %collective-permute-start.8 = (bf16[512,128]{1,0:T(8,128)(2,1)S(1)}, bf16[512,128]{1,0:T(8,128)(2,1)S(1)}, u32[]{:S(2)}, u32[]{:S(2)}) collective-permute-start(bf16[512,128]{1,0:T(8,128)(2,1)S(1)} %collective-permute-done.4), channel_id=1, source_target_pairs={{0,2},{1,3},{4,0},{5,1},{8,4},{9,5},{12,8},{13,9},{14,12},{15,13},... | collective-permute-start | bytes 393224 | tf_op jit(solution)/shard_map/ppermute | solution.py:379
  16.0 0.4 collective-permute-start.7
  16.4 0.5 collective-permute-done.6
  16.9 0.3 collective-permute-start.10
  17.3 1.8 %collective-permute-done.9 = bf16[512,128]{1,0:T(8,128)(2,1)S(1)} collective-permute-done((bf16[512,128]{1,0:T(8,128)(2,1)S(1)}, bf16[512,128]{1,0:T(8,128)(2,1)S(1)}, u32[]{:S(2)}, u32[]{:S(2)}) %collective-permute-start.9) | collective-permute-done | bytes 131104 | tf_op jit(solution)/shard_map/ppermute | solution.py:379
  19.0 1.6 %collective-permute-start.13 = (bf16[512,128]{1,0:T(8,128)(2,1)S(1)}, bf16[512,128]{1,0:T(8,128)(2,1)S(1)}, u32[]{:S(2)}, u32[]{:S(2)}) collective-permute-start(bf16[512,128]{1,0:T(8,128)(2,1)S(1)} %collective-permute-done.9), channel_id=1, source_target_pairs={{0,2},{1,3},{4,0},{5,1},{8,4},{9,5},{12,8},{13,9},{14,12},{15,13},... | collective-permute-start | bytes 393224 | tf_op jit(solution)/shard_map/ppermute | solution.py:379
  20.7 1.1 %collective-permute-done.8 = bf16[512,128]{1,0:T(8,128)(2,1)S(1)} collective-permute-done((bf16[512,128]{1,0:T(8,128)(2,1)S(1)}, bf16[512,128]{1,0:T(8,128)(2,1)S(1)}, u32[]{:S(2)}, u32[]{:S(2)}) %collective-permute-start.8) | collective-permute-done | bytes 131104 | tf_op jit(solution)/shard_map/ppermute | solution.py:379
  21.8 1.6 %collective-permute-start.12 = (bf16[512,128]{1,0:T(8,128)(2,1)S(1)}, bf16[512,128]{1,0:T(8,128)(2,1)S(1)}, u32[]{:S(2)}, u32[]{:S(2)}) collective-permute-start(bf16[512,128]{1,0:T(8,128)(2,1)S(1)} %collective-permute-done.8), channel_id=1, source_target_pairs={{0,2},{1,3},{4,0},{5,1},{8,4},{9,5},{12,8},{13,9},{14,12},{15,13},... | collective-permute-start | bytes 393224 | tf_op jit(solution)/shard_map/ppermute | solution.py:379
  23.5 0.4 collective-permute-start.11
  23.9 1.8 %collective-permute-start.14 = (bf16[512,128]{1,0:T(8,128)(2,1)S(1)}, bf16[512,128]{1,0:T(8,128)(2,1)S(1)}, u32[]{:S(2)}, u32[]{:S(2)}) collective-permute-start(bf16[512,128]{1,0:T(8,128)(2,1)S(1)} %collective-permute-done.10), channel_id=1, source_target_pairs={{0,4},{1,5},{4,8},{5,9},{8,12},{9,13},{12,14},{13,15},{14,10},{15,... | collective-permute-start | bytes 393224 | tf_op jit(solution)/shard_map/ppermute | solution.py:379
  25.7 0.7 %collective-permute-start.15 = (bf16[512,128]{1,0:T(8,128)(2,1)S(1)}, bf16[512,128]{1,0:T(8,128)(2,1)S(1)}, u32[]{:S(2)}, u32[]{:S(2)}) collective-permute-start(bf16[512,128]{1,0:T(8,128)(2,1)S(1)} %collective-permute-done.13), channel_id=1, source_target_pairs={{0,2},{1,3},{4,0},{5,1},{8,4},{9,5},{12,8},{13,9},{14,12},{15,13},... | collective-permute-start | bytes 393224 | tf_op jit(solution)/shard_map/ppermute | solution.py:379
  26.3 0.9 %mix_early.1.early_ref = bf16[64,16,128]{2,1,0:T(8,128)(2,1)S(1)} custom-call(bf16[80,128]{1,0:T(8,128)(2,1)S(1)} %fusion.1.order_ref, bf16[64,8,128]{2,1,0:T(8,128)(2,1)S(1)} %bitcast.35, bf16[64,8,128]{2,1,0:T(8,128)(2,1)S(1)} %bitcast.37, bf16[64,8,128]{2,1,0:T(8,128)(2,1)S(1)} %bitcast.49, bf16[64,8,128]{2,1,0:T(8,128)(2,1)S(1)} %bitcast.52, ...), custom_call_target="tpu_custom_call" | custom-call | flops 1000000000 | bytes 4194304 | tf_op jit(solution)/shard_map/mix_early/pallas_call | solution.py:400
  27.3 0.4 collective-permute-done.12
  27.7 0.8 %collective-permute-done.11 = bf16[512,128]{1,0:T(8,128)(2,1)S(1)} collective-permute-done((bf16[512,128]{1,0:T(8,128)(2,1)S(1)}, bf16[512,128]{1,0:T(8,128)(2,1)S(1)}, u32[]{:S(2)}, u32[]{:S(2)}) %collective-permute-start.11) | collective-permute-done | bytes 131104 | tf_op jit(solution)/shard_map/ppermute | solution.py:379
  28.5 1.4 %collective-permute-done.14 = bf16[512,128]{1,0:T(8,128)(2,1)S(1)} collective-permute-done((bf16[512,128]{1,0:T(8,128)(2,1)S(1)}, bf16[512,128]{1,0:T(8,128)(2,1)S(1)}, u32[]{:S(2)}, u32[]{:S(2)}) %collective-permute-start.14) | collective-permute-done | bytes 131104 | tf_op jit(solution)/shard_map/ppermute | solution.py:379
  29.9 0.8 %collective-permute-done.15 = bf16[512,128]{1,0:T(8,128)(2,1)S(1)} collective-permute-done((bf16[512,128]{1,0:T(8,128)(2,1)S(1)}, bf16[512,128]{1,0:T(8,128)(2,1)S(1)}, u32[]{:S(2)}, u32[]{:S(2)}) %collective-permute-start.15) | collective-permute-done | bytes 131104 | tf_op jit(solution)/shard_map/ppermute | solution.py:379
  30.6 0.7 %mix_late.1 = (bf16[64,8,128]{2,1,0:T(8,128)(2,1)S(1)}, bf16[64,8,128]{2,1,0:T(8,128)(2,1)S(1)}) custom-call(bf16[48,128]{1,0:T(8,128)(2,1)S(1)} %fusion.2.order_ref, bf16[64,8,128]{2,1,0:T(8,128)(2,1)S(1)} %bitcast.36, bf16[64,8,128]{2,1,0:T(8,128)(2,1)S(1)} %bitcast.38, bf16[64,16,128]{2,1,0:T(8,128)(2,1)S(1)} %mix_early.1.early_ref, ...), custom_call_target="tpu_custom_call" | custom-call | tf_op jit(solution)/shard_map/mix_late/pallas_call | solution.py:410
  31.4 1.2 %collective-permute-done.16 = bf16[64,8,128]{2,1,0:T(8,128)(2,1)S(1)} collective-permute-done((bf16[64,8,128]{2,1,0:T(8,128)(2,1)S(1)}, bf16[64,8,128]{2,1,0:T(8,128)(2,1)S(1)}, u32[]{:S(2)}, u32[]{:S(2)}) %collective-permute-start.16) | collective-permute-done | bytes 131104 | tf_op jit(solution)/shard_map/ppermute | solution.py:419
  32.7 1.4 %finish_project.1 = (bf16[512,128]{1,0:T(8,128)(2,1)S(1)}, bf16[512,128]{1,0:T(8,128)(2,1)S(1)}, bf16[512,128]{1,0:T(8,128)(2,1)S(1)}, bf16[512,128]{1,0:T(8,128...) custom-call(s32[1]{0:T(128)} %bitcast.refs_0_, bf16[512,128]{1,0:T(8,128)(2,1)S(1)} %bitcast.40, ...), custom_call_target="tpu_custom_call" | custom-call | tf_op jit(solution)/shard_map/finish_project/pallas_call | solution.py:422
  34.1 0.2 collective-permute-start.17
  34.3 0.4 collective-permute-start.18
  34.6 0.3 fusion.order_ref
  35.0 0.5 collective-permute-done.17
  35.5 0.2 collective-permute-done.18
  35.7 0.7 %scatter_start.3 = (f32[32,128,128]{2,1,0:T(8,128)S(1)}, bf16[32,16,128]{2,1,0:T(8,128)(2,1)S(1)}, bf16[32,16,128]{2,1,0:T(8,128)(2,1)S(1)}) custom-call(bf16[128,128]{1,0:T(8,128)(2,1)S(1)} %fusion.order_ref, bf16[64,8,128]{2,1,0:T(8,128)(2,1)S(1)} %bitcast.27, bf16[64,8,128]{2,1,0:T(8,128)(2,1)S(1)} %bitcast.31, bf16[64,8,128]{2,1,0:T(8,128)(2,1)S(1)} %bitcast.29, ...), custom_call_target="tpu_custom_call" | custom-call | tf_op jit(solution)/shard_map/scatter_start/pallas_call | solution.py:443
  36.3 0.9 %collective-permute-start.29 = (bf16[32,16,128]{2,1,0:T(8,128)(2,1)S(1)}, bf16[32,16,128]{2,1,0:T(8,128)(2,1)S(1)}, u32[]{:S(2)}, u32[]{:S(2)}) collective-permute-start(bf16[32,16,128]{2,1,0:T(8,128)(2,1)S(1)} %get-tuple-element.52), channel_id=1, source_target_pairs={{0,2},{1,3},{4,0},{5,1},{8,4},{9,5},{12,8},{13,9},{14,12},{15,13},... | collective-permute-start | bytes 393224 | tf_op jit(solution)/shard_map/ppermute | solution.py:379
  37.2 0.7 %scatter_start.2 = (f32[32,128,128]{2,1,0:T(8,128)S(1)}, bf16[32,16,128]{2,1,0:T(8,128)(2,1)S(1)}, bf16[32,16,128]{2,1,0:T(8,128)(2,1)S(1)}) custom-call(bf16[128,128]{1,0:T(8,128)(2,1)S(1)} %fusion.order_ref, bf16[64,8,128]{2,1,0:T(8,128)(2,1)S(1)} %bitcast.28, bf16[64,8,128]{2,1,0:T(8,128)(2,1)S(1)} %bitcast.32, bf16[64,8,128]{2,1,0:T(8,128)(2,1)S(1)} %bitcast.30, ...), custom_call_target="tpu_custom_call" | custom-call | tf_op jit(solution)/shard_map/scatter_start/pallas_call | solution.py:443
  37.9 1.3 %collective-permute-start.19 = (bf16[32,16,128]{2,1,0:T(8,128)(2,1)S(1)}, bf16[32,16,128]{2,1,0:T(8,128)(2,1)S(1)}, u32[]{:S(2)}, u32[]{:S(2)}) collective-permute-start(bf16[32,16,128]{2,1,0:T(8,128)(2,1)S(1)} %get-tuple-element.48), channel_id=1, source_target_pairs={{0,4},{1,5},{4,8},{5,9},{8,12},{9,13},{12,14},{13,15},{14,10},{15,... | collective-permute-start | bytes 393224 | tf_op jit(solution)/shard_map/ppermute | solution.py:379
  39.1 1.6 %collective-permute-start.26 = (bf16[32,16,128]{2,1,0:T(8,128)(2,1)S(1)}, bf16[32,16,128]{2,1,0:T(8,128)(2,1)S(1)}, u32[]{:S(2)}, u32[]{:S(2)}) collective-permute-start(bf16[32,16,128]{2,1,0:T(8,128)(2,1)S(1)} %get-tuple-element.51), channel_id=1, source_target_pairs={{0,4},{1,5},{4,8},{5,9},{8,12},{9,13},{12,14},{13,15},{14,10},{15,... | collective-permute-start | bytes 393224 | tf_op jit(solution)/shard_map/ppermute | solution.py:379
  40.7 0.4 collective-permute-start.23
  41.2 1.0 %collective-permute-done.29.got_ref = bf16[32,16,128]{2,1,0:T(8,128)(2,1)S(1)} collective-permute-done((bf16[32,16,128]{2,1,0:T(8,128)(2,1)S(1)}, bf16[32,16,128]{2,1,0:T(8,128)(2,1)S(1)}, u32[]{:S(2)}, u32[]{:S(2)}) %collective-permute-start.29) | collective-permute-done | bytes 131104 | tf_op jit(solution)/shard_map/ppermute | solution.py:379
  42.1 0.9 %collective-permute-start.30 = (bf16[32,16,128]{2,1,0:T(8,128)(2,1)S(1)}, bf16[32,16,128]{2,1,0:T(8,128)(2,1)S(1)}, u32[]{:S(2)}, u32[]{:S(2)}) collective-permute-start(bf16[32,16,128]{2,1,0:T(8,128)(2,1)S(1)} %scatter_add.17), channel_id=1, source_target_pairs={{0,2},{1,3},{4,0},{5,1},{8,4},{9,5},{12,8},{13,9},{14,12},{15,13},... | collective-permute-start | bytes 393224 | tf_op jit(solution)/shard_map/ppermute | solution.py:379
  43.0 1.3 %collective-permute-done.19.got_ref = bf16[32,16,128]{2,1,0:T(8,128)(2,1)S(1)} collective-permute-done((bf16[32,16,128]{2,1,0:T(8,128)(2,1)S(1)}, bf16[32,16,128]{2,1,0:T(8,128)(2,1)S(1)}, u32[]{:S(2)}, u32[]{:S(2)}) %collective-permute-start.19) | collective-permute-done | bytes 131104 | tf_op jit(solution)/shard_map/ppermute | solution.py:379
  44.3 1.3 %collective-permute-start.20 = (bf16[32,16,128]{2,1,0:T(8,128)(2,1)S(1)}, bf16[32,16,128]{2,1,0:T(8,128)(2,1)S(1)}, u32[]{:S(2)}, u32[]{:S(2)}) collective-permute-start(bf16[32,16,128]{2,1,0:T(8,128)(2,1)S(1)} %scatter_add.10), channel_id=1, source_target_pairs={{0,4},{1,5},{4,8},{5,9},{8,12},{9,13},{12,14},{13,15},{14,10},{15,... | collective-permute-start | bytes 393224 | tf_op jit(solution)/shard_map/ppermute | solution.py:379
  45.6 1.5 %collective-permute-done.26.got_ref = bf16[32,16,128]{2,1,0:T(8,128)(2,1)S(1)} collective-permute-done((bf16[32,16,128]{2,1,0:T(8,128)(2,1)S(1)}, bf16[32,16,128]{2,1,0:T(8,128)(2,1)S(1)}, u32[]{:S(2)}, u32[]{:S(2)}) %collective-permute-start.26) | collective-permute-done | bytes 131104 | tf_op jit(solution)/shard_map/ppermute | solution.py:379
  47.1 1.3 %collective-permute-start.27 = (bf16[32,16,128]{2,1,0:T(8,128)(2,1)S(1)}, bf16[32,16,128]{2,1,0:T(8,128)(2,1)S(1)}, u32[]{:S(2)}, u32[]{:S(2)}) collective-permute-start(bf16[32,16,128]{2,1,0:T(8,128)(2,1)S(1)} %scatter_add.15), channel_id=1, source_target_pairs={{0,4},{1,5},{4,8},{5,9},{8,12},{9,13},{12,14},{13,15},{14,10},{15,... | collective-permute-start | bytes 393224 | tf_op jit(solution)/shard_map/ppermute | solution.py:379
  48.4 0.9 %collective-permute-start.24 = (bf16[32,16,128]{2,1,0:T(8,128)(2,1)S(1)}, bf16[32,16,128]{2,1,0:T(8,128)(2,1)S(1)}, u32[]{:S(2)}, u32[]{:S(2)}) collective-permute-start(bf16[32,16,128]{2,1,0:T(8,128)(2,1)S(1)} %scatter_add.13), channel_id=1, source_target_pairs={{0,2},{1,3},{4,0},{5,1},{8,4},{9,5},{12,8},{13,9},{14,12},{15,13},... | collective-permute-start | bytes 393224 | tf_op jit(solution)/shard_map/ppermute | solution.py:379
  49.3 1.6 %collective-permute-start.31 = (bf16[32,16,128]{2,1,0:T(8,128)(2,1)S(1)}, bf16[32,16,128]{2,1,0:T(8,128)(2,1)S(1)}, u32[]{:S(2)}, u32[]{:S(2)}) collective-permute-start(bf16[32,16,128]{2,1,0:T(8,128)(2,1)S(1)} %scatter_add.18), channel_id=1, source_target_pairs={{0,2},{1,3},{4,0},{5,1},{8,4},{9,5},{12,8},{13,9},{14,12},{15,13},... | collective-permute-start | bytes 393224 | tf_op jit(solution)/shard_map/ppermute | solution.py:379
  51.0 0.9 %collective-permute-start.21 = (bf16[32,16,128]{2,1,0:T(8,128)(2,1)S(1)}, bf16[32,16,128]{2,1,0:T(8,128)(2,1)S(1)}, u32[]{:S(2)}, u32[]{:S(2)}) collective-permute-start(bf16[32,16,128]{2,1,0:T(8,128)(2,1)S(1)} %scatter_add.11), channel_id=1, source_target_pairs={{0,4},{1,5},{4,8},{5,9},{8,12},{9,13},{12,14},{13,15},{14,10},{15,... | collective-permute-start | bytes 393224 | tf_op jit(solution)/shard_map/ppermute | solution.py:379
  51.9 1.3 %collective-permute-done.27.got_ref = bf16[32,16,128]{2,1,0:T(8,128)(2,1)S(1)} collective-permute-done((bf16[32,16,128]{2,1,0:T(8,128)(2,1)S(1)}, bf16[32,16,128]{2,1,0:T(8,128)(2,1)S(1)}, u32[]{:S(2)}, u32[]{:S(2)}) %collective-permute-start.27) | collective-permute-done | bytes 131104 | tf_op jit(solution)/shard_map/ppermute | solution.py:379
  53.2 1.7 %collective-permute-start.28 = (bf16[32,16,128]{2,1,0:T(8,128)(2,1)S(1)}, bf16[32,16,128]{2,1,0:T(8,128)(2,1)S(1)}, u32[]{:S(2)}, u32[]{:S(2)}) collective-permute-start(bf16[32,16,128]{2,1,0:T(8,128)(2,1)S(1)} %scatter_add.16), channel_id=1, source_target_pairs={{0,4},{1,5},{4,8},{5,9},{8,12},{9,13},{12,14},{13,15},{14,10},{15,... | collective-permute-start | bytes 393224 | tf_op jit(solution)/shard_map/ppermute | solution.py:379
  54.9 0.5 collective-permute-start.25
  55.4 1.6 %collective-permute-start.32 = (bf16[32,16,128]{2,1,0:T(8,128)(2,1)S(1)}, bf16[32,16,128]{2,1,0:T(8,128)(2,1)S(1)}, u32[]{:S(2)}, u32[]{:S(2)}) collective-permute-start(bf16[32,16,128]{2,1,0:T(8,128)(2,1)S(1)} %scatter_add.19), channel_id=1, source_target_pairs={{0,2},{1,3},{4,0},{5,1},{8,4},{9,5},{12,8},{13,9},{14,12},{15,13},... | collective-permute-start | bytes 393224 | tf_op jit(solution)/shard_map/ppermute | solution.py:379
  57.1 0.6 collective-permute-start.22
  57.7 1.6 %collective-permute-done.28.refs_4_ = bf16[32,16,128]{2,1,0:T(8,128)(2,1)S(1)} collective-permute-done((bf16[32,16,128]{2,1,0:T(8,128)(2,1)S(1)}, bf16[32,16,128]{2,1,0:T(8,128)(2,1)S(1)}, u32[]{:S(2)}, u32[]{:S(2)}) %collective-permute-start.28) | collective-permute-done | bytes 131104 | tf_op jit(solution)/shard_map/ppermute | solution.py:379
  59.2 0.7 %collective-permute-done.25.refs_2_ = bf16[32,16,128]{2,1,0:T(8,128)(2,1)S(1)} collective-permute-done((bf16[32,16,128]{2,1,0:T(8,128)(2,1)S(1)}, bf16[32,16,128]{2,1,0:T(8,128)(2,1)S(1)}, u32[]{:S(2)}, u32[]{:S(2)}) %collective-permute-start.25) | collective-permute-done | bytes 131104 | tf_op jit(solution)/shard_map/ppermute | solution.py:379
  59.9 1.4 %collective-permute-done.32.refs_5_ = bf16[32,16,128]{2,1,0:T(8,128)(2,1)S(1)} collective-permute-done((bf16[32,16,128]{2,1,0:T(8,128)(2,1)S(1)}, bf16[32,16,128]{2,1,0:T(8,128)(2,1)S(1)}, u32[]{:S(2)}, u32[]{:S(2)}) %collective-permute-start.32) | collective-permute-done | bytes 131104 | tf_op jit(solution)/shard_map/ppermute | solution.py:379
  61.3 0.8 %collective-permute-done.22.refs_1_ = bf16[32,16,128]{2,1,0:T(8,128)(2,1)S(1)} collective-permute-done((bf16[32,16,128]{2,1,0:T(8,128)(2,1)S(1)}, bf16[32,16,128]{2,1,0:T(8,128)(2,1)S(1)}, u32[]{:S(2)}, u32[]{:S(2)}) %collective-permute-start.22) | collective-permute-done | bytes 131104 | tf_op jit(solution)/shard_map/ppermute | solution.py:379
  62.1 0.1 scatter_end.1
  62.3 1.3 %collective-permute-done.33 = bf16[64,8,128]{2,1,0:T(8,128)(2,1)S(1)} collective-permute-done((bf16[64,8,128]{2,1,0:T(8,128)(2,1)S(1)}, bf16[64,8,128]{2,1,0:T(8,128)(2,1)S(1)}, u32[]{:S(2)}, u32[]{:S(2)}) %collective-permute-start.33) | collective-permute-done | bytes 131104 | tf_op jit(solution)/shard_map/ppermute | solution.py:472
  63.6 1.3 %finish.1 = bf16[8,128,128]{2,1,0:T(8,128)(2,1)} custom-call(s32[1]{0:T(128)} %bitcast.refs_0_, bf16[512,128]{1,0:T(8,128)(2,1)S(1)} %bitcast.47, bf16[512,128]{1,0:T(8,128)(2,1)S(1)} %bitcast.48, bf16[128,1024]{1,0:T(8,128)(2,1)S(1)} %get-tuple-element.55.refs_3_, bf16[128,1024]{1,0:T(8,128)(2,1)S(1)} %get-tuple-element.56.refs_4_, ...), custom_call_target="tpu_custom_call" | custom-call | tf_op jit(solution)/shard_map/finish/pallas_call | solution.py:475
  (44 shorter events, 0.5 us)
Async XLA Ops:
  2.0 12.3 %collective-permute-start.4 = (bf16[512,128]{1,0:T(8,128)(2,1)S(1)}, bf16[512,128]{1,0:T(8,128)(2,1)S(1)}, u32[]{:S(2)}, u32[]{:S(2)}) collective-permute-start(bf16[512,128]{1,0:T(8,128)(2,1)S(1)} %get-tuple-element.33), channel_id=1, source_target_pairs={{0,2},{1,3},{4,0},{5,1},{8,4},{9,5},{12,8},{13,9},{14,12},{15,13},... | collective-permute-start | bytes 393224 | tf_op jit(solution)/shard_map/ppermute | solution.py:379
  5.0 5.0 %collective-permute-start.2 = (bf16[512,128]{1,0:T(8,128)(2,1)S(1)}, bf16[512,128]{1,0:T(8,128)(2,1)S(1)}, u32[]{:S(2)}, u32[]{:S(2)}) collective-permute-start(bf16[512,128]{1,0:T(8,128)(2,1)S(1)} %get-tuple-element.33), channel_id=1, source_target_pairs={{0,4},{1,5},{4,8},{5,9},{8,12},{9,13},{12,14},{13,15},{14,10},{15,... | collective-permute-start | bytes 393224 | tf_op jit(solution)/shard_map/ppermute | solution.py:379
  5.2 21.2 %collective-permute-start = (bf16[512,128]{1,0:T(8,128)(2,1)S(1)}, bf16[512,128]{1,0:T(8,128)(2,1)S(1)}, u32[]{:S(2)}, u32[]{:S(2)}) collective-permute-start(bf16[512,128]{1,0:T(8,128)(2,1)S(1)} %get-tuple-element.32), channel_id=1, source_target_pairs={{0,1},{1,0},{2,3},{3,2},{4,5},{5,4},{6,7},{7,6},{8,9},{9,8},{10,11... | collective-permute-start | bytes 393224 | tf_op jit(solution)/shard_map/ppermute | solution.py:389
  5.2 1.5 %collective-permute-start.1 = (bf16[512,128]{1,0:T(8,128)(2,1)S(1)}, bf16[512,128]{1,0:T(8,128)(2,1)S(1)}, u32[]{:S(2)}, u32[]{:S(2)}) collective-permute-start(bf16[512,128]{1,0:T(8,128)(2,1)S(1)} %get-tuple-element.34), channel_id=1, source_target_pairs={{0,1},{1,0},{2,3},{3,2},{4,5},{5,4},{6,7},{7,6},{8,9},{9,8},{10,11... | collective-permute-start | bytes 393224 | tf_op jit(solution)/shard_map/ppermute | solution.py:388
  6.7 5.9 %collective-permute-start.5 = (bf16[512,128]{1,0:T(8,128)(2,1)S(1)}, bf16[512,128]{1,0:T(8,128)(2,1)S(1)}, u32[]{:S(2)}, u32[]{:S(2)}) collective-permute-start(bf16[512,128]{1,0:T(8,128)(2,1)S(1)} %collective-permute-done.1), channel_id=1, source_target_pairs={{0,2},{1,3},{4,0},{5,1},{8,4},{9,5},{12,8},{13,9},{14,12},{15,13},... | collective-permute-start | bytes 393224 | tf_op jit(solution)/shard_map/ppermute | solution.py:379
  8.6 7.4 %collective-permute-start.3 = (bf16[512,128]{1,0:T(8,128)(2,1)S(1)}, bf16[512,128]{1,0:T(8,128)(2,1)S(1)}, u32[]{:S(2)}, u32[]{:S(2)}) collective-permute-start(bf16[512,128]{1,0:T(8,128)(2,1)S(1)} %collective-permute-done.1), channel_id=1, source_target_pairs={{0,4},{1,5},{4,8},{5,9},{8,12},{9,13},{12,14},{13,15},{14,10},{15,... | collective-permute-start | bytes 393224 | tf_op jit(solution)/shard_map/ppermute | solution.py:379
  10.0 6.9 %collective-permute-start.6 = (bf16[512,128]{1,0:T(8,128)(2,1)S(1)}, bf16[512,128]{1,0:T(8,128)(2,1)S(1)}, u32[]{:S(2)}, u32[]{:S(2)}) collective-permute-start(bf16[512,128]{1,0:T(8,128)(2,1)S(1)} %collective-permute-done.2), channel_id=1, source_target_pairs={{0,4},{1,5},{4,8},{5,9},{8,12},{9,13},{12,14},{13,15},{14,10},{15,... | collective-permute-start | bytes 393224 | tf_op jit(solution)/shard_map/ppermute | solution.py:379
  12.6 6.4 %collective-permute-start.9 = (bf16[512,128]{1,0:T(8,128)(2,1)S(1)}, bf16[512,128]{1,0:T(8,128)(2,1)S(1)}, u32[]{:S(2)}, u32[]{:S(2)}) collective-permute-start(bf16[512,128]{1,0:T(8,128)(2,1)S(1)} %collective-permute-done.5), channel_id=1, source_target_pairs={{0,2},{1,3},{4,0},{5,1},{8,4},{9,5},{12,8},{13,9},{14,12},{15,13},... | collective-permute-start | bytes 393224 | tf_op jit(solution)/shard_map/ppermute | solution.py:379
  14.3 7.5 %collective-permute-start.8 = (bf16[512,128]{1,0:T(8,128)(2,1)S(1)}, bf16[512,128]{1,0:T(8,128)(2,1)S(1)}, u32[]{:S(2)}, u32[]{:S(2)}) collective-permute-start(bf16[512,128]{1,0:T(8,128)(2,1)S(1)} %collective-permute-done.4), channel_id=1, source_target_pairs={{0,2},{1,3},{4,0},{5,1},{8,4},{9,5},{12,8},{13,9},{14,12},{15,13},... | collective-permute-start | bytes 393224 | tf_op jit(solution)/shard_map/ppermute | solution.py:379
  16.0 7.5 %collective-permute-start.7 = (bf16[512,128]{1,0:T(8,128)(2,1)S(1)}, bf16[512,128]{1,0:T(8,128)(2,1)S(1)}, u32[]{:S(2)}, u32[]{:S(2)}) collective-permute-start(bf16[512,128]{1,0:T(8,128)(2,1)S(1)} %collective-permute-done.3), channel_id=1, source_target_pairs={{0,4},{1,5},{4,8},{5,9},{8,12},{9,13},{12,14},{13,15},{14,10},{15,... | collective-permute-start | bytes 393224 | tf_op jit(solution)/shard_map/ppermute | solution.py:379
  16.9 7.0 %collective-permute-start.10 = (bf16[512,128]{1,0:T(8,128)(2,1)S(1)}, bf16[512,128]{1,0:T(8,128)(2,1)S(1)}, u32[]{:S(2)}, u32[]{:S(2)}) collective-permute-start(bf16[512,128]{1,0:T(8,128)(2,1)S(1)} %collective-permute-done.6), channel_id=1, source_target_pairs={{0,4},{1,5},{4,8},{5,9},{8,12},{9,13},{12,14},{13,15},{14,10},{15,... | collective-permute-start | bytes 393224 | tf_op jit(solution)/shard_map/ppermute | solution.py:379
  19.0 6.6 %collective-permute-start.13 = (bf16[512,128]{1,0:T(8,128)(2,1)S(1)}, bf16[512,128]{1,0:T(8,128)(2,1)S(1)}, u32[]{:S(2)}, u32[]{:S(2)}) collective-permute-start(bf16[512,128]{1,0:T(8,128)(2,1)S(1)} %collective-permute-done.9), channel_id=1, source_target_pairs={{0,2},{1,3},{4,0},{5,1},{8,4},{9,5},{12,8},{13,9},{14,12},{15,13},... | collective-permute-start | bytes 393224 | tf_op jit(solution)/shard_map/ppermute | solution.py:379
  21.8 5.9 %collective-permute-start.12 = (bf16[512,128]{1,0:T(8,128)(2,1)S(1)}, bf16[512,128]{1,0:T(8,128)(2,1)S(1)}, u32[]{:S(2)}, u32[]{:S(2)}) collective-permute-start(bf16[512,128]{1,0:T(8,128)(2,1)S(1)} %collective-permute-done.8), channel_id=1, source_target_pairs={{0,2},{1,3},{4,0},{5,1},{8,4},{9,5},{12,8},{13,9},{14,12},{15,13},... | collective-permute-start | bytes 393224 | tf_op jit(solution)/shard_map/ppermute | solution.py:379
  23.5 5.0 %collective-permute-start.11 = (bf16[512,128]{1,0:T(8,128)(2,1)S(1)}, bf16[512,128]{1,0:T(8,128)(2,1)S(1)}, u32[]{:S(2)}, u32[]{:S(2)}) collective-permute-start(bf16[512,128]{1,0:T(8,128)(2,1)S(1)} %collective-permute-done.7), channel_id=1, source_target_pairs={{0,4},{1,5},{4,8},{5,9},{8,12},{9,13},{12,14},{13,15},{14,10},{15,... | collective-permute-start | bytes 393224 | tf_op jit(solution)/shard_map/ppermute | solution.py:379
  23.9 6.0 %collective-permute-start.14 = (bf16[512,128]{1,0:T(8,128)(2,1)S(1)}, bf16[512,128]{1,0:T(8,128)(2,1)S(1)}, u32[]{:S(2)}, u32[]{:S(2)}) collective-permute-start(bf16[512,128]{1,0:T(8,128)(2,1)S(1)} %collective-permute-done.10), channel_id=1, source_target_pairs={{0,4},{1,5},{4,8},{5,9},{8,12},{9,13},{12,14},{13,15},{14,10},{15,... | collective-permute-start | bytes 393224 | tf_op jit(solution)/shard_map/ppermute | solution.py:379
  25.7 5.0 %collective-permute-start.15 = (bf16[512,128]{1,0:T(8,128)(2,1)S(1)}, bf16[512,128]{1,0:T(8,128)(2,1)S(1)}, u32[]{:S(2)}, u32[]{:S(2)}) collective-permute-start(bf16[512,128]{1,0:T(8,128)(2,1)S(1)} %collective-permute-done.13), channel_id=1, source_target_pairs={{0,2},{1,3},{4,0},{5,1},{8,4},{9,5},{12,8},{13,9},{14,12},{15,13},... | collective-permute-start | bytes 393224 | tf_op jit(solution)/shard_map/ppermute | solution.py:379
  31.3 1.4 %collective-permute-start.16 = (bf16[64,8,128]{2,1,0:T(8,128)(2,1)S(1)}, bf16[64,8,128]{2,1,0:T(8,128)(2,1)S(1)}, u32[]{:S(2)}, u32[]{:S(2)}) collective-permute-start(bf16[64,8,128]{2,1,0:T(8,128)(2,1)S(1)} %get-tuple-element.36), channel_id=1, source_target_pairs={{0,1},{1,0},{2,3},{3,2},{4,5},{5,4},{6,7},{7,6},{8,9},{9,8},{10,11... | collective-permute-start | bytes 393224 | tf_op jit(solution)/shard_map/ppermute | solution.py:419
  34.1 1.4 %collective-permute-start.17 = (bf16[512,128]{1,0:T(8,128)(2,1)S(1)}, bf16[512,128]{1,0:T(8,128)(2,1)S(1)}, u32[]{:S(2)}, u32[]{:S(2)}) collective-permute-start(bf16[512,128]{1,0:T(8,128)(2,1)S(1)} %get-tuple-element.44), channel_id=1, source_target_pairs={{0,1},{1,0},{2,3},{3,2},{4,5},{5,4},{6,7},{7,6},{8,9},{9,8},{10,11... | collective-permute-start | bytes 393224 | tf_op jit(solution)/shard_map/ppermute | solution.py:434
  34.3 1.4 %collective-permute-start.18 = (bf16[512,128]{1,0:T(8,128)(2,1)S(1)}, bf16[512,128]{1,0:T(8,128)(2,1)S(1)}, u32[]{:S(2)}, u32[]{:S(2)}) collective-permute-start(bf16[512,128]{1,0:T(8,128)(2,1)S(1)} %get-tuple-element.46), channel_id=1, source_target_pairs={{0,1},{1,0},{2,3},{3,2},{4,5},{5,4},{6,7},{7,6},{8,9},{9,8},{10,11... | collective-permute-start | bytes 393224 | tf_op jit(solution)/shard_map/ppermute | solution.py:435
  36.3 5.8 %collective-permute-start.29 = (bf16[32,16,128]{2,1,0:T(8,128)(2,1)S(1)}, bf16[32,16,128]{2,1,0:T(8,128)(2,1)S(1)}, u32[]{:S(2)}, u32[]{:S(2)}) collective-permute-start(bf16[32,16,128]{2,1,0:T(8,128)(2,1)S(1)} %get-tuple-element.52), channel_id=1, source_target_pairs={{0,2},{1,3},{4,0},{5,1},{8,4},{9,5},{12,8},{13,9},{14,12},{15,13},... | collective-permute-start | bytes 393224 | tf_op jit(solution)/shard_map/ppermute | solution.py:379
  37.9 6.4 %collective-permute-start.19 = (bf16[32,16,128]{2,1,0:T(8,128)(2,1)S(1)}, bf16[32,16,128]{2,1,0:T(8,128)(2,1)S(1)}, u32[]{:S(2)}, u32[]{:S(2)}) collective-permute-start(bf16[32,16,128]{2,1,0:T(8,128)(2,1)S(1)} %get-tuple-element.48), channel_id=1, source_target_pairs={{0,4},{1,5},{4,8},{5,9},{8,12},{9,13},{12,14},{13,15},{14,10},{15,... | collective-permute-start | bytes 393224 | tf_op jit(solution)/shard_map/ppermute | solution.py:379
  39.1 8.0 %collective-permute-start.26 = (bf16[32,16,128]{2,1,0:T(8,128)(2,1)S(1)}, bf16[32,16,128]{2,1,0:T(8,128)(2,1)S(1)}, u32[]{:S(2)}, u32[]{:S(2)}) collective-permute-start(bf16[32,16,128]{2,1,0:T(8,128)(2,1)S(1)} %get-tuple-element.51), channel_id=1, source_target_pairs={{0,4},{1,5},{4,8},{5,9},{8,12},{9,13},{12,14},{13,15},{14,10},{15,... | collective-permute-start | bytes 393224 | tf_op jit(solution)/shard_map/ppermute | solution.py:379
  40.7 7.7 %collective-permute-start.23 = (bf16[32,16,128]{2,1,0:T(8,128)(2,1)S(1)}, bf16[32,16,128]{2,1,0:T(8,128)(2,1)S(1)}, u32[]{:S(2)}, u32[]{:S(2)}) collective-permute-start(bf16[32,16,128]{2,1,0:T(8,128)(2,1)S(1)} %get-tuple-element.49), channel_id=1, source_target_pairs={{0,2},{1,3},{4,0},{5,1},{8,4},{9,5},{12,8},{13,9},{14,12},{15,13},... | collective-permute-start | bytes 393224 | tf_op jit(solution)/shard_map/ppermute | solution.py:379
  42.1 7.1 %collective-permute-start.30 = (bf16[32,16,128]{2,1,0:T(8,128)(2,1)S(1)}, bf16[32,16,128]{2,1,0:T(8,128)(2,1)S(1)}, u32[]{:S(2)}, u32[]{:S(2)}) collective-permute-start(bf16[32,16,128]{2,1,0:T(8,128)(2,1)S(1)} %scatter_add.17), channel_id=1, source_target_pairs={{0,2},{1,3},{4,0},{5,1},{8,4},{9,5},{12,8},{13,9},{14,12},{15,13},... | collective-permute-start | bytes 393224 | tf_op jit(solution)/shard_map/ppermute | solution.py:379
  44.3 6.6 %collective-permute-start.20 = (bf16[32,16,128]{2,1,0:T(8,128)(2,1)S(1)}, bf16[32,16,128]{2,1,0:T(8,128)(2,1)S(1)}, u32[]{:S(2)}, u32[]{:S(2)}) collective-permute-start(bf16[32,16,128]{2,1,0:T(8,128)(2,1)S(1)} %scatter_add.10), channel_id=1, source_target_pairs={{0,4},{1,5},{4,8},{5,9},{8,12},{9,13},{12,14},{13,15},{14,10},{15,... | collective-permute-start | bytes 393224 | tf_op jit(solution)/shard_map/ppermute | solution.py:379
  47.1 6.1 %collective-permute-start.27 = (bf16[32,16,128]{2,1,0:T(8,128)(2,1)S(1)}, bf16[32,16,128]{2,1,0:T(8,128)(2,1)S(1)}, u32[]{:S(2)}, u32[]{:S(2)}) collective-permute-start(bf16[32,16,128]{2,1,0:T(8,128)(2,1)S(1)} %scatter_add.15), channel_id=1, source_target_pairs={{0,4},{1,5},{4,8},{5,9},{8,12},{9,13},{12,14},{13,15},{14,10},{15,... | collective-permute-start | bytes 393224 | tf_op jit(solution)/shard_map/ppermute | solution.py:379
  48.4 6.5 %collective-permute-start.24 = (bf16[32,16,128]{2,1,0:T(8,128)(2,1)S(1)}, bf16[32,16,128]{2,1,0:T(8,128)(2,1)S(1)}, u32[]{:S(2)}, u32[]{:S(2)}) collective-permute-start(bf16[32,16,128]{2,1,0:T(8,128)(2,1)S(1)} %scatter_add.13), channel_id=1, source_target_pairs={{0,2},{1,3},{4,0},{5,1},{8,4},{9,5},{12,8},{13,9},{14,12},{15,13},... | collective-permute-start | bytes 393224 | tf_op jit(solution)/shard_map/ppermute | solution.py:379
  49.3 6.1 %collective-permute-start.31 = (bf16[32,16,128]{2,1,0:T(8,128)(2,1)S(1)}, bf16[32,16,128]{2,1,0:T(8,128)(2,1)S(1)}, u32[]{:S(2)}, u32[]{:S(2)}) collective-permute-start(bf16[32,16,128]{2,1,0:T(8,128)(2,1)S(1)} %scatter_add.18), channel_id=1, source_target_pairs={{0,2},{1,3},{4,0},{5,1},{8,4},{9,5},{12,8},{13,9},{14,12},{15,13},... | collective-permute-start | bytes 393224 | tf_op jit(solution)/shard_map/ppermute | solution.py:379
  51.0 6.1 %collective-permute-start.21 = (bf16[32,16,128]{2,1,0:T(8,128)(2,1)S(1)}, bf16[32,16,128]{2,1,0:T(8,128)(2,1)S(1)}, u32[]{:S(2)}, u32[]{:S(2)}) collective-permute-start(bf16[32,16,128]{2,1,0:T(8,128)(2,1)S(1)} %scatter_add.11), channel_id=1, source_target_pairs={{0,4},{1,5},{4,8},{5,9},{8,12},{9,13},{12,14},{13,15},{14,10},{15,... | collective-permute-start | bytes 393224 | tf_op jit(solution)/shard_map/ppermute | solution.py:379
  53.2 6.0 %collective-permute-start.28 = (bf16[32,16,128]{2,1,0:T(8,128)(2,1)S(1)}, bf16[32,16,128]{2,1,0:T(8,128)(2,1)S(1)}, u32[]{:S(2)}, u32[]{:S(2)}) collective-permute-start(bf16[32,16,128]{2,1,0:T(8,128)(2,1)S(1)} %scatter_add.16), channel_id=1, source_target_pairs={{0,4},{1,5},{4,8},{5,9},{8,12},{9,13},{12,14},{13,15},{14,10},{15,... | collective-permute-start | bytes 393224 | tf_op jit(solution)/shard_map/ppermute | solution.py:379
  54.9 5.0 %collective-permute-start.25 = (bf16[32,16,128]{2,1,0:T(8,128)(2,1)S(1)}, bf16[32,16,128]{2,1,0:T(8,128)(2,1)S(1)}, u32[]{:S(2)}, u32[]{:S(2)}) collective-permute-start(bf16[32,16,128]{2,1,0:T(8,128)(2,1)S(1)} %scatter_add.14), channel_id=1, source_target_pairs={{0,2},{1,3},{4,0},{5,1},{8,4},{9,5},{12,8},{13,9},{14,12},{15,13},... | collective-permute-start | bytes 393224 | tf_op jit(solution)/shard_map/ppermute | solution.py:379
  55.4 5.9 %collective-permute-start.32 = (bf16[32,16,128]{2,1,0:T(8,128)(2,1)S(1)}, bf16[32,16,128]{2,1,0:T(8,128)(2,1)S(1)}, u32[]{:S(2)}, u32[]{:S(2)}) collective-permute-start(bf16[32,16,128]{2,1,0:T(8,128)(2,1)S(1)} %scatter_add.19), channel_id=1, source_target_pairs={{0,2},{1,3},{4,0},{5,1},{8,4},{9,5},{12,8},{13,9},{14,12},{15,13},... | collective-permute-start | bytes 393224 | tf_op jit(solution)/shard_map/ppermute | solution.py:379
  57.1 5.0 %collective-permute-start.22 = (bf16[32,16,128]{2,1,0:T(8,128)(2,1)S(1)}, bf16[32,16,128]{2,1,0:T(8,128)(2,1)S(1)}, u32[]{:S(2)}, u32[]{:S(2)}) collective-permute-start(bf16[32,16,128]{2,1,0:T(8,128)(2,1)S(1)} %scatter_add.12), channel_id=1, source_target_pairs={{0,4},{1,5},{4,8},{5,9},{8,12},{9,13},{12,14},{13,15},{14,10},{15,... | collective-permute-start | bytes 393224 | tf_op jit(solution)/shard_map/ppermute | solution.py:379
  62.2 1.4 %collective-permute-start.33 = (bf16[64,8,128]{2,1,0:T(8,128)(2,1)S(1)}, bf16[64,8,128]{2,1,0:T(8,128)(2,1)S(1)}, u32[]{:S(2)}, u32[]{:S(2)}) collective-permute-start(bf16[64,8,128]{2,1,0:T(8,128)(2,1)S(1)} %get-tuple-element.54), channel_id=1, source_target_pairs={{0,1},{1,0},{2,3},{3,2},{4,5},{5,4},{6,7},{7,6},{8,9},{9,8},{10,11... | collective-permute-start | bytes 393224 | tf_op jit(solution)/shard_map/ppermute | solution.py:472

commit v24 on v23

--- a/solution.py
+++ b/solution.py
@@ -121,6 +121,80 @@
         pack_panels(panels, both_ref)
 
 
+def gated_side(panels, rows, chunk, tokens, products, half_mask):
+    channels = products.shape[0] // 2
+    gated = (jnp.tanh(products[:channels]) + 1.0) * (products[channels:] * half_mask)
+    for h, r in enumerate(chunk):
+        for c in range(0, channels, 8):
+            for t in range(tokens // LANES):
+                first = h * tokens + t * LANES
+                panels[t, pl.ds(c * rows + r, 8, stride=rows), :] = gated[c : c + 8, first : first + LANES]
+
+
+def split_side(panels, core_ref, own_ref, other_ref):
+    size = own_ref.shape[0]
+    for t in range(own_ref.shape[1] // LANES):
+        for half, ref in ((core_ref[0], own_ref), (1 - core_ref[0], other_ref)):
+            start = pl.multiple_of(half * size, size)
+            ref[:, t * LANES : (t + 1) * LANES] = panels[t, pl.ds(start, size), :].astype(BF16)
+
+
+def side_weights(proj_ref, side, channels):
+    gate, value = [proj_ref[0, :, (2 * side + n) * channels : (2 * side + n + 1) * channels].T for n in range(2)]
+    return jnp.concatenate([gate * 0.5, value], axis=0)
+
+
+def fetch(pairs, sems):
+    copies = [pltpu.make_async_copy(src, dst, sems.at[n]) for n, (src, dst) in enumerate(pairs)]
+    for copy in copies:
+        copy.start()
+    for copy in copies:
+        copy.wait()
+
+
+def right_kernel(core_ref, pair_hbm, mask_hbm, gain_hbm, bias_hbm, proj_hbm, *refs):
+    own_ref, other_ref, pair_t_ref, normed_t_ref, mask_ref, columns_ref = refs[:6]
+    pair_ref, gain_ref, bias_ref, proj_ref, panels, sems = refs[6:]
+    held = (pair_ref, mask_ref, gain_ref, bias_ref, proj_ref)
+    fetch(zip((pair_hbm, mask_hbm, gain_hbm, bias_hbm, proj_hbm), held), sems)
+    rows, tokens, channels = pair_ref.shape
+    small = jnp.concatenate([ref[which] for ref in (gain_ref, bias_ref) for which in range(2)], axis=0).T
+    for n in range(4):
+        for side in range(2):
+            place = 4 * side + n
+            columns_ref[2 * n + side] = jnp.broadcast_to(small[:, place : place + 1], (channels, tokens))
+    weights = side_weights(proj_ref, 1, channels)
+    for chunk in chunks(rows, tokens, 256):
+        part = span(chunk, tokens)
+        pair_t = lanes([pair_ref[r].T for r in chunk])
+        pair_t_ref[:, part] = pair_t
+        normed = affine(unit(pair_t.astype(F32), 0), columns_ref[0], columns_ref[1], tokens)
+        normed_t_ref[:, part] = normed
+        gated_side(panels, rows, chunk, tokens, dot(weights, normed, NN), half_lanes(mask_ref, chunk))
+    split_side(panels, core_ref, own_ref, other_ref)
+
+
+def left_kernel(core_ref, normed_t_ref, mask_ref, proj_hbm, gatew_hbm, outw_hbm, *refs):
+    own_ref, other_ref, gate_t_ref, proj_t_ref, outw_t_ref, proj_ref, gatew_ref, outw_ref, panels, sems = refs
+    fetch(zip((proj_hbm, gatew_hbm, outw_hbm), (proj_ref, gatew_ref, outw_ref)), sems)
+    rows, tokens = mask_ref.shape
+    channels = normed_t_ref.shape[0]
+    weights = side_weights(proj_ref, 0, channels)
+    gate_weights = gatew_ref[0].T * 0.5
+    for chunk in chunks(rows, tokens, 256):
+        part = span(chunk, tokens)
+        normed = normed_t_ref[:, part]
+        gated_side(panels, rows, chunk, tokens, dot(weights, normed, NN), half_lanes(mask_ref, chunk))
+        gate_t_ref[:, part] = (0.5 * jnp.tanh(dot(gate_weights, normed, NN)) + 0.5).astype(BF16)
+    split_side(panels, core_ref, own_ref, other_ref)
+    for part in range(4):
+        block = proj_ref[1, :, part * channels : (part + 1) * channels].T
+        proj_t_ref[1, part * channels : (part + 1) * channels] = block if part % 2 else block * 0.5
+    proj_t_ref[1, 4 * channels :] = gatew_ref[1].T * 0.5
+    for which in range(2):
+        outw_t_ref[which] = outw_ref[which].T
+
+
 def mix_kernel(per_group, rows, incoming, both_ref, product_ref):
     groups, _, tokens = both_ref.shape
     step = 2 * rows
@@ -350,27 +424,57 @@
     core = (lax.axis_index("row") % 2).astype(jnp.int32).reshape(1)
     half_shape = shape((half * rows, tokens), BF16)
     projected = (half_shape,) * 4 if by_core else (both_shape,)
-    results = pl.pallas_call(
-        functools.partial(project_kernel, half if by_core else per_group, by_core),
-        out_shape=projected
-        + (
-            flat_shape,
-            flat_shape,
-            shape((rows, tokens), inputs[1].dtype),
-            shape((8, channels, tokens), F32),
-            shape((2, 5 * channels, channels), BF16),
-            shape((2, channels, channels), BF16),
-        ),
-        in_specs=[smem] * by_core + [hbm] * 7,
-        out_specs=(whole,) * (len(projected) + 6),
-        scratch_shapes=[pltpu.VMEM(inputs[n].shape, inputs[n].dtype) for n in (0, 2, 3, 4, 5, 6)]
-        + [panels, pltpu.SemaphoreType.DMA((7,))],
-        compiler_params=params,
-        name="project",
-    )(*[core] * by_core, *(pltpu.with_memory_space_constraint(a, pltpu.HBM) for a in inputs))
-    pair_t, gate_t, mask, columns, proj_t, outw_t = results[-6:]
+    columns_shape = shape((8, channels, tokens), F32)
+    proj_t_shape = shape((2, 5 * channels, channels), BF16)
     if by_core:
-        left, right, other_left, other_right = results[:4]
+        pair, mask, gains, biases, proj, gatew, outw = (
+            pltpu.with_memory_space_constraint(a, pltpu.HBM) for a in inputs
+        )
+        side_panels = pltpu.VMEM((tokens // LANES, channels * rows, LANES), F32)
+
+        def held(*arrays):
+            return [pltpu.VMEM(a.shape, a.dtype) for a in arrays] + [side_panels, pltpu.SemaphoreType.DMA((len(arrays) + 1,))]
+
+        right, other_right, pair_t, normed_t, mask, columns = pl.pallas_call(
+            right_kernel,
+            out_shape=(half_shape, half_shape, flat_shape, flat_shape, shape(mask.shape, mask.dtype), columns_shape),
+            in_specs=[smem] + [hbm] * 5,
+            out_specs=(whole,) * 6,
+            scratch_shapes=held(pair, gains, biases, proj),
+            compiler_params=params,
+            name="project_right",
+        )(core, pair, mask, gains, biases, proj)
+        left, other_left, gate_t, proj_t, outw_t = pl.pallas_call(
+            left_kernel,
+            out_shape=(half_shape, half_shape, flat_shape, proj_t_shape, shape(outw.shape, BF16)),
+            in_specs=[smem] + [whole] * 2 + [hbm] * 3,
+            out_specs=(whole,) * 5,
+            scratch_shapes=held(proj, gatew, outw),
+            compiler_params=params,
+            cost_estimate=pl.CostEstimate(flops=10**9, bytes_accessed=4 * 2**20, transcendentals=0),
+            name="project_left",
+        )(core, normed_t, mask, proj, gatew, outw)
+    else:
+        results = pl.pallas_call(
+            functools.partial(project_kernel, half if by_core else per_group, by_core),
+            out_shape=projected
+            + (
+                flat_shape,
+                flat_shape,
+                shape((rows, tokens), inputs[1].dtype),
+                shape((8, channels, tokens), F32),
+                shape((2, 5 * channels, channels), BF16),
+                shape((2, channels, channels), BF16),
+            ),
+            in_specs=[smem] * by_core + [hbm] * 7,
+            out_specs=(whole,) * (len(projected) + 6),
+            scratch_shapes=[pltpu.VMEM(inputs[n].shape, inputs[n].dtype) for n in (0, 2, 3, 4, 5, 6)]
+            + [panels, pltpu.SemaphoreType.DMA((7,))],
+            compiler_params=params,
+            name="project",
+        )(*[core] * by_core, *(pltpu.with_memory_space_constraint(a, pltpu.HBM) for a in inputs))
+        pair_t, gate_t, mask, columns, proj_t, outw_t = results[-6:]
+    if by_core:
         chips = groups // 2
         ring = ring_chips(chips)
 

time: 65 us -> 65.4 us (level)
  waiting for transfers between devices: 23.2 us -> 21.7 us
  Pallas kernels: 7.86 us -> 8.97 us
  starting transfers between devices: 32.7 us -> 33.5 us
    pallas_call x1 -> x2, Pallas kernels: 2 us -> 3.1 us  [the longest x1 1.68 us: on_device(): pl.pallas_call(right_kernel, out_shape=(half_shape, half_shape, flat_shap...]
    ppermute x28, waiting for transfers between devices: 19.4 us -> 18.5 us  [along(): return lax.ppermute(array, 'row', pairs)]
    ppermute x28, starting transfers between devices: 31.5 us -> 32.2 us  [along(): return lax.ppermute(array, 'row', pairs)]
  transfers between devices with their start and end apart: 34 -> 34, of which waited for: 22 -> 21; matrix products, arithmetic and copies ran while one was open for 1% -> 1% of each run, Pallas kernels for 3% -> 5%
where the time goes in v24:
time: 65.4 us; the launch traced here: 65.2 us
  starting transfers between devices  33.5 us (51%)
  waiting for transfers between devices  21.7 us (33%)
  Pallas kernels  8.97 us (14%)
  other arithmetic  0.73 us (1%)
    ppermute x28, starting transfers between devices, along(): return lax.ppermute(array, 'row', pairs)  32.2 us
    ppermute x28, waiting for transfers between devices, along(): return lax.ppermute(array, 'row', pairs)  18.5 us
    ppermute x2, waiting for transfers between devices, on_device(): lax.ppermute(send, 'row', swap).reshape(half * rows, tokens)  2.58 us
    pallas_call x1, Pallas kernels, on_device(): pl.pallas_call(right_kernel, out_shape=(half_shape, half_shape, flat_shap...  1.68 us
    pallas_call x1, Pallas kernels, on_device(): pl.pallas_call(left_kernel, out_shape=(half_shape, half_shape, flat_shape...  1.42 us
    pallas_call x1, Pallas kernels, on_device(): pl.pallas_call(functools.partial(step_kernel, half if by_core else per_gr...  1.38 us
    pallas_call x2, Pallas kernels, on_device(): pl.pallas_call(functools.partial(scatter_start, piece * size, hops[0], ch...  1.33 us
  transfers between devices with their start and end apart: 34, of which 21 were waited for; matrix products, arithmetic and copies ran while one was open for 1% of the time, Pallas kernels for 5%

profile of v24, /device:TPU:0, one launch (start us, length us, event | category | flops | bytes accessed | tf_op | source)
XLA Modules:
  0.0 65.2 jit_solution(17270571215579618688)
XLA Ops:
  0.0 1.7 %project_right.1 = (bf16[512,128]{1,0:T(8,128)(2,1)S(1)}, bf16[512,128]{1,0:T(8,128)(2,1)S(1)}, bf16[128,1024]{1,0:T(8,128)(2,1)S(1)}, bf16[128,1024]{1,0:T(8,12...) custom-call(s32[1]{0:T(128)} %bitcast.core_ref.refs_0_, bf16[8,128,128]{2,1,0:T(8,128)(2,1)} %pair_hbm.1, ...), custom_call_target="tpu_custom_call" | custom-call | tf_op jit(solution)/shard_map/project_right/pallas_call | solution.py:438
  1.7 3.0 %collective-permute-start.4 = (bf16[512,128]{1,0:T(8,128)(2,1)S(1)}, bf16[512,128]{1,0:T(8,128)(2,1)S(1)}, u32[]{:S(2)}, u32[]{:S(2)}) collective-permute-start(bf16[512,128]{1,0:T(8,128)(2,1)S(1)} %get-tuple-element.36), channel_id=1, source_target_pairs={{0,2},{1,3},{4,0},{5,1},{8,4},{9,5},{12,8},{13,9},{14,12},{15,13},... | collective-permute-start | bytes 393224 | tf_op jit(solution)/shard_map/ppermute | solution.py:483
  4.7 0.1 collective-permute-start.2
  4.8 1.4 %project_left.1 = (bf16[512,128]{1,0:T(8,128)(2,1)S(1)}, bf16[512,128]{1,0:T(8,128)(2,1)S(1)}, bf16[128,1024]{1,0:T(8,128)(2,1)S(1)}, bf16[2,640,128]{2,1,0:T(8,128)(2,1)S(1)}, bf16[2,128,128]{2,1,0:T(8,128)(2,1)S(1)}) custom-call(s32[1]{0:T(128)} %bitcast.core_ref.refs_0_, bf16[128,1024]{1,0:T(8,128)(2,1)S(1)} %get-tuple-element.32.normed_t_ref, ...), custom_call_target="tpu_custom_call" | custom-call | flops 1000000000 | bytes 4194304 | tf_op jit(solution)/shard_map/project_left/pallas_call | solution.py:447
  6.3 0.6 collective-permute-start
  7.0 0.2 fusion.1.order_ref
  7.2 0.1 fusion.2.order_ref
  7.3 2.0 %collective-permute-start.5 = (bf16[512,128]{1,0:T(8,128)(2,1)S(1)}, bf16[512,128]{1,0:T(8,128)(2,1)S(1)}, u32[]{:S(2)}, u32[]{:S(2)}) collective-permute-start(bf16[512,128]{1,0:T(8,128)(2,1)S(1)} %collective-permute-done.1), channel_id=1, source_target_pairs={{0,2},{1,3},{4,0},{5,1},{8,4},{9,5},{12,8},{13,9},{14,12},{15,13},... | collective-permute-start | bytes 393224 | tf_op jit(solution)/shard_map/ppermute | solution.py:483
  9.3 0.2 collective-permute-start.3
  9.4 0.2 collective-permute-done.2
  9.7 1.7 %collective-permute-start.6 = (bf16[512,128]{1,0:T(8,128)(2,1)S(1)}, bf16[512,128]{1,0:T(8,128)(2,1)S(1)}, u32[]{:S(2)}, u32[]{:S(2)}) collective-permute-start(bf16[512,128]{1,0:T(8,128)(2,1)S(1)} %collective-permute-done.2), channel_id=1, source_target_pairs={{0,4},{1,5},{4,8},{5,9},{8,12},{9,13},{12,14},{13,15},{14,10},{15,... | collective-permute-start | bytes 393224 | tf_op jit(solution)/shard_map/ppermute | solution.py:483
  11.4 1.7 %collective-permute-done.5 = bf16[512,128]{1,0:T(8,128)(2,1)S(1)} collective-permute-done((bf16[512,128]{1,0:T(8,128)(2,1)S(1)}, bf16[512,128]{1,0:T(8,128)(2,1)S(1)}, u32[]{:S(2)}, u32[]{:S(2)}) %collective-permute-start.5) | collective-permute-done | bytes 131104 | tf_op jit(solution)/shard_map/ppermute | solution.py:483
  13.2 1.7 %collective-permute-start.9 = (bf16[512,128]{1,0:T(8,128)(2,1)S(1)}, bf16[512,128]{1,0:T(8,128)(2,1)S(1)}, u32[]{:S(2)}, u32[]{:S(2)}) collective-permute-start(bf16[512,128]{1,0:T(8,128)(2,1)S(1)} %collective-permute-done.5), channel_id=1, source_target_pairs={{0,2},{1,3},{4,0},{5,1},{8,4},{9,5},{12,8},{13,9},{14,12},{15,13},... | collective-permute-start | bytes 393224 | tf_op jit(solution)/shard_map/ppermute | solution.py:483
  14.9 1.6 %collective-permute-start.8 = (bf16[512,128]{1,0:T(8,128)(2,1)S(1)}, bf16[512,128]{1,0:T(8,128)(2,1)S(1)}, u32[]{:S(2)}, u32[]{:S(2)}) collective-permute-start(bf16[512,128]{1,0:T(8,128)(2,1)S(1)} %collective-permute-done.4), channel_id=1, source_target_pairs={{0,2},{1,3},{4,0},{5,1},{8,4},{9,5},{12,8},{13,9},{14,12},{15,13},... | collective-permute-start | bytes 393224 | tf_op jit(solution)/shard_map/ppermute | solution.py:483
  16.5 0.4 collective-permute-start.7
  17.0 0.5 collective-permute-done.6
  17.4 0.4 collective-permute-start.10
  17.8 1.8 %collective-permute-done.9 = bf16[512,128]{1,0:T(8,128)(2,1)S(1)} collective-permute-done((bf16[512,128]{1,0:T(8,128)(2,1)S(1)}, bf16[512,128]{1,0:T(8,128)(2,1)S(1)}, u32[]{:S(2)}, u32[]{:S(2)}) %collective-permute-start.9) | collective-permute-done | bytes 131104 | tf_op jit(solution)/shard_map/ppermute | solution.py:483
  19.6 1.5 %collective-permute-start.13 = (bf16[512,128]{1,0:T(8,128)(2,1)S(1)}, bf16[512,128]{1,0:T(8,128)(2,1)S(1)}, u32[]{:S(2)}, u32[]{:S(2)}) collective-permute-start(bf16[512,128]{1,0:T(8,128)(2,1)S(1)} %collective-permute-done.9), channel_id=1, source_target_pairs={{0,2},{1,3},{4,0},{5,1},{8,4},{9,5},{12,8},{13,9},{14,12},{15,13},... | collective-permute-start | bytes 393224 | tf_op jit(solution)/shard_map/ppermute | solution.py:483
  21.1 1.3 %collective-permute-done.8 = bf16[512,128]{1,0:T(8,128)(2,1)S(1)} collective-permute-done((bf16[512,128]{1,0:T(8,128)(2,1)S(1)}, bf16[512,128]{1,0:T(8,128)(2,1)S(1)}, u32[]{:S(2)}, u32[]{:S(2)}) %collective-permute-start.8) | collective-permute-done | bytes 131104 | tf_op jit(solution)/shard_map/ppermute | solution.py:483
  22.4 1.5 %collective-permute-start.12 = (bf16[512,128]{1,0:T(8,128)(2,1)S(1)}, bf16[512,128]{1,0:T(8,128)(2,1)S(1)}, u32[]{:S(2)}, u32[]{:S(2)}) collective-permute-start(bf16[512,128]{1,0:T(8,128)(2,1)S(1)} %collective-permute-done.8), channel_id=1, source_target_pairs={{0,2},{1,3},{4,0},{5,1},{8,4},{9,5},{12,8},{13,9},{14,12},{15,13},... | collective-permute-start | bytes 393224 | tf_op jit(solution)/shard_map/ppermute | solution.py:483
  23.9 0.6 collective-permute-start.11
  24.4 1.6 %collective-permute-start.14 = (bf16[512,128]{1,0:T(8,128)(2,1)S(1)}, bf16[512,128]{1,0:T(8,128)(2,1)S(1)}, u32[]{:S(2)}, u32[]{:S(2)}) collective-permute-start(bf16[512,128]{1,0:T(8,128)(2,1)S(1)} %collective-permute-done.10), channel_id=1, source_target_pairs={{0,4},{1,5},{4,8},{5,9},{8,12},{9,13},{12,14},{13,15},{14,10},{15,... | collective-permute-start | bytes 393224 | tf_op jit(solution)/shard_map/ppermute | solution.py:483
  26.0 0.7 %collective-permute-start.15 = (bf16[512,128]{1,0:T(8,128)(2,1)S(1)}, bf16[512,128]{1,0:T(8,128)(2,1)S(1)}, u32[]{:S(2)}, u32[]{:S(2)}) collective-permute-start(bf16[512,128]{1,0:T(8,128)(2,1)S(1)} %collective-permute-done.13), channel_id=1, source_target_pairs={{0,2},{1,3},{4,0},{5,1},{8,4},{9,5},{12,8},{13,9},{14,12},{15,13},... | collective-permute-start | bytes 393224 | tf_op jit(solution)/shard_map/ppermute | solution.py:483
  26.7 0.9 %mix_early.1.early_ref = bf16[64,16,128]{2,1,0:T(8,128)(2,1)S(1)} custom-call(bf16[80,128]{1,0:T(8,128)(2,1)S(1)} %fusion.1.order_ref, bf16[64,8,128]{2,1,0:T(8,128)(2,1)S(1)} %bitcast.35, bf16[64,8,128]{2,1,0:T(8,128)(2,1)S(1)} %bitcast.37, bf16[64,8,128]{2,1,0:T(8,128)(2,1)S(1)} %bitcast.49, bf16[64,8,128]{2,1,0:T(8,128)(2,1)S(1)} %bitcast.52, ...), custom_call_target="tpu_custom_call" | custom-call | flops 1000000000 | bytes 4194304 | tf_op jit(solution)/shard_map/mix_early/pallas_call | solution.py:504
  27.6 0.4 collective-permute-done.12
  28.0 0.8 %collective-permute-done.11 = bf16[512,128]{1,0:T(8,128)(2,1)S(1)} collective-permute-done((bf16[512,128]{1,0:T(8,128)(2,1)S(1)}, bf16[512,128]{1,0:T(8,128)(2,1)S(1)}, u32[]{:S(2)}, u32[]{:S(2)}) %collective-permute-start.11) | collective-permute-done | bytes 131104 | tf_op jit(solution)/shard_map/ppermute | solution.py:483
  28.8 1.4 %collective-permute-done.14 = bf16[512,128]{1,0:T(8,128)(2,1)S(1)} collective-permute-done((bf16[512,128]{1,0:T(8,128)(2,1)S(1)}, bf16[512,128]{1,0:T(8,128)(2,1)S(1)}, u32[]{:S(2)}, u32[]{:S(2)}) %collective-permute-start.14) | collective-permute-done | bytes 131104 | tf_op jit(solution)/shard_map/ppermute | solution.py:483
  30.2 0.8 %collective-permute-done.15 = bf16[512,128]{1,0:T(8,128)(2,1)S(1)} collective-permute-done((bf16[512,128]{1,0:T(8,128)(2,1)S(1)}, bf16[512,128]{1,0:T(8,128)(2,1)S(1)}, u32[]{:S(2)}, u32[]{:S(2)}) %collective-permute-start.15) | collective-permute-done | bytes 131104 | tf_op jit(solution)/shard_map/ppermute | solution.py:483
  31.0 0.7 %mix_late.1 = (bf16[64,8,128]{2,1,0:T(8,128)(2,1)S(1)}, bf16[64,8,128]{2,1,0:T(8,128)(2,1)S(1)}) custom-call(bf16[48,128]{1,0:T(8,128)(2,1)S(1)} %fusion.2.order_ref, bf16[64,8,128]{2,1,0:T(8,128)(2,1)S(1)} %bitcast.36, bf16[64,8,128]{2,1,0:T(8,128)(2,1)S(1)} %bitcast.38, bf16[64,16,128]{2,1,0:T(8,128)(2,1)S(1)} %mix_early.1.early_ref, ...), custom_call_target="tpu_custom_call" | custom-call | tf_op jit(solution)/shard_map/mix_late/pallas_call | solution.py:514
  31.8 1.2 %collective-permute-done.16 = bf16[64,8,128]{2,1,0:T(8,128)(2,1)S(1)} collective-permute-done((bf16[64,8,128]{2,1,0:T(8,128)(2,1)S(1)}, bf16[64,8,128]{2,1,0:T(8,128)(2,1)S(1)}, u32[]{:S(2)}, u32[]{:S(2)}) %collective-permute-start.16) | collective-permute-done | bytes 131104 | tf_op jit(solution)/shard_map/ppermute | solution.py:523
  33.1 1.4 %finish_project.1 = (bf16[512,128]{1,0:T(8,128)(2,1)S(1)}, bf16[512,128]{1,0:T(8,128)(2,1)S(1)}, bf16[512,128]{1,0:T(8,128)(2,1)S(1)}, bf16[512,128]{1,0:T(8,128...) custom-call(s32[1]{0:T(128)} %bitcast.core_ref.refs_0_, bf16[512,128]{1,0:T(8,128)(2,1)S(1)} %bitcast.39, ...), custom_call_target="tpu_custom_call" | custom-call | tf_op jit(solution)/shard_map/finish_project/pallas_call | solution.py:526
  34.4 0.2 collective-permute-start.17
  34.7 0.4 collective-permute-start.18
  35.0 0.3 fusion.order_ref
  35.4 0.5 collective-permute-done.17
  35.9 0.2 collective-permute-done.18
  36.0 0.7 %scatter_start.3 = (f32[32,128,128]{2,1,0:T(8,128)S(1)}, bf16[32,16,128]{2,1,0:T(8,128)(2,1)S(1)}, bf16[32,16,128]{2,1,0:T(8,128)(2,1)S(1)}) custom-call(bf16[128,128]{1,0:T(8,128)(2,1)S(1)} %fusion.order_ref, bf16[64,8,128]{2,1,0:T(8,128)(2,1)S(1)} %bitcast.27, bf16[64,8,128]{2,1,0:T(8,128)(2,1)S(1)} %bitcast.31, bf16[64,8,128]{2,1,0:T(8,128)(2,1)S(1)} %bitcast.29, ...), custom_call_target="tpu_custom_call" | custom-call | tf_op jit(solution)/shard_map/scatter_start/pallas_call | solution.py:547
  36.7 0.9 %collective-permute-start.29 = (bf16[32,16,128]{2,1,0:T(8,128)(2,1)S(1)}, bf16[32,16,128]{2,1,0:T(8,128)(2,1)S(1)}, u32[]{:S(2)}, u32[]{:S(2)}) collective-permute-start(bf16[32,16,128]{2,1,0:T(8,128)(2,1)S(1)} %get-tuple-element.54), channel_id=1, source_target_pairs={{0,2},{1,3},{4,0},{5,1},{8,4},{9,5},{12,8},{13,9},{14,12},{15,13},... | collective-permute-start | bytes 393224 | tf_op jit(solution)/shard_map/ppermute | solution.py:483
  37.6 0.7 %scatter_start.2 = (f32[32,128,128]{2,1,0:T(8,128)S(1)}, bf16[32,16,128]{2,1,0:T(8,128)(2,1)S(1)}, bf16[32,16,128]{2,1,0:T(8,128)(2,1)S(1)}) custom-call(bf16[128,128]{1,0:T(8,128)(2,1)S(1)} %fusion.order_ref, bf16[64,8,128]{2,1,0:T(8,128)(2,1)S(1)} %bitcast.28, bf16[64,8,128]{2,1,0:T(8,128)(2,1)S(1)} %bitcast.32, bf16[64,8,128]{2,1,0:T(8,128)(2,1)S(1)} %bitcast.30, ...), custom_call_target="tpu_custom_call" | custom-call | tf_op jit(solution)/shard_map/scatter_start/pallas_call | solution.py:547
  38.2 1.3 %collective-permute-start.19 = (bf16[32,16,128]{2,1,0:T(8,128)(2,1)S(1)}, bf16[32,16,128]{2,1,0:T(8,128)(2,1)S(1)}, u32[]{:S(2)}, u32[]{:S(2)}) collective-permute-start(bf16[32,16,128]{2,1,0:T(8,128)(2,1)S(1)} %get-tuple-element.50), channel_id=1, source_target_pairs={{0,4},{1,5},{4,8},{5,9},{8,12},{9,13},{12,14},{13,15},{14,10},{15,... | collective-permute-start | bytes 393224 | tf_op jit(solution)/shard_map/ppermute | solution.py:483
  39.5 1.5 %collective-permute-start.26 = (bf16[32,16,128]{2,1,0:T(8,128)(2,1)S(1)}, bf16[32,16,128]{2,1,0:T(8,128)(2,1)S(1)}, u32[]{:S(2)}, u32[]{:S(2)}) collective-permute-start(bf16[32,16,128]{2,1,0:T(8,128)(2,1)S(1)} %get-tuple-element.53), channel_id=1, source_target_pairs={{0,4},{1,5},{4,8},{5,9},{8,12},{9,13},{12,14},{13,15},{14,10},{15,... | collective-permute-start | bytes 393224 | tf_op jit(solution)/shard_map/ppermute | solution.py:483
  41.0 0.5 collective-permute-start.23
  41.5 1.0 %collective-permute-done.29.got_ref = bf16[32,16,128]{2,1,0:T(8,128)(2,1)S(1)} collective-permute-done((bf16[32,16,128]{2,1,0:T(8,128)(2,1)S(1)}, bf16[32,16,128]{2,1,0:T(8,128)(2,1)S(1)}, u32[]{:S(2)}, u32[]{:S(2)}) %collective-permute-start.29) | collective-permute-done | bytes 131104 | tf_op jit(solution)/shard_map/ppermute | solution.py:483
  42.5 0.9 %collective-permute-start.30 = (bf16[32,16,128]{2,1,0:T(8,128)(2,1)S(1)}, bf16[32,16,128]{2,1,0:T(8,128)(2,1)S(1)}, u32[]{:S(2)}, u32[]{:S(2)}) collective-permute-start(bf16[32,16,128]{2,1,0:T(8,128)(2,1)S(1)} %scatter_add.17), channel_id=1, source_target_pairs={{0,2},{1,3},{4,0},{5,1},{8,4},{9,5},{12,8},{13,9},{14,12},{15,13},... | collective-permute-start | bytes 393224 | tf_op jit(solution)/shard_map/ppermute | solution.py:483
  43.4 1.3 %collective-permute-done.19.got_ref = bf16[32,16,128]{2,1,0:T(8,128)(2,1)S(1)} collective-permute-done((bf16[32,16,128]{2,1,0:T(8,128)(2,1)S(1)}, bf16[32,16,128]{2,1,0:T(8,128)(2,1)S(1)}, u32[]{:S(2)}, u32[]{:S(2)}) %collective-permute-start.19) | collective-permute-done | bytes 131104 | tf_op jit(solution)/shard_map/ppermute | solution.py:483
  44.7 1.3 %collective-permute-start.20 = (bf16[32,16,128]{2,1,0:T(8,128)(2,1)S(1)}, bf16[32,16,128]{2,1,0:T(8,128)(2,1)S(1)}, u32[]{:S(2)}, u32[]{:S(2)}) collective-permute-start(bf16[32,16,128]{2,1,0:T(8,128)(2,1)S(1)} %scatter_add.10), channel_id=1, source_target_pairs={{0,4},{1,5},{4,8},{5,9},{8,12},{9,13},{12,14},{13,15},{14,10},{15,... | collective-permute-start | bytes 393224 | tf_op jit(solution)/shard_map/ppermute | solution.py:483
  45.9 1.5 %collective-permute-done.26.got_ref = bf16[32,16,128]{2,1,0:T(8,128)(2,1)S(1)} collective-permute-done((bf16[32,16,128]{2,1,0:T(8,128)(2,1)S(1)}, bf16[32,16,128]{2,1,0:T(8,128)(2,1)S(1)}, u32[]{:S(2)}, u32[]{:S(2)}) %collective-permute-start.26) | collective-permute-done | bytes 131104 | tf_op jit(solution)/shard_map/ppermute | solution.py:483
  47.5 1.3 %collective-permute-start.27 = (bf16[32,16,128]{2,1,0:T(8,128)(2,1)S(1)}, bf16[32,16,128]{2,1,0:T(8,128)(2,1)S(1)}, u32[]{:S(2)}, u32[]{:S(2)}) collective-permute-start(bf16[32,16,128]{2,1,0:T(8,128)(2,1)S(1)} %scatter_add.15), channel_id=1, source_target_pairs={{0,4},{1,5},{4,8},{5,9},{8,12},{9,13},{12,14},{13,15},{14,10},{15,... | collective-permute-start | bytes 393224 | tf_op jit(solution)/shard_map/ppermute | solution.py:483
  48.8 0.9 %collective-permute-start.24 = (bf16[32,16,128]{2,1,0:T(8,128)(2,1)S(1)}, bf16[32,16,128]{2,1,0:T(8,128)(2,1)S(1)}, u32[]{:S(2)}, u32[]{:S(2)}) collective-permute-start(bf16[32,16,128]{2,1,0:T(8,128)(2,1)S(1)} %scatter_add.13), channel_id=1, source_target_pairs={{0,2},{1,3},{4,0},{5,1},{8,4},{9,5},{12,8},{13,9},{14,12},{15,13},... | collective-permute-start | bytes 393224 | tf_op jit(solution)/shard_map/ppermute | solution.py:483
  49.7 1.6 %collective-permute-start.31 = (bf16[32,16,128]{2,1,0:T(8,128)(2,1)S(1)}, bf16[32,16,128]{2,1,0:T(8,128)(2,1)S(1)}, u32[]{:S(2)}, u32[]{:S(2)}) collective-permute-start(bf16[32,16,128]{2,1,0:T(8,128)(2,1)S(1)} %scatter_add.18), channel_id=1, source_target_pairs={{0,2},{1,3},{4,0},{5,1},{8,4},{9,5},{12,8},{13,9},{14,12},{15,13},... | collective-permute-start | bytes 393224 | tf_op jit(solution)/shard_map/ppermute | solution.py:483
  51.3 0.9 %collective-permute-start.21 = (bf16[32,16,128]{2,1,0:T(8,128)(2,1)S(1)}, bf16[32,16,128]{2,1,0:T(8,128)(2,1)S(1)}, u32[]{:S(2)}, u32[]{:S(2)}) collective-permute-start(bf16[32,16,128]{2,1,0:T(8,128)(2,1)S(1)} %scatter_add.11), channel_id=1, source_target_pairs={{0,4},{1,5},{4,8},{5,9},{8,12},{9,13},{12,14},{13,15},{14,10},{15,... | collective-permute-start | bytes 393224 | tf_op jit(solution)/shard_map/ppermute | solution.py:483
  52.3 1.3 %collective-permute-done.27.got_ref = bf16[32,16,128]{2,1,0:T(8,128)(2,1)S(1)} collective-permute-done((bf16[32,16,128]{2,1,0:T(8,128)(2,1)S(1)}, bf16[32,16,128]{2,1,0:T(8,128)(2,1)S(1)}, u32[]{:S(2)}, u32[]{:S(2)}) %collective-permute-start.27) | collective-permute-done | bytes 131104 | tf_op jit(solution)/shard_map/ppermute | solution.py:483
  53.6 1.7 %collective-permute-start.28 = (bf16[32,16,128]{2,1,0:T(8,128)(2,1)S(1)}, bf16[32,16,128]{2,1,0:T(8,128)(2,1)S(1)}, u32[]{:S(2)}, u32[]{:S(2)}) collective-permute-start(bf16[32,16,128]{2,1,0:T(8,128)(2,1)S(1)} %scatter_add.16), channel_id=1, source_target_pairs={{0,4},{1,5},{4,8},{5,9},{8,12},{9,13},{12,14},{13,15},{14,10},{15,... | collective-permute-start | bytes 393224 | tf_op jit(solution)/shard_map/ppermute | solution.py:483
  55.3 0.5 collective-permute-start.25
  55.8 1.6 %collective-permute-start.32 = (bf16[32,16,128]{2,1,0:T(8,128)(2,1)S(1)}, bf16[32,16,128]{2,1,0:T(8,128)(2,1)S(1)}, u32[]{:S(2)}, u32[]{:S(2)}) collective-permute-start(bf16[32,16,128]{2,1,0:T(8,128)(2,1)S(1)} %scatter_add.19), channel_id=1, source_target_pairs={{0,2},{1,3},{4,0},{5,1},{8,4},{9,5},{12,8},{13,9},{14,12},{15,13},... | collective-permute-start | bytes 393224 | tf_op jit(solution)/shard_map/ppermute | solution.py:483
  57.5 0.6 collective-permute-start.22
  58.0 1.5 %collective-permute-done.28.refs_4_ = bf16[32,16,128]{2,1,0:T(8,128)(2,1)S(1)} collective-permute-done((bf16[32,16,128]{2,1,0:T(8,128)(2,1)S(1)}, bf16[32,16,128]{2,1,0:T(8,128)(2,1)S(1)}, u32[]{:S(2)}, u32[]{:S(2)}) %collective-permute-start.28) | collective-permute-done | bytes 131104 | tf_op jit(solution)/shard_map/ppermute | solution.py:483
  59.6 0.7 %collective-permute-done.25.refs_2_ = bf16[32,16,128]{2,1,0:T(8,128)(2,1)S(1)} collective-permute-done((bf16[32,16,128]{2,1,0:T(8,128)(2,1)S(1)}, bf16[32,16,128]{2,1,0:T(8,128)(2,1)S(1)}, u32[]{:S(2)}, u32[]{:S(2)}) %collective-permute-start.25) | collective-permute-done | bytes 131104 | tf_op jit(solution)/shard_map/ppermute | solution.py:483
  60.3 1.4 %collective-permute-done.32.refs_5_ = bf16[32,16,128]{2,1,0:T(8,128)(2,1)S(1)} collective-permute-done((bf16[32,16,128]{2,1,0:T(8,128)(2,1)S(1)}, bf16[32,16,128]{2,1,0:T(8,128)(2,1)S(1)}, u32[]{:S(2)}, u32[]{:S(2)}) %collective-permute-start.32) | collective-permute-done | bytes 131104 | tf_op jit(solution)/shard_map/ppermute | solution.py:483
  61.7 0.7 %collective-permute-done.22.refs_1_ = bf16[32,16,128]{2,1,0:T(8,128)(2,1)S(1)} collective-permute-done((bf16[32,16,128]{2,1,0:T(8,128)(2,1)S(1)}, bf16[32,16,128]{2,1,0:T(8,128)(2,1)S(1)}, u32[]{:S(2)}, u32[]{:S(2)}) %collective-permute-start.22) | collective-permute-done | bytes 131104 | tf_op jit(solution)/shard_map/ppermute | solution.py:483
  62.5 0.1 scatter_end.1
  62.6 1.3 %collective-permute-done.33 = bf16[64,8,128]{2,1,0:T(8,128)(2,1)S(1)} collective-permute-done((bf16[64,8,128]{2,1,0:T(8,128)(2,1)S(1)}, bf16[64,8,128]{2,1,0:T(8,128)(2,1)S(1)}, u32[]{:S(2)}, u32[]{:S(2)}) %collective-permute-start.33) | collective-permute-done | bytes 131104 | tf_op jit(solution)/shard_map/ppermute | solution.py:576
  64.0 1.3 %finish.1 = bf16[8,128,128]{2,1,0:T(8,128)(2,1)} custom-call(s32[1]{0:T(128)} %bitcast.core_ref.refs_0_, bf16[512,128]{1,0:T(8,128)(2,1)S(1)} %bitcast.47, bf16[512,128]{1,0:T(8,128)(2,1)S(1)} %bitcast.48, bf16[128,1024]{1,0:T(8,128)(2,1)S(1)} %get-tuple-element.57.refs_3_, bf16[128,1024]{1,0:T(8,128)(2,1)S(1)} %get-tuple-element.58.refs_4_, ...), custom_call_target="tpu_custom_call" | custom-call | tf_op jit(solution)/shard_map/finish/pallas_call | solution.py:579
  (45 shorter events, 0.5 us)
Async XLA Ops:
  1.7 13.2 %collective-permute-start.4 = (bf16[512,128]{1,0:T(8,128)(2,1)S(1)}, bf16[512,128]{1,0:T(8,128)(2,1)S(1)}, u32[]{:S(2)}, u32[]{:S(2)}) collective-permute-start(bf16[512,128]{1,0:T(8,128)(2,1)S(1)} %get-tuple-element.36), channel_id=1, source_target_pairs={{0,2},{1,3},{4,0},{5,1},{8,4},{9,5},{12,8},{13,9},{14,12},{15,13},... | collective-permute-start | bytes 393224 | tf_op jit(solution)/shard_map/ppermute | solution.py:483
  4.7 5.0 %collective-permute-start.2 = (bf16[512,128]{1,0:T(8,128)(2,1)S(1)}, bf16[512,128]{1,0:T(8,128)(2,1)S(1)}, u32[]{:S(2)}, u32[]{:S(2)}) collective-permute-start(bf16[512,128]{1,0:T(8,128)(2,1)S(1)} %get-tuple-element.36), channel_id=1, source_target_pairs={{0,4},{1,5},{4,8},{5,9},{8,12},{9,13},{12,14},{13,15},{14,10},{15,... | collective-permute-start | bytes 393224 | tf_op jit(solution)/shard_map/ppermute | solution.py:483
  4.8 2.5 %collective-permute-start.1 = (bf16[512,128]{1,0:T(8,128)(2,1)S(1)}, bf16[512,128]{1,0:T(8,128)(2,1)S(1)}, u32[]{:S(2)}, u32[]{:S(2)}) collective-permute-start(bf16[512,128]{1,0:T(8,128)(2,1)S(1)} %get-tuple-element.37), channel_id=1, source_target_pairs={{0,1},{1,0},{2,3},{3,2},{4,5},{5,4},{6,7},{7,6},{8,9},{9,8},{10,11... | collective-permute-start | bytes 393224 | tf_op jit(solution)/shard_map/ppermute | solution.py:492
  6.3 20.4 %collective-permute-start = (bf16[512,128]{1,0:T(8,128)(2,1)S(1)}, bf16[512,128]{1,0:T(8,128)(2,1)S(1)}, u32[]{:S(2)}, u32[]{:S(2)}) collective-permute-start(bf16[512,128]{1,0:T(8,128)(2,1)S(1)} %get-tuple-element.35), channel_id=1, source_target_pairs={{0,1},{1,0},{2,3},{3,2},{4,5},{5,4},{6,7},{7,6},{8,9},{9,8},{10,11... | collective-permute-start | bytes 393224 | tf_op jit(solution)/shard_map/ppermute | solution.py:493
  7.3 5.9 %collective-permute-start.5 = (bf16[512,128]{1,0:T(8,128)(2,1)S(1)}, bf16[512,128]{1,0:T(8,128)(2,1)S(1)}, u32[]{:S(2)}, u32[]{:S(2)}) collective-permute-start(bf16[512,128]{1,0:T(8,128)(2,1)S(1)} %collective-permute-done.1), channel_id=1, source_target_pairs={{0,2},{1,3},{4,0},{5,1},{8,4},{9,5},{12,8},{13,9},{14,12},{15,13},... | collective-permute-start | bytes 393224 | tf_op jit(solution)/shard_map/ppermute | solution.py:483
  9.3 7.2 %collective-permute-start.3 = (bf16[512,128]{1,0:T(8,128)(2,1)S(1)}, bf16[512,128]{1,0:T(8,128)(2,1)S(1)}, u32[]{:S(2)}, u32[]{:S(2)}) collective-permute-start(bf16[512,128]{1,0:T(8,128)(2,1)S(1)} %collective-permute-done.1), channel_id=1, source_target_pairs={{0,4},{1,5},{4,8},{5,9},{8,12},{9,13},{12,14},{13,15},{14,10},{15,... | collective-permute-start | bytes 393224 | tf_op jit(solution)/shard_map/ppermute | solution.py:483
  9.7 7.8 %collective-permute-start.6 = (bf16[512,128]{1,0:T(8,128)(2,1)S(1)}, bf16[512,128]{1,0:T(8,128)(2,1)S(1)}, u32[]{:S(2)}, u32[]{:S(2)}) collective-permute-start(bf16[512,128]{1,0:T(8,128)(2,1)S(1)} %collective-permute-done.2), channel_id=1, source_target_pairs={{0,4},{1,5},{4,8},{5,9},{8,12},{9,13},{12,14},{13,15},{14,10},{15,... | collective-permute-start | bytes 393224 | tf_op jit(solution)/shard_map/ppermute | solution.py:483
  13.2 6.4 %collective-permute-start.9 = (bf16[512,128]{1,0:T(8,128)(2,1)S(1)}, bf16[512,128]{1,0:T(8,128)(2,1)S(1)}, u32[]{:S(2)}, u32[]{:S(2)}) collective-permute-start(bf16[512,128]{1,0:T(8,128)(2,1)S(1)} %collective-permute-done.5), channel_id=1, source_target_pairs={{0,2},{1,3},{4,0},{5,1},{8,4},{9,5},{12,8},{13,9},{14,12},{15,13},... | collective-permute-start | bytes 393224 | tf_op jit(solution)/shard_map/ppermute | solution.py:483
  14.9 7.5 %collective-permute-start.8 = (bf16[512,128]{1,0:T(8,128)(2,1)S(1)}, bf16[512,128]{1,0:T(8,128)(2,1)S(1)}, u32[]{:S(2)}, u32[]{:S(2)}) collective-permute-start(bf16[512,128]{1,0:T(8,128)(2,1)S(1)} %collective-permute-done.4), channel_id=1, source_target_pairs={{0,2},{1,3},{4,0},{5,1},{8,4},{9,5},{12,8},{13,9},{14,12},{15,13},... | collective-permute-start | bytes 393224 | tf_op jit(solution)/shard_map/ppermute | solution.py:483
  16.5 7.3 %collective-permute-start.7 = (bf16[512,128]{1,0:T(8,128)(2,1)S(1)}, bf16[512,128]{1,0:T(8,128)(2,1)S(1)}, u32[]{:S(2)}, u32[]{:S(2)}) collective-permute-start(bf16[512,128]{1,0:T(8,128)(2,1)S(1)} %collective-permute-done.3), channel_id=1, source_target_pairs={{0,4},{1,5},{4,8},{5,9},{8,12},{9,13},{12,14},{13,15},{14,10},{15,... | collective-permute-start | bytes 393224 | tf_op jit(solution)/shard_map/ppermute | solution.py:483
  17.4 7.0 %collective-permute-start.10 = (bf16[512,128]{1,0:T(8,128)(2,1)S(1)}, bf16[512,128]{1,0:T(8,128)(2,1)S(1)}, u32[]{:S(2)}, u32[]{:S(2)}) collective-permute-start(bf16[512,128]{1,0:T(8,128)(2,1)S(1)} %collective-permute-done.6), channel_id=1, source_target_pairs={{0,4},{1,5},{4,8},{5,9},{8,12},{9,13},{12,14},{13,15},{14,10},{15,... | collective-permute-start | bytes 393224 | tf_op jit(solution)/shard_map/ppermute | solution.py:483
  19.6 6.4 %collective-permute-start.13 = (bf16[512,128]{1,0:T(8,128)(2,1)S(1)}, bf16[512,128]{1,0:T(8,128)(2,1)S(1)}, u32[]{:S(2)}, u32[]{:S(2)}) collective-permute-start(bf16[512,128]{1,0:T(8,128)(2,1)S(1)} %collective-permute-done.9), channel_id=1, source_target_pairs={{0,2},{1,3},{4,0},{5,1},{8,4},{9,5},{12,8},{13,9},{14,12},{15,13},... | collective-permute-start | bytes 393224 | tf_op jit(solution)/shard_map/ppermute | solution.py:483
  22.4 5.6 %collective-permute-start.12 = (bf16[512,128]{1,0:T(8,128)(2,1)S(1)}, bf16[512,128]{1,0:T(8,128)(2,1)S(1)}, u32[]{:S(2)}, u32[]{:S(2)}) collective-permute-start(bf16[512,128]{1,0:T(8,128)(2,1)S(1)} %collective-permute-done.8), channel_id=1, source_target_pairs={{0,2},{1,3},{4,0},{5,1},{8,4},{9,5},{12,8},{13,9},{14,12},{15,13},... | collective-permute-start | bytes 393224 | tf_op jit(solution)/shard_map/ppermute | solution.py:483
  23.9 5.0 %collective-permute-start.11 = (bf16[512,128]{1,0:T(8,128)(2,1)S(1)}, bf16[512,128]{1,0:T(8,128)(2,1)S(1)}, u32[]{:S(2)}, u32[]{:S(2)}) collective-permute-start(bf16[512,128]{1,0:T(8,128)(2,1)S(1)} %collective-permute-done.7), channel_id=1, source_target_pairs={{0,4},{1,5},{4,8},{5,9},{8,12},{9,13},{12,14},{13,15},{14,10},{15,... | collective-permute-start | bytes 393224 | tf_op jit(solution)/shard_map/ppermute | solution.py:483
  24.4 5.8 %collective-permute-start.14 = (bf16[512,128]{1,0:T(8,128)(2,1)S(1)}, bf16[512,128]{1,0:T(8,128)(2,1)S(1)}, u32[]{:S(2)}, u32[]{:S(2)}) collective-permute-start(bf16[512,128]{1,0:T(8,128)(2,1)S(1)} %collective-permute-done.10), channel_id=1, source_target_pairs={{0,4},{1,5},{4,8},{5,9},{8,12},{9,13},{12,14},{13,15},{14,10},{15,... | collective-permute-start | bytes 393224 | tf_op jit(solution)/shard_map/ppermute | solution.py:483
  26.0 5.0 %collective-permute-start.15 = (bf16[512,128]{1,0:T(8,128)(2,1)S(1)}, bf16[512,128]{1,0:T(8,128)(2,1)S(1)}, u32[]{:S(2)}, u32[]{:S(2)}) collective-permute-start(bf16[512,128]{1,0:T(8,128)(2,1)S(1)} %collective-permute-done.13), channel_id=1, source_target_pairs={{0,2},{1,3},{4,0},{5,1},{8,4},{9,5},{12,8},{13,9},{14,12},{15,13},... | collective-permute-start | bytes 393224 | tf_op jit(solution)/shard_map/ppermute | solution.py:483
  31.7 1.4 %collective-permute-start.16 = (bf16[64,8,128]{2,1,0:T(8,128)(2,1)S(1)}, bf16[64,8,128]{2,1,0:T(8,128)(2,1)S(1)}, u32[]{:S(2)}, u32[]{:S(2)}) collective-permute-start(bf16[64,8,128]{2,1,0:T(8,128)(2,1)S(1)} %get-tuple-element.39), channel_id=1, source_target_pairs={{0,1},{1,0},{2,3},{3,2},{4,5},{5,4},{6,7},{7,6},{8,9},{9,8},{10,11... | collective-permute-start | bytes 393224 | tf_op jit(solution)/shard_map/ppermute | solution.py:523
  34.4 1.4 %collective-permute-start.17 = (bf16[512,128]{1,0:T(8,128)(2,1)S(1)}, bf16[512,128]{1,0:T(8,128)(2,1)S(1)}, u32[]{:S(2)}, u32[]{:S(2)}) collective-permute-start(bf16[512,128]{1,0:T(8,128)(2,1)S(1)} %get-tuple-element.46), channel_id=1, source_target_pairs={{0,1},{1,0},{2,3},{3,2},{4,5},{5,4},{6,7},{7,6},{8,9},{9,8},{10,11... | collective-permute-start | bytes 393224 | tf_op jit(solution)/shard_map/ppermute | solution.py:538
  34.7 1.4 %collective-permute-start.18 = (bf16[512,128]{1,0:T(8,128)(2,1)S(1)}, bf16[512,128]{1,0:T(8,128)(2,1)S(1)}, u32[]{:S(2)}, u32[]{:S(2)}) collective-permute-start(bf16[512,128]{1,0:T(8,128)(2,1)S(1)} %get-tuple-element.48), channel_id=1, source_target_pairs={{0,1},{1,0},{2,3},{3,2},{4,5},{5,4},{6,7},{7,6},{8,9},{9,8},{10,11... | collective-permute-start | bytes 393224 | tf_op jit(solution)/shard_map/ppermute | solution.py:539
  36.7 5.8 %collective-permute-start.29 = (bf16[32,16,128]{2,1,0:T(8,128)(2,1)S(1)}, bf16[32,16,128]{2,1,0:T(8,128)(2,1)S(1)}, u32[]{:S(2)}, u32[]{:S(2)}) collective-permute-start(bf16[32,16,128]{2,1,0:T(8,128)(2,1)S(1)} %get-tuple-element.54), channel_id=1, source_target_pairs={{0,2},{1,3},{4,0},{5,1},{8,4},{9,5},{12,8},{13,9},{14,12},{15,13},... | collective-permute-start | bytes 393224 | tf_op jit(solution)/shard_map/ppermute | solution.py:483
  38.2 6.4 %collective-permute-start.19 = (bf16[32,16,128]{2,1,0:T(8,128)(2,1)S(1)}, bf16[32,16,128]{2,1,0:T(8,128)(2,1)S(1)}, u32[]{:S(2)}, u32[]{:S(2)}) collective-permute-start(bf16[32,16,128]{2,1,0:T(8,128)(2,1)S(1)} %get-tuple-element.50), channel_id=1, source_target_pairs={{0,4},{1,5},{4,8},{5,9},{8,12},{9,13},{12,14},{13,15},{14,10},{15,... | collective-permute-start | bytes 393224 | tf_op jit(solution)/shard_map/ppermute | solution.py:483
  39.5 7.9 %collective-permute-start.26 = (bf16[32,16,128]{2,1,0:T(8,128)(2,1)S(1)}, bf16[32,16,128]{2,1,0:T(8,128)(2,1)S(1)}, u32[]{:S(2)}, u32[]{:S(2)}) collective-permute-start(bf16[32,16,128]{2,1,0:T(8,128)(2,1)S(1)} %get-tuple-element.53), channel_id=1, source_target_pairs={{0,4},{1,5},{4,8},{5,9},{8,12},{9,13},{12,14},{13,15},{14,10},{15,... | collective-permute-start | bytes 393224 | tf_op jit(solution)/shard_map/ppermute | solution.py:483
  41.0 7.8 %collective-permute-start.23 = (bf16[32,16,128]{2,1,0:T(8,128)(2,1)S(1)}, bf16[32,16,128]{2,1,0:T(8,128)(2,1)S(1)}, u32[]{:S(2)}, u32[]{:S(2)}) collective-permute-start(bf16[32,16,128]{2,1,0:T(8,128)(2,1)S(1)} %get-tuple-element.51), channel_id=1, source_target_pairs={{0,2},{1,3},{4,0},{5,1},{8,4},{9,5},{12,8},{13,9},{14,12},{15,13},... | collective-permute-start | bytes 393224 | tf_op jit(solution)/shard_map/ppermute | solution.py:483
  42.5 7.1 %collective-permute-start.30 = (bf16[32,16,128]{2,1,0:T(8,128)(2,1)S(1)}, bf16[32,16,128]{2,1,0:T(8,128)(2,1)S(1)}, u32[]{:S(2)}, u32[]{:S(2)}) collective-permute-start(bf16[32,16,128]{2,1,0:T(8,128)(2,1)S(1)} %scatter_add.17), channel_id=1, source_target_pairs={{0,2},{1,3},{4,0},{5,1},{8,4},{9,5},{12,8},{13,9},{14,12},{15,13},... | collective-permute-start | bytes 393224 | tf_op jit(solution)/shard_map/ppermute | solution.py:483
  44.7 6.6 %collective-permute-start.20 = (bf16[32,16,128]{2,1,0:T(8,128)(2,1)S(1)}, bf16[32,16,128]{2,1,0:T(8,128)(2,1)S(1)}, u32[]{:S(2)}, u32[]{:S(2)}) collective-permute-start(bf16[32,16,128]{2,1,0:T(8,128)(2,1)S(1)} %scatter_add.10), channel_id=1, source_target_pairs={{0,4},{1,5},{4,8},{5,9},{8,12},{9,13},{12,14},{13,15},{14,10},{15,... | collective-permute-start | bytes 393224 | tf_op jit(solution)/shard_map/ppermute | solution.py:483
  47.5 6.1 %collective-permute-start.27 = (bf16[32,16,128]{2,1,0:T(8,128)(2,1)S(1)}, bf16[32,16,128]{2,1,0:T(8,128)(2,1)S(1)}, u32[]{:S(2)}, u32[]{:S(2)}) collective-permute-start(bf16[32,16,128]{2,1,0:T(8,128)(2,1)S(1)} %scatter_add.15), channel_id=1, source_target_pairs={{0,4},{1,5},{4,8},{5,9},{8,12},{9,13},{12,14},{13,15},{14,10},{15,... | collective-permute-start | bytes 393224 | tf_op jit(solution)/shard_map/ppermute | solution.py:483
  48.8 6.5 %collective-permute-start.24 = (bf16[32,16,128]{2,1,0:T(8,128)(2,1)S(1)}, bf16[32,16,128]{2,1,0:T(8,128)(2,1)S(1)}, u32[]{:S(2)}, u32[]{:S(2)}) collective-permute-start(bf16[32,16,128]{2,1,0:T(8,128)(2,1)S(1)} %scatter_add.13), channel_id=1, source_target_pairs={{0,2},{1,3},{4,0},{5,1},{8,4},{9,5},{12,8},{13,9},{14,12},{15,13},... | collective-permute-start | bytes 393224 | tf_op jit(solution)/shard_map/ppermute | solution.py:483
  49.7 6.1 %collective-permute-start.31 = (bf16[32,16,128]{2,1,0:T(8,128)(2,1)S(1)}, bf16[32,16,128]{2,1,0:T(8,128)(2,1)S(1)}, u32[]{:S(2)}, u32[]{:S(2)}) collective-permute-start(bf16[32,16,128]{2,1,0:T(8,128)(2,1)S(1)} %scatter_add.18), channel_id=1, source_target_pairs={{0,2},{1,3},{4,0},{5,1},{8,4},{9,5},{12,8},{13,9},{14,12},{15,13},... | collective-permute-start | bytes 393224 | tf_op jit(solution)/shard_map/ppermute | solution.py:483
  51.3 6.1 %collective-permute-start.21 = (bf16[32,16,128]{2,1,0:T(8,128)(2,1)S(1)}, bf16[32,16,128]{2,1,0:T(8,128)(2,1)S(1)}, u32[]{:S(2)}, u32[]{:S(2)}) collective-permute-start(bf16[32,16,128]{2,1,0:T(8,128)(2,1)S(1)} %scatter_add.11), channel_id=1, source_target_pairs={{0,4},{1,5},{4,8},{5,9},{8,12},{9,13},{12,14},{13,15},{14,10},{15,... | collective-permute-start | bytes 393224 | tf_op jit(solution)/shard_map/ppermute | solution.py:483
  53.6 6.0 %collective-permute-start.28 = (bf16[32,16,128]{2,1,0:T(8,128)(2,1)S(1)}, bf16[32,16,128]{2,1,0:T(8,128)(2,1)S(1)}, u32[]{:S(2)}, u32[]{:S(2)}) collective-permute-start(bf16[32,16,128]{2,1,0:T(8,128)(2,1)S(1)} %scatter_add.16), channel_id=1, source_target_pairs={{0,4},{1,5},{4,8},{5,9},{8,12},{9,13},{12,14},{13,15},{14,10},{15,... | collective-permute-start | bytes 393224 | tf_op jit(solution)/shard_map/ppermute | solution.py:483
  55.3 5.0 %collective-permute-start.25 = (bf16[32,16,128]{2,1,0:T(8,128)(2,1)S(1)}, bf16[32,16,128]{2,1,0:T(8,128)(2,1)S(1)}, u32[]{:S(2)}, u32[]{:S(2)}) collective-permute-start(bf16[32,16,128]{2,1,0:T(8,128)(2,1)S(1)} %scatter_add.14), channel_id=1, source_target_pairs={{0,2},{1,3},{4,0},{5,1},{8,4},{9,5},{12,8},{13,9},{14,12},{15,13},... | collective-permute-start | bytes 393224 | tf_op jit(solution)/shard_map/ppermute | solution.py:483
  55.8 5.9 %collective-permute-start.32 = (bf16[32,16,128]{2,1,0:T(8,128)(2,1)S(1)}, bf16[32,16,128]{2,1,0:T(8,128)(2,1)S(1)}, u32[]{:S(2)}, u32[]{:S(2)}) collective-permute-start(bf16[32,16,128]{2,1,0:T(8,128)(2,1)S(1)} %scatter_add.19), channel_id=1, source_target_pairs={{0,2},{1,3},{4,0},{5,1},{8,4},{9,5},{12,8},{13,9},{14,12},{15,13},... | collective-permute-start | bytes 393224 | tf_op jit(solution)/shard_map/ppermute | solution.py:483
  57.5 5.0 %collective-permute-start.22 = (bf16[32,16,128]{2,1,0:T(8,128)(2,1)S(1)}, bf16[32,16,128]{2,1,0:T(8,128)(2,1)S(1)}, u32[]{:S(2)}, u32[]{:S(2)}) collective-permute-start(bf16[32,16,128]{2,1,0:T(8,128)(2,1)S(1)} %scatter_add.12), channel_id=1, source_target_pairs={{0,4},{1,5},{4,8},{5,9},{8,12},{9,13},{12,14},{13,15},{14,10},{15,... | collective-permute-start | bytes 393224 | tf_op jit(solution)/shard_map/ppermute | solution.py:483
  62.6 1.4 %collective-permute-start.33 = (bf16[64,8,128]{2,1,0:T(8,128)(2,1)S(1)}, bf16[64,8,128]{2,1,0:T(8,128)(2,1)S(1)}, u32[]{:S(2)}, u32[]{:S(2)}) collective-permute-start(bf16[64,8,128]{2,1,0:T(8,128)(2,1)S(1)} %get-tuple-element.56), channel_id=1, source_target_pairs={{0,1},{1,0},{2,3},{3,2},{4,5},{5,4},{6,7},{7,6},{8,9},{9,8},{10,11... | collective-permute-start | bytes 393224 | tf_op jit(solution)/shard_map/ppermute | solution.py:576

commit v25 on v24

--- a/solution.py
+++ b/solution.py
@@ -152,11 +152,11 @@
         copy.wait()
 
 
-def right_kernel(core_ref, pair_hbm, mask_hbm, gain_hbm, bias_hbm, proj_hbm, *refs):
-    own_ref, other_ref, pair_t_ref, normed_t_ref, mask_ref, columns_ref = refs[:6]
-    pair_ref, gain_ref, bias_ref, proj_ref, panels, sems = refs[6:]
-    held = (pair_ref, mask_ref, gain_ref, bias_ref, proj_ref)
-    fetch(zip((pair_hbm, mask_hbm, gain_hbm, bias_hbm, proj_hbm), held), sems)
+def right_kernel(core_ref, pair_hbm, mask_hbm, gain_hbm, bias_hbm, proj_hbm, gatew_hbm, outw_hbm, *refs):
+    own_ref, other_ref, pair_t_ref, normed_t_ref, mask_ref, columns_ref, proj_ref, gatew_ref, outw_ref = refs[:9]
+    pair_ref, gain_ref, bias_ref, panels, sems = refs[9:]
+    held = (pair_ref, mask_ref, gain_ref, bias_ref, proj_ref, gatew_ref, outw_ref)
+    fetch(zip((pair_hbm, mask_hbm, gain_hbm, bias_hbm, proj_hbm, gatew_hbm, outw_hbm), held), sems)
     rows, tokens, channels = pair_ref.shape
     small = jnp.concatenate([ref[which] for ref in (gain_ref, bias_ref) for which in range(2)], axis=0).T
     for n in range(4):
@@ -174,9 +174,8 @@
     split_side(panels, core_ref, own_ref, other_ref)
 
 
-def left_kernel(core_ref, normed_t_ref, mask_ref, proj_hbm, gatew_hbm, outw_hbm, *refs):
-    own_ref, other_ref, gate_t_ref, proj_t_ref, outw_t_ref, proj_ref, gatew_ref, outw_ref, panels, sems = refs
-    fetch(zip((proj_hbm, gatew_hbm, outw_hbm), (proj_ref, gatew_ref, outw_ref)), sems)
+def left_kernel(core_ref, normed_t_ref, mask_ref, proj_ref, gatew_ref, outw_ref, *refs):
+    own_ref, other_ref, gate_t_ref, proj_t_ref, outw_t_ref, panels = refs
     rows, tokens = mask_ref.shape
     channels = normed_t_ref.shape[0]
     weights = side_weights(proj_ref, 0, channels)
@@ -432,24 +431,26 @@
         )
         side_panels = pltpu.VMEM((tokens // LANES, channels * rows, LANES), F32)
 
-        def held(*arrays):
-            return [pltpu.VMEM(a.shape, a.dtype) for a in arrays] + [side_panels, pltpu.SemaphoreType.DMA((len(arrays) + 1,))]
-
-        right, other_right, pair_t, normed_t, mask, columns = pl.pallas_call(
+        def like(array):
+            return shape(array.shape, array.dtype)
+
+        right, other_right, pair_t, normed_t, mask, columns, proj, gatew, outw = pl.pallas_call(
             right_kernel,
-            out_shape=(half_shape, half_shape, flat_shape, flat_shape, shape(mask.shape, mask.dtype), columns_shape),
-            in_specs=[smem] + [hbm] * 5,
-            out_specs=(whole,) * 6,
-            scratch_shapes=held(pair, gains, biases, proj),
+            out_shape=(half_shape, half_shape, flat_shape, flat_shape, like(mask), columns_shape)
+            + (like(proj), like(gatew), like(outw)),
+            in_specs=[smem] + [hbm] * 7,
+            out_specs=(whole,) * 9,
+            scratch_shapes=[pltpu.VMEM(a.shape, a.dtype) for a in (pair, gains, biases)]
+            + [side_panels, pltpu.SemaphoreType.DMA((7,))],
             compiler_params=params,
             name="project_right",
-        )(core, pair, mask, gains, biases, proj)
+        )(core, pair, mask, gains, biases, proj, gatew, outw)
         left, other_left, gate_t, proj_t, outw_t = pl.pallas_call(
             left_kernel,
             out_shape=(half_shape, half_shape, flat_shape, proj_t_shape, shape(outw.shape, BF16)),
-            in_specs=[smem] + [whole] * 2 + [hbm] * 3,
+            in_specs=[smem] + [whole] * 5,
             out_specs=(whole,) * 5,
-            scratch_shapes=held(proj, gatew, outw),
+            scratch_shapes=[side_panels],
             compiler_params=params,
             cost_estimate=pl.CostEstimate(flops=10**9, bytes_accessed=4 * 2**20, transcendentals=0),
             name="project_left",

time: 65.4 us -> 64.4 us (0.985)
  starting transfers between devices: 33.5 us -> 32.4 us
  waiting for transfers between devices: 21.7 us -> 22.8 us
  Pallas kernels: 8.97 us -> 8.01 us
    ppermute x28, waiting for transfers between devices: 18.5 us -> 19.5 us  [along(): return lax.ppermute(array, 'row', pairs)]
    ppermute x28, starting transfers between devices: 32.2 us -> 31.2 us  [along(): return lax.ppermute(array, 'row', pairs)]
    pallas_call x1, Pallas kernels: 1.42 us -> 0.44 us  [on_device(): pl.pallas_call(left_kernel, out_shape=(half_shape, half_shape, flat_shape...]
  transfers between devices with their start and end apart: 34 -> 34, of which waited for: 21 -> 21; matrix products, arithmetic and copies ran while one was open for 1% -> 1% of each run, Pallas kernels for 5% -> 4%
where the time goes in v25:
time: 64.4 us; the launch traced here: 64.3 us
  starting transfers between devices  32.4 us (50%)
  waiting for transfers between devices  22.8 us (35%)
  Pallas kernels  8.01 us (12%)
  other arithmetic  0.73 us (1%)
    ppermute x28, starting transfers between devices, along(): return lax.ppermute(array, 'row', pairs)  31.2 us
    ppermute x28, waiting for transfers between devices, along(): return lax.ppermute(array, 'row', pairs)  19.5 us
    ppermute x2, waiting for transfers between devices, on_device(): lax.ppermute(send, 'row', swap).reshape(half * rows, tokens)  2.58 us
    pallas_call x1, Pallas kernels, on_device(): pl.pallas_call(right_kernel, out_shape=(half_shape, half_shape, flat_shap...  1.7 us
    pallas_call x1, Pallas kernels, on_device(): pl.pallas_call(functools.partial(step_kernel, half if by_core else per_gr...  1.37 us
    pallas_call x2, Pallas kernels, on_device(): pl.pallas_call(functools.partial(scatter_start, piece * size, hops[0], ch...  1.33 us
  transfers between devices with their start and end apart: 34, of which 21 were waited for; matrix products, arithmetic and copies ran while one was open for 1% of the time, Pallas kernels for 4%

profile of v25, /device:TPU:0, one launch (start us, length us, event | category | flops | bytes accessed | tf_op | source)
XLA Modules:
  0.0 64.3 jit_solution(3450882411012591137)
XLA Ops:
  0.0 1.7 %project_right.1 = (bf16[512,128]{1,0:T(8,128)(2,1)S(1)}, bf16[512,128]{1,0:T(8,128)(2,1)S(1)}, bf16[128,1024]{1,0:T(8,128)(2,1)S(1)}, bf16[128,1024]{1,0:T(8,12...) custom-call(s32[1]{0:T(128)} %bitcast.core_ref.refs_0_, ...), custom_call_target="tpu_custom_call" | custom-call | tf_op jit(solution)/shard_map/project_right/pallas_call | solution.py:437
  1.7 3.0 %collective-permute-start.4 = (bf16[512,128]{1,0:T(8,128)(2,1)S(1)}, bf16[512,128]{1,0:T(8,128)(2,1)S(1)}, u32[]{:S(2)}, u32[]{:S(2)}) collective-permute-start(bf16[512,128]{1,0:T(8,128)(2,1)S(1)} %get-tuple-element.42), channel_id=1, source_target_pairs={{0,2},{1,3},{4,0},{5,1},{8,4},{9,5},{12,8},{13,9},{14,12},{15,13},... | collective-permute-start | bytes 393224 | tf_op jit(solution)/shard_map/ppermute | solution.py:484
  4.7 0.1 collective-permute-start.2
  4.8 0.4 project_left.1
  5.3 0.6 collective-permute-start
  6.0 0.2 fusion.1.order_ref
  6.2 0.1 fusion.2.order_ref
  6.3 2.0 %collective-permute-start.5 = (bf16[512,128]{1,0:T(8,128)(2,1)S(1)}, bf16[512,128]{1,0:T(8,128)(2,1)S(1)}, u32[]{:S(2)}, u32[]{:S(2)}) collective-permute-start(bf16[512,128]{1,0:T(8,128)(2,1)S(1)} %collective-permute-done.1), channel_id=1, source_target_pairs={{0,2},{1,3},{4,0},{5,1},{8,4},{9,5},{12,8},{13,9},{14,12},{15,13},... | collective-permute-start | bytes 393224 | tf_op jit(solution)/shard_map/ppermute | solution.py:484
  8.3 0.2 collective-permute-start.3
  8.5 1.2 %collective-permute-done.2 = bf16[512,128]{1,0:T(8,128)(2,1)S(1)} collective-permute-done((bf16[512,128]{1,0:T(8,128)(2,1)S(1)}, bf16[512,128]{1,0:T(8,128)(2,1)S(1)}, u32[]{:S(2)}, u32[]{:S(2)}) %collective-permute-start.2) | collective-permute-done | bytes 131104 | tf_op jit(solution)/shard_map/ppermute | solution.py:484
  9.7 0.7 %collective-permute-start.6 = (bf16[512,128]{1,0:T(8,128)(2,1)S(1)}, bf16[512,128]{1,0:T(8,128)(2,1)S(1)}, u32[]{:S(2)}, u32[]{:S(2)}) collective-permute-start(bf16[512,128]{1,0:T(8,128)(2,1)S(1)} %collective-permute-done.2), channel_id=1, source_target_pairs={{0,4},{1,5},{4,8},{5,9},{8,12},{9,13},{12,14},{13,15},{14,10},{15,... | collective-permute-start | bytes 393224 | tf_op jit(solution)/shard_map/ppermute | solution.py:484
  10.4 1.7 %collective-permute-done.5 = bf16[512,128]{1,0:T(8,128)(2,1)S(1)} collective-permute-done((bf16[512,128]{1,0:T(8,128)(2,1)S(1)}, bf16[512,128]{1,0:T(8,128)(2,1)S(1)}, u32[]{:S(2)}, u32[]{:S(2)}) %collective-permute-start.5) | collective-permute-done | bytes 131104 | tf_op jit(solution)/shard_map/ppermute | solution.py:484
  12.2 1.7 %collective-permute-start.9 = (bf16[512,128]{1,0:T(8,128)(2,1)S(1)}, bf16[512,128]{1,0:T(8,128)(2,1)S(1)}, u32[]{:S(2)}, u32[]{:S(2)}) collective-permute-start(bf16[512,128]{1,0:T(8,128)(2,1)S(1)} %collective-permute-done.5), channel_id=1, source_target_pairs={{0,2},{1,3},{4,0},{5,1},{8,4},{9,5},{12,8},{13,9},{14,12},{15,13},... | collective-permute-start | bytes 393224 | tf_op jit(solution)/shard_map/ppermute | solution.py:484
  13.9 1.6 %collective-permute-start.8 = (bf16[512,128]{1,0:T(8,128)(2,1)S(1)}, bf16[512,128]{1,0:T(8,128)(2,1)S(1)}, u32[]{:S(2)}, u32[]{:S(2)}) collective-permute-start(bf16[512,128]{1,0:T(8,128)(2,1)S(1)} %collective-permute-done.4), channel_id=1, source_target_pairs={{0,2},{1,3},{4,0},{5,1},{8,4},{9,5},{12,8},{13,9},{14,12},{15,13},... | collective-permute-start | bytes 393224 | tf_op jit(solution)/shard_map/ppermute | solution.py:484
  15.5 0.4 collective-permute-start.7
  16.0 0.5 collective-permute-done.6
  16.5 0.4 collective-permute-start.10
  16.8 1.8 %collective-permute-done.9 = bf16[512,128]{1,0:T(8,128)(2,1)S(1)} collective-permute-done((bf16[512,128]{1,0:T(8,128)(2,1)S(1)}, bf16[512,128]{1,0:T(8,128)(2,1)S(1)}, u32[]{:S(2)}, u32[]{:S(2)}) %collective-permute-start.9) | collective-permute-done | bytes 131104 | tf_op jit(solution)/shard_map/ppermute | solution.py:484
  18.6 1.5 %collective-permute-start.13 = (bf16[512,128]{1,0:T(8,128)(2,1)S(1)}, bf16[512,128]{1,0:T(8,128)(2,1)S(1)}, u32[]{:S(2)}, u32[]{:S(2)}) collective-permute-start(bf16[512,128]{1,0:T(8,128)(2,1)S(1)} %collective-permute-done.9), channel_id=1, source_target_pairs={{0,2},{1,3},{4,0},{5,1},{8,4},{9,5},{12,8},{13,9},{14,12},{15,13},... | collective-permute-start | bytes 393224 | tf_op jit(solution)/shard_map/ppermute | solution.py:484
  20.1 1.3 %collective-permute-done.8 = bf16[512,128]{1,0:T(8,128)(2,1)S(1)} collective-permute-done((bf16[512,128]{1,0:T(8,128)(2,1)S(1)}, bf16[512,128]{1,0:T(8,128)(2,1)S(1)}, u32[]{:S(2)}, u32[]{:S(2)}) %collective-permute-start.8) | collective-permute-done | bytes 131104 | tf_op jit(solution)/shard_map/ppermute | solution.py:484
  21.4 1.5 %collective-permute-start.12 = (bf16[512,128]{1,0:T(8,128)(2,1)S(1)}, bf16[512,128]{1,0:T(8,128)(2,1)S(1)}, u32[]{:S(2)}, u32[]{:S(2)}) collective-permute-start(bf16[512,128]{1,0:T(8,128)(2,1)S(1)} %collective-permute-done.8), channel_id=1, source_target_pairs={{0,2},{1,3},{4,0},{5,1},{8,4},{9,5},{12,8},{13,9},{14,12},{15,13},... | collective-permute-start | bytes 393224 | tf_op jit(solution)/shard_map/ppermute | solution.py:484
  22.9 0.6 collective-permute-start.11
  23.5 1.6 %collective-permute-start.14 = (bf16[512,128]{1,0:T(8,128)(2,1)S(1)}, bf16[512,128]{1,0:T(8,128)(2,1)S(1)}, u32[]{:S(2)}, u32[]{:S(2)}) collective-permute-start(bf16[512,128]{1,0:T(8,128)(2,1)S(1)} %collective-permute-done.10), channel_id=1, source_target_pairs={{0,4},{1,5},{4,8},{5,9},{8,12},{9,13},{12,14},{13,15},{14,10},{15,... | collective-permute-start | bytes 393224 | tf_op jit(solution)/shard_map/ppermute | solution.py:484
  25.1 0.7 %collective-permute-start.15 = (bf16[512,128]{1,0:T(8,128)(2,1)S(1)}, bf16[512,128]{1,0:T(8,128)(2,1)S(1)}, u32[]{:S(2)}, u32[]{:S(2)}) collective-permute-start(bf16[512,128]{1,0:T(8,128)(2,1)S(1)} %collective-permute-done.13), channel_id=1, source_target_pairs={{0,2},{1,3},{4,0},{5,1},{8,4},{9,5},{12,8},{13,9},{14,12},{15,13},... | collective-permute-start | bytes 393224 | tf_op jit(solution)/shard_map/ppermute | solution.py:484
  25.7 0.9 %mix_early.1.early_ref = bf16[64,16,128]{2,1,0:T(8,128)(2,1)S(1)} custom-call(bf16[80,128]{1,0:T(8,128)(2,1)S(1)} %fusion.1.order_ref, bf16[64,8,128]{2,1,0:T(8,128)(2,1)S(1)} %bitcast.35, bf16[64,8,128]{2,1,0:T(8,128)(2,1)S(1)} %bitcast.37, bf16[64,8,128]{2,1,0:T(8,128)(2,1)S(1)} %bitcast.49, bf16[64,8,128]{2,1,0:T(8,128)(2,1)S(1)} %bitcast.52, ...), custom_call_target="tpu_custom_call" | custom-call | flops 1000000000 | bytes 4194304 | tf_op jit(solution)/shard_map/mix_early/pallas_call | solution.py:505
  26.7 0.4 collective-permute-done.12
  27.0 0.8 %collective-permute-done.11 = bf16[512,128]{1,0:T(8,128)(2,1)S(1)} collective-permute-done((bf16[512,128]{1,0:T(8,128)(2,1)S(1)}, bf16[512,128]{1,0:T(8,128)(2,1)S(1)}, u32[]{:S(2)}, u32[]{:S(2)}) %collective-permute-start.11) | collective-permute-done | bytes 131104 | tf_op jit(solution)/shard_map/ppermute | solution.py:484
  27.9 1.4 %collective-permute-done.14 = bf16[512,128]{1,0:T(8,128)(2,1)S(1)} collective-permute-done((bf16[512,128]{1,0:T(8,128)(2,1)S(1)}, bf16[512,128]{1,0:T(8,128)(2,1)S(1)}, u32[]{:S(2)}, u32[]{:S(2)}) %collective-permute-start.14) | collective-permute-done | bytes 131104 | tf_op jit(solution)/shard_map/ppermute | solution.py:484
  29.3 0.8 %collective-permute-done.15 = bf16[512,128]{1,0:T(8,128)(2,1)S(1)} collective-permute-done((bf16[512,128]{1,0:T(8,128)(2,1)S(1)}, bf16[512,128]{1,0:T(8,128)(2,1)S(1)}, u32[]{:S(2)}, u32[]{:S(2)}) %collective-permute-start.15) | collective-permute-done | bytes 131104 | tf_op jit(solution)/shard_map/ppermute | solution.py:484
  30.0 0.7 %mix_late.1 = (bf16[64,8,128]{2,1,0:T(8,128)(2,1)S(1)}, bf16[64,8,128]{2,1,0:T(8,128)(2,1)S(1)}) custom-call(bf16[48,128]{1,0:T(8,128)(2,1)S(1)} %fusion.2.order_ref, bf16[64,8,128]{2,1,0:T(8,128)(2,1)S(1)} %bitcast.36, bf16[64,8,128]{2,1,0:T(8,128)(2,1)S(1)} %bitcast.38, bf16[64,16,128]{2,1,0:T(8,128)(2,1)S(1)} %mix_early.1.early_ref, ...), custom_call_target="tpu_custom_call" | custom-call | tf_op jit(solution)/shard_map/mix_late/pallas_call | solution.py:515
  30.8 1.2 %collective-permute-done.16 = bf16[64,8,128]{2,1,0:T(8,128)(2,1)S(1)} collective-permute-done((bf16[64,8,128]{2,1,0:T(8,128)(2,1)S(1)}, bf16[64,8,128]{2,1,0:T(8,128)(2,1)S(1)}, u32[]{:S(2)}, u32[]{:S(2)}) %collective-permute-start.16) | collective-permute-done | bytes 131104 | tf_op jit(solution)/shard_map/ppermute | solution.py:524
  32.1 1.4 %finish_project.1 = (bf16[512,128]{1,0:T(8,128)(2,1)S(1)}, bf16[512,128]{1,0:T(8,128)(2,1)S(1)}, bf16[512,128]{1,0:T(8,128)(2,1)S(1)}, bf16[512,128]{1,0:T(8,128...) custom-call(s32[1]{0:T(128)} %bitcast.core_ref.refs_0_, bf16[512,128]{1,0:T(8,128)(2,1)S(1)} %bitcast.39, ...), custom_call_target="tpu_custom_call" | custom-call | tf_op jit(solution)/shard_map/finish_project/pallas_call | solution.py:527
  33.5 0.2 collective-permute-start.17
  33.7 0.4 collective-permute-start.18
  34.0 0.3 fusion.order_ref
  34.4 0.5 collective-permute-done.17
  34.9 0.2 collective-permute-done.18
  35.1 0.7 %scatter_start.3 = (f32[32,128,128]{2,1,0:T(8,128)S(1)}, bf16[32,16,128]{2,1,0:T(8,128)(2,1)S(1)}, bf16[32,16,128]{2,1,0:T(8,128)(2,1)S(1)}) custom-call(bf16[128,128]{1,0:T(8,128)(2,1)S(1)} %fusion.order_ref, bf16[64,8,128]{2,1,0:T(8,128)(2,1)S(1)} %bitcast.27, bf16[64,8,128]{2,1,0:T(8,128)(2,1)S(1)} %bitcast.31, bf16[64,8,128]{2,1,0:T(8,128)(2,1)S(1)} %bitcast.29, ...), custom_call_target="tpu_custom_call" | custom-call | tf_op jit(solution)/shard_map/scatter_start/pallas_call | solution.py:548
  35.7 0.9 %collective-permute-start.29 = (bf16[32,16,128]{2,1,0:T(8,128)(2,1)S(1)}, bf16[32,16,128]{2,1,0:T(8,128)(2,1)S(1)}, u32[]{:S(2)}, u32[]{:S(2)}) collective-permute-start(bf16[32,16,128]{2,1,0:T(8,128)(2,1)S(1)} %get-tuple-element.60), channel_id=1, source_target_pairs={{0,2},{1,3},{4,0},{5,1},{8,4},{9,5},{12,8},{13,9},{14,12},{15,13},... | collective-permute-start | bytes 393224 | tf_op jit(solution)/shard_map/ppermute | solution.py:484
  36.6 0.7 %scatter_start.2 = (f32[32,128,128]{2,1,0:T(8,128)S(1)}, bf16[32,16,128]{2,1,0:T(8,128)(2,1)S(1)}, bf16[32,16,128]{2,1,0:T(8,128)(2,1)S(1)}) custom-call(bf16[128,128]{1,0:T(8,128)(2,1)S(1)} %fusion.order_ref, bf16[64,8,128]{2,1,0:T(8,128)(2,1)S(1)} %bitcast.28, bf16[64,8,128]{2,1,0:T(8,128)(2,1)S(1)} %bitcast.32, bf16[64,8,128]{2,1,0:T(8,128)(2,1)S(1)} %bitcast.30, ...), custom_call_target="tpu_custom_call" | custom-call | tf_op jit(solution)/shard_map/scatter_start/pallas_call | solution.py:548
  37.3 1.3 %collective-permute-start.19 = (bf16[32,16,128]{2,1,0:T(8,128)(2,1)S(1)}, bf16[32,16,128]{2,1,0:T(8,128)(2,1)S(1)}, u32[]{:S(2)}, u32[]{:S(2)}) collective-permute-start(bf16[32,16,128]{2,1,0:T(8,128)(2,1)S(1)} %get-tuple-element.56), channel_id=1, source_target_pairs={{0,4},{1,5},{4,8},{5,9},{8,12},{9,13},{12,14},{13,15},{14,10},{15,... | collective-permute-start | bytes 393224 | tf_op jit(solution)/shard_map/ppermute | solution.py:484
  38.5 1.5 %collective-permute-start.26 = (bf16[32,16,128]{2,1,0:T(8,128)(2,1)S(1)}, bf16[32,16,128]{2,1,0:T(8,128)(2,1)S(1)}, u32[]{:S(2)}, u32[]{:S(2)}) collective-permute-start(bf16[32,16,128]{2,1,0:T(8,128)(2,1)S(1)} %get-tuple-element.59), channel_id=1, source_target_pairs={{0,4},{1,5},{4,8},{5,9},{8,12},{9,13},{12,14},{13,15},{14,10},{15,... | collective-permute-start | bytes 393224 | tf_op jit(solution)/shard_map/ppermute | solution.py:484
  40.0 0.5 collective-permute-start.23
  40.6 1.0 %collective-permute-done.29.got_ref = bf16[32,16,128]{2,1,0:T(8,128)(2,1)S(1)} collective-permute-done((bf16[32,16,128]{2,1,0:T(8,128)(2,1)S(1)}, bf16[32,16,128]{2,1,0:T(8,128)(2,1)S(1)}, u32[]{:S(2)}, u32[]{:S(2)}) %collective-permute-start.29) | collective-permute-done | bytes 131104 | tf_op jit(solution)/shard_map/ppermute | solution.py:484
  41.5 0.9 %collective-permute-start.30 = (bf16[32,16,128]{2,1,0:T(8,128)(2,1)S(1)}, bf16[32,16,128]{2,1,0:T(8,128)(2,1)S(1)}, u32[]{:S(2)}, u32[]{:S(2)}) collective-permute-start(bf16[32,16,128]{2,1,0:T(8,128)(2,1)S(1)} %scatter_add.17), channel_id=1, source_target_pairs={{0,2},{1,3},{4,0},{5,1},{8,4},{9,5},{12,8},{13,9},{14,12},{15,13},... | collective-permute-start | bytes 393224 | tf_op jit(solution)/shard_map/ppermute | solution.py:484
  42.4 1.3 %collective-permute-done.19.got_ref = bf16[32,16,128]{2,1,0:T(8,128)(2,1)S(1)} collective-permute-done((bf16[32,16,128]{2,1,0:T(8,128)(2,1)S(1)}, bf16[32,16,128]{2,1,0:T(8,128)(2,1)S(1)}, u32[]{:S(2)}, u32[]{:S(2)}) %collective-permute-start.19) | collective-permute-done | bytes 131104 | tf_op jit(solution)/shard_map/ppermute | solution.py:484
  43.7 1.3 %collective-permute-start.20 = (bf16[32,16,128]{2,1,0:T(8,128)(2,1)S(1)}, bf16[32,16,128]{2,1,0:T(8,128)(2,1)S(1)}, u32[]{:S(2)}, u32[]{:S(2)}) collective-permute-start(bf16[32,16,128]{2,1,0:T(8,128)(2,1)S(1)} %scatter_add.10), channel_id=1, source_target_pairs={{0,4},{1,5},{4,8},{5,9},{8,12},{9,13},{12,14},{13,15},{14,10},{15,... | collective-permute-start | bytes 393224 | tf_op jit(solution)/shard_map/ppermute | solution.py:484
  45.0 1.5 %collective-permute-done.26.got_ref = bf16[32,16,128]{2,1,0:T(8,128)(2,1)S(1)} collective-permute-done((bf16[32,16,128]{2,1,0:T(8,128)(2,1)S(1)}, bf16[32,16,128]{2,1,0:T(8,128)(2,1)S(1)}, u32[]{:S(2)}, u32[]{:S(2)}) %collective-permute-start.26) | collective-permute-done | bytes 131104 | tf_op jit(solution)/shard_map/ppermute | solution.py:484
  46.5 1.3 %collective-permute-start.27 = (bf16[32,16,128]{2,1,0:T(8,128)(2,1)S(1)}, bf16[32,16,128]{2,1,0:T(8,128)(2,1)S(1)}, u32[]{:S(2)}, u32[]{:S(2)}) collective-permute-start(bf16[32,16,128]{2,1,0:T(8,128)(2,1)S(1)} %scatter_add.15), channel_id=1, source_target_pairs={{0,4},{1,5},{4,8},{5,9},{8,12},{9,13},{12,14},{13,15},{14,10},{15,... | collective-permute-start | bytes 393224 | tf_op jit(solution)/shard_map/ppermute | solution.py:484
  47.8 0.9 %collective-permute-start.24 = (bf16[32,16,128]{2,1,0:T(8,128)(2,1)S(1)}, bf16[32,16,128]{2,1,0:T(8,128)(2,1)S(1)}, u32[]{:S(2)}, u32[]{:S(2)}) collective-permute-start(bf16[32,16,128]{2,1,0:T(8,128)(2,1)S(1)} %scatter_add.13), channel_id=1, source_target_pairs={{0,2},{1,3},{4,0},{5,1},{8,4},{9,5},{12,8},{13,9},{14,12},{15,13},... | collective-permute-start | bytes 393224 | tf_op jit(solution)/shard_map/ppermute | solution.py:484
  48.7 1.6 %collective-permute-start.31 = (bf16[32,16,128]{2,1,0:T(8,128)(2,1)S(1)}, bf16[32,16,128]{2,1,0:T(8,128)(2,1)S(1)}, u32[]{:S(2)}, u32[]{:S(2)}) collective-permute-start(bf16[32,16,128]{2,1,0:T(8,128)(2,1)S(1)} %scatter_add.18), channel_id=1, source_target_pairs={{0,2},{1,3},{4,0},{5,1},{8,4},{9,5},{12,8},{13,9},{14,12},{15,13},... | collective-permute-start | bytes 393224 | tf_op jit(solution)/shard_map/ppermute | solution.py:484
  50.4 0.9 %collective-permute-start.21 = (bf16[32,16,128]{2,1,0:T(8,128)(2,1)S(1)}, bf16[32,16,128]{2,1,0:T(8,128)(2,1)S(1)}, u32[]{:S(2)}, u32[]{:S(2)}) collective-permute-start(bf16[32,16,128]{2,1,0:T(8,128)(2,1)S(1)} %scatter_add.11), channel_id=1, source_target_pairs={{0,4},{1,5},{4,8},{5,9},{8,12},{9,13},{12,14},{13,15},{14,10},{15,... | collective-permute-start | bytes 393224 | tf_op jit(solution)/shard_map/ppermute | solution.py:484
  51.3 1.3 %collective-permute-done.27.got_ref = bf16[32,16,128]{2,1,0:T(8,128)(2,1)S(1)} collective-permute-done((bf16[32,16,128]{2,1,0:T(8,128)(2,1)S(1)}, bf16[32,16,128]{2,1,0:T(8,128)(2,1)S(1)}, u32[]{:S(2)}, u32[]{:S(2)}) %collective-permute-start.27) | collective-permute-done | bytes 131104 | tf_op jit(solution)/shard_map/ppermute | solution.py:484
  52.7 1.6 %collective-permute-start.28 = (bf16[32,16,128]{2,1,0:T(8,128)(2,1)S(1)}, bf16[32,16,128]{2,1,0:T(8,128)(2,1)S(1)}, u32[]{:S(2)}, u32[]{:S(2)}) collective-permute-start(bf16[32,16,128]{2,1,0:T(8,128)(2,1)S(1)} %scatter_add.16), channel_id=1, source_target_pairs={{0,4},{1,5},{4,8},{5,9},{8,12},{9,13},{12,14},{13,15},{14,10},{15,... | collective-permute-start | bytes 393224 | tf_op jit(solution)/shard_map/ppermute | solution.py:484
  54.3 0.5 collective-permute-start.25
  54.9 1.6 %collective-permute-start.32 = (bf16[32,16,128]{2,1,0:T(8,128)(2,1)S(1)}, bf16[32,16,128]{2,1,0:T(8,128)(2,1)S(1)}, u32[]{:S(2)}, u32[]{:S(2)}) collective-permute-start(bf16[32,16,128]{2,1,0:T(8,128)(2,1)S(1)} %scatter_add.19), channel_id=1, source_target_pairs={{0,2},{1,3},{4,0},{5,1},{8,4},{9,5},{12,8},{13,9},{14,12},{15,13},... | collective-permute-start | bytes 393224 | tf_op jit(solution)/shard_map/ppermute | solution.py:484
  56.5 0.6 collective-permute-start.22
  57.1 1.6 %collective-permute-done.28.refs_4_ = bf16[32,16,128]{2,1,0:T(8,128)(2,1)S(1)} collective-permute-done((bf16[32,16,128]{2,1,0:T(8,128)(2,1)S(1)}, bf16[32,16,128]{2,1,0:T(8,128)(2,1)S(1)}, u32[]{:S(2)}, u32[]{:S(2)}) %collective-permute-start.28) | collective-permute-done | bytes 131104 | tf_op jit(solution)/shard_map/ppermute | solution.py:484
  58.6 0.7 %collective-permute-done.25.refs_2_ = bf16[32,16,128]{2,1,0:T(8,128)(2,1)S(1)} collective-permute-done((bf16[32,16,128]{2,1,0:T(8,128)(2,1)S(1)}, bf16[32,16,128]{2,1,0:T(8,128)(2,1)S(1)}, u32[]{:S(2)}, u32[]{:S(2)}) %collective-permute-start.25) | collective-permute-done | bytes 131104 | tf_op jit(solution)/shard_map/ppermute | solution.py:484
  59.3 1.4 %collective-permute-done.32.refs_5_ = bf16[32,16,128]{2,1,0:T(8,128)(2,1)S(1)} collective-permute-done((bf16[32,16,128]{2,1,0:T(8,128)(2,1)S(1)}, bf16[32,16,128]{2,1,0:T(8,128)(2,1)S(1)}, u32[]{:S(2)}, u32[]{:S(2)}) %collective-permute-start.32) | collective-permute-done | bytes 131104 | tf_op jit(solution)/shard_map/ppermute | solution.py:484
  60.8 0.8 %collective-permute-done.22.refs_1_ = bf16[32,16,128]{2,1,0:T(8,128)(2,1)S(1)} collective-permute-done((bf16[32,16,128]{2,1,0:T(8,128)(2,1)S(1)}, bf16[32,16,128]{2,1,0:T(8,128)(2,1)S(1)}, u32[]{:S(2)}, u32[]{:S(2)}) %collective-permute-start.22) | collective-permute-done | bytes 131104 | tf_op jit(solution)/shard_map/ppermute | solution.py:484
  61.5 0.1 scatter_end.1
  61.7 1.3 %collective-permute-done.33 = bf16[64,8,128]{2,1,0:T(8,128)(2,1)S(1)} collective-permute-done((bf16[64,8,128]{2,1,0:T(8,128)(2,1)S(1)}, bf16[64,8,128]{2,1,0:T(8,128)(2,1)S(1)}, u32[]{:S(2)}, u32[]{:S(2)}) %collective-permute-start.33) | collective-permute-done | bytes 131104 | tf_op jit(solution)/shard_map/ppermute | solution.py:577
  63.0 1.3 %finish.1 = bf16[8,128,128]{2,1,0:T(8,128)(2,1)} custom-call(s32[1]{0:T(128)} %bitcast.core_ref.refs_0_, bf16[512,128]{1,0:T(8,128)(2,1)S(1)} %bitcast.47, bf16[512,128]{1,0:T(8,128)(2,1)S(1)} %bitcast.48, bf16[128,1024]{1,0:T(8,128)(2,1)S(1)} %get-tuple-element.63.refs_3_, bf16[128,1024]{1,0:T(8,128)(2,1)S(1)} %get-tuple-element.64.refs_4_, ...), custom_call_target="tpu_custom_call" | custom-call | tf_op jit(solution)/shard_map/finish/pallas_call | solution.py:580
  (45 shorter events, 0.5 us)
Async XLA Ops:
  1.7 12.2 %collective-permute-start.4 = (bf16[512,128]{1,0:T(8,128)(2,1)S(1)}, bf16[512,128]{1,0:T(8,128)(2,1)S(1)}, u32[]{:S(2)}, u32[]{:S(2)}) collective-permute-start(bf16[512,128]{1,0:T(8,128)(2,1)S(1)} %get-tuple-element.42), channel_id=1, source_target_pairs={{0,2},{1,3},{4,0},{5,1},{8,4},{9,5},{12,8},{13,9},{14,12},{15,13},... | collective-permute-start | bytes 393224 | tf_op jit(solution)/shard_map/ppermute | solution.py:484
  4.7 5.0 %collective-permute-start.2 = (bf16[512,128]{1,0:T(8,128)(2,1)S(1)}, bf16[512,128]{1,0:T(8,128)(2,1)S(1)}, u32[]{:S(2)}, u32[]{:S(2)}) collective-permute-start(bf16[512,128]{1,0:T(8,128)(2,1)S(1)} %get-tuple-element.42), channel_id=1, source_target_pairs={{0,4},{1,5},{4,8},{5,9},{8,12},{9,13},{12,14},{13,15},{14,10},{15,... | collective-permute-start | bytes 393224 | tf_op jit(solution)/shard_map/ppermute | solution.py:484
  4.8 1.5 %collective-permute-start.1 = (bf16[512,128]{1,0:T(8,128)(2,1)S(1)}, bf16[512,128]{1,0:T(8,128)(2,1)S(1)}, u32[]{:S(2)}, u32[]{:S(2)}) collective-permute-start(bf16[512,128]{1,0:T(8,128)(2,1)S(1)} %get-tuple-element.43), channel_id=1, source_target_pairs={{0,1},{1,0},{2,3},{3,2},{4,5},{5,4},{6,7},{7,6},{8,9},{9,8},{10,11... | collective-permute-start | bytes 393224 | tf_op jit(solution)/shard_map/ppermute | solution.py:493
  5.3 20.4 %collective-permute-start = (bf16[512,128]{1,0:T(8,128)(2,1)S(1)}, bf16[512,128]{1,0:T(8,128)(2,1)S(1)}, u32[]{:S(2)}, u32[]{:S(2)}) collective-permute-start(bf16[512,128]{1,0:T(8,128)(2,1)S(1)} %get-tuple-element.41), channel_id=1, source_target_pairs={{0,1},{1,0},{2,3},{3,2},{4,5},{5,4},{6,7},{7,6},{8,9},{9,8},{10,11... | collective-permute-start | bytes 393224 | tf_op jit(solution)/shard_map/ppermute | solution.py:494
  6.3 5.9 %collective-permute-start.5 = (bf16[512,128]{1,0:T(8,128)(2,1)S(1)}, bf16[512,128]{1,0:T(8,128)(2,1)S(1)}, u32[]{:S(2)}, u32[]{:S(2)}) collective-permute-start(bf16[512,128]{1,0:T(8,128)(2,1)S(1)} %collective-permute-done.1), channel_id=1, source_target_pairs={{0,2},{1,3},{4,0},{5,1},{8,4},{9,5},{12,8},{13,9},{14,12},{15,13},... | collective-permute-start | bytes 393224 | tf_op jit(solution)/shard_map/ppermute | solution.py:484
  8.3 7.2 %collective-permute-start.3 = (bf16[512,128]{1,0:T(8,128)(2,1)S(1)}, bf16[512,128]{1,0:T(8,128)(2,1)S(1)}, u32[]{:S(2)}, u32[]{:S(2)}) collective-permute-start(bf16[512,128]{1,0:T(8,128)(2,1)S(1)} %collective-permute-done.1), channel_id=1, source_target_pairs={{0,4},{1,5},{4,8},{5,9},{8,12},{9,13},{12,14},{13,15},{14,10},{15,... | collective-permute-start | bytes 393224 | tf_op jit(solution)/shard_map/ppermute | solution.py:484
  9.7 6.8 %collective-permute-start.6 = (bf16[512,128]{1,0:T(8,128)(2,1)S(1)}, bf16[512,128]{1,0:T(8,128)(2,1)S(1)}, u32[]{:S(2)}, u32[]{:S(2)}) collective-permute-start(bf16[512,128]{1,0:T(8,128)(2,1)S(1)} %collective-permute-done.2), channel_id=1, source_target_pairs={{0,4},{1,5},{4,8},{5,9},{8,12},{9,13},{12,14},{13,15},{14,10},{15,... | collective-permute-start | bytes 393224 | tf_op jit(solution)/shard_map/ppermute | solution.py:484
  12.2 6.4 %collective-permute-start.9 = (bf16[512,128]{1,0:T(8,128)(2,1)S(1)}, bf16[512,128]{1,0:T(8,128)(2,1)S(1)}, u32[]{:S(2)}, u32[]{:S(2)}) collective-permute-start(bf16[512,128]{1,0:T(8,128)(2,1)S(1)} %collective-permute-done.5), channel_id=1, source_target_pairs={{0,2},{1,3},{4,0},{5,1},{8,4},{9,5},{12,8},{13,9},{14,12},{15,13},... | collective-permute-start | bytes 393224 | tf_op jit(solution)/shard_map/ppermute | solution.py:484
  13.9 7.5 %collective-permute-start.8 = (bf16[512,128]{1,0:T(8,128)(2,1)S(1)}, bf16[512,128]{1,0:T(8,128)(2,1)S(1)}, u32[]{:S(2)}, u32[]{:S(2)}) collective-permute-start(bf16[512,128]{1,0:T(8,128)(2,1)S(1)} %collective-permute-done.4), channel_id=1, source_target_pairs={{0,2},{1,3},{4,0},{5,1},{8,4},{9,5},{12,8},{13,9},{14,12},{15,13},... | collective-permute-start | bytes 393224 | tf_op jit(solution)/shard_map/ppermute | solution.py:484
  15.5 7.3 %collective-permute-start.7 = (bf16[512,128]{1,0:T(8,128)(2,1)S(1)}, bf16[512,128]{1,0:T(8,128)(2,1)S(1)}, u32[]{:S(2)}, u32[]{:S(2)}) collective-permute-start(bf16[512,128]{1,0:T(8,128)(2,1)S(1)} %collective-permute-done.3), channel_id=1, source_target_pairs={{0,4},{1,5},{4,8},{5,9},{8,12},{9,13},{12,14},{13,15},{14,10},{15,... | collective-permute-start | bytes 393224 | tf_op jit(solution)/shard_map/ppermute | solution.py:484
  16.5 7.0 %collective-permute-start.10 = (bf16[512,128]{1,0:T(8,128)(2,1)S(1)}, bf16[512,128]{1,0:T(8,128)(2,1)S(1)}, u32[]{:S(2)}, u32[]{:S(2)}) collective-permute-start(bf16[512,128]{1,0:T(8,128)(2,1)S(1)} %collective-permute-done.6), channel_id=1, source_target_pairs={{0,4},{1,5},{4,8},{5,9},{8,12},{9,13},{12,14},{13,15},{14,10},{15,... | collective-permute-start | bytes 393224 | tf_op jit(solution)/shard_map/ppermute | solution.py:484
  18.6 6.4 %collective-permute-start.13 = (bf16[512,128]{1,0:T(8,128)(2,1)S(1)}, bf16[512,128]{1,0:T(8,128)(2,1)S(1)}, u32[]{:S(2)}, u32[]{:S(2)}) collective-permute-start(bf16[512,128]{1,0:T(8,128)(2,1)S(1)} %collective-permute-done.9), channel_id=1, source_target_pairs={{0,2},{1,3},{4,0},{5,1},{8,4},{9,5},{12,8},{13,9},{14,12},{15,13},... | collective-permute-start | bytes 393224 | tf_op jit(solution)/shard_map/ppermute | solution.py:484
  21.4 5.6 %collective-permute-start.12 = (bf16[512,128]{1,0:T(8,128)(2,1)S(1)}, bf16[512,128]{1,0:T(8,128)(2,1)S(1)}, u32[]{:S(2)}, u32[]{:S(2)}) collective-permute-start(bf16[512,128]{1,0:T(8,128)(2,1)S(1)} %collective-permute-done.8), channel_id=1, source_target_pairs={{0,2},{1,3},{4,0},{5,1},{8,4},{9,5},{12,8},{13,9},{14,12},{15,13},... | collective-permute-start | bytes 393224 | tf_op jit(solution)/shard_map/ppermute | solution.py:484
  22.9 5.0 %collective-permute-start.11 = (bf16[512,128]{1,0:T(8,128)(2,1)S(1)}, bf16[512,128]{1,0:T(8,128)(2,1)S(1)}, u32[]{:S(2)}, u32[]{:S(2)}) collective-permute-start(bf16[512,128]{1,0:T(8,128)(2,1)S(1)} %collective-permute-done.7), channel_id=1, source_target_pairs={{0,4},{1,5},{4,8},{5,9},{8,12},{9,13},{12,14},{13,15},{14,10},{15,... | collective-permute-start | bytes 393224 | tf_op jit(solution)/shard_map/ppermute | solution.py:484
  23.5 5.8 %collective-permute-start.14 = (bf16[512,128]{1,0:T(8,128)(2,1)S(1)}, bf16[512,128]{1,0:T(8,128)(2,1)S(1)}, u32[]{:S(2)}, u32[]{:S(2)}) collective-permute-start(bf16[512,128]{1,0:T(8,128)(2,1)S(1)} %collective-permute-done.10), channel_id=1, source_target_pairs={{0,4},{1,5},{4,8},{5,9},{8,12},{9,13},{12,14},{13,15},{14,10},{15,... | collective-permute-start | bytes 393224 | tf_op jit(solution)/shard_map/ppermute | solution.py:484
  25.1 5.0 %collective-permute-start.15 = (bf16[512,128]{1,0:T(8,128)(2,1)S(1)}, bf16[512,128]{1,0:T(8,128)(2,1)S(1)}, u32[]{:S(2)}, u32[]{:S(2)}) collective-permute-start(bf16[512,128]{1,0:T(8,128)(2,1)S(1)} %collective-permute-done.13), channel_id=1, source_target_pairs={{0,2},{1,3},{4,0},{5,1},{8,4},{9,5},{12,8},{13,9},{14,12},{15,13},... | collective-permute-start | bytes 393224 | tf_op jit(solution)/shard_map/ppermute | solution.py:484
  30.7 1.4 %collective-permute-start.16 = (bf16[64,8,128]{2,1,0:T(8,128)(2,1)S(1)}, bf16[64,8,128]{2,1,0:T(8,128)(2,1)S(1)}, u32[]{:S(2)}, u32[]{:S(2)}) collective-permute-start(bf16[64,8,128]{2,1,0:T(8,128)(2,1)S(1)} %get-tuple-element.45), channel_id=1, source_target_pairs={{0,1},{1,0},{2,3},{3,2},{4,5},{5,4},{6,7},{7,6},{8,9},{9,8},{10,11... | collective-permute-start | bytes 393224 | tf_op jit(solution)/shard_map/ppermute | solution.py:524
  33.5 1.4 %collective-permute-start.17 = (bf16[512,128]{1,0:T(8,128)(2,1)S(1)}, bf16[512,128]{1,0:T(8,128)(2,1)S(1)}, u32[]{:S(2)}, u32[]{:S(2)}) collective-permute-start(bf16[512,128]{1,0:T(8,128)(2,1)S(1)} %get-tuple-element.52), channel_id=1, source_target_pairs={{0,1},{1,0},{2,3},{3,2},{4,5},{5,4},{6,7},{7,6},{8,9},{9,8},{10,11... | collective-permute-start | bytes 393224 | tf_op jit(solution)/shard_map/ppermute | solution.py:539
  33.7 1.4 %collective-permute-start.18 = (bf16[512,128]{1,0:T(8,128)(2,1)S(1)}, bf16[512,128]{1,0:T(8,128)(2,1)S(1)}, u32[]{:S(2)}, u32[]{:S(2)}) collective-permute-start(bf16[512,128]{1,0:T(8,128)(2,1)S(1)} %get-tuple-element.54), channel_id=1, source_target_pairs={{0,1},{1,0},{2,3},{3,2},{4,5},{5,4},{6,7},{7,6},{8,9},{9,8},{10,11... | collective-permute-start | bytes 393224 | tf_op jit(solution)/shard_map/ppermute | solution.py:540
  35.7 5.8 %collective-permute-start.29 = (bf16[32,16,128]{2,1,0:T(8,128)(2,1)S(1)}, bf16[32,16,128]{2,1,0:T(8,128)(2,1)S(1)}, u32[]{:S(2)}, u32[]{:S(2)}) collective-permute-start(bf16[32,16,128]{2,1,0:T(8,128)(2,1)S(1)} %get-tuple-element.60), channel_id=1, source_target_pairs={{0,2},{1,3},{4,0},{5,1},{8,4},{9,5},{12,8},{13,9},{14,12},{15,13},... | collective-permute-start | bytes 393224 | tf_op jit(solution)/shard_map/ppermute | solution.py:484
  37.3 6.4 %collective-permute-start.19 = (bf16[32,16,128]{2,1,0:T(8,128)(2,1)S(1)}, bf16[32,16,128]{2,1,0:T(8,128)(2,1)S(1)}, u32[]{:S(2)}, u32[]{:S(2)}) collective-permute-start(bf16[32,16,128]{2,1,0:T(8,128)(2,1)S(1)} %get-tuple-element.56), channel_id=1, source_target_pairs={{0,4},{1,5},{4,8},{5,9},{8,12},{9,13},{12,14},{13,15},{14,10},{15,... | collective-permute-start | bytes 393224 | tf_op jit(solution)/shard_map/ppermute | solution.py:484
  38.5 8.0 %collective-permute-start.26 = (bf16[32,16,128]{2,1,0:T(8,128)(2,1)S(1)}, bf16[32,16,128]{2,1,0:T(8,128)(2,1)S(1)}, u32[]{:S(2)}, u32[]{:S(2)}) collective-permute-start(bf16[32,16,128]{2,1,0:T(8,128)(2,1)S(1)} %get-tuple-element.59), channel_id=1, source_target_pairs={{0,4},{1,5},{4,8},{5,9},{8,12},{9,13},{12,14},{13,15},{14,10},{15,... | collective-permute-start | bytes 393224 | tf_op jit(solution)/shard_map/ppermute | solution.py:484
  40.0 7.8 %collective-permute-start.23 = (bf16[32,16,128]{2,1,0:T(8,128)(2,1)S(1)}, bf16[32,16,128]{2,1,0:T(8,128)(2,1)S(1)}, u32[]{:S(2)}, u32[]{:S(2)}) collective-permute-start(bf16[32,16,128]{2,1,0:T(8,128)(2,1)S(1)} %get-tuple-element.57), channel_id=1, source_target_pairs={{0,2},{1,3},{4,0},{5,1},{8,4},{9,5},{12,8},{13,9},{14,12},{15,13},... | collective-permute-start | bytes 393224 | tf_op jit(solution)/shard_map/ppermute | solution.py:484
  41.5 7.1 %collective-permute-start.30 = (bf16[32,16,128]{2,1,0:T(8,128)(2,1)S(1)}, bf16[32,16,128]{2,1,0:T(8,128)(2,1)S(1)}, u32[]{:S(2)}, u32[]{:S(2)}) collective-permute-start(bf16[32,16,128]{2,1,0:T(8,128)(2,1)S(1)} %scatter_add.17), channel_id=1, source_target_pairs={{0,2},{1,3},{4,0},{5,1},{8,4},{9,5},{12,8},{13,9},{14,12},{15,13},... | collective-permute-start | bytes 393224 | tf_op jit(solution)/shard_map/ppermute | solution.py:484
  43.7 6.6 %collective-permute-start.20 = (bf16[32,16,128]{2,1,0:T(8,128)(2,1)S(1)}, bf16[32,16,128]{2,1,0:T(8,128)(2,1)S(1)}, u32[]{:S(2)}, u32[]{:S(2)}) collective-permute-start(bf16[32,16,128]{2,1,0:T(8,128)(2,1)S(1)} %scatter_add.10), channel_id=1, source_target_pairs={{0,4},{1,5},{4,8},{5,9},{8,12},{9,13},{12,14},{13,15},{14,10},{15,... | collective-permute-start | bytes 393224 | tf_op jit(solution)/shard_map/ppermute | solution.py:484
  46.5 6.1 %collective-permute-start.27 = (bf16[32,16,128]{2,1,0:T(8,128)(2,1)S(1)}, bf16[32,16,128]{2,1,0:T(8,128)(2,1)S(1)}, u32[]{:S(2)}, u32[]{:S(2)}) collective-permute-start(bf16[32,16,128]{2,1,0:T(8,128)(2,1)S(1)} %scatter_add.15), channel_id=1, source_target_pairs={{0,4},{1,5},{4,8},{5,9},{8,12},{9,13},{12,14},{13,15},{14,10},{15,... | collective-permute-start | bytes 393224 | tf_op jit(solution)/shard_map/ppermute | solution.py:484
  47.8 6.5 %collective-permute-start.24 = (bf16[32,16,128]{2,1,0:T(8,128)(2,1)S(1)}, bf16[32,16,128]{2,1,0:T(8,128)(2,1)S(1)}, u32[]{:S(2)}, u32[]{:S(2)}) collective-permute-start(bf16[32,16,128]{2,1,0:T(8,128)(2,1)S(1)} %scatter_add.13), channel_id=1, source_target_pairs={{0,2},{1,3},{4,0},{5,1},{8,4},{9,5},{12,8},{13,9},{14,12},{15,13},... | collective-permute-start | bytes 393224 | tf_op jit(solution)/shard_map/ppermute | solution.py:484
  48.7 6.1 %collective-permute-start.31 = (bf16[32,16,128]{2,1,0:T(8,128)(2,1)S(1)}, bf16[32,16,128]{2,1,0:T(8,128)(2,1)S(1)}, u32[]{:S(2)}, u32[]{:S(2)}) collective-permute-start(bf16[32,16,128]{2,1,0:T(8,128)(2,1)S(1)} %scatter_add.18), channel_id=1, source_target_pairs={{0,2},{1,3},{4,0},{5,1},{8,4},{9,5},{12,8},{13,9},{14,12},{15,13},... | collective-permute-start | bytes 393224 | tf_op jit(solution)/shard_map/ppermute | solution.py:484
  50.4 6.1 %collective-permute-start.21 = (bf16[32,16,128]{2,1,0:T(8,128)(2,1)S(1)}, bf16[32,16,128]{2,1,0:T(8,128)(2,1)S(1)}, u32[]{:S(2)}, u32[]{:S(2)}) collective-permute-start(bf16[32,16,128]{2,1,0:T(8,128)(2,1)S(1)} %scatter_add.11), channel_id=1, source_target_pairs={{0,4},{1,5},{4,8},{5,9},{8,12},{9,13},{12,14},{13,15},{14,10},{15,... | collective-permute-start | bytes 393224 | tf_op jit(solution)/shard_map/ppermute | solution.py:484
  52.7 6.0 %collective-permute-start.28 = (bf16[32,16,128]{2,1,0:T(8,128)(2,1)S(1)}, bf16[32,16,128]{2,1,0:T(8,128)(2,1)S(1)}, u32[]{:S(2)}, u32[]{:S(2)}) collective-permute-start(bf16[32,16,128]{2,1,0:T(8,128)(2,1)S(1)} %scatter_add.16), channel_id=1, source_target_pairs={{0,4},{1,5},{4,8},{5,9},{8,12},{9,13},{12,14},{13,15},{14,10},{15,... | collective-permute-start | bytes 393224 | tf_op jit(solution)/shard_map/ppermute | solution.py:484
  54.3 5.0 %collective-permute-start.25 = (bf16[32,16,128]{2,1,0:T(8,128)(2,1)S(1)}, bf16[32,16,128]{2,1,0:T(8,128)(2,1)S(1)}, u32[]{:S(2)}, u32[]{:S(2)}) collective-permute-start(bf16[32,16,128]{2,1,0:T(8,128)(2,1)S(1)} %scatter_add.14), channel_id=1, source_target_pairs={{0,2},{1,3},{4,0},{5,1},{8,4},{9,5},{12,8},{13,9},{14,12},{15,13},... | collective-permute-start | bytes 393224 | tf_op jit(solution)/shard_map/ppermute | solution.py:484
  54.9 5.9 %collective-permute-start.32 = (bf16[32,16,128]{2,1,0:T(8,128)(2,1)S(1)}, bf16[32,16,128]{2,1,0:T(8,128)(2,1)S(1)}, u32[]{:S(2)}, u32[]{:S(2)}) collective-permute-start(bf16[32,16,128]{2,1,0:T(8,128)(2,1)S(1)} %scatter_add.19), channel_id=1, source_target_pairs={{0,2},{1,3},{4,0},{5,1},{8,4},{9,5},{12,8},{13,9},{14,12},{15,13},... | collective-permute-start | bytes 393224 | tf_op jit(solution)/shard_map/ppermute | solution.py:484
  56.5 5.0 %collective-permute-start.22 = (bf16[32,16,128]{2,1,0:T(8,128)(2,1)S(1)}, bf16[32,16,128]{2,1,0:T(8,128)(2,1)S(1)}, u32[]{:S(2)}, u32[]{:S(2)}) collective-permute-start(bf16[32,16,128]{2,1,0:T(8,128)(2,1)S(1)} %scatter_add.12), channel_id=1, source_target_pairs={{0,4},{1,5},{4,8},{5,9},{8,12},{9,13},{12,14},{13,15},{14,10},{15,... | collective-permute-start | bytes 393224 | tf_op jit(solution)/shard_map/ppermute | solution.py:484
  61.6 1.4 %collective-permute-start.33 = (bf16[64,8,128]{2,1,0:T(8,128)(2,1)S(1)}, bf16[64,8,128]{2,1,0:T(8,128)(2,1)S(1)}, u32[]{:S(2)}, u32[]{:S(2)}) collective-permute-start(bf16[64,8,128]{2,1,0:T(8,128)(2,1)S(1)} %get-tuple-element.62), channel_id=1, source_target_pairs={{0,1},{1,0},{2,3},{3,2},{4,5},{5,4},{6,7},{7,6},{8,9},{9,8},{10,11... | collective-permute-start | bytes 393224 | tf_op jit(solution)/shard_map/ppermute | solution.py:577

commit v26 on v25

--- a/solution.py
+++ b/solution.py
@@ -496,7 +496,7 @@
         ups = [rounds(right, 1, middle), rounds(got_right, 1, middle - 1)]
         downs = [rounds(right, -1, middle - 1), rounds(got_right, -1, middle)]
         distances = sorted(range(chips), key=lambda d: min(d, chips - d))
-        early = 2 * (chips // 2 + 1)
+        early = 2 * (chips - 1)
         rights = [
             ups[piece][d] if d < len(ups[piece]) else downs[piece][chips - d] for d in distances for piece in range(2)
         ]

time: 64.4 us -> 64.3 us (level)
  no operation moved by 1% of the time
where the time goes in v26:
time: 64.3 us; the launch traced here: 64.2 us
  starting transfers between devices  32.7 us (51%)
  waiting for transfers between devices  22.2 us (35%)
  Pallas kernels  8.07 us (13%)
  other arithmetic  0.8 us (1%)
    ppermute x28, starting transfers between devices, along(): return lax.ppermute(array, 'row', pairs)  31.4 us
    ppermute x28, waiting for transfers between devices, along(): return lax.ppermute(array, 'row', pairs)  18.9 us
    ppermute x2, waiting for transfers between devices, on_device(): lax.ppermute(send, 'row', swap).reshape(half * rows, tokens)  2.59 us
    pallas_call x1, Pallas kernels, on_device(): pl.pallas_call(right_kernel, out_shape=(half_shape, half_shape, flat_shap...  1.7 us
    pallas_call x1, Pallas kernels, on_device(): pl.pallas_call(functools.partial(step_kernel, half if by_core else per_gr...  1.37 us
    pallas_call x2, Pallas kernels, on_device(): pl.pallas_call(functools.partial(scatter_start, piece * size, hops[0], ch...  1.33 us
  transfers between devices with their start and end apart: 34, of which 21 were waited for; matrix products, arithmetic and copies ran while one was open for 1% of the time, Pallas kernels for 4%

profile of v26, /device:TPU:0, one launch (start us, length us, event | category | flops | bytes accessed | tf_op | source)
XLA Modules:
  0.0 64.2 jit_solution(6536160524629151731)
XLA Ops:
  0.0 1.7 %project_right.1 = (bf16[512,128]{1,0:T(8,128)(2,1)S(1)}, bf16[512,128]{1,0:T(8,128)(2,1)S(1)}, bf16[128,1024]{1,0:T(8,128)(2,1)S(1)}, bf16[128,1024]{1,0:T(8,12...) custom-call(s32[1]{0:T(128)} %bitcast.core_ref.refs_0_, ...), custom_call_target="tpu_custom_call" | custom-call | tf_op jit(solution)/shard_map/project_right/pallas_call | solution.py:437
  1.7 3.0 %collective-permute-start.4 = (bf16[512,128]{1,0:T(8,128)(2,1)S(1)}, bf16[512,128]{1,0:T(8,128)(2,1)S(1)}, u32[]{:S(2)}, u32[]{:S(2)}) collective-permute-start(bf16[512,128]{1,0:T(8,128)(2,1)S(1)} %get-tuple-element.42), channel_id=1, source_target_pairs={{0,2},{1,3},{4,0},{5,1},{8,4},{9,5},{12,8},{13,9},{14,12},{15,13},... | collective-permute-start | bytes 393224 | tf_op jit(solution)/shard_map/ppermute | solution.py:484
  4.7 0.1 collective-permute-start.2
  4.8 0.4 project_left.1
  5.3 0.6 collective-permute-start
  6.0 0.3 fusion.1.order_ref
  6.3 0.1 fusion.2.order_ref
  6.4 2.0 %collective-permute-start.5 = (bf16[512,128]{1,0:T(8,128)(2,1)S(1)}, bf16[512,128]{1,0:T(8,128)(2,1)S(1)}, u32[]{:S(2)}, u32[]{:S(2)}) collective-permute-start(bf16[512,128]{1,0:T(8,128)(2,1)S(1)} %collective-permute-done.1), channel_id=1, source_target_pairs={{0,2},{1,3},{4,0},{5,1},{8,4},{9,5},{12,8},{13,9},{14,12},{15,13},... | collective-permute-start | bytes 393224 | tf_op jit(solution)/shard_map/ppermute | solution.py:484
  8.4 0.1 collective-permute-start.3
  8.5 1.2 %collective-permute-done.2 = bf16[512,128]{1,0:T(8,128)(2,1)S(1)} collective-permute-done((bf16[512,128]{1,0:T(8,128)(2,1)S(1)}, bf16[512,128]{1,0:T(8,128)(2,1)S(1)}, u32[]{:S(2)}, u32[]{:S(2)}) %collective-permute-start.2) | collective-permute-done | bytes 131104 | tf_op jit(solution)/shard_map/ppermute | solution.py:484
  9.7 0.8 %collective-permute-start.6 = (bf16[512,128]{1,0:T(8,128)(2,1)S(1)}, bf16[512,128]{1,0:T(8,128)(2,1)S(1)}, u32[]{:S(2)}, u32[]{:S(2)}) collective-permute-start(bf16[512,128]{1,0:T(8,128)(2,1)S(1)} %collective-permute-done.2), channel_id=1, source_target_pairs={{0,4},{1,5},{4,8},{5,9},{8,12},{9,13},{12,14},{13,15},{14,10},{15,... | collective-permute-start | bytes 393224 | tf_op jit(solution)/shard_map/ppermute | solution.py:484
  10.5 1.8 %collective-permute-done.5 = bf16[512,128]{1,0:T(8,128)(2,1)S(1)} collective-permute-done((bf16[512,128]{1,0:T(8,128)(2,1)S(1)}, bf16[512,128]{1,0:T(8,128)(2,1)S(1)}, u32[]{:S(2)}, u32[]{:S(2)}) %collective-permute-start.5) | collective-permute-done | bytes 131104 | tf_op jit(solution)/shard_map/ppermute | solution.py:484
  12.3 1.7 %collective-permute-start.9 = (bf16[512,128]{1,0:T(8,128)(2,1)S(1)}, bf16[512,128]{1,0:T(8,128)(2,1)S(1)}, u32[]{:S(2)}, u32[]{:S(2)}) collective-permute-start(bf16[512,128]{1,0:T(8,128)(2,1)S(1)} %collective-permute-done.5), channel_id=1, source_target_pairs={{0,2},{1,3},{4,0},{5,1},{8,4},{9,5},{12,8},{13,9},{14,12},{15,13},... | collective-permute-start | bytes 393224 | tf_op jit(solution)/shard_map/ppermute | solution.py:484
  14.0 1.6 %collective-permute-start.8 = (bf16[512,128]{1,0:T(8,128)(2,1)S(1)}, bf16[512,128]{1,0:T(8,128)(2,1)S(1)}, u32[]{:S(2)}, u32[]{:S(2)}) collective-permute-start(bf16[512,128]{1,0:T(8,128)(2,1)S(1)} %collective-permute-done.4), channel_id=1, source_target_pairs={{0,2},{1,3},{4,0},{5,1},{8,4},{9,5},{12,8},{13,9},{14,12},{15,13},... | collective-permute-start | bytes 393224 | tf_op jit(solution)/shard_map/ppermute | solution.py:484
  15.6 0.4 collective-permute-start.7
  16.0 0.4 collective-permute-done.6
  16.5 0.4 collective-permute-start.10
  16.9 1.8 %collective-permute-done.9 = bf16[512,128]{1,0:T(8,128)(2,1)S(1)} collective-permute-done((bf16[512,128]{1,0:T(8,128)(2,1)S(1)}, bf16[512,128]{1,0:T(8,128)(2,1)S(1)}, u32[]{:S(2)}, u32[]{:S(2)}) %collective-permute-start.9) | collective-permute-done | bytes 131104 | tf_op jit(solution)/shard_map/ppermute | solution.py:484
  18.7 1.5 %collective-permute-start.13 = (bf16[512,128]{1,0:T(8,128)(2,1)S(1)}, bf16[512,128]{1,0:T(8,128)(2,1)S(1)}, u32[]{:S(2)}, u32[]{:S(2)}) collective-permute-start(bf16[512,128]{1,0:T(8,128)(2,1)S(1)} %collective-permute-done.9), channel_id=1, source_target_pairs={{0,2},{1,3},{4,0},{5,1},{8,4},{9,5},{12,8},{13,9},{14,12},{15,13},... | collective-permute-start | bytes 393224 | tf_op jit(solution)/shard_map/ppermute | solution.py:484
  20.2 1.3 %collective-permute-done.8 = bf16[512,128]{1,0:T(8,128)(2,1)S(1)} collective-permute-done((bf16[512,128]{1,0:T(8,128)(2,1)S(1)}, bf16[512,128]{1,0:T(8,128)(2,1)S(1)}, u32[]{:S(2)}, u32[]{:S(2)}) %collective-permute-start.8) | collective-permute-done | bytes 131104 | tf_op jit(solution)/shard_map/ppermute | solution.py:484
  21.5 1.5 %collective-permute-start.12 = (bf16[512,128]{1,0:T(8,128)(2,1)S(1)}, bf16[512,128]{1,0:T(8,128)(2,1)S(1)}, u32[]{:S(2)}, u32[]{:S(2)}) collective-permute-start(bf16[512,128]{1,0:T(8,128)(2,1)S(1)} %collective-permute-done.8), channel_id=1, source_target_pairs={{0,2},{1,3},{4,0},{5,1},{8,4},{9,5},{12,8},{13,9},{14,12},{15,13},... | collective-permute-start | bytes 393224 | tf_op jit(solution)/shard_map/ppermute | solution.py:484
  23.0 0.6 collective-permute-start.11
  23.5 1.7 %collective-permute-start.14 = (bf16[512,128]{1,0:T(8,128)(2,1)S(1)}, bf16[512,128]{1,0:T(8,128)(2,1)S(1)}, u32[]{:S(2)}, u32[]{:S(2)}) collective-permute-start(bf16[512,128]{1,0:T(8,128)(2,1)S(1)} %collective-permute-done.10), channel_id=1, source_target_pairs={{0,4},{1,5},{4,8},{5,9},{8,12},{9,13},{12,14},{13,15},{14,10},{15,... | collective-permute-start | bytes 393224 | tf_op jit(solution)/shard_map/ppermute | solution.py:484
  25.2 0.6 collective-permute-start.15
  25.8 1.3 %collective-permute-done.12 = bf16[512,128]{1,0:T(8,128)(2,1)S(1)} collective-permute-done((bf16[512,128]{1,0:T(8,128)(2,1)S(1)}, bf16[512,128]{1,0:T(8,128)(2,1)S(1)}, u32[]{:S(2)}, u32[]{:S(2)}) %collective-permute-start.12) | collective-permute-done | bytes 131104 | tf_op jit(solution)/shard_map/ppermute | solution.py:484
  27.1 0.8 %collective-permute-done.11 = bf16[512,128]{1,0:T(8,128)(2,1)S(1)} collective-permute-done((bf16[512,128]{1,0:T(8,128)(2,1)S(1)}, bf16[512,128]{1,0:T(8,128)(2,1)S(1)}, u32[]{:S(2)}, u32[]{:S(2)}) %collective-permute-start.11) | collective-permute-done | bytes 131104 | tf_op jit(solution)/shard_map/ppermute | solution.py:484
  27.9 1.2 %mix_early.1.early_ref = bf16[64,16,128]{2,1,0:T(8,128)(2,1)S(1)} custom-call(bf16[112,128]{1,0:T(8,128)(2,1)S(1)} %fusion.1.order_ref, bf16[64,8,128]{2,1,0:T(8,128)(2,1)S(1)} %bitcast.39, bf16[64,8,128]{2,1,0:T(8,128)(2,1)S(1)} %bitcast.41, bf16[64,8,128]{2,1,0:T(8,128)(2,1)S(1)} %bitcast.45, bf16[64,8,128]{2,1,0:T(8,128)(2,1)S(1)} %bitcast.48, ...), custom_call_target="tpu_custom_call" | custom-call | flops 1000000000 | bytes 4194304 | tf_op jit(solution)/shard_map/mix_early/pallas_call | solution.py:505
  29.1 0.2 collective-permute-done.14
  29.3 0.9 %collective-permute-done.15 = bf16[512,128]{1,0:T(8,128)(2,1)S(1)} collective-permute-done((bf16[512,128]{1,0:T(8,128)(2,1)S(1)}, bf16[512,128]{1,0:T(8,128)(2,1)S(1)}, u32[]{:S(2)}, u32[]{:S(2)}) %collective-permute-start.15) | collective-permute-done | bytes 131104 | tf_op jit(solution)/shard_map/ppermute | solution.py:484
  30.2 0.4 mix_late.1
  30.8 1.3 %collective-permute-done.16 = bf16[64,8,128]{2,1,0:T(8,128)(2,1)S(1)} collective-permute-done((bf16[64,8,128]{2,1,0:T(8,128)(2,1)S(1)}, bf16[64,8,128]{2,1,0:T(8,128)(2,1)S(1)}, u32[]{:S(2)}, u32[]{:S(2)}) %collective-permute-start.16) | collective-permute-done | bytes 131104 | tf_op jit(solution)/shard_map/ppermute | solution.py:524
  32.1 1.4 %finish_project.1 = (bf16[512,128]{1,0:T(8,128)(2,1)S(1)}, bf16[512,128]{1,0:T(8,128)(2,1)S(1)}, bf16[512,128]{1,0:T(8,128)(2,1)S(1)}, bf16[512,128]{1,0:T(8,128...) custom-call(s32[1]{0:T(128)} %bitcast.core_ref.refs_0_, bf16[512,128]{1,0:T(8,128)(2,1)S(1)} %bitcast.35, ...), custom_call_target="tpu_custom_call" | custom-call | tf_op jit(solution)/shard_map/finish_project/pallas_call | solution.py:527
  33.4 0.2 collective-permute-start.17
  33.7 0.4 collective-permute-start.18
  34.0 0.3 fusion.order_ref
  34.4 0.5 collective-permute-done.17
  34.9 0.2 collective-permute-done.18
  35.0 0.7 %scatter_start.3 = (f32[32,128,128]{2,1,0:T(8,128)S(1)}, bf16[32,16,128]{2,1,0:T(8,128)(2,1)S(1)}, bf16[32,16,128]{2,1,0:T(8,128)(2,1)S(1)}) custom-call(bf16[128,128]{1,0:T(8,128)(2,1)S(1)} %fusion.order_ref, bf16[64,8,128]{2,1,0:T(8,128)(2,1)S(1)} %bitcast.27, bf16[64,8,128]{2,1,0:T(8,128)(2,1)S(1)} %bitcast.31, bf16[64,8,128]{2,1,0:T(8,128)(2,1)S(1)} %bitcast.29, ...), custom_call_target="tpu_custom_call" | custom-call | tf_op jit(solution)/shard_map/scatter_start/pallas_call | solution.py:548
  35.7 0.8 %collective-permute-start.29 = (bf16[32,16,128]{2,1,0:T(8,128)(2,1)S(1)}, bf16[32,16,128]{2,1,0:T(8,128)(2,1)S(1)}, u32[]{:S(2)}, u32[]{:S(2)}) collective-permute-start(bf16[32,16,128]{2,1,0:T(8,128)(2,1)S(1)} %get-tuple-element.60), channel_id=1, source_target_pairs={{0,2},{1,3},{4,0},{5,1},{8,4},{9,5},{12,8},{13,9},{14,12},{15,13},... | collective-permute-start | bytes 393224 | tf_op jit(solution)/shard_map/ppermute | solution.py:484
  36.5 0.7 %scatter_start.2 = (f32[32,128,128]{2,1,0:T(8,128)S(1)}, bf16[32,16,128]{2,1,0:T(8,128)(2,1)S(1)}, bf16[32,16,128]{2,1,0:T(8,128)(2,1)S(1)}) custom-call(bf16[128,128]{1,0:T(8,128)(2,1)S(1)} %fusion.order_ref, bf16[64,8,128]{2,1,0:T(8,128)(2,1)S(1)} %bitcast.28, bf16[64,8,128]{2,1,0:T(8,128)(2,1)S(1)} %bitcast.32, bf16[64,8,128]{2,1,0:T(8,128)(2,1)S(1)} %bitcast.30, ...), custom_call_target="tpu_custom_call" | custom-call | tf_op jit(solution)/shard_map/scatter_start/pallas_call | solution.py:548
  37.1 1.4 %collective-permute-start.19 = (bf16[32,16,128]{2,1,0:T(8,128)(2,1)S(1)}, bf16[32,16,128]{2,1,0:T(8,128)(2,1)S(1)}, u32[]{:S(2)}, u32[]{:S(2)}) collective-permute-start(bf16[32,16,128]{2,1,0:T(8,128)(2,1)S(1)} %get-tuple-element.56), channel_id=1, source_target_pairs={{0,4},{1,5},{4,8},{5,9},{8,12},{9,13},{12,14},{13,15},{14,10},{15,... | collective-permute-start | bytes 393224 | tf_op jit(solution)/shard_map/ppermute | solution.py:484
  38.5 1.4 %collective-permute-start.26 = (bf16[32,16,128]{2,1,0:T(8,128)(2,1)S(1)}, bf16[32,16,128]{2,1,0:T(8,128)(2,1)S(1)}, u32[]{:S(2)}, u32[]{:S(2)}) collective-permute-start(bf16[32,16,128]{2,1,0:T(8,128)(2,1)S(1)} %get-tuple-element.59), channel_id=1, source_target_pairs={{0,4},{1,5},{4,8},{5,9},{8,12},{9,13},{12,14},{13,15},{14,10},{15,... | collective-permute-start | bytes 393224 | tf_op jit(solution)/shard_map/ppermute | solution.py:484
  40.0 0.6 collective-permute-start.23
  40.5 1.0 %collective-permute-done.29.got_ref = bf16[32,16,128]{2,1,0:T(8,128)(2,1)S(1)} collective-permute-done((bf16[32,16,128]{2,1,0:T(8,128)(2,1)S(1)}, bf16[32,16,128]{2,1,0:T(8,128)(2,1)S(1)}, u32[]{:S(2)}, u32[]{:S(2)}) %collective-permute-start.29) | collective-permute-done | bytes 131104 | tf_op jit(solution)/shard_map/ppermute | solution.py:484
  41.5 0.8 %collective-permute-start.30 = (bf16[32,16,128]{2,1,0:T(8,128)(2,1)S(1)}, bf16[32,16,128]{2,1,0:T(8,128)(2,1)S(1)}, u32[]{:S(2)}, u32[]{:S(2)}) collective-permute-start(bf16[32,16,128]{2,1,0:T(8,128)(2,1)S(1)} %scatter_add.17), channel_id=1, source_target_pairs={{0,2},{1,3},{4,0},{5,1},{8,4},{9,5},{12,8},{13,9},{14,12},{15,13},... | collective-permute-start | bytes 393224 | tf_op jit(solution)/shard_map/ppermute | solution.py:484
  42.3 1.3 %collective-permute-done.19.got_ref = bf16[32,16,128]{2,1,0:T(8,128)(2,1)S(1)} collective-permute-done((bf16[32,16,128]{2,1,0:T(8,128)(2,1)S(1)}, bf16[32,16,128]{2,1,0:T(8,128)(2,1)S(1)}, u32[]{:S(2)}, u32[]{:S(2)}) %collective-permute-start.19) | collective-permute-done | bytes 131104 | tf_op jit(solution)/shard_map/ppermute | solution.py:484
  43.6 1.4 %collective-permute-start.20 = (bf16[32,16,128]{2,1,0:T(8,128)(2,1)S(1)}, bf16[32,16,128]{2,1,0:T(8,128)(2,1)S(1)}, u32[]{:S(2)}, u32[]{:S(2)}) collective-permute-start(bf16[32,16,128]{2,1,0:T(8,128)(2,1)S(1)} %scatter_add.10), channel_id=1, source_target_pairs={{0,4},{1,5},{4,8},{5,9},{8,12},{9,13},{12,14},{13,15},{14,10},{15,... | collective-permute-start | bytes 393224 | tf_op jit(solution)/shard_map/ppermute | solution.py:484
  45.0 1.4 %collective-permute-done.26.got_ref = bf16[32,16,128]{2,1,0:T(8,128)(2,1)S(1)} collective-permute-done((bf16[32,16,128]{2,1,0:T(8,128)(2,1)S(1)}, bf16[32,16,128]{2,1,0:T(8,128)(2,1)S(1)}, u32[]{:S(2)}, u32[]{:S(2)}) %collective-permute-start.26) | collective-permute-done | bytes 131104 | tf_op jit(solution)/shard_map/ppermute | solution.py:484
  46.4 1.4 %collective-permute-start.27 = (bf16[32,16,128]{2,1,0:T(8,128)(2,1)S(1)}, bf16[32,16,128]{2,1,0:T(8,128)(2,1)S(1)}, u32[]{:S(2)}, u32[]{:S(2)}) collective-permute-start(bf16[32,16,128]{2,1,0:T(8,128)(2,1)S(1)} %scatter_add.15), channel_id=1, source_target_pairs={{0,4},{1,5},{4,8},{5,9},{8,12},{9,13},{12,14},{13,15},{14,10},{15,... | collective-permute-start | bytes 393224 | tf_op jit(solution)/shard_map/ppermute | solution.py:484
  47.8 0.8 %collective-permute-start.24 = (bf16[32,16,128]{2,1,0:T(8,128)(2,1)S(1)}, bf16[32,16,128]{2,1,0:T(8,128)(2,1)S(1)}, u32[]{:S(2)}, u32[]{:S(2)}) collective-permute-start(bf16[32,16,128]{2,1,0:T(8,128)(2,1)S(1)} %scatter_add.13), channel_id=1, source_target_pairs={{0,2},{1,3},{4,0},{5,1},{8,4},{9,5},{12,8},{13,9},{14,12},{15,13},... | collective-permute-start | bytes 393224 | tf_op jit(solution)/shard_map/ppermute | solution.py:484
  48.6 1.6 %collective-permute-start.31 = (bf16[32,16,128]{2,1,0:T(8,128)(2,1)S(1)}, bf16[32,16,128]{2,1,0:T(8,128)(2,1)S(1)}, u32[]{:S(2)}, u32[]{:S(2)}) collective-permute-start(bf16[32,16,128]{2,1,0:T(8,128)(2,1)S(1)} %scatter_add.18), channel_id=1, source_target_pairs={{0,2},{1,3},{4,0},{5,1},{8,4},{9,5},{12,8},{13,9},{14,12},{15,13},... | collective-permute-start | bytes 393224 | tf_op jit(solution)/shard_map/ppermute | solution.py:484
  50.2 1.0 %collective-permute-start.21 = (bf16[32,16,128]{2,1,0:T(8,128)(2,1)S(1)}, bf16[32,16,128]{2,1,0:T(8,128)(2,1)S(1)}, u32[]{:S(2)}, u32[]{:S(2)}) collective-permute-start(bf16[32,16,128]{2,1,0:T(8,128)(2,1)S(1)} %scatter_add.11), channel_id=1, source_target_pairs={{0,4},{1,5},{4,8},{5,9},{8,12},{9,13},{12,14},{13,15},{14,10},{15,... | collective-permute-start | bytes 393224 | tf_op jit(solution)/shard_map/ppermute | solution.py:484
  51.3 1.2 %collective-permute-done.27.got_ref = bf16[32,16,128]{2,1,0:T(8,128)(2,1)S(1)} collective-permute-done((bf16[32,16,128]{2,1,0:T(8,128)(2,1)S(1)}, bf16[32,16,128]{2,1,0:T(8,128)(2,1)S(1)}, u32[]{:S(2)}, u32[]{:S(2)}) %collective-permute-start.27) | collective-permute-done | bytes 131104 | tf_op jit(solution)/shard_map/ppermute | solution.py:484
  52.5 1.8 %collective-permute-start.28 = (bf16[32,16,128]{2,1,0:T(8,128)(2,1)S(1)}, bf16[32,16,128]{2,1,0:T(8,128)(2,1)S(1)}, u32[]{:S(2)}, u32[]{:S(2)}) collective-permute-start(bf16[32,16,128]{2,1,0:T(8,128)(2,1)S(1)} %scatter_add.16), channel_id=1, source_target_pairs={{0,4},{1,5},{4,8},{5,9},{8,12},{9,13},{12,14},{13,15},{14,10},{15,... | collective-permute-start | bytes 393224 | tf_op jit(solution)/shard_map/ppermute | solution.py:484
  54.3 0.4 collective-permute-start.25
  54.7 1.6 %collective-permute-start.32 = (bf16[32,16,128]{2,1,0:T(8,128)(2,1)S(1)}, bf16[32,16,128]{2,1,0:T(8,128)(2,1)S(1)}, u32[]{:S(2)}, u32[]{:S(2)}) collective-permute-start(bf16[32,16,128]{2,1,0:T(8,128)(2,1)S(1)} %scatter_add.19), channel_id=1, source_target_pairs={{0,2},{1,3},{4,0},{5,1},{8,4},{9,5},{12,8},{13,9},{14,12},{15,13},... | collective-permute-start | bytes 393224 | tf_op jit(solution)/shard_map/ppermute | solution.py:484
  56.4 0.7 %collective-permute-start.22 = (bf16[32,16,128]{2,1,0:T(8,128)(2,1)S(1)}, bf16[32,16,128]{2,1,0:T(8,128)(2,1)S(1)}, u32[]{:S(2)}, u32[]{:S(2)}) collective-permute-start(bf16[32,16,128]{2,1,0:T(8,128)(2,1)S(1)} %scatter_add.12), channel_id=1, source_target_pairs={{0,4},{1,5},{4,8},{5,9},{8,12},{9,13},{12,14},{13,15},{14,10},{15,... | collective-permute-start | bytes 393224 | tf_op jit(solution)/shard_map/ppermute | solution.py:484
  57.0 1.5 %collective-permute-done.28.refs_4_ = bf16[32,16,128]{2,1,0:T(8,128)(2,1)S(1)} collective-permute-done((bf16[32,16,128]{2,1,0:T(8,128)(2,1)S(1)}, bf16[32,16,128]{2,1,0:T(8,128)(2,1)S(1)}, u32[]{:S(2)}, u32[]{:S(2)}) %collective-permute-start.28) | collective-permute-done | bytes 131104 | tf_op jit(solution)/shard_map/ppermute | solution.py:484
  58.5 0.8 %collective-permute-done.25.refs_2_ = bf16[32,16,128]{2,1,0:T(8,128)(2,1)S(1)} collective-permute-done((bf16[32,16,128]{2,1,0:T(8,128)(2,1)S(1)}, bf16[32,16,128]{2,1,0:T(8,128)(2,1)S(1)}, u32[]{:S(2)}, u32[]{:S(2)}) %collective-permute-start.25) | collective-permute-done | bytes 131104 | tf_op jit(solution)/shard_map/ppermute | solution.py:484
  59.3 1.4 %collective-permute-done.32.refs_5_ = bf16[32,16,128]{2,1,0:T(8,128)(2,1)S(1)} collective-permute-done((bf16[32,16,128]{2,1,0:T(8,128)(2,1)S(1)}, bf16[32,16,128]{2,1,0:T(8,128)(2,1)S(1)}, u32[]{:S(2)}, u32[]{:S(2)}) %collective-permute-start.32) | collective-permute-done | bytes 131104 | tf_op jit(solution)/shard_map/ppermute | solution.py:484
  60.7 0.7 %collective-permute-done.22.refs_1_ = bf16[32,16,128]{2,1,0:T(8,128)(2,1)S(1)} collective-permute-done((bf16[32,16,128]{2,1,0:T(8,128)(2,1)S(1)}, bf16[32,16,128]{2,1,0:T(8,128)(2,1)S(1)}, u32[]{:S(2)}, u32[]{:S(2)}) %collective-permute-start.22) | collective-permute-done | bytes 131104 | tf_op jit(solution)/shard_map/ppermute | solution.py:484
  61.4 0.1 scatter_end.1
  61.6 1.3 %collective-permute-done.33 = bf16[64,8,128]{2,1,0:T(8,128)(2,1)S(1)} collective-permute-done((bf16[64,8,128]{2,1,0:T(8,128)(2,1)S(1)}, bf16[64,8,128]{2,1,0:T(8,128)(2,1)S(1)}, u32[]{:S(2)}, u32[]{:S(2)}) %collective-permute-start.33) | collective-permute-done | bytes 131104 | tf_op jit(solution)/shard_map/ppermute | solution.py:577
  62.9 1.3 %finish.1 = bf16[8,128,128]{2,1,0:T(8,128)(2,1)} custom-call(s32[1]{0:T(128)} %bitcast.core_ref.refs_0_, bf16[512,128]{1,0:T(8,128)(2,1)S(1)} %bitcast.37, bf16[512,128]{1,0:T(8,128)(2,1)S(1)} %bitcast.38, bf16[128,1024]{1,0:T(8,128)(2,1)S(1)} %get-tuple-element.63.refs_3_, bf16[128,1024]{1,0:T(8,128)(2,1)S(1)} %get-tuple-element.64.refs_4_, ...), custom_call_target="tpu_custom_call" | custom-call | tf_op jit(solution)/shard_map/finish/pallas_call | solution.py:580
  (45 shorter events, 0.5 us)
Async XLA Ops:
  1.7 12.3 %collective-permute-start.4 = (bf16[512,128]{1,0:T(8,128)(2,1)S(1)}, bf16[512,128]{1,0:T(8,128)(2,1)S(1)}, u32[]{:S(2)}, u32[]{:S(2)}) collective-permute-start(bf16[512,128]{1,0:T(8,128)(2,1)S(1)} %get-tuple-element.42), channel_id=1, source_target_pairs={{0,2},{1,3},{4,0},{5,1},{8,4},{9,5},{12,8},{13,9},{14,12},{15,13},... | collective-permute-start | bytes 393224 | tf_op jit(solution)/shard_map/ppermute | solution.py:484
  4.7 5.0 %collective-permute-start.2 = (bf16[512,128]{1,0:T(8,128)(2,1)S(1)}, bf16[512,128]{1,0:T(8,128)(2,1)S(1)}, u32[]{:S(2)}, u32[]{:S(2)}) collective-permute-start(bf16[512,128]{1,0:T(8,128)(2,1)S(1)} %get-tuple-element.42), channel_id=1, source_target_pairs={{0,4},{1,5},{4,8},{5,9},{8,12},{9,13},{12,14},{13,15},{14,10},{15,... | collective-permute-start | bytes 393224 | tf_op jit(solution)/shard_map/ppermute | solution.py:484
  4.8 1.6 %collective-permute-start.1 = (bf16[512,128]{1,0:T(8,128)(2,1)S(1)}, bf16[512,128]{1,0:T(8,128)(2,1)S(1)}, u32[]{:S(2)}, u32[]{:S(2)}) collective-permute-start(bf16[512,128]{1,0:T(8,128)(2,1)S(1)} %get-tuple-element.43), channel_id=1, source_target_pairs={{0,1},{1,0},{2,3},{3,2},{4,5},{5,4},{6,7},{7,6},{8,9},{9,8},{10,11... | collective-permute-start | bytes 393224 | tf_op jit(solution)/shard_map/ppermute | solution.py:493
  5.3 20.5 %collective-permute-start = (bf16[512,128]{1,0:T(8,128)(2,1)S(1)}, bf16[512,128]{1,0:T(8,128)(2,1)S(1)}, u32[]{:S(2)}, u32[]{:S(2)}) collective-permute-start(bf16[512,128]{1,0:T(8,128)(2,1)S(1)} %get-tuple-element.41), channel_id=1, source_target_pairs={{0,1},{1,0},{2,3},{3,2},{4,5},{5,4},{6,7},{7,6},{8,9},{9,8},{10,11... | collective-permute-start | bytes 393224 | tf_op jit(solution)/shard_map/ppermute | solution.py:494
  6.4 5.9 %collective-permute-start.5 = (bf16[512,128]{1,0:T(8,128)(2,1)S(1)}, bf16[512,128]{1,0:T(8,128)(2,1)S(1)}, u32[]{:S(2)}, u32[]{:S(2)}) collective-permute-start(bf16[512,128]{1,0:T(8,128)(2,1)S(1)} %collective-permute-done.1), channel_id=1, source_target_pairs={{0,2},{1,3},{4,0},{5,1},{8,4},{9,5},{12,8},{13,9},{14,12},{15,13},... | collective-permute-start | bytes 393224 | tf_op jit(solution)/shard_map/ppermute | solution.py:484
  8.4 7.2 %collective-permute-start.3 = (bf16[512,128]{1,0:T(8,128)(2,1)S(1)}, bf16[512,128]{1,0:T(8,128)(2,1)S(1)}, u32[]{:S(2)}, u32[]{:S(2)}) collective-permute-start(bf16[512,128]{1,0:T(8,128)(2,1)S(1)} %collective-permute-done.1), channel_id=1, source_target_pairs={{0,4},{1,5},{4,8},{5,9},{8,12},{9,13},{12,14},{13,15},{14,10},{15,... | collective-permute-start | bytes 393224 | tf_op jit(solution)/shard_map/ppermute | solution.py:484
  9.7 6.8 %collective-permute-start.6 = (bf16[512,128]{1,0:T(8,128)(2,1)S(1)}, bf16[512,128]{1,0:T(8,128)(2,1)S(1)}, u32[]{:S(2)}, u32[]{:S(2)}) collective-permute-start(bf16[512,128]{1,0:T(8,128)(2,1)S(1)} %collective-permute-done.2), channel_id=1, source_target_pairs={{0,4},{1,5},{4,8},{5,9},{8,12},{9,13},{12,14},{13,15},{14,10},{15,... | collective-permute-start | bytes 393224 | tf_op jit(solution)/shard_map/ppermute | solution.py:484
  12.3 6.4 %collective-permute-start.9 = (bf16[512,128]{1,0:T(8,128)(2,1)S(1)}, bf16[512,128]{1,0:T(8,128)(2,1)S(1)}, u32[]{:S(2)}, u32[]{:S(2)}) collective-permute-start(bf16[512,128]{1,0:T(8,128)(2,1)S(1)} %collective-permute-done.5), channel_id=1, source_target_pairs={{0,2},{1,3},{4,0},{5,1},{8,4},{9,5},{12,8},{13,9},{14,12},{15,13},... | collective-permute-start | bytes 393224 | tf_op jit(solution)/shard_map/ppermute | solution.py:484
  14.0 7.5 %collective-permute-start.8 = (bf16[512,128]{1,0:T(8,128)(2,1)S(1)}, bf16[512,128]{1,0:T(8,128)(2,1)S(1)}, u32[]{:S(2)}, u32[]{:S(2)}) collective-permute-start(bf16[512,128]{1,0:T(8,128)(2,1)S(1)} %collective-permute-done.4), channel_id=1, source_target_pairs={{0,2},{1,3},{4,0},{5,1},{8,4},{9,5},{12,8},{13,9},{14,12},{15,13},... | collective-permute-start | bytes 393224 | tf_op jit(solution)/shard_map/ppermute | solution.py:484
  15.6 7.4 %collective-permute-start.7 = (bf16[512,128]{1,0:T(8,128)(2,1)S(1)}, bf16[512,128]{1,0:T(8,128)(2,1)S(1)}, u32[]{:S(2)}, u32[]{:S(2)}) collective-permute-start(bf16[512,128]{1,0:T(8,128)(2,1)S(1)} %collective-permute-done.3), channel_id=1, source_target_pairs={{0,4},{1,5},{4,8},{5,9},{8,12},{9,13},{12,14},{13,15},{14,10},{15,... | collective-permute-start | bytes 393224 | tf_op jit(solution)/shard_map/ppermute | solution.py:484
  16.5 7.0 %collective-permute-start.10 = (bf16[512,128]{1,0:T(8,128)(2,1)S(1)}, bf16[512,128]{1,0:T(8,128)(2,1)S(1)}, u32[]{:S(2)}, u32[]{:S(2)}) collective-permute-start(bf16[512,128]{1,0:T(8,128)(2,1)S(1)} %collective-permute-done.6), channel_id=1, source_target_pairs={{0,4},{1,5},{4,8},{5,9},{8,12},{9,13},{12,14},{13,15},{14,10},{15,... | collective-permute-start | bytes 393224 | tf_op jit(solution)/shard_map/ppermute | solution.py:484
  18.7 6.6 %collective-permute-start.13 = (bf16[512,128]{1,0:T(8,128)(2,1)S(1)}, bf16[512,128]{1,0:T(8,128)(2,1)S(1)}, u32[]{:S(2)}, u32[]{:S(2)}) collective-permute-start(bf16[512,128]{1,0:T(8,128)(2,1)S(1)} %collective-permute-done.9), channel_id=1, source_target_pairs={{0,2},{1,3},{4,0},{5,1},{8,4},{9,5},{12,8},{13,9},{14,12},{15,13},... | collective-permute-start | bytes 393224 | tf_op jit(solution)/shard_map/ppermute | solution.py:484
  21.5 5.6 %collective-permute-start.12 = (bf16[512,128]{1,0:T(8,128)(2,1)S(1)}, bf16[512,128]{1,0:T(8,128)(2,1)S(1)}, u32[]{:S(2)}, u32[]{:S(2)}) collective-permute-start(bf16[512,128]{1,0:T(8,128)(2,1)S(1)} %collective-permute-done.8), channel_id=1, source_target_pairs={{0,2},{1,3},{4,0},{5,1},{8,4},{9,5},{12,8},{13,9},{14,12},{15,13},... | collective-permute-start | bytes 393224 | tf_op jit(solution)/shard_map/ppermute | solution.py:484
  23.0 5.0 %collective-permute-start.11 = (bf16[512,128]{1,0:T(8,128)(2,1)S(1)}, bf16[512,128]{1,0:T(8,128)(2,1)S(1)}, u32[]{:S(2)}, u32[]{:S(2)}) collective-permute-start(bf16[512,128]{1,0:T(8,128)(2,1)S(1)} %collective-permute-done.7), channel_id=1, source_target_pairs={{0,4},{1,5},{4,8},{5,9},{8,12},{9,13},{12,14},{13,15},{14,10},{15,... | collective-permute-start | bytes 393224 | tf_op jit(solution)/shard_map/ppermute | solution.py:484
  23.5 5.8 %collective-permute-start.14 = (bf16[512,128]{1,0:T(8,128)(2,1)S(1)}, bf16[512,128]{1,0:T(8,128)(2,1)S(1)}, u32[]{:S(2)}, u32[]{:S(2)}) collective-permute-start(bf16[512,128]{1,0:T(8,128)(2,1)S(1)} %collective-permute-done.10), channel_id=1, source_target_pairs={{0,4},{1,5},{4,8},{5,9},{8,12},{9,13},{12,14},{13,15},{14,10},{15,... | collective-permute-start | bytes 393224 | tf_op jit(solution)/shard_map/ppermute | solution.py:484
  25.2 5.0 %collective-permute-start.15 = (bf16[512,128]{1,0:T(8,128)(2,1)S(1)}, bf16[512,128]{1,0:T(8,128)(2,1)S(1)}, u32[]{:S(2)}, u32[]{:S(2)}) collective-permute-start(bf16[512,128]{1,0:T(8,128)(2,1)S(1)} %collective-permute-done.13), channel_id=1, source_target_pairs={{0,2},{1,3},{4,0},{5,1},{8,4},{9,5},{12,8},{13,9},{14,12},{15,13},... | collective-permute-start | bytes 393224 | tf_op jit(solution)/shard_map/ppermute | solution.py:484
  30.7 1.4 %collective-permute-start.16 = (bf16[64,8,128]{2,1,0:T(8,128)(2,1)S(1)}, bf16[64,8,128]{2,1,0:T(8,128)(2,1)S(1)}, u32[]{:S(2)}, u32[]{:S(2)}) collective-permute-start(bf16[64,8,128]{2,1,0:T(8,128)(2,1)S(1)} %get-tuple-element.45), channel_id=1, source_target_pairs={{0,1},{1,0},{2,3},{3,2},{4,5},{5,4},{6,7},{7,6},{8,9},{9,8},{10,11... | collective-permute-start | bytes 393224 | tf_op jit(solution)/shard_map/ppermute | solution.py:524
  33.4 1.4 %collective-permute-start.17 = (bf16[512,128]{1,0:T(8,128)(2,1)S(1)}, bf16[512,128]{1,0:T(8,128)(2,1)S(1)}, u32[]{:S(2)}, u32[]{:S(2)}) collective-permute-start(bf16[512,128]{1,0:T(8,128)(2,1)S(1)} %get-tuple-element.52), channel_id=1, source_target_pairs={{0,1},{1,0},{2,3},{3,2},{4,5},{5,4},{6,7},{7,6},{8,9},{9,8},{10,11... | collective-permute-start | bytes 393224 | tf_op jit(solution)/shard_map/ppermute | solution.py:539
  33.7 1.4 %collective-permute-start.18 = (bf16[512,128]{1,0:T(8,128)(2,1)S(1)}, bf16[512,128]{1,0:T(8,128)(2,1)S(1)}, u32[]{:S(2)}, u32[]{:S(2)}) collective-permute-start(bf16[512,128]{1,0:T(8,128)(2,1)S(1)} %get-tuple-element.54), channel_id=1, source_target_pairs={{0,1},{1,0},{2,3},{3,2},{4,5},{5,4},{6,7},{7,6},{8,9},{9,8},{10,11... | collective-permute-start | bytes 393224 | tf_op jit(solution)/shard_map/ppermute | solution.py:540
  35.7 5.8 %collective-permute-start.29 = (bf16[32,16,128]{2,1,0:T(8,128)(2,1)S(1)}, bf16[32,16,128]{2,1,0:T(8,128)(2,1)S(1)}, u32[]{:S(2)}, u32[]{:S(2)}) collective-permute-start(bf16[32,16,128]{2,1,0:T(8,128)(2,1)S(1)} %get-tuple-element.60), channel_id=1, source_target_pairs={{0,2},{1,3},{4,0},{5,1},{8,4},{9,5},{12,8},{13,9},{14,12},{15,13},... | collective-permute-start | bytes 393224 | tf_op jit(solution)/shard_map/ppermute | solution.py:484
  37.1 6.4 %collective-permute-start.19 = (bf16[32,16,128]{2,1,0:T(8,128)(2,1)S(1)}, bf16[32,16,128]{2,1,0:T(8,128)(2,1)S(1)}, u32[]{:S(2)}, u32[]{:S(2)}) collective-permute-start(bf16[32,16,128]{2,1,0:T(8,128)(2,1)S(1)} %get-tuple-element.56), channel_id=1, source_target_pairs={{0,4},{1,5},{4,8},{5,9},{8,12},{9,13},{12,14},{13,15},{14,10},{15,... | collective-permute-start | bytes 393224 | tf_op jit(solution)/shard_map/ppermute | solution.py:484
  38.5 7.8 %collective-permute-start.26 = (bf16[32,16,128]{2,1,0:T(8,128)(2,1)S(1)}, bf16[32,16,128]{2,1,0:T(8,128)(2,1)S(1)}, u32[]{:S(2)}, u32[]{:S(2)}) collective-permute-start(bf16[32,16,128]{2,1,0:T(8,128)(2,1)S(1)} %get-tuple-element.59), channel_id=1, source_target_pairs={{0,4},{1,5},{4,8},{5,9},{8,12},{9,13},{12,14},{13,15},{14,10},{15,... | collective-permute-start | bytes 393224 | tf_op jit(solution)/shard_map/ppermute | solution.py:484
  40.0 7.8 %collective-permute-start.23 = (bf16[32,16,128]{2,1,0:T(8,128)(2,1)S(1)}, bf16[32,16,128]{2,1,0:T(8,128)(2,1)S(1)}, u32[]{:S(2)}, u32[]{:S(2)}) collective-permute-start(bf16[32,16,128]{2,1,0:T(8,128)(2,1)S(1)} %get-tuple-element.57), channel_id=1, source_target_pairs={{0,2},{1,3},{4,0},{5,1},{8,4},{9,5},{12,8},{13,9},{14,12},{15,13},... | collective-permute-start | bytes 393224 | tf_op jit(solution)/shard_map/ppermute | solution.py:484
  41.5 7.0 %collective-permute-start.30 = (bf16[32,16,128]{2,1,0:T(8,128)(2,1)S(1)}, bf16[32,16,128]{2,1,0:T(8,128)(2,1)S(1)}, u32[]{:S(2)}, u32[]{:S(2)}) collective-permute-start(bf16[32,16,128]{2,1,0:T(8,128)(2,1)S(1)} %scatter_add.17), channel_id=1, source_target_pairs={{0,2},{1,3},{4,0},{5,1},{8,4},{9,5},{12,8},{13,9},{14,12},{15,13},... | collective-permute-start | bytes 393224 | tf_op jit(solution)/shard_map/ppermute | solution.py:484
  43.6 6.6 %collective-permute-start.20 = (bf16[32,16,128]{2,1,0:T(8,128)(2,1)S(1)}, bf16[32,16,128]{2,1,0:T(8,128)(2,1)S(1)}, u32[]{:S(2)}, u32[]{:S(2)}) collective-permute-start(bf16[32,16,128]{2,1,0:T(8,128)(2,1)S(1)} %scatter_add.10), channel_id=1, source_target_pairs={{0,4},{1,5},{4,8},{5,9},{8,12},{9,13},{12,14},{13,15},{14,10},{15,... | collective-permute-start | bytes 393224 | tf_op jit(solution)/shard_map/ppermute | solution.py:484
  46.4 6.1 %collective-permute-start.27 = (bf16[32,16,128]{2,1,0:T(8,128)(2,1)S(1)}, bf16[32,16,128]{2,1,0:T(8,128)(2,1)S(1)}, u32[]{:S(2)}, u32[]{:S(2)}) collective-permute-start(bf16[32,16,128]{2,1,0:T(8,128)(2,1)S(1)} %scatter_add.15), channel_id=1, source_target_pairs={{0,4},{1,5},{4,8},{5,9},{8,12},{9,13},{12,14},{13,15},{14,10},{15,... | collective-permute-start | bytes 393224 | tf_op jit(solution)/shard_map/ppermute | solution.py:484
  47.8 6.5 %collective-permute-start.24 = (bf16[32,16,128]{2,1,0:T(8,128)(2,1)S(1)}, bf16[32,16,128]{2,1,0:T(8,128)(2,1)S(1)}, u32[]{:S(2)}, u32[]{:S(2)}) collective-permute-start(bf16[32,16,128]{2,1,0:T(8,128)(2,1)S(1)} %scatter_add.13), channel_id=1, source_target_pairs={{0,2},{1,3},{4,0},{5,1},{8,4},{9,5},{12,8},{13,9},{14,12},{15,13},... | collective-permute-start | bytes 393224 | tf_op jit(solution)/shard_map/ppermute | solution.py:484
  48.6 6.1 %collective-permute-start.31 = (bf16[32,16,128]{2,1,0:T(8,128)(2,1)S(1)}, bf16[32,16,128]{2,1,0:T(8,128)(2,1)S(1)}, u32[]{:S(2)}, u32[]{:S(2)}) collective-permute-start(bf16[32,16,128]{2,1,0:T(8,128)(2,1)S(1)} %scatter_add.18), channel_id=1, source_target_pairs={{0,2},{1,3},{4,0},{5,1},{8,4},{9,5},{12,8},{13,9},{14,12},{15,13},... | collective-permute-start | bytes 393224 | tf_op jit(solution)/shard_map/ppermute | solution.py:484
  50.2 6.1 %collective-permute-start.21 = (bf16[32,16,128]{2,1,0:T(8,128)(2,1)S(1)}, bf16[32,16,128]{2,1,0:T(8,128)(2,1)S(1)}, u32[]{:S(2)}, u32[]{:S(2)}) collective-permute-start(bf16[32,16,128]{2,1,0:T(8,128)(2,1)S(1)} %scatter_add.11), channel_id=1, source_target_pairs={{0,4},{1,5},{4,8},{5,9},{8,12},{9,13},{12,14},{13,15},{14,10},{15,... | collective-permute-start | bytes 393224 | tf_op jit(solution)/shard_map/ppermute | solution.py:484
  52.5 6.0 %collective-permute-start.28 = (bf16[32,16,128]{2,1,0:T(8,128)(2,1)S(1)}, bf16[32,16,128]{2,1,0:T(8,128)(2,1)S(1)}, u32[]{:S(2)}, u32[]{:S(2)}) collective-permute-start(bf16[32,16,128]{2,1,0:T(8,128)(2,1)S(1)} %scatter_add.16), channel_id=1, source_target_pairs={{0,4},{1,5},{4,8},{5,9},{8,12},{9,13},{12,14},{13,15},{14,10},{15,... | collective-permute-start | bytes 393224 | tf_op jit(solution)/shard_map/ppermute | solution.py:484
  54.3 5.0 %collective-permute-start.25 = (bf16[32,16,128]{2,1,0:T(8,128)(2,1)S(1)}, bf16[32,16,128]{2,1,0:T(8,128)(2,1)S(1)}, u32[]{:S(2)}, u32[]{:S(2)}) collective-permute-start(bf16[32,16,128]{2,1,0:T(8,128)(2,1)S(1)} %scatter_add.14), channel_id=1, source_target_pairs={{0,2},{1,3},{4,0},{5,1},{8,4},{9,5},{12,8},{13,9},{14,12},{15,13},... | collective-permute-start | bytes 393224 | tf_op jit(solution)/shard_map/ppermute | solution.py:484
  54.7 6.0 %collective-permute-start.32 = (bf16[32,16,128]{2,1,0:T(8,128)(2,1)S(1)}, bf16[32,16,128]{2,1,0:T(8,128)(2,1)S(1)}, u32[]{:S(2)}, u32[]{:S(2)}) collective-permute-start(bf16[32,16,128]{2,1,0:T(8,128)(2,1)S(1)} %scatter_add.19), channel_id=1, source_target_pairs={{0,2},{1,3},{4,0},{5,1},{8,4},{9,5},{12,8},{13,9},{14,12},{15,13},... | collective-permute-start | bytes 393224 | tf_op jit(solution)/shard_map/ppermute | solution.py:484
  56.4 5.0 %collective-permute-start.22 = (bf16[32,16,128]{2,1,0:T(8,128)(2,1)S(1)}, bf16[32,16,128]{2,1,0:T(8,128)(2,1)S(1)}, u32[]{:S(2)}, u32[]{:S(2)}) collective-permute-start(bf16[32,16,128]{2,1,0:T(8,128)(2,1)S(1)} %scatter_add.12), channel_id=1, source_target_pairs={{0,4},{1,5},{4,8},{5,9},{8,12},{9,13},{12,14},{13,15},{14,10},{15,... | collective-permute-start | bytes 393224 | tf_op jit(solution)/shard_map/ppermute | solution.py:484
  61.5 1.4 %collective-permute-start.33 = (bf16[64,8,128]{2,1,0:T(8,128)(2,1)S(1)}, bf16[64,8,128]{2,1,0:T(8,128)(2,1)S(1)}, u32[]{:S(2)}, u32[]{:S(2)}) collective-permute-start(bf16[64,8,128]{2,1,0:T(8,128)(2,1)S(1)} %get-tuple-element.62), channel_id=1, source_target_pairs={{0,1},{1,0},{2,3},{3,2},{4,5},{5,4},{6,7},{7,6},{8,9},{9,8},{10,11... | collective-permute-start | bytes 393224 | tf_op jit(solution)/shard_map/ppermute | solution.py:577

commit v27 on v26

--- a/solution.py
+++ b/solution.py
@@ -275,7 +275,7 @@
         units = ((sums(part) - average) * inverse).reshape(16 * rows, tokens)
         for t in tiles:
             unit_scratch[t, part, :] = units[:, t * LANES : (t + 1) * LANES]
-    for chunk in chunks(rows, tokens, 256):
+    for chunk in chunks(rows, tokens, 512):
         part = span(chunk, tokens)
         units = lanes([unit_scratch[t, pl.ds(r, channels, stride=rows), :] for r in chunk for t in tiles])
         normed = affine(units, gain, bias, tokens)

time: 64.3 us -> 64.3 us (level)
  no operation moved by 1% of the time
where the time goes in v27:
time: 64.3 us; the launch traced here: 64.1 us
  starting transfers between devices  32.7 us (51%)
  waiting for transfers between devices  22.2 us (35%)
  Pallas kernels  8.08 us (13%)
  other arithmetic  0.8 us (1%)
    ppermute x28, starting transfers between devices, along(): return lax.ppermute(array, 'row', pairs)  31.4 us
    ppermute x28, waiting for transfers between devices, along(): return lax.ppermute(array, 'row', pairs)  18.9 us
    ppermute x2, waiting for transfers between devices, on_device(): lax.ppermute(send, 'row', swap).reshape(half * rows, tokens)  2.59 us
    pallas_call x1, Pallas kernels, on_device(): pl.pallas_call(right_kernel, out_shape=(half_shape, half_shape, flat_shap...  1.7 us
    pallas_call x1, Pallas kernels, on_device(): pl.pallas_call(functools.partial(step_kernel, half if by_core else per_gr...  1.38 us
    pallas_call x2, Pallas kernels, on_device(): pl.pallas_call(functools.partial(scatter_start, piece * size, hops[0], ch...  1.33 us
  transfers between devices with their start and end apart: 34, of which 21 were waited for; matrix products, arithmetic and copies ran while one was open for 1% of the time, Pallas kernels for 4%

profile of v27, /device:TPU:0, one launch (start us, length us, event | category | flops | bytes accessed | tf_op | source)
XLA Modules:
  0.0 64.1 jit_solution(17813801890642306271)
XLA Ops:
  0.0 1.7 %project_right.1 = (bf16[512,128]{1,0:T(8,128)(2,1)S(1)}, bf16[512,128]{1,0:T(8,128)(2,1)S(1)}, bf16[128,1024]{1,0:T(8,128)(2,1)S(1)}, bf16[128,1024]{1,0:T(8,12...) custom-call(s32[1]{0:T(128)} %bitcast.core_ref.refs_0_, ...), custom_call_target="tpu_custom_call" | custom-call | tf_op jit(solution)/shard_map/project_right/pallas_call | solution.py:437
  1.7 3.0 %collective-permute-start.4 = (bf16[512,128]{1,0:T(8,128)(2,1)S(1)}, bf16[512,128]{1,0:T(8,128)(2,1)S(1)}, u32[]{:S(2)}, u32[]{:S(2)}) collective-permute-start(bf16[512,128]{1,0:T(8,128)(2,1)S(1)} %get-tuple-element.42), channel_id=1, source_target_pairs={{0,2},{1,3},{4,0},{5,1},{8,4},{9,5},{12,8},{13,9},{14,12},{15,13},... | collective-permute-start | bytes 393224 | tf_op jit(solution)/shard_map/ppermute | solution.py:484
  4.7 0.1 collective-permute-start.2
  4.8 0.4 project_left.1
  5.3 0.6 collective-permute-start
  6.0 0.3 fusion.1.order_ref
  6.3 0.1 fusion.2.order_ref
  6.4 2.0 %collective-permute-start.5 = (bf16[512,128]{1,0:T(8,128)(2,1)S(1)}, bf16[512,128]{1,0:T(8,128)(2,1)S(1)}, u32[]{:S(2)}, u32[]{:S(2)}) collective-permute-start(bf16[512,128]{1,0:T(8,128)(2,1)S(1)} %collective-permute-done.1), channel_id=1, source_target_pairs={{0,2},{1,3},{4,0},{5,1},{8,4},{9,5},{12,8},{13,9},{14,12},{15,13},... | collective-permute-start | bytes 393224 | tf_op jit(solution)/shard_map/ppermute | solution.py:484
  8.4 0.1 collective-permute-start.3
  8.5 1.2 %collective-permute-done.2 = bf16[512,128]{1,0:T(8,128)(2,1)S(1)} collective-permute-done((bf16[512,128]{1,0:T(8,128)(2,1)S(1)}, bf16[512,128]{1,0:T(8,128)(2,1)S(1)}, u32[]{:S(2)}, u32[]{:S(2)}) %collective-permute-start.2) | collective-permute-done | bytes 131104 | tf_op jit(solution)/shard_map/ppermute | solution.py:484
  9.7 0.8 %collective-permute-start.6 = (bf16[512,128]{1,0:T(8,128)(2,1)S(1)}, bf16[512,128]{1,0:T(8,128)(2,1)S(1)}, u32[]{:S(2)}, u32[]{:S(2)}) collective-permute-start(bf16[512,128]{1,0:T(8,128)(2,1)S(1)} %collective-permute-done.2), channel_id=1, source_target_pairs={{0,4},{1,5},{4,8},{5,9},{8,12},{9,13},{12,14},{13,15},{14,10},{15,... | collective-permute-start | bytes 393224 | tf_op jit(solution)/shard_map/ppermute | solution.py:484
  10.5 1.8 %collective-permute-done.5 = bf16[512,128]{1,0:T(8,128)(2,1)S(1)} collective-permute-done((bf16[512,128]{1,0:T(8,128)(2,1)S(1)}, bf16[512,128]{1,0:T(8,128)(2,1)S(1)}, u32[]{:S(2)}, u32[]{:S(2)}) %collective-permute-start.5) | collective-permute-done | bytes 131104 | tf_op jit(solution)/shard_map/ppermute | solution.py:484
  12.3 1.7 %collective-permute-start.9 = (bf16[512,128]{1,0:T(8,128)(2,1)S(1)}, bf16[512,128]{1,0:T(8,128)(2,1)S(1)}, u32[]{:S(2)}, u32[]{:S(2)}) collective-permute-start(bf16[512,128]{1,0:T(8,128)(2,1)S(1)} %collective-permute-done.5), channel_id=1, source_target_pairs={{0,2},{1,3},{4,0},{5,1},{8,4},{9,5},{12,8},{13,9},{14,12},{15,13},... | collective-permute-start | bytes 393224 | tf_op jit(solution)/shard_map/ppermute | solution.py:484
  14.0 1.6 %collective-permute-start.8 = (bf16[512,128]{1,0:T(8,128)(2,1)S(1)}, bf16[512,128]{1,0:T(8,128)(2,1)S(1)}, u32[]{:S(2)}, u32[]{:S(2)}) collective-permute-start(bf16[512,128]{1,0:T(8,128)(2,1)S(1)} %collective-permute-done.4), channel_id=1, source_target_pairs={{0,2},{1,3},{4,0},{5,1},{8,4},{9,5},{12,8},{13,9},{14,12},{15,13},... | collective-permute-start | bytes 393224 | tf_op jit(solution)/shard_map/ppermute | solution.py:484
  15.6 0.4 collective-permute-start.7
  16.0 0.4 collective-permute-done.6
  16.5 0.4 collective-permute-start.10
  16.9 1.8 %collective-permute-done.9 = bf16[512,128]{1,0:T(8,128)(2,1)S(1)} collective-permute-done((bf16[512,128]{1,0:T(8,128)(2,1)S(1)}, bf16[512,128]{1,0:T(8,128)(2,1)S(1)}, u32[]{:S(2)}, u32[]{:S(2)}) %collective-permute-start.9) | collective-permute-done | bytes 131104 | tf_op jit(solution)/shard_map/ppermute | solution.py:484
  18.7 1.5 %collective-permute-start.13 = (bf16[512,128]{1,0:T(8,128)(2,1)S(1)}, bf16[512,128]{1,0:T(8,128)(2,1)S(1)}, u32[]{:S(2)}, u32[]{:S(2)}) collective-permute-start(bf16[512,128]{1,0:T(8,128)(2,1)S(1)} %collective-permute-done.9), channel_id=1, source_target_pairs={{0,2},{1,3},{4,0},{5,1},{8,4},{9,5},{12,8},{13,9},{14,12},{15,13},... | collective-permute-start | bytes 393224 | tf_op jit(solution)/shard_map/ppermute | solution.py:484
  20.2 1.3 %collective-permute-done.8 = bf16[512,128]{1,0:T(8,128)(2,1)S(1)} collective-permute-done((bf16[512,128]{1,0:T(8,128)(2,1)S(1)}, bf16[512,128]{1,0:T(8,128)(2,1)S(1)}, u32[]{:S(2)}, u32[]{:S(2)}) %collective-permute-start.8) | collective-permute-done | bytes 131104 | tf_op jit(solution)/shard_map/ppermute | solution.py:484
  21.5 1.5 %collective-permute-start.12 = (bf16[512,128]{1,0:T(8,128)(2,1)S(1)}, bf16[512,128]{1,0:T(8,128)(2,1)S(1)}, u32[]{:S(2)}, u32[]{:S(2)}) collective-permute-start(bf16[512,128]{1,0:T(8,128)(2,1)S(1)} %collective-permute-done.8), channel_id=1, source_target_pairs={{0,2},{1,3},{4,0},{5,1},{8,4},{9,5},{12,8},{13,9},{14,12},{15,13},... | collective-permute-start | bytes 393224 | tf_op jit(solution)/shard_map/ppermute | solution.py:484
  23.0 0.6 collective-permute-start.11
  23.5 1.7 %collective-permute-start.14 = (bf16[512,128]{1,0:T(8,128)(2,1)S(1)}, bf16[512,128]{1,0:T(8,128)(2,1)S(1)}, u32[]{:S(2)}, u32[]{:S(2)}) collective-permute-start(bf16[512,128]{1,0:T(8,128)(2,1)S(1)} %collective-permute-done.10), channel_id=1, source_target_pairs={{0,4},{1,5},{4,8},{5,9},{8,12},{9,13},{12,14},{13,15},{14,10},{15,... | collective-permute-start | bytes 393224 | tf_op jit(solution)/shard_map/ppermute | solution.py:484
  25.2 0.6 collective-permute-start.15
  25.8 1.3 %collective-permute-done.12 = bf16[512,128]{1,0:T(8,128)(2,1)S(1)} collective-permute-done((bf16[512,128]{1,0:T(8,128)(2,1)S(1)}, bf16[512,128]{1,0:T(8,128)(2,1)S(1)}, u32[]{:S(2)}, u32[]{:S(2)}) %collective-permute-start.12) | collective-permute-done | bytes 131104 | tf_op jit(solution)/shard_map/ppermute | solution.py:484
  27.1 0.8 %collective-permute-done.11 = bf16[512,128]{1,0:T(8,128)(2,1)S(1)} collective-permute-done((bf16[512,128]{1,0:T(8,128)(2,1)S(1)}, bf16[512,128]{1,0:T(8,128)(2,1)S(1)}, u32[]{:S(2)}, u32[]{:S(2)}) %collective-permute-start.11) | collective-permute-done | bytes 131104 | tf_op jit(solution)/shard_map/ppermute | solution.py:484
  27.9 1.2 %mix_early.1.early_ref = bf16[64,16,128]{2,1,0:T(8,128)(2,1)S(1)} custom-call(bf16[112,128]{1,0:T(8,128)(2,1)S(1)} %fusion.1.order_ref, bf16[64,8,128]{2,1,0:T(8,128)(2,1)S(1)} %bitcast.39, bf16[64,8,128]{2,1,0:T(8,128)(2,1)S(1)} %bitcast.41, bf16[64,8,128]{2,1,0:T(8,128)(2,1)S(1)} %bitcast.45, bf16[64,8,128]{2,1,0:T(8,128)(2,1)S(1)} %bitcast.48, ...), custom_call_target="tpu_custom_call" | custom-call | flops 1000000000 | bytes 4194304 | tf_op jit(solution)/shard_map/mix_early/pallas_call | solution.py:505
  29.1 0.2 collective-permute-done.14
  29.3 0.9 %collective-permute-done.15 = bf16[512,128]{1,0:T(8,128)(2,1)S(1)} collective-permute-done((bf16[512,128]{1,0:T(8,128)(2,1)S(1)}, bf16[512,128]{1,0:T(8,128)(2,1)S(1)}, u32[]{:S(2)}, u32[]{:S(2)}) %collective-permute-start.15) | collective-permute-done | bytes 131104 | tf_op jit(solution)/shard_map/ppermute | solution.py:484
  30.2 0.4 mix_late.1
  30.8 1.3 %collective-permute-done.16 = bf16[64,8,128]{2,1,0:T(8,128)(2,1)S(1)} collective-permute-done((bf16[64,8,128]{2,1,0:T(8,128)(2,1)S(1)}, bf16[64,8,128]{2,1,0:T(8,128)(2,1)S(1)}, u32[]{:S(2)}, u32[]{:S(2)}) %collective-permute-start.16) | collective-permute-done | bytes 131104 | tf_op jit(solution)/shard_map/ppermute | solution.py:524
  32.1 1.4 %finish_project.1 = (bf16[512,128]{1,0:T(8,128)(2,1)S(1)}, bf16[512,128]{1,0:T(8,128)(2,1)S(1)}, bf16[512,128]{1,0:T(8,128)(2,1)S(1)}, bf16[512,128]{1,0:T(8,128...) custom-call(s32[1]{0:T(128)} %bitcast.core_ref.refs_0_, bf16[512,128]{1,0:T(8,128)(2,1)S(1)} %bitcast.35, ...), custom_call_target="tpu_custom_call" | custom-call | tf_op jit(solution)/shard_map/finish_project/pallas_call | solution.py:527
  33.5 0.2 collective-permute-start.17
  33.7 0.4 collective-permute-start.18
  34.0 0.3 fusion.order_ref
  34.4 0.5 collective-permute-done.17
  34.9 0.2 collective-permute-done.18
  35.1 0.7 %scatter_start.3 = (f32[32,128,128]{2,1,0:T(8,128)S(1)}, bf16[32,16,128]{2,1,0:T(8,128)(2,1)S(1)}, bf16[32,16,128]{2,1,0:T(8,128)(2,1)S(1)}) custom-call(bf16[128,128]{1,0:T(8,128)(2,1)S(1)} %fusion.order_ref, bf16[64,8,128]{2,1,0:T(8,128)(2,1)S(1)} %bitcast.27, bf16[64,8,128]{2,1,0:T(8,128)(2,1)S(1)} %bitcast.31, bf16[64,8,128]{2,1,0:T(8,128)(2,1)S(1)} %bitcast.29, ...), custom_call_target="tpu_custom_call" | custom-call | tf_op jit(solution)/shard_map/scatter_start/pallas_call | solution.py:548
  35.7 0.8 %collective-permute-start.29 = (bf16[32,16,128]{2,1,0:T(8,128)(2,1)S(1)}, bf16[32,16,128]{2,1,0:T(8,128)(2,1)S(1)}, u32[]{:S(2)}, u32[]{:S(2)}) collective-permute-start(bf16[32,16,128]{2,1,0:T(8,128)(2,1)S(1)} %get-tuple-element.60), channel_id=1, source_target_pairs={{0,2},{1,3},{4,0},{5,1},{8,4},{9,5},{12,8},{13,9},{14,12},{15,13},... | collective-permute-start | bytes 393224 | tf_op jit(solution)/shard_map/ppermute | solution.py:484
  36.5 0.7 %scatter_start.2 = (f32[32,128,128]{2,1,0:T(8,128)S(1)}, bf16[32,16,128]{2,1,0:T(8,128)(2,1)S(1)}, bf16[32,16,128]{2,1,0:T(8,128)(2,1)S(1)}) custom-call(bf16[128,128]{1,0:T(8,128)(2,1)S(1)} %fusion.order_ref, bf16[64,8,128]{2,1,0:T(8,128)(2,1)S(1)} %bitcast.28, bf16[64,8,128]{2,1,0:T(8,128)(2,1)S(1)} %bitcast.32, bf16[64,8,128]{2,1,0:T(8,128)(2,1)S(1)} %bitcast.30, ...), custom_call_target="tpu_custom_call" | custom-call | tf_op jit(solution)/shard_map/scatter_start/pallas_call | solution.py:548
  37.1 1.4 %collective-permute-start.19 = (bf16[32,16,128]{2,1,0:T(8,128)(2,1)S(1)}, bf16[32,16,128]{2,1,0:T(8,128)(2,1)S(1)}, u32[]{:S(2)}, u32[]{:S(2)}) collective-permute-start(bf16[32,16,128]{2,1,0:T(8,128)(2,1)S(1)} %get-tuple-element.56), channel_id=1, source_target_pairs={{0,4},{1,5},{4,8},{5,9},{8,12},{9,13},{12,14},{13,15},{14,10},{15,... | collective-permute-start | bytes 393224 | tf_op jit(solution)/shard_map/ppermute | solution.py:484
  38.5 1.4 %collective-permute-start.26 = (bf16[32,16,128]{2,1,0:T(8,128)(2,1)S(1)}, bf16[32,16,128]{2,1,0:T(8,128)(2,1)S(1)}, u32[]{:S(2)}, u32[]{:S(2)}) collective-permute-start(bf16[32,16,128]{2,1,0:T(8,128)(2,1)S(1)} %get-tuple-element.59), channel_id=1, source_target_pairs={{0,4},{1,5},{4,8},{5,9},{8,12},{9,13},{12,14},{13,15},{14,10},{15,... | collective-permute-start | bytes 393224 | tf_op jit(solution)/shard_map/ppermute | solution.py:484
  39.9 0.6 collective-permute-start.23
  40.5 1.0 %collective-permute-done.29.got_ref = bf16[32,16,128]{2,1,0:T(8,128)(2,1)S(1)} collective-permute-done((bf16[32,16,128]{2,1,0:T(8,128)(2,1)S(1)}, bf16[32,16,128]{2,1,0:T(8,128)(2,1)S(1)}, u32[]{:S(2)}, u32[]{:S(2)}) %collective-permute-start.29) | collective-permute-done | bytes 131104 | tf_op jit(solution)/shard_map/ppermute | solution.py:484
  41.5 0.8 %collective-permute-start.30 = (bf16[32,16,128]{2,1,0:T(8,128)(2,1)S(1)}, bf16[32,16,128]{2,1,0:T(8,128)(2,1)S(1)}, u32[]{:S(2)}, u32[]{:S(2)}) collective-permute-start(bf16[32,16,128]{2,1,0:T(8,128)(2,1)S(1)} %scatter_add.17), channel_id=1, source_target_pairs={{0,2},{1,3},{4,0},{5,1},{8,4},{9,5},{12,8},{13,9},{14,12},{15,13},... | collective-permute-start | bytes 393224 | tf_op jit(solution)/shard_map/ppermute | solution.py:484
  42.3 1.3 %collective-permute-done.19.got_ref = bf16[32,16,128]{2,1,0:T(8,128)(2,1)S(1)} collective-permute-done((bf16[32,16,128]{2,1,0:T(8,128)(2,1)S(1)}, bf16[32,16,128]{2,1,0:T(8,128)(2,1)S(1)}, u32[]{:S(2)}, u32[]{:S(2)}) %collective-permute-start.19) | collective-permute-done | bytes 131104 | tf_op jit(solution)/shard_map/ppermute | solution.py:484
  43.6 1.4 %collective-permute-start.20 = (bf16[32,16,128]{2,1,0:T(8,128)(2,1)S(1)}, bf16[32,16,128]{2,1,0:T(8,128)(2,1)S(1)}, u32[]{:S(2)}, u32[]{:S(2)}) collective-permute-start(bf16[32,16,128]{2,1,0:T(8,128)(2,1)S(1)} %scatter_add.10), channel_id=1, source_target_pairs={{0,4},{1,5},{4,8},{5,9},{8,12},{9,13},{12,14},{13,15},{14,10},{15,... | collective-permute-start | bytes 393224 | tf_op jit(solution)/shard_map/ppermute | solution.py:484
  45.0 1.4 %collective-permute-done.26.got_ref = bf16[32,16,128]{2,1,0:T(8,128)(2,1)S(1)} collective-permute-done((bf16[32,16,128]{2,1,0:T(8,128)(2,1)S(1)}, bf16[32,16,128]{2,1,0:T(8,128)(2,1)S(1)}, u32[]{:S(2)}, u32[]{:S(2)}) %collective-permute-start.26) | collective-permute-done | bytes 131104 | tf_op jit(solution)/shard_map/ppermute | solution.py:484
  46.4 1.4 %collective-permute-start.27 = (bf16[32,16,128]{2,1,0:T(8,128)(2,1)S(1)}, bf16[32,16,128]{2,1,0:T(8,128)(2,1)S(1)}, u32[]{:S(2)}, u32[]{:S(2)}) collective-permute-start(bf16[32,16,128]{2,1,0:T(8,128)(2,1)S(1)} %scatter_add.15), channel_id=1, source_target_pairs={{0,4},{1,5},{4,8},{5,9},{8,12},{9,13},{12,14},{13,15},{14,10},{15,... | collective-permute-start | bytes 393224 | tf_op jit(solution)/shard_map/ppermute | solution.py:484
  47.8 0.8 %collective-permute-start.24 = (bf16[32,16,128]{2,1,0:T(8,128)(2,1)S(1)}, bf16[32,16,128]{2,1,0:T(8,128)(2,1)S(1)}, u32[]{:S(2)}, u32[]{:S(2)}) collective-permute-start(bf16[32,16,128]{2,1,0:T(8,128)(2,1)S(1)} %scatter_add.13), channel_id=1, source_target_pairs={{0,2},{1,3},{4,0},{5,1},{8,4},{9,5},{12,8},{13,9},{14,12},{15,13},... | collective-permute-start | bytes 393224 | tf_op jit(solution)/shard_map/ppermute | solution.py:484
  48.6 1.6 %collective-permute-start.31 = (bf16[32,16,128]{2,1,0:T(8,128)(2,1)S(1)}, bf16[32,16,128]{2,1,0:T(8,128)(2,1)S(1)}, u32[]{:S(2)}, u32[]{:S(2)}) collective-permute-start(bf16[32,16,128]{2,1,0:T(8,128)(2,1)S(1)} %scatter_add.18), channel_id=1, source_target_pairs={{0,2},{1,3},{4,0},{5,1},{8,4},{9,5},{12,8},{13,9},{14,12},{15,13},... | collective-permute-start | bytes 393224 | tf_op jit(solution)/shard_map/ppermute | solution.py:484
  50.2 1.0 %collective-permute-start.21 = (bf16[32,16,128]{2,1,0:T(8,128)(2,1)S(1)}, bf16[32,16,128]{2,1,0:T(8,128)(2,1)S(1)}, u32[]{:S(2)}, u32[]{:S(2)}) collective-permute-start(bf16[32,16,128]{2,1,0:T(8,128)(2,1)S(1)} %scatter_add.11), channel_id=1, source_target_pairs={{0,4},{1,5},{4,8},{5,9},{8,12},{9,13},{12,14},{13,15},{14,10},{15,... | collective-permute-start | bytes 393224 | tf_op jit(solution)/shard_map/ppermute | solution.py:484
  51.3 1.2 %collective-permute-done.27.got_ref = bf16[32,16,128]{2,1,0:T(8,128)(2,1)S(1)} collective-permute-done((bf16[32,16,128]{2,1,0:T(8,128)(2,1)S(1)}, bf16[32,16,128]{2,1,0:T(8,128)(2,1)S(1)}, u32[]{:S(2)}, u32[]{:S(2)}) %collective-permute-start.27) | collective-permute-done | bytes 131104 | tf_op jit(solution)/shard_map/ppermute | solution.py:484
  52.5 1.7 %collective-permute-start.28 = (bf16[32,16,128]{2,1,0:T(8,128)(2,1)S(1)}, bf16[32,16,128]{2,1,0:T(8,128)(2,1)S(1)}, u32[]{:S(2)}, u32[]{:S(2)}) collective-permute-start(bf16[32,16,128]{2,1,0:T(8,128)(2,1)S(1)} %scatter_add.16), channel_id=1, source_target_pairs={{0,4},{1,5},{4,8},{5,9},{8,12},{9,13},{12,14},{13,15},{14,10},{15,... | collective-permute-start | bytes 393224 | tf_op jit(solution)/shard_map/ppermute | solution.py:484
  54.3 0.4 collective-permute-start.25
  54.7 1.6 %collective-permute-start.32 = (bf16[32,16,128]{2,1,0:T(8,128)(2,1)S(1)}, bf16[32,16,128]{2,1,0:T(8,128)(2,1)S(1)}, u32[]{:S(2)}, u32[]{:S(2)}) collective-permute-start(bf16[32,16,128]{2,1,0:T(8,128)(2,1)S(1)} %scatter_add.19), channel_id=1, source_target_pairs={{0,2},{1,3},{4,0},{5,1},{8,4},{9,5},{12,8},{13,9},{14,12},{15,13},... | collective-permute-start | bytes 393224 | tf_op jit(solution)/shard_map/ppermute | solution.py:484
  56.4 0.7 %collective-permute-start.22 = (bf16[32,16,128]{2,1,0:T(8,128)(2,1)S(1)}, bf16[32,16,128]{2,1,0:T(8,128)(2,1)S(1)}, u32[]{:S(2)}, u32[]{:S(2)}) collective-permute-start(bf16[32,16,128]{2,1,0:T(8,128)(2,1)S(1)} %scatter_add.12), channel_id=1, source_target_pairs={{0,4},{1,5},{4,8},{5,9},{8,12},{9,13},{12,14},{13,15},{14,10},{15,... | collective-permute-start | bytes 393224 | tf_op jit(solution)/shard_map/ppermute | solution.py:484
  57.0 1.5 %collective-permute-done.28.refs_4_ = bf16[32,16,128]{2,1,0:T(8,128)(2,1)S(1)} collective-permute-done((bf16[32,16,128]{2,1,0:T(8,128)(2,1)S(1)}, bf16[32,16,128]{2,1,0:T(8,128)(2,1)S(1)}, u32[]{:S(2)}, u32[]{:S(2)}) %collective-permute-start.28) | collective-permute-done | bytes 131104 | tf_op jit(solution)/shard_map/ppermute | solution.py:484
  58.5 0.8 %collective-permute-done.25.refs_2_ = bf16[32,16,128]{2,1,0:T(8,128)(2,1)S(1)} collective-permute-done((bf16[32,16,128]{2,1,0:T(8,128)(2,1)S(1)}, bf16[32,16,128]{2,1,0:T(8,128)(2,1)S(1)}, u32[]{:S(2)}, u32[]{:S(2)}) %collective-permute-start.25) | collective-permute-done | bytes 131104 | tf_op jit(solution)/shard_map/ppermute | solution.py:484
  59.3 1.4 %collective-permute-done.32.refs_5_ = bf16[32,16,128]{2,1,0:T(8,128)(2,1)S(1)} collective-permute-done((bf16[32,16,128]{2,1,0:T(8,128)(2,1)S(1)}, bf16[32,16,128]{2,1,0:T(8,128)(2,1)S(1)}, u32[]{:S(2)}, u32[]{:S(2)}) %collective-permute-start.32) | collective-permute-done | bytes 131104 | tf_op jit(solution)/shard_map/ppermute | solution.py:484
  60.7 0.6 collective-permute-done.22.refs_1_
  61.4 0.1 scatter_end.1
  61.5 1.3 %collective-permute-done.33 = bf16[64,8,128]{2,1,0:T(8,128)(2,1)S(1)} collective-permute-done((bf16[64,8,128]{2,1,0:T(8,128)(2,1)S(1)}, bf16[64,8,128]{2,1,0:T(8,128)(2,1)S(1)}, u32[]{:S(2)}, u32[]{:S(2)}) %collective-permute-start.33) | collective-permute-done | bytes 131104 | tf_op jit(solution)/shard_map/ppermute | solution.py:577
  62.9 1.3 %finish.1 = bf16[8,128,128]{2,1,0:T(8,128)(2,1)} custom-call(s32[1]{0:T(128)} %bitcast.core_ref.refs_0_, bf16[512,128]{1,0:T(8,128)(2,1)S(1)} %bitcast.37, bf16[512,128]{1,0:T(8,128)(2,1)S(1)} %bitcast.38, bf16[128,1024]{1,0:T(8,128)(2,1)S(1)} %get-tuple-element.63.refs_3_, bf16[128,1024]{1,0:T(8,128)(2,1)S(1)} %get-tuple-element.64.refs_4_, ...), custom_call_target="tpu_custom_call" | custom-call | tf_op jit(solution)/shard_map/finish/pallas_call | solution.py:580
  (45 shorter events, 0.5 us)
Async XLA Ops:
  1.7 12.3 %collective-permute-start.4 = (bf16[512,128]{1,0:T(8,128)(2,1)S(1)}, bf16[512,128]{1,0:T(8,128)(2,1)S(1)}, u32[]{:S(2)}, u32[]{:S(2)}) collective-permute-start(bf16[512,128]{1,0:T(8,128)(2,1)S(1)} %get-tuple-element.42), channel_id=1, source_target_pairs={{0,2},{1,3},{4,0},{5,1},{8,4},{9,5},{12,8},{13,9},{14,12},{15,13},... | collective-permute-start | bytes 393224 | tf_op jit(solution)/shard_map/ppermute | solution.py:484
  4.7 5.0 %collective-permute-start.2 = (bf16[512,128]{1,0:T(8,128)(2,1)S(1)}, bf16[512,128]{1,0:T(8,128)(2,1)S(1)}, u32[]{:S(2)}, u32[]{:S(2)}) collective-permute-start(bf16[512,128]{1,0:T(8,128)(2,1)S(1)} %get-tuple-element.42), channel_id=1, source_target_pairs={{0,4},{1,5},{4,8},{5,9},{8,12},{9,13},{12,14},{13,15},{14,10},{15,... | collective-permute-start | bytes 393224 | tf_op jit(solution)/shard_map/ppermute | solution.py:484
  4.8 1.6 %collective-permute-start.1 = (bf16[512,128]{1,0:T(8,128)(2,1)S(1)}, bf16[512,128]{1,0:T(8,128)(2,1)S(1)}, u32[]{:S(2)}, u32[]{:S(2)}) collective-permute-start(bf16[512,128]{1,0:T(8,128)(2,1)S(1)} %get-tuple-element.43), channel_id=1, source_target_pairs={{0,1},{1,0},{2,3},{3,2},{4,5},{5,4},{6,7},{7,6},{8,9},{9,8},{10,11... | collective-permute-start | bytes 393224 | tf_op jit(solution)/shard_map/ppermute | solution.py:493
  5.3 20.5 %collective-permute-start = (bf16[512,128]{1,0:T(8,128)(2,1)S(1)}, bf16[512,128]{1,0:T(8,128)(2,1)S(1)}, u32[]{:S(2)}, u32[]{:S(2)}) collective-permute-start(bf16[512,128]{1,0:T(8,128)(2,1)S(1)} %get-tuple-element.41), channel_id=1, source_target_pairs={{0,1},{1,0},{2,3},{3,2},{4,5},{5,4},{6,7},{7,6},{8,9},{9,8},{10,11... | collective-permute-start | bytes 393224 | tf_op jit(solution)/shard_map/ppermute | solution.py:494
  6.4 5.9 %collective-permute-start.5 = (bf16[512,128]{1,0:T(8,128)(2,1)S(1)}, bf16[512,128]{1,0:T(8,128)(2,1)S(1)}, u32[]{:S(2)}, u32[]{:S(2)}) collective-permute-start(bf16[512,128]{1,0:T(8,128)(2,1)S(1)} %collective-permute-done.1), channel_id=1, source_target_pairs={{0,2},{1,3},{4,0},{5,1},{8,4},{9,5},{12,8},{13,9},{14,12},{15,13},... | collective-permute-start | bytes 393224 | tf_op jit(solution)/shard_map/ppermute | solution.py:484
  8.4 7.2 %collective-permute-start.3 = (bf16[512,128]{1,0:T(8,128)(2,1)S(1)}, bf16[512,128]{1,0:T(8,128)(2,1)S(1)}, u32[]{:S(2)}, u32[]{:S(2)}) collective-permute-start(bf16[512,128]{1,0:T(8,128)(2,1)S(1)} %collective-permute-done.1), channel_id=1, source_target_pairs={{0,4},{1,5},{4,8},{5,9},{8,12},{9,13},{12,14},{13,15},{14,10},{15,... | collective-permute-start | bytes 393224 | tf_op jit(solution)/shard_map/ppermute | solution.py:484
  9.7 6.8 %collective-permute-start.6 = (bf16[512,128]{1,0:T(8,128)(2,1)S(1)}, bf16[512,128]{1,0:T(8,128)(2,1)S(1)}, u32[]{:S(2)}, u32[]{:S(2)}) collective-permute-start(bf16[512,128]{1,0:T(8,128)(2,1)S(1)} %collective-permute-done.2), channel_id=1, source_target_pairs={{0,4},{1,5},{4,8},{5,9},{8,12},{9,13},{12,14},{13,15},{14,10},{15,... | collective-permute-start | bytes 393224 | tf_op jit(solution)/shard_map/ppermute | solution.py:484
  12.3 6.4 %collective-permute-start.9 = (bf16[512,128]{1,0:T(8,128)(2,1)S(1)}, bf16[512,128]{1,0:T(8,128)(2,1)S(1)}, u32[]{:S(2)}, u32[]{:S(2)}) collective-permute-start(bf16[512,128]{1,0:T(8,128)(2,1)S(1)} %collective-permute-done.5), channel_id=1, source_target_pairs={{0,2},{1,3},{4,0},{5,1},{8,4},{9,5},{12,8},{13,9},{14,12},{15,13},... | collective-permute-start | bytes 393224 | tf_op jit(solution)/shard_map/ppermute | solution.py:484
  14.0 7.5 %collective-permute-start.8 = (bf16[512,128]{1,0:T(8,128)(2,1)S(1)}, bf16[512,128]{1,0:T(8,128)(2,1)S(1)}, u32[]{:S(2)}, u32[]{:S(2)}) collective-permute-start(bf16[512,128]{1,0:T(8,128)(2,1)S(1)} %collective-permute-done.4), channel_id=1, source_target_pairs={{0,2},{1,3},{4,0},{5,1},{8,4},{9,5},{12,8},{13,9},{14,12},{15,13},... | collective-permute-start | bytes 393224 | tf_op jit(solution)/shard_map/ppermute | solution.py:484
  15.6 7.4 %collective-permute-start.7 = (bf16[512,128]{1,0:T(8,128)(2,1)S(1)}, bf16[512,128]{1,0:T(8,128)(2,1)S(1)}, u32[]{:S(2)}, u32[]{:S(2)}) collective-permute-start(bf16[512,128]{1,0:T(8,128)(2,1)S(1)} %collective-permute-done.3), channel_id=1, source_target_pairs={{0,4},{1,5},{4,8},{5,9},{8,12},{9,13},{12,14},{13,15},{14,10},{15,... | collective-permute-start | bytes 393224 | tf_op jit(solution)/shard_map/ppermute | solution.py:484
  16.5 7.0 %collective-permute-start.10 = (bf16[512,128]{1,0:T(8,128)(2,1)S(1)}, bf16[512,128]{1,0:T(8,128)(2,1)S(1)}, u32[]{:S(2)}, u32[]{:S(2)}) collective-permute-start(bf16[512,128]{1,0:T(8,128)(2,1)S(1)} %collective-permute-done.6), channel_id=1, source_target_pairs={{0,4},{1,5},{4,8},{5,9},{8,12},{9,13},{12,14},{13,15},{14,10},{15,... | collective-permute-start | bytes 393224 | tf_op jit(solution)/shard_map/ppermute | solution.py:484
  18.7 6.6 %collective-permute-start.13 = (bf16[512,128]{1,0:T(8,128)(2,1)S(1)}, bf16[512,128]{1,0:T(8,128)(2,1)S(1)}, u32[]{:S(2)}, u32[]{:S(2)}) collective-permute-start(bf16[512,128]{1,0:T(8,128)(2,1)S(1)} %collective-permute-done.9), channel_id=1, source_target_pairs={{0,2},{1,3},{4,0},{5,1},{8,4},{9,5},{12,8},{13,9},{14,12},{15,13},... | collective-permute-start | bytes 393224 | tf_op jit(solution)/shard_map/ppermute | solution.py:484
  21.5 5.6 %collective-permute-start.12 = (bf16[512,128]{1,0:T(8,128)(2,1)S(1)}, bf16[512,128]{1,0:T(8,128)(2,1)S(1)}, u32[]{:S(2)}, u32[]{:S(2)}) collective-permute-start(bf16[512,128]{1,0:T(8,128)(2,1)S(1)} %collective-permute-done.8), channel_id=1, source_target_pairs={{0,2},{1,3},{4,0},{5,1},{8,4},{9,5},{12,8},{13,9},{14,12},{15,13},... | collective-permute-start | bytes 393224 | tf_op jit(solution)/shard_map/ppermute | solution.py:484
  23.0 5.0 %collective-permute-start.11 = (bf16[512,128]{1,0:T(8,128)(2,1)S(1)}, bf16[512,128]{1,0:T(8,128)(2,1)S(1)}, u32[]{:S(2)}, u32[]{:S(2)}) collective-permute-start(bf16[512,128]{1,0:T(8,128)(2,1)S(1)} %collective-permute-done.7), channel_id=1, source_target_pairs={{0,4},{1,5},{4,8},{5,9},{8,12},{9,13},{12,14},{13,15},{14,10},{15,... | collective-permute-start | bytes 393224 | tf_op jit(solution)/shard_map/ppermute | solution.py:484
  23.5 5.8 %collective-permute-start.14 = (bf16[512,128]{1,0:T(8,128)(2,1)S(1)}, bf16[512,128]{1,0:T(8,128)(2,1)S(1)}, u32[]{:S(2)}, u32[]{:S(2)}) collective-permute-start(bf16[512,128]{1,0:T(8,128)(2,1)S(1)} %collective-permute-done.10), channel_id=1, source_target_pairs={{0,4},{1,5},{4,8},{5,9},{8,12},{9,13},{12,14},{13,15},{14,10},{15,... | collective-permute-start | bytes 393224 | tf_op jit(solution)/shard_map/ppermute | solution.py:484
  25.2 5.0 %collective-permute-start.15 = (bf16[512,128]{1,0:T(8,128)(2,1)S(1)}, bf16[512,128]{1,0:T(8,128)(2,1)S(1)}, u32[]{:S(2)}, u32[]{:S(2)}) collective-permute-start(bf16[512,128]{1,0:T(8,128)(2,1)S(1)} %collective-permute-done.13), channel_id=1, source_target_pairs={{0,2},{1,3},{4,0},{5,1},{8,4},{9,5},{12,8},{13,9},{14,12},{15,13},... | collective-permute-start | bytes 393224 | tf_op jit(solution)/shard_map/ppermute | solution.py:484
  30.7 1.4 %collective-permute-start.16 = (bf16[64,8,128]{2,1,0:T(8,128)(2,1)S(1)}, bf16[64,8,128]{2,1,0:T(8,128)(2,1)S(1)}, u32[]{:S(2)}, u32[]{:S(2)}) collective-permute-start(bf16[64,8,128]{2,1,0:T(8,128)(2,1)S(1)} %get-tuple-element.45), channel_id=1, source_target_pairs={{0,1},{1,0},{2,3},{3,2},{4,5},{5,4},{6,7},{7,6},{8,9},{9,8},{10,11... | collective-permute-start | bytes 393224 | tf_op jit(solution)/shard_map/ppermute | solution.py:524
  33.5 1.4 %collective-permute-start.17 = (bf16[512,128]{1,0:T(8,128)(2,1)S(1)}, bf16[512,128]{1,0:T(8,128)(2,1)S(1)}, u32[]{:S(2)}, u32[]{:S(2)}) collective-permute-start(bf16[512,128]{1,0:T(8,128)(2,1)S(1)} %get-tuple-element.52), channel_id=1, source_target_pairs={{0,1},{1,0},{2,3},{3,2},{4,5},{5,4},{6,7},{7,6},{8,9},{9,8},{10,11... | collective-permute-start | bytes 393224 | tf_op jit(solution)/shard_map/ppermute | solution.py:539
  33.7 1.4 %collective-permute-start.18 = (bf16[512,128]{1,0:T(8,128)(2,1)S(1)}, bf16[512,128]{1,0:T(8,128)(2,1)S(1)}, u32[]{:S(2)}, u32[]{:S(2)}) collective-permute-start(bf16[512,128]{1,0:T(8,128)(2,1)S(1)} %get-tuple-element.54), channel_id=1, source_target_pairs={{0,1},{1,0},{2,3},{3,2},{4,5},{5,4},{6,7},{7,6},{8,9},{9,8},{10,11... | collective-permute-start | bytes 393224 | tf_op jit(solution)/shard_map/ppermute | solution.py:540
  35.7 5.8 %collective-permute-start.29 = (bf16[32,16,128]{2,1,0:T(8,128)(2,1)S(1)}, bf16[32,16,128]{2,1,0:T(8,128)(2,1)S(1)}, u32[]{:S(2)}, u32[]{:S(2)}) collective-permute-start(bf16[32,16,128]{2,1,0:T(8,128)(2,1)S(1)} %get-tuple-element.60), channel_id=1, source_target_pairs={{0,2},{1,3},{4,0},{5,1},{8,4},{9,5},{12,8},{13,9},{14,12},{15,13},... | collective-permute-start | bytes 393224 | tf_op jit(solution)/shard_map/ppermute | solution.py:484
  37.1 6.4 %collective-permute-start.19 = (bf16[32,16,128]{2,1,0:T(8,128)(2,1)S(1)}, bf16[32,16,128]{2,1,0:T(8,128)(2,1)S(1)}, u32[]{:S(2)}, u32[]{:S(2)}) collective-permute-start(bf16[32,16,128]{2,1,0:T(8,128)(2,1)S(1)} %get-tuple-element.56), channel_id=1, source_target_pairs={{0,4},{1,5},{4,8},{5,9},{8,12},{9,13},{12,14},{13,15},{14,10},{15,... | collective-permute-start | bytes 393224 | tf_op jit(solution)/shard_map/ppermute | solution.py:484
  38.5 7.8 %collective-permute-start.26 = (bf16[32,16,128]{2,1,0:T(8,128)(2,1)S(1)}, bf16[32,16,128]{2,1,0:T(8,128)(2,1)S(1)}, u32[]{:S(2)}, u32[]{:S(2)}) collective-permute-start(bf16[32,16,128]{2,1,0:T(8,128)(2,1)S(1)} %get-tuple-element.59), channel_id=1, source_target_pairs={{0,4},{1,5},{4,8},{5,9},{8,12},{9,13},{12,14},{13,15},{14,10},{15,... | collective-permute-start | bytes 393224 | tf_op jit(solution)/shard_map/ppermute | solution.py:484
  39.9 7.8 %collective-permute-start.23 = (bf16[32,16,128]{2,1,0:T(8,128)(2,1)S(1)}, bf16[32,16,128]{2,1,0:T(8,128)(2,1)S(1)}, u32[]{:S(2)}, u32[]{:S(2)}) collective-permute-start(bf16[32,16,128]{2,1,0:T(8,128)(2,1)S(1)} %get-tuple-element.57), channel_id=1, source_target_pairs={{0,2},{1,3},{4,0},{5,1},{8,4},{9,5},{12,8},{13,9},{14,12},{15,13},... | collective-permute-start | bytes 393224 | tf_op jit(solution)/shard_map/ppermute | solution.py:484
  41.5 7.0 %collective-permute-start.30 = (bf16[32,16,128]{2,1,0:T(8,128)(2,1)S(1)}, bf16[32,16,128]{2,1,0:T(8,128)(2,1)S(1)}, u32[]{:S(2)}, u32[]{:S(2)}) collective-permute-start(bf16[32,16,128]{2,1,0:T(8,128)(2,1)S(1)} %scatter_add.17), channel_id=1, source_target_pairs={{0,2},{1,3},{4,0},{5,1},{8,4},{9,5},{12,8},{13,9},{14,12},{15,13},... | collective-permute-start | bytes 393224 | tf_op jit(solution)/shard_map/ppermute | solution.py:484
  43.6 6.6 %collective-permute-start.20 = (bf16[32,16,128]{2,1,0:T(8,128)(2,1)S(1)}, bf16[32,16,128]{2,1,0:T(8,128)(2,1)S(1)}, u32[]{:S(2)}, u32[]{:S(2)}) collective-permute-start(bf16[32,16,128]{2,1,0:T(8,128)(2,1)S(1)} %scatter_add.10), channel_id=1, source_target_pairs={{0,4},{1,5},{4,8},{5,9},{8,12},{9,13},{12,14},{13,15},{14,10},{15,... | collective-permute-start | bytes 393224 | tf_op jit(solution)/shard_map/ppermute | solution.py:484
  46.4 6.1 %collective-permute-start.27 = (bf16[32,16,128]{2,1,0:T(8,128)(2,1)S(1)}, bf16[32,16,128]{2,1,0:T(8,128)(2,1)S(1)}, u32[]{:S(2)}, u32[]{:S(2)}) collective-permute-start(bf16[32,16,128]{2,1,0:T(8,128)(2,1)S(1)} %scatter_add.15), channel_id=1, source_target_pairs={{0,4},{1,5},{4,8},{5,9},{8,12},{9,13},{12,14},{13,15},{14,10},{15,... | collective-permute-start | bytes 393224 | tf_op jit(solution)/shard_map/ppermute | solution.py:484
  47.8 6.5 %collective-permute-start.24 = (bf16[32,16,128]{2,1,0:T(8,128)(2,1)S(1)}, bf16[32,16,128]{2,1,0:T(8,128)(2,1)S(1)}, u32[]{:S(2)}, u32[]{:S(2)}) collective-permute-start(bf16[32,16,128]{2,1,0:T(8,128)(2,1)S(1)} %scatter_add.13), channel_id=1, source_target_pairs={{0,2},{1,3},{4,0},{5,1},{8,4},{9,5},{12,8},{13,9},{14,12},{15,13},... | collective-permute-start | bytes 393224 | tf_op jit(solution)/shard_map/ppermute | solution.py:484
  48.6 6.1 %collective-permute-start.31 = (bf16[32,16,128]{2,1,0:T(8,128)(2,1)S(1)}, bf16[32,16,128]{2,1,0:T(8,128)(2,1)S(1)}, u32[]{:S(2)}, u32[]{:S(2)}) collective-permute-start(bf16[32,16,128]{2,1,0:T(8,128)(2,1)S(1)} %scatter_add.18), channel_id=1, source_target_pairs={{0,2},{1,3},{4,0},{5,1},{8,4},{9,5},{12,8},{13,9},{14,12},{15,13},... | collective-permute-start | bytes 393224 | tf_op jit(solution)/shard_map/ppermute | solution.py:484
  50.2 6.1 %collective-permute-start.21 = (bf16[32,16,128]{2,1,0:T(8,128)(2,1)S(1)}, bf16[32,16,128]{2,1,0:T(8,128)(2,1)S(1)}, u32[]{:S(2)}, u32[]{:S(2)}) collective-permute-start(bf16[32,16,128]{2,1,0:T(8,128)(2,1)S(1)} %scatter_add.11), channel_id=1, source_target_pairs={{0,4},{1,5},{4,8},{5,9},{8,12},{9,13},{12,14},{13,15},{14,10},{15,... | collective-permute-start | bytes 393224 | tf_op jit(solution)/shard_map/ppermute | solution.py:484
  52.5 6.0 %collective-permute-start.28 = (bf16[32,16,128]{2,1,0:T(8,128)(2,1)S(1)}, bf16[32,16,128]{2,1,0:T(8,128)(2,1)S(1)}, u32[]{:S(2)}, u32[]{:S(2)}) collective-permute-start(bf16[32,16,128]{2,1,0:T(8,128)(2,1)S(1)} %scatter_add.16), channel_id=1, source_target_pairs={{0,4},{1,5},{4,8},{5,9},{8,12},{9,13},{12,14},{13,15},{14,10},{15,... | collective-permute-start | bytes 393224 | tf_op jit(solution)/shard_map/ppermute | solution.py:484
  54.3 5.0 %collective-permute-start.25 = (bf16[32,16,128]{2,1,0:T(8,128)(2,1)S(1)}, bf16[32,16,128]{2,1,0:T(8,128)(2,1)S(1)}, u32[]{:S(2)}, u32[]{:S(2)}) collective-permute-start(bf16[32,16,128]{2,1,0:T(8,128)(2,1)S(1)} %scatter_add.14), channel_id=1, source_target_pairs={{0,2},{1,3},{4,0},{5,1},{8,4},{9,5},{12,8},{13,9},{14,12},{15,13},... | collective-permute-start | bytes 393224 | tf_op jit(solution)/shard_map/ppermute | solution.py:484
  54.7 6.0 %collective-permute-start.32 = (bf16[32,16,128]{2,1,0:T(8,128)(2,1)S(1)}, bf16[32,16,128]{2,1,0:T(8,128)(2,1)S(1)}, u32[]{:S(2)}, u32[]{:S(2)}) collective-permute-start(bf16[32,16,128]{2,1,0:T(8,128)(2,1)S(1)} %scatter_add.19), channel_id=1, source_target_pairs={{0,2},{1,3},{4,0},{5,1},{8,4},{9,5},{12,8},{13,9},{14,12},{15,13},... | collective-permute-start | bytes 393224 | tf_op jit(solution)/shard_map/ppermute | solution.py:484
  56.4 5.0 %collective-permute-start.22 = (bf16[32,16,128]{2,1,0:T(8,128)(2,1)S(1)}, bf16[32,16,128]{2,1,0:T(8,128)(2,1)S(1)}, u32[]{:S(2)}, u32[]{:S(2)}) collective-permute-start(bf16[32,16,128]{2,1,0:T(8,128)(2,1)S(1)} %scatter_add.12), channel_id=1, source_target_pairs={{0,4},{1,5},{4,8},{5,9},{8,12},{9,13},{12,14},{13,15},{14,10},{15,... | collective-permute-start | bytes 393224 | tf_op jit(solution)/shard_map/ppermute | solution.py:484
  61.5 1.4 %collective-permute-start.33 = (bf16[64,8,128]{2,1,0:T(8,128)(2,1)S(1)}, bf16[64,8,128]{2,1,0:T(8,128)(2,1)S(1)}, u32[]{:S(2)}, u32[]{:S(2)}) collective-permute-start(bf16[64,8,128]{2,1,0:T(8,128)(2,1)S(1)} %get-tuple-element.62), channel_id=1, source_target_pairs={{0,1},{1,0},{2,3},{3,2},{4,5},{5,4},{6,7},{7,6},{8,9},{9,8},{10,11... | collective-permute-start | bytes 393224 | tf_op jit(solution)/shard_map/ppermute | solution.py:577
